TPU v7x, 32 devices: a whole 2x2x4 slice. The times are simulated.
32 devices in a mesh: gx: 4 (over y, core), gy: 8 (over z, x).
Axes of the slice: x: 2, y: 2, z: 4, core: 2. Of those that a mesh axis runs over, the one named last changes fastest.
Arguments:
- inputs: bfloat16 [64, 4, 2304], P('gy', None, 'gx'), may hold values from -8 to 8
- cache_pool: bfloat16 [2, 40, 1024, 1024], P(None, 'gx', 'gy'), may hold values from -6 to 6
- lengths: int32 [8], P('gy'), may hold values from 1 to 32768, as said below
- block_table: int32 [8, 33], P('gy'), may hold values from -1 to 39, as said below
- parents: int32 [3, 64], P(None, 'gy'), may hold values from 0 to 7
- norm_gains: float32 [4, 2304], P(None, 'gx'), may hold values from -0.5 to 1
- w_query: bfloat16 [2304, 2048], P('gx', 'gy'), may hold values from -0.125 to 0.125
- w_key: bfloat16 [2304, 1024], P('gx', 'gy'), may hold values from -0.125 to 0.125
- w_value: bfloat16 [2304, 1024], P('gx', 'gy'), may hold values from -0.125 to 0.125
- w_out: bfloat16 [2048, 2304], P('gy', 'gx'), may hold values from -1 to 1
- w_gate: bfloat16 [2304, 9216], P('gx', 'gy'), may hold values from -0.125 to 0.125
- w_up: bfloat16 [2304, 9216], P('gx', 'gy'), may hold values from -0.125 to 0.125
- w_down: bfloat16 [9216, 2304], P('gy', 'gx'), may hold values from -1 to 1
Outputs:
- outputs: bfloat16 [64, 4, 2304], P('gy', None, 'gx')
Inputs may be any that keep to these rules, and one draw needn't show every extreme that they name: `lengths`: a group's beams share its prompt length. block_table[g, j] is the slot, numbered over the index of gy that holds group g as gx index times 10 plus the device's slot, of page first(g) + j of the group, for j up to (lengths[g] - 1) // 128 - first(g), and -1 beyond; no slot is named twice; a device holds at most 10 pages, and some device holds 10. Beam b at step s + 1 continues beam parents[s, b] of its own group, numbered within the group.
All inputs are finite; a program needn't handle non-finite values.
Results may differ from a plain program's by a relative error of at most 0.015.
Values may be sent and summed in bfloat16 or wider, within the bound.
No kernel may reach another device: no remote copies, remote signals or barrier semaphores. Data moves between devices by JAX's collectives and lax.ppermute only.
A program may use at most 64 MiB of HBM per device.

v0:
```python
import jax
import jax.numpy as jnp
from jax import lax
from jax.sharding import PartitionSpec as P

D = 2304
HEADS = 8
KV_HEADS = 4
HEAD_DIM = 256
WINDOW = 4096
PAGE = 128
BEAM = 8


EPSILON = 1e-06
SOFT_CAP = 50.0
ROPE_BASE = 10000.0


def rotate(values, positions):
    half_width = values.shape[-1] // 2
    inverse_freq = ROPE_BASE ** (
        -jnp.arange(half_width, dtype=jnp.float32) * 2.0 / values.shape[-1]
    )
    angles = positions[..., None].astype(jnp.float32) * inverse_freq
    cosine = jnp.cos(angles)[..., None, :]
    sine_part = jnp.sin(angles)[..., None, :]
    first_half = values[..., :half_width]
    second_half = values[..., half_width:]
    return jnp.concatenate(
        [
            first_half * cosine - second_half * sine_part,
            second_half * cosine + first_half * sine_part,
        ],
        axis=-1,
    )


def ancestry(parents, beam_count, group_size, steps_count):
    beam_ids = jnp.arange(beam_count, dtype=jnp.int32)
    group_base = beam_ids // group_size * group_size
    table_rows = []
    for moment in range(steps_count):
        current = beam_ids
        chain_list = [beam_ids] * steps_count
        for earlier in range(moment, 0, -1):
            current = group_base + jnp.take(parents[earlier - 1], current)
            chain_list[earlier - 1] = current
        table_rows.append(jnp.stack(chain_list))
    return jnp.stack(table_rows)


def tail_terms(grouped, key_steps, value_steps, ancestors):
    steps_count = grouped.shape[1]
    step_ids = jnp.arange(steps_count, dtype=jnp.int32)
    tail_keys = key_steps[ancestors, step_ids[None, :, None]]
    tail_values = value_steps[ancestors, step_ids[None, :, None]]
    scores = jnp.einsum(
        "bskgd,sjbkd->bskgj", grouped, tail_keys, preferred_element_type=jnp.float32
    )
    allowed = step_ids[None, :] <= step_ids[:, None]
    weights = jnp.where(
        allowed[None, :, None, None, :], jnp.exp(SOFT_CAP * jnp.tanh(scores / SOFT_CAP)), 0.0
    )
    numerator = jnp.einsum(
        "bskgj,sjbkd->bskgd",
        weights.astype(jnp.bfloat16),
        tail_values,
        preferred_element_type=jnp.float32,
    )
    return (numerator, jnp.sum(weights, axis=-1))


def body(
    inputs,
    cache_pool,
    lengths,
    block_table,
    parents,
    norm_gains,
    w_query,
    w_key,
    w_value,
    w_out,
    w_gate,
    w_up,
    w_down,
):
    col_beams, steps_count, width_part = inputs.shape
    group_count = lengths.shape[0]
    slot_count = cache_pool.shape[1]
    rep_heads = HEADS // KV_HEADS
    x_wide = inputs.astype(jnp.float32)
    gain_rows = 1.0 + norm_gains
    square_sum = lax.psum(jnp.sum(x_wide * x_wide, axis=-1), "gx")
    normed_share = (x_wide * lax.rsqrt(square_sum / D + EPSILON)[..., None] * gain_rows[0]).astype(
        jnp.bfloat16
    )
    normed = lax.all_gather(normed_share, "gy", axis=0, tiled=True)
    all_beams = normed.shape[0]
    flat_rows = normed.reshape(-1, width_part)

    def project(weight):
        return jnp.dot(flat_rows, weight, preferred_element_type=jnp.float32).reshape(
            all_beams, steps_count, weight.shape[1]
        )

    query_sum, key_sum, value_sum = lax.psum(
        (project(w_query), project(w_key), project(w_value)), "gx"
    )
    query_raw, key_raw, value_raw = (
        lax.all_to_all(query_sum, "gy", split_axis=0, concat_axis=2, tiled=True),
        lax.all_to_all(key_sum, "gy", split_axis=0, concat_axis=2, tiled=True),
        lax.all_to_all(value_sum, "gy", split_axis=0, concat_axis=2, tiled=True),
    )
    beam_lengths = jnp.repeat(lengths, BEAM)
    step_ids = jnp.arange(steps_count, dtype=jnp.int32)
    positions = beam_lengths[:, None] + step_ids[None, :]
    queries = (
        rotate(query_raw.reshape(col_beams, steps_count, HEADS, HEAD_DIM), positions)
        * HEAD_DIM ** (-0.5)
    ).astype(jnp.bfloat16)
    key_steps = rotate(
        key_raw.reshape(col_beams, steps_count, KV_HEADS, HEAD_DIM), positions
    ).astype(jnp.bfloat16)
    value_steps = value_raw.reshape(col_beams, steps_count, KV_HEADS, HEAD_DIM).astype(jnp.bfloat16)
    grouped = queries.reshape(col_beams, steps_count, KV_HEADS, rep_heads, HEAD_DIM)
    slot_ids = lax.axis_index("gx") * slot_count + jnp.arange(slot_count, dtype=jnp.int32)
    matches = block_table[:, :, None] == slot_ids[None, None, :]
    owner_mask = jnp.any(matches, axis=1)
    slot_used = jnp.any(owner_mask, axis=0)
    page_number = jnp.sum(
        jnp.where(matches, jnp.arange(block_table.shape[1], dtype=jnp.int32)[None, :, None], 0),
        axis=(0, 1),
    )
    first_page = jnp.maximum(lengths - WINDOW + 1, 0) // PAGE
    slot_first = jnp.sum(jnp.where(owner_mask, first_page[:, None], 0), axis=0)
    slot_length = jnp.sum(jnp.where(owner_mask, lengths[:, None], 0), axis=0)
    key_positions = (slot_first + page_number)[:, None] * PAGE + jnp.arange(PAGE, dtype=jnp.int32)[
        None, :
    ]
    group_queries = grouped.reshape(group_count, BEAM, steps_count, KV_HEADS, rep_heads, HEAD_DIM)
    slot_queries = jnp.einsum(
        "an,abskgd->nbskgd",
        owner_mask.astype(jnp.bfloat16),
        group_queries,
        preferred_element_type=jnp.float32,
    ).astype(jnp.bfloat16)
    page_keys = cache_pool[0].reshape(slot_count, PAGE, KV_HEADS, HEAD_DIM)
    page_values = cache_pool[1].reshape(slot_count, PAGE, KV_HEADS, HEAD_DIM)
    scores = jnp.einsum(
        "nbskgd,ntkd->nbskgt", slot_queries, page_keys, preferred_element_type=jnp.float32
    )
    lower_bound = slot_length[:, None] + step_ids[None, :] - WINDOW + 1
    visible = (
        slot_used[:, None, None]
        & (key_positions[:, None, :] < slot_length[:, None, None])
        & (key_positions[:, None, :] >= lower_bound[:, :, None])
    )
    weights = jnp.where(
        visible[:, None, :, None, None, :], jnp.exp(SOFT_CAP * jnp.tanh(scores / SOFT_CAP)), 0.0
    )
    page_den = jnp.sum(weights, axis=-1)
    page_num = jnp.einsum(
        "nbskgt,ntkd->nbskgd",
        weights.astype(jnp.bfloat16),
        page_values,
        preferred_element_type=jnp.float32,
    )
    owner_wide = owner_mask.astype(jnp.float32)
    group_num = jnp.sum(owner_wide[:, :, None, None, None, None, None] * page_num[None], axis=1)
    group_den = jnp.sum(owner_wide[:, :, None, None, None, None] * page_den[None], axis=1)
    total_num, total_den = lax.psum((group_num, group_den), "gx")
    ancestors = ancestry(parents, col_beams, BEAM, steps_count)
    tail_num, tail_den = tail_terms(grouped, key_steps, value_steps, ancestors)
    numerator = total_num.reshape(col_beams, steps_count, KV_HEADS, rep_heads, HEAD_DIM) + tail_num
    denominator = total_den.reshape(col_beams, steps_count, KV_HEADS, rep_heads) + tail_den
    attended = (
        (numerator / denominator[..., None])
        .astype(jnp.bfloat16)
        .reshape(col_beams, steps_count, HEADS * HEAD_DIM)
    )
    head_rows = lax.all_to_all(attended, "gy", split_axis=2, concat_axis=0, tiled=True)
    head_width = head_rows.shape[2]
    attn_part = jnp.dot(
        head_rows.reshape(-1, head_width), w_out, preferred_element_type=jnp.float32
    ).reshape(all_beams, steps_count, width_part)
    attn_full = lax.psum(attn_part, "gy")
    residual = lax.all_gather(inputs, "gy", axis=0, tiled=True).astype(jnp.float32)
    attn_square = lax.psum(jnp.sum(attn_full * attn_full, axis=-1), "gx")
    mixed_full = (
        residual + attn_full * lax.rsqrt(attn_square / D + EPSILON)[..., None] * gain_rows[1]
    )
    mixed_square = lax.psum(jnp.sum(mixed_full * mixed_full, axis=-1), "gx")
    ff_input = (
        mixed_full * lax.rsqrt(mixed_square / D + EPSILON)[..., None] * gain_rows[2]
    ).astype(jnp.bfloat16)
    mixed_rows = lax.dynamic_slice_in_dim(
        mixed_full, lax.axis_index("gy") * col_beams, col_beams, 0
    )
    gate_width = w_gate.shape[1]
    matrix_rows = ff_input.reshape(-1, width_part)
    gate_and_up = jnp.concatenate(
        [
            jnp.dot(matrix_rows, w_gate, preferred_element_type=jnp.float32),
            jnp.dot(matrix_rows, w_up, preferred_element_type=jnp.float32),
        ],
        axis=1,
    )
    activate_gate_and_up = lax.psum_scatter(
        gate_and_up.reshape(ff_input.shape[0], steps_count, 2 * gate_width),
        "gx",
        scatter_dimension=0,
        tiled=True,
    )
    hidden_share = (
        jax.nn.gelu(activate_gate_and_up[..., :gate_width], approximate=True)
        * activate_gate_and_up[..., gate_width:]
    ).astype(jnp.bfloat16)
    hidden_rows = lax.all_gather(hidden_share, "gx", axis=0, tiled=True)
    down_part = jnp.dot(
        hidden_rows.reshape(-1, gate_width), w_down, preferred_element_type=jnp.float32
    ).reshape(hidden_rows.shape[0], steps_count, width_part)
    down_own = lax.psum_scatter(down_part, "gy", scatter_dimension=0, tiled=True)
    out_square = lax.psum(jnp.sum(down_own * down_own, axis=-1), "gx")
    return (
        mixed_rows + down_own * lax.rsqrt(out_square / D + EPSILON)[..., None] * gain_rows[3]
    ).astype(jnp.bfloat16)


def solution(mesh):
    return jax.shard_map(
        body,
        mesh=mesh,
        in_specs=(
            P("gy", None, "gx"),
            P(None, "gx", "gy", None),
            P("gy"),
            P("gy", None),
            P(None, "gy"),
            P(None, "gx"),
            P("gx", "gy"),
            P("gx", "gy"),
            P("gx", "gy"),
            P("gy", "gx"),
            P("gx", "gy"),
            P("gx", "gy"),
            P("gy", "gx"),
        ),
        out_specs=P("gy", None, "gx"),
        check_vma=False,
    )
```

profile of v0, /device:TPU:0, one launch (start us, length us, event | category | flops | bytes accessed | tf_op | source)
XLA Modules:
  0.0 411.9 jit_solution(1449051580651375950)
XLA Ops:
  8.9 8.3 %psum.70 = f32[8,4]{0,1:T(4,128)S(1)} all-reduce(f32[8,4]{0,1:T(4,128)S(1)} %fusion.37), channel_id=1, replica_groups=mesh['gx'=4,'gy'=8] {'gx'}, use_global_device_ids=true, to_apply=%region_3.0 | all-reduce | flops 32 | bytes 256 | tf_op jit(solution)/shard_map/psum | solution.py:95
  18.1 31.3 %all_gather.10 = bf16[64,4,576]{2,0,1:T(8,128)(2,1)S(1)} all-gather(bf16[8,4,576]{2,0,1:T(8,128)(2,1)S(1)} %fusion.39), channel_id=1, replica_groups=mesh['gx'=4,'gy'=8] {'gy'}, dimensions={0}, use_global_device_ids=true | all-gather | bytes 331776 | tf_op jit(solution)/shard_map/all_gather | solution.py:99
  49.4 1.9 fusion.27
  53.0 5.7 %fusion.60 = (bf16[1,10,128,1024]{3,2,1,0:T(8,128)(2,1)}, bf16[1,10,128,1024]{3,2,1,0:T(8,128)(2,1)}) fusion(bf16[2,10,128,1024]{3,2,1,0:T(8,128)(2,1)} %param.16), kind=kLoop, calls=%fused_computation.142 | loop fusion | bytes 10485760 | tf_op jit(solution)/shard_map/slice | solution.py:149
  58.7 4.5 %copy.183 = bf16[1,10,128,1024]{2,3,1,0:T(8,128)(2,1)} copy(bf16[1,10,128,1024]{3,2,1,0:T(8,128)(2,1)} %get-tuple-element.19) | data formatting | bytes 5242880
  63.2 4.4 %copy.182 = bf16[1,10,128,1024]{2,3,1,0:T(8,128)(2,1)} copy(bf16[1,10,128,1024]{3,2,1,0:T(8,128)(2,1)} %get-tuple-element.18) | data formatting | bytes 5242880
  72.1 11.3 %all-reduce.7.cloned.1.call-done = f32[64,4,256]{2,0,1:T(8,128)} async-done(((f32[64,4,256]{2,0,1:T(8,128)}), f32[64,4,256]{2,0,1:T(8,128)}) %all-reduce.7.cloned.1.call-update) | async-done | bytes 262160 | tf_op jit(solution)/shard_map/psum | solution.py:108
  83.4 1.8 copy.146
  85.2 5.6 %all-to-all-start = ((f32[64,4,256]{2,1,0:T(4,128)}), f32[64,4,256]{2,1,0:T(4,128)S(1)}, u32[]{:S(2)}, u32[]{:S(2)}) async-start(f32[64,4,256]{2,1,0:T(4,128)} %copy.146), calls=%async_computation | async-start | bytes 524288 | tf_op jit(solution)/shard_map/all_to_all | solution.py:112
  91.7 7.3 %all-to-all-done = f32[64,4,256]{2,1,0:T(4,128)S(1)} async-done(((f32[64,4,256]{2,1,0:T(4,128)}), f32[64,4,256]{2,1,0:T(4,128)S(1)}, u32[]{:S(2)}, u32[]{:S(2)}) %all-to-all-start) | async-done | bytes 262176 | tf_op jit(solution)/shard_map/all_to_all | solution.py:112
  99.5 2.8 fusion.61
  104.4 12.3 %all-reduce.12 = (bf16[64,4,128]{2,0,1:T(8,128)(2,1)S(1)}, f32[8,4,4,2]{0,2,3,1:T(4,128)S(1)}) all-reduce(f32[64,4,128]{2,0,1:T(8,128)S(1)} %fusion.32, f32[8,4,4,2]{0,2,3,1:T(4,128)S(1)} %copy.162), channel_id=1, replica_groups=mesh['gx'=4,'gy'=8] {'gx'}, use_global_device_ids=true, to_apply=%region_8.10 | all-reduce | flops 33024 | bytes 198656 | tf_op jit(solution)/shard_map/psum | solution.py:108
  117.3 3.3 all-to-all-start.2
  121.4 35.9 %all-reduce.11.cloned.1.call-done = (f32[8,4,4,2,256]{4,3,2,1,0:T(2,128)}, f32[64,4,128]{2,0,1:T(8,128)}) async-done(((f32[8,4,4,2,256]{4,3,2,1,0:T(2,128)}, f32[64,4,128]{2,0,1:T(8,128)}), (f32[8,4,4,2,256]{4,3,2,1,0:T(2,128)}, f32[64,4,128]{2,0,1:T(8,128)})) %all-reduce.11.cloned.1.call-update) | async-done | bytes 393232 | tf_op jit(solution)/shard_map/psum | solution.py:173
  157.3 1.6 copy.154
  159.0 5.5 %all-to-all-start.1 = ((f32[64,4,128]{2,1,0:T(4,128)}), f32[64,4,128]{2,1,0:T(4,128)S(1)}, u32[]{:S(2)}, u32[]{:S(2)}) async-start(f32[64,4,128]{2,1,0:T(4,128)} %copy.154), calls=%async_computation.1 | async-start | bytes 262144 | tf_op jit(solution)/shard_map/all_to_all | solution.py:113
  165.8 6.0 %all-to-all-done.1 = f32[64,4,128]{2,1,0:T(4,128)S(1)} async-done(((f32[64,4,128]{2,1,0:T(4,128)}), f32[64,4,128]{2,1,0:T(4,128)S(1)}, u32[]{:S(2)}, u32[]{:S(2)}) %all-to-all-start.1) | async-done | bytes 131104 | tf_op jit(solution)/shard_map/all_to_all | solution.py:113
  175.7 2.2 reshape.614
  177.9 10.4 %all_to_all.54 = bf16[8,2,4096]{2,1,0:T(2,128)(2,1)} all-to-all(bf16[8,2,4096]{2,1,0:T(2,128)(2,1)S(1)} %reshape.614), channel_id=1, replica_groups=mesh['gx'=4,'gy'=8] {'gy'}, dimensions={0} | all-to-all | bytes 262144 | tf_op jit(solution)/shard_map/all_to_all | solution.py:183
  188.3 3.3 reshape.615
  192.8 2.1 fusion.25
  195.0 31.9 %all_gather.9 = bf16[64,4,576]{2,0,1:T(8,128)(2,1)S(1)} all-gather(bf16[8,4,576]{2,0,1:T(8,128)(2,1)S(1)} %copy.143), channel_id=1, replica_groups=mesh['gx'=4,'gy'=8] {'gy'}, dimensions={0}, use_global_device_ids=true | all-gather | bytes 331776 | tf_op jit(solution)/shard_map/all_gather | solution.py:189
  227.0 39.3 %all-reduce.9.cloned.1.call-done = f32[64,4,576]{2,0,1:T(8,128)} async-done(((f32[64,4,576]{2,0,1:T(8,128)}), f32[64,4,576]{2,0,1:T(8,128)}) %all-reduce.9.cloned.1.call-update) | async-done | bytes 589840 | tf_op jit(solution)/shard_map/psum | solution.py:188
  267.5 5.7 %psum.77 = f32[64,4]{0,1:T(4,128)S(1)} all-reduce(f32[64,4]{0,1:T(4,128)S(1)} %multiply_reduce_fusion.2), channel_id=1, replica_groups=mesh['gx'=4,'gy'=8] {'gx'}, use_global_device_ids=true, to_apply=%region_15.17 | all-reduce | flops 256 | bytes 2048 | tf_op jit(solution)/shard_map/psum | solution.py:190
  274.5 6.6 %psum.78 = f32[64,4]{0,1:T(4,128)S(1)} all-reduce(f32[64,4]{0,1:T(4,128)S(1)} %get-tuple-element.14), channel_id=1, replica_groups=mesh['gx'=4,'gy'=8] {'gx'}, use_global_device_ids=true, to_apply=%region_17.19 | all-reduce | flops 256 | bytes 2048 | tf_op jit(solution)/shard_map/psum | solution.py:194
  283.7 1.6 pad_maximum_fusion
  285.3 3.4 reshape.522
  288.6 3.5 copy.168
  292.2 31.9 %reduce-scatter.3.cloned.1.call-done = f32[16,4,2304]{2,0,1:T(8,128)} async-done(((f32[64,4,2304]{2,0,1:T(8,128)}), f32[16,4,2304]{2,0,1:T(8,128)}) %reduce-scatter.3.cloned.1.call-update) | async-done | bytes 589840 | tf_op jit(solution)/shard_map/reduce_scatter | solution.py:210
  325.3 7.1 %all_gather.11 = bf16[64,4,1152]{2,0,1:T(8,128)(2,1)S(1)} all-gather(bf16[16,4,1152]{2,0,1:T(8,128)(2,1)S(1)} %fusion.24), channel_id=1, replica_groups=mesh['gx'=4,'gy'=8] {'gx'}, dimensions={0}, use_global_device_ids=true | all-gather | bytes 737280 | tf_op jit(solution)/shard_map/all_gather | solution.py:220
  334.0 63.1 %reduce-scatter.5.cloned.1.call-done = f32[8,4,576]{2,0,1:T(8,128)} async-done(((f32[64,4,576]{2,0,1:T(8,128)}), f32[8,4,576]{2,0,1:T(8,128)}) %reduce-scatter.5.cloned.1.call-update) | async-done | bytes 73744 | tf_op jit(solution)/shard_map/reduce_scatter | solution.py:224
  398.1 5.6 %psum.79 = f32[8,4]{0,1:T(4,128)S(1)} all-reduce(f32[8,4]{0,1:T(4,128)S(1)} %multiply_reduce_fusion.4), channel_id=1, replica_groups=mesh['gx'=4,'gy'=8] {'gx'}, use_global_device_ids=true, to_apply=%region_21.23 | all-reduce | flops 32 | bytes 256 | tf_op jit(solution)/shard_map/psum | solution.py:225
  (119 shorter events, 30.1 us)
Async XLA Ops:
  6.5 275.2 %copy-start = (bf16[576,1152]{1,0:T(8,128)(2,1)S(1)}, bf16[576,1152]{1,0:T(8,128)(2,1)}, u32[]{:S(2)}) copy-start(bf16[576,1152]{1,0:T(8,128)(2,1)} %param.26) | copy-start | bytes 3981316
  6.5 44.9 %copy-start.12 = (s32[1,33]{1,0:T(1,128)S(1)}, s32[1,33]{1,0:T(1,128)}, u32[]{:S(2)}) copy-start(s32[1,33]{1,0:T(1,128)} %param.18) | copy-start | bytes 400
  6.5 76.8 %all-reduce.7.cloned.1.call-start = ((), (), s32[]{:S(2)}) async-start(), calls=%async_computation.6 | async-start | bytes 524288 | tf_op jit(solution)/shard_map/psum | solution.py:108
  63.2 4.4 %copy-start.5 = (bf16[576,128]{1,0:T(8,128)(2,1)S(1)}, bf16[576,128]{1,0:T(8,128)(2,1)}, u32[]{:S(2)}) copy-start(bf16[576,128]{1,0:T(8,128)(2,1)} %param.23) | copy-start | bytes 442372
  63.2 4.7 %copy-start.10 = (s32[3,8]{1,0:T(4,128)S(1)}, s32[3,8]{1,0:T(4,128)}, u32[]{:S(2)}) copy-start(s32[3,8]{1,0:T(4,128)} %param.19) | copy-start | bytes 292
  69.9 20.9 %copy-start.6 = (bf16[576,128]{1,0:T(8,128)(2,1)S(1)}, bf16[576,128]{1,0:T(8,128)(2,1)}, u32[]{:S(2)}) copy-start(bf16[576,128]{1,0:T(8,128)(2,1)} %param.22) | copy-start | bytes 442372
  85.2 13.8 %all-to-all-start = ((f32[64,4,256]{2,1,0:T(4,128)}), f32[64,4,256]{2,1,0:T(4,128)S(1)}, u32[]{:S(2)}, u32[]{:S(2)}) async-start(f32[64,4,256]{2,1,0:T(4,128)} %copy.146), calls=%async_computation | async-start | bytes 524288 | tf_op jit(solution)/shard_map/all_to_all | solution.py:112
  99.5 2.8 copy-start.1
  117.3 41.6 %all-to-all-start.2 = ((bf16[64,4,128]{2,1,0:T(4,128)(2,1)}), bf16[64,4,128]{2,1,0:T(4,128)(2,1)S(1)}, u32[]{:S(2)}, u32[]{:S(2)}) async-start(bf16[64,4,128]{2,1,0:T(4,128)(2,1)} %copy.158), calls=%async_computation.2 | async-start | bytes 131072 | tf_op jit(solution)/shard_map/all_to_all | solution.py:114
  120.7 36.6 %all-reduce.11.cloned.1.call-start = ((), (), s32[]{:S(2)}) async-start(), calls=%async_computation.10 | async-start | bytes 786432 | tf_op jit(solution)/shard_map/psum | solution.py:173
  159.0 12.9 %all-to-all-start.1 = ((f32[64,4,128]{2,1,0:T(4,128)}), f32[64,4,128]{2,1,0:T(4,128)S(1)}, u32[]{:S(2)}, u32[]{:S(2)}) async-start(f32[64,4,128]{2,1,0:T(4,128)} %copy.154), calls=%async_computation.1 | async-start | bytes 262144 | tf_op jit(solution)/shard_map/all_to_all | solution.py:113
  164.5 101.8 %all-reduce.9.cloned.1.call-start = ((), (), s32[]{:S(2)}) async-start(), calls=%async_computation.7 | async-start | bytes 1310720 | tf_op jit(solution)/shard_map/psum | solution.py:188
  173.1 1.0 copy-start.11
  192.8 2.2 copy-start.4
  192.8 80.4 %copy-start.8 = (f32[576]{0:T(1024)S(1)}, f32[576]{0:T(1024)}, u32[]{:S(2)}) copy-start(f32[576]{0:T(1024)} %get-tuple-element.8) | copy-start | bytes 6916
  195.0 129.2 %reduce-scatter.3.cloned.1.call-start = ((), (), s32[]{:S(2)}) async-start(), calls=%async_computation.8 | async-start | bytes 2949120 | tf_op jit(solution)/shard_map/reduce_scatter | solution.py:210
  195.0 86.1 %copy-start.7 = (f32[576]{0:T(1024)S(1)}, f32[576]{0:T(1024)}, u32[]{:S(2)}) copy-start(f32[576]{0:T(1024)} %get-tuple-element.7) | copy-start | bytes 6916
  281.7 1.3 copy-start.3
  292.1 40.3 %copy-start.2 = (bf16[1152,576]{0,1:T(8,128)(2,1)S(1)}, bf16[1152,576]{0,1:T(8,128)(2,1)}, u32[]{:S(2)}) copy-start(bf16[1152,576]{0,1:T(8,128)(2,1)} %param.27) | copy-start | bytes 3981316
  292.2 105.0 %reduce-scatter.5.cloned.1.call-start = ((), (), s32[]{:S(2)}) async-start(), calls=%async_computation.9 | async-start | bytes 737280 | tf_op jit(solution)/shard_map/reduce_scatter | solution.py:224
  332.4 71.3 %copy-start.9 = (f32[576]{0:T(1024)S(1)}, f32[576]{0:T(1024)}, u32[]{:S(2)}) copy-start(f32[576]{0:T(1024)} %get-tuple-element.6) | copy-start | bytes 6916
Sparse Core Ops, SparseCore 0:
  51.5 31.8 all-reduce.6
  124.1 33.1 all-reduce.10
  195.1 71.1 all-reduce.8
  292.3 31.8 reduce-scatter.2
  334.1 62.9 reduce-scatter.4
where the time goes:
time: 413 us; the launch traced here: 412 us
  waiting for transfers between devices  196 us (47%)
  blocking collectives  119 us (29%)
  local copies, waits for them, and re-layouts  43.7 us (11%)
  starting transfers between devices  14.6 us (4%)
  between operations  14.3 us (3%)
  matrix products  12.7 us (3%)
  other arithmetic  11.6 us (3%)
    reduce_scatter x1, waiting for transfers between devices, body(): lax.psum_scatter(down_part, 'gy', scatter_dimension=0, tiled=True)  63.1 us
    psum x1, waiting for transfers between devices, body(): attn_full = lax.psum(attn_part, 'gy')  39.3 us
    psum x1, waiting for transfers between devices, body(): total_num, total_den = lax.psum((group_num, group_den), 'gx')  35.9 us
    all_gather x1, blocking collectives, body(): lax.all_gather(inputs, 'gy', axis=0, tiled=True).astype(jnp.float32)  31.9 us
    reduce_scatter x1, waiting for transfers between devices, body(): lax.psum_scatter(gate_and_up.reshape(ff_input.shape[0], steps_count, 2 *...  31.9 us
    all_gather x1, blocking collectives, body(): normed = lax.all_gather(normed_share, 'gy', axis=0, tiled=True)  31.3 us
    unnamed x31, local copies, waits for them, and re-layouts  15.2 us
    psum x1, blocking collectives, body(): lax.psum((project(w_query), project(w_key), project(w_value)), 'gx')  12.3 us
  transfers between devices with their start and end apart: 8, of which 7 were waited for; matrix products, arithmetic and copies ran while one was open for 6% of the time, Pallas kernels for 0%

commit v1 on v0

v1 whole, which is shorter than its diff:
```python
import jax
import jax.numpy as jnp
from jax import lax
from jax.experimental import pallas as pl
from jax.experimental.pallas import tpu as pltpu
from jax.sharding import PartitionSpec as P

D = 2304
HEADS = 8
KV_HEADS = 4
HEAD_DIM = 256
HALF = HEAD_DIM // 2
WINDOW = 4096
PAGE = 128
BEAM = 8
EPSILON = 1e-06
SOFT_CAP = 50.0
ROPE_BASE = 10000.0
BF = jnp.bfloat16
F32 = jnp.float32
MIB = 1024 * 1024
GAIN_ROWS = 16


def stage(fast, name, f, outs, *args, limit=16):
    if not fast:
        return f(*args)

    def kernel(*refs):
        results = f(*[r[...] for r in refs[: len(args)]])
        for ref, result in zip(refs[len(args) :], results):
            ref[...] = result.astype(ref.dtype)

    return pl.pallas_call(
        kernel,
        out_shape=[jax.ShapeDtypeStruct(s, d) for s, d in outs],
        compiler_params=pltpu.CompilerParams(vmem_limit_bytes=limit * MIB),
        name=name,
    )(*args)


def exchange(values, axes):
    return lax.all_to_all(values, axes, split_axis=0, concat_axis=0, tiled=True)


def exchange_all(values):
    nx, ny = values.shape[:2]
    flat = values.reshape((nx * ny,) + values.shape[2:])
    return exchange(flat, ("gx", "gy")).reshape(values.shape)


def weight_of(scores):
    return jnp.exp(SOFT_CAP * jnp.tanh(scores * (1.0 / SOFT_CAP)))


def attention_kernel(
    table_ref, length_ref, parents_ref, g_ref, x_ref, cos_ref, sin_ref, pool_ref, out_ref, page_ref
):
    parts, reps, part_rows = out_ref.shape[:3]
    rows = parts * part_rows
    steps = rows // BEAM
    slots = pool_ref.shape[1]
    first_owner = lax.axis_index("gx") * slots
    length = length_ref[0]
    first_page = jnp.maximum(length - WINDOW + 1, 0) // PAGE
    x = x_ref[...].astype(F32)
    square = jnp.sum(jnp.sum(x * x, axis=0), axis=-1, keepdims=True)
    scale = lax.rsqrt(square / D + EPSILON)
    cos, sin = cos_ref[...], sin_ref[...]

    def rotated(u, w):
        u, w = u.astype(F32) * scale, w.astype(F32) * scale
        return u * cos - w * sin, w * cos + u * sin

    query = []
    for rep in range(reps):
        u, w = rotated(g_ref[0, rep], g_ref[1, rep])
        query.append(jnp.concatenate([u, w], axis=1) * HEAD_DIM ** (-0.5))
    query = jnp.concatenate(query, axis=0).astype(BF)
    key_step = jnp.concatenate(rotated(g_ref[2, 0], g_ref[2, 1]), axis=1).astype(BF)
    value_step = jnp.concatenate(
        [g_ref[3, 0].astype(F32) * scale, g_ref[3, 1].astype(F32) * scale], axis=1
    ).astype(BF)

    for slot in range(slots):
        page_ref[slot] = -1

    def place(j, carry):
        slot = table_ref[0, j] - first_owner

        @pl.when((slot >= 0) & (slot < slots))
        def _():
            page_ref[slot] = j

        return carry

    lax.fori_loop(0, table_ref.shape[1], place, 0)
    lane = lax.broadcasted_iota(jnp.int32, (1, PAGE), 1)
    far = jnp.int32(2**30)
    position = jnp.concatenate(
        [
            lane + jnp.where(page_ref[s] >= 0, (first_page + page_ref[s]) * PAGE, far)
            for s in range(slots)
        ],
        axis=1,
    )
    step_of = lax.broadcasted_iota(jnp.int32, (reps * rows, 1), 0) % steps
    lower = length + step_of - (WINDOW - 1)
    seen = (position < length) & (position >= lower)
    keys = pool_ref[0].reshape(slots * PAGE, HEAD_DIM)
    values = pool_ref[1].reshape(slots * PAGE, HEAD_DIM)
    contract_last = (((1,), (1,)), ((), ()))
    scores = lax.dot_general(query, keys, contract_last, preferred_element_type=F32)
    weights = jnp.where(seen, weight_of(scores), 0.0)
    den = jnp.sum(weights, axis=-1, keepdims=True)
    num = jnp.dot(weights.astype(BF), values, preferred_element_type=F32)

    shape = (reps * rows, rows)
    row = lax.broadcasted_iota(jnp.int32, shape, 0) % rows
    column = lax.broadcasted_iota(jnp.int32, shape, 1)
    row_step, column_step, column_beam = row % steps, column % steps, column // steps
    current = row // steps
    visible = jnp.zeros(shape, jnp.bool_)
    for j in range(steps - 1, -1, -1):
        if j < steps - 1:
            parent = jnp.zeros(shape, jnp.int32)
            for beam in range(BEAM):
                parent = jnp.where(current == beam, parents_ref[j, beam], parent)
            current = jnp.where(row_step > j, parent, current)
        visible = visible | ((column_step == j) & (row_step >= j) & (column_beam == current))
    visible = visible & (lax.axis_index("gx") == 0)
    scores = lax.dot_general(query, key_step, contract_last, preferred_element_type=F32)
    weights = jnp.where(visible, weight_of(scores), 0.0)
    den = den + jnp.sum(weights, axis=-1, keepdims=True)
    num = num + jnp.dot(weights.astype(BF), value_step, preferred_element_type=F32)

    high = den.astype(BF).astype(F32)
    wide = lax.broadcasted_iota(jnp.int32, (reps * rows, PAGE), 1)
    den_lanes = jnp.where(wide < PAGE // 2, high, den - high)
    for part in range(parts):
        for rep in range(reps):
            here = slice(rep * rows + part * part_rows, rep * rows + (part + 1) * part_rows)
            out_ref[part, rep, :, 0:HEAD_DIM] = num[here].astype(BF)
            out_ref[part, rep, :, HEAD_DIM:] = den_lanes[here].astype(BF)


def attention(parts, table, lengths, parents, g, wide, x_block, cos, sin, pool):
    rows = g.shape[2]
    reps = HEADS // KV_HEADS
    nx, _, width = wide.shape
    slots = pool.shape[1]
    smem = pl.BlockSpec(memory_space=pltpu.SMEM)
    return pl.pallas_call(
        attention_kernel,
        grid=(KV_HEADS,),
        in_specs=[
            smem,
            smem,
            smem,
            pl.BlockSpec((4, 2, rows, HALF), lambda h: (0, h, 0, 0)),
            pl.BlockSpec((nx, rows, width), lambda h: (0, x_block, 0)),
            pl.BlockSpec((rows, HALF), lambda h: (0, 0)),
            pl.BlockSpec((rows, HALF), lambda h: (0, 0)),
            pl.BlockSpec((2, slots, PAGE, HEAD_DIM), lambda h: (0, 0, 0, h)),
        ],
        out_specs=pl.BlockSpec(
            (parts, reps, rows // parts, HEAD_DIM + PAGE), lambda h: (0, h, 0, 0)
        ),
        out_shape=jax.ShapeDtypeStruct((parts, HEADS, rows // parts, HEAD_DIM + PAGE), BF),
        scratch_shapes=[pltpu.SMEM((slots,), jnp.int32)],
        compiler_params=pltpu.CompilerParams(vmem_limit_bytes=24 * MIB),
        name="attention",
    )(table, lengths, parents, g, wide, cos, sin, pool)


def body(
    inputs,
    cache_pool,
    lengths,
    block_table,
    parents,
    norm_gains,
    w_query,
    w_key,
    w_value,
    w_out,
    w_gate,
    w_up,
    w_down,
):
    beams, steps, width = inputs.shape
    nx, ny = lax.axis_size("gx"), lax.axis_size("gy")
    rows = beams * steps
    part = rows // nx
    head_part = w_out.shape[0]
    hidden_part = w_gate.shape[1]
    query_part, key_part = w_query.shape[1], w_key.shape[1]
    columns = query_part + 2 * key_part
    share = columns // nx
    fast = part % 8 == 0 and share == HALF and head_part == HEAD_DIM and query_part == 2 * share
    x_own = inputs.reshape(rows, width)

    def rounded(v):
        return lax.reduce_precision(v, 8, 7)

    gain_high = rounded(norm_gains)
    gain_mid = rounded(norm_gains - gain_high)
    gain_low = norm_gains - gain_high - gain_mid
    gain_pad = jnp.zeros((GAIN_ROWS - 12, width), F32)
    gain_block = jnp.concatenate([gain_high, gain_mid, gain_low, gain_pad], axis=0).astype(BF)
    wide = lax.all_gather(jnp.concatenate([w_out, x_own, gain_block], axis=0), "gx", axis=0)

    x_all = exchange(jnp.broadcast_to(x_own[None], (ny, rows, width)), "gy")

    def project(x, gains, wq, wk, wv):
        flat = (x.astype(F32) * (1.0 + gains[0:1])).astype(BF).reshape(ny * rows, width)
        sums = [jnp.dot(flat, w, preferred_element_type=F32) for w in (wq, wk, wv)]
        if fast:
            sums = [sums[0][:, :share], sums[0][:, share:], sums[1], sums[2]]
            return [jnp.stack([s.reshape(ny, rows, share) for s in sums]).astype(BF)]
        both = jnp.concatenate(sums, axis=1).reshape(ny, rows, nx, share)
        return [both.transpose(2, 0, 1, 3).astype(BF)]

    (send,) = stage(
        fast,
        "project",
        project,
        [((nx, ny, rows, share), BF)],
        x_all,
        norm_gains,
        w_query,
        w_key,
        w_value,
    )
    received = exchange_all(send)
    (shares,) = stage(
        fast,
        "sum_shares",
        lambda v: [jnp.sum(v.astype(F32), axis=0).astype(BF)],
        [((ny, rows, share), BF)],
        received,
    )
    g = lax.all_gather(shares, "gx", axis=0)
    if not fast:
        every = g.transpose(2, 1, 0, 3).reshape(rows, ny, columns)
        q = every[..., :query_part].reshape(rows, HEADS, 2, HALF).transpose(2, 1, 0, 3)
        k, v = (
            every[..., start : start + key_part].reshape(rows, 2 * KV_HEADS, HALF).transpose(1, 0, 2)
            for start in (query_part, query_part + key_part)
        )
        g = jnp.concatenate([q, k[None], v[None]], axis=0)

    positions = lengths[0] + jnp.arange(rows, dtype=jnp.int32) % steps
    inverse_freq = ROPE_BASE ** (-jnp.arange(HALF, dtype=F32) * 2.0 / HEAD_DIM)
    angles = positions[:, None].astype(F32) * inverse_freq
    terms = attention(
        nx if fast else 1,
        block_table,
        lengths,
        parents,
        g,
        wide,
        head_part // rows,
        jnp.cos(angles),
        jnp.sin(angles),
        cache_pool,
    )
    if not fast:
        terms = terms.reshape(HEADS, rows, HEAD_DIM + PAGE)
        num = terms[..., :HEAD_DIM].transpose(1, 0, 2).reshape(nx, part, ny, head_part)
        den = terms[..., HEAD_DIM :: PAGE // 2].transpose(1, 0, 2)
        den = jnp.repeat(den, ny // HEADS, axis=1).reshape(nx, part, ny, 2)
        terms = jnp.concatenate([num, den], axis=-1).transpose(0, 2, 1, 3)
    terms = exchange_all(terms)

    def project_out(t, w_wide):
        t = jnp.sum(t.astype(F32), axis=0)
        den = t[..., head_part : head_part + 1] + t[..., -1:]
        attended = (t[..., :head_part] / den).reshape(ny * part, head_part).astype(BF)
        return [
            jnp.stack(
                [
                    jnp.dot(attended, w_wide[k, :head_part], preferred_element_type=F32).reshape(
                        ny, part, width
                    )
                    for k in range(nx)
                ],
                axis=1,
            ).astype(BF)
        ]

    (attn_parts,) = stage(
        fast, "project_out", project_out, [((ny, nx, part, width), BF)], terms, wide
    )
    attn_parts = exchange(attn_parts, "gy")
    x_rows = lax.dynamic_slice_in_dim(wide, head_part + lax.axis_index("gx") * part, part, 1)
    gains_wide = wide[:, head_part + rows :]

    def gain_of(gains, index):
        gains = gains.astype(F32)
        high, mid, low = (gains[:, 4 * t + index : 4 * t + index + 1] for t in range(3))
        return 1.0 + (high + (mid + low))

    def row_scale(v):
        square = jnp.sum(jnp.sum(v * v, axis=0), axis=-1, keepdims=True)
        return lax.rsqrt(square / D + EPSILON)[None]

    def mix(parts, x, gains):
        attn = jnp.sum(parts.astype(F32), axis=0)
        mixed = x.astype(F32) + attn * row_scale(attn) * gain_of(gains, 1)
        ff_input = (mixed * row_scale(mixed) * gain_of(gains, 2)).astype(BF)
        return [mixed, jnp.broadcast_to(ff_input[:, None], (nx, ny, part, width))]

    mixed, ff_input = stage(
        fast,
        "mix",
        mix,
        [((nx, part, width), F32), ((nx, ny, part, width), BF)],
        attn_parts,
        x_rows,
        gains_wide,
    )
    ff_input = exchange_all(ff_input)

    def gate_up(ff, wg, wu):
        flat = ff.astype(F32).reshape(nx * ny * part, width).astype(BF)
        both = [jnp.dot(flat, w, preferred_element_type=F32).astype(BF) for w in (wg, wu)]
        return [jnp.concatenate(both, axis=1).reshape(nx, ny * part, 2 * hidden_part)]

    (both,) = stage(
        fast,
        "gate_up",
        gate_up,
        [((nx, ny * part, 2 * hidden_part), BF)],
        ff_input,
        w_gate,
        w_up,
        limit=24,
    )
    both = exchange(both, "gx")

    def activate(v):
        v = jnp.sum(v.astype(F32), axis=0)
        gate, up = v[:, :hidden_part], v[:, hidden_part:]
        return [(jax.nn.gelu(gate, approximate=True) * up).astype(BF)]

    (hidden,) = stage(fast, "activate", activate, [((ny * part, hidden_part), BF)], both)
    hidden = lax.all_gather(hidden, "gx", axis=0)

    def project_down(h, w):
        down = jnp.dot(
            h.reshape(nx * ny * part, hidden_part), w, preferred_element_type=F32
        )
        return [down.reshape(nx, ny, part, width).astype(BF)]

    (down,) = stage(
        fast, "project_down", project_down, [((nx, ny, part, width), BF)], hidden, w_down
    )
    down = exchange_all(down)

    def finish(parts, mixed_rows, gains):
        total = jnp.sum(parts.astype(F32), axis=1)
        return [(mixed_rows + total * row_scale(total) * gain_of(gains, 3)).astype(BF)]

    (out,) = stage(fast, "finish", finish, [((nx, part, width), BF)], down, mixed, gains_wide)
    return exchange(out, "gx").reshape(beams, steps, width)


def solution(mesh):
    return jax.shard_map(
        body,
        mesh=mesh,
        in_specs=(
            P("gy", None, "gx"),
            P(None, "gx", "gy", None),
            P("gy"),
            P("gy", None),
            P(None, "gy"),
            P(None, "gx"),
            P("gx", "gy"),
            P("gx", "gy"),
            P("gx", "gy"),
            P("gy", "gx"),
            P("gx", "gy"),
            P("gx", "gy"),
            P("gy", "gx"),
        ),
        out_specs=P("gy", None, "gx"),
        check_vma=False,
    )
```

time: 413 us -> 162 us (0.39)
  waiting for transfers between devices: 196 us -> 32.3 us
  blocking collectives: 119 us -> 78 us
  local copies, waits for them, and re-layouts: 43.7 us -> 13.7 us
  matrix products: 12.7 us -> 0 us
  Pallas kernels: 0 us -> 11.3 us
  other arithmetic: 11.6 us -> 0.87 us
    reduce_scatter x2 -> x0, waiting for transfers between devices: 95.1 us -> none  [the longest x1 63.1 us: body(): lax.psum_scatter(down_part, 'gy', scatter_dimension=0, tiled=True)]
    psum x3 -> x0, waiting for transfers between devices: 86.5 us -> none  [the longest x1 39.3 us: body(): attn_full = lax.psum(attn_part, 'gy')]
    all_gather x3 -> x2, blocking collectives: 70.4 us -> 12.7 us  [the longest x1 6.94 us: body(): hidden = lax.all_gather(hidden, 'gx', axis=0)]
    all_to_all x1 -> x5, blocking collectives: 10.4 us -> 65.2 us  [exchange(): return lax.all_to_all(values, axes, split_axis=0, concat_axis=0, tiled=True)]
    psum x5 -> x0, blocking collectives: 38.5 us -> none  [the longest x1 12.3 us: body(): lax.psum((project(w_query), project(w_key), project(w_value)), 'gx')]
    all_to_all x3, waiting for transfers between devices: 13.3 us -> 32.2 us  [exchange(): return lax.all_to_all(values, axes, split_axis=0, concat_axis=0, tiled=True)]
    dot_general x11 -> x0, matrix products: 12.7 us -> none  [the longest x3 3.08 us: project(): jnp.dot(flat_rows, weight, preferred_element_type=jnp.float32)]
    pallas_call x0 -> x9, Pallas kernels: none -> 11.3 us  [the longest x8 5.86 us: stage(): pl.pallas_call(kernel, out_shape=[jax.ShapeDtypeStruct(s, d) for s, d in...]
  transfers between devices with their start and end apart: 8 -> 4, of which waited for: 7 -> 3; matrix products, arithmetic and copies ran while one was open for 6% -> 2% of each run, Pallas kernels for 0% -> 1%
where the time goes in v1:
time: 162 us; the launch traced here: 161 us
  blocking collectives  78 us (48%)
  waiting for transfers between devices  32.3 us (20%)
  between operations  14.2 us (9%)
  local copies, waits for them, and re-layouts  13.7 us (8%)
  Pallas kernels  11.3 us (7%)
  starting transfers between devices  10.6 us (7%)
    all_to_all x5, blocking collectives, exchange(): return lax.all_to_all(values, axes, split_axis=0, concat_axis=0, tiled=True)  65.2 us
    all_to_all x3, waiting for transfers between devices, exchange(): return lax.all_to_all(values, axes, split_axis=0, concat_axis=0, tiled=True)  32.2 us
    all_to_all x3, starting transfers between devices, exchange(): return lax.all_to_all(values, axes, split_axis=0, concat_axis=0, tiled=True)  10.6 us
    unnamed x22, local copies, waits for them, and re-layouts  7.23 us
    all_gather x1, blocking collectives, body(): hidden = lax.all_gather(hidden, 'gx', axis=0)  6.94 us
    pallas_call x8, Pallas kernels, stage(): pl.pallas_call(kernel, out_shape=[jax.ShapeDtypeStruct(s, d) for s, d in...  5.86 us
    all_gather x1, blocking collectives, body(): g = lax.all_gather(shares, 'gx', axis=0)  5.79 us
    pallas_call x1, Pallas kernels, attention(): pl.pallas_call(attention_kernel, grid=(KV_HEADS,), in_specs=[smem, smem,...  5.48 us
  transfers between devices with their start and end apart: 4, of which 3 were waited for; matrix products, arithmetic and copies ran while one was open for 2% of the time, Pallas kernels for 1%

profile of v1, /device:TPU:0, one launch (start us, length us, event | category | flops | bytes accessed | tf_op | source)
XLA Modules:
  0.0 160.9 jit_solution(16756229041295941013)
XLA Ops:
  6.5 0.7 fusion
  7.2 0.8 broadcast_in_dim.12
  8.1 1.2 copy.25
  9.3 3.3 %concatenate.6 = bf16[304,576]{1,0:T(8,128)(2,1)} concatenate(bf16[256,576]{1,0:T(8,128)(2,1)S(1)} %copy.25, bf16[32,576]{1,0:T(8,128)(2,1)S(1)} %broadcast_in_dim.12, bf16[4,576]{1,0:T(4,128)(2,1)S(1)} %get-tuple-element.11, bf16[4,576]{1,0:T(4,128)(2,1)S(1)} %get-tuple-element.10, bf16[4,576]{1,0:T(4,128)(2,1)S(1)} %get-tuple-element.9, bf16[4,576]{1,0:T(4,128)(2,1)S(1)} %broadcast_in_dim.14), dimensions={0} | concatenate | bytes 700416 | tf_op jit(solution)/shard_map/concatenate | solution.py:211
  12.7 18.0 %all_to_all.40.refs_0_ = bf16[8,32,576]{2,1,0:T(8,128)(2,1)S(1)} all-to-all(bf16[8,32,576]{2,1,0:T(8,128)(2,1)S(1)} %broadcast_in_dim.13), channel_id=1, replica_groups=mesh['gx'=4,'gy'=8] {'gy'}, dimensions={0} | all-to-all | bytes 589824 | tf_op jit(solution)/shard_map/all_to_all | solution.py:43
  30.7 1.1 project.1
  31.8 3.0 %all-to-all-start.1 = ((bf16[32,32,128]{2,1,0:T(8,128)(2,1)}), bf16[32,32,128]{2,1,0:T(8,128)(2,1)S(1)}, u32[]{:S(2)}, u32[]{:S(2)}) async-start(bf16[32,32,128]{2,1,0:T(8,128)(2,1)} %bitcast), calls=%async_computation.1 | async-start | bytes 524288 | tf_op jit(solution)/shard_map/all_to_all | solution.py:43
  35.5 0.1 multiply_sine_fusion
  35.7 9.8 %all-to-all-done.1 = bf16[32,32,128]{2,1,0:T(8,128)(2,1)S(1)} async-done(((bf16[32,32,128]{2,1,0:T(8,128)(2,1)}), bf16[32,32,128]{2,1,0:T(8,128)(2,1)S(1)}, u32[]{:S(2)}, u32[]{:S(2)}) %all-to-all-start.1) | async-done | bytes 262176 | tf_op jit(solution)/shard_map/all_to_all | solution.py:43
  45.5 5.8 %all-gather = bf16[32,32,128]{2,1,0:T(8,128)(2,1)S(1)} all-gather(bf16[8,32,128]{2,1,0:T(8,128)(2,1)S(1)} %sum_shares.1), channel_id=2, replica_groups=mesh['gx'=4,'gy'=8] {'gx'}, dimensions={0}, use_global_device_ids=true | all-gather | bytes 327680 | tf_op jit(solution)/shard_map/all_gather | solution.py:243
  51.3 1.4 copy-done
  52.7 2.5 %copy-done.1 = bf16[2,10,128,1024]{3,2,1,0:T(8,128)(2,1)S(1)} copy-done((bf16[2,10,128,1024]{3,2,1,0:T(8,128)(2,1)S(1)}, bf16[2,10,128,1024]{3,2,1,0:T(8,128)(2,1)}, u32[]{:S(2)}) %copy-start.1) | copy-done | bytes 5242904
  55.2 5.5 %attention.1 = bf16[4,8,8,384]{3,2,1,0:T(8,128)(2,1)S(1)} custom-call(s32[1,33]{1,0:T(1,128)S(1)} %copy-done.9, s32[1]{0:T(128)} %copy.27.length_ref, s32[3,8]{1,0:T(4,128)S(1)} %copy-done.8, bf16[4,8,32,128]{3,2,1,0:T(8,128)(2,1)S(1)} %bitcast.21, bf16[4,304,576]{2,1,0:T(8,128)(2,1)S(1)} %bitcast.15, f32[32,128]{1,0:T(8,128)S(1)} %get-tuple-element.13.cos_ref, ...), custom_call_target="tpu_custom_call" | custom-call | tf_op jit(solution)/shard_map/attention/pallas_call | solution.py:153
  60.7 10.7 %all_to_all.41 = bf16[32,8,384]{2,1,0:T(8,128)(2,1)S(1)} all-to-all(bf16[32,8,384]{2,1,0:T(8,128)(2,1)S(1)} %bitcast.23), channel_id=1, replica_groups=mesh['gx'=4,'gy'=8] {'gx','gy'}, dimensions={0} | all-to-all | bytes 393216 | tf_op jit(solution)/shard_map/all_to_all | solution.py:43
  71.4 1.2 project_out.1
  72.6 4.0 %all-to-all-start.3 = ((bf16[8,4,8,576]{3,2,1,0:T(8,128)(2,1)}), bf16[8,4,8,576]{3,2,1,0:T(8,128)(2,1)S(1)}, u32[]{:S(2)}, u32[]{:S(2)}) async-start(bf16[8,4,8,576]{3,2,1,0:T(8,128)(2,1)} %project_out.1), calls=%async_computation.3 | async-start | bytes 655360 | tf_op jit(solution)/shard_map/all_to_all | solution.py:43
  76.6 0.9 slice.4.refs_2_
  77.5 0.8 constant_dynamic-slice_fusion.refs_1_
  78.3 8.7 %all-to-all-done.3.refs_0_ = bf16[8,4,8,576]{3,2,1,0:T(8,128)(2,1)S(1)} async-done(((bf16[8,4,8,576]{3,2,1,0:T(8,128)(2,1)}), bf16[8,4,8,576]{3,2,1,0:T(8,128)(2,1)S(1)}, u32[]{:S(2)}, u32[]{:S(2)}) %all-to-all-start.3) | async-done | bytes 294944 | tf_op jit(solution)/shard_map/all_to_all | solution.py:43
  87.0 0.3 mix.1
  87.3 15.6 %all_to_all.42 = bf16[32,8,576]{2,1,0:T(8,128)(2,1)S(1)} all-to-all(bf16[32,8,576]{2,1,0:T(8,128)(2,1)S(1)} %bitcast.25), channel_id=1, replica_groups=mesh['gx'=4,'gy'=8] {'gx','gy'}, dimensions={0} | all-to-all | bytes 589824 | tf_op jit(solution)/shard_map/all_to_all | solution.py:43
  102.8 2.2 %gate_up.1 = bf16[4,64,2304]{2,1,0:T(8,128)(2,1)} custom-call(bf16[4,8,8,576]{3,2,1,0:T(8,128)(2,1)S(1)} %bitcast.18, bf16[576,1152]{1,0:T(8,128)(2,1)S(1)} %copy-done.2, bf16[576,1152]{1,0:T(8,128)(2,1)S(1)} %copy-done.3), custom_call_target="tpu_custom_call" | custom-call | tf_op jit(solution)/shard_map/gate_up/pallas_call | solution.py:34
  105.0 3.5 %all-to-all-start.5 = ((bf16[4,64,2304]{2,1,0:T(8,128)(2,1)}), bf16[4,64,2304]{2,1,0:T(8,128)(2,1)S(1)}, u32[]{:S(2)}, u32[]{:S(2)}) async-start(bf16[4,64,2304]{2,1,0:T(8,128)(2,1)} %gate_up.1), calls=%async_computation.5 | async-start | bytes 2359296 | tf_op jit(solution)/shard_map/all_to_all | solution.py:43
  108.6 2.1 %copy.26.refs_1_ = bf16[1152,576]{1,0:T(8,128)(2,1)S(1)} copy(bf16[1152,576]{0,1:T(8,128)(2,1)} %param.25) | data formatting | bytes 2654208 | tf_op args[12]
  110.7 13.7 %all-to-all-done.5.refs_0_ = bf16[4,64,2304]{2,1,0:T(8,128)(2,1)S(1)} async-done(((bf16[4,64,2304]{2,1,0:T(8,128)(2,1)}), bf16[4,64,2304]{2,1,0:T(8,128)(2,1)S(1)}, u32[]{:S(2)}, u32[]{:S(2)}) %all-to-all-start.5) | async-done | bytes 1179680 | tf_op jit(solution)/shard_map/all_to_all | solution.py:43
  124.4 0.2 activate.1
  124.6 6.9 %all-gather.2 = bf16[256,1152]{1,0:T(8,128)(2,1)S(1)} all-gather(bf16[64,1152]{1,0:T(8,128)(2,1)S(1)} %activate.1), channel_id=4, replica_groups=mesh['gx'=4,'gy'=8] {'gx'}, dimensions={0}, use_global_device_ids=true | all-gather | bytes 737280 | tf_op jit(solution)/shard_map/all_gather | solution.py:348
  131.6 0.7 project_down.1
  132.2 14.7 %all_to_all.43 = bf16[32,8,576]{2,1,0:T(8,128)(2,1)S(1)} all-to-all(bf16[32,8,576]{2,1,0:T(8,128)(2,1)S(1)} %bitcast.19), channel_id=1, replica_groups=mesh['gx'=4,'gy'=8] {'gx','gy'}, dimensions={0} | all-to-all | bytes 589824 | tf_op jit(solution)/shard_map/all_to_all | solution.py:43
  146.9 0.2 finish.1
  147.1 6.3 %all_to_all.44 = bf16[4,8,576]{2,1,0:T(8,128)(2,1)S(1)} all-to-all(bf16[4,8,576]{2,1,0:T(8,128)(2,1)S(1)} %finish.1), channel_id=1, replica_groups=mesh['gx'=4,'gy'=8] {'gx'}, dimensions={0} | all-to-all | bytes 73728 | tf_op jit(solution)/shard_map/all_to_all | solution.py:43
  153.4 0.6 reshape.55
  (26 shorter events, 0.2 us)
Async XLA Ops:
  6.5 44.8 %all-gather.5.cloned.1.call-start = ((), (), s32[]{:S(2)}) async-start(), calls=%async_computation.8 | async-start | bytes 1945600 | tf_op jit(solution)/shard_map/all_gather | solution.py:211
  8.1 22.6 %copy-start.4 = (bf16[576,256]{1,0:T(8,128)(2,1)S(1)}, bf16[576,256]{1,0:T(8,128)(2,1)}, u32[]{:S(2)}) copy-start(bf16[576,256]{1,0:T(8,128)(2,1)} %refs_2_.2) | copy-start | bytes 884740
  8.1 22.6 %copy-start.5 = (bf16[576,128]{1,0:T(8,128)(2,1)S(1)}, bf16[576,128]{1,0:T(8,128)(2,1)}, u32[]{:S(2)}) copy-start(bf16[576,128]{1,0:T(8,128)(2,1)} %refs_3_.1) | copy-start | bytes 442372
  8.1 22.6 %copy-start.6 = (bf16[576,128]{1,0:T(8,128)(2,1)S(1)}, bf16[576,128]{1,0:T(8,128)(2,1)}, u32[]{:S(2)}) copy-start(bf16[576,128]{1,0:T(8,128)(2,1)} %refs_4_.1) | copy-start | bytes 442372
  8.1 22.6 %copy-start.7 = (f32[4,576]{1,0:T(4,128)S(1)}, f32[4,576]{1,0:T(4,128)}, u32[]{:S(2)}) copy-start(f32[4,576]{1,0:T(4,128)} %refs_1_.3) | copy-start | bytes 27652
  30.7 20.7 %copy-start.8 = (s32[3,8]{1,0:T(4,128)S(1)}, s32[3,8]{1,0:T(4,128)}, u32[]{:S(2)}) copy-start(s32[3,8]{1,0:T(4,128)} %parents_ref.1) | copy-start | bytes 292
  30.7 20.7 %copy-start.9 = (s32[1,33]{1,0:T(1,128)S(1)}, s32[1,33]{1,0:T(1,128)}, u32[]{:S(2)}) copy-start(s32[1,33]{1,0:T(1,128)} %table_ref.1) | copy-start | bytes 400
  31.8 13.7 %all-to-all-start.1 = ((bf16[32,32,128]{2,1,0:T(8,128)(2,1)}), bf16[32,32,128]{2,1,0:T(8,128)(2,1)S(1)}, u32[]{:S(2)}, u32[]{:S(2)}) async-start(bf16[32,32,128]{2,1,0:T(8,128)(2,1)} %bitcast), calls=%async_computation.1 | async-start | bytes 524288 | tf_op jit(solution)/shard_map/all_to_all | solution.py:43
  51.3 1.4 copy-start
  52.7 2.5 %copy-start.1 = (bf16[2,10,128,1024]{3,2,1,0:T(8,128)(2,1)S(1)}, bf16[2,10,128,1024]{3,2,1,0:T(8,128)(2,1)}, u32[]{:S(2)}) copy-start(bf16[2,10,128,1024]{3,2,1,0:T(8,128)(2,1)} %pool_ref.1) | copy-start | bytes 15728644
  71.4 31.4 %copy-start.3 = (bf16[576,1152]{1,0:T(8,128)(2,1)S(1)}, bf16[576,1152]{1,0:T(8,128)(2,1)}, u32[]{:S(2)}) copy-start(bf16[576,1152]{1,0:T(8,128)(2,1)} %refs_2_.3) | copy-start | bytes 3981316
  72.6 30.2 %copy-start.2 = (bf16[576,1152]{1,0:T(8,128)(2,1)S(1)}, bf16[576,1152]{1,0:T(8,128)(2,1)}, u32[]{:S(2)}) copy-start(bf16[576,1152]{1,0:T(8,128)(2,1)} %refs_1_.4) | copy-start | bytes 3981316
  72.6 14.4 %all-to-all-start.3 = ((bf16[8,4,8,576]{3,2,1,0:T(8,128)(2,1)}), bf16[8,4,8,576]{3,2,1,0:T(8,128)(2,1)S(1)}, u32[]{:S(2)}, u32[]{:S(2)}) async-start(bf16[8,4,8,576]{3,2,1,0:T(8,128)(2,1)} %project_out.1), calls=%async_computation.3 | async-start | bytes 655360 | tf_op jit(solution)/shard_map/all_to_all | solution.py:43
  105.0 19.4 %all-to-all-start.5 = ((bf16[4,64,2304]{2,1,0:T(8,128)(2,1)}), bf16[4,64,2304]{2,1,0:T(8,128)(2,1)S(1)}, u32[]{:S(2)}, u32[]{:S(2)}) async-start(bf16[4,64,2304]{2,1,0:T(8,128)(2,1)} %gate_up.1), calls=%async_computation.5 | async-start | bytes 2359296 | tf_op jit(solution)/shard_map/all_to_all | solution.py:43
Sparse Core Ops, SparseCore 0:
  12.8 22.2 all-gather.4

commit v2 on v1

--- a/solution.py
+++ b/solution.py
@@ -22,7 +22,7 @@
 GAIN_ROWS = 16
 
 
-def stage(fast, name, f, outs, *args, limit=16):
+def stage(fast, name, f, outs, *args, limit=16, specs=None):
     if not fast:
         return f(*args)
 
@@ -31,11 +31,21 @@
         for ref, result in zip(refs[len(args) :], results):
             ref[...] = result.astype(ref.dtype)
 
+    return run(kernel, name, outs, args, limit, specs)
+
+
+def run(kernel, name, outs, args, limit=16, specs=None, scratch=()):
+    more = {}
+    if specs is not None:
+        whole = pl.BlockSpec(memory_space=pltpu.VMEM)
+        more = {"in_specs": [whole if s is None else s for s in specs], "grid": (1,)}
     return pl.pallas_call(
         kernel,
         out_shape=[jax.ShapeDtypeStruct(s, d) for s, d in outs],
+        scratch_shapes=scratch,
         compiler_params=pltpu.CompilerParams(vmem_limit_bytes=limit * MIB),
         name=name,
+        **more,
     )(*args)
 
 
@@ -54,7 +64,16 @@
 
 
 def attention_kernel(
-    table_ref, length_ref, parents_ref, g_ref, x_ref, cos_ref, sin_ref, pool_ref, out_ref, page_ref
+    table_ref,
+    length_ref,
+    parents_ref,
+    g_ref,
+    square_ref,
+    cos_ref,
+    sin_ref,
+    pool_ref,
+    out_ref,
+    page_ref,
 ):
     parts, reps, part_rows = out_ref.shape[:3]
     rows = parts * part_rows
@@ -63,8 +82,8 @@
     first_owner = lax.axis_index("gx") * slots
     length = length_ref[0]
     first_page = jnp.maximum(length - WINDOW + 1, 0) // PAGE
-    x = x_ref[...].astype(F32)
-    square = jnp.sum(jnp.sum(x * x, axis=0), axis=-1, keepdims=True)
+    square = jnp.sum(square_ref[:, 0].astype(F32), axis=0)
+    square = square[:, 0:1] + square[:, HALF // 2 : HALF // 2 + 1]
     scale = lax.rsqrt(square / D + EPSILON)
     cos, sin = cos_ref[...], sin_ref[...]
 
@@ -134,9 +153,7 @@
     den = den + jnp.sum(weights, axis=-1, keepdims=True)
     num = num + jnp.dot(weights.astype(BF), value_step, preferred_element_type=F32)
 
-    high = den.astype(BF).astype(F32)
-    wide = lax.broadcasted_iota(jnp.int32, (reps * rows, PAGE), 1)
-    den_lanes = jnp.where(wide < PAGE // 2, high, den - high)
+    den_lanes = high_low(den, PAGE)
     for part in range(parts):
         for rep in range(reps):
             here = slice(rep * rows + part * part_rows, rep * rows + (part + 1) * part_rows)
@@ -144,10 +161,9 @@
             out_ref[part, rep, :, HEAD_DIM:] = den_lanes[here].astype(BF)
 
 
-def attention(parts, table, lengths, parents, g, wide, x_block, cos, sin, pool):
+def attention(parts, table, lengths, parents, g, cos, sin, pool):
     rows = g.shape[2]
     reps = HEADS // KV_HEADS
-    nx, _, width = wide.shape
     slots = pool.shape[1]
     smem = pl.BlockSpec(memory_space=pltpu.SMEM)
     return pl.pallas_call(
@@ -158,7 +174,7 @@
             smem,
             smem,
             pl.BlockSpec((4, 2, rows, HALF), lambda h: (0, h, 0, 0)),
-            pl.BlockSpec((nx, rows, width), lambda h: (0, x_block, 0)),
+            pl.BlockSpec((4, 1, rows, HALF), lambda h: (0, 2 * KV_HEADS, 0, 0)),
             pl.BlockSpec((rows, HALF), lambda h: (0, 0)),
             pl.BlockSpec((rows, HALF), lambda h: (0, 0)),
             pl.BlockSpec((2, slots, PAGE, HEAD_DIM), lambda h: (0, 0, 0, h)),
@@ -168,9 +184,27 @@
         ),
         out_shape=jax.ShapeDtypeStruct((parts, HEADS, rows // parts, HEAD_DIM + PAGE), BF),
         scratch_shapes=[pltpu.SMEM((slots,), jnp.int32)],
-        compiler_params=pltpu.CompilerParams(vmem_limit_bytes=24 * MIB),
+        compiler_params=pltpu.CompilerParams(vmem_limit_bytes=60 * MIB),
         name="attention",
-    )(table, lengths, parents, g, wide, cos, sin, pool)
+    )(table, lengths, parents, g, g, cos, sin, pool)
+
+
+def rounded(v):
+    return lax.reduce_precision(v, 8, 7)
+
+
+def high_low(column, lanes):
+    shape = (column.shape[0], lanes)
+    high = column.astype(BF).astype(F32)
+    lane = lax.broadcasted_iota(jnp.int32, shape, 1)
+    return jnp.where(lane < lanes // 2, high, column - high)
+
+
+def partner_send(blocks):
+    count = len(blocks)
+    return [blocks[0]] + [
+        lax.ppermute(blocks[m], "gx", [(i, i ^ m) for i in range(count)]) for m in range(1, count)
+    ]
 
 
 def body(
@@ -199,17 +233,7 @@
     share = columns // nx
     fast = part % 8 == 0 and share == HALF and head_part == HEAD_DIM and query_part == 2 * share
     x_own = inputs.reshape(rows, width)
-
-    def rounded(v):
-        return lax.reduce_precision(v, 8, 7)
-
-    gain_high = rounded(norm_gains)
-    gain_mid = rounded(norm_gains - gain_high)
-    gain_low = norm_gains - gain_high - gain_mid
-    gain_pad = jnp.zeros((GAIN_ROWS - 12, width), F32)
-    gain_block = jnp.concatenate([gain_high, gain_mid, gain_low, gain_pad], axis=0).astype(BF)
-    wide = lax.all_gather(jnp.concatenate([w_out, x_own, gain_block], axis=0), "gx", axis=0)
-
+    me = lax.axis_index("gx")
     x_all = exchange(jnp.broadcast_to(x_own[None], (ny, rows, width)), "gy")
 
     def project(x, gains, wq, wk, wv):
@@ -233,22 +257,90 @@
         w_value,
     )
     received = exchange_all(send)
-    (shares,) = stage(
-        fast,
-        "sum_shares",
-        lambda v: [jnp.sum(v.astype(F32), axis=0).astype(BF)],
-        [((ny, rows, share), BF)],
-        received,
-    )
-    g = lax.all_gather(shares, "gx", axis=0)
-    if not fast:
-        every = g.transpose(2, 1, 0, 3).reshape(rows, ny, columns)
+
+    x_late, _ = lax.optimization_barrier((x_own, x_all))
+    chunks = [(c, min(c + head_part, width)) for c in range(0, width, head_part)]
+    if fast:
+        side_rows = len(chunks) * (rows + GAIN_ROWS)
+
+        def prepare(w_ref, x_ref, gain_ref, out_ref):
+            out_ref[0:width] = w_ref[...]
+            x = x_ref[...]
+            gains = gain_ref[...]
+            high = gains.astype(BF).astype(F32)
+            mid = (gains - high).astype(BF).astype(F32)
+            row = lax.broadcasted_iota(jnp.int32, gains.shape, 0)
+            split = jnp.where(row < 4, high, jnp.where(row < 8, mid, gains - high - mid))
+            split = jnp.where(row < 12, split, 0.0).astype(BF)
+            out_ref[width:] = jnp.zeros((side_rows, head_part), BF)
+            for n, (start, end) in enumerate(chunks):
+                at = width + n * rows
+                out_ref[at : at + rows, 0 : end - start] = x[:, start:end]
+                at = width + len(chunks) * rows + n * GAIN_ROWS
+                out_ref[at : at + GAIN_ROWS, 0 : end - start] = split[:, start:end]
+
+        (side,) = run(
+            prepare,
+            "prepare",
+            [((width + side_rows, head_part), BF)],
+            (w_out.T, x_late, jnp.tile(norm_gains, (GAIN_ROWS // 4, 1))),
+        )
+        side = lax.all_gather(side, "gx", axis=0)
+        out_spec = pl.BlockSpec((nx, width, head_part), lambda i: (0, 0, 0))
+        side_spec = pl.BlockSpec((nx, side_rows, head_part), lambda i: (0, width // side_rows, 0))
+        w_wide, x_and_gains = side, side
+    else:
+        w_wide = lax.all_gather(w_out.T, "gx", axis=0)
+        x_and_gains = (lax.all_gather(x_late, "gx", axis=0), lax.all_gather(norm_gains, "gx"))
+        out_spec = side_spec = None
+
+    def rows_and_gain(values, index=None):
+        if not fast:
+            if index is not None:
+                return 1.0 + values[1][:, index : index + 1]
+            return lax.dynamic_slice_in_dim(values[0], me * part, part, 1).astype(F32)
+        values = values.astype(F32)
+        pieces = []
+        for n, (start, end) in enumerate(chunks):
+            if index is None:
+                at = n * rows
+                mine = lax.axis_index("gx")
+                piece = sum(
+                    jnp.where(mine == p, values[:, at + p * part : at + (p + 1) * part], 0.0)
+                    for p in range(nx)
+                )
+            else:
+                at = len(chunks) * rows + n * GAIN_ROWS + index
+                high, mid, low = (values[:, at + 4 * t : at + 4 * t + 1] for t in range(3))
+                piece = 1.0 + (high + (mid + low))
+            pieces.append(piece[..., : end - start])
+        return jnp.concatenate(pieces, axis=-1)
+
+    def sum_shares(parts, x):
+        x = x.astype(F32)
+        squares = high_low(jnp.sum(x * x, axis=-1, keepdims=True), HALF)
+        return [jnp.concatenate([jnp.sum(parts.astype(F32), axis=0), squares[None]], axis=0)]
+
+    if fast:
+        (shares,) = stage(
+            fast, "sum_shares", sum_shares, [((ny + 1, rows, share), BF)], received, x_own
+        )
+        g = lax.all_gather(shares, "gx", axis=0)
+    else:
+        shares = jnp.sum(received.astype(F32), axis=0).astype(BF)
+        every = lax.all_gather(shares, "gx", axis=0)
+        every = every.transpose(2, 1, 0, 3).reshape(rows, ny, columns)
         q = every[..., :query_part].reshape(rows, HEADS, 2, HALF).transpose(2, 1, 0, 3)
         k, v = (
             every[..., start : start + key_part].reshape(rows, 2 * KV_HEADS, HALF).transpose(1, 0, 2)
             for start in (query_part, query_part + key_part)
         )
         g = jnp.concatenate([q, k[None], v[None]], axis=0)
+        square = lax.psum(jnp.sum(jnp.square(x_own.astype(F32)), axis=-1, keepdims=True), "gx")
+        lane = jnp.arange(HALF)
+        square = jnp.where(lane < HALF // 2, rounded(square), square - rounded(square)).astype(BF)
+        square = jnp.concatenate([square[None], jnp.zeros((3, rows, HALF), BF)], axis=0)
+        g = jnp.concatenate([g, square[:, None]], axis=1)
 
     positions = lengths[0] + jnp.arange(rows, dtype=jnp.int32) % steps
     inverse_freq = ROPE_BASE ** (-jnp.arange(HALF, dtype=F32) * 2.0 / HEAD_DIM)
@@ -259,8 +351,6 @@
         lengths,
         parents,
         g,
-        wide,
-        head_part // rows,
         jnp.cos(angles),
         jnp.sin(angles),
         cache_pool,
@@ -273,97 +363,124 @@
         terms = jnp.concatenate([num, den], axis=-1).transpose(0, 2, 1, 3)
     terms = exchange_all(terms)
 
-    def project_out(t, w_wide):
+    contract_last = (((1,), (1,)), ((), ()))
+
+    def project_out(t, w):
         t = jnp.sum(t.astype(F32), axis=0)
         den = t[..., head_part : head_part + 1] + t[..., -1:]
         attended = (t[..., :head_part] / den).reshape(ny * part, head_part).astype(BF)
-        return [
-            jnp.stack(
-                [
-                    jnp.dot(attended, w_wide[k, :head_part], preferred_element_type=F32).reshape(
-                        ny, part, width
-                    )
-                    for k in range(nx)
-                ],
-                axis=1,
-            ).astype(BF)
+        slices = [
+            lax.dot_general(attended, w[k], contract_last, preferred_element_type=F32)
+            for k in range(nx)
         ]
+        return [jnp.stack([v.reshape(ny, part, width) for v in slices], axis=1).astype(BF)]
 
     (attn_parts,) = stage(
-        fast, "project_out", project_out, [((ny, nx, part, width), BF)], terms, wide
+        fast,
+        "project_out",
+        project_out,
+        [((ny, nx, part, width), BF)],
+        terms,
+        w_wide,
+        specs=(None, out_spec),
     )
     attn_parts = exchange(attn_parts, "gy")
-    x_rows = lax.dynamic_slice_in_dim(wide, head_part + lax.axis_index("gx") * part, part, 1)
-    gains_wide = wide[:, head_part + rows :]
-
-    def gain_of(gains, index):
-        gains = gains.astype(F32)
-        high, mid, low = (gains[:, 4 * t + index : 4 * t + index + 1] for t in range(3))
-        return 1.0 + (high + (mid + low))
 
     def row_scale(v):
         square = jnp.sum(jnp.sum(v * v, axis=0), axis=-1, keepdims=True)
         return lax.rsqrt(square / D + EPSILON)[None]
 
-    def mix(parts, x, gains):
+    def mix(parts, others):
         attn = jnp.sum(parts.astype(F32), axis=0)
-        mixed = x.astype(F32) + attn * row_scale(attn) * gain_of(gains, 1)
-        ff_input = (mixed * row_scale(mixed) * gain_of(gains, 2)).astype(BF)
-        return [mixed, jnp.broadcast_to(ff_input[:, None], (nx, ny, part, width))]
-
-    mixed, ff_input = stage(
+        mixed = rows_and_gain(others) + attn * row_scale(attn) * rows_and_gain(others, 1)
+        ff_input = mixed * row_scale(mixed) * rows_and_gain(others, 2)
+        ff_input = jnp.broadcast_to(ff_input[:, None], (nx, ny, part, width))
+        last_gain = jnp.broadcast_to(rows_and_gain(others, 3), (nx, 8, width))
+        return [mixed, last_gain, ff_input.astype(BF)]
+
+    mixed, last_gain, ff_input = stage(
         fast,
         "mix",
         mix,
-        [((nx, part, width), F32), ((nx, ny, part, width), BF)],
+        [((nx, part, width), F32), ((nx, 8, width), F32), ((nx, ny, part, width), BF)],
         attn_parts,
-        x_rows,
-        gains_wide,
+        x_and_gains,
+        specs=(None, side_spec),
     )
     ff_input = exchange_all(ff_input)
 
-    def gate_up(ff, wg, wu):
-        flat = ff.astype(F32).reshape(nx * ny * part, width).astype(BF)
-        both = [jnp.dot(flat, w, preferred_element_type=F32).astype(BF) for w in (wg, wu)]
-        return [jnp.concatenate(both, axis=1).reshape(nx, ny * part, 2 * hidden_part)]
-
-    (both,) = stage(
-        fast,
-        "gate_up",
-        gate_up,
-        [((nx, ny * part, 2 * hidden_part), BF)],
-        ff_input,
-        w_gate,
-        w_up,
-        limit=24,
-    )
-    both = exchange(both, "gx")
-
-    def activate(v):
-        v = jnp.sum(v.astype(F32), axis=0)
-        gate, up = v[:, :hidden_part], v[:, hidden_part:]
+    block_shape = (ny * part, 2 * hidden_part)
+    if fast:
+
+        def gate_up(ff_ref, gate_ref, up_ref, *out_refs):
+            mine = lax.axis_index("gx")
+            blocks = [ff_ref[mine ^ m].astype(F32).reshape(ny * part, width) for m in range(nx)]
+            flat = jnp.concatenate(blocks, axis=0).astype(BF)
+            for n, w_ref in enumerate((gate_ref, up_ref)):
+                sums = jnp.dot(flat, w_ref[...], preferred_element_type=F32).astype(BF)
+                for m, out_ref in enumerate(out_refs):
+                    out_ref[:, n * hidden_part : (n + 1) * hidden_part] = sums[
+                        m * ny * part : (m + 1) * ny * part
+                    ]
+
+        blocks = run(
+            gate_up, "gate_up", [(block_shape, BF)] * nx, (ff_input, w_gate, w_up), limit=24
+        )
+    else:
+        flat = ff_input.reshape(-1, width)
+        both = [jnp.dot(flat, w, preferred_element_type=F32).astype(BF) for w in (w_gate, w_up)]
+        both = jnp.concatenate(both, axis=1).reshape((nx,) + block_shape)
+        blocks = [lax.dynamic_index_in_dim(both, me ^ m, 0, False) for m in range(nx)]
+    blocks = partner_send(blocks)
+
+    def activate(*parts):
+        total = sum(v.astype(F32) for v in parts)
+        gate, up = total[:, :hidden_part], total[:, hidden_part:]
         return [(jax.nn.gelu(gate, approximate=True) * up).astype(BF)]
 
-    (hidden,) = stage(fast, "activate", activate, [((ny * part, hidden_part), BF)], both)
+    (hidden,) = stage(fast, "activate", activate, [((ny * part, hidden_part), BF)], *blocks)
     hidden = lax.all_gather(hidden, "gx", axis=0)
 
     def project_down(h, w):
-        down = jnp.dot(
-            h.reshape(nx * ny * part, hidden_part), w, preferred_element_type=F32
+        flat = h.reshape(nx * ny * part, hidden_part)
+        down = lax.dot_general(flat, w, contract_last, preferred_element_type=F32)
+        return [down.reshape(nx, ny, part, width).astype(BF)]
+
+    (down,) = stage(
+        fast, "project_down", project_down, [((nx, ny, part, width), BF)], hidden, w_down.T
+    )
+    down = exchange_all(down)
+
+    def finish(parts, mixed_rows, gain):
+        total = jnp.sum(parts.astype(F32), axis=1)
+        return mixed_rows + total * row_scale(total) * gain[:, 0:1]
+
+    if fast:
+
+        def finish_kernel(parts_ref, mixed_ref, gain_ref, *refs):
+            mine = lax.axis_index("gx")
+            whole_ref = refs[-1]
+            whole_ref[...] = finish(parts_ref[...], mixed_ref[...], gain_ref[...])
+            for m in range(nx):
+                refs[m][...] = whole_ref[mine ^ m].astype(BF)
+
+        blocks = run(
+            finish_kernel,
+            "finish",
+            [((part, width), BF)] * nx,
+            (down, mixed, last_gain),
+            scratch=[pltpu.VMEM((nx, part, width), F32)],
         )
-        return [down.reshape(nx, ny, part, width).astype(BF)]
-
-    (down,) = stage(
-        fast, "project_down", project_down, [((nx, ny, part, width), BF)], hidden, w_down
-    )
-    down = exchange_all(down)
-
-    def finish(parts, mixed_rows, gains):
-        total = jnp.sum(parts.astype(F32), axis=1)
-        return [(mixed_rows + total * row_scale(total) * gain_of(gains, 3)).astype(BF)]
-
-    (out,) = stage(fast, "finish", finish, [((nx, part, width), BF)], down, mixed, gains_wide)
-    return exchange(out, "gx").reshape(beams, steps, width)
+
+        def gather_rows(*refs):
+            mine = lax.axis_index("gx")
+            for m in range(nx):
+                refs[-1][mine ^ m] = refs[m][...]
+
+        (out,) = run(gather_rows, "gather_rows", [((nx, part, width), BF)], partner_send(blocks))
+    else:
+        out = exchange(finish(down, mixed, last_gain).astype(BF), "gx")
+    return out.reshape(beams, steps, width)
 
 
 def solution(mesh):

time: 162 us -> 151 us (0.932)
  local copies, waits for them, and re-layouts: 13.7 us -> 4.42 us
  blocking collectives: 78 us -> 69.7 us
  starting transfers between devices: 10.6 us -> 14.8 us
  waiting for transfers between devices: 32.3 us -> 34.3 us
    ppermute x0 -> x6, waiting for transfers between devices: none -> 15.5 us  [partner_send(): lax.ppermute(blocks[m], 'gx', [(i, i ^ m) for i in range(count)])]
    all_to_all x3 -> x2, waiting for transfers between devices: 32.2 us -> 18.8 us  [exchange(): return lax.all_to_all(values, axes, split_axis=0, concat_axis=0, tiled=True)]
    all_to_all x5 -> x4, blocking collectives: 65.2 us -> 55.8 us  [exchange(): return lax.all_to_all(values, axes, split_axis=0, concat_axis=0, tiled=True)]
    unnamed x22 -> x20, local copies, waits for them, and re-layouts: 7.23 us -> 1.41 us
    ppermute x0 -> x6, starting transfers between devices: none -> 3.87 us  [partner_send(): lax.ppermute(blocks[m], 'gx', [(i, i ^ m) for i in range(count)])]
    concatenate x1 -> x0, local copies, waits for them, and re-layouts: 3.29 us -> none  [body(): jnp.concatenate([w_out, x_own, gain_block], axis=0)]
    pallas_call x8 -> x10, Pallas kernels: 5.86 us -> 5.1 us  [run(): pl.pallas_call(kernel, out_shape=[jax.ShapeDtypeStruct(s, d) for s, d in...]
    all_to_all x3 -> x2, starting transfers between devices: 10.6 us -> 10.9 us  [exchange(): return lax.all_to_all(values, axes, split_axis=0, concat_axis=0, tiled=True)]
  transfers between devices with their start and end apart: 4 -> 9, of which waited for: 3 -> 6; matrix products, arithmetic and copies ran while one was open for 2% -> 1% of each run, Pallas kernels for 1% -> 5%
where the time goes in v2:
time: 151 us; the launch traced here: 150 us
  blocking collectives  69.7 us (46%)
  waiting for transfers between devices  34.3 us (23%)
  starting transfers between devices  14.8 us (10%)
  between operations  14.2 us (9%)
  Pallas kernels  11.9 us (8%)
  local copies, waits for them, and re-layouts  4.42 us (3%)
    all_to_all x4, blocking collectives, exchange(): return lax.all_to_all(values, axes, split_axis=0, concat_axis=0, tiled=True)  55.8 us
    all_to_all x2, waiting for transfers between devices, exchange(): return lax.all_to_all(values, axes, split_axis=0, concat_axis=0, tiled=True)  18.8 us
    ppermute x6, waiting for transfers between devices, partner_send(): lax.ppermute(blocks[m], 'gx', [(i, i ^ m) for i in range(count)])  15.5 us
    all_to_all x2, starting transfers between devices, exchange(): return lax.all_to_all(values, axes, split_axis=0, concat_axis=0, tiled=True)  10.9 us
    all_gather x1, blocking collectives, body(): hidden = lax.all_gather(hidden, 'gx', axis=0)  7.58 us
    pallas_call x1, Pallas kernels, attention(): pl.pallas_call(attention_kernel, grid=(KV_HEADS,), in_specs=[smem, smem,...  6.79 us
    all_gather x1, blocking collectives, body(): g = lax.all_gather(shares, 'gx', axis=0)  6.31 us
    pallas_call x10, Pallas kernels, run(): pl.pallas_call(kernel, out_shape=[jax.ShapeDtypeStruct(s, d) for s, d in...  5.1 us
  transfers between devices with their start and end apart: 9, of which 6 were waited for; matrix products, arithmetic and copies ran while one was open for 1% of the time, Pallas kernels for 5%

profile of v2, /device:TPU:0, one launch (start us, length us, event | category | flops | bytes accessed | tf_op | source)
XLA Modules:
  0.0 150.1 jit_solution(5102779972817216987)
XLA Ops:
  6.5 0.9 broadcast_in_dim.4.refs_1_.x_ref
  7.4 0.8 broadcast_in_dim.10
  8.2 7.3 %all-to-all-start = ((bf16[8,32,576]{2,1,0:T(8,128)(2,1)}), bf16[8,32,576]{2,1,0:T(8,128)(2,1)S(1)}, u32[]{:S(2)}, u32[]{:S(2)}) async-start(bf16[8,32,576]{2,1,0:T(8,128)(2,1)} %broadcast_in_dim.10), calls=%async_computation | async-start | bytes 655360 | tf_op jit(solution)/shard_map/all_to_all | solution.py:53
  15.5 0.7 tile.4
  16.2 9.5 %all-to-all-done.refs_0_ = bf16[8,32,576]{2,1,0:T(8,128)(2,1)S(1)} async-done(((bf16[8,32,576]{2,1,0:T(8,128)(2,1)}), bf16[8,32,576]{2,1,0:T(8,128)(2,1)S(1)}, u32[]{:S(2)}, u32[]{:S(2)}) %all-to-all-start) | async-done | bytes 294944 | tf_op jit(solution)/shard_map/all_to_all | solution.py:53
  25.8 0.8 prepare.1
  26.6 1.1 project.1
  27.8 3.6 %all-to-all-start.1 = ((bf16[32,32,128]{2,1,0:T(8,128)(2,1)}), bf16[32,32,128]{2,1,0:T(8,128)(2,1)S(1)}, u32[]{:S(2)}, u32[]{:S(2)}) async-start(bf16[32,32,128]{2,1,0:T(8,128)(2,1)} %bitcast), calls=%async_computation.1 | async-start | bytes 524288 | tf_op jit(solution)/shard_map/all_to_all | solution.py:53
  32.1 0.8 multiply_sine_fusion
  32.8 9.2 %all-to-all-done.1 = bf16[32,32,128]{2,1,0:T(8,128)(2,1)S(1)} async-done(((bf16[32,32,128]{2,1,0:T(8,128)(2,1)}), bf16[32,32,128]{2,1,0:T(8,128)(2,1)S(1)}, u32[]{:S(2)}, u32[]{:S(2)}) %all-to-all-start.1) | async-done | bytes 262176 | tf_op jit(solution)/shard_map/all_to_all | solution.py:53
  42.1 6.3 %all-gather = bf16[36,32,128]{2,1,0:T(8,128)(2,1)} all-gather(bf16[9,32,128]{2,1,0:T(8,128)(2,1)S(1)} %sum_shares.1), channel_id=2, replica_groups=mesh['gx'=4,'gy'=8] {'gx'}, dimensions={0}, use_global_device_ids=true | all-gather | bytes 368640 | tf_op jit(solution)/shard_map/all_gather | solution.py:328
  48.4 6.8 %attention.1 = bf16[4,8,8,384]{3,2,1,0:T(8,128)(2,1)} custom-call(s32[1,33]{1,0:T(1,128)} %table_ref.1, s32[1]{0:T(128)} %copy.14.length_ref, s32[3,8]{1,0:T(4,128)} %parents_ref.1, bf16[4,9,32,128]{3,2,1,0:T(8,128)(2,1)} %bitcast.26, bf16[4,9,32,128]{3,2,1,0:T(8,128)(2,1)} %bitcast.27, f32[32,128]{1,0:T(8,128)} %get-tuple-element.30.cos_ref, ...), custom_call_target="tpu_custom_call" | custom-call | tf_op jit(solution)/shard_map/attention/pallas_call | solution.py:169
  55.2 12.6 %all_to_all.30 = bf16[32,8,384]{2,1,0:T(8,128)(2,1)S(1)} all-to-all(bf16[32,8,384]{2,1,0:T(8,128)(2,1)} %bitcast.28), channel_id=1, replica_groups=mesh['gx'=4,'gy'=8] {'gx','gy'}, dimensions={0} | all-to-all | bytes 393216 | tf_op jit(solution)/shard_map/all_to_all | solution.py:53
  67.9 1.4 copy-done
  69.3 0.5 project_out.1
  69.8 14.7 %all_to_all.31.refs_0_ = bf16[8,4,8,576]{3,2,1,0:T(8,128)(2,1)S(1)} all-to-all(bf16[8,4,8,576]{3,2,1,0:T(8,128)(2,1)S(1)} %project_out.1), channel_id=1, replica_groups=mesh['gx'=4,'gy'=8] {'gy'}, dimensions={0} | all-to-all | bytes 589824 | tf_op jit(solution)/shard_map/all_to_all | solution.py:53
  84.5 0.3 mix.1
  84.8 14.3 %all_to_all.32 = bf16[32,8,576]{2,1,0:T(8,128)(2,1)S(1)} all-to-all(bf16[32,8,576]{2,1,0:T(8,128)(2,1)S(1)} %bitcast.24), channel_id=1, replica_groups=mesh['gx'=4,'gy'=8] {'gx','gy'}, dimensions={0} | all-to-all | bytes 589824 | tf_op jit(solution)/shard_map/all_to_all | solution.py:53
  99.1 1.2 gate_up.1
  100.3 0.8 collective-permute-start.1
  101.2 1.0 collective-permute-start.2
  102.2 8.0 %collective-permute-done.1.refs_2_ = bf16[64,2304]{1,0:T(8,128)(2,1)S(1)} collective-permute-done((bf16[64,2304]{1,0:T(8,128)(2,1)S(1)}, bf16[64,2304]{1,0:T(8,128)(2,1)S(1)}, u32[]{:S(2)}, u32[]{:S(2)}) %collective-permute-start.1) | collective-permute-done | bytes 294944 | tf_op jit(solution)/shard_map/ppermute | solution.py:206
  110.2 5.4 %collective-permute-done.2.refs_3_ = bf16[64,2304]{1,0:T(8,128)(2,1)S(1)} collective-permute-done((bf16[64,2304]{1,0:T(8,128)(2,1)S(1)}, bf16[64,2304]{1,0:T(8,128)(2,1)S(1)}, u32[]{:S(2)}, u32[]{:S(2)}) %collective-permute-start.2) | collective-permute-done | bytes 294944 | tf_op jit(solution)/shard_map/ppermute | solution.py:206
  115.6 0.2 activate.1
  115.9 7.6 %all-gather.2 = bf16[256,1152]{1,0:T(8,128)(2,1)S(1)} all-gather(bf16[64,1152]{1,0:T(8,128)(2,1)S(1)} %activate.1), channel_id=4, replica_groups=mesh['gx'=4,'gy'=8] {'gx'}, dimensions={0}, use_global_device_ids=true | all-gather | bytes 737280 | tf_op jit(solution)/shard_map/all_gather | solution.py:442
  123.4 0.7 project_down.1
  124.2 14.2 %all_to_all.33 = bf16[32,8,576]{2,1,0:T(8,128)(2,1)S(1)} all-to-all(bf16[32,8,576]{2,1,0:T(8,128)(2,1)S(1)} %bitcast.20), channel_id=1, replica_groups=mesh['gx'=4,'gy'=8] {'gx','gy'}, dimensions={0} | all-to-all | bytes 589824 | tf_op jit(solution)/shard_map/all_to_all | solution.py:53
  138.6 0.8 collective-permute-start.4
  139.5 1.0 collective-permute-start.5
  140.5 1.9 %collective-permute-done.4.refs_2_ = bf16[8,576]{1,0:T(8,128)(2,1)S(1)} collective-permute-done((bf16[8,576]{1,0:T(8,128)(2,1)S(1)}, bf16[8,576]{1,0:T(8,128)(2,1)S(1)}, u32[]{:S(2)}, u32[]{:S(2)}) %collective-permute-start.4) | collective-permute-done | bytes 9248 | tf_op jit(solution)/shard_map/ppermute | solution.py:206
  142.4 0.2 collective-permute-done.5.refs_3_
  142.6 0.6 reshape.59
  (32 shorter events, 0.5 us)
Async XLA Ops:
  6.5 20.1 %copy-start.9 = (f32[4,576]{1,0:T(4,128)S(1)}, f32[4,576]{1,0:T(4,128)}, u32[]{:S(2)}) copy-start(f32[4,576]{1,0:T(4,128)} %refs_1_.1) | copy-start | bytes 27652
  6.5 19.2 %copy-start.5 = (bf16[256,576]{0,1:T(8,128)(2,1)S(1)}, bf16[256,576]{0,1:T(8,128)(2,1)}, u32[]{:S(2)}) copy-start(bf16[256,576]{0,1:T(8,128)(2,1)} %param.22) | copy-start | bytes 884740
  6.5 20.1 %copy-start.8 = (bf16[576,128]{1,0:T(8,128)(2,1)S(1)}, bf16[576,128]{1,0:T(8,128)(2,1)}, u32[]{:S(2)}) copy-start(bf16[576,128]{1,0:T(8,128)(2,1)} %refs_4_.1) | copy-start | bytes 442372
  6.5 20.1 %copy-start.7 = (bf16[576,128]{1,0:T(8,128)(2,1)S(1)}, bf16[576,128]{1,0:T(8,128)(2,1)}, u32[]{:S(2)}) copy-start(bf16[576,128]{1,0:T(8,128)(2,1)} %refs_3_.1) | copy-start | bytes 442372
  6.5 20.1 %copy-start.6 = (bf16[576,256]{1,0:T(8,128)(2,1)S(1)}, bf16[576,256]{1,0:T(8,128)(2,1)}, u32[]{:S(2)}) copy-start(bf16[576,256]{1,0:T(8,128)(2,1)} %refs_2_.1) | copy-start | bytes 884740
  8.2 17.6 %all-to-all-start = ((bf16[8,32,576]{2,1,0:T(8,128)(2,1)}), bf16[8,32,576]{2,1,0:T(8,128)(2,1)S(1)}, u32[]{:S(2)}, u32[]{:S(2)}) async-start(bf16[8,32,576]{2,1,0:T(8,128)(2,1)} %broadcast_in_dim.10), calls=%async_computation | async-start | bytes 655360 | tf_op jit(solution)/shard_map/all_to_all | solution.py:53
  15.4 52.4 %all-gather.5.cloned.1.call-start = ((), (), s32[]{:S(2)}) async-start(), calls=%async_computation.6 | async-start | bytes 1843200 | tf_op jit(solution)/shard_map/all_gather | solution.py:288
  27.8 14.3 %all-to-all-start.1 = ((bf16[32,32,128]{2,1,0:T(8,128)(2,1)}), bf16[32,32,128]{2,1,0:T(8,128)(2,1)S(1)}, u32[]{:S(2)}, u32[]{:S(2)}) async-start(bf16[32,32,128]{2,1,0:T(8,128)(2,1)} %bitcast), calls=%async_computation.1 | async-start | bytes 524288 | tf_op jit(solution)/shard_map/all_to_all | solution.py:53
  67.9 1.4 copy-start
  69.3 15.2 %copy-start.1 = (bf16[2880,256]{1,0:T(8,128)(2,1)S(1)}, bf16[2880,256]{1,0:T(8,128)(2,1)}, u32[]{:S(2)}) copy-start(bf16[2880,256]{1,0:T(8,128)(2,1)} %all-gather.5.cloned.1.call-done) | copy-start | bytes 4423684
  69.8 29.3 %copy-start.4 = (bf16[576,1152]{1,0:T(8,128)(2,1)S(1)}, bf16[576,1152]{1,0:T(8,128)(2,1)}, u32[]{:S(2)}) copy-start(bf16[576,1152]{1,0:T(8,128)(2,1)} %up_ref.1) | copy-start | bytes 3981316
  84.5 14.6 %copy-start.3 = (bf16[576,1152]{1,0:T(8,128)(2,1)S(1)}, bf16[576,1152]{1,0:T(8,128)(2,1)}, u32[]{:S(2)}) copy-start(bf16[576,1152]{1,0:T(8,128)(2,1)} %gate_ref.1) | copy-start | bytes 3981316
  100.2 23.2 %copy-start.2 = (bf16[1152,576]{0,1:T(8,128)(2,1)S(1)}, bf16[1152,576]{0,1:T(8,128)(2,1)}, u32[]{:S(2)}) copy-start(bf16[1152,576]{0,1:T(8,128)(2,1)} %param.25) | copy-start | bytes 3981316
  100.3 1.9 %collective-permute-start = (bf16[64,2304]{1,0:T(8,128)(2,1)S(1)}, bf16[64,2304]{1,0:T(8,128)(2,1)S(1)}, u32[]{:S(2)}, u32[]{:S(2)}) collective-permute-start(bf16[64,2304]{1,0:T(8,128)(2,1)S(1)} %get-tuple-element.20), channel_id=1, source_target_pairs={{0,8},{8,0},{16,24},{24,16},{1,9},{9,1},{17,25},{25,17},{2,10},{10... | collective-permute-start | bytes 884744 | tf_op jit(solution)/shard_map/ppermute | solution.py:206
  100.3 9.9 %collective-permute-start.1 = (bf16[64,2304]{1,0:T(8,128)(2,1)S(1)}, bf16[64,2304]{1,0:T(8,128)(2,1)S(1)}, u32[]{:S(2)}, u32[]{:S(2)}) collective-permute-start(bf16[64,2304]{1,0:T(8,128)(2,1)S(1)} %get-tuple-element.21), channel_id=1, source_target_pairs={{0,16},{8,24},{16,0},{24,8},{1,17},{9,25},{17,1},{25,9},{2,18},{10... | collective-permute-start | bytes 884744 | tf_op jit(solution)/shard_map/ppermute | solution.py:206
  101.2 14.4 %collective-permute-start.2 = (bf16[64,2304]{1,0:T(8,128)(2,1)S(1)}, bf16[64,2304]{1,0:T(8,128)(2,1)S(1)}, u32[]{:S(2)}, u32[]{:S(2)}) collective-permute-start(bf16[64,2304]{1,0:T(8,128)(2,1)S(1)} %get-tuple-element.22), channel_id=1, source_target_pairs={{0,24},{8,16},{16,8},{24,0},{1,25},{9,17},{17,9},{25,1},{2,26},{10... | collective-permute-start | bytes 884744 | tf_op jit(solution)/shard_map/ppermute | solution.py:206
  138.5 1.9 %collective-permute-start.3 = (bf16[8,576]{1,0:T(8,128)(2,1)S(1)}, bf16[8,576]{1,0:T(8,128)(2,1)S(1)}, u32[]{:S(2)}, u32[]{:S(2)}) collective-permute-start(bf16[8,576]{1,0:T(8,128)(2,1)S(1)} %get-tuple-element.26), channel_id=1, source_target_pairs={{0,8},{8,0},{16,24},{24,16},{1,9},{9,1},{17,25},{25,17},{2,10},{10... | collective-permute-start | bytes 27656 | tf_op jit(solution)/shard_map/ppermute | solution.py:206
  138.6 3.7 %collective-permute-start.4 = (bf16[8,576]{1,0:T(8,128)(2,1)S(1)}, bf16[8,576]{1,0:T(8,128)(2,1)S(1)}, u32[]{:S(2)}, u32[]{:S(2)}) collective-permute-start(bf16[8,576]{1,0:T(8,128)(2,1)S(1)} %get-tuple-element.27), channel_id=1, source_target_pairs={{0,16},{8,24},{16,0},{24,8},{1,17},{9,25},{17,1},{25,9},{2,18},{10... | collective-permute-start | bytes 27656 | tf_op jit(solution)/shard_map/ppermute | solution.py:206
  139.5 3.1 %collective-permute-start.5 = (bf16[8,576]{1,0:T(8,128)(2,1)S(1)}, bf16[8,576]{1,0:T(8,128)(2,1)S(1)}, u32[]{:S(2)}, u32[]{:S(2)}) collective-permute-start(bf16[8,576]{1,0:T(8,128)(2,1)S(1)} %get-tuple-element.28), channel_id=1, source_target_pairs={{0,24},{8,16},{16,8},{24,0},{1,25},{9,17},{17,9},{25,1},{2,26},{10... | collective-permute-start | bytes 27656 | tf_op jit(solution)/shard_map/ppermute | solution.py:206
Sparse Core Ops, SparseCore 0:
  26.7 20.5 all-gather.4

commit v3 on v1

v3 whole, which is shorter than its diff:
```python
import jax
import jax.numpy as jnp
from jax import lax
from jax.experimental import pallas as pl
from jax.experimental.pallas import tpu as pltpu
from jax.sharding import PartitionSpec as P

D = 2304
HEADS = 8
KV_HEADS = 4
HEAD_DIM = 256
HALF = HEAD_DIM // 2
WINDOW = 4096
PAGE = 128
BEAM = 8
EPSILON = 1e-06
SOFT_CAP = 50.0
ROPE_BASE = 10000.0
REPS = HEADS // KV_HEADS
WIDE = HEAD_DIM + PAGE
BF = jnp.bfloat16
F32 = jnp.float32
MIB = 1024 * 1024
NT = (((1,), (1,)), ((), ()))


def run(name, kernel, outs, args, scratch=(), limit=16):
    return pl.pallas_call(
        kernel,
        out_shape=[jax.ShapeDtypeStruct(s, d) for s, d in outs],
        scratch_shapes=scratch,
        compiler_params=pltpu.CompilerParams(vmem_limit_bytes=limit * MIB),
        name=name,
    )(*args)


def exchange(values, axes):
    return lax.all_to_all(values, axes, split_axis=0, concat_axis=0, tiled=True)


def exchange_all(values):
    nx, ny = values.shape[:2]
    flat = values.reshape((nx * ny,) + values.shape[2:])
    return exchange(flat, ("gx", "gy")).reshape(values.shape)


def permute(values, axis, m):
    count = lax.axis_size(axis)
    return lax.ppermute(values, axis, [(i, i ^ m) for i in range(count)])


def trade(blocks, axis):
    return [blocks[0]] + [permute(blocks[m], axis, m) for m in range(1, len(blocks))]


def gather_gx(values):
    across = permute(values, "gx", 2)
    return [values, permute(values, "gx", 1), across, permute(across, "gx", 1)]


def weight_of(scores):
    return jnp.exp(SOFT_CAP * jnp.tanh(scores * (1.0 / SOFT_CAP)))


def high_low(column, lanes):
    shape = column.shape[:-1] + (lanes,)
    high = column.astype(BF).astype(F32)
    lane = lax.broadcasted_iota(jnp.int32, shape, len(shape) - 1)
    return jnp.where(lane < lanes // 2, high, column - high)


def row_sum(v):
    return jnp.sum(v, axis=-1, keepdims=True)


def attend(shares, squares, refs):
    table_ref, length_ref, parents_ref, cos_ref, sin_ref, pool_ref, page_ref = refs
    first_owner = lax.axis_index("gx") * pool_ref.shape[1]
    length = length_ref[0]
    first_page = jnp.maximum(length - WINDOW + 1, 0) // PAGE
    square = jnp.sum(squares.astype(F32), axis=0)
    square = square[:, 0:1] + square[:, HALF // 2 : HALF // 2 + 1]
    scale = lax.rsqrt(square / D + EPSILON)
    cos, sin = cos_ref[...], sin_ref[...]
    rows = cos.shape[0]
    reps = REPS
    steps = rows // BEAM
    slots = pool_ref.shape[1]

    def rotated(u, w):
        u, w = u.astype(F32) * scale, w.astype(F32) * scale
        return u * cos - w * sin, w * cos + u * sin

    query = []
    for rep in range(reps):
        u, w = rotated(shares(0, rep), shares(1, rep))
        query.append(jnp.concatenate([u, w], axis=1) * HEAD_DIM ** (-0.5))
    query = jnp.concatenate(query, axis=0).astype(BF)
    key_step = jnp.concatenate(rotated(shares(2, 0), shares(2, 1)), axis=1).astype(BF)
    value_step = jnp.concatenate(
        [shares(3, 0).astype(F32) * scale, shares(3, 1).astype(F32) * scale], axis=1
    ).astype(BF)

    for slot in range(slots):
        page_ref[slot] = -1

    def place(j, carry):
        slot = table_ref[0, j] - first_owner

        @pl.when((slot >= 0) & (slot < slots))
        def _():
            page_ref[slot] = j

        return carry

    lax.fori_loop(0, table_ref.shape[1], place, 0)
    lane = lax.broadcasted_iota(jnp.int32, (1, PAGE), 1)
    far = jnp.int32(2**30)
    position = jnp.concatenate(
        [
            lane + jnp.where(page_ref[s] >= 0, (first_page + page_ref[s]) * PAGE, far)
            for s in range(slots)
        ],
        axis=1,
    )
    step_of = lax.broadcasted_iota(jnp.int32, (reps * rows, 1), 0) % steps
    lower = length + step_of - (WINDOW - 1)
    seen = (position < length) & (position >= lower)
    keys = pool_ref[0].reshape(slots * PAGE, HEAD_DIM)
    values = pool_ref[1].reshape(slots * PAGE, HEAD_DIM)
    scores = lax.dot_general(query, keys, NT, preferred_element_type=F32)
    weights = jnp.where(seen, weight_of(scores), 0.0)
    den = jnp.sum(weights, axis=-1, keepdims=True)
    num = jnp.dot(weights.astype(BF), values, preferred_element_type=F32)

    shape = (reps * rows, rows)
    row = lax.broadcasted_iota(jnp.int32, shape, 0) % rows
    column = lax.broadcasted_iota(jnp.int32, shape, 1)
    row_step, column_step, column_beam = row % steps, column % steps, column // steps
    current = row // steps
    visible = jnp.zeros(shape, jnp.bool_)
    for j in range(steps - 1, -1, -1):
        if j < steps - 1:
            parent = jnp.zeros(shape, jnp.int32)
            for beam in range(BEAM):
                parent = jnp.where(current == beam, parents_ref[j, beam], parent)
            current = jnp.where(row_step > j, parent, current)
        visible = visible | ((column_step == j) & (row_step >= j) & (column_beam == current))
    visible = visible & (lax.axis_index("gx") == 0)
    scores = lax.dot_general(query, key_step, NT, preferred_element_type=F32)
    weights = jnp.where(visible, weight_of(scores), 0.0)
    den = den + jnp.sum(weights, axis=-1, keepdims=True)
    num = num + jnp.dot(weights.astype(BF), value_step, preferred_element_type=F32)

    return num, den


def attention_call(kernel, scalars, blocks, block_specs, pool, outs, out_specs, scratch):
    slots = pool.shape[1]
    smem = pl.BlockSpec(memory_space=pltpu.SMEM)
    return pl.pallas_call(
        kernel,
        grid=(KV_HEADS,),
        in_specs=[smem] * len(scalars)
        + block_specs
        + [pl.BlockSpec((2, slots, PAGE, HEAD_DIM), lambda h: (0, 0, 0, h))],
        out_specs=out_specs,
        out_shape=[jax.ShapeDtypeStruct(s, BF) for s in outs],
        scratch_shapes=[pltpu.SMEM((slots,), jnp.int32)] + scratch,
        compiler_params=pltpu.CompilerParams(vmem_limit_bytes=60 * MIB),
        name="attention",
    )(*scalars, *blocks, pool)


def whole_block(shape):
    return pl.BlockSpec(shape, lambda h: (0,) * len(shape))


def rope_tables(lengths, rows, steps):
    positions = lengths[0] + jnp.arange(rows, dtype=jnp.int32) % steps
    inverse_freq = ROPE_BASE ** (-jnp.arange(HALF, dtype=F32) * 2.0 / HEAD_DIM)
    angles = positions[:, None].astype(F32) * inverse_freq
    return jnp.cos(angles), jnp.sin(angles)


def body_permutes(
    inputs,
    cache_pool,
    lengths,
    block_table,
    parents,
    norm_gains,
    w_query,
    w_key,
    w_value,
    w_out,
    w_gate,
    w_up,
    w_down,
):
    beams, steps, width = inputs.shape
    nx, ny = lax.axis_size("gx"), lax.axis_size("gy")
    rows = beams * steps
    part = rows // nx
    all_rows = ny * rows
    share_rows = all_rows // nx
    hidden = w_gate.shape[1]
    x_own = inputs.reshape(rows, width)
    cos, sin = rope_tables(lengths, rows, steps)

    def my(axis):
        return lax.axis_index(axis)

    def project(*refs):
        x_refs, (gain_ref, q_ref, k_ref, v_ref, z0_ref, z2_ref, z13_ref, held) = refs[:ny], refs[ny:]
        gain = 1.0 + gain_ref[0:1]
        flat = jnp.concatenate([(r[...].astype(F32) * gain).astype(BF) for r in x_refs], axis=0)
        query = jnp.dot(flat, q_ref[...], preferred_element_type=F32).astype(BF)
        held[0], held[1] = query[:, :HALF], query[:, HALF:]
        held[2] = jnp.dot(flat, k_ref[...], preferred_element_type=F32).astype(BF)
        held[3] = jnp.dot(flat, v_ref[...], preferred_element_type=F32).astype(BF)
        me = my("gx")
        z0_ref[...], z2_ref[...] = held[me], held[me ^ 2]
        z13_ref[0], z13_ref[1] = held[me ^ 1], held[me ^ 3]

    x_blocks = trade([x_own] * ny, "gy")
    shape = (all_rows, HALF)
    z0, z2, z13 = run(
        "project",
        project,
        [(shape, BF), (shape, BF), ((2,) + shape, BF)],
        (*x_blocks, norm_gains, w_query, w_key, w_value),
        scratch=[pltpu.VMEM((nx,) + shape, BF)],
    )
    z13 = permute(z13, "gx", 1)

    def pair_sum(z_ref, from_pair_ref, out_ref):
        total = z_ref[...].astype(F32) + from_pair_ref[1].astype(F32)
        out_ref[...] = total.astype(BF)

    (z2,) = run("pair_sum", pair_sum, [(shape, BF)], (z2, z13))
    z2 = permute(z2, "gx", 2)

    def share_sum(z0_ref, z13_ref, z2_ref, *out_refs):
        total = z0_ref[...].astype(F32) + z13_ref[0].astype(F32) + z2_ref[...].astype(F32)
        for m, out_ref in enumerate(out_refs):
            out_ref[...] = total[m * rows : (m + 1) * rows].astype(BF)

    blocks = run("share_sum", share_sum, [((rows, HALF), BF)] * ny, (z0, z13, z2))
    blocks = trade(blocks, "gy")

    def pack_shares(*refs):
        x = refs[ny][...].astype(F32)
        me = my("gy")
        for m in range(ny):
            refs[-1][me ^ m] = refs[m][...]
        refs[-1][ny] = high_low(row_sum(x * x), HALF).astype(BF)

    (shares,) = run(
        "pack_shares", pack_shares, [((ny + 1, rows, HALF), BF)], (*blocks, x_own)
    )
    shares = gather_gx(shares)

    def attention(*refs):
        table, length, parent, a0, a1, a2, a3, cos_ref, sin_ref, pool_ref = refs[:10]
        z0_ref, z2_ref, z13_ref, page_ref, held, num_held, den_held = refs[10:]
        me = my("gx")
        h = pl.program_id(0)

        @pl.when(h == 0)
        def _():
            for n, ref in enumerate((a0, a1, a2, a3)):
                held[me ^ n] = ref[...]

        num, den = attend(
            lambda share, which: held[share, 2 * h + which],
            held[:, ny],
            (table, length, parent, cos_ref, sin_ref, pool_ref, page_ref),
        )
        num_held[...] = num.reshape(REPS, nx, part, HEAD_DIM)
        den_held[...] = high_low(den, PAGE).reshape(REPS, nx, part, PAGE)
        for rep in range(REPS):
            for n, out in enumerate((z0_ref, z13_ref.at[0], z2_ref, z13_ref.at[1])):
                out[rep, :, 0:HEAD_DIM] = num_held[rep, me ^ n].astype(BF)
                out[rep, :, HEAD_DIM:] = den_held[rep, me ^ n].astype(BF)

    shape = (HEADS, part, WIDE)
    half_spec = pl.BlockSpec((REPS, part, WIDE), lambda h: (h, 0, 0))
    z0, z2, z13 = attention_call(
        attention,
        (block_table, lengths, parents),
        (*shares, cos, sin),
        [whole_block(shares[0].shape)] * nx + [whole_block(cos.shape)] * 2,
        cache_pool,
        [shape, shape, (2,) + shape],
        [
            half_spec,
            half_spec,
            pl.BlockSpec((2, REPS, part, WIDE), lambda h: (0, h, 0, 0)),
        ],
        [
            pltpu.VMEM((nx,) + shares[0].shape, BF),
            pltpu.VMEM((REPS, nx, part, HEAD_DIM), F32),
            pltpu.VMEM((REPS, nx, part, PAGE), F32),
        ],
    )
    z13 = permute(z13, "gx", 1)

    def pair_terms(z_ref, from_pair_ref, out_ref):
        total = z_ref[...].astype(F32) + from_pair_ref[1].astype(F32)
        den = total[..., HEAD_DIM : HEAD_DIM + 1] + total[..., WIDE - 1 :]
        out_ref[..., 0:HEAD_DIM] = total[..., 0:HEAD_DIM].astype(BF)
        out_ref[..., HEAD_DIM:] = high_low(den, PAGE).astype(BF)

    (z2,) = run("pair_terms", pair_terms, [(shape, BF)], (z2, z13))
    z2 = permute(z2, "gx", 2)

    def divide(z0_ref, z13_ref, z2_ref, *refs):
        total = z0_ref[...].astype(F32) + z13_ref[0].astype(F32) + z2_ref[...].astype(F32)
        den = total[..., HEAD_DIM : HEAD_DIM + 1] + total[..., WIDE - 1 :]
        held = refs[ny]
        held[...] = total[..., 0:HEAD_DIM] / den
        me = my("gy")
        for m in range(ny):
            refs[m][...] = held[me ^ m].astype(BF)

    blocks = run(
        "divide",
        divide,
        [((part, HEAD_DIM), BF)] * ny,
        (z0, z13, z2),
        scratch=[pltpu.VMEM((HEADS, part, HEAD_DIM), F32)],
    )
    blocks = trade(blocks, "gy")

    def pack_heads(*refs):
        for m in range(ny):
            refs[ny][m] = refs[m][...]

    (attended,) = run("pack_heads", pack_heads, [((ny, part, HEAD_DIM), BF)], blocks)
    attended = gather_gx(attended)

    def project_out(*refs):
        w_ref, held = refs[nx], refs[-1]
        me = my("gx")
        for n in range(nx):
            held[:, me ^ n] = refs[n][...].astype(F32)
        flat = held[...].reshape(all_rows, HEAD_DIM).astype(BF)
        sums = lax.dot_general(flat, w_ref[...], NT, preferred_element_type=F32).astype(BF)
        for m in range(ny):
            refs[nx + 1 + m][...] = sums[m * rows : (m + 1) * rows]

    blocks = run(
        "project_out",
        project_out,
        [((rows, width), BF)] * ny,
        (*attended, w_out.T),
        scratch=[pltpu.VMEM((ny, nx, part, HEAD_DIM), F32)],
    )
    blocks = trade(blocks, "gy")

    def attn_sum(*refs):
        x_ref, gain_ref, attn_ref, sums_ref = refs[ny:]
        attn = sum(r[...].astype(F32) for r in refs[:ny])
        attn_ref[...] = attn
        x = x_ref[...].astype(F32)
        scaled = attn * (1.0 + gain_ref[1:2])
        lane = lax.broadcasted_iota(jnp.int32, (rows, PAGE), 1)
        sums = jnp.zeros((rows, PAGE), F32)
        for n, terms in enumerate((attn * attn, scaled * scaled, x * scaled, x * x)):
            sums = jnp.where(lane == n, row_sum(terms), sums)
        sums_ref[...] = sums

    attn, sums = run(
        "attn_sum",
        attn_sum,
        [((rows, width), F32), ((rows, PAGE), F32)],
        (*blocks, x_own, norm_gains),
    )
    sums = trade([sums] * nx, "gx")

    def mix(*refs):
        attn_ref, x_ref, gain_ref, mixed_ref, ff_ref = refs[nx:]
        total = sum(r[...] for r in refs[:nx])
        plain, scaled, cross, square = (total[:, n : n + 1] for n in range(4))
        scale = lax.rsqrt(plain / D + EPSILON)
        mixed = x_ref[...].astype(F32) + attn_ref[...] * scale * (1.0 + gain_ref[1:2])
        square = jnp.maximum(square + 2.0 * scale * cross + scale * scale * scaled, 0.0)
        mixed_ref[...] = mixed
        scale = lax.rsqrt(square / D + EPSILON)
        ff_ref[...] = (mixed * scale * (1.0 + gain_ref[2:3])).astype(BF)

    mixed, ff_input = run(
        "mix",
        mix,
        [((rows, width), F32), ((rows, width), BF)],
        (*sums, attn, x_own, norm_gains),
    )
    blocks = trade([ff_input] * ny, "gy")

    def gate_up(*refs):
        w_refs, z0_ref, z2_ref, z13_ref, held = refs[ny : ny + 2], *refs[ny + 2 :]
        me = my("gx")
        for m in range(ny):
            held[m // 2, m % 2 * rows : (m % 2 + 1) * rows] = refs[m][...]
        flat = jnp.concatenate([held[me ^ n] for n in range(nx)], axis=0)
        for n, w_ref in enumerate(w_refs):
            sums = jnp.dot(flat, w_ref[...], preferred_element_type=F32).astype(BF)
            here = pl.ds(n * hidden, hidden)
            for p, out in enumerate((z0_ref, z13_ref.at[0], z2_ref, z13_ref.at[1])):
                out[:, here] = sums[p * share_rows : (p + 1) * share_rows]

    shape = (share_rows, 2 * hidden)
    z0, z2, z13 = run(
        "gate_up",
        gate_up,
        [(shape, BF), (shape, BF), ((2,) + shape, BF)],
        (*blocks, w_gate, w_up),
        scratch=[pltpu.VMEM((nx, share_rows, width), BF)],
        limit=24,
    )
    z13 = permute(z13, "gx", 1)
    (z2,) = run("pair_sum_ff", pair_sum, [(shape, BF)], (z2, z13))
    z2 = permute(z2, "gx", 2)

    def activate(z0_ref, z13_ref, z2_ref, out_ref):
        total = z0_ref[...].astype(F32) + z13_ref[0].astype(F32) + z2_ref[...].astype(F32)
        gate, up = total[:, :hidden], total[:, hidden:]
        out_ref[...] = (jax.nn.gelu(gate, approximate=True) * up).astype(BF)

    (blocks,) = run("activate", activate, [((share_rows, hidden), BF)], (z0, z13, z2))
    blocks = gather_gx(blocks)

    def project_down(*refs):
        w_ref, held = refs[nx], refs[-1]
        me = my("gx")
        flat = jnp.concatenate([r[...] for r in refs[:nx]], axis=0)
        sums = lax.dot_general(flat, w_ref[...], NT, preferred_element_type=F32)
        held[...] = sums.reshape(nx, share_rows, width).astype(BF)
        for m in range(ny):
            refs[nx + 1 + m][...] = held[me ^ (m // 2), m % 2 * rows : (m % 2 + 1) * rows]

    blocks = run(
        "project_down",
        project_down,
        [((rows, width), BF)] * ny,
        (*blocks, w_down.T),
        scratch=[pltpu.VMEM((nx, share_rows, width), BF)],
    )
    blocks = trade(blocks, "gy")

    def down_sum(*refs):
        down = sum(r[...].astype(F32) for r in refs[:ny])
        refs[ny][...] = down
        refs[ny + 1][...] = jnp.broadcast_to(row_sum(down * down), (rows, PAGE))

    down, sums = run(
        "down_sum", down_sum, [((rows, width), F32), ((rows, PAGE), F32)], blocks
    )
    sums = trade([sums] * nx, "gx")

    def finish(*refs):
        down_ref, mixed_ref, gain_ref, out_ref = refs[nx:]
        square = sum(r[...] for r in refs[:nx])[:, 0:1]
        scale = lax.rsqrt(square / D + EPSILON)
        out = mixed_ref[...] + down_ref[...] * scale * (1.0 + gain_ref[3:4])
        out_ref[...] = out.astype(BF)

    (out,) = run(
        "finish", finish, [((rows, width), BF)], (*sums, down, mixed, norm_gains)
    )
    return out.reshape(beams, steps, width)


def body_general(
    inputs,
    cache_pool,
    lengths,
    block_table,
    parents,
    norm_gains,
    w_query,
    w_key,
    w_value,
    w_out,
    w_gate,
    w_up,
    w_down,
):
    beams, steps, width = inputs.shape
    nx, ny = lax.axis_size("gx"), lax.axis_size("gy")
    rows = beams * steps
    part = rows // nx
    head_part = w_out.shape[0]
    hidden_part = w_gate.shape[1]
    query_part, key_part = w_query.shape[1], w_key.shape[1]
    columns = query_part + 2 * key_part
    share = columns // nx
    x_own = inputs.reshape(rows, width)
    me = lax.axis_index("gx")

    x_all = exchange(jnp.broadcast_to(x_own[None], (ny, rows, width)), "gy")
    flat = (x_all.astype(F32) * (1.0 + norm_gains[0:1])).astype(BF).reshape(ny * rows, width)
    sums = [jnp.dot(flat, w, preferred_element_type=F32) for w in (w_query, w_key, w_value)]
    sums = jnp.concatenate(sums, axis=1).reshape(ny, rows, nx, share)
    received = exchange_all(sums.transpose(2, 0, 1, 3).astype(BF))
    shares = jnp.sum(received.astype(F32), axis=0).astype(BF)
    every = lax.all_gather(shares, "gx", axis=0)
    every = every.transpose(2, 1, 0, 3).reshape(rows, ny, columns)
    q = every[..., :query_part].reshape(rows, HEADS, 2, HALF).transpose(2, 1, 0, 3)
    k, v = (
        every[..., start : start + key_part].reshape(rows, 2 * KV_HEADS, HALF).transpose(1, 0, 2)
        for start in (query_part, query_part + key_part)
    )
    shares = jnp.concatenate([q, k[None], v[None]], axis=0)
    square = lax.psum(row_sum(jnp.square(x_own.astype(F32))), "gx")
    high = lax.reduce_precision(square, 8, 7)
    squares = jnp.where(jnp.arange(HALF) < HALF // 2, high, square - high).astype(BF)[None]
    cos, sin = rope_tables(lengths, rows, steps)

    def attention(*refs):
        table, length, parent, g_ref, square_ref, cos_ref, sin_ref, pool_ref = refs[:8]
        out_ref, page_ref = refs[8:]
        num, den = attend(
            lambda share, which: g_ref[share, which],
            square_ref[...],
            (table, length, parent, cos_ref, sin_ref, pool_ref, page_ref),
        )
        den = high_low(den, PAGE)
        for rep in range(REPS):
            here = slice(rep * rows, (rep + 1) * rows)
            out_ref[rep, :, 0:HEAD_DIM] = num[here].astype(BF)
            out_ref[rep, :, HEAD_DIM:] = den[here].astype(BF)

    (terms,) = attention_call(
        attention,
        (block_table, lengths, parents),
        (shares, squares, cos, sin),
        [
            pl.BlockSpec((4, 2, rows, HALF), lambda h: (0, h, 0, 0)),
            whole_block(squares.shape),
            whole_block(cos.shape),
            whole_block(sin.shape),
        ],
        cache_pool,
        [(HEADS, rows, WIDE)],
        [pl.BlockSpec((REPS, rows, WIDE), lambda h: (h, 0, 0))],
        [],
    )
    num = terms[..., :HEAD_DIM].transpose(1, 0, 2).reshape(nx, part, ny, head_part)
    den = terms[..., HEAD_DIM :: PAGE // 2].transpose(1, 0, 2)
    den = jnp.repeat(den, ny // HEADS, axis=1).reshape(nx, part, ny, 2)
    terms = exchange_all(jnp.concatenate([num, den], axis=-1).transpose(0, 2, 1, 3))

    w_wide = lax.all_gather(w_out, "gx", axis=1, tiled=True)
    x_wide = lax.all_gather(x_own, "gx", axis=1, tiled=True)
    x_rows = lax.dynamic_slice_in_dim(x_wide, me * part, part, 0).astype(F32)
    gains = 1.0 + lax.all_gather(norm_gains, "gx", axis=1, tiled=True)

    def scaled(v, gain):
        return v * lax.rsqrt(row_sum(v * v) / D + EPSILON) * gain

    terms = jnp.sum(terms.astype(F32), axis=0)
    den = terms[..., head_part : head_part + 1] + terms[..., -1:]
    attended = (terms[..., :head_part] / den).reshape(ny * part, head_part).astype(BF)
    attn = jnp.dot(attended, w_wide, preferred_element_type=F32).astype(BF)
    attn = exchange(attn.reshape(ny, part, D), "gy").astype(F32).sum(axis=0)
    mixed = x_rows + scaled(attn, gains[1])
    ff_input = scaled(mixed, gains[2]).astype(BF)
    ff_input = ff_input.reshape(part, nx, width).transpose(1, 0, 2)[:, None]
    ff_input = exchange_all(jnp.broadcast_to(ff_input, (nx, ny, part, width)))

    flat = ff_input.reshape(-1, width)
    both = [jnp.dot(flat, w, preferred_element_type=F32).astype(BF) for w in (w_gate, w_up)]
    both = jnp.stack(both, axis=1).reshape(nx, ny * part, 2, hidden_part)
    both = jnp.sum(exchange(both, "gx").astype(F32), axis=0)
    hidden = (jax.nn.gelu(both[:, 0], approximate=True) * both[:, 1]).astype(BF)
    hidden = lax.all_gather(hidden, "gx", axis=0, tiled=True)
    down = jnp.dot(hidden, w_down, preferred_element_type=F32).astype(BF)
    down = exchange_all(down.reshape(nx, ny, part, width)).astype(F32).sum(axis=1)
    down = down.transpose(1, 0, 2).reshape(part, D)
    out = (mixed + scaled(down, gains[3])).astype(BF)
    out = exchange(out.reshape(part, nx, width).transpose(1, 0, 2), "gx")
    return out.reshape(beams, steps, width)


def solution(mesh):
    sizes = dict(mesh.shape)
    fits = sizes["gx"] == 4 and sizes["gy"] == HEADS
    return jax.shard_map(
        body_permutes if fits else body_general,
        mesh=mesh,
        in_specs=(
            P("gy", None, "gx"),
            P(None, "gx", "gy", None),
            P("gy"),
            P("gy", None),
            P(None, "gy"),
            P(None, "gx"),
            P("gx", "gy"),
            P("gx", "gy"),
            P("gx", "gy"),
            P("gy", "gx"),
            P("gx", "gy"),
            P("gx", "gy"),
            P("gy", "gx"),
        ),
        out_specs=P("gy", None, "gx"),
        check_vma=False,
    )
```

time: 162 us -> 158 us (0.975)
  blocking collectives: 78 us -> 0 us
  starting transfers between devices: 10.6 us -> 82.1 us
  waiting for transfers between devices: 32.3 us -> 55.6 us
  between operations: 14.2 us -> 0.89 us
  local copies, waits for them, and re-layouts: 13.7 us -> 7.17 us
    ppermute x0 -> x63, starting transfers between devices: none -> 82.1 us  [permute(): return lax.ppermute(values, axis, [(i, i ^ m) for i in range(count)])]
    all_to_all x5 -> x0, blocking collectives: 65.2 us -> none  [exchange(): return lax.all_to_all(values, axes, split_axis=0, concat_axis=0, tiled=True)]
    ppermute x0 -> x63, waiting for transfers between devices: none -> 55.6 us  [permute(): return lax.ppermute(values, axis, [(i, i ^ m) for i in range(count)])]
    all_to_all x3 -> x0, waiting for transfers between devices: 32.2 us -> none  [exchange(): return lax.all_to_all(values, axes, split_axis=0, concat_axis=0, tiled=True)]
    all_gather x2 -> x0, blocking collectives: 12.7 us -> none  [the longest x1 6.94 us: body(): hidden = lax.all_gather(hidden, 'gx', axis=0)]
    all_to_all x3 -> x0, starting transfers between devices: 10.6 us -> none  [exchange(): return lax.all_to_all(values, axes, split_axis=0, concat_axis=0, tiled=True)]
    concatenate x1 -> x0, local copies, waits for them, and re-layouts: 3.29 us -> none  [body(): jnp.concatenate([w_out, x_own, gain_block], axis=0)]
    unnamed x22 -> x30, local copies, waits for them, and re-layouts: 7.23 us -> 5.74 us
  transfers between devices with their start and end apart: 4 -> 63, of which waited for: 3 -> 32; matrix products, arithmetic and copies ran while one was open for 2% -> 0% of each run, Pallas kernels for 1% -> 0%
where the time goes in v3:
time: 158 us; the launch traced here: 157 us
  starting transfers between devices  82.1 us (52%)
  waiting for transfers between devices  55.6 us (35%)
  Pallas kernels  10.9 us (7%)
  local copies, waits for them, and re-layouts  7.17 us (5%)
    ppermute x63, starting transfers between devices, permute(): return lax.ppermute(values, axis, [(i, i ^ m) for i in range(count)])  82.1 us
    ppermute x63, waiting for transfers between devices, permute(): return lax.ppermute(values, axis, [(i, i ^ m) for i in range(count)])  55.6 us
    pallas_call x1, Pallas kernels, attention_call(): pl.pallas_call(kernel, grid=(KV_HEADS,), in_specs=[smem] * len(scalars) +...  6.98 us
    unnamed x30, local copies, waits for them, and re-layouts  5.74 us
    pallas_call x16, Pallas kernels, run(): pl.pallas_call(kernel, out_shape=[jax.ShapeDtypeStruct(s, d) for s, d in...  3.97 us
  transfers between devices with their start and end apart: 63, of which 32 were waited for; matrix products, arithmetic and copies ran while one was open for 0% of the time, Pallas kernels for 0%

profile of v3, /device:TPU:0, one launch (start us, length us, event | category | flops | bytes accessed | tf_op | source)
XLA Modules:
  0.0 157.5 jit_solution(6720415840329876300)
XLA Ops:
  0.8 6.0 %collective-permute-start.6 = (bf16[32,576]{1,0:T(8,128)(2,1)S(1)}, bf16[32,576]{1,0:T(8,128)(2,1)S(1)}, u32[]{:S(2)}, u32[]{:S(2)}) collective-permute-start(bf16[32,576]{1,0:T(8,128)(2,1)S(1)} %reshape.24.refs_0_.refs_8_.refs_5_), channel_id=1, source_target_pairs={{0,7},{1,6},{2,5},{3,4},{4,3},{5,2},{6,1},{7,0},{8,15},{9,14},{10,... | collective-permute-start | bytes 110600 | tf_op jit(solution)/shard_map/ppermute | solution.py:49
  7.8 2.0 %collective-permute-start.3 = (bf16[32,576]{1,0:T(8,128)(2,1)S(1)}, bf16[32,576]{1,0:T(8,128)(2,1)S(1)}, u32[]{:S(2)}, u32[]{:S(2)}) collective-permute-start(bf16[32,576]{1,0:T(8,128)(2,1)S(1)} %reshape.24.refs_0_.refs_8_.refs_5_), channel_id=1, source_target_pairs={{0,4},{1,5},{2,6},{3,7},{4,0},{5,1},{6,2},{7,3},{8,12},{9,13},{10,... | collective-permute-start | bytes 110600 | tf_op jit(solution)/shard_map/ppermute | solution.py:49
  9.9 2.3 %collective-permute-start.2 = (bf16[32,576]{1,0:T(8,128)(2,1)S(1)}, bf16[32,576]{1,0:T(8,128)(2,1)S(1)}, u32[]{:S(2)}, u32[]{:S(2)}) collective-permute-start(bf16[32,576]{1,0:T(8,128)(2,1)S(1)} %reshape.24.refs_0_.refs_8_.refs_5_), channel_id=1, source_target_pairs={{0,3},{1,2},{2,1},{3,0},{4,7},{5,6},{6,5},{7,4},{8,11},{9,10},{10,... | collective-permute-start | bytes 110600 | tf_op jit(solution)/shard_map/ppermute | solution.py:49
  22.3 1.6 %collective-permute-start.8 = (bf16[256,128]{1,0:T(8,128)(2,1)S(1)}, bf16[256,128]{1,0:T(8,128)(2,1)S(1)}, u32[]{:S(2)}, u32[]{:S(2)}) collective-permute-start(bf16[256,128]{1,0:T(8,128)(2,1)S(1)} %pair_sum.1), channel_id=1, source_target_pairs={{0,16},{8,24},{16,0},{24,8},{1,17},{9,25},{17,1},{25,9},{2,18},{10... | collective-permute-start | bytes 196616 | tf_op jit(solution)/shard_map/ppermute | solution.py:49
  23.9 2.7 %collective-permute-done.8.z2_ref = bf16[256,128]{1,0:T(8,128)(2,1)S(1)} collective-permute-done((bf16[256,128]{1,0:T(8,128)(2,1)S(1)}, bf16[256,128]{1,0:T(8,128)(2,1)S(1)}, u32[]{:S(2)}, u32[]{:S(2)}) %collective-permute-start.8) | collective-permute-done | bytes 65568 | tf_op jit(solution)/shard_map/ppermute | solution.py:49
  28.5 1.7 %collective-permute-start.11 = (bf16[32,128]{1,0:T(8,128)(2,1)S(1)}, bf16[32,128]{1,0:T(8,128)(2,1)S(1)}, u32[]{:S(2)}, u32[]{:S(2)}) collective-permute-start(bf16[32,128]{1,0:T(8,128)(2,1)S(1)} %get-tuple-element.58), channel_id=1, source_target_pairs={{0,3},{1,2},{2,1},{3,0},{4,7},{5,6},{6,5},{7,4},{8,11},{9,10},{10,... | collective-permute-start | bytes 24584 | tf_op jit(solution)/shard_map/ppermute | solution.py:49
  30.2 2.2 %collective-permute-start.12 = (bf16[32,128]{1,0:T(8,128)(2,1)S(1)}, bf16[32,128]{1,0:T(8,128)(2,1)S(1)}, u32[]{:S(2)}, u32[]{:S(2)}) collective-permute-start(bf16[32,128]{1,0:T(8,128)(2,1)S(1)} %get-tuple-element.59), channel_id=1, source_target_pairs={{0,4},{1,5},{2,6},{3,7},{4,0},{5,1},{6,2},{7,3},{8,12},{9,13},{10,... | collective-permute-start | bytes 24584 | tf_op jit(solution)/shard_map/ppermute | solution.py:49
  33.0 3.7 %collective-permute-start.14 = (bf16[32,128]{1,0:T(8,128)(2,1)S(1)}, bf16[32,128]{1,0:T(8,128)(2,1)S(1)}, u32[]{:S(2)}, u32[]{:S(2)}) collective-permute-start(bf16[32,128]{1,0:T(8,128)(2,1)S(1)} %get-tuple-element.61), channel_id=1, source_target_pairs={{0,6},{1,7},{2,4},{3,5},{4,2},{5,3},{6,0},{7,1},{8,14},{9,15},{10,... | collective-permute-start | bytes 24584 | tf_op jit(solution)/shard_map/ppermute | solution.py:49
  38.6 4.5 %collective-permute-done.15.refs_7_ = bf16[32,128]{1,0:T(8,128)(2,1)S(1)} collective-permute-done((bf16[32,128]{1,0:T(8,128)(2,1)S(1)}, bf16[32,128]{1,0:T(8,128)(2,1)S(1)}, u32[]{:S(2)}, u32[]{:S(2)}) %collective-permute-start.15) | collective-permute-done | bytes 8224 | tf_op jit(solution)/shard_map/ppermute | solution.py:49
  44.7 2.8 %collective-permute-done.17.refs_5_ = bf16[9,32,128]{2,1,0:T(8,128)(2,1)S(1)} collective-permute-done((bf16[9,32,128]{2,1,0:T(8,128)(2,1)S(1)}, bf16[9,32,128]{2,1,0:T(8,128)(2,1)S(1)}, u32[]{:S(2)}, u32[]{:S(2)}) %collective-permute-start.17) | collective-permute-done | bytes 73760 | tf_op jit(solution)/shard_map/ppermute | solution.py:49
  49.5 7.0 %attention.1 = (bf16[8,8,384]{2,1,0:T(8,128)(2,1)}, bf16[8,8,384]{2,1,0:T(8,128)(2,1)}, bf16[2,8,8,384]{3,2,1,0:T(8,128)(2,1)}) custom-call(s32[1,33]{1,0:T(1,128)} %refs_0_.1, s32[1]{0:T(128)} %copy.14.refs_1_, s32[3,8]{1,0:T(4,128)} %refs_2_.1, bf16[9,32,128]{2,1,0:T(8,128)(2,1)} %copy-done.5, bf16[9,32,128]{2,1,0:T(8,128)(2,1)} %copy-done.13, ...), custom_call_target="tpu_custom_call" | custom-call | tf_op jit(solution)/shard_map/attention/pallas_call | solution.py:161
  59.0 1.6 %collective-permute-start.20 = (bf16[8,8,384]{2,1,0:T(8,128)(2,1)S(1)}, bf16[8,8,384]{2,1,0:T(8,128)(2,1)S(1)}, u32[]{:S(2)}, u32[]{:S(2)}) collective-permute-start(bf16[8,8,384]{2,1,0:T(8,128)(2,1)S(1)} %pair_terms.1), channel_id=1, source_target_pairs={{0,16},{8,24},{16,0},{24,8},{1,17},{9,25},{17,1},{25,9},{2,18},{10... | collective-permute-start | bytes 147464 | tf_op jit(solution)/shard_map/ppermute | solution.py:49
  60.6 2.6 %collective-permute-done.20.z2_ref = bf16[8,8,384]{2,1,0:T(8,128)(2,1)S(1)} collective-permute-done((bf16[8,8,384]{2,1,0:T(8,128)(2,1)S(1)}, bf16[8,8,384]{2,1,0:T(8,128)(2,1)S(1)}, u32[]{:S(2)}, u32[]{:S(2)}) %collective-permute-start.20) | collective-permute-done | bytes 49184 | tf_op jit(solution)/shard_map/ppermute | solution.py:49
  65.7 2.0 %collective-permute-start.23 = (bf16[8,256]{1,0:T(8,128)(2,1)S(1)}, bf16[8,256]{1,0:T(8,128)(2,1)S(1)}, u32[]{:S(2)}, u32[]{:S(2)}) collective-permute-start(bf16[8,256]{1,0:T(8,128)(2,1)S(1)} %get-tuple-element.69), channel_id=1, source_target_pairs={{0,3},{1,2},{2,1},{3,0},{4,7},{5,6},{6,5},{7,4},{8,11},{9,10},{10,... | collective-permute-start | bytes 12296 | tf_op jit(solution)/shard_map/ppermute | solution.py:49
  67.7 3.8 %collective-permute-start.25 = (bf16[8,256]{1,0:T(8,128)(2,1)S(1)}, bf16[8,256]{1,0:T(8,128)(2,1)S(1)}, u32[]{:S(2)}, u32[]{:S(2)}) collective-permute-start(bf16[8,256]{1,0:T(8,128)(2,1)S(1)} %get-tuple-element.71), channel_id=1, source_target_pairs={{0,5},{1,4},{2,7},{3,6},{4,1},{5,0},{6,3},{7,2},{8,13},{9,12},{10,... | collective-permute-start | bytes 12296 | tf_op jit(solution)/shard_map/ppermute | solution.py:49
  71.8 3.6 %collective-permute-start.27 = (bf16[8,256]{1,0:T(8,128)(2,1)S(1)}, bf16[8,256]{1,0:T(8,128)(2,1)S(1)}, u32[]{:S(2)}, u32[]{:S(2)}) collective-permute-start(bf16[8,256]{1,0:T(8,128)(2,1)S(1)} %get-tuple-element.73), channel_id=1, source_target_pairs={{0,7},{1,6},{2,5},{3,4},{4,3},{5,2},{6,1},{7,0},{8,15},{9,14},{10,... | collective-permute-start | bytes 12296 | tf_op jit(solution)/shard_map/ppermute | solution.py:49
  75.3 1.6 %collective-permute-done.26.refs_6_ = bf16[8,256]{1,0:T(8,128)(2,1)S(1)} collective-permute-done((bf16[8,256]{1,0:T(8,128)(2,1)S(1)}, bf16[8,256]{1,0:T(8,128)(2,1)S(1)}, u32[]{:S(2)}, u32[]{:S(2)}) %collective-permute-start.26) | collective-permute-done | bytes 4128 | tf_op jit(solution)/shard_map/ppermute | solution.py:49
  79.6 2.4 %collective-permute-done.29.refs_2_ = bf16[8,8,256]{2,1,0:T(8,128)(2,1)S(1)} collective-permute-done((bf16[8,8,256]{2,1,0:T(8,128)(2,1)S(1)}, bf16[8,8,256]{2,1,0:T(8,128)(2,1)S(1)}, u32[]{:S(2)}, u32[]{:S(2)}) %collective-permute-start.29) | collective-permute-done | bytes 32800 | tf_op jit(solution)/shard_map/ppermute | solution.py:49
  84.0 3.1 %collective-permute-start.33 = (bf16[32,576]{1,0:T(8,128)(2,1)S(1)}, bf16[32,576]{1,0:T(8,128)(2,1)S(1)}, u32[]{:S(2)}, u32[]{:S(2)}) collective-permute-start(bf16[32,576]{1,0:T(8,128)(2,1)S(1)} %get-tuple-element.77), channel_id=1, source_target_pairs={{0,3},{1,2},{2,1},{3,0},{4,7},{5,6},{6,5},{7,4},{8,11},{9,10},{10,... | collective-permute-start | bytes 110600 | tf_op jit(solution)/shard_map/ppermute | solution.py:49
  87.0 2.1 %collective-permute-start.34 = (bf16[32,576]{1,0:T(8,128)(2,1)S(1)}, bf16[32,576]{1,0:T(8,128)(2,1)S(1)}, u32[]{:S(2)}, u32[]{:S(2)}) collective-permute-start(bf16[32,576]{1,0:T(8,128)(2,1)S(1)} %get-tuple-element.78), channel_id=1, source_target_pairs={{0,4},{1,5},{2,6},{3,7},{4,0},{5,1},{6,2},{7,3},{8,12},{9,13},{10,... | collective-permute-start | bytes 110600 | tf_op jit(solution)/shard_map/ppermute | solution.py:49
  89.8 3.7 %collective-permute-start.36 = (bf16[32,576]{1,0:T(8,128)(2,1)S(1)}, bf16[32,576]{1,0:T(8,128)(2,1)S(1)}, u32[]{:S(2)}, u32[]{:S(2)}) collective-permute-start(bf16[32,576]{1,0:T(8,128)(2,1)S(1)} %get-tuple-element.80), channel_id=1, source_target_pairs={{0,6},{1,7},{2,4},{3,5},{4,2},{5,3},{6,0},{7,1},{8,14},{9,15},{10,... | collective-permute-start | bytes 110600 | tf_op jit(solution)/shard_map/ppermute | solution.py:49
  96.1 4.2 %collective-permute-done.37.refs_7_ = bf16[32,576]{1,0:T(8,128)(2,1)S(1)} collective-permute-done((bf16[32,576]{1,0:T(8,128)(2,1)S(1)}, bf16[32,576]{1,0:T(8,128)(2,1)S(1)}, u32[]{:S(2)}, u32[]{:S(2)}) %collective-permute-start.37) | collective-permute-done | bytes 36896 | tf_op jit(solution)/shard_map/ppermute | solution.py:49
  105.7 3.6 %collective-permute-start.46 = (bf16[32,576]{1,0:T(8,128)(2,1)S(1)}, bf16[32,576]{1,0:T(8,128)(2,1)S(1)}, u32[]{:S(2)}, u32[]{:S(2)}) collective-permute-start(bf16[32,576]{1,0:T(8,128)(2,1)S(1)} %get-tuple-element.84.refs_0_), channel_id=1, source_target_pairs={{0,6},{1,7},{2,4},{3,5},{4,2},{5,3},{6,0},{7,1},{8,14},{9,15},{10,... | collective-permute-start | bytes 110600 | tf_op jit(solution)/shard_map/ppermute | solution.py:49
  109.4 2.9 %collective-permute-start.44 = (bf16[32,576]{1,0:T(8,128)(2,1)S(1)}, bf16[32,576]{1,0:T(8,128)(2,1)S(1)}, u32[]{:S(2)}, u32[]{:S(2)}) collective-permute-start(bf16[32,576]{1,0:T(8,128)(2,1)S(1)} %get-tuple-element.84.refs_0_), channel_id=1, source_target_pairs={{0,4},{1,5},{2,6},{3,7},{4,0},{5,1},{6,2},{7,3},{8,12},{9,13},{10,... | collective-permute-start | bytes 110600 | tf_op jit(solution)/shard_map/ppermute | solution.py:49
  112.3 3.0 %collective-permute-start.42 = (bf16[32,576]{1,0:T(8,128)(2,1)S(1)}, bf16[32,576]{1,0:T(8,128)(2,1)S(1)}, u32[]{:S(2)}, u32[]{:S(2)}) collective-permute-start(bf16[32,576]{1,0:T(8,128)(2,1)S(1)} %get-tuple-element.84.refs_0_), channel_id=1, source_target_pairs={{0,2},{1,3},{2,0},{3,1},{4,6},{5,7},{6,4},{7,5},{8,10},{9,11},{10,... | collective-permute-start | bytes 110600 | tf_op jit(solution)/shard_map/ppermute | solution.py:49
  117.6 1.6 %collective-permute-done.41.refs_1_ = bf16[32,576]{1,0:T(8,128)(2,1)S(1)} collective-permute-done((bf16[32,576]{1,0:T(8,128)(2,1)S(1)}, bf16[32,576]{1,0:T(8,128)(2,1)S(1)}, u32[]{:S(2)}, u32[]{:S(2)}) %collective-permute-start.41) | collective-permute-done | bytes 36896 | tf_op jit(solution)/shard_map/ppermute | solution.py:49
  120.5 2.0 %collective-permute-done.48.from_pair_ref.z13_ref = bf16[2,64,2304]{2,1,0:T(8,128)(2,1)S(1)} collective-permute-done((bf16[2,64,2304]{2,1,0:T(8,128)(2,1)S(1)}, bf16[2,64,2304]{2,1,0:T(8,128)(2,1)S(1)}, u32[]{:S(2)}, u32[]{:S(2)}) %collective-permute-start.48) | collective-permute-done | bytes 589856 | tf_op jit(solution)/shard_map/ppermute | solution.py:49
  124.1 7.5 %collective-permute-done.49.z2_ref = bf16[64,2304]{1,0:T(8,128)(2,1)S(1)} collective-permute-done((bf16[64,2304]{1,0:T(8,128)(2,1)S(1)}, bf16[64,2304]{1,0:T(8,128)(2,1)S(1)}, u32[]{:S(2)}, u32[]{:S(2)}) %collective-permute-start.49) | collective-permute-done | bytes 294944 | tf_op jit(solution)/shard_map/ppermute | solution.py:49
  133.5 3.6 %collective-permute-done.51.refs_2_ = bf16[64,1152]{1,0:T(8,128)(2,1)S(1)} collective-permute-done((bf16[64,1152]{1,0:T(8,128)(2,1)S(1)}, bf16[64,1152]{1,0:T(8,128)(2,1)S(1)}, u32[]{:S(2)}, u32[]{:S(2)}) %collective-permute-start.51) | collective-permute-done | bytes 147488 | tf_op jit(solution)/shard_map/ppermute | solution.py:49
  139.9 2.9 %collective-permute-start.55 = (bf16[32,576]{1,0:T(8,128)(2,1)S(1)}, bf16[32,576]{1,0:T(8,128)(2,1)S(1)}, u32[]{:S(2)}, u32[]{:S(2)}) collective-permute-start(bf16[32,576]{1,0:T(8,128)(2,1)S(1)} %get-tuple-element.91), channel_id=1, source_target_pairs={{0,3},{1,2},{2,1},{3,0},{4,7},{5,6},{6,5},{7,4},{8,11},{9,10},{10,... | collective-permute-start | bytes 110600 | tf_op jit(solution)/shard_map/ppermute | solution.py:49
  142.7 2.9 %collective-permute-start.57 = (bf16[32,576]{1,0:T(8,128)(2,1)S(1)}, bf16[32,576]{1,0:T(8,128)(2,1)S(1)}, u32[]{:S(2)}, u32[]{:S(2)}) collective-permute-start(bf16[32,576]{1,0:T(8,128)(2,1)S(1)} %get-tuple-element.93), channel_id=1, source_target_pairs={{0,5},{1,4},{2,7},{3,6},{4,1},{5,0},{6,3},{7,2},{8,13},{9,12},{10,... | collective-permute-start | bytes 110600 | tf_op jit(solution)/shard_map/ppermute | solution.py:49
  146.1 4.3 %collective-permute-start.59 = (bf16[32,576]{1,0:T(8,128)(2,1)S(1)}, bf16[32,576]{1,0:T(8,128)(2,1)S(1)}, u32[]{:S(2)}, u32[]{:S(2)}) collective-permute-start(bf16[32,576]{1,0:T(8,128)(2,1)S(1)} %get-tuple-element.95), channel_id=1, source_target_pairs={{0,7},{1,6},{2,5},{3,4},{4,3},{5,2},{6,1},{7,0},{8,15},{9,14},{10,... | collective-permute-start | bytes 110600 | tf_op jit(solution)/shard_map/ppermute | solution.py:49
  (146 shorter events, 55.1 us)
Async XLA Ops:
  0.8 11.3 %collective-permute-start.6 = (bf16[32,576]{1,0:T(8,128)(2,1)S(1)}, bf16[32,576]{1,0:T(8,128)(2,1)S(1)}, u32[]{:S(2)}, u32[]{:S(2)}) collective-permute-start(bf16[32,576]{1,0:T(8,128)(2,1)S(1)} %reshape.24.refs_0_.refs_8_.refs_5_), channel_id=1, source_target_pairs={{0,7},{1,6},{2,5},{3,4},{4,3},{5,2},{6,1},{7,0},{8,15},{9,14},{10,... | collective-permute-start | bytes 110600 | tf_op jit(solution)/shard_map/ppermute | solution.py:49
  7.1 6.8 %collective-permute-start.4 = (bf16[32,576]{1,0:T(8,128)(2,1)S(1)}, bf16[32,576]{1,0:T(8,128)(2,1)S(1)}, u32[]{:S(2)}, u32[]{:S(2)}) collective-permute-start(bf16[32,576]{1,0:T(8,128)(2,1)S(1)} %reshape.24.refs_0_.refs_8_.refs_5_), channel_id=1, source_target_pairs={{0,5},{1,4},{2,7},{3,6},{4,1},{5,0},{6,3},{7,2},{8,13},{9,12},{10,... | collective-permute-start | bytes 110600 | tf_op jit(solution)/shard_map/ppermute | solution.py:49
  7.8 6.2 %collective-permute-start.3 = (bf16[32,576]{1,0:T(8,128)(2,1)S(1)}, bf16[32,576]{1,0:T(8,128)(2,1)S(1)}, u32[]{:S(2)}, u32[]{:S(2)}) collective-permute-start(bf16[32,576]{1,0:T(8,128)(2,1)S(1)} %reshape.24.refs_0_.refs_8_.refs_5_), channel_id=1, source_target_pairs={{0,4},{1,5},{2,6},{3,7},{4,0},{5,1},{6,2},{7,3},{8,12},{9,13},{10,... | collective-permute-start | bytes 110600 | tf_op jit(solution)/shard_map/ppermute | solution.py:49
  26.7 6.3 %collective-permute-start.9 = (bf16[32,128]{1,0:T(8,128)(2,1)S(1)}, bf16[32,128]{1,0:T(8,128)(2,1)S(1)}, u32[]{:S(2)}, u32[]{:S(2)}) collective-permute-start(bf16[32,128]{1,0:T(8,128)(2,1)S(1)} %get-tuple-element.56), channel_id=1, source_target_pairs={{0,1},{1,0},{2,3},{3,2},{4,5},{5,4},{6,7},{7,6},{8,9},{9,8},{10,11... | collective-permute-start | bytes 24584 | tf_op jit(solution)/shard_map/ppermute | solution.py:49
  27.1 9.6 %collective-permute-start.10 = (bf16[32,128]{1,0:T(8,128)(2,1)S(1)}, bf16[32,128]{1,0:T(8,128)(2,1)S(1)}, u32[]{:S(2)}, u32[]{:S(2)}) collective-permute-start(bf16[32,128]{1,0:T(8,128)(2,1)S(1)} %get-tuple-element.57), channel_id=1, source_target_pairs={{0,2},{1,3},{2,0},{3,1},{4,6},{5,7},{6,4},{7,5},{8,10},{9,11},{10,... | collective-permute-start | bytes 24584 | tf_op jit(solution)/shard_map/ppermute | solution.py:49
  28.5 10.0 %collective-permute-start.11 = (bf16[32,128]{1,0:T(8,128)(2,1)S(1)}, bf16[32,128]{1,0:T(8,128)(2,1)S(1)}, u32[]{:S(2)}, u32[]{:S(2)}) collective-permute-start(bf16[32,128]{1,0:T(8,128)(2,1)S(1)} %get-tuple-element.58), channel_id=1, source_target_pairs={{0,3},{1,2},{2,1},{3,0},{4,7},{5,6},{6,5},{7,4},{8,11},{9,10},{10,... | collective-permute-start | bytes 24584 | tf_op jit(solution)/shard_map/ppermute | solution.py:49
  30.2 8.3 %collective-permute-start.12 = (bf16[32,128]{1,0:T(8,128)(2,1)S(1)}, bf16[32,128]{1,0:T(8,128)(2,1)S(1)}, u32[]{:S(2)}, u32[]{:S(2)}) collective-permute-start(bf16[32,128]{1,0:T(8,128)(2,1)S(1)} %get-tuple-element.59), channel_id=1, source_target_pairs={{0,4},{1,5},{2,6},{3,7},{4,0},{5,1},{6,2},{7,3},{8,12},{9,13},{10,... | collective-permute-start | bytes 24584 | tf_op jit(solution)/shard_map/ppermute | solution.py:49
  32.4 6.1 %collective-permute-start.13 = (bf16[32,128]{1,0:T(8,128)(2,1)S(1)}, bf16[32,128]{1,0:T(8,128)(2,1)S(1)}, u32[]{:S(2)}, u32[]{:S(2)}) collective-permute-start(bf16[32,128]{1,0:T(8,128)(2,1)S(1)} %get-tuple-element.60), channel_id=1, source_target_pairs={{0,5},{1,4},{2,7},{3,6},{4,1},{5,0},{6,3},{7,2},{8,13},{9,12},{10,... | collective-permute-start | bytes 24584 | tf_op jit(solution)/shard_map/ppermute | solution.py:49
  36.7 6.3 %collective-permute-start.15 = (bf16[32,128]{1,0:T(8,128)(2,1)S(1)}, bf16[32,128]{1,0:T(8,128)(2,1)S(1)}, u32[]{:S(2)}, u32[]{:S(2)}) collective-permute-start(bf16[32,128]{1,0:T(8,128)(2,1)S(1)} %get-tuple-element.62), channel_id=1, source_target_pairs={{0,7},{1,6},{2,5},{3,4},{4,3},{5,2},{6,1},{7,0},{8,15},{9,14},{10,... | collective-permute-start | bytes 24584 | tf_op jit(solution)/shard_map/ppermute | solution.py:49
  64.1 7.4 %collective-permute-start.21 = (bf16[8,256]{1,0:T(8,128)(2,1)S(1)}, bf16[8,256]{1,0:T(8,128)(2,1)S(1)}, u32[]{:S(2)}, u32[]{:S(2)}) collective-permute-start(bf16[8,256]{1,0:T(8,128)(2,1)S(1)} %get-tuple-element.67), channel_id=1, source_target_pairs={{0,1},{1,0},{2,3},{3,2},{4,5},{5,4},{6,7},{7,6},{8,9},{9,8},{10,11... | collective-permute-start | bytes 12296 | tf_op jit(solution)/shard_map/ppermute | solution.py:49
  65.7 9.7 %collective-permute-start.23 = (bf16[8,256]{1,0:T(8,128)(2,1)S(1)}, bf16[8,256]{1,0:T(8,128)(2,1)S(1)}, u32[]{:S(2)}, u32[]{:S(2)}) collective-permute-start(bf16[8,256]{1,0:T(8,128)(2,1)S(1)} %get-tuple-element.69), channel_id=1, source_target_pairs={{0,3},{1,2},{2,1},{3,0},{4,7},{5,6},{6,5},{7,4},{8,11},{9,10},{10,... | collective-permute-start | bytes 12296 | tf_op jit(solution)/shard_map/ppermute | solution.py:49
  67.7 7.7 %collective-permute-start.24 = (bf16[8,256]{1,0:T(8,128)(2,1)S(1)}, bf16[8,256]{1,0:T(8,128)(2,1)S(1)}, u32[]{:S(2)}, u32[]{:S(2)}) collective-permute-start(bf16[8,256]{1,0:T(8,128)(2,1)S(1)} %get-tuple-element.70), channel_id=1, source_target_pairs={{0,4},{1,5},{2,6},{3,7},{4,0},{5,1},{6,2},{7,3},{8,12},{9,13},{10,... | collective-permute-start | bytes 12296 | tf_op jit(solution)/shard_map/ppermute | solution.py:49
  67.7 7.7 %collective-permute-start.25 = (bf16[8,256]{1,0:T(8,128)(2,1)S(1)}, bf16[8,256]{1,0:T(8,128)(2,1)S(1)}, u32[]{:S(2)}, u32[]{:S(2)}) collective-permute-start(bf16[8,256]{1,0:T(8,128)(2,1)S(1)} %get-tuple-element.71), channel_id=1, source_target_pairs={{0,5},{1,4},{2,7},{3,6},{4,1},{5,0},{6,3},{7,2},{8,13},{9,12},{10,... | collective-permute-start | bytes 12296 | tf_op jit(solution)/shard_map/ppermute | solution.py:49
  71.8 6.3 %collective-permute-start.27 = (bf16[8,256]{1,0:T(8,128)(2,1)S(1)}, bf16[8,256]{1,0:T(8,128)(2,1)S(1)}, u32[]{:S(2)}, u32[]{:S(2)}) collective-permute-start(bf16[8,256]{1,0:T(8,128)(2,1)S(1)} %get-tuple-element.73), channel_id=1, source_target_pairs={{0,7},{1,6},{2,5},{3,4},{4,3},{5,2},{6,1},{7,0},{8,15},{9,14},{10,... | collective-permute-start | bytes 12296 | tf_op jit(solution)/shard_map/ppermute | solution.py:49
  83.5 6.3 %collective-permute-start.31 = (bf16[32,576]{1,0:T(8,128)(2,1)S(1)}, bf16[32,576]{1,0:T(8,128)(2,1)S(1)}, u32[]{:S(2)}, u32[]{:S(2)}) collective-permute-start(bf16[32,576]{1,0:T(8,128)(2,1)S(1)} %get-tuple-element.75), channel_id=1, source_target_pairs={{0,1},{1,0},{2,3},{3,2},{4,5},{5,4},{6,7},{7,6},{8,9},{9,8},{10,11... | collective-permute-start | bytes 110600 | tf_op jit(solution)/shard_map/ppermute | solution.py:49
  84.0 9.6 %collective-permute-start.32 = (bf16[32,576]{1,0:T(8,128)(2,1)S(1)}, bf16[32,576]{1,0:T(8,128)(2,1)S(1)}, u32[]{:S(2)}, u32[]{:S(2)}) collective-permute-start(bf16[32,576]{1,0:T(8,128)(2,1)S(1)} %get-tuple-element.76), channel_id=1, source_target_pairs={{0,2},{1,3},{2,0},{3,1},{4,6},{5,7},{6,4},{7,5},{8,10},{9,11},{10,... | collective-permute-start | bytes 110600 | tf_op jit(solution)/shard_map/ppermute | solution.py:49
  84.0 10.7 %collective-permute-start.33 = (bf16[32,576]{1,0:T(8,128)(2,1)S(1)}, bf16[32,576]{1,0:T(8,128)(2,1)S(1)}, u32[]{:S(2)}, u32[]{:S(2)}) collective-permute-start(bf16[32,576]{1,0:T(8,128)(2,1)S(1)} %get-tuple-element.77), channel_id=1, source_target_pairs={{0,3},{1,2},{2,1},{3,0},{4,7},{5,6},{6,5},{7,4},{8,11},{9,10},{10,... | collective-permute-start | bytes 110600 | tf_op jit(solution)/shard_map/ppermute | solution.py:49
  87.0 7.7 %collective-permute-start.34 = (bf16[32,576]{1,0:T(8,128)(2,1)S(1)}, bf16[32,576]{1,0:T(8,128)(2,1)S(1)}, u32[]{:S(2)}, u32[]{:S(2)}) collective-permute-start(bf16[32,576]{1,0:T(8,128)(2,1)S(1)} %get-tuple-element.78), channel_id=1, source_target_pairs={{0,4},{1,5},{2,6},{3,7},{4,0},{5,1},{6,2},{7,3},{8,12},{9,13},{10,... | collective-permute-start | bytes 110600 | tf_op jit(solution)/shard_map/ppermute | solution.py:49
  89.2 6.6 %collective-permute-start.35 = (bf16[32,576]{1,0:T(8,128)(2,1)S(1)}, bf16[32,576]{1,0:T(8,128)(2,1)S(1)}, u32[]{:S(2)}, u32[]{:S(2)}) collective-permute-start(bf16[32,576]{1,0:T(8,128)(2,1)S(1)} %get-tuple-element.79), channel_id=1, source_target_pairs={{0,5},{1,4},{2,7},{3,6},{4,1},{5,0},{6,3},{7,2},{8,13},{9,12},{10,... | collective-permute-start | bytes 110600 | tf_op jit(solution)/shard_map/ppermute | solution.py:49
  89.8 6.2 %collective-permute-start.36 = (bf16[32,576]{1,0:T(8,128)(2,1)S(1)}, bf16[32,576]{1,0:T(8,128)(2,1)S(1)}, u32[]{:S(2)}, u32[]{:S(2)}) collective-permute-start(bf16[32,576]{1,0:T(8,128)(2,1)S(1)} %get-tuple-element.80), channel_id=1, source_target_pairs={{0,6},{1,7},{2,4},{3,5},{4,2},{5,3},{6,0},{7,1},{8,14},{9,15},{10,... | collective-permute-start | bytes 110600 | tf_op jit(solution)/shard_map/ppermute | solution.py:49
  93.6 6.7 %collective-permute-start.37 = (bf16[32,576]{1,0:T(8,128)(2,1)S(1)}, bf16[32,576]{1,0:T(8,128)(2,1)S(1)}, u32[]{:S(2)}, u32[]{:S(2)}) collective-permute-start(bf16[32,576]{1,0:T(8,128)(2,1)S(1)} %get-tuple-element.81), channel_id=1, source_target_pairs={{0,7},{1,6},{2,5},{3,4},{4,3},{5,2},{6,1},{7,0},{8,15},{9,14},{10,... | collective-permute-start | bytes 110600 | tf_op jit(solution)/shard_map/ppermute | solution.py:49
  104.5 7.7 %collective-permute-start.47 = (bf16[32,576]{1,0:T(8,128)(2,1)S(1)}, bf16[32,576]{1,0:T(8,128)(2,1)S(1)}, u32[]{:S(2)}, u32[]{:S(2)}) collective-permute-start(bf16[32,576]{1,0:T(8,128)(2,1)S(1)} %get-tuple-element.84.refs_0_), channel_id=1, source_target_pairs={{0,7},{1,6},{2,5},{3,4},{4,3},{5,2},{6,1},{7,0},{8,15},{9,14},{10,... | collective-permute-start | bytes 110600 | tf_op jit(solution)/shard_map/ppermute | solution.py:49
  105.7 9.5 %collective-permute-start.46 = (bf16[32,576]{1,0:T(8,128)(2,1)S(1)}, bf16[32,576]{1,0:T(8,128)(2,1)S(1)}, u32[]{:S(2)}, u32[]{:S(2)}) collective-permute-start(bf16[32,576]{1,0:T(8,128)(2,1)S(1)} %get-tuple-element.84.refs_0_), channel_id=1, source_target_pairs={{0,6},{1,7},{2,4},{3,5},{4,2},{5,3},{6,0},{7,1},{8,14},{9,15},{10,... | collective-permute-start | bytes 110600 | tf_op jit(solution)/shard_map/ppermute | solution.py:49
  109.4 6.4 %collective-permute-start.45 = (bf16[32,576]{1,0:T(8,128)(2,1)S(1)}, bf16[32,576]{1,0:T(8,128)(2,1)S(1)}, u32[]{:S(2)}, u32[]{:S(2)}) collective-permute-start(bf16[32,576]{1,0:T(8,128)(2,1)S(1)} %get-tuple-element.84.refs_0_), channel_id=1, source_target_pairs={{0,5},{1,4},{2,7},{3,6},{4,1},{5,0},{6,3},{7,2},{8,13},{9,12},{10,... | collective-permute-start | bytes 110600 | tf_op jit(solution)/shard_map/ppermute | solution.py:49
  109.4 6.4 %collective-permute-start.44 = (bf16[32,576]{1,0:T(8,128)(2,1)S(1)}, bf16[32,576]{1,0:T(8,128)(2,1)S(1)}, u32[]{:S(2)}, u32[]{:S(2)}) collective-permute-start(bf16[32,576]{1,0:T(8,128)(2,1)S(1)} %get-tuple-element.84.refs_0_), channel_id=1, source_target_pairs={{0,4},{1,5},{2,6},{3,7},{4,0},{5,1},{6,2},{7,3},{8,12},{9,13},{10,... | collective-permute-start | bytes 110600 | tf_op jit(solution)/shard_map/ppermute | solution.py:49
  122.6 9.1 %collective-permute-start.49 = (bf16[64,2304]{1,0:T(8,128)(2,1)S(1)}, bf16[64,2304]{1,0:T(8,128)(2,1)S(1)}, u32[]{:S(2)}, u32[]{:S(2)}) collective-permute-start(bf16[64,2304]{1,0:T(8,128)(2,1)S(1)} %pair_sum_ff.1), channel_id=1, source_target_pairs={{0,16},{8,24},{16,0},{24,8},{1,17},{9,25},{17,1},{25,9},{2,18},{10... | collective-permute-start | bytes 884744 | tf_op jit(solution)/shard_map/ppermute | solution.py:49
  139.2 6.5 %collective-permute-start.53 = (bf16[32,576]{1,0:T(8,128)(2,1)S(1)}, bf16[32,576]{1,0:T(8,128)(2,1)S(1)}, u32[]{:S(2)}, u32[]{:S(2)}) collective-permute-start(bf16[32,576]{1,0:T(8,128)(2,1)S(1)} %get-tuple-element.89), channel_id=1, source_target_pairs={{0,1},{1,0},{2,3},{3,2},{4,5},{5,4},{6,7},{7,6},{8,9},{9,8},{10,11... | collective-permute-start | bytes 110600 | tf_op jit(solution)/shard_map/ppermute | solution.py:49
  139.8 6.3 %collective-permute-start.54 = (bf16[32,576]{1,0:T(8,128)(2,1)S(1)}, bf16[32,576]{1,0:T(8,128)(2,1)S(1)}, u32[]{:S(2)}, u32[]{:S(2)}) collective-permute-start(bf16[32,576]{1,0:T(8,128)(2,1)S(1)} %get-tuple-element.90), channel_id=1, source_target_pairs={{0,2},{1,3},{2,0},{3,1},{4,6},{5,7},{6,4},{7,5},{8,10},{9,11},{10,... | collective-permute-start | bytes 110600 | tf_op jit(solution)/shard_map/ppermute | solution.py:49
  139.9 10.5 %collective-permute-start.55 = (bf16[32,576]{1,0:T(8,128)(2,1)S(1)}, bf16[32,576]{1,0:T(8,128)(2,1)S(1)}, u32[]{:S(2)}, u32[]{:S(2)}) collective-permute-start(bf16[32,576]{1,0:T(8,128)(2,1)S(1)} %get-tuple-element.91), channel_id=1, source_target_pairs={{0,3},{1,2},{2,1},{3,0},{4,7},{5,6},{6,5},{7,4},{8,11},{9,10},{10,... | collective-permute-start | bytes 110600 | tf_op jit(solution)/shard_map/ppermute | solution.py:49
  142.7 7.7 %collective-permute-start.56 = (bf16[32,576]{1,0:T(8,128)(2,1)S(1)}, bf16[32,576]{1,0:T(8,128)(2,1)S(1)}, u32[]{:S(2)}, u32[]{:S(2)}) collective-permute-start(bf16[32,576]{1,0:T(8,128)(2,1)S(1)} %get-tuple-element.92), channel_id=1, source_target_pairs={{0,4},{1,5},{2,6},{3,7},{4,0},{5,1},{6,2},{7,3},{8,12},{9,13},{10,... | collective-permute-start | bytes 110600 | tf_op jit(solution)/shard_map/ppermute | solution.py:49
  142.7 7.7 %collective-permute-start.57 = (bf16[32,576]{1,0:T(8,128)(2,1)S(1)}, bf16[32,576]{1,0:T(8,128)(2,1)S(1)}, u32[]{:S(2)}, u32[]{:S(2)}) collective-permute-start(bf16[32,576]{1,0:T(8,128)(2,1)S(1)} %get-tuple-element.93), channel_id=1, source_target_pairs={{0,5},{1,4},{2,7},{3,6},{4,1},{5,0},{6,3},{7,2},{8,13},{9,12},{10,... | collective-permute-start | bytes 110600 | tf_op jit(solution)/shard_map/ppermute | solution.py:49
  146.1 6.7 %collective-permute-start.59 = (bf16[32,576]{1,0:T(8,128)(2,1)S(1)}, bf16[32,576]{1,0:T(8,128)(2,1)S(1)}, u32[]{:S(2)}, u32[]{:S(2)}) collective-permute-start(bf16[32,576]{1,0:T(8,128)(2,1)S(1)} %get-tuple-element.95), channel_id=1, source_target_pairs={{0,7},{1,6},{2,5},{3,4},{4,3},{5,2},{6,1},{7,0},{8,15},{9,14},{10,... | collective-permute-start | bytes 110600 | tf_op jit(solution)/shard_map/ppermute | solution.py:49
  (46 other events, 364.3 us)

commit v4 on v3

--- a/solution.py
+++ b/solution.py
@@ -167,7 +167,7 @@
         out_specs=out_specs,
         out_shape=[jax.ShapeDtypeStruct(s, BF) for s in outs],
         scratch_shapes=[pltpu.SMEM((slots,), jnp.int32)] + scratch,
-        compiler_params=pltpu.CompilerParams(vmem_limit_bytes=60 * MIB),
+        compiler_params=pltpu.CompilerParams(vmem_limit_bytes=58 * MIB),
         name="attention",
     )(*scalars, *blocks, pool)
 
@@ -201,20 +201,30 @@
     beams, steps, width = inputs.shape
     nx, ny = lax.axis_size("gx"), lax.axis_size("gy")
     rows = beams * steps
-    part = rows // nx
+    half = rows // 2
     all_rows = ny * rows
     share_rows = all_rows // nx
     hidden = w_gate.shape[1]
-    x_own = inputs.reshape(rows, width)
     cos, sin = rope_tables(lengths, rows, steps)
+    w_wide = lax.all_gather(w_out.T, "gy", axis=0)
 
     def my(axis):
         return lax.axis_index(axis)
 
-    def project(*refs):
-        x_refs, (gain_ref, q_ref, k_ref, v_ref, z0_ref, z2_ref, z13_ref, held) = refs[:ny], refs[ny:]
-        gain = 1.0 + gain_ref[0:1]
-        flat = jnp.concatenate([(r[...].astype(F32) * gain).astype(BF) for r in x_refs], axis=0)
+    def spread(x_ref, own_ref, out_ref):
+        own = x_ref[...].astype(F32).reshape(rows, width).astype(BF)
+        own_ref[...] = own
+        for m in range(ny):
+            out_ref[m] = own
+
+    x_own, x_all = run(
+        "spread", spread, [((rows, width), BF), ((ny, rows, width), BF)], (inputs,)
+    )
+    x_all = exchange(x_all, "gy")
+
+    def project(x_ref, gain_ref, q_ref, k_ref, v_ref, z0_ref, z2_ref, z13_ref, held):
+        x = x_ref[...].reshape(all_rows, width).astype(F32)
+        flat = (x * (1.0 + gain_ref[0:1])).astype(BF)
         query = jnp.dot(flat, q_ref[...], preferred_element_type=F32).astype(BF)
         held[0], held[1] = query[:, :HALF], query[:, HALF:]
         held[2] = jnp.dot(flat, k_ref[...], preferred_element_type=F32).astype(BF)
@@ -223,13 +233,12 @@
         z0_ref[...], z2_ref[...] = held[me], held[me ^ 2]
         z13_ref[0], z13_ref[1] = held[me ^ 1], held[me ^ 3]
 
-    x_blocks = trade([x_own] * ny, "gy")
     shape = (all_rows, HALF)
     z0, z2, z13 = run(
         "project",
         project,
         [(shape, BF), (shape, BF), ((2,) + shape, BF)],
-        (*x_blocks, norm_gains, w_query, w_key, w_value),
+        (x_all, norm_gains, w_query, w_key, w_value),
         scratch=[pltpu.VMEM((nx,) + shape, BF)],
     )
     z13 = permute(z13, "gx", 1)
@@ -241,29 +250,24 @@
     (z2,) = run("pair_sum", pair_sum, [(shape, BF)], (z2, z13))
     z2 = permute(z2, "gx", 2)
 
-    def share_sum(z0_ref, z13_ref, z2_ref, *out_refs):
+    def share_sum(z0_ref, z13_ref, z2_ref, out_ref):
         total = z0_ref[...].astype(F32) + z13_ref[0].astype(F32) + z2_ref[...].astype(F32)
-        for m, out_ref in enumerate(out_refs):
-            out_ref[...] = total[m * rows : (m + 1) * rows].astype(BF)
-
-    blocks = run("share_sum", share_sum, [((rows, HALF), BF)] * ny, (z0, z13, z2))
-    blocks = trade(blocks, "gy")
-
-    def pack_shares(*refs):
-        x = refs[ny][...].astype(F32)
-        me = my("gy")
-        for m in range(ny):
-            refs[-1][me ^ m] = refs[m][...]
-        refs[-1][ny] = high_low(row_sum(x * x), HALF).astype(BF)
-
-    (shares,) = run(
-        "pack_shares", pack_shares, [((ny + 1, rows, HALF), BF)], (*blocks, x_own)
-    )
+        out_ref[...] = total.reshape(ny, rows, HALF).astype(BF)
+
+    (shares,) = run("share_sum", share_sum, [((ny, rows, HALF), BF)], (z0, z13, z2))
+    shares = exchange(shares, "gy")
+
+    def pack_shares(share_ref, x_ref, out_ref):
+        x = x_ref[...].astype(F32)
+        out_ref[0:ny] = share_ref[...]
+        out_ref[ny] = high_low(row_sum(x * x), HALF).astype(BF)
+
+    (shares,) = run("pack_shares", pack_shares, [((ny + 1, rows, HALF), BF)], (shares, x_own))
     shares = gather_gx(shares)
 
     def attention(*refs):
         table, length, parent, a0, a1, a2, a3, cos_ref, sin_ref, pool_ref = refs[:10]
-        z0_ref, z2_ref, z13_ref, page_ref, held, num_held, den_held = refs[10:]
+        own_ref, pair_ref, page_ref, held, num_held, den_held = refs[10:]
         me = my("gx")
         h = pl.program_id(0)
 
@@ -277,91 +281,56 @@
             held[:, ny],
             (table, length, parent, cos_ref, sin_ref, pool_ref, page_ref),
         )
-        num_held[...] = num.reshape(REPS, nx, part, HEAD_DIM)
-        den_held[...] = high_low(den, PAGE).reshape(REPS, nx, part, PAGE)
+        num_held[...] = num.reshape(REPS, 2, half, HEAD_DIM)
+        den_held[...] = high_low(den, PAGE).reshape(REPS, 2, half, PAGE)
+        core = me & 1
         for rep in range(REPS):
-            for n, out in enumerate((z0_ref, z13_ref.at[0], z2_ref, z13_ref.at[1])):
-                out[rep, :, 0:HEAD_DIM] = num_held[rep, me ^ n].astype(BF)
-                out[rep, :, HEAD_DIM:] = den_held[rep, me ^ n].astype(BF)
-
-    shape = (HEADS, part, WIDE)
-    half_spec = pl.BlockSpec((REPS, part, WIDE), lambda h: (h, 0, 0))
-    z0, z2, z13 = attention_call(
+            for n, out in enumerate((own_ref, pair_ref)):
+                out[rep, :, 0:HEAD_DIM] = num_held[rep, core ^ n].astype(BF)
+                out[rep, :, HEAD_DIM:] = den_held[rep, core ^ n].astype(BF)
+
+    shape = (HEADS, half, WIDE)
+    half_spec = pl.BlockSpec((REPS, half, WIDE), lambda h: (h, 0, 0))
+    own, pair = attention_call(
         attention,
         (block_table, lengths, parents),
         (*shares, cos, sin),
         [whole_block(shares[0].shape)] * nx + [whole_block(cos.shape)] * 2,
         cache_pool,
-        [shape, shape, (2,) + shape],
-        [
-            half_spec,
-            half_spec,
-            pl.BlockSpec((2, REPS, part, WIDE), lambda h: (0, h, 0, 0)),
-        ],
+        [shape, shape],
+        [half_spec, half_spec],
         [
             pltpu.VMEM((nx,) + shares[0].shape, BF),
-            pltpu.VMEM((REPS, nx, part, HEAD_DIM), F32),
-            pltpu.VMEM((REPS, nx, part, PAGE), F32),
+            pltpu.VMEM((REPS, 2, half, HEAD_DIM), F32),
+            pltpu.VMEM((REPS, 2, half, PAGE), F32),
         ],
     )
-    z13 = permute(z13, "gx", 1)
-
-    def pair_terms(z_ref, from_pair_ref, out_ref):
-        total = z_ref[...].astype(F32) + from_pair_ref[1].astype(F32)
+    pair = permute(pair, "gx", 1)
+
+    def pair_terms(own_ref, pair_ref, out_ref):
+        total = own_ref[...].astype(F32) + pair_ref[...].astype(F32)
         den = total[..., HEAD_DIM : HEAD_DIM + 1] + total[..., WIDE - 1 :]
         out_ref[..., 0:HEAD_DIM] = total[..., 0:HEAD_DIM].astype(BF)
         out_ref[..., HEAD_DIM:] = high_low(den, PAGE).astype(BF)
 
-    (z2,) = run("pair_terms", pair_terms, [(shape, BF)], (z2, z13))
-    z2 = permute(z2, "gx", 2)
-
-    def divide(z0_ref, z13_ref, z2_ref, *refs):
-        total = z0_ref[...].astype(F32) + z13_ref[0].astype(F32) + z2_ref[...].astype(F32)
+    (own,) = run("pair_terms", pair_terms, [(shape, BF)], (own, pair))
+    across = permute(own, "gx", 2)
+
+    def divide(own_ref, across_ref, out_ref):
+        total = own_ref[...].astype(F32) + across_ref[...].astype(F32)
         den = total[..., HEAD_DIM : HEAD_DIM + 1] + total[..., WIDE - 1 :]
-        held = refs[ny]
-        held[...] = total[..., 0:HEAD_DIM] / den
-        me = my("gy")
-        for m in range(ny):
-            refs[m][...] = held[me ^ m].astype(BF)
-
-    blocks = run(
-        "divide",
-        divide,
-        [((part, HEAD_DIM), BF)] * ny,
-        (z0, z13, z2),
-        scratch=[pltpu.VMEM((HEADS, part, HEAD_DIM), F32)],
-    )
-    blocks = trade(blocks, "gy")
-
-    def pack_heads(*refs):
-        for m in range(ny):
-            refs[ny][m] = refs[m][...]
-
-    (attended,) = run("pack_heads", pack_heads, [((ny, part, HEAD_DIM), BF)], blocks)
-    attended = gather_gx(attended)
-
-    def project_out(*refs):
-        w_ref, held = refs[nx], refs[-1]
-        me = my("gx")
-        for n in range(nx):
-            held[:, me ^ n] = refs[n][...].astype(F32)
-        flat = held[...].reshape(all_rows, HEAD_DIM).astype(BF)
-        sums = lax.dot_general(flat, w_ref[...], NT, preferred_element_type=F32).astype(BF)
-        for m in range(ny):
-            refs[nx + 1 + m][...] = sums[m * rows : (m + 1) * rows]
-
-    blocks = run(
-        "project_out",
-        project_out,
-        [((rows, width), BF)] * ny,
-        (*attended, w_out.T),
-        scratch=[pltpu.VMEM((ny, nx, part, HEAD_DIM), F32)],
-    )
-    blocks = trade(blocks, "gy")
-
-    def attn_sum(*refs):
-        x_ref, gain_ref, attn_ref, sums_ref = refs[ny:]
-        attn = sum(r[...].astype(F32) for r in refs[:ny])
+        out_ref[...] = (total[..., 0:HEAD_DIM] / den).astype(BF)
+
+    (attended,) = run("divide", divide, [((HEADS, half, HEAD_DIM), BF)], (own, across))
+    others = permute(attended, "gx", 1)
+
+    def project_out(own_ref, other_ref, w_ref, x_ref, gain_ref, attn_ref, sums_ref, held):
+        core = my("gx") & 1
+        held[core], held[1 - core] = own_ref[...], other_ref[...]
+        attn = jnp.zeros((rows, width), F32)
+        for head in range(HEADS):
+            flat = jnp.concatenate([held[0, head], held[1, head]], axis=0)
+            attn = attn + lax.dot_general(flat, w_ref[head], NT, preferred_element_type=F32)
         attn_ref[...] = attn
         x = x_ref[...].astype(F32)
         scaled = attn * (1.0 + gain_ref[1:2])
@@ -372,10 +341,11 @@
         sums_ref[...] = sums
 
     attn, sums = run(
-        "attn_sum",
-        attn_sum,
+        "project_out",
+        project_out,
         [((rows, width), F32), ((rows, PAGE), F32)],
-        (*blocks, x_own, norm_gains),
+        (attended, others, w_wide, x_own, norm_gains),
+        scratch=[pltpu.VMEM((2, HEADS, half, HEAD_DIM), BF)],
     )
     sums = trade([sums] * nx, "gx")
 
@@ -388,22 +358,27 @@
         square = jnp.maximum(square + 2.0 * scale * cross + scale * scale * scaled, 0.0)
         mixed_ref[...] = mixed
         scale = lax.rsqrt(square / D + EPSILON)
-        ff_ref[...] = (mixed * scale * (1.0 + gain_ref[2:3])).astype(BF)
+        ff_input = (mixed * scale * (1.0 + gain_ref[2:3])).astype(BF)
+        for m in range(ny):
+            ff_ref[m] = ff_input
 
     mixed, ff_input = run(
         "mix",
         mix,
-        [((rows, width), F32), ((rows, width), BF)],
+        [((rows, width), F32), ((ny, rows, width), BF)],
         (*sums, attn, x_own, norm_gains),
     )
-    blocks = trade([ff_input] * ny, "gy")
-
-    def gate_up(*refs):
-        w_refs, z0_ref, z2_ref, z13_ref, held = refs[ny : ny + 2], *refs[ny + 2 :]
+    ff_input = exchange(ff_input, "gy")
+
+    groups = ny // nx
+
+    def gate_up(ff_ref, gate_ref, up_ref, z0_ref, z2_ref, z13_ref):
         me = my("gx")
-        for m in range(ny):
-            held[m // 2, m % 2 * rows : (m % 2 + 1) * rows] = refs[m][...]
-        flat = jnp.concatenate([held[me ^ n] for n in range(nx)], axis=0)
+        flat = [
+            ff_ref[pl.ds((me ^ n) * groups, groups)].reshape(share_rows, width) for n in range(nx)
+        ]
+        flat = jnp.concatenate(flat, axis=0)
+        w_refs = gate_ref, up_ref
         for n, w_ref in enumerate(w_refs):
             sums = jnp.dot(flat, w_ref[...], preferred_element_type=F32).astype(BF)
             here = pl.ds(n * hidden, hidden)
@@ -415,8 +390,7 @@
         "gate_up",
         gate_up,
         [(shape, BF), (shape, BF), ((2,) + shape, BF)],
-        (*blocks, w_gate, w_up),
-        scratch=[pltpu.VMEM((nx, share_rows, width), BF)],
+        (ff_input, w_gate, w_up),
         limit=24,
     )
     z13 = permute(z13, "gx", 1)
@@ -432,30 +406,26 @@
     blocks = gather_gx(blocks)
 
     def project_down(*refs):
-        w_ref, held = refs[nx], refs[-1]
+        w_ref, out_ref = refs[nx:]
         me = my("gx")
         flat = jnp.concatenate([r[...] for r in refs[:nx]], axis=0)
         sums = lax.dot_general(flat, w_ref[...], NT, preferred_element_type=F32)
-        held[...] = sums.reshape(nx, share_rows, width).astype(BF)
-        for m in range(ny):
-            refs[nx + 1 + m][...] = held[me ^ (m // 2), m % 2 * rows : (m % 2 + 1) * rows]
-
-    blocks = run(
-        "project_down",
-        project_down,
-        [((rows, width), BF)] * ny,
-        (*blocks, w_down.T),
-        scratch=[pltpu.VMEM((nx, share_rows, width), BF)],
-    )
-    blocks = trade(blocks, "gy")
-
-    def down_sum(*refs):
-        down = sum(r[...].astype(F32) for r in refs[:ny])
-        refs[ny][...] = down
-        refs[ny + 1][...] = jnp.broadcast_to(row_sum(down * down), (rows, PAGE))
+        sums = sums.reshape(nx, groups, rows, width).astype(BF)
+        for n in range(nx):
+            out_ref[pl.ds((me ^ n) * groups, groups)] = sums[n]
+
+    (down,) = run(
+        "project_down", project_down, [((ny, rows, width), BF)], (*blocks, w_down.T)
+    )
+    down = exchange(down, "gy")
+
+    def down_sum(parts_ref, down_ref, sums_ref):
+        down = jnp.sum(parts_ref[...].astype(F32), axis=0)
+        down_ref[...] = down
+        sums_ref[...] = jnp.broadcast_to(row_sum(down * down), (rows, PAGE))
 
     down, sums = run(
-        "down_sum", down_sum, [((rows, width), F32), ((rows, PAGE), F32)], blocks
+        "down_sum", down_sum, [((rows, width), F32), ((rows, PAGE), F32)], (down,)
     )
     sums = trade([sums] * nx, "gx")
 
@@ -464,12 +434,10 @@
         square = sum(r[...] for r in refs[:nx])[:, 0:1]
         scale = lax.rsqrt(square / D + EPSILON)
         out = mixed_ref[...] + down_ref[...] * scale * (1.0 + gain_ref[3:4])
-        out_ref[...] = out.astype(BF)
-
-    (out,) = run(
-        "finish", finish, [((rows, width), BF)], (*sums, down, mixed, norm_gains)
-    )
-    return out.reshape(beams, steps, width)
+        out_ref[...] = out.reshape(beams, steps, width).astype(BF)
+
+    (out,) = run("finish", finish, [(inputs.shape, BF)], (*sums, down, mixed, norm_gains))
+    return out
 
 
 def body_general(

time: 158 us -> 141 us (0.89)
  starting transfers between devices: 82.1 us -> 14.7 us
  blocking collectives: 0 us -> 47.9 us
  between operations: 0.89 us -> 14.2 us
  waiting for transfers between devices: 55.6 us -> 42.4 us
  Pallas kernels: 10.9 us -> 12.5 us
    ppermute x63 -> x19, starting transfers between devices: 82.1 us -> 11.1 us  [permute(): return lax.ppermute(values, axis, [(i, i ^ m) for i in range(count)])]
    all_to_all x0 -> x3, blocking collectives: none -> 47.9 us  [exchange(): return lax.all_to_all(values, axes, split_axis=0, concat_axis=0, tiled=True)]
    ppermute x63 -> x19, waiting for transfers between devices: 55.6 us -> 34.5 us  [permute(): return lax.ppermute(values, axis, [(i, i ^ m) for i in range(count)])]
    all_to_all x0 -> x1, waiting for transfers between devices: none -> 7.11 us  [exchange(): return lax.all_to_all(values, axes, split_axis=0, concat_axis=0, tiled=True)]
    all_to_all x0 -> x1, starting transfers between devices: none -> 3.57 us  [exchange(): return lax.all_to_all(values, axes, split_axis=0, concat_axis=0, tiled=True)]
    unnamed x30, local copies, waits for them, and re-layouts: 5.74 us -> 7.46 us
    pallas_call x16 -> x15, Pallas kernels: 3.97 us -> 5.62 us  [run(): pl.pallas_call(kernel, out_shape=[jax.ShapeDtypeStruct(s, d) for s, d in...]
  transfers between devices with their start and end apart: 63 -> 21, of which waited for: 32 -> 16; matrix products, arithmetic and copies ran while one was open for 0% -> 1% of each run, Pallas kernels for 0% -> 6%
where the time goes in v4:
time: 141 us; the launch traced here: 140 us
  blocking collectives  47.9 us (34%)
  waiting for transfers between devices  42.4 us (30%)
  starting transfers between devices  14.7 us (10%)
  between operations  14.2 us (10%)
  Pallas kernels  12.5 us (9%)
  local copies, waits for them, and re-layouts  7.46 us (5%)
    all_to_all x3, blocking collectives, exchange(): return lax.all_to_all(values, axes, split_axis=0, concat_axis=0, tiled=True)  47.9 us
    ppermute x19, waiting for transfers between devices, permute(): return lax.ppermute(values, axis, [(i, i ^ m) for i in range(count)])  34.5 us
    ppermute x19, starting transfers between devices, permute(): return lax.ppermute(values, axis, [(i, i ^ m) for i in range(count)])  11.1 us
    unnamed x30, local copies, waits for them, and re-layouts  7.46 us
    all_to_all x1, waiting for transfers between devices, exchange(): return lax.all_to_all(values, axes, split_axis=0, concat_axis=0, tiled=True)  7.11 us
    pallas_call x1, Pallas kernels, attention_call(): pl.pallas_call(kernel, grid=(KV_HEADS,), in_specs=[smem] * len(scalars) +...  6.88 us
    pallas_call x15, Pallas kernels, run(): pl.pallas_call(kernel, out_shape=[jax.ShapeDtypeStruct(s, d) for s, d in...  5.62 us
    all_to_all x1, starting transfers between devices, exchange(): return lax.all_to_all(values, axes, split_axis=0, concat_axis=0, tiled=True)  3.57 us
  transfers between devices with their start and end apart: 21, of which 16 were waited for; matrix products, arithmetic and copies ran while one was open for 1% of the time, Pallas kernels for 6%

profile of v4, /device:TPU:0, one launch (start us, length us, event | category | flops | bytes accessed | tf_op | source)
XLA Modules:
  0.0 139.9 jit_solution(3758897700953589019)
XLA Ops:
  7.3 0.8 copy-done.11
  8.1 21.0 %all_to_all.20.x_ref = bf16[8,32,576]{2,1,0:T(8,128)(2,1)S(1)} all-to-all(bf16[8,32,576]{2,1,0:T(8,128)(2,1)S(1)} %get-tuple-element.21), channel_id=1, replica_groups=mesh['gx'=4,'gy'=8] {'gy'}, dimensions={0} | all-to-all | bytes 589824 | tf_op jit(solution)/shard_map/all_to_all | solution.py:38
  29.1 1.0 copy-done.4
  30.8 0.9 copy-done.8
  31.7 0.9 copy-done.9
  33.1 1.3 collective-permute-done.from_pair_ref.z13_ref
  34.5 2.0 %collective-permute-start.1 = (bf16[256,128]{1,0:T(8,128)(2,1)S(1)}, bf16[256,128]{1,0:T(8,128)(2,1)S(1)}, u32[]{:S(2)}, u32[]{:S(2)}) collective-permute-start(bf16[256,128]{1,0:T(8,128)(2,1)S(1)} %pair_sum.1), channel_id=1, source_target_pairs={{0,16},{8,24},{16,0},{24,8},{1,17},{9,25},{17,1},{25,9},{2,18},{10... | collective-permute-start | bytes 196616 | tf_op jit(solution)/shard_map/ppermute | solution.py:49
  36.5 2.4 %collective-permute-done.1.z2_ref = bf16[256,128]{1,0:T(8,128)(2,1)S(1)} collective-permute-done((bf16[256,128]{1,0:T(8,128)(2,1)S(1)}, bf16[256,128]{1,0:T(8,128)(2,1)S(1)}, u32[]{:S(2)}, u32[]{:S(2)}) %collective-permute-start.1) | collective-permute-done | bytes 65568 | tf_op jit(solution)/shard_map/ppermute | solution.py:49
  39.5 3.6 %all-to-all-start.1 = ((bf16[8,32,128]{2,1,0:T(8,128)(2,1)}), bf16[8,32,128]{2,1,0:T(8,128)(2,1)S(1)}, u32[]{:S(2)}, u32[]{:S(2)}) async-start(bf16[8,32,128]{2,1,0:T(8,128)(2,1)} %share_sum.1), calls=%async_computation.1 | async-start | bytes 131072 | tf_op jit(solution)/shard_map/all_to_all | solution.py:38
  43.8 7.1 %all-to-all-done.1.share_ref = bf16[8,32,128]{2,1,0:T(8,128)(2,1)S(1)} async-done(((bf16[8,32,128]{2,1,0:T(8,128)(2,1)}), bf16[8,32,128]{2,1,0:T(8,128)(2,1)S(1)}, u32[]{:S(2)}, u32[]{:S(2)}) %all-to-all-start.1) | async-done | bytes 65568 | tf_op jit(solution)/shard_map/all_to_all | solution.py:38
  51.0 1.7 %collective-permute-start.3 = (bf16[9,32,128]{2,1,0:T(8,128)(2,1)S(1)}, bf16[9,32,128]{2,1,0:T(8,128)(2,1)S(1)}, u32[]{:S(2)}, u32[]{:S(2)}) collective-permute-start(bf16[9,32,128]{2,1,0:T(8,128)(2,1)S(1)} %pack_shares.1.refs_3_), channel_id=1, source_target_pairs={{0,16},{8,24},{16,0},{24,8},{1,17},{9,25},{17,1},{25,9},{2,18},{10... | collective-permute-start | bytes 221192 | tf_op jit(solution)/shard_map/ppermute | solution.py:49
  52.6 2.7 %collective-permute-done.3.refs_5_ = bf16[9,32,128]{2,1,0:T(8,128)(2,1)S(1)} collective-permute-done((bf16[9,32,128]{2,1,0:T(8,128)(2,1)S(1)}, bf16[9,32,128]{2,1,0:T(8,128)(2,1)S(1)}, u32[]{:S(2)}, u32[]{:S(2)}) %collective-permute-start.3) | collective-permute-done | bytes 73760 | tf_op jit(solution)/shard_map/ppermute | solution.py:49
  57.2 6.9 %attention.1 = (bf16[8,16,384]{2,1,0:T(8,128)(2,1)}, bf16[8,16,384]{2,1,0:T(8,128)(2,1)}) custom-call(s32[1,33]{1,0:T(1,128)} %refs_0_.1, s32[1]{0:T(128)} %copy.14.refs_1_, s32[3,8]{1,0:T(4,128)} %refs_2_.1, bf16[9,32,128]{2,1,0:T(8,128)(2,1)} %copy-done.5, bf16[9,32,128]{2,1,0:T(8,128)(2,1)} %copy-done.13, bf16[9,32,128]{2,1,0:T(8,128)(2,1)} %copy-done.12, ...), custom_call_target="tpu_custom_call" | custom-call | tf_op jit(solution)/shard_map/attention/pallas_call | solution.py:161
  64.3 1.3 collective-permute-done.5.pair_ref
  65.6 0.9 copy-done.10
  66.7 1.7 %collective-permute-start.6 = (bf16[8,16,384]{2,1,0:T(8,128)(2,1)S(1)}, bf16[8,16,384]{2,1,0:T(8,128)(2,1)S(1)}, u32[]{:S(2)}, u32[]{:S(2)}) collective-permute-start(bf16[8,16,384]{2,1,0:T(8,128)(2,1)S(1)} %pair_terms.1.own_ref), channel_id=1, source_target_pairs={{0,16},{8,24},{16,0},{24,8},{1,17},{9,25},{17,1},{25,9},{2,18},{10... | collective-permute-start | bytes 294920 | tf_op jit(solution)/shard_map/ppermute | solution.py:49
  68.4 3.3 %collective-permute-done.6.across_ref = bf16[8,16,384]{2,1,0:T(8,128)(2,1)S(1)} collective-permute-done((bf16[8,16,384]{2,1,0:T(8,128)(2,1)S(1)}, bf16[8,16,384]{2,1,0:T(8,128)(2,1)S(1)}, u32[]{:S(2)}, u32[]{:S(2)}) %collective-permute-start.6) | collective-permute-done | bytes 98336 | tf_op jit(solution)/shard_map/ppermute | solution.py:49
  71.9 1.2 collective-permute-done.7.other_ref
  73.1 1.7 %copy-done = bf16[4608,256]{1,0:T(8,128)(2,1)S(1)} copy-done((bf16[4608,256]{1,0:T(8,128)(2,1)S(1)}, bf16[4608,256]{1,0:T(8,128)(2,1)}, u32[]{:S(2)}) %copy-start) | copy-done | bytes 2359320
  74.8 0.8 project_out.1
  75.6 1.4 %collective-permute-start.10 = (f32[32,128]{1,0:T(8,128)S(1)}, f32[32,128]{1,0:T(8,128)S(1)}, u32[]{:S(2)}, u32[]{:S(2)}) collective-permute-start(f32[32,128]{1,0:T(8,128)S(1)} %get-tuple-element.28.refs_0_), channel_id=1, source_target_pairs={{0,24},{8,16},{16,8},{24,0},{1,25},{9,17},{17,9},{25,1},{2,26},{10... | collective-permute-start | bytes 49160 | tf_op jit(solution)/shard_map/ppermute | solution.py:49
  77.9 1.0 collective-permute-done.10.refs_3_
  78.9 2.3 %collective-permute-done.9.refs_2_ = f32[32,128]{1,0:T(8,128)S(1)} collective-permute-done((f32[32,128]{1,0:T(8,128)S(1)}, f32[32,128]{1,0:T(8,128)S(1)}, u32[]{:S(2)}, u32[]{:S(2)}) %collective-permute-start.9) | collective-permute-done | bytes 16416 | tf_op jit(solution)/shard_map/ppermute | solution.py:49
  81.4 12.8 %all_to_all.21.ff_ref = bf16[8,32,576]{2,1,0:T(8,128)(2,1)S(1)} all-to-all(bf16[8,32,576]{2,1,0:T(8,128)(2,1)S(1)} %get-tuple-element.30), channel_id=1, replica_groups=mesh['gx'=4,'gy'=8] {'gy'}, dimensions={0} | all-to-all | bytes 589824 | tf_op jit(solution)/shard_map/all_to_all | solution.py:38
  94.2 1.2 gate_up.1
  95.5 2.0 %collective-permute-done.11.from_pair_ref.z13_ref = bf16[2,64,2304]{2,1,0:T(8,128)(2,1)S(1)} collective-permute-done((bf16[2,64,2304]{2,1,0:T(8,128)(2,1)S(1)}, bf16[2,64,2304]{2,1,0:T(8,128)(2,1)S(1)}, u32[]{:S(2)}, u32[]{:S(2)}) %collective-permute-start.11) | collective-permute-done | bytes 589856 | tf_op jit(solution)/shard_map/ppermute | solution.py:49
  98.3 8.4 %collective-permute-done.12.z2_ref = bf16[64,2304]{1,0:T(8,128)(2,1)S(1)} collective-permute-done((bf16[64,2304]{1,0:T(8,128)(2,1)S(1)}, bf16[64,2304]{1,0:T(8,128)(2,1)S(1)}, u32[]{:S(2)}, u32[]{:S(2)}) %collective-permute-start.12) | collective-permute-done | bytes 294944 | tf_op jit(solution)/shard_map/ppermute | solution.py:49
  107.6 4.5 %collective-permute-done.14.refs_2_ = bf16[64,1152]{1,0:T(8,128)(2,1)S(1)} collective-permute-done((bf16[64,1152]{1,0:T(8,128)(2,1)S(1)}, bf16[64,1152]{1,0:T(8,128)(2,1)S(1)}, u32[]{:S(2)}, u32[]{:S(2)}) %collective-permute-start.14) | collective-permute-done | bytes 147488 | tf_op jit(solution)/shard_map/ppermute | solution.py:49
  112.1 1.4 collective-permute-done.15.refs_3_
  114.2 14.0 %all_to_all.22.parts_ref = bf16[8,32,576]{2,1,0:T(8,128)(2,1)S(1)} all-to-all(bf16[8,32,576]{2,1,0:T(8,128)(2,1)S(1)} %project_down.1), channel_id=1, replica_groups=mesh['gx'=4,'gy'=8] {'gy'}, dimensions={0} | all-to-all | bytes 589824 | tf_op jit(solution)/shard_map/all_to_all | solution.py:38
  129.0 1.2 collective-permute-start.18
  130.2 2.1 %collective-permute-done.17.refs_2_ = f32[32,128]{1,0:T(8,128)S(1)} collective-permute-done((f32[32,128]{1,0:T(8,128)S(1)}, f32[32,128]{1,0:T(8,128)S(1)}, u32[]{:S(2)}, u32[]{:S(2)}) %collective-permute-start.17) | collective-permute-done | bytes 16416 | tf_op jit(solution)/shard_map/ppermute | solution.py:49
  (63 shorter events, 10.3 us)
Async XLA Ops:
  6.5 66.6 %all-gather.3.cloned.1.call-start = ((), (), s32[]{:S(2)}) async-start(), calls=%async_computation.4 | async-start | bytes 2654208 | tf_op jit(solution)/shard_map/all_gather | solution.py:209
  29.1 1.0 copy-start.4
  30.8 0.9 copy-start.8
  31.7 0.9 copy-start.9
  33.1 1.4 %collective-permute-start = (bf16[2,256,128]{2,1,0:T(8,128)(2,1)S(1)}, bf16[2,256,128]{2,1,0:T(8,128)(2,1)S(1)}, u32[]{:S(2)}, u32[]{:S(2)}) collective-permute-start(bf16[2,256,128]{2,1,0:T(8,128)(2,1)S(1)} %get-tuple-element.23), channel_id=1, source_target_pairs={{0,8},{8,0},{16,24},{24,16},{1,9},{9,1},{17,25},{25,17},{2,10},{10... | collective-permute-start | bytes 393224 | tf_op jit(solution)/shard_map/ppermute | solution.py:49
  34.5 4.4 %collective-permute-start.1 = (bf16[256,128]{1,0:T(8,128)(2,1)S(1)}, bf16[256,128]{1,0:T(8,128)(2,1)S(1)}, u32[]{:S(2)}, u32[]{:S(2)}) collective-permute-start(bf16[256,128]{1,0:T(8,128)(2,1)S(1)} %pair_sum.1), channel_id=1, source_target_pairs={{0,16},{8,24},{16,0},{24,8},{1,17},{9,25},{17,1},{25,9},{2,18},{10... | collective-permute-start | bytes 196616 | tf_op jit(solution)/shard_map/ppermute | solution.py:49
  39.5 11.3 %all-to-all-start.1 = ((bf16[8,32,128]{2,1,0:T(8,128)(2,1)}), bf16[8,32,128]{2,1,0:T(8,128)(2,1)S(1)}, u32[]{:S(2)}, u32[]{:S(2)}) async-start(bf16[8,32,128]{2,1,0:T(8,128)(2,1)} %share_sum.1), calls=%async_computation.1 | async-start | bytes 131072 | tf_op jit(solution)/shard_map/all_to_all | solution.py:38
  50.9 5.7 %copy-start.5 = (bf16[9,32,128]{2,1,0:T(8,128)(2,1)}, bf16[9,32,128]{2,1,0:T(8,128)(2,1)S(1)}, u32[]{:S(2)}) copy-start(bf16[9,32,128]{2,1,0:T(8,128)(2,1)S(1)} %pack_shares.1.refs_3_) | copy-start | bytes 221188
  51.0 4.4 %collective-permute-start.3 = (bf16[9,32,128]{2,1,0:T(8,128)(2,1)S(1)}, bf16[9,32,128]{2,1,0:T(8,128)(2,1)S(1)}, u32[]{:S(2)}, u32[]{:S(2)}) collective-permute-start(bf16[9,32,128]{2,1,0:T(8,128)(2,1)S(1)} %pack_shares.1.refs_3_), channel_id=1, source_target_pairs={{0,16},{8,24},{16,0},{24,8},{1,17},{9,25},{17,1},{25,9},{2,18},{10... | collective-permute-start | bytes 221192 | tf_op jit(solution)/shard_map/ppermute | solution.py:49
  52.6 3.5 %collective-permute-start.2 = (bf16[9,32,128]{2,1,0:T(8,128)(2,1)S(1)}, bf16[9,32,128]{2,1,0:T(8,128)(2,1)S(1)}, u32[]{:S(2)}, u32[]{:S(2)}) collective-permute-start(bf16[9,32,128]{2,1,0:T(8,128)(2,1)S(1)} %pack_shares.1.refs_3_), channel_id=1, source_target_pairs={{0,8},{8,0},{16,24},{24,16},{1,9},{9,1},{17,25},{25,17},{2,10},{10... | collective-permute-start | bytes 221192 | tf_op jit(solution)/shard_map/ppermute | solution.py:49
  55.3 1.3 copy-start.12
  55.4 1.3 collective-permute-start.4
  57.2 15.9 %copy-start.7 = (f32[4,576]{1,0:T(4,128)S(1)}, f32[4,576]{1,0:T(4,128)}, u32[]{:S(2)}) copy-start(f32[4,576]{1,0:T(4,128)} %refs_6_.3) | copy-start | bytes 27652
  64.1 1.5 %collective-permute-start.5 = (bf16[8,16,384]{2,1,0:T(8,128)(2,1)}, bf16[8,16,384]{2,1,0:T(8,128)(2,1)S(1)}, u32[]{:S(2)}, u32[]{:S(2)}) collective-permute-start(bf16[8,16,384]{2,1,0:T(8,128)(2,1)} %get-tuple-element.27), channel_id=1, source_target_pairs={{0,8},{8,0},{16,24},{24,16},{1,9},{9,1},{17,25},{25,17},{2,10},{10... | collective-permute-start | bytes 294920 | tf_op jit(solution)/shard_map/ppermute | solution.py:49
  65.6 0.9 copy-start.10
  66.7 4.9 %collective-permute-start.6 = (bf16[8,16,384]{2,1,0:T(8,128)(2,1)S(1)}, bf16[8,16,384]{2,1,0:T(8,128)(2,1)S(1)}, u32[]{:S(2)}, u32[]{:S(2)}) collective-permute-start(bf16[8,16,384]{2,1,0:T(8,128)(2,1)S(1)} %pair_terms.1.own_ref), channel_id=1, source_target_pairs={{0,16},{8,24},{16,0},{24,8},{1,17},{9,25},{17,1},{25,9},{2,18},{10... | collective-permute-start | bytes 294920 | tf_op jit(solution)/shard_map/ppermute | solution.py:49
  71.8 1.3 collective-permute-start.7
  73.1 1.7 %copy-start = (bf16[4608,256]{1,0:T(8,128)(2,1)S(1)}, bf16[4608,256]{1,0:T(8,128)(2,1)}, u32[]{:S(2)}) copy-start(bf16[4608,256]{1,0:T(8,128)(2,1)} %all-gather.3.cloned.1.call-done) | copy-start | bytes 7077892
  74.8 19.4 %copy-start.2 = (bf16[576,1152]{1,0:T(8,128)(2,1)S(1)}, bf16[576,1152]{1,0:T(8,128)(2,1)}, u32[]{:S(2)}) copy-start(bf16[576,1152]{1,0:T(8,128)(2,1)} %gate_ref.1) | copy-start | bytes 3981316
  74.8 19.4 %copy-start.3 = (bf16[576,1152]{1,0:T(8,128)(2,1)S(1)}, bf16[576,1152]{1,0:T(8,128)(2,1)}, u32[]{:S(2)}) copy-start(bf16[576,1152]{1,0:T(8,128)(2,1)} %up_ref.1) | copy-start | bytes 3981316
  75.6 3.2 %collective-permute-start.10 = (f32[32,128]{1,0:T(8,128)S(1)}, f32[32,128]{1,0:T(8,128)S(1)}, u32[]{:S(2)}, u32[]{:S(2)}) collective-permute-start(f32[32,128]{1,0:T(8,128)S(1)} %get-tuple-element.28.refs_0_), channel_id=1, source_target_pairs={{0,24},{8,16},{16,8},{24,0},{1,25},{9,17},{17,9},{25,1},{2,26},{10... | collective-permute-start | bytes 49160 | tf_op jit(solution)/shard_map/ppermute | solution.py:49
  77.1 1.8 %collective-permute-start.8 = (f32[32,128]{1,0:T(8,128)S(1)}, f32[32,128]{1,0:T(8,128)S(1)}, u32[]{:S(2)}, u32[]{:S(2)}) collective-permute-start(f32[32,128]{1,0:T(8,128)S(1)} %get-tuple-element.28.refs_0_), channel_id=1, source_target_pairs={{0,8},{8,0},{16,24},{24,16},{1,9},{9,1},{17,25},{25,17},{2,10},{10... | collective-permute-start | bytes 49160 | tf_op jit(solution)/shard_map/ppermute | solution.py:49
  77.4 3.7 %collective-permute-start.9 = (f32[32,128]{1,0:T(8,128)S(1)}, f32[32,128]{1,0:T(8,128)S(1)}, u32[]{:S(2)}, u32[]{:S(2)}) collective-permute-start(f32[32,128]{1,0:T(8,128)S(1)} %get-tuple-element.28.refs_0_), channel_id=1, source_target_pairs={{0,16},{8,24},{16,0},{24,8},{1,17},{9,25},{17,1},{25,9},{2,18},{10... | collective-permute-start | bytes 49160 | tf_op jit(solution)/shard_map/ppermute | solution.py:49
  95.4 18.1 %copy-start.1 = (bf16[1152,576]{0,1:T(8,128)(2,1)S(1)}, bf16[1152,576]{0,1:T(8,128)(2,1)}, u32[]{:S(2)}) copy-start(bf16[1152,576]{0,1:T(8,128)(2,1)} %param.25) | copy-start | bytes 3981316
  95.4 2.1 %collective-permute-start.11 = (bf16[2,64,2304]{2,1,0:T(8,128)(2,1)S(1)}, bf16[2,64,2304]{2,1,0:T(8,128)(2,1)S(1)}, u32[]{:S(2)}, u32[]{:S(2)}) collective-permute-start(bf16[2,64,2304]{2,1,0:T(8,128)(2,1)S(1)} %get-tuple-element.32), channel_id=1, source_target_pairs={{0,8},{8,0},{16,24},{24,16},{1,9},{9,1},{17,25},{25,17},{2,10},{10... | collective-permute-start | bytes 1769480 | tf_op jit(solution)/shard_map/ppermute | solution.py:49
  97.6 9.1 %collective-permute-start.12 = (bf16[64,2304]{1,0:T(8,128)(2,1)S(1)}, bf16[64,2304]{1,0:T(8,128)(2,1)S(1)}, u32[]{:S(2)}, u32[]{:S(2)}) collective-permute-start(bf16[64,2304]{1,0:T(8,128)(2,1)S(1)} %pair_sum_ff.1), channel_id=1, source_target_pairs={{0,16},{8,24},{16,0},{24,8},{1,17},{9,25},{17,1},{25,9},{2,18},{10... | collective-permute-start | bytes 884744 | tf_op jit(solution)/shard_map/ppermute | solution.py:49
  106.9 5.2 %collective-permute-start.14 = (bf16[64,1152]{1,0:T(8,128)(2,1)S(1)}, bf16[64,1152]{1,0:T(8,128)(2,1)S(1)}, u32[]{:S(2)}, u32[]{:S(2)}) collective-permute-start(bf16[64,1152]{1,0:T(8,128)(2,1)S(1)} %activate.1.refs_0_), channel_id=1, source_target_pairs={{0,16},{8,24},{16,0},{24,8},{1,17},{9,25},{17,1},{25,9},{2,18},{10... | collective-permute-start | bytes 442376 | tf_op jit(solution)/shard_map/ppermute | solution.py:49
  107.6 4.5 %collective-permute-start.13 = (bf16[64,1152]{1,0:T(8,128)(2,1)S(1)}, bf16[64,1152]{1,0:T(8,128)(2,1)S(1)}, u32[]{:S(2)}, u32[]{:S(2)}) collective-permute-start(bf16[64,1152]{1,0:T(8,128)(2,1)S(1)} %activate.1.refs_0_), channel_id=1, source_target_pairs={{0,8},{8,0},{16,24},{24,16},{1,9},{9,1},{17,25},{25,17},{2,10},{10... | collective-permute-start | bytes 442376 | tf_op jit(solution)/shard_map/ppermute | solution.py:49
  112.1 1.4 collective-permute-start.15
  128.3 1.9 %collective-permute-start.16 = (f32[32,128]{1,0:T(8,128)S(1)}, f32[32,128]{1,0:T(8,128)S(1)}, u32[]{:S(2)}, u32[]{:S(2)}) collective-permute-start(f32[32,128]{1,0:T(8,128)S(1)} %get-tuple-element.34.refs_0_), channel_id=1, source_target_pairs={{0,8},{8,0},{16,24},{24,16},{1,9},{9,1},{17,25},{25,17},{2,10},{10... | collective-permute-start | bytes 49160 | tf_op jit(solution)/shard_map/ppermute | solution.py:49
  128.3 3.9 %collective-permute-start.17 = (f32[32,128]{1,0:T(8,128)S(1)}, f32[32,128]{1,0:T(8,128)S(1)}, u32[]{:S(2)}, u32[]{:S(2)}) collective-permute-start(f32[32,128]{1,0:T(8,128)S(1)} %get-tuple-element.34.refs_0_), channel_id=1, source_target_pairs={{0,16},{8,24},{16,0},{24,8},{1,17},{9,25},{17,1},{25,9},{2,18},{10... | collective-permute-start | bytes 49160 | tf_op jit(solution)/shard_map/ppermute | solution.py:49
  129.0 3.3 %collective-permute-start.18 = (f32[32,128]{1,0:T(8,128)S(1)}, f32[32,128]{1,0:T(8,128)S(1)}, u32[]{:S(2)}, u32[]{:S(2)}) collective-permute-start(f32[32,128]{1,0:T(8,128)S(1)} %get-tuple-element.34.refs_0_), channel_id=1, source_target_pairs={{0,24},{8,16},{16,8},{24,0},{1,25},{9,17},{17,9},{25,1},{2,26},{10... | collective-permute-start | bytes 49160 | tf_op jit(solution)/shard_map/ppermute | solution.py:49
  (4 other events, 2.7 us)
Sparse Core Ops, SparseCore 0:
  9.5 56.6 all-gather.2

commit v5 on v4

--- a/solution.py
+++ b/solution.py
@@ -22,12 +22,17 @@
 F32 = jnp.float32
 MIB = 1024 * 1024
 NT = (((1,), (1,)), ((), ()))
-
-
-def run(name, kernel, outs, args, scratch=(), limit=16):
+IN_HBM = pl.BlockSpec(memory_space=pltpu.HBM)
+IN_SMEM = pl.BlockSpec(memory_space=pltpu.SMEM)
+
+
+def run(name, kernel, outs, args, scratch=(), limit=16, specs=None):
+    specs = specs or {}
+    vmem = pl.BlockSpec(memory_space=pltpu.VMEM)
     return pl.pallas_call(
         kernel,
         out_shape=[jax.ShapeDtypeStruct(s, d) for s, d in outs],
+        in_specs=[specs.get(n, vmem) for n in range(len(args))],
         scratch_shapes=scratch,
         compiler_params=pltpu.CompilerParams(vmem_limit_bytes=limit * MIB),
         name=name,
@@ -73,107 +78,103 @@
     return jnp.sum(v, axis=-1, keepdims=True)
 
 
-def attend(shares, squares, refs):
-    table_ref, length_ref, parents_ref, cos_ref, sin_ref, pool_ref, page_ref = refs
-    first_owner = lax.axis_index("gx") * pool_ref.shape[1]
-    length = length_ref[0]
-    first_page = jnp.maximum(length - WINDOW + 1, 0) // PAGE
+def make_tables(table, lengths, parents, slots, rows, steps):
+    def tables(table_ref, length_ref, parents_ref, cached_ref, own_ref, page_ref):
+        first_owner = lax.axis_index("gx") * slots
+        length = length_ref[0]
+        first_page = jnp.maximum(length - WINDOW + 1, 0) // PAGE
+        for slot in range(slots + 1):
+            page_ref[slot] = -1
+        for j in range(table_ref.shape[1]):
+            slot = table_ref[0, j] - first_owner
+            page_ref[jnp.where((slot >= 0) & (slot < slots), slot, slots)] = j
+        step = lax.broadcasted_iota(jnp.int32, (8, PAGE), 0) % steps
+        lane = lax.broadcasted_iota(jnp.int32, (8, PAGE), 1)
+        for slot in range(slots):
+            page = page_ref[slot]
+            position = lane + jnp.where(page >= 0, (first_page + page) * PAGE, 2**30)
+            seen = (position < length) & (position >= length + step - (WINDOW - 1))
+            cached_ref[:, slot * PAGE : (slot + 1) * PAGE] = jnp.where(seen, 1.0, 0.0)
+
+        shape = (REPS * rows, rows)
+        row = lax.broadcasted_iota(jnp.int32, shape, 0) % rows
+        column = lax.broadcasted_iota(jnp.int32, shape, 1)
+        row_step, column_step, column_beam = row % steps, column % steps, column // steps
+        current = row // steps
+        visible = jnp.zeros(shape, jnp.bool_)
+        for j in range(steps - 1, -1, -1):
+            if j < steps - 1:
+                parent = jnp.zeros(shape, jnp.int32)
+                for beam in range(BEAM):
+                    parent = jnp.where(current == beam, parents_ref[j, beam], parent)
+                current = jnp.where(row_step > j, parent, current)
+            visible = visible | ((column_step == j) & (row_step >= j) & (column_beam == current))
+        visible = visible & (lax.axis_index("gx") == 0)
+        own_ref[...] = jnp.where(visible, 1.0, 0.0)
+
+    return run(
+        "tables",
+        tables,
+        [((8, slots * PAGE), F32), ((REPS * rows, rows), F32)],
+        (table, lengths, parents),
+        scratch=[pltpu.SMEM((slots + 1,), jnp.int32)],
+        specs={0: IN_SMEM, 1: IN_SMEM, 2: IN_SMEM},
+    )
+
+
+def attend(shares, squares, tables, pool_ref, kept, store):
+    cos_ref, sin_ref, cached_ref, own_ref = tables
+    keys_ref, sems = kept
+    slots = pool_ref.shape[1]
+    rows = cos_ref.shape[0]
+    copies = []
+    for head in range(KV_HEADS):
+        here = pool_ref.at[:, :, :, head * HEAD_DIM : (head + 1) * HEAD_DIM]
+        copies.append(pltpu.make_async_copy(here, keys_ref.at[head], sems.at[head]))
+        copies[-1].start()
     square = jnp.sum(squares.astype(F32), axis=0)
     square = square[:, 0:1] + square[:, HALF // 2 : HALF // 2 + 1]
     scale = lax.rsqrt(square / D + EPSILON)
-    cos, sin = cos_ref[...], sin_ref[...]
-    rows = cos.shape[0]
-    reps = REPS
-    steps = rows // BEAM
-    slots = pool_ref.shape[1]
+    cos, sin = cos_ref[...] * scale, sin_ref[...] * scale
+    cached, own = cached_ref[...], own_ref[...]
 
     def rotated(u, w):
-        u, w = u.astype(F32) * scale, w.astype(F32) * scale
+        u, w = u.astype(F32), w.astype(F32)
         return u * cos - w * sin, w * cos + u * sin
 
-    query = []
-    for rep in range(reps):
-        u, w = rotated(shares(0, rep), shares(1, rep))
-        query.append(jnp.concatenate([u, w], axis=1) * HEAD_DIM ** (-0.5))
-    query = jnp.concatenate(query, axis=0).astype(BF)
-    key_step = jnp.concatenate(rotated(shares(2, 0), shares(2, 1)), axis=1).astype(BF)
-    value_step = jnp.concatenate(
-        [shares(3, 0).astype(F32) * scale, shares(3, 1).astype(F32) * scale], axis=1
-    ).astype(BF)
-
-    for slot in range(slots):
-        page_ref[slot] = -1
-
-    def place(j, carry):
-        slot = table_ref[0, j] - first_owner
-
-        @pl.when((slot >= 0) & (slot < slots))
-        def _():
-            page_ref[slot] = j
-
-        return carry
-
-    lax.fori_loop(0, table_ref.shape[1], place, 0)
-    lane = lax.broadcasted_iota(jnp.int32, (1, PAGE), 1)
-    far = jnp.int32(2**30)
-    position = jnp.concatenate(
-        [
-            lane + jnp.where(page_ref[s] >= 0, (first_page + page_ref[s]) * PAGE, far)
-            for s in range(slots)
-        ],
-        axis=1,
-    )
-    step_of = lax.broadcasted_iota(jnp.int32, (reps * rows, 1), 0) % steps
-    lower = length + step_of - (WINDOW - 1)
-    seen = (position < length) & (position >= lower)
-    keys = pool_ref[0].reshape(slots * PAGE, HEAD_DIM)
-    values = pool_ref[1].reshape(slots * PAGE, HEAD_DIM)
-    scores = lax.dot_general(query, keys, NT, preferred_element_type=F32)
-    weights = jnp.where(seen, weight_of(scores), 0.0)
-    den = jnp.sum(weights, axis=-1, keepdims=True)
-    num = jnp.dot(weights.astype(BF), values, preferred_element_type=F32)
-
-    shape = (reps * rows, rows)
-    row = lax.broadcasted_iota(jnp.int32, shape, 0) % rows
-    column = lax.broadcasted_iota(jnp.int32, shape, 1)
-    row_step, column_step, column_beam = row % steps, column % steps, column // steps
-    current = row // steps
-    visible = jnp.zeros(shape, jnp.bool_)
-    for j in range(steps - 1, -1, -1):
-        if j < steps - 1:
-            parent = jnp.zeros(shape, jnp.int32)
-            for beam in range(BEAM):
-                parent = jnp.where(current == beam, parents_ref[j, beam], parent)
-            current = jnp.where(row_step > j, parent, current)
-        visible = visible | ((column_step == j) & (row_step >= j) & (column_beam == current))
-    visible = visible & (lax.axis_index("gx") == 0)
-    scores = lax.dot_general(query, key_step, NT, preferred_element_type=F32)
-    weights = jnp.where(visible, weight_of(scores), 0.0)
-    den = den + jnp.sum(weights, axis=-1, keepdims=True)
-    num = num + jnp.dot(weights.astype(BF), value_step, preferred_element_type=F32)
-
-    return num, den
-
-
-def attention_call(kernel, scalars, blocks, block_specs, pool, outs, out_specs, scratch):
-    slots = pool.shape[1]
-    smem = pl.BlockSpec(memory_space=pltpu.SMEM)
-    return pl.pallas_call(
-        kernel,
-        grid=(KV_HEADS,),
-        in_specs=[smem] * len(scalars)
-        + block_specs
-        + [pl.BlockSpec((2, slots, PAGE, HEAD_DIM), lambda h: (0, 0, 0, h))],
-        out_specs=out_specs,
-        out_shape=[jax.ShapeDtypeStruct(s, BF) for s in outs],
-        scratch_shapes=[pltpu.SMEM((slots,), jnp.int32)] + scratch,
-        compiler_params=pltpu.CompilerParams(vmem_limit_bytes=58 * MIB),
-        name="attention",
-    )(*scalars, *blocks, pool)
-
-
-def whole_block(shape):
-    return pl.BlockSpec(shape, lambda h: (0,) * len(shape))
+    for head in range(KV_HEADS):
+        query = []
+        for rep in range(REPS):
+            u, w = rotated(shares(0, REPS * head + rep), shares(1, REPS * head + rep))
+            query.append(jnp.concatenate([u, w], axis=1) * HEAD_DIM ** (-0.5))
+        query = jnp.concatenate(query, axis=0).astype(BF)
+        first, second = 2 * head, 2 * head + 1
+        key_step = rotated(shares(2, first), shares(2, second))
+        key_step = jnp.concatenate(key_step, axis=1).astype(BF)
+        value_step = [shares(3, n).astype(F32) * scale for n in (first, second)]
+        value_step = jnp.concatenate(value_step, axis=1).astype(BF)
+
+        scores = lax.dot_general(query, key_step, NT, preferred_element_type=F32)
+        weights = weight_of(scores) * own
+        den = row_sum(weights)
+        num = jnp.dot(weights.astype(BF), value_step, preferred_element_type=F32)
+
+        copies[head].wait()
+        keys = keys_ref[head, 0].reshape(slots * PAGE, HEAD_DIM)
+        values = keys_ref[head, 1].reshape(slots * PAGE, HEAD_DIM)
+        scores = lax.dot_general(query, keys, NT, preferred_element_type=F32)
+        weights = weight_of(scores).reshape(REPS * rows // 8, 8, slots * PAGE) * cached[None]
+        weights = weights.reshape(REPS * rows, slots * PAGE)
+        den = den + row_sum(weights)
+        num = num + jnp.dot(weights.astype(BF), values, preferred_element_type=F32)
+        store(head, num, den)
+
+
+def key_scratch(pool):
+    return [
+        pltpu.VMEM((KV_HEADS, 2) + pool.shape[1:3] + (HEAD_DIM,), BF),
+        pltpu.SemaphoreType.DMA((KV_HEADS,)),
+    ]
 
 
 def rope_tables(lengths, rows, steps):
@@ -206,7 +207,7 @@
     share_rows = all_rows // nx
     hidden = w_gate.shape[1]
     cos, sin = rope_tables(lengths, rows, steps)
-    w_wide = lax.all_gather(w_out.T, "gy", axis=0)
+    tables = make_tables(block_table, lengths, parents, cache_pool.shape[1], rows, steps)
 
     def my(axis):
         return lax.axis_index(axis)
@@ -222,12 +223,28 @@
     )
     x_all = exchange(x_all, "gy")
 
-    def project(x_ref, gain_ref, q_ref, k_ref, v_ref, z0_ref, z2_ref, z13_ref, held):
+    w_blocks = [None] * ny
+    w_blocks[0], _ = lax.optimization_barrier((w_out.T, x_all))
+    for m in (4, 2, 1):
+        w_blocks[m] = permute(w_blocks[0], "gy", m)
+
+    def project(x_ref, gain_hbm, q_hbm, k_hbm, v_hbm, z0_ref, z2_ref, z13_ref, *kept):
+        held, gain_ref, q_ref, k_ref, v_ref, sems = kept
+        pairs = (gain_hbm, gain_ref), (q_hbm, q_ref), (k_hbm, k_ref), (v_hbm, v_ref)
+        copies = [
+            pltpu.make_async_copy(src, dst, sems.at[n]) for n, (src, dst) in enumerate(pairs)
+        ]
+        for copy in copies:
+            copy.start()
         x = x_ref[...].reshape(all_rows, width).astype(F32)
+        copies[0].wait()
         flat = (x * (1.0 + gain_ref[0:1])).astype(BF)
+        copies[1].wait()
         query = jnp.dot(flat, q_ref[...], preferred_element_type=F32).astype(BF)
         held[0], held[1] = query[:, :HALF], query[:, HALF:]
+        copies[2].wait()
         held[2] = jnp.dot(flat, k_ref[...], preferred_element_type=F32).astype(BF)
+        copies[3].wait()
         held[3] = jnp.dot(flat, v_ref[...], preferred_element_type=F32).astype(BF)
         me = my("gx")
         z0_ref[...], z2_ref[...] = held[me], held[me ^ 2]
@@ -239,7 +256,13 @@
         project,
         [(shape, BF), (shape, BF), ((2,) + shape, BF)],
         (x_all, norm_gains, w_query, w_key, w_value),
-        scratch=[pltpu.VMEM((nx,) + shape, BF)],
+        scratch=[
+            pltpu.VMEM((nx,) + shape, BF),
+            pltpu.VMEM(norm_gains.shape, F32),
+            *[pltpu.VMEM(w.shape, BF) for w in (w_query, w_key, w_value)],
+            pltpu.SemaphoreType.DMA((4,)),
+        ],
+        specs={n: IN_HBM for n in range(1, 5)},
     )
     z13 = permute(z13, "gx", 1)
 
@@ -256,6 +279,10 @@
 
     (shares,) = run("share_sum", share_sum, [((ny, rows, HALF), BF)], (z0, z13, z2))
     shares = exchange(shares, "gy")
+    _, (w_late, w_later) = lax.optimization_barrier((shares, (w_blocks[4], w_blocks[2])))
+    w_blocks[6] = permute(w_late, "gy", 2)
+    w_blocks[5] = permute(w_late, "gy", 1)
+    w_blocks[3] = permute(w_later, "gy", 1)
 
     def pack_shares(share_ref, x_ref, out_ref):
         x = x_ref[...].astype(F32)
@@ -266,45 +293,48 @@
     shares = gather_gx(shares)
 
     def attention(*refs):
-        table, length, parent, a0, a1, a2, a3, cos_ref, sin_ref, pool_ref = refs[:10]
-        own_ref, pair_ref, page_ref, held, num_held, den_held = refs[10:]
+        a_refs, tables, pool_ref, outs = refs[:nx], refs[nx : nx + 4], refs[nx + 4], refs[nx + 5 :]
+        own_ref, pair_ref, keys_ref, sems, held, num_held, den_held = outs
         me = my("gx")
-        h = pl.program_id(0)
-
-        @pl.when(h == 0)
-        def _():
-            for n, ref in enumerate((a0, a1, a2, a3)):
-                held[me ^ n] = ref[...]
-
-        num, den = attend(
-            lambda share, which: held[share, 2 * h + which],
+        core = me & 1
+        for n, ref in enumerate(a_refs):
+            held[me ^ n] = ref[...]
+
+        def store(head, num, den):
+            num_held[head] = num.reshape(REPS, 2, half, HEAD_DIM)
+            den_held[head] = high_low(den, PAGE).reshape(REPS, 2, half, PAGE)
+            for rep in range(REPS):
+                for n, out in enumerate((own_ref, pair_ref)):
+                    at = REPS * head + rep
+                    out[at, :, 0:HEAD_DIM] = num_held[head, rep, core ^ n].astype(BF)
+                    out[at, :, HEAD_DIM:] = den_held[head, rep, core ^ n].astype(BF)
+
+        attend(
+            lambda share, which: held[share, which],
             held[:, ny],
-            (table, length, parent, cos_ref, sin_ref, pool_ref, page_ref),
+            tables,
+            pool_ref,
+            (keys_ref, sems),
+            store,
         )
-        num_held[...] = num.reshape(REPS, 2, half, HEAD_DIM)
-        den_held[...] = high_low(den, PAGE).reshape(REPS, 2, half, PAGE)
-        core = me & 1
-        for rep in range(REPS):
-            for n, out in enumerate((own_ref, pair_ref)):
-                out[rep, :, 0:HEAD_DIM] = num_held[rep, core ^ n].astype(BF)
-                out[rep, :, HEAD_DIM:] = den_held[rep, core ^ n].astype(BF)
 
     shape = (HEADS, half, WIDE)
-    half_spec = pl.BlockSpec((REPS, half, WIDE), lambda h: (h, 0, 0))
-    own, pair = attention_call(
+    own, pair = run(
+        "attention",
         attention,
-        (block_table, lengths, parents),
-        (*shares, cos, sin),
-        [whole_block(shares[0].shape)] * nx + [whole_block(cos.shape)] * 2,
-        cache_pool,
-        [shape, shape],
-        [half_spec, half_spec],
-        [
+        [(shape, BF), (shape, BF)],
+        (*shares, cos, sin, *tables, cache_pool),
+        scratch=key_scratch(cache_pool)
+        + [
             pltpu.VMEM((nx,) + shares[0].shape, BF),
-            pltpu.VMEM((REPS, 2, half, HEAD_DIM), F32),
-            pltpu.VMEM((REPS, 2, half, PAGE), F32),
+            pltpu.VMEM((KV_HEADS, REPS, 2, half, HEAD_DIM), F32),
+            pltpu.VMEM((KV_HEADS, REPS, 2, half, PAGE), F32),
         ],
-    )
+        limit=24,
+        specs={nx + 4: IN_HBM},
+    )
+    _, w_last = lax.optimization_barrier((own, w_blocks[6]))
+    w_blocks[7] = permute(w_last, "gy", 1)
     pair = permute(pair, "gx", 1)
 
     def pair_terms(own_ref, pair_ref, out_ref):
@@ -324,13 +354,15 @@
     (attended,) = run("divide", divide, [((HEADS, half, HEAD_DIM), BF)], (own, across))
     others = permute(attended, "gx", 1)
 
-    def project_out(own_ref, other_ref, w_ref, x_ref, gain_ref, attn_ref, sums_ref, held):
+    def project_out(own_ref, other_ref, x_ref, gain_ref, *refs):
+        w_refs, (attn_ref, sums_ref, held) = refs[:ny], refs[ny:]
         core = my("gx") & 1
         held[core], held[1 - core] = own_ref[...], other_ref[...]
+        me = my("gy")
         attn = jnp.zeros((rows, width), F32)
-        for head in range(HEADS):
-            flat = jnp.concatenate([held[0, head], held[1, head]], axis=0)
-            attn = attn + lax.dot_general(flat, w_ref[head], NT, preferred_element_type=F32)
+        for m, w_ref in enumerate(w_refs):
+            flat = jnp.concatenate([held[0, me ^ m], held[1, me ^ m]], axis=0)
+            attn = attn + lax.dot_general(flat, w_ref[...], NT, preferred_element_type=F32)
         attn_ref[...] = attn
         x = x_ref[...].astype(F32)
         scaled = attn * (1.0 + gain_ref[1:2])
@@ -344,7 +376,7 @@
         "project_out",
         project_out,
         [((rows, width), F32), ((rows, PAGE), F32)],
-        (attended, others, w_wide, x_own, norm_gains),
+        (attended, others, x_own, norm_gains, *w_blocks),
         scratch=[pltpu.VMEM((2, HEADS, half, HEAD_DIM), BF)],
     )
     sums = trade([sums] * nx, "gx")
@@ -487,33 +519,34 @@
     cos, sin = rope_tables(lengths, rows, steps)
 
     def attention(*refs):
-        table, length, parent, g_ref, square_ref, cos_ref, sin_ref, pool_ref = refs[:8]
-        out_ref, page_ref = refs[8:]
-        num, den = attend(
+        g_ref, square_ref, tables, pool_ref = refs[0], refs[1], refs[2:6], refs[6]
+        out_ref, keys_ref, sems = refs[7:]
+
+        def store(head, num, den):
+            den = high_low(den, PAGE)
+            for rep in range(REPS):
+                here = slice(rep * rows, (rep + 1) * rows)
+                out_ref[REPS * head + rep, :, 0:HEAD_DIM] = num[here].astype(BF)
+                out_ref[REPS * head + rep, :, HEAD_DIM:] = den[here].astype(BF)
+
+        attend(
             lambda share, which: g_ref[share, which],
             square_ref[...],
-            (table, length, parent, cos_ref, sin_ref, pool_ref, page_ref),
+            tables,
+            pool_ref,
+            (keys_ref, sems),
+            store,
         )
-        den = high_low(den, PAGE)
-        for rep in range(REPS):
-            here = slice(rep * rows, (rep + 1) * rows)
-            out_ref[rep, :, 0:HEAD_DIM] = num[here].astype(BF)
-            out_ref[rep, :, HEAD_DIM:] = den[here].astype(BF)
-
-    (terms,) = attention_call(
+
+    tables = make_tables(block_table, lengths, parents, cache_pool.shape[1], rows, steps)
+    (terms,) = run(
+        "attention",
         attention,
-        (block_table, lengths, parents),
-        (shares, squares, cos, sin),
-        [
-            pl.BlockSpec((4, 2, rows, HALF), lambda h: (0, h, 0, 0)),
-            whole_block(squares.shape),
-            whole_block(cos.shape),
-            whole_block(sin.shape),
-        ],
-        cache_pool,
-        [(HEADS, rows, WIDE)],
-        [pl.BlockSpec((REPS, rows, WIDE), lambda h: (h, 0, 0))],
-        [],
+        [((HEADS, rows, WIDE), BF)],
+        (shares, squares, cos, sin, *tables, cache_pool),
+        scratch=key_scratch(cache_pool),
+        limit=24,
+        specs={6: IN_HBM},
     )
     num = terms[..., :HEAD_DIM].transpose(1, 0, 2).reshape(nx, part, ny, head_part)
     den = terms[..., HEAD_DIM :: PAGE // 2].transpose(1, 0, 2)

time: 141 us -> 135 us (0.957)
  between operations: 14.2 us -> 0.88 us
  waiting for transfers between devices: 42.4 us -> 48.6 us
  starting transfers between devices: 14.7 us -> 20.8 us
  blocking collectives: 47.9 us -> 46.1 us
  Pallas kernels: 12.5 us -> 10.9 us
    ppermute x19 -> x26, waiting for transfers between devices: 34.5 us -> 42.2 us  [permute(): return lax.ppermute(values, axis, [(i, i ^ m) for i in range(count)])]
    pallas_call x1 -> x0, Pallas kernels: 6.88 us -> none  [attention_call(): pl.pallas_call(kernel, grid=(KV_HEADS,), in_specs=[smem] * len(scalars) +...]
    ppermute x19 -> x26, starting transfers between devices: 11.1 us -> 16.9 us  [permute(): return lax.ppermute(values, axis, [(i, i ^ m) for i in range(count)])]
    pallas_call x15 -> x17, Pallas kernels: 5.62 us -> 10.9 us  [run(): pl.pallas_call(kernel, out_shape=[jax.ShapeDtypeStruct(s, d) for s, d in...]
    all_to_all x3, blocking collectives: 47.9 us -> 46.1 us  [exchange(): return lax.all_to_all(values, axes, split_axis=0, concat_axis=0, tiled=True)]
    unnamed x30 -> x26, local copies, waits for them, and re-layouts: 7.46 us -> 6.83 us
  transfers between devices with their start and end apart: 21 -> 27, of which waited for: 16 -> 15; matrix products, arithmetic and copies ran while one was open for 1% -> 0% of each run, Pallas kernels for 6% -> 4%
where the time goes in v5:
time: 135 us; the launch traced here: 134 us
  waiting for transfers between devices  48.6 us (36%)
  blocking collectives  46.1 us (34%)
  starting transfers between devices  20.8 us (15%)
  Pallas kernels  10.9 us (8%)
  local copies, waits for them, and re-layouts  6.83 us (5%)
    all_to_all x3, blocking collectives, exchange(): return lax.all_to_all(values, axes, split_axis=0, concat_axis=0, tiled=True)  46.1 us
    ppermute x26, waiting for transfers between devices, permute(): return lax.ppermute(values, axis, [(i, i ^ m) for i in range(count)])  42.2 us
    ppermute x26, starting transfers between devices, permute(): return lax.ppermute(values, axis, [(i, i ^ m) for i in range(count)])  16.9 us
    pallas_call x17, Pallas kernels, run(): pl.pallas_call(kernel, out_shape=[jax.ShapeDtypeStruct(s, d) for s, d in...  10.9 us
    unnamed x26, local copies, waits for them, and re-layouts  6.83 us
    all_to_all x1, waiting for transfers between devices, exchange(): return lax.all_to_all(values, axes, split_axis=0, concat_axis=0, tiled=True)  6.42 us
    all_to_all x1, starting transfers between devices, exchange(): return lax.all_to_all(values, axes, split_axis=0, concat_axis=0, tiled=True)  3.9 us
  transfers between devices with their start and end apart: 27, of which 15 were waited for; matrix products, arithmetic and copies ran while one was open for 0% of the time, Pallas kernels for 4%

profile of v5, /device:TPU:0, one launch (start us, length us, event | category | flops | bytes accessed | tf_op | source)
XLA Modules:
  0.0 134.3 jit_solution(12233851660270322071)
XLA Ops:
  0.9 18.0 %all_to_all.20.x_ref = bf16[8,32,576]{2,1,0:T(8,128)(2,1)S(1)} all-to-all(bf16[8,32,576]{2,1,0:T(8,128)(2,1)S(1)} %get-tuple-element.27), channel_id=1, replica_groups=mesh['gx'=4,'gy'=8] {'gy'}, dimensions={0} | all-to-all | bytes 589824 | tf_op jit(solution)/shard_map/all_to_all | solution.py:43
  18.8 1.0 copy-done.4
  20.5 0.9 copy-done.8
  22.3 1.5 %project.1 = (bf16[256,128]{1,0:T(8,128)(2,1)S(1)}, bf16[256,128]{1,0:T(8,128)(2,1)S(1)}, bf16[2,256,128]{2,1,0:T(8,128)(2,1)S(1)}) custom-call(bf16[8,32,576]{2,1,0:T(8,128)(2,1)S(1)} %all_to_all.20.x_ref, f32[4,576]{1,0:T(4,128)S(1)} %copy-done.6, bf16[576,256]{1,0:T(8,128)(2,1)S(1)} %copy-done.4, bf16[576,128]{1,0:T(8,128)(2,1)S(1)} %copy-done.8, ...), custom_call_target="tpu_custom_call" | custom-call | tf_op jit(solution)/shard_map/project/pallas_call | solution.py:32
  24.7 1.3 collective-permute-start.9
  26.0 1.6 %collective-permute-start.1 = (bf16[256,128]{1,0:T(8,128)(2,1)S(1)}, bf16[256,128]{1,0:T(8,128)(2,1)S(1)}, u32[]{:S(2)}, u32[]{:S(2)}) collective-permute-start(bf16[256,128]{1,0:T(8,128)(2,1)S(1)} %pair_sum.1), channel_id=1, source_target_pairs={{0,16},{8,24},{16,0},{24,8},{1,17},{9,25},{17,1},{25,9},{2,18},{10... | collective-permute-start | bytes 196616 | tf_op jit(solution)/shard_map/ppermute | solution.py:54
  27.6 2.7 %collective-permute-done.1.z2_ref = bf16[256,128]{1,0:T(8,128)(2,1)S(1)} collective-permute-done((bf16[256,128]{1,0:T(8,128)(2,1)S(1)}, bf16[256,128]{1,0:T(8,128)(2,1)S(1)}, u32[]{:S(2)}, u32[]{:S(2)}) %collective-permute-start.1) | collective-permute-done | bytes 65568 | tf_op jit(solution)/shard_map/ppermute | solution.py:54
  31.0 3.9 %all-to-all-start.1 = ((bf16[8,32,128]{2,1,0:T(8,128)(2,1)}), bf16[8,32,128]{2,1,0:T(8,128)(2,1)S(1)}, u32[]{:S(2)}, u32[]{:S(2)}) async-start(bf16[8,32,128]{2,1,0:T(8,128)(2,1)} %share_sum.1), calls=%async_computation.1 | async-start | bytes 131072 | tf_op jit(solution)/shard_map/all_to_all | solution.py:43
  35.6 6.4 %all-to-all-done.1.share_ref = bf16[8,32,128]{2,1,0:T(8,128)(2,1)S(1)} async-done(((bf16[8,32,128]{2,1,0:T(8,128)(2,1)}), bf16[8,32,128]{2,1,0:T(8,128)(2,1)S(1)}, u32[]{:S(2)}, u32[]{:S(2)}) %all-to-all-start.1) | async-done | bytes 65568 | tf_op jit(solution)/shard_map/all_to_all | solution.py:43
  42.1 1.5 %collective-permute-start.3 = (bf16[9,32,128]{2,1,0:T(8,128)(2,1)S(1)}, bf16[9,32,128]{2,1,0:T(8,128)(2,1)S(1)}, u32[]{:S(2)}, u32[]{:S(2)}) collective-permute-start(bf16[9,32,128]{2,1,0:T(8,128)(2,1)S(1)} %pack_shares.1.refs_0_), channel_id=1, source_target_pairs={{0,16},{8,24},{16,0},{24,8},{1,17},{9,25},{17,1},{25,9},{2,18},{10... | collective-permute-start | bytes 221192 | tf_op jit(solution)/shard_map/ppermute | solution.py:54
  44.2 2.3 %collective-permute-done.3.refs_2_ = bf16[9,32,128]{2,1,0:T(8,128)(2,1)S(1)} collective-permute-done((bf16[9,32,128]{2,1,0:T(8,128)(2,1)S(1)}, bf16[9,32,128]{2,1,0:T(8,128)(2,1)S(1)}, u32[]{:S(2)}, u32[]{:S(2)}) %collective-permute-start.3) | collective-permute-done | bytes 73760 | tf_op jit(solution)/shard_map/ppermute | solution.py:54
  47.4 1.4 %collective-permute-start.8 = (bf16[576,256]{1,0:T(8,128)(2,1)S(1)}, bf16[576,256]{1,0:T(8,128)(2,1)S(1)}, u32[]{:S(2)}, u32[]{:S(2)}) collective-permute-start(bf16[576,256]{1,0:T(8,128)(2,1)S(1)} %bitcast.7), channel_id=1, source_target_pairs={{0,1},{1,0},{2,3},{3,2},{4,5},{5,4},{6,7},{7,6},{8,9},{9,8},{10,11... | collective-permute-start | bytes 884744 | tf_op jit(solution)/shard_map/ppermute | solution.py:54
  49.5 1.4 %collective-permute-start.11 = (bf16[576,256]{1,0:T(8,128)(2,1)S(1)}, bf16[576,256]{1,0:T(8,128)(2,1)S(1)}, u32[]{:S(2)}, u32[]{:S(2)}) collective-permute-start(bf16[576,256]{1,0:T(8,128)(2,1)S(1)} %collective-permute-done.9.refs_2_), channel_id=1, source_target_pairs={{0,1},{1,0},{2,3},{3,2},{4,5},{5,4},{6,7},{7,6},{8,9},{9,8},{10,11... | collective-permute-start | bytes 884744 | tf_op jit(solution)/shard_map/ppermute | solution.py:54
  50.8 2.5 %copy-done = bf16[2,10,128,1024]{3,2,1,0:T(8,128)(2,1)S(1)} copy-done((bf16[2,10,128,1024]{3,2,1,0:T(8,128)(2,1)S(1)}, bf16[2,10,128,1024]{3,2,1,0:T(8,128)(2,1)}, u32[]{:S(2)}) %copy-start) | copy-done | bytes 5242904
  53.3 3.5 %attention.1 = (bf16[8,16,384]{2,1,0:T(8,128)(2,1)S(1)}, bf16[8,16,384]{2,1,0:T(8,128)(2,1)S(1)}) custom-call(bf16[9,32,128]{2,1,0:T(8,128)(2,1)S(1)} %pack_shares.1.refs_0_, bf16[9,32,128]{2,1,0:T(8,128)(2,1)S(1)} %collective-permute-done.2.refs_1_, bf16[9,32,128]{2,1,0:T(8,128)(2,1)S(1)} %collective-permute-done.3.refs_2_, ...), custom_call_target="tpu_custom_call" | custom-call | tf_op jit(solution)/shard_map/attention/pallas_call | solution.py:32
  57.5 1.3 collective-permute-done.5.pair_ref
  59.0 1.6 %collective-permute-start.6 = (bf16[8,16,384]{2,1,0:T(8,128)(2,1)S(1)}, bf16[8,16,384]{2,1,0:T(8,128)(2,1)S(1)}, u32[]{:S(2)}, u32[]{:S(2)}) collective-permute-start(bf16[8,16,384]{2,1,0:T(8,128)(2,1)S(1)} %pair_terms.1.own_ref), channel_id=1, source_target_pairs={{0,16},{8,24},{16,0},{24,8},{1,17},{9,25},{17,1},{25,9},{2,18},{10... | collective-permute-start | bytes 294920 | tf_op jit(solution)/shard_map/ppermute | solution.py:54
  60.6 3.3 %collective-permute-done.6.across_ref = bf16[8,16,384]{2,1,0:T(8,128)(2,1)S(1)} collective-permute-done((bf16[8,16,384]{2,1,0:T(8,128)(2,1)S(1)}, bf16[8,16,384]{2,1,0:T(8,128)(2,1)S(1)}, u32[]{:S(2)}, u32[]{:S(2)}) %collective-permute-start.6) | collective-permute-done | bytes 98336 | tf_op jit(solution)/shard_map/ppermute | solution.py:54
  64.2 5.7 %collective-permute-done.11.refs_3_ = bf16[576,256]{1,0:T(8,128)(2,1)S(1)} collective-permute-done((bf16[576,256]{1,0:T(8,128)(2,1)S(1)}, bf16[576,256]{1,0:T(8,128)(2,1)S(1)}, u32[]{:S(2)}, u32[]{:S(2)}) %collective-permute-start.11) | collective-permute-done | bytes 294944 | tf_op jit(solution)/shard_map/ppermute | solution.py:54
  69.9 5.9 %collective-permute-done.14.refs_7_ = bf16[576,256]{1,0:T(8,128)(2,1)S(1)} collective-permute-done((bf16[576,256]{1,0:T(8,128)(2,1)S(1)}, bf16[576,256]{1,0:T(8,128)(2,1)S(1)}, u32[]{:S(2)}, u32[]{:S(2)}) %collective-permute-start.14) | collective-permute-done | bytes 294944 | tf_op jit(solution)/shard_map/ppermute | solution.py:54
  76.6 0.9 collective-permute-start.17
  78.6 1.4 %collective-permute-done.17.refs_3_ = f32[32,128]{1,0:T(8,128)S(1)} collective-permute-done((f32[32,128]{1,0:T(8,128)S(1)}, f32[32,128]{1,0:T(8,128)S(1)}, u32[]{:S(2)}, u32[]{:S(2)}) %collective-permute-start.17) | collective-permute-done | bytes 16416 | tf_op jit(solution)/shard_map/ppermute | solution.py:54
  80.0 1.3 collective-permute-done.16.refs_2_
  81.6 14.1 %all_to_all.21.ff_ref = bf16[8,32,576]{2,1,0:T(8,128)(2,1)S(1)} all-to-all(bf16[8,32,576]{2,1,0:T(8,128)(2,1)S(1)} %get-tuple-element.42), channel_id=1, replica_groups=mesh['gx'=4,'gy'=8] {'gy'}, dimensions={0} | all-to-all | bytes 589824 | tf_op jit(solution)/shard_map/all_to_all | solution.py:43
  95.7 1.2 gate_up.1
  96.9 2.0 %collective-permute-done.18.from_pair_ref.z13_ref = bf16[2,64,2304]{2,1,0:T(8,128)(2,1)S(1)} collective-permute-done((bf16[2,64,2304]{2,1,0:T(8,128)(2,1)S(1)}, bf16[2,64,2304]{2,1,0:T(8,128)(2,1)S(1)}, u32[]{:S(2)}, u32[]{:S(2)}) %collective-permute-start.18) | collective-permute-done | bytes 589856 | tf_op jit(solution)/shard_map/ppermute | solution.py:54
  99.7 8.4 %collective-permute-done.19.z2_ref = bf16[64,2304]{1,0:T(8,128)(2,1)S(1)} collective-permute-done((bf16[64,2304]{1,0:T(8,128)(2,1)S(1)}, bf16[64,2304]{1,0:T(8,128)(2,1)S(1)}, u32[]{:S(2)}, u32[]{:S(2)}) %collective-permute-start.19) | collective-permute-done | bytes 294944 | tf_op jit(solution)/shard_map/ppermute | solution.py:54
  109.0 4.5 %collective-permute-done.21.refs_2_ = bf16[64,1152]{1,0:T(8,128)(2,1)S(1)} collective-permute-done((bf16[64,1152]{1,0:T(8,128)(2,1)S(1)}, bf16[64,1152]{1,0:T(8,128)(2,1)S(1)}, u32[]{:S(2)}, u32[]{:S(2)}) %collective-permute-start.21) | collective-permute-done | bytes 147488 | tf_op jit(solution)/shard_map/ppermute | solution.py:54
  113.5 1.4 %collective-permute-done.22.refs_3_ = bf16[64,1152]{1,0:T(8,128)(2,1)S(1)} collective-permute-done((bf16[64,1152]{1,0:T(8,128)(2,1)S(1)}, bf16[64,1152]{1,0:T(8,128)(2,1)S(1)}, u32[]{:S(2)}, u32[]{:S(2)}) %collective-permute-start.22) | collective-permute-done | bytes 147488 | tf_op jit(solution)/shard_map/ppermute | solution.py:54
  115.6 14.0 %all_to_all.22.parts_ref = bf16[8,32,576]{2,1,0:T(8,128)(2,1)S(1)} all-to-all(bf16[8,32,576]{2,1,0:T(8,128)(2,1)S(1)} %project_down.1), channel_id=1, replica_groups=mesh['gx'=4,'gy'=8] {'gy'}, dimensions={0} | all-to-all | bytes 589824 | tf_op jit(solution)/shard_map/all_to_all | solution.py:43
  130.4 1.2 collective-permute-start.23
  131.6 1.3 collective-permute-done.25.refs_3_
  (71 shorter events, 14.1 us)
Async XLA Ops:
  0.0 23.9 %copy-start.5 = (bf16[256,576]{0,1:T(8,128)(2,1)S(1)}, bf16[256,576]{0,1:T(8,128)(2,1)}, u32[]{:S(2)}) copy-start(bf16[256,576]{0,1:T(8,128)(2,1)} %param.22) | copy-start | bytes 884740
  0.8 45.8 %copy-start.11 = (s32[3,8]{1,0:T(4,128)S(1)}, s32[3,8]{1,0:T(4,128)}, u32[]{:S(2)}) copy-start(s32[3,8]{1,0:T(4,128)} %parents_ref.1) | copy-start | bytes 292
  0.8 45.8 %copy-start.12 = (s32[1,33]{1,0:T(1,128)S(1)}, s32[1,33]{1,0:T(1,128)}, u32[]{:S(2)}) copy-start(s32[1,33]{1,0:T(1,128)} %table_ref.1) | copy-start | bytes 400
  23.8 2.2 %collective-permute-start = (bf16[2,256,128]{2,1,0:T(8,128)(2,1)S(1)}, bf16[2,256,128]{2,1,0:T(8,128)(2,1)S(1)}, u32[]{:S(2)}, u32[]{:S(2)}) collective-permute-start(bf16[2,256,128]{2,1,0:T(8,128)(2,1)S(1)} %get-tuple-element.29), channel_id=1, source_target_pairs={{0,8},{8,0},{16,24},{24,16},{1,9},{9,1},{17,25},{25,17},{2,10},{10... | collective-permute-start | bytes 393224 | tf_op jit(solution)/shard_map/ppermute | solution.py:54
  23.9 19.7 %collective-permute-start.10 = (bf16[576,256]{1,0:T(8,128)(2,1)S(1)}, bf16[576,256]{1,0:T(8,128)(2,1)S(1)}, u32[]{:S(2)}, u32[]{:S(2)}) collective-permute-start(bf16[576,256]{1,0:T(8,128)(2,1)S(1)} %bitcast.5), channel_id=1, source_target_pairs={{0,4},{1,5},{2,6},{3,7},{4,0},{5,1},{6,2},{7,3},{8,12},{9,13},{10,... | collective-permute-start | bytes 884744 | tf_op jit(solution)/shard_map/ppermute | solution.py:54
  24.7 18.9 %collective-permute-start.9 = (bf16[576,256]{1,0:T(8,128)(2,1)S(1)}, bf16[576,256]{1,0:T(8,128)(2,1)S(1)}, u32[]{:S(2)}, u32[]{:S(2)}) collective-permute-start(bf16[576,256]{1,0:T(8,128)(2,1)S(1)} %bitcast.6), channel_id=1, source_target_pairs={{0,2},{1,3},{2,0},{3,1},{4,6},{5,7},{6,4},{7,5},{8,10},{9,11},{10,... | collective-permute-start | bytes 884744 | tf_op jit(solution)/shard_map/ppermute | solution.py:54
  26.0 4.3 %collective-permute-start.1 = (bf16[256,128]{1,0:T(8,128)(2,1)S(1)}, bf16[256,128]{1,0:T(8,128)(2,1)S(1)}, u32[]{:S(2)}, u32[]{:S(2)}) collective-permute-start(bf16[256,128]{1,0:T(8,128)(2,1)S(1)} %pair_sum.1), channel_id=1, source_target_pairs={{0,16},{8,24},{16,0},{24,8},{1,17},{9,25},{17,1},{25,9},{2,18},{10... | collective-permute-start | bytes 196616 | tf_op jit(solution)/shard_map/ppermute | solution.py:54
  31.0 11.0 %all-to-all-start.1 = ((bf16[8,32,128]{2,1,0:T(8,128)(2,1)}), bf16[8,32,128]{2,1,0:T(8,128)(2,1)S(1)}, u32[]{:S(2)}, u32[]{:S(2)}) async-start(bf16[8,32,128]{2,1,0:T(8,128)(2,1)} %share_sum.1), calls=%async_computation.1 | async-start | bytes 131072 | tf_op jit(solution)/shard_map/all_to_all | solution.py:43
  42.1 4.4 %collective-permute-start.3 = (bf16[9,32,128]{2,1,0:T(8,128)(2,1)S(1)}, bf16[9,32,128]{2,1,0:T(8,128)(2,1)S(1)}, u32[]{:S(2)}, u32[]{:S(2)}) collective-permute-start(bf16[9,32,128]{2,1,0:T(8,128)(2,1)S(1)} %pack_shares.1.refs_0_), channel_id=1, source_target_pairs={{0,16},{8,24},{16,0},{24,8},{1,17},{9,25},{17,1},{25,9},{2,18},{10... | collective-permute-start | bytes 221192 | tf_op jit(solution)/shard_map/ppermute | solution.py:54
  43.6 13.2 %collective-permute-start.13 = (bf16[576,256]{1,0:T(8,128)(2,1)S(1)}, bf16[576,256]{1,0:T(8,128)(2,1)S(1)}, u32[]{:S(2)}, u32[]{:S(2)}) collective-permute-start(bf16[576,256]{1,0:T(8,128)(2,1)S(1)} %collective-permute-done.10.refs_4_), channel_id=1, source_target_pairs={{0,2},{1,3},{2,0},{3,1},{4,6},{5,7},{6,4},{7,5},{8,10},{9,11},{10,... | collective-permute-start | bytes 884744 | tf_op jit(solution)/shard_map/ppermute | solution.py:54
  44.2 5.3 %collective-permute-start.2 = (bf16[9,32,128]{2,1,0:T(8,128)(2,1)S(1)}, bf16[9,32,128]{2,1,0:T(8,128)(2,1)S(1)}, u32[]{:S(2)}, u32[]{:S(2)}) collective-permute-start(bf16[9,32,128]{2,1,0:T(8,128)(2,1)S(1)} %pack_shares.1.refs_0_), channel_id=1, source_target_pairs={{0,8},{8,0},{16,24},{24,16},{1,9},{9,1},{17,25},{25,17},{2,10},{10... | collective-permute-start | bytes 221192 | tf_op jit(solution)/shard_map/ppermute | solution.py:54
  46.5 4.4 %collective-permute-start.4 = (bf16[9,32,128]{2,1,0:T(8,128)(2,1)S(1)}, bf16[9,32,128]{2,1,0:T(8,128)(2,1)S(1)}, u32[]{:S(2)}, u32[]{:S(2)}) collective-permute-start(bf16[9,32,128]{2,1,0:T(8,128)(2,1)S(1)} %collective-permute-done.3.refs_2_), channel_id=1, source_target_pairs={{0,8},{8,0},{16,24},{24,16},{1,9},{9,1},{17,25},{25,17},{2,10},{10... | collective-permute-start | bytes 221192 | tf_op jit(solution)/shard_map/ppermute | solution.py:54
  47.4 16.8 %collective-permute-start.8 = (bf16[576,256]{1,0:T(8,128)(2,1)S(1)}, bf16[576,256]{1,0:T(8,128)(2,1)S(1)}, u32[]{:S(2)}, u32[]{:S(2)}) collective-permute-start(bf16[576,256]{1,0:T(8,128)(2,1)S(1)} %bitcast.7), channel_id=1, source_target_pairs={{0,1},{1,0},{2,3},{3,2},{4,5},{5,4},{6,7},{7,6},{8,9},{9,8},{10,11... | collective-permute-start | bytes 884744 | tf_op jit(solution)/shard_map/ppermute | solution.py:54
  48.8 21.1 %collective-permute-start.12 = (bf16[576,256]{1,0:T(8,128)(2,1)S(1)}, bf16[576,256]{1,0:T(8,128)(2,1)S(1)}, u32[]{:S(2)}, u32[]{:S(2)}) collective-permute-start(bf16[576,256]{1,0:T(8,128)(2,1)S(1)} %collective-permute-done.10.refs_4_), channel_id=1, source_target_pairs={{0,1},{1,0},{2,3},{3,2},{4,5},{5,4},{6,7},{7,6},{8,9},{9,8},{10,11... | collective-permute-start | bytes 884744 | tf_op jit(solution)/shard_map/ppermute | solution.py:54
  49.5 20.4 %collective-permute-start.11 = (bf16[576,256]{1,0:T(8,128)(2,1)S(1)}, bf16[576,256]{1,0:T(8,128)(2,1)S(1)}, u32[]{:S(2)}, u32[]{:S(2)}) collective-permute-start(bf16[576,256]{1,0:T(8,128)(2,1)S(1)} %collective-permute-done.9.refs_2_), channel_id=1, source_target_pairs={{0,1},{1,0},{2,3},{3,2},{4,5},{5,4},{6,7},{7,6},{8,9},{9,8},{10,11... | collective-permute-start | bytes 884744 | tf_op jit(solution)/shard_map/ppermute | solution.py:54
  56.8 19.0 %collective-permute-start.14 = (bf16[576,256]{1,0:T(8,128)(2,1)S(1)}, bf16[576,256]{1,0:T(8,128)(2,1)S(1)}, u32[]{:S(2)}, u32[]{:S(2)}) collective-permute-start(bf16[576,256]{1,0:T(8,128)(2,1)S(1)} %collective-permute-done.13.refs_6_), channel_id=1, source_target_pairs={{0,1},{1,0},{2,3},{3,2},{4,5},{5,4},{6,7},{7,6},{8,9},{9,8},{10,11... | collective-permute-start | bytes 884744 | tf_op jit(solution)/shard_map/ppermute | solution.py:54
  57.5 1.3 collective-permute-start.5
  59.0 4.9 %collective-permute-start.6 = (bf16[8,16,384]{2,1,0:T(8,128)(2,1)S(1)}, bf16[8,16,384]{2,1,0:T(8,128)(2,1)S(1)}, u32[]{:S(2)}, u32[]{:S(2)}) collective-permute-start(bf16[8,16,384]{2,1,0:T(8,128)(2,1)S(1)} %pair_terms.1.own_ref), channel_id=1, source_target_pairs={{0,16},{8,24},{16,0},{24,8},{1,17},{9,25},{17,1},{25,9},{2,18},{10... | collective-permute-start | bytes 294920 | tf_op jit(solution)/shard_map/ppermute | solution.py:54
  64.1 31.6 %copy-start.2 = (bf16[576,1152]{1,0:T(8,128)(2,1)S(1)}, bf16[576,1152]{1,0:T(8,128)(2,1)}, u32[]{:S(2)}) copy-start(bf16[576,1152]{1,0:T(8,128)(2,1)} %gate_ref.1) | copy-start | bytes 3981316
  64.1 31.6 %copy-start.3 = (bf16[576,1152]{1,0:T(8,128)(2,1)S(1)}, bf16[576,1152]{1,0:T(8,128)(2,1)}, u32[]{:S(2)}) copy-start(bf16[576,1152]{1,0:T(8,128)(2,1)} %up_ref.1) | copy-start | bytes 3981316
  64.1 5.8 %collective-permute-start.7 = (bf16[8,16,256]{2,1,0:T(8,128)(2,1)S(1)}, bf16[8,16,256]{2,1,0:T(8,128)(2,1)S(1)}, u32[]{:S(2)}, u32[]{:S(2)}) collective-permute-start(bf16[8,16,256]{2,1,0:T(8,128)(2,1)S(1)} %divide.1.own_ref), channel_id=1, source_target_pairs={{0,8},{8,0},{16,24},{24,16},{1,9},{9,1},{17,25},{25,17},{2,10},{10... | collective-permute-start | bytes 196616 | tf_op jit(solution)/shard_map/ppermute | solution.py:54
  76.6 3.3 %collective-permute-start.17 = (f32[32,128]{1,0:T(8,128)S(1)}, f32[32,128]{1,0:T(8,128)S(1)}, u32[]{:S(2)}, u32[]{:S(2)}) collective-permute-start(f32[32,128]{1,0:T(8,128)S(1)} %get-tuple-element.40.refs_0_), channel_id=1, source_target_pairs={{0,24},{8,16},{16,8},{24,0},{1,25},{9,17},{17,9},{25,1},{2,26},{10... | collective-permute-start | bytes 49160 | tf_op jit(solution)/shard_map/ppermute | solution.py:54
  77.6 3.7 %collective-permute-start.16 = (f32[32,128]{1,0:T(8,128)S(1)}, f32[32,128]{1,0:T(8,128)S(1)}, u32[]{:S(2)}, u32[]{:S(2)}) collective-permute-start(f32[32,128]{1,0:T(8,128)S(1)} %get-tuple-element.40.refs_0_), channel_id=1, source_target_pairs={{0,16},{8,24},{16,0},{24,8},{1,17},{9,25},{17,1},{25,9},{2,18},{10... | collective-permute-start | bytes 49160 | tf_op jit(solution)/shard_map/ppermute | solution.py:54
  78.3 3.0 %collective-permute-start.15 = (f32[32,128]{1,0:T(8,128)S(1)}, f32[32,128]{1,0:T(8,128)S(1)}, u32[]{:S(2)}, u32[]{:S(2)}) collective-permute-start(f32[32,128]{1,0:T(8,128)S(1)} %get-tuple-element.40.refs_0_), channel_id=1, source_target_pairs={{0,8},{8,0},{16,24},{24,16},{1,9},{9,1},{17,25},{25,17},{2,10},{10... | collective-permute-start | bytes 49160 | tf_op jit(solution)/shard_map/ppermute | solution.py:54
  96.8 2.1 %collective-permute-start.18 = (bf16[2,64,2304]{2,1,0:T(8,128)(2,1)S(1)}, bf16[2,64,2304]{2,1,0:T(8,128)(2,1)S(1)}, u32[]{:S(2)}, u32[]{:S(2)}) collective-permute-start(bf16[2,64,2304]{2,1,0:T(8,128)(2,1)S(1)} %get-tuple-element.44), channel_id=1, source_target_pairs={{0,8},{8,0},{16,24},{24,16},{1,9},{9,1},{17,25},{25,17},{2,10},{10... | collective-permute-start | bytes 1769480 | tf_op jit(solution)/shard_map/ppermute | solution.py:54
  99.0 9.1 %collective-permute-start.19 = (bf16[64,2304]{1,0:T(8,128)(2,1)S(1)}, bf16[64,2304]{1,0:T(8,128)(2,1)S(1)}, u32[]{:S(2)}, u32[]{:S(2)}) collective-permute-start(bf16[64,2304]{1,0:T(8,128)(2,1)S(1)} %pair_sum_ff.1), channel_id=1, source_target_pairs={{0,16},{8,24},{16,0},{24,8},{1,17},{9,25},{17,1},{25,9},{2,18},{10... | collective-permute-start | bytes 884744 | tf_op jit(solution)/shard_map/ppermute | solution.py:54
  108.3 5.2 %collective-permute-start.21 = (bf16[64,1152]{1,0:T(8,128)(2,1)S(1)}, bf16[64,1152]{1,0:T(8,128)(2,1)S(1)}, u32[]{:S(2)}, u32[]{:S(2)}) collective-permute-start(bf16[64,1152]{1,0:T(8,128)(2,1)S(1)} %activate.1.refs_0_), channel_id=1, source_target_pairs={{0,16},{8,24},{16,0},{24,8},{1,17},{9,25},{17,1},{25,9},{2,18},{10... | collective-permute-start | bytes 442376 | tf_op jit(solution)/shard_map/ppermute | solution.py:54
  109.0 4.5 %collective-permute-start.20 = (bf16[64,1152]{1,0:T(8,128)(2,1)S(1)}, bf16[64,1152]{1,0:T(8,128)(2,1)S(1)}, u32[]{:S(2)}, u32[]{:S(2)}) collective-permute-start(bf16[64,1152]{1,0:T(8,128)(2,1)S(1)} %activate.1.refs_0_), channel_id=1, source_target_pairs={{0,8},{8,0},{16,24},{24,16},{1,9},{9,1},{17,25},{25,17},{2,10},{10... | collective-permute-start | bytes 442376 | tf_op jit(solution)/shard_map/ppermute | solution.py:54
  113.5 1.4 %collective-permute-start.22 = (bf16[64,1152]{1,0:T(8,128)(2,1)S(1)}, bf16[64,1152]{1,0:T(8,128)(2,1)S(1)}, u32[]{:S(2)}, u32[]{:S(2)}) collective-permute-start(bf16[64,1152]{1,0:T(8,128)(2,1)S(1)} %collective-permute-done.21.refs_2_), channel_id=1, source_target_pairs={{0,8},{8,0},{16,24},{24,16},{1,9},{9,1},{17,25},{25,17},{2,10},{10... | collective-permute-start | bytes 442376 | tf_op jit(solution)/shard_map/ppermute | solution.py:54
  129.7 3.2 %collective-permute-start.25 = (f32[32,128]{1,0:T(8,128)S(1)}, f32[32,128]{1,0:T(8,128)S(1)}, u32[]{:S(2)}, u32[]{:S(2)}) collective-permute-start(f32[32,128]{1,0:T(8,128)S(1)} %get-tuple-element.46.refs_0_), channel_id=1, source_target_pairs={{0,24},{8,16},{16,8},{24,0},{1,25},{9,17},{17,9},{25,1},{2,26},{10... | collective-permute-start | bytes 49160 | tf_op jit(solution)/shard_map/ppermute | solution.py:54
  129.7 3.8 %collective-permute-start.24 = (f32[32,128]{1,0:T(8,128)S(1)}, f32[32,128]{1,0:T(8,128)S(1)}, u32[]{:S(2)}, u32[]{:S(2)}) collective-permute-start(f32[32,128]{1,0:T(8,128)S(1)} %get-tuple-element.46.refs_0_), channel_id=1, source_target_pairs={{0,16},{8,24},{16,0},{24,8},{1,17},{9,25},{17,1},{25,9},{2,18},{10... | collective-permute-start | bytes 49160 | tf_op jit(solution)/shard_map/ppermute | solution.py:54
  130.4 3.1 %collective-permute-start.23 = (f32[32,128]{1,0:T(8,128)S(1)}, f32[32,128]{1,0:T(8,128)S(1)}, u32[]{:S(2)}, u32[]{:S(2)}) collective-permute-start(f32[32,128]{1,0:T(8,128)S(1)} %get-tuple-element.46.refs_0_), channel_id=1, source_target_pairs={{0,8},{8,0},{16,24},{24,16},{1,9},{9,1},{17,25},{25,17},{2,10},{10... | collective-permute-start | bytes 49160 | tf_op jit(solution)/shard_map/ppermute | solution.py:54
  (8 other events, 47.3 us)

commit v6 on v5

--- a/solution.py
+++ b/solution.py
@@ -26,7 +26,8 @@
 IN_SMEM = pl.BlockSpec(memory_space=pltpu.SMEM)
 
 
-def run(name, kernel, outs, args, scratch=(), limit=16, specs=None):
+def run(name, kernel, outs, args, scratch=(), limit=16, specs=None, micros=0):
+    cost = pl.CostEstimate(flops=micros * 10**9, bytes_accessed=0, transcendentals=0)
     specs = specs or {}
     vmem = pl.BlockSpec(memory_space=pltpu.VMEM)
     return pl.pallas_call(
@@ -35,6 +36,7 @@
         in_specs=[specs.get(n, vmem) for n in range(len(args))],
         scratch_shapes=scratch,
         compiler_params=pltpu.CompilerParams(vmem_limit_bytes=limit * MIB),
+        cost_estimate=cost if micros else None,
         name=name,
     )(*args)
 
@@ -72,6 +74,21 @@
     high = column.astype(BF).astype(F32)
     lane = lax.broadcasted_iota(jnp.int32, shape, len(shape) - 1)
     return jnp.where(lane < lanes // 2, high, column - high)
+
+
+def pack_lanes(v):
+    rows, width = v.shape
+    whole = width // 128 * 128
+    tiles = [v[:, c : c + 128] for c in range(0, whole, 128)]
+    last = jnp.concatenate([v[: rows // 2, whole:], v[rows // 2 :, whole:]], axis=1)
+    return jnp.concatenate(tiles + [last], axis=0)
+
+
+def unpack_lanes(v, rows):
+    whole = v.shape[0] // rows * rows
+    tiles = [v[r : r + rows] for r in range(0, whole, rows)]
+    last = jnp.concatenate([v[whole:, :64], v[whole:, 64:]], axis=0)
+    return jnp.concatenate(tiles + [last], axis=1)
 
 
 def row_sum(v):
@@ -206,8 +223,7 @@
     all_rows = ny * rows
     share_rows = all_rows // nx
     hidden = w_gate.shape[1]
-    cos, sin = rope_tables(lengths, rows, steps)
-    tables = make_tables(block_table, lengths, parents, cache_pool.shape[1], rows, steps)
+    packed = rows * width // 128
 
     def my(axis):
         return lax.axis_index(axis)
@@ -215,36 +231,30 @@
     def spread(x_ref, own_ref, out_ref):
         own = x_ref[...].astype(F32).reshape(rows, width).astype(BF)
         own_ref[...] = own
+        own = pack_lanes(own)
         for m in range(ny):
             out_ref[m] = own
 
     x_own, x_all = run(
-        "spread", spread, [((rows, width), BF), ((ny, rows, width), BF)], (inputs,)
+        "spread", spread, [((rows, width), BF), ((ny, packed, 128), BF)], (inputs,), micros=12
     )
     x_all = exchange(x_all, "gy")
 
-    w_blocks = [None] * ny
-    w_blocks[0], _ = lax.optimization_barrier((w_out.T, x_all))
-    for m in (4, 2, 1):
-        w_blocks[m] = permute(w_blocks[0], "gy", m)
-
-    def project(x_ref, gain_hbm, q_hbm, k_hbm, v_hbm, z0_ref, z2_ref, z13_ref, *kept):
-        held, gain_ref, q_ref, k_ref, v_ref, sems = kept
-        pairs = (gain_hbm, gain_ref), (q_hbm, q_ref), (k_hbm, k_ref), (v_hbm, v_ref)
-        copies = [
-            pltpu.make_async_copy(src, dst, sems.at[n]) for n, (src, dst) in enumerate(pairs)
+    w_own = w_out.T
+    w_blocks = [w_own, permute(w_own, "gy", 1), permute(w_own, "gy", 2)] + [None] * (ny - 3)
+    (w_late, _, w_later), _ = lax.optimization_barrier((w_blocks[:3], x_all))
+    w_blocks[4] = permute(w_late, "gy", 4)
+    w_blocks[3] = permute(w_later, "gy", 1)
+
+    def project(x_ref, gain_ref, q_ref, k_ref, v_ref, z0_ref, z2_ref, z13_ref, held):
+        gain = 1.0 + gain_ref[0:1]
+        flat = [
+            (unpack_lanes(x_ref[m], rows).astype(F32) * gain).astype(BF) for m in range(ny)
         ]
-        for copy in copies:
-            copy.start()
-        x = x_ref[...].reshape(all_rows, width).astype(F32)
-        copies[0].wait()
-        flat = (x * (1.0 + gain_ref[0:1])).astype(BF)
-        copies[1].wait()
+        flat = jnp.concatenate(flat, axis=0)
         query = jnp.dot(flat, q_ref[...], preferred_element_type=F32).astype(BF)
         held[0], held[1] = query[:, :HALF], query[:, HALF:]
-        copies[2].wait()
         held[2] = jnp.dot(flat, k_ref[...], preferred_element_type=F32).astype(BF)
-        copies[3].wait()
         held[3] = jnp.dot(flat, v_ref[...], preferred_element_type=F32).astype(BF)
         me = my("gx")
         z0_ref[...], z2_ref[...] = held[me], held[me ^ 2]
@@ -258,11 +268,7 @@
         (x_all, norm_gains, w_query, w_key, w_value),
         scratch=[
             pltpu.VMEM((nx,) + shape, BF),
-            pltpu.VMEM(norm_gains.shape, F32),
-            *[pltpu.VMEM(w.shape, BF) for w in (w_query, w_key, w_value)],
-            pltpu.SemaphoreType.DMA((4,)),
         ],
-        specs={n: IN_HBM for n in range(1, 5)},
     )
     z13 = permute(z13, "gx", 1)
 
@@ -277,12 +283,13 @@
         total = z0_ref[...].astype(F32) + z13_ref[0].astype(F32) + z2_ref[...].astype(F32)
         out_ref[...] = total.reshape(ny, rows, HALF).astype(BF)
 
-    (shares,) = run("share_sum", share_sum, [((ny, rows, HALF), BF)], (z0, z13, z2))
+    (shares,) = run(
+        "share_sum", share_sum, [((ny, rows, HALF), BF)], (z0, z13, z2), micros=6
+    )
+    cos, sin = rope_tables(lengths, rows, steps)
+    tables = make_tables(block_table, lengths, parents, cache_pool.shape[1], rows, steps)
     shares = exchange(shares, "gy")
-    _, (w_late, w_later) = lax.optimization_barrier((shares, (w_blocks[4], w_blocks[2])))
-    w_blocks[6] = permute(w_late, "gy", 2)
-    w_blocks[5] = permute(w_late, "gy", 1)
-    w_blocks[3] = permute(w_later, "gy", 1)
+    shares, _ = lax.optimization_barrier((shares, w_blocks[3]))
 
     def pack_shares(share_ref, x_ref, out_ref):
         x = x_ref[...].astype(F32)
@@ -291,6 +298,9 @@
 
     (shares,) = run("pack_shares", pack_shares, [((ny + 1, rows, HALF), BF)], (shares, x_own))
     shares = gather_gx(shares)
+    _, w_late = lax.optimization_barrier((shares[2], w_blocks[4]))
+    w_blocks[6] = permute(w_late, "gy", 2)
+    w_blocks[5] = permute(w_late, "gy", 1)
 
     def attention(*refs):
         a_refs, tables, pool_ref, outs = refs[:nx], refs[nx : nx + 4], refs[nx + 4], refs[nx + 5 :]
@@ -333,8 +343,6 @@
         limit=24,
         specs={nx + 4: IN_HBM},
     )
-    _, w_last = lax.optimization_barrier((own, w_blocks[6]))
-    w_blocks[7] = permute(w_last, "gy", 1)
     pair = permute(pair, "gx", 1)
 
     def pair_terms(own_ref, pair_ref, out_ref):
@@ -345,6 +353,8 @@
 
     (own,) = run("pair_terms", pair_terms, [(shape, BF)], (own, pair))
     across = permute(own, "gx", 2)
+    _, w_last, _ = lax.optimization_barrier((own, w_blocks[6], w_blocks[5]))
+    w_blocks[7] = permute(w_last, "gy", 1)
 
     def divide(own_ref, across_ref, out_ref):
         total = own_ref[...].astype(F32) + across_ref[...].astype(F32)
@@ -391,13 +401,14 @@
         mixed_ref[...] = mixed
         scale = lax.rsqrt(square / D + EPSILON)
         ff_input = (mixed * scale * (1.0 + gain_ref[2:3])).astype(BF)
+        ff_input = pack_lanes(ff_input)
         for m in range(ny):
             ff_ref[m] = ff_input
 
     mixed, ff_input = run(
         "mix",
         mix,
-        [((rows, width), F32), ((ny, rows, width), BF)],
+        [((rows, width), F32), ((ny, packed, 128), BF)],
         (*sums, attn, x_own, norm_gains),
     )
     ff_input = exchange(ff_input, "gy")
@@ -407,7 +418,9 @@
     def gate_up(ff_ref, gate_ref, up_ref, z0_ref, z2_ref, z13_ref):
         me = my("gx")
         flat = [
-            ff_ref[pl.ds((me ^ n) * groups, groups)].reshape(share_rows, width) for n in range(nx)
+            unpack_lanes(ff_ref[(me ^ n) * groups + group], rows)
+            for n in range(nx)
+            for group in range(groups)
         ]
         flat = jnp.concatenate(flat, axis=0)
         w_refs = gate_ref, up_ref
@@ -442,17 +455,19 @@
         me = my("gx")
         flat = jnp.concatenate([r[...] for r in refs[:nx]], axis=0)
         sums = lax.dot_general(flat, w_ref[...], NT, preferred_element_type=F32)
-        sums = sums.reshape(nx, groups, rows, width).astype(BF)
         for n in range(nx):
-            out_ref[pl.ds((me ^ n) * groups, groups)] = sums[n]
+            for group in range(groups):
+                at = (n * groups + group) * rows
+                block = pack_lanes(sums[at : at + rows].astype(BF))
+                out_ref[(me ^ n) * groups + group] = block
 
     (down,) = run(
-        "project_down", project_down, [((ny, rows, width), BF)], (*blocks, w_down.T)
+        "project_down", project_down, [((ny, packed, 128), BF)], (*blocks, w_down.T)
     )
     down = exchange(down, "gy")
 
     def down_sum(parts_ref, down_ref, sums_ref):
-        down = jnp.sum(parts_ref[...].astype(F32), axis=0)
+        down = unpack_lanes(jnp.sum(parts_ref[...].astype(F32), axis=0), rows)
         down_ref[...] = down
         sums_ref[...] = jnp.broadcast_to(row_sum(down * down), (rows, PAGE))
 

time: 135 us -> 123 us (0.911)
  blocking collectives: 46.1 us -> 28.1 us
  starting transfers between devices: 20.8 us -> 28.5 us
  local copies, waits for them, and re-layouts: 6.83 us -> 3.38 us
  waiting for transfers between devices: 48.6 us -> 50.8 us
    all_to_all x3 -> x2, blocking collectives: 46.1 us -> 28.1 us  [exchange(): return lax.all_to_all(values, axes, split_axis=0, concat_axis=0, tiled=True)]
    all_to_all x1 -> x2, waiting for transfers between devices: 6.42 us -> 16.2 us  [exchange(): return lax.all_to_all(values, axes, split_axis=0, concat_axis=0, tiled=True)]
    ppermute x26, waiting for transfers between devices: 42.2 us -> 34.6 us  [permute(): return lax.ppermute(values, axis, [(i, i ^ m) for i in range(count)])]
    all_to_all x1 -> x2, starting transfers between devices: 3.9 us -> 10.6 us  [exchange(): return lax.all_to_all(values, axes, split_axis=0, concat_axis=0, tiled=True)]
    unnamed x26 -> x24, local copies, waits for them, and re-layouts: 6.83 us -> 3.38 us
  transfers between devices with their start and end apart: 27 -> 28, of which waited for: 15 -> 18; matrix products, arithmetic and copies ran while one was open for 0% -> 0% of each run, Pallas kernels for 4% -> 5%
where the time goes in v6:
time: 123 us; the launch traced here: 122 us
  waiting for transfers between devices  50.8 us (41%)
  starting transfers between devices  28.5 us (23%)
  blocking collectives  28.1 us (23%)
  Pallas kernels  10.7 us (9%)
  local copies, waits for them, and re-layouts  3.38 us (3%)
    ppermute x26, waiting for transfers between devices, permute(): return lax.ppermute(values, axis, [(i, i ^ m) for i in range(count)])  34.6 us
    all_to_all x2, blocking collectives, exchange(): return lax.all_to_all(values, axes, split_axis=0, concat_axis=0, tiled=True)  28.1 us
    ppermute x26, starting transfers between devices, permute(): return lax.ppermute(values, axis, [(i, i ^ m) for i in range(count)])  17.9 us
    all_to_all x2, waiting for transfers between devices, exchange(): return lax.all_to_all(values, axes, split_axis=0, concat_axis=0, tiled=True)  16.2 us
    pallas_call x17, Pallas kernels, run(): pl.pallas_call(kernel, out_shape=[jax.ShapeDtypeStruct(s, d) for s, d in...  10.7 us
    all_to_all x2, starting transfers between devices, exchange(): return lax.all_to_all(values, axes, split_axis=0, concat_axis=0, tiled=True)  10.6 us
    unnamed x24, local copies, waits for them, and re-layouts  3.38 us
  transfers between devices with their start and end apart: 28, of which 18 were waited for; matrix products, arithmetic and copies ran while one was open for 0% of the time, Pallas kernels for 5%

profile of v6, /device:TPU:0, one launch (start us, length us, event | category | flops | bytes accessed | tf_op | source)
XLA Modules:
  0.0 122.5 jit_solution(5538695816623535074)
XLA Ops:
  0.0 0.8 copy-done.11
  1.7 7.3 %all-to-all-start = ((bf16[8,144,128]{2,1,0:T(8,128)(2,1)}), bf16[8,144,128]{2,1,0:T(8,128)(2,1)S(1)}, u32[]{:S(2)}, u32[]{:S(2)}) async-start(bf16[8,144,128]{2,1,0:T(8,128)(2,1)} %get-tuple-element.28), calls=%async_computation | async-start | bytes 589824 | tf_op jit(solution)/shard_map/all_to_all | solution.py:45
  8.9 2.0 %collective-permute-start.3 = (bf16[576,256]{1,0:T(8,128)(2,1)S(1)}, bf16[576,256]{1,0:T(8,128)(2,1)S(1)}, u32[]{:S(2)}, u32[]{:S(2)}) collective-permute-start(bf16[576,256]{1,0:T(8,128)(2,1)S(1)} %bitcast.5), channel_id=1, source_target_pairs={{0,2},{1,3},{2,0},{3,1},{4,6},{5,7},{6,4},{7,5},{8,10},{9,11},{10,... | collective-permute-start | bytes 884744 | tf_op jit(solution)/shard_map/ppermute | solution.py:56
  10.9 1.5 %collective-permute-start.2 = (bf16[576,256]{1,0:T(8,128)(2,1)S(1)}, bf16[576,256]{1,0:T(8,128)(2,1)S(1)}, u32[]{:S(2)}, u32[]{:S(2)}) collective-permute-start(bf16[576,256]{1,0:T(8,128)(2,1)S(1)} %bitcast.6), channel_id=1, source_target_pairs={{0,1},{1,0},{2,3},{3,2},{4,5},{5,4},{6,7},{7,6},{8,9},{9,8},{10,11... | collective-permute-start | bytes 884744 | tf_op jit(solution)/shard_map/ppermute | solution.py:56
  12.4 7.0 %all-to-all-done.x_ref = bf16[8,144,128]{2,1,0:T(8,128)(2,1)S(1)} async-done(((bf16[8,144,128]{2,1,0:T(8,128)(2,1)}), bf16[8,144,128]{2,1,0:T(8,128)(2,1)S(1)}, u32[]{:S(2)}, u32[]{:S(2)}) %all-to-all-start) | async-done | bytes 294944 | tf_op jit(solution)/shard_map/all_to_all | solution.py:45
  20.0 1.3 %collective-permute-done.from_pair_ref.z13_ref = bf16[2,256,128]{2,1,0:T(8,128)(2,1)S(1)} collective-permute-done((bf16[2,256,128]{2,1,0:T(8,128)(2,1)S(1)}, bf16[2,256,128]{2,1,0:T(8,128)(2,1)S(1)}, u32[]{:S(2)}, u32[]{:S(2)}) %collective-permute-start) | collective-permute-done | bytes 131104 | tf_op jit(solution)/shard_map/ppermute | solution.py:56
  21.3 1.6 %collective-permute-start.1 = (bf16[256,128]{1,0:T(8,128)(2,1)S(1)}, bf16[256,128]{1,0:T(8,128)(2,1)S(1)}, u32[]{:S(2)}, u32[]{:S(2)}) collective-permute-start(bf16[256,128]{1,0:T(8,128)(2,1)S(1)} %pair_sum.1), channel_id=1, source_target_pairs={{0,16},{8,24},{16,0},{24,8},{1,17},{9,25},{17,1},{25,9},{2,18},{10... | collective-permute-start | bytes 196616 | tf_op jit(solution)/shard_map/ppermute | solution.py:56
  22.9 0.9 collective-permute-start.4
  23.8 2.4 %collective-permute-start.11 = (bf16[576,256]{1,0:T(8,128)(2,1)S(1)}, bf16[576,256]{1,0:T(8,128)(2,1)S(1)}, u32[]{:S(2)}, u32[]{:S(2)}) collective-permute-start(bf16[576,256]{1,0:T(8,128)(2,1)S(1)} %bitcast.7), channel_id=1, source_target_pairs={{0,4},{1,5},{2,6},{3,7},{4,0},{5,1},{6,2},{7,3},{8,12},{9,13},{10,... | collective-permute-start | bytes 884744 | tf_op jit(solution)/shard_map/ppermute | solution.py:56
  26.8 3.3 %all-to-all-start.1 = ((bf16[8,32,128]{2,1,0:T(8,128)(2,1)}), bf16[8,32,128]{2,1,0:T(8,128)(2,1)S(1)}, u32[]{:S(2)}, u32[]{:S(2)}) async-start(bf16[8,32,128]{2,1,0:T(8,128)(2,1)} %share_sum.1), calls=%async_computation.1 | async-start | bytes 131072 | tf_op jit(solution)/shard_map/all_to_all | solution.py:45
  30.9 0.9 collective-permute-done.4.refs_3_
  31.8 9.2 %all-to-all-done.1.share_ref = bf16[8,32,128]{2,1,0:T(8,128)(2,1)S(1)} async-done(((bf16[8,32,128]{2,1,0:T(8,128)(2,1)}), bf16[8,32,128]{2,1,0:T(8,128)(2,1)S(1)}, u32[]{:S(2)}, u32[]{:S(2)}) %all-to-all-start.1) | async-done | bytes 65568 | tf_op jit(solution)/shard_map/all_to_all | solution.py:45
  41.8 3.6 %collective-permute-done.6.refs_2_ = bf16[9,32,128]{2,1,0:T(8,128)(2,1)S(1)} collective-permute-done((bf16[9,32,128]{2,1,0:T(8,128)(2,1)S(1)}, bf16[9,32,128]{2,1,0:T(8,128)(2,1)S(1)}, u32[]{:S(2)}, u32[]{:S(2)}) %collective-permute-start.6) | collective-permute-done | bytes 73760 | tf_op jit(solution)/shard_map/ppermute | solution.py:56
  45.4 0.9 collective-permute-start.13
  48.0 2.5 %copy-done = bf16[2,10,128,1024]{3,2,1,0:T(8,128)(2,1)S(1)} copy-done((bf16[2,10,128,1024]{3,2,1,0:T(8,128)(2,1)S(1)}, bf16[2,10,128,1024]{3,2,1,0:T(8,128)(2,1)}, u32[]{:S(2)}) %copy-start) | copy-done | bytes 5242904
  50.5 3.4 %attention.1 = (bf16[8,16,384]{2,1,0:T(8,128)(2,1)S(1)}, bf16[8,16,384]{2,1,0:T(8,128)(2,1)S(1)}) custom-call(bf16[9,32,128]{2,1,0:T(8,128)(2,1)S(1)} %pack_shares.1.refs_0_, bf16[9,32,128]{2,1,0:T(8,128)(2,1)S(1)} %collective-permute-done.5.refs_1_, bf16[9,32,128]{2,1,0:T(8,128)(2,1)S(1)} %collective-permute-done.6.refs_2_, ...), custom_call_target="tpu_custom_call" | custom-call | tf_op jit(solution)/shard_map/attention/pallas_call | solution.py:33
  54.2 1.1 collective-permute-done.8.pair_ref
  55.5 1.7 %collective-permute-start.14 = (bf16[576,256]{1,0:T(8,128)(2,1)S(1)}, bf16[576,256]{1,0:T(8,128)(2,1)S(1)}, u32[]{:S(2)}, u32[]{:S(2)}) collective-permute-start(bf16[576,256]{1,0:T(8,128)(2,1)S(1)} %collective-permute-done.13.refs_6_), channel_id=1, source_target_pairs={{0,1},{1,0},{2,3},{3,2},{4,5},{5,4},{6,7},{7,6},{8,9},{9,8},{10,11... | collective-permute-start | bytes 884744 | tf_op jit(solution)/shard_map/ppermute | solution.py:56
  57.7 4.1 %collective-permute-done.9.across_ref = bf16[8,16,384]{2,1,0:T(8,128)(2,1)S(1)} collective-permute-done((bf16[8,16,384]{2,1,0:T(8,128)(2,1)S(1)}, bf16[8,16,384]{2,1,0:T(8,128)(2,1)S(1)}, u32[]{:S(2)}, u32[]{:S(2)}) %collective-permute-start.9) | collective-permute-done | bytes 98336 | tf_op jit(solution)/shard_map/ppermute | solution.py:56
  62.1 1.2 %collective-permute-done.10.other_ref = bf16[8,16,256]{2,1,0:T(8,128)(2,1)S(1)} collective-permute-done((bf16[8,16,256]{2,1,0:T(8,128)(2,1)S(1)}, bf16[8,16,256]{2,1,0:T(8,128)(2,1)S(1)}, u32[]{:S(2)}, u32[]{:S(2)}) %collective-permute-start.10) | collective-permute-done | bytes 65568 | tf_op jit(solution)/shard_map/ppermute | solution.py:56
  63.3 1.3 %collective-permute-done.14.refs_7_ = bf16[576,256]{1,0:T(8,128)(2,1)S(1)} collective-permute-done((bf16[576,256]{1,0:T(8,128)(2,1)S(1)}, bf16[576,256]{1,0:T(8,128)(2,1)S(1)}, u32[]{:S(2)}, u32[]{:S(2)}) %collective-permute-start.14) | collective-permute-done | bytes 294944 | tf_op jit(solution)/shard_map/ppermute | solution.py:56
  65.7 1.1 collective-permute-start.16
  67.4 1.3 %collective-permute-done.17.refs_3_ = f32[32,128]{1,0:T(8,128)S(1)} collective-permute-done((f32[32,128]{1,0:T(8,128)S(1)}, f32[32,128]{1,0:T(8,128)S(1)}, u32[]{:S(2)}, u32[]{:S(2)}) %collective-permute-start.17) | collective-permute-done | bytes 16416 | tf_op jit(solution)/shard_map/ppermute | solution.py:56
  69.7 14.8 %all_to_all.20.ff_ref = bf16[8,144,128]{2,1,0:T(8,128)(2,1)S(1)} all-to-all(bf16[8,144,128]{2,1,0:T(8,128)(2,1)S(1)} %get-tuple-element.44), channel_id=1, replica_groups=mesh['gx'=4,'gy'=8] {'gy'}, dimensions={0} | all-to-all | bytes 589824 | tf_op jit(solution)/shard_map/all_to_all | solution.py:45
  84.5 1.2 gate_up.1
  85.8 2.0 %collective-permute-done.18.from_pair_ref.z13_ref = bf16[2,64,2304]{2,1,0:T(8,128)(2,1)S(1)} collective-permute-done((bf16[2,64,2304]{2,1,0:T(8,128)(2,1)S(1)}, bf16[2,64,2304]{2,1,0:T(8,128)(2,1)S(1)}, u32[]{:S(2)}, u32[]{:S(2)}) %collective-permute-start.18) | collective-permute-done | bytes 589856 | tf_op jit(solution)/shard_map/ppermute | solution.py:56
  88.4 8.6 %collective-permute-done.19.z2_ref = bf16[64,2304]{1,0:T(8,128)(2,1)S(1)} collective-permute-done((bf16[64,2304]{1,0:T(8,128)(2,1)S(1)}, bf16[64,2304]{1,0:T(8,128)(2,1)S(1)}, u32[]{:S(2)}, u32[]{:S(2)}) %collective-permute-start.19) | collective-permute-done | bytes 294944 | tf_op jit(solution)/shard_map/ppermute | solution.py:56
  97.7 4.7 %collective-permute-done.21.refs_2_ = bf16[64,1152]{1,0:T(8,128)(2,1)S(1)} collective-permute-done((bf16[64,1152]{1,0:T(8,128)(2,1)S(1)}, bf16[64,1152]{1,0:T(8,128)(2,1)S(1)}, u32[]{:S(2)}, u32[]{:S(2)}) %collective-permute-start.21) | collective-permute-done | bytes 147488 | tf_op jit(solution)/shard_map/ppermute | solution.py:56
  102.4 1.4 %collective-permute-done.22.refs_3_ = bf16[64,1152]{1,0:T(8,128)(2,1)S(1)} collective-permute-done((bf16[64,1152]{1,0:T(8,128)(2,1)S(1)}, bf16[64,1152]{1,0:T(8,128)(2,1)S(1)}, u32[]{:S(2)}, u32[]{:S(2)}) %collective-permute-start.22) | collective-permute-done | bytes 147488 | tf_op jit(solution)/shard_map/ppermute | solution.py:56
  104.5 13.3 %all_to_all.21.parts_ref = bf16[8,144,128]{2,1,0:T(8,128)(2,1)S(1)} all-to-all(bf16[8,144,128]{2,1,0:T(8,128)(2,1)S(1)} %project_down.1), channel_id=1, replica_groups=mesh['gx'=4,'gy'=8] {'gy'}, dimensions={0} | all-to-all | bytes 589824 | tf_op jit(solution)/shard_map/all_to_all | solution.py:45
  118.5 1.3 %collective-permute-start.23 = (f32[32,128]{1,0:T(8,128)S(1)}, f32[32,128]{1,0:T(8,128)S(1)}, u32[]{:S(2)}, u32[]{:S(2)}) collective-permute-start(f32[32,128]{1,0:T(8,128)S(1)} %get-tuple-element.48.refs_0_), channel_id=1, source_target_pairs={{0,8},{8,0},{16,24},{24,16},{1,9},{9,1},{17,25},{25,17},{2,10},{10... | collective-permute-start | bytes 49160 | tf_op jit(solution)/shard_map/ppermute | solution.py:56
  119.8 1.3 %collective-permute-done.25.refs_3_ = f32[32,128]{1,0:T(8,128)S(1)} collective-permute-done((f32[32,128]{1,0:T(8,128)S(1)}, f32[32,128]{1,0:T(8,128)S(1)}, u32[]{:S(2)}, u32[]{:S(2)}) %collective-permute-start.25) | collective-permute-done | bytes 16416 | tf_op jit(solution)/shard_map/ppermute | solution.py:56
  (70 shorter events, 12.5 us)
Async XLA Ops:
  1.7 17.7 %all-to-all-start = ((bf16[8,144,128]{2,1,0:T(8,128)(2,1)}), bf16[8,144,128]{2,1,0:T(8,128)(2,1)S(1)}, u32[]{:S(2)}, u32[]{:S(2)}) async-start(bf16[8,144,128]{2,1,0:T(8,128)(2,1)} %get-tuple-element.28), calls=%async_computation | async-start | bytes 589824 | tf_op jit(solution)/shard_map/all_to_all | solution.py:45
  8.9 14.0 %collective-permute-start.3 = (bf16[576,256]{1,0:T(8,128)(2,1)S(1)}, bf16[576,256]{1,0:T(8,128)(2,1)S(1)}, u32[]{:S(2)}, u32[]{:S(2)}) collective-permute-start(bf16[576,256]{1,0:T(8,128)(2,1)S(1)} %bitcast.5), channel_id=1, source_target_pairs={{0,2},{1,3},{2,0},{3,1},{4,6},{5,7},{6,4},{7,5},{8,10},{9,11},{10,... | collective-permute-start | bytes 884744 | tf_op jit(solution)/shard_map/ppermute | solution.py:56
  10.9 12.0 %collective-permute-start.2 = (bf16[576,256]{1,0:T(8,128)(2,1)S(1)}, bf16[576,256]{1,0:T(8,128)(2,1)S(1)}, u32[]{:S(2)}, u32[]{:S(2)}) collective-permute-start(bf16[576,256]{1,0:T(8,128)(2,1)S(1)} %bitcast.6), channel_id=1, source_target_pairs={{0,1},{1,0},{2,3},{3,2},{4,5},{5,4},{6,7},{7,6},{8,9},{9,8},{10,11... | collective-permute-start | bytes 884744 | tf_op jit(solution)/shard_map/ppermute | solution.py:56
  19.9 1.4 %collective-permute-start = (bf16[2,256,128]{2,1,0:T(8,128)(2,1)S(1)}, bf16[2,256,128]{2,1,0:T(8,128)(2,1)S(1)}, u32[]{:S(2)}, u32[]{:S(2)}) collective-permute-start(bf16[2,256,128]{2,1,0:T(8,128)(2,1)S(1)} %get-tuple-element.30), channel_id=1, source_target_pairs={{0,8},{8,0},{16,24},{24,16},{1,9},{9,1},{17,25},{25,17},{2,10},{10... | collective-permute-start | bytes 393224 | tf_op jit(solution)/shard_map/ppermute | solution.py:56
  21.3 4.9 %collective-permute-start.1 = (bf16[256,128]{1,0:T(8,128)(2,1)S(1)}, bf16[256,128]{1,0:T(8,128)(2,1)S(1)}, u32[]{:S(2)}, u32[]{:S(2)}) collective-permute-start(bf16[256,128]{1,0:T(8,128)(2,1)S(1)} %pair_sum.1), channel_id=1, source_target_pairs={{0,16},{8,24},{16,0},{24,8},{1,17},{9,25},{17,1},{25,9},{2,18},{10... | collective-permute-start | bytes 196616 | tf_op jit(solution)/shard_map/ppermute | solution.py:56
  22.9 8.9 %collective-permute-start.4 = (bf16[576,256]{1,0:T(8,128)(2,1)S(1)}, bf16[576,256]{1,0:T(8,128)(2,1)S(1)}, u32[]{:S(2)}, u32[]{:S(2)}) collective-permute-start(bf16[576,256]{1,0:T(8,128)(2,1)S(1)} %collective-permute-done.3.refs_2_), channel_id=1, source_target_pairs={{0,1},{1,0},{2,3},{3,2},{4,5},{5,4},{6,7},{7,6},{8,9},{9,8},{10,11... | collective-permute-start | bytes 884744 | tf_op jit(solution)/shard_map/ppermute | solution.py:56
  23.8 18.0 %collective-permute-start.11 = (bf16[576,256]{1,0:T(8,128)(2,1)S(1)}, bf16[576,256]{1,0:T(8,128)(2,1)S(1)}, u32[]{:S(2)}, u32[]{:S(2)}) collective-permute-start(bf16[576,256]{1,0:T(8,128)(2,1)S(1)} %bitcast.7), channel_id=1, source_target_pairs={{0,4},{1,5},{2,6},{3,7},{4,0},{5,1},{6,2},{7,3},{8,12},{9,13},{10,... | collective-permute-start | bytes 884744 | tf_op jit(solution)/shard_map/ppermute | solution.py:56
  26.2 20.7 %copy-start.9 = (s32[3,8]{1,0:T(4,128)S(1)}, s32[3,8]{1,0:T(4,128)}, u32[]{:S(2)}) copy-start(s32[3,8]{1,0:T(4,128)} %parents_ref.1) | copy-start | bytes 292
  26.2 20.7 %copy-start.10 = (s32[1,33]{1,0:T(1,128)S(1)}, s32[1,33]{1,0:T(1,128)}, u32[]{:S(2)}) copy-start(s32[1,33]{1,0:T(1,128)} %table_ref.1) | copy-start | bytes 400
  26.8 14.1 %all-to-all-start.1 = ((bf16[8,32,128]{2,1,0:T(8,128)(2,1)}), bf16[8,32,128]{2,1,0:T(8,128)(2,1)S(1)}, u32[]{:S(2)}, u32[]{:S(2)}) async-start(bf16[8,32,128]{2,1,0:T(8,128)(2,1)} %share_sum.1), calls=%async_computation.1 | async-start | bytes 131072 | tf_op jit(solution)/shard_map/all_to_all | solution.py:45
  41.1 4.4 %collective-permute-start.6 = (bf16[9,32,128]{2,1,0:T(8,128)(2,1)S(1)}, bf16[9,32,128]{2,1,0:T(8,128)(2,1)S(1)}, u32[]{:S(2)}, u32[]{:S(2)}) collective-permute-start(bf16[9,32,128]{2,1,0:T(8,128)(2,1)S(1)} %pack_shares.1.refs_0_), channel_id=1, source_target_pairs={{0,16},{8,24},{16,0},{24,8},{1,17},{9,25},{17,1},{25,9},{2,18},{10... | collective-permute-start | bytes 221192 | tf_op jit(solution)/shard_map/ppermute | solution.py:56
  41.8 5.9 %collective-permute-start.5 = (bf16[9,32,128]{2,1,0:T(8,128)(2,1)S(1)}, bf16[9,32,128]{2,1,0:T(8,128)(2,1)S(1)}, u32[]{:S(2)}, u32[]{:S(2)}) collective-permute-start(bf16[9,32,128]{2,1,0:T(8,128)(2,1)S(1)} %pack_shares.1.refs_0_), channel_id=1, source_target_pairs={{0,8},{8,0},{16,24},{24,16},{1,9},{9,1},{17,25},{25,17},{2,10},{10... | collective-permute-start | bytes 221192 | tf_op jit(solution)/shard_map/ppermute | solution.py:56
  45.4 10.1 %collective-permute-start.13 = (bf16[576,256]{1,0:T(8,128)(2,1)S(1)}, bf16[576,256]{1,0:T(8,128)(2,1)S(1)}, u32[]{:S(2)}, u32[]{:S(2)}) collective-permute-start(bf16[576,256]{1,0:T(8,128)(2,1)S(1)} %collective-permute-done.11.refs_4_), channel_id=1, source_target_pairs={{0,2},{1,3},{2,0},{3,1},{4,6},{5,7},{6,4},{7,5},{8,10},{9,11},{10,... | collective-permute-start | bytes 884744 | tf_op jit(solution)/shard_map/ppermute | solution.py:56
  46.3 9.2 %collective-permute-start.12 = (bf16[576,256]{1,0:T(8,128)(2,1)S(1)}, bf16[576,256]{1,0:T(8,128)(2,1)S(1)}, u32[]{:S(2)}, u32[]{:S(2)}) collective-permute-start(bf16[576,256]{1,0:T(8,128)(2,1)S(1)} %collective-permute-done.11.refs_4_), channel_id=1, source_target_pairs={{0,1},{1,0},{2,3},{3,2},{4,5},{5,4},{6,7},{7,6},{8,9},{9,8},{10,11... | collective-permute-start | bytes 884744 | tf_op jit(solution)/shard_map/ppermute | solution.py:56
  46.7 1.3 %collective-permute-start.7 = (bf16[9,32,128]{2,1,0:T(8,128)(2,1)S(1)}, bf16[9,32,128]{2,1,0:T(8,128)(2,1)S(1)}, u32[]{:S(2)}, u32[]{:S(2)}) collective-permute-start(bf16[9,32,128]{2,1,0:T(8,128)(2,1)S(1)} %collective-permute-done.6.refs_2_), channel_id=1, source_target_pairs={{0,8},{8,0},{16,24},{24,16},{1,9},{9,1},{17,25},{25,17},{2,10},{10... | collective-permute-start | bytes 221192 | tf_op jit(solution)/shard_map/ppermute | solution.py:56
  53.9 1.4 %collective-permute-start.8 = (bf16[8,16,384]{2,1,0:T(8,128)(2,1)S(1)}, bf16[8,16,384]{2,1,0:T(8,128)(2,1)S(1)}, u32[]{:S(2)}, u32[]{:S(2)}) collective-permute-start(bf16[8,16,384]{2,1,0:T(8,128)(2,1)S(1)} %get-tuple-element.38), channel_id=1, source_target_pairs={{0,8},{8,0},{16,24},{24,16},{1,9},{9,1},{17,25},{25,17},{2,10},{10... | collective-permute-start | bytes 294920 | tf_op jit(solution)/shard_map/ppermute | solution.py:56
  55.5 9.2 %collective-permute-start.14 = (bf16[576,256]{1,0:T(8,128)(2,1)S(1)}, bf16[576,256]{1,0:T(8,128)(2,1)S(1)}, u32[]{:S(2)}, u32[]{:S(2)}) collective-permute-start(bf16[576,256]{1,0:T(8,128)(2,1)S(1)} %collective-permute-done.13.refs_6_), channel_id=1, source_target_pairs={{0,1},{1,0},{2,3},{3,2},{4,5},{5,4},{6,7},{7,6},{8,9},{9,8},{10,11... | collective-permute-start | bytes 884744 | tf_op jit(solution)/shard_map/ppermute | solution.py:56
  57.2 4.6 %collective-permute-start.9 = (bf16[8,16,384]{2,1,0:T(8,128)(2,1)S(1)}, bf16[8,16,384]{2,1,0:T(8,128)(2,1)S(1)}, u32[]{:S(2)}, u32[]{:S(2)}) collective-permute-start(bf16[8,16,384]{2,1,0:T(8,128)(2,1)S(1)} %pair_terms.1.own_ref), channel_id=1, source_target_pairs={{0,16},{8,24},{16,0},{24,8},{1,17},{9,25},{17,1},{25,9},{2,18},{10... | collective-permute-start | bytes 294920 | tf_op jit(solution)/shard_map/ppermute | solution.py:56
  62.0 22.5 %copy-start.2 = (bf16[576,1152]{1,0:T(8,128)(2,1)S(1)}, bf16[576,1152]{1,0:T(8,128)(2,1)}, u32[]{:S(2)}) copy-start(bf16[576,1152]{1,0:T(8,128)(2,1)} %gate_ref.1) | copy-start | bytes 3981316
  62.0 22.5 %copy-start.3 = (bf16[576,1152]{1,0:T(8,128)(2,1)S(1)}, bf16[576,1152]{1,0:T(8,128)(2,1)}, u32[]{:S(2)}) copy-start(bf16[576,1152]{1,0:T(8,128)(2,1)} %up_ref.1) | copy-start | bytes 3981316
  62.0 1.3 %collective-permute-start.10 = (bf16[8,16,256]{2,1,0:T(8,128)(2,1)S(1)}, bf16[8,16,256]{2,1,0:T(8,128)(2,1)S(1)}, u32[]{:S(2)}, u32[]{:S(2)}) collective-permute-start(bf16[8,16,256]{2,1,0:T(8,128)(2,1)S(1)} %divide.1.own_ref), channel_id=1, source_target_pairs={{0,8},{8,0},{16,24},{24,16},{1,9},{9,1},{17,25},{25,17},{2,10},{10... | collective-permute-start | bytes 196616 | tf_op jit(solution)/shard_map/ppermute | solution.py:56
  65.5 3.2 %collective-permute-start.17 = (f32[32,128]{1,0:T(8,128)S(1)}, f32[32,128]{1,0:T(8,128)S(1)}, u32[]{:S(2)}, u32[]{:S(2)}) collective-permute-start(f32[32,128]{1,0:T(8,128)S(1)} %get-tuple-element.42.refs_0_), channel_id=1, source_target_pairs={{0,24},{8,16},{16,8},{24,0},{1,25},{9,17},{17,9},{25,1},{2,26},{10... | collective-permute-start | bytes 49160 | tf_op jit(solution)/shard_map/ppermute | solution.py:56
  65.7 3.7 %collective-permute-start.16 = (f32[32,128]{1,0:T(8,128)S(1)}, f32[32,128]{1,0:T(8,128)S(1)}, u32[]{:S(2)}, u32[]{:S(2)}) collective-permute-start(f32[32,128]{1,0:T(8,128)S(1)} %get-tuple-element.42.refs_0_), channel_id=1, source_target_pairs={{0,16},{8,24},{16,0},{24,8},{1,17},{9,25},{17,1},{25,9},{2,18},{10... | collective-permute-start | bytes 49160 | tf_op jit(solution)/shard_map/ppermute | solution.py:56
  66.8 2.6 %collective-permute-start.15 = (f32[32,128]{1,0:T(8,128)S(1)}, f32[32,128]{1,0:T(8,128)S(1)}, u32[]{:S(2)}, u32[]{:S(2)}) collective-permute-start(f32[32,128]{1,0:T(8,128)S(1)} %get-tuple-element.42.refs_0_), channel_id=1, source_target_pairs={{0,8},{8,0},{16,24},{24,16},{1,9},{9,1},{17,25},{25,17},{2,10},{10... | collective-permute-start | bytes 49160 | tf_op jit(solution)/shard_map/ppermute | solution.py:56
  85.7 2.1 %collective-permute-start.18 = (bf16[2,64,2304]{2,1,0:T(8,128)(2,1)S(1)}, bf16[2,64,2304]{2,1,0:T(8,128)(2,1)S(1)}, u32[]{:S(2)}, u32[]{:S(2)}) collective-permute-start(bf16[2,64,2304]{2,1,0:T(8,128)(2,1)S(1)} %get-tuple-element.46), channel_id=1, source_target_pairs={{0,8},{8,0},{16,24},{24,16},{1,9},{9,1},{17,25},{25,17},{2,10},{10... | collective-permute-start | bytes 1769480 | tf_op jit(solution)/shard_map/ppermute | solution.py:56
  87.8 9.1 %collective-permute-start.19 = (bf16[64,2304]{1,0:T(8,128)(2,1)S(1)}, bf16[64,2304]{1,0:T(8,128)(2,1)S(1)}, u32[]{:S(2)}, u32[]{:S(2)}) collective-permute-start(bf16[64,2304]{1,0:T(8,128)(2,1)S(1)} %pair_sum_ff.1), channel_id=1, source_target_pairs={{0,16},{8,24},{16,0},{24,8},{1,17},{9,25},{17,1},{25,9},{2,18},{10... | collective-permute-start | bytes 884744 | tf_op jit(solution)/shard_map/ppermute | solution.py:56
  97.2 5.2 %collective-permute-start.21 = (bf16[64,1152]{1,0:T(8,128)(2,1)S(1)}, bf16[64,1152]{1,0:T(8,128)(2,1)S(1)}, u32[]{:S(2)}, u32[]{:S(2)}) collective-permute-start(bf16[64,1152]{1,0:T(8,128)(2,1)S(1)} %activate.1.refs_0_), channel_id=1, source_target_pairs={{0,16},{8,24},{16,0},{24,8},{1,17},{9,25},{17,1},{25,9},{2,18},{10... | collective-permute-start | bytes 442376 | tf_op jit(solution)/shard_map/ppermute | solution.py:56
  97.7 4.7 %collective-permute-start.20 = (bf16[64,1152]{1,0:T(8,128)(2,1)S(1)}, bf16[64,1152]{1,0:T(8,128)(2,1)S(1)}, u32[]{:S(2)}, u32[]{:S(2)}) collective-permute-start(bf16[64,1152]{1,0:T(8,128)(2,1)S(1)} %activate.1.refs_0_), channel_id=1, source_target_pairs={{0,8},{8,0},{16,24},{24,16},{1,9},{9,1},{17,25},{25,17},{2,10},{10... | collective-permute-start | bytes 442376 | tf_op jit(solution)/shard_map/ppermute | solution.py:56
  102.4 1.4 %collective-permute-start.22 = (bf16[64,1152]{1,0:T(8,128)(2,1)S(1)}, bf16[64,1152]{1,0:T(8,128)(2,1)S(1)}, u32[]{:S(2)}, u32[]{:S(2)}) collective-permute-start(bf16[64,1152]{1,0:T(8,128)(2,1)S(1)} %collective-permute-done.21.refs_2_), channel_id=1, source_target_pairs={{0,8},{8,0},{16,24},{24,16},{1,9},{9,1},{17,25},{25,17},{2,10},{10... | collective-permute-start | bytes 442376 | tf_op jit(solution)/shard_map/ppermute | solution.py:56
  118.0 3.2 %collective-permute-start.25 = (f32[32,128]{1,0:T(8,128)S(1)}, f32[32,128]{1,0:T(8,128)S(1)}, u32[]{:S(2)}, u32[]{:S(2)}) collective-permute-start(f32[32,128]{1,0:T(8,128)S(1)} %get-tuple-element.48.refs_0_), channel_id=1, source_target_pairs={{0,24},{8,16},{16,8},{24,0},{1,25},{9,17},{17,9},{25,1},{2,26},{10... | collective-permute-start | bytes 49160 | tf_op jit(solution)/shard_map/ppermute | solution.py:56
  118.0 3.8 %collective-permute-start.24 = (f32[32,128]{1,0:T(8,128)S(1)}, f32[32,128]{1,0:T(8,128)S(1)}, u32[]{:S(2)}, u32[]{:S(2)}) collective-permute-start(f32[32,128]{1,0:T(8,128)S(1)} %get-tuple-element.48.refs_0_), channel_id=1, source_target_pairs={{0,16},{8,24},{16,0},{24,8},{1,17},{9,25},{17,1},{25,9},{2,18},{10... | collective-permute-start | bytes 49160 | tf_op jit(solution)/shard_map/ppermute | solution.py:56
  118.5 3.3 %collective-permute-start.23 = (f32[32,128]{1,0:T(8,128)S(1)}, f32[32,128]{1,0:T(8,128)S(1)}, u32[]{:S(2)}, u32[]{:S(2)}) collective-permute-start(f32[32,128]{1,0:T(8,128)S(1)} %get-tuple-element.48.refs_0_), channel_id=1, source_target_pairs={{0,8},{8,0},{16,24},{24,16},{1,9},{9,1},{17,25},{25,17},{2,10},{10... | collective-permute-start | bytes 49160 | tf_op jit(solution)/shard_map/ppermute | solution.py:56
  (8 other events, 107.9 us)

commit v7 on v6

--- a/solution.py
+++ b/solution.py
@@ -18,6 +18,7 @@
 ROPE_BASE = 10000.0
 REPS = HEADS // KV_HEADS
 WIDE = HEAD_DIM + PAGE
+HALF_PAGE = PAGE // 2
 BF = jnp.bfloat16
 F32 = jnp.float32
 MIB = 1024 * 1024
@@ -241,10 +242,10 @@
     x_all = exchange(x_all, "gy")
 
     w_own = w_out.T
-    w_blocks = [w_own, permute(w_own, "gy", 1), permute(w_own, "gy", 2)] + [None] * (ny - 3)
-    (w_late, _, w_later), _ = lax.optimization_barrier((w_blocks[:3], x_all))
-    w_blocks[4] = permute(w_late, "gy", 4)
-    w_blocks[3] = permute(w_later, "gy", 1)
+    w_blocks = {0: w_own, 1: permute(w_own, "gy", 1), 4: permute(w_own, "gy", 4)}
+    w_late, _ = lax.optimization_barrier((w_blocks, x_all))
+    w_blocks[2] = permute(w_late[0], "gy", 2)
+    w_blocks[5] = permute(w_late[4], "gy", 1)
 
     def project(x_ref, gain_ref, q_ref, k_ref, v_ref, z0_ref, z2_ref, z13_ref, held):
         gain = 1.0 + gain_ref[0:1]
@@ -283,24 +284,26 @@
         total = z0_ref[...].astype(F32) + z13_ref[0].astype(F32) + z2_ref[...].astype(F32)
         out_ref[...] = total.reshape(ny, rows, HALF).astype(BF)
 
-    (shares,) = run(
-        "share_sum", share_sum, [((ny, rows, HALF), BF)], (z0, z13, z2), micros=6
-    )
-    cos, sin = rope_tables(lengths, rows, steps)
-    tables = make_tables(block_table, lengths, parents, cache_pool.shape[1], rows, steps)
+    (shares,) = run("share_sum", share_sum, [((ny, rows, HALF), BF)], (z0, z13, z2))
+    shares, *late = lax.optimization_barrier((shares, block_table, lengths, parents))
+    cos, sin = rope_tables(late[1], rows, steps)
+    tables = make_tables(*late, cache_pool.shape[1], rows, steps)
     shares = exchange(shares, "gy")
-    shares, _ = lax.optimization_barrier((shares, w_blocks[3]))
+    beside = tables, cos, sin, w_blocks[2], w_blocks[5]
+    shares, (tables, cos, sin, *_) = lax.optimization_barrier((shares, beside))
 
     def pack_shares(share_ref, x_ref, out_ref):
         x = x_ref[...].astype(F32)
         out_ref[0:ny] = share_ref[...]
         out_ref[ny] = high_low(row_sum(x * x), HALF).astype(BF)
 
-    (shares,) = run("pack_shares", pack_shares, [((ny + 1, rows, HALF), BF)], (shares, x_own))
+    (shares,) = run(
+        "pack_shares", pack_shares, [((ny + 1, rows, HALF), BF)], (shares, x_own), micros=5
+    )
     shares = gather_gx(shares)
-    _, w_late = lax.optimization_barrier((shares[2], w_blocks[4]))
-    w_blocks[6] = permute(w_late, "gy", 2)
-    w_blocks[5] = permute(w_late, "gy", 1)
+    w_late, _ = lax.optimization_barrier((w_blocks, shares[2]))
+    w_blocks[6] = permute(w_late[4], "gy", 2)
+    w_blocks[3] = permute(w_late[2], "gy", 1)
 
     def attention(*refs):
         a_refs, tables, pool_ref, outs = refs[:nx], refs[nx : nx + 4], refs[nx + 4], refs[nx + 5 :]
@@ -309,15 +312,19 @@
         core = me & 1
         for n, ref in enumerate(a_refs):
             held[me ^ n] = ref[...]
+        den_held[...] = jnp.zeros(den_held.shape, F32)
+        lane = lax.broadcasted_iota(jnp.int32, (2, half, PAGE), 2)
 
         def store(head, num, den):
             num_held[head] = num.reshape(REPS, 2, half, HEAD_DIM)
-            den_held[head] = high_low(den, PAGE).reshape(REPS, 2, half, PAGE)
+            den = high_low(den, PAGE).reshape(REPS, 2, half, PAGE)
             for rep in range(REPS):
+                at = REPS * head + rep
+                den_held[...] = jnp.where(lane % HALF_PAGE == at, den[rep], den_held[...])
                 for n, out in enumerate((own_ref, pair_ref)):
-                    at = REPS * head + rep
-                    out[at, :, 0:HEAD_DIM] = num_held[head, rep, core ^ n].astype(BF)
-                    out[at, :, HEAD_DIM:] = den_held[head, rep, core ^ n].astype(BF)
+                    for tile in range(2):
+                        here = num_held[head, rep, core ^ n, :, tile * PAGE : (tile + 1) * PAGE]
+                        out[2 * at + tile] = here.astype(BF)
 
         attend(
             lambda share, which: held[share, which],
@@ -327,8 +334,10 @@
             (keys_ref, sems),
             store,
         )
-
-    shape = (HEADS, half, WIDE)
+        for n, out in enumerate((own_ref, pair_ref)):
+            out[2 * HEADS] = den_held[core ^ n].astype(BF)
+
+    shape = (2 * HEADS + 1, half, PAGE)
     own, pair = run(
         "attention",
         attention,
@@ -338,30 +347,37 @@
         + [
             pltpu.VMEM((nx,) + shares[0].shape, BF),
             pltpu.VMEM((KV_HEADS, REPS, 2, half, HEAD_DIM), F32),
-            pltpu.VMEM((KV_HEADS, REPS, 2, half, PAGE), F32),
+            pltpu.VMEM((2, half, PAGE), F32),
         ],
         limit=24,
         specs={nx + 4: IN_HBM},
     )
+    w_late, _ = lax.optimization_barrier((w_blocks, own))
+    w_blocks[7] = permute(w_late[6], "gy", 1)
     pair = permute(pair, "gx", 1)
 
     def pair_terms(own_ref, pair_ref, out_ref):
         total = own_ref[...].astype(F32) + pair_ref[...].astype(F32)
-        den = total[..., HEAD_DIM : HEAD_DIM + 1] + total[..., WIDE - 1 :]
-        out_ref[..., 0:HEAD_DIM] = total[..., 0:HEAD_DIM].astype(BF)
-        out_ref[..., HEAD_DIM:] = high_low(den, PAGE).astype(BF)
+        out_ref[0 : 2 * HEADS] = total[0 : 2 * HEADS].astype(BF)
+        den = total[2 * HEADS]
+        den = den[:, :HALF_PAGE] + den[:, HALF_PAGE:]
+        high = den.astype(BF).astype(F32)
+        out_ref[2 * HEADS] = jnp.concatenate([high, den - high], axis=1).astype(BF)
 
     (own,) = run("pair_terms", pair_terms, [(shape, BF)], (own, pair))
     across = permute(own, "gx", 2)
-    _, w_last, _ = lax.optimization_barrier((own, w_blocks[6], w_blocks[5]))
-    w_blocks[7] = permute(w_last, "gy", 1)
 
     def divide(own_ref, across_ref, out_ref):
         total = own_ref[...].astype(F32) + across_ref[...].astype(F32)
-        den = total[..., HEAD_DIM : HEAD_DIM + 1] + total[..., WIDE - 1 :]
-        out_ref[...] = (total[..., 0:HEAD_DIM] / den).astype(BF)
-
-    (attended,) = run("divide", divide, [((HEADS, half, HEAD_DIM), BF)], (own, across))
+        den = total[2 * HEADS]
+        den = den[:, :HALF_PAGE] + den[:, HALF_PAGE:]
+        for head in range(HEADS):
+            scale = 1.0 / den[:, head : head + 1]
+            for tile in range(2):
+                at = 2 * head + tile
+                out_ref[at] = (total[at] * scale).astype(BF)
+
+    (attended,) = run("divide", divide, [((2 * HEADS, half, PAGE), BF)], (own, across))
     others = permute(attended, "gx", 1)
 
     def project_out(own_ref, other_ref, x_ref, gain_ref, *refs):
@@ -371,7 +387,9 @@
         me = my("gy")
         attn = jnp.zeros((rows, width), F32)
         for m, w_ref in enumerate(w_refs):
-            flat = jnp.concatenate([held[0, me ^ m], held[1, me ^ m]], axis=0)
+            at = 2 * (me ^ m)
+            flat = [jnp.concatenate([held[n, at], held[n, at + 1]], axis=1) for n in range(2)]
+            flat = jnp.concatenate(flat, axis=0)
             attn = attn + lax.dot_general(flat, w_ref[...], NT, preferred_element_type=F32)
         attn_ref[...] = attn
         x = x_ref[...].astype(F32)
@@ -386,8 +404,8 @@
         "project_out",
         project_out,
         [((rows, width), F32), ((rows, PAGE), F32)],
-        (attended, others, x_own, norm_gains, *w_blocks),
-        scratch=[pltpu.VMEM((2, HEADS, half, HEAD_DIM), BF)],
+        (attended, others, x_own, norm_gains, *[w_blocks[m] for m in range(ny)]),
+        scratch=[pltpu.VMEM((2, 2 * HEADS, half, PAGE), BF)],
     )
     sums = trade([sums] * nx, "gx")
 

time: 123 us -> 126 us (1.024)
  waiting for transfers between devices: 50.8 us -> 57.6 us
  local copies, waits for them, and re-layouts: 3.38 us -> 0.9 us
  blocking collectives: 28.1 us -> 26.3 us
    ppermute x26, waiting for transfers between devices: 34.6 us -> 38.7 us  [permute(): return lax.ppermute(values, axis, [(i, i ^ m) for i in range(count)])]
    all_to_all x2, waiting for transfers between devices: 16.2 us -> 19 us  [exchange(): return lax.all_to_all(values, axes, split_axis=0, concat_axis=0, tiled=True)]
    unnamed x24 -> x26, local copies, waits for them, and re-layouts: 3.38 us -> 0.9 us
    all_to_all x2, blocking collectives: 28.1 us -> 26.3 us  [exchange(): return lax.all_to_all(values, axes, split_axis=0, concat_axis=0, tiled=True)]
  transfers between devices with their start and end apart: 28 -> 28, of which waited for: 18 -> 20; matrix products, arithmetic and copies ran while one was open for 0% -> 0% of each run, Pallas kernels for 5% -> 4%
where the time goes in v7:
time: 126 us
  waiting for transfers between devices  57.6 us (46%)
  starting transfers between devices  29.1 us (23%)
  blocking collectives  26.3 us (21%)
  Pallas kernels  10.7 us (8%)
    ppermute x26, waiting for transfers between devices, permute(): return lax.ppermute(values, axis, [(i, i ^ m) for i in range(count)])  38.7 us
    all_to_all x2, blocking collectives, exchange(): return lax.all_to_all(values, axes, split_axis=0, concat_axis=0, tiled=True)  26.3 us
    all_to_all x2, waiting for transfers between devices, exchange(): return lax.all_to_all(values, axes, split_axis=0, concat_axis=0, tiled=True)  19 us
    ppermute x26, starting transfers between devices, permute(): return lax.ppermute(values, axis, [(i, i ^ m) for i in range(count)])  18.4 us
    all_to_all x2, starting transfers between devices, exchange(): return lax.all_to_all(values, axes, split_axis=0, concat_axis=0, tiled=True)  10.7 us
    pallas_call x17, Pallas kernels, run(): pl.pallas_call(kernel, out_shape=[jax.ShapeDtypeStruct(s, d) for s, d in...  10.7 us
  transfers between devices with their start and end apart: 28, of which 20 were waited for; matrix products, arithmetic and copies ran while one was open for 0% of the time, Pallas kernels for 4%

profile of v7, /device:TPU:0, one launch (start us, length us, event | category | flops | bytes accessed | tf_op | source)
XLA Modules:
  0.0 125.6 jit_solution(12797742319507486905)
XLA Ops:
  0.0 0.8 copy-done.10
  1.7 7.4 %all-to-all-start = ((bf16[8,144,128]{2,1,0:T(8,128)(2,1)}), bf16[8,144,128]{2,1,0:T(8,128)(2,1)S(1)}, u32[]{:S(2)}, u32[]{:S(2)}) async-start(bf16[8,144,128]{2,1,0:T(8,128)(2,1)} %get-tuple-element.37), calls=%async_computation | async-start | bytes 589824 | tf_op jit(solution)/shard_map/all_to_all | solution.py:46
  9.1 2.9 %collective-permute-start.3 = (bf16[576,256]{1,0:T(8,128)(2,1)S(1)}, bf16[576,256]{1,0:T(8,128)(2,1)S(1)}, u32[]{:S(2)}, u32[]{:S(2)}) collective-permute-start(bf16[576,256]{1,0:T(8,128)(2,1)S(1)} %bitcast.7), channel_id=1, source_target_pairs={{0,4},{1,5},{2,6},{3,7},{4,0},{5,1},{6,2},{7,3},{8,12},{9,13},{10,... | collective-permute-start | bytes 884744 | tf_op jit(solution)/shard_map/ppermute | solution.py:57
  12.0 1.5 %collective-permute-start.2 = (bf16[576,256]{1,0:T(8,128)(2,1)S(1)}, bf16[576,256]{1,0:T(8,128)(2,1)S(1)}, u32[]{:S(2)}, u32[]{:S(2)}) collective-permute-start(bf16[576,256]{1,0:T(8,128)(2,1)S(1)} %bitcast.8), channel_id=1, source_target_pairs={{0,1},{1,0},{2,3},{3,2},{4,5},{5,4},{6,7},{7,6},{8,9},{9,8},{10,11... | collective-permute-start | bytes 884744 | tf_op jit(solution)/shard_map/ppermute | solution.py:57
  13.4 13.0 %all-to-all-done.x_ref = bf16[8,144,128]{2,1,0:T(8,128)(2,1)S(1)} async-done(((bf16[8,144,128]{2,1,0:T(8,128)(2,1)}), bf16[8,144,128]{2,1,0:T(8,128)(2,1)S(1)}, u32[]{:S(2)}, u32[]{:S(2)}) %all-to-all-start) | async-done | bytes 294944 | tf_op jit(solution)/shard_map/all_to_all | solution.py:46
  27.7 3.7 %collective-permute-done.3.refs_4_ = bf16[576,256]{1,0:T(8,128)(2,1)S(1)} collective-permute-done((bf16[576,256]{1,0:T(8,128)(2,1)S(1)}, bf16[576,256]{1,0:T(8,128)(2,1)S(1)}, u32[]{:S(2)}, u32[]{:S(2)}) %collective-permute-start.3) | collective-permute-done | bytes 294944 | tf_op jit(solution)/shard_map/ppermute | solution.py:57
  31.3 1.4 %collective-permute-start.5 = (bf16[576,256]{1,0:T(8,128)(2,1)S(1)}, bf16[576,256]{1,0:T(8,128)(2,1)S(1)}, u32[]{:S(2)}, u32[]{:S(2)}) collective-permute-start(bf16[576,256]{1,0:T(8,128)(2,1)S(1)} %collective-permute-done.3.refs_4_), channel_id=1, source_target_pairs={{0,1},{1,0},{2,3},{3,2},{4,5},{5,4},{6,7},{7,6},{8,9},{9,8},{10,11... | collective-permute-start | bytes 884744 | tf_op jit(solution)/shard_map/ppermute | solution.py:57
  32.8 1.6 %collective-permute-start.1 = (bf16[256,128]{1,0:T(8,128)(2,1)S(1)}, bf16[256,128]{1,0:T(8,128)(2,1)S(1)}, u32[]{:S(2)}, u32[]{:S(2)}) collective-permute-start(bf16[256,128]{1,0:T(8,128)(2,1)S(1)} %pair_sum.1), channel_id=1, source_target_pairs={{0,16},{8,24},{16,0},{24,8},{1,17},{9,25},{17,1},{25,9},{2,18},{10... | collective-permute-start | bytes 196616 | tf_op jit(solution)/shard_map/ppermute | solution.py:57
  34.4 2.7 %collective-permute-done.1.z2_ref = bf16[256,128]{1,0:T(8,128)(2,1)S(1)} collective-permute-done((bf16[256,128]{1,0:T(8,128)(2,1)S(1)}, bf16[256,128]{1,0:T(8,128)(2,1)S(1)}, u32[]{:S(2)}, u32[]{:S(2)}) %collective-permute-start.1) | collective-permute-done | bytes 65568 | tf_op jit(solution)/shard_map/ppermute | solution.py:57
  37.7 3.3 %all-to-all-start.1 = ((bf16[8,32,128]{2,1,0:T(8,128)(2,1)}), bf16[8,32,128]{2,1,0:T(8,128)(2,1)S(1)}, u32[]{:S(2)}, u32[]{:S(2)}) async-start(bf16[8,32,128]{2,1,0:T(8,128)(2,1)} %share_sum.1), calls=%async_computation.1 | async-start | bytes 131072 | tf_op jit(solution)/shard_map/all_to_all | solution.py:46
  42.0 6.0 %all-to-all-done.1.share_ref = bf16[8,32,128]{2,1,0:T(8,128)(2,1)S(1)} async-done(((bf16[8,32,128]{2,1,0:T(8,128)(2,1)}), bf16[8,32,128]{2,1,0:T(8,128)(2,1)S(1)}, u32[]{:S(2)}, u32[]{:S(2)}) %all-to-all-start.1) | async-done | bytes 65568 | tf_op jit(solution)/shard_map/all_to_all | solution.py:46
  48.1 1.5 %collective-permute-start.7 = (bf16[9,32,128]{2,1,0:T(8,128)(2,1)S(1)}, bf16[9,32,128]{2,1,0:T(8,128)(2,1)S(1)}, u32[]{:S(2)}, u32[]{:S(2)}) collective-permute-start(bf16[9,32,128]{2,1,0:T(8,128)(2,1)S(1)} %pack_shares.1.refs_0_), channel_id=1, source_target_pairs={{0,16},{8,24},{16,0},{24,8},{1,17},{9,25},{17,1},{25,9},{2,18},{10... | collective-permute-start | bytes 221192 | tf_op jit(solution)/shard_map/ppermute | solution.py:57
  49.6 2.8 %collective-permute-done.7.refs_2_ = bf16[9,32,128]{2,1,0:T(8,128)(2,1)S(1)} collective-permute-done((bf16[9,32,128]{2,1,0:T(8,128)(2,1)S(1)}, bf16[9,32,128]{2,1,0:T(8,128)(2,1)S(1)}, u32[]{:S(2)}, u32[]{:S(2)}) %collective-permute-start.7) | collective-permute-done | bytes 73760 | tf_op jit(solution)/shard_map/ppermute | solution.py:57
  52.8 0.8 collective-permute-start.13
  55.1 3.5 %attention.1 = (bf16[17,16,128]{2,1,0:T(8,128)(2,1)S(1)}, bf16[17,16,128]{2,1,0:T(8,128)(2,1)S(1)}) custom-call(bf16[9,32,128]{2,1,0:T(8,128)(2,1)S(1)} %pack_shares.1.refs_0_, bf16[9,32,128]{2,1,0:T(8,128)(2,1)S(1)} %collective-permute-done.6.refs_1_, bf16[9,32,128]{2,1,0:T(8,128)(2,1)S(1)} %collective-permute-done.7.refs_2_, ...), custom_call_target="tpu_custom_call" | custom-call | tf_op jit(solution)/shard_map/attention/pallas_call | solution.py:34
  59.6 1.6 %collective-permute-start.14 = (bf16[576,256]{1,0:T(8,128)(2,1)S(1)}, bf16[576,256]{1,0:T(8,128)(2,1)S(1)}, u32[]{:S(2)}, u32[]{:S(2)}) collective-permute-start(bf16[576,256]{1,0:T(8,128)(2,1)S(1)} %collective-permute-done.13.refs_6_), channel_id=1, source_target_pairs={{0,1},{1,0},{2,3},{3,2},{4,5},{5,4},{6,7},{7,6},{8,9},{9,8},{10,11... | collective-permute-start | bytes 884744 | tf_op jit(solution)/shard_map/ppermute | solution.py:57
  61.2 1.3 %collective-permute-done.9.pair_ref = bf16[17,16,128]{2,1,0:T(8,128)(2,1)S(1)} collective-permute-done((bf16[17,16,128]{2,1,0:T(8,128)(2,1)S(1)}, bf16[17,16,128]{2,1,0:T(8,128)(2,1)S(1)}, u32[]{:S(2)}, u32[]{:S(2)}) %collective-permute-start.9) | collective-permute-done | bytes 69664 | tf_op jit(solution)/shard_map/ppermute | solution.py:57
  62.6 1.5 %collective-permute-start.10 = (bf16[17,16,128]{2,1,0:T(8,128)(2,1)S(1)}, bf16[17,16,128]{2,1,0:T(8,128)(2,1)S(1)}, u32[]{:S(2)}, u32[]{:S(2)}) collective-permute-start(bf16[17,16,128]{2,1,0:T(8,128)(2,1)S(1)} %pair_terms.1.own_ref), channel_id=1, source_target_pairs={{0,16},{8,24},{16,0},{24,8},{1,17},{9,25},{17,1},{25,9},{2,18},{10... | collective-permute-start | bytes 208904 | tf_op jit(solution)/shard_map/ppermute | solution.py:57
  64.1 2.8 %collective-permute-done.10.across_ref = bf16[17,16,128]{2,1,0:T(8,128)(2,1)S(1)} collective-permute-done((bf16[17,16,128]{2,1,0:T(8,128)(2,1)S(1)}, bf16[17,16,128]{2,1,0:T(8,128)(2,1)S(1)}, u32[]{:S(2)}, u32[]{:S(2)}) %collective-permute-start.10) | collective-permute-done | bytes 69664 | tf_op jit(solution)/shard_map/ppermute | solution.py:57
  67.2 1.2 collective-permute-done.11.other_ref
  69.3 1.3 %collective-permute-start.17 = (f32[32,128]{1,0:T(8,128)S(1)}, f32[32,128]{1,0:T(8,128)S(1)}, u32[]{:S(2)}, u32[]{:S(2)}) collective-permute-start(f32[32,128]{1,0:T(8,128)S(1)} %get-tuple-element.60.refs_0_), channel_id=1, source_target_pairs={{0,24},{8,16},{16,8},{24,0},{1,25},{9,17},{17,9},{25,1},{2,26},{10... | collective-permute-start | bytes 49160 | tf_op jit(solution)/shard_map/ppermute | solution.py:57
  71.2 1.3 %collective-permute-done.17.refs_3_ = f32[32,128]{1,0:T(8,128)S(1)} collective-permute-done((f32[32,128]{1,0:T(8,128)S(1)}, f32[32,128]{1,0:T(8,128)S(1)}, u32[]{:S(2)}, u32[]{:S(2)}) %collective-permute-start.17) | collective-permute-done | bytes 16416 | tf_op jit(solution)/shard_map/ppermute | solution.py:57
  72.5 1.9 %collective-permute-done.16.refs_2_ = f32[32,128]{1,0:T(8,128)S(1)} collective-permute-done((f32[32,128]{1,0:T(8,128)S(1)}, f32[32,128]{1,0:T(8,128)S(1)}, u32[]{:S(2)}, u32[]{:S(2)}) %collective-permute-start.16) | collective-permute-done | bytes 16416 | tf_op jit(solution)/shard_map/ppermute | solution.py:57
  74.7 13.0 %all_to_all.20.ff_ref = bf16[8,144,128]{2,1,0:T(8,128)(2,1)S(1)} all-to-all(bf16[8,144,128]{2,1,0:T(8,128)(2,1)S(1)} %get-tuple-element.62), channel_id=1, replica_groups=mesh['gx'=4,'gy'=8] {'gy'}, dimensions={0} | all-to-all | bytes 589824 | tf_op jit(solution)/shard_map/all_to_all | solution.py:46
  87.6 1.2 gate_up.1
  88.9 2.0 %collective-permute-done.18.from_pair_ref.z13_ref = bf16[2,64,2304]{2,1,0:T(8,128)(2,1)S(1)} collective-permute-done((bf16[2,64,2304]{2,1,0:T(8,128)(2,1)S(1)}, bf16[2,64,2304]{2,1,0:T(8,128)(2,1)S(1)}, u32[]{:S(2)}, u32[]{:S(2)}) %collective-permute-start.18) | collective-permute-done | bytes 589856 | tf_op jit(solution)/shard_map/ppermute | solution.py:57
  91.2 8.9 %collective-permute-done.19.z2_ref = bf16[64,2304]{1,0:T(8,128)(2,1)S(1)} collective-permute-done((bf16[64,2304]{1,0:T(8,128)(2,1)S(1)}, bf16[64,2304]{1,0:T(8,128)(2,1)S(1)}, u32[]{:S(2)}, u32[]{:S(2)}) %collective-permute-start.19) | collective-permute-done | bytes 294944 | tf_op jit(solution)/shard_map/ppermute | solution.py:57
  100.6 4.9 %collective-permute-done.21.refs_2_ = bf16[64,1152]{1,0:T(8,128)(2,1)S(1)} collective-permute-done((bf16[64,1152]{1,0:T(8,128)(2,1)S(1)}, bf16[64,1152]{1,0:T(8,128)(2,1)S(1)}, u32[]{:S(2)}, u32[]{:S(2)}) %collective-permute-start.21) | collective-permute-done | bytes 147488 | tf_op jit(solution)/shard_map/ppermute | solution.py:57
  105.5 1.4 %collective-permute-done.22.refs_3_ = bf16[64,1152]{1,0:T(8,128)(2,1)S(1)} collective-permute-done((bf16[64,1152]{1,0:T(8,128)(2,1)S(1)}, bf16[64,1152]{1,0:T(8,128)(2,1)S(1)}, u32[]{:S(2)}, u32[]{:S(2)}) %collective-permute-start.22) | collective-permute-done | bytes 147488 | tf_op jit(solution)/shard_map/ppermute | solution.py:57
  107.6 13.3 %all_to_all.21.parts_ref = bf16[8,144,128]{2,1,0:T(8,128)(2,1)S(1)} all-to-all(bf16[8,144,128]{2,1,0:T(8,128)(2,1)S(1)} %project_down.1), channel_id=1, replica_groups=mesh['gx'=4,'gy'=8] {'gy'}, dimensions={0} | all-to-all | bytes 589824 | tf_op jit(solution)/shard_map/all_to_all | solution.py:46
  121.5 1.4 %collective-permute-start.23 = (f32[32,128]{1,0:T(8,128)S(1)}, f32[32,128]{1,0:T(8,128)S(1)}, u32[]{:S(2)}, u32[]{:S(2)}) collective-permute-start(f32[32,128]{1,0:T(8,128)S(1)} %get-tuple-element.66.refs_0_), channel_id=1, source_target_pairs={{0,8},{8,0},{16,24},{24,16},{1,9},{9,1},{17,25},{25,17},{2,10},{10... | collective-permute-start | bytes 49160 | tf_op jit(solution)/shard_map/ppermute | solution.py:57
  123.0 1.3 %collective-permute-done.25.refs_3_ = f32[32,128]{1,0:T(8,128)S(1)} collective-permute-done((f32[32,128]{1,0:T(8,128)S(1)}, f32[32,128]{1,0:T(8,128)S(1)}, u32[]{:S(2)}, u32[]{:S(2)}) %collective-permute-start.25) | collective-permute-done | bytes 16416 | tf_op jit(solution)/shard_map/ppermute | solution.py:57
  (73 shorter events, 11.6 us)
Async XLA Ops:
  0.0 26.4 %copy-start.6 = (bf16[576,128]{1,0:T(8,128)(2,1)S(1)}, bf16[576,128]{1,0:T(8,128)(2,1)}, u32[]{:S(2)}) copy-start(bf16[576,128]{1,0:T(8,128)(2,1)} %k_ref.1) | copy-start | bytes 442372
  0.0 26.4 %copy-start.3 = (bf16[576,256]{1,0:T(8,128)(2,1)S(1)}, bf16[576,256]{1,0:T(8,128)(2,1)}, u32[]{:S(2)}) copy-start(bf16[576,256]{1,0:T(8,128)(2,1)} %q_ref.1) | copy-start | bytes 884740
  1.7 39.6 %copy-start.8 = (s32[3,8]{1,0:T(4,128)S(1)}, s32[3,8]{1,0:T(4,128)}, u32[]{:S(2)}) copy-start(s32[3,8]{1,0:T(4,128)} %parents_ref) | copy-start | bytes 292
  1.7 39.6 %copy-start.9 = (s32[1,33]{1,0:T(1,128)S(1)}, s32[1,33]{1,0:T(1,128)}, u32[]{:S(2)}) copy-start(s32[1,33]{1,0:T(1,128)} %table_ref) | copy-start | bytes 400
  1.7 24.8 %all-to-all-start = ((bf16[8,144,128]{2,1,0:T(8,128)(2,1)}), bf16[8,144,128]{2,1,0:T(8,128)(2,1)S(1)}, u32[]{:S(2)}, u32[]{:S(2)}) async-start(bf16[8,144,128]{2,1,0:T(8,128)(2,1)} %get-tuple-element.37), calls=%async_computation | async-start | bytes 589824 | tf_op jit(solution)/shard_map/all_to_all | solution.py:46
  9.1 22.3 %collective-permute-start.3 = (bf16[576,256]{1,0:T(8,128)(2,1)S(1)}, bf16[576,256]{1,0:T(8,128)(2,1)S(1)}, u32[]{:S(2)}, u32[]{:S(2)}) collective-permute-start(bf16[576,256]{1,0:T(8,128)(2,1)S(1)} %bitcast.7), channel_id=1, source_target_pairs={{0,4},{1,5},{2,6},{3,7},{4,0},{5,1},{6,2},{7,3},{8,12},{9,13},{10,... | collective-permute-start | bytes 884744 | tf_op jit(solution)/shard_map/ppermute | solution.py:57
  12.0 19.3 %collective-permute-start.2 = (bf16[576,256]{1,0:T(8,128)(2,1)S(1)}, bf16[576,256]{1,0:T(8,128)(2,1)S(1)}, u32[]{:S(2)}, u32[]{:S(2)}) collective-permute-start(bf16[576,256]{1,0:T(8,128)(2,1)S(1)} %bitcast.8), channel_id=1, source_target_pairs={{0,1},{1,0},{2,3},{3,2},{4,5},{5,4},{6,7},{7,6},{8,9},{9,8},{10,11... | collective-permute-start | bytes 884744 | tf_op jit(solution)/shard_map/ppermute | solution.py:57
  26.9 5.8 %collective-permute-start = (bf16[2,256,128]{2,1,0:T(8,128)(2,1)S(1)}, bf16[2,256,128]{2,1,0:T(8,128)(2,1)S(1)}, u32[]{:S(2)}, u32[]{:S(2)}) collective-permute-start(bf16[2,256,128]{2,1,0:T(8,128)(2,1)S(1)} %get-tuple-element.39), channel_id=1, source_target_pairs={{0,8},{8,0},{16,24},{24,16},{1,9},{9,1},{17,25},{25,17},{2,10},{10... | collective-permute-start | bytes 393224 | tf_op jit(solution)/shard_map/ppermute | solution.py:57
  31.3 10.7 %collective-permute-start.4 = (bf16[576,256]{1,0:T(8,128)(2,1)S(1)}, bf16[576,256]{1,0:T(8,128)(2,1)S(1)}, u32[]{:S(2)}, u32[]{:S(2)}) collective-permute-start(bf16[576,256]{1,0:T(8,128)(2,1)S(1)} %bitcast.9), channel_id=1, source_target_pairs={{0,2},{1,3},{2,0},{3,1},{4,6},{5,7},{6,4},{7,5},{8,10},{9,11},{10,... | collective-permute-start | bytes 884744 | tf_op jit(solution)/shard_map/ppermute | solution.py:57
  31.3 10.7 %collective-permute-start.5 = (bf16[576,256]{1,0:T(8,128)(2,1)S(1)}, bf16[576,256]{1,0:T(8,128)(2,1)S(1)}, u32[]{:S(2)}, u32[]{:S(2)}) collective-permute-start(bf16[576,256]{1,0:T(8,128)(2,1)S(1)} %collective-permute-done.3.refs_4_), channel_id=1, source_target_pairs={{0,1},{1,0},{2,3},{3,2},{4,5},{5,4},{6,7},{7,6},{8,9},{9,8},{10,11... | collective-permute-start | bytes 884744 | tf_op jit(solution)/shard_map/ppermute | solution.py:57
  32.8 4.3 %collective-permute-start.1 = (bf16[256,128]{1,0:T(8,128)(2,1)S(1)}, bf16[256,128]{1,0:T(8,128)(2,1)S(1)}, u32[]{:S(2)}, u32[]{:S(2)}) collective-permute-start(bf16[256,128]{1,0:T(8,128)(2,1)S(1)} %pair_sum.1), channel_id=1, source_target_pairs={{0,16},{8,24},{16,0},{24,8},{1,17},{9,25},{17,1},{25,9},{2,18},{10... | collective-permute-start | bytes 196616 | tf_op jit(solution)/shard_map/ppermute | solution.py:57
  37.7 10.3 %all-to-all-start.1 = ((bf16[8,32,128]{2,1,0:T(8,128)(2,1)}), bf16[8,32,128]{2,1,0:T(8,128)(2,1)S(1)}, u32[]{:S(2)}, u32[]{:S(2)}) async-start(bf16[8,32,128]{2,1,0:T(8,128)(2,1)} %share_sum.1), calls=%async_computation.1 | async-start | bytes 131072 | tf_op jit(solution)/shard_map/all_to_all | solution.py:46
  48.1 4.4 %collective-permute-start.7 = (bf16[9,32,128]{2,1,0:T(8,128)(2,1)S(1)}, bf16[9,32,128]{2,1,0:T(8,128)(2,1)S(1)}, u32[]{:S(2)}, u32[]{:S(2)}) collective-permute-start(bf16[9,32,128]{2,1,0:T(8,128)(2,1)S(1)} %pack_shares.1.refs_0_), channel_id=1, source_target_pairs={{0,16},{8,24},{16,0},{24,8},{1,17},{9,25},{17,1},{25,9},{2,18},{10... | collective-permute-start | bytes 221192 | tf_op jit(solution)/shard_map/ppermute | solution.py:57
  52.4 6.7 %collective-permute-start.12 = (bf16[576,256]{1,0:T(8,128)(2,1)S(1)}, bf16[576,256]{1,0:T(8,128)(2,1)S(1)}, u32[]{:S(2)}, u32[]{:S(2)}) collective-permute-start(bf16[576,256]{1,0:T(8,128)(2,1)S(1)} %collective-permute-done.4.refs_2_), channel_id=1, source_target_pairs={{0,1},{1,0},{2,3},{3,2},{4,5},{5,4},{6,7},{7,6},{8,9},{9,8},{10,11... | collective-permute-start | bytes 884744 | tf_op jit(solution)/shard_map/ppermute | solution.py:57
  52.8 6.7 %collective-permute-start.13 = (bf16[576,256]{1,0:T(8,128)(2,1)S(1)}, bf16[576,256]{1,0:T(8,128)(2,1)S(1)}, u32[]{:S(2)}, u32[]{:S(2)}) collective-permute-start(bf16[576,256]{1,0:T(8,128)(2,1)S(1)} %collective-permute-done.3.refs_4_), channel_id=1, source_target_pairs={{0,2},{1,3},{2,0},{3,1},{4,6},{5,7},{6,4},{7,5},{8,10},{9,11},{10,... | collective-permute-start | bytes 884744 | tf_op jit(solution)/shard_map/ppermute | solution.py:57
  53.7 1.3 %collective-permute-start.6 = (bf16[9,32,128]{2,1,0:T(8,128)(2,1)S(1)}, bf16[9,32,128]{2,1,0:T(8,128)(2,1)S(1)}, u32[]{:S(2)}, u32[]{:S(2)}) collective-permute-start(bf16[9,32,128]{2,1,0:T(8,128)(2,1)S(1)} %pack_shares.1.refs_0_), channel_id=1, source_target_pairs={{0,8},{8,0},{16,24},{24,16},{1,9},{9,1},{17,25},{25,17},{2,10},{10... | collective-permute-start | bytes 221192 | tf_op jit(solution)/shard_map/ppermute | solution.py:57
  53.7 1.4 %collective-permute-start.8 = (bf16[9,32,128]{2,1,0:T(8,128)(2,1)S(1)}, bf16[9,32,128]{2,1,0:T(8,128)(2,1)S(1)}, u32[]{:S(2)}, u32[]{:S(2)}) collective-permute-start(bf16[9,32,128]{2,1,0:T(8,128)(2,1)S(1)} %collective-permute-done.7.refs_2_), channel_id=1, source_target_pairs={{0,8},{8,0},{16,24},{24,16},{1,9},{9,1},{17,25},{25,17},{2,10},{10... | collective-permute-start | bytes 221192 | tf_op jit(solution)/shard_map/ppermute | solution.py:57
  59.6 8.9 %collective-permute-start.14 = (bf16[576,256]{1,0:T(8,128)(2,1)S(1)}, bf16[576,256]{1,0:T(8,128)(2,1)S(1)}, u32[]{:S(2)}, u32[]{:S(2)}) collective-permute-start(bf16[576,256]{1,0:T(8,128)(2,1)S(1)} %collective-permute-done.13.refs_6_), channel_id=1, source_target_pairs={{0,1},{1,0},{2,3},{3,2},{4,5},{5,4},{6,7},{7,6},{8,9},{9,8},{10,11... | collective-permute-start | bytes 884744 | tf_op jit(solution)/shard_map/ppermute | solution.py:57
  61.2 1.3 %collective-permute-start.9 = (bf16[17,16,128]{2,1,0:T(8,128)(2,1)S(1)}, bf16[17,16,128]{2,1,0:T(8,128)(2,1)S(1)}, u32[]{:S(2)}, u32[]{:S(2)}) collective-permute-start(bf16[17,16,128]{2,1,0:T(8,128)(2,1)S(1)} %get-tuple-element.56), channel_id=1, source_target_pairs={{0,8},{8,0},{16,24},{24,16},{1,9},{9,1},{17,25},{25,17},{2,10},{10... | collective-permute-start | bytes 208904 | tf_op jit(solution)/shard_map/ppermute | solution.py:57
  62.6 4.3 %collective-permute-start.10 = (bf16[17,16,128]{2,1,0:T(8,128)(2,1)S(1)}, bf16[17,16,128]{2,1,0:T(8,128)(2,1)S(1)}, u32[]{:S(2)}, u32[]{:S(2)}) collective-permute-start(bf16[17,16,128]{2,1,0:T(8,128)(2,1)S(1)} %pair_terms.1.own_ref), channel_id=1, source_target_pairs={{0,16},{8,24},{16,0},{24,8},{1,17},{9,25},{17,1},{25,9},{2,18},{10... | collective-permute-start | bytes 208904 | tf_op jit(solution)/shard_map/ppermute | solution.py:57
  67.1 1.3 %collective-permute-start.11 = (bf16[16,16,128]{2,1,0:T(8,128)(2,1)S(1)}, bf16[16,16,128]{2,1,0:T(8,128)(2,1)S(1)}, u32[]{:S(2)}, u32[]{:S(2)}) collective-permute-start(bf16[16,16,128]{2,1,0:T(8,128)(2,1)S(1)} %divide.1.own_ref), channel_id=1, source_target_pairs={{0,8},{8,0},{16,24},{24,16},{1,9},{9,1},{17,25},{25,17},{2,10},{10... | collective-permute-start | bytes 196616 | tf_op jit(solution)/shard_map/ppermute | solution.py:57
  69.3 3.2 %collective-permute-start.17 = (f32[32,128]{1,0:T(8,128)S(1)}, f32[32,128]{1,0:T(8,128)S(1)}, u32[]{:S(2)}, u32[]{:S(2)}) collective-permute-start(f32[32,128]{1,0:T(8,128)S(1)} %get-tuple-element.60.refs_0_), channel_id=1, source_target_pairs={{0,24},{8,16},{16,8},{24,0},{1,25},{9,17},{17,9},{25,1},{2,26},{10... | collective-permute-start | bytes 49160 | tf_op jit(solution)/shard_map/ppermute | solution.py:57
  70.6 3.7 %collective-permute-start.16 = (f32[32,128]{1,0:T(8,128)S(1)}, f32[32,128]{1,0:T(8,128)S(1)}, u32[]{:S(2)}, u32[]{:S(2)}) collective-permute-start(f32[32,128]{1,0:T(8,128)S(1)} %get-tuple-element.60.refs_0_), channel_id=1, source_target_pairs={{0,16},{8,24},{16,0},{24,8},{1,17},{9,25},{17,1},{25,9},{2,18},{10... | collective-permute-start | bytes 49160 | tf_op jit(solution)/shard_map/ppermute | solution.py:57
  71.1 3.2 %collective-permute-start.15 = (f32[32,128]{1,0:T(8,128)S(1)}, f32[32,128]{1,0:T(8,128)S(1)}, u32[]{:S(2)}, u32[]{:S(2)}) collective-permute-start(f32[32,128]{1,0:T(8,128)S(1)} %get-tuple-element.60.refs_0_), channel_id=1, source_target_pairs={{0,8},{8,0},{16,24},{24,16},{1,9},{9,1},{17,25},{25,17},{2,10},{10... | collective-permute-start | bytes 49160 | tf_op jit(solution)/shard_map/ppermute | solution.py:57
  88.8 2.1 %collective-permute-start.18 = (bf16[2,64,2304]{2,1,0:T(8,128)(2,1)S(1)}, bf16[2,64,2304]{2,1,0:T(8,128)(2,1)S(1)}, u32[]{:S(2)}, u32[]{:S(2)}) collective-permute-start(bf16[2,64,2304]{2,1,0:T(8,128)(2,1)S(1)} %get-tuple-element.64), channel_id=1, source_target_pairs={{0,8},{8,0},{16,24},{24,16},{1,9},{9,1},{17,25},{25,17},{2,10},{10... | collective-permute-start | bytes 1769480 | tf_op jit(solution)/shard_map/ppermute | solution.py:57
  90.9 9.1 %collective-permute-start.19 = (bf16[64,2304]{1,0:T(8,128)(2,1)S(1)}, bf16[64,2304]{1,0:T(8,128)(2,1)S(1)}, u32[]{:S(2)}, u32[]{:S(2)}) collective-permute-start(bf16[64,2304]{1,0:T(8,128)(2,1)S(1)} %pair_sum_ff.1), channel_id=1, source_target_pairs={{0,16},{8,24},{16,0},{24,8},{1,17},{9,25},{17,1},{25,9},{2,18},{10... | collective-permute-start | bytes 884744 | tf_op jit(solution)/shard_map/ppermute | solution.py:57
  100.3 5.2 %collective-permute-start.21 = (bf16[64,1152]{1,0:T(8,128)(2,1)S(1)}, bf16[64,1152]{1,0:T(8,128)(2,1)S(1)}, u32[]{:S(2)}, u32[]{:S(2)}) collective-permute-start(bf16[64,1152]{1,0:T(8,128)(2,1)S(1)} %activate.1.refs_0_), channel_id=1, source_target_pairs={{0,16},{8,24},{16,0},{24,8},{1,17},{9,25},{17,1},{25,9},{2,18},{10... | collective-permute-start | bytes 442376 | tf_op jit(solution)/shard_map/ppermute | solution.py:57
  100.6 4.9 %collective-permute-start.20 = (bf16[64,1152]{1,0:T(8,128)(2,1)S(1)}, bf16[64,1152]{1,0:T(8,128)(2,1)S(1)}, u32[]{:S(2)}, u32[]{:S(2)}) collective-permute-start(bf16[64,1152]{1,0:T(8,128)(2,1)S(1)} %activate.1.refs_0_), channel_id=1, source_target_pairs={{0,8},{8,0},{16,24},{24,16},{1,9},{9,1},{17,25},{25,17},{2,10},{10... | collective-permute-start | bytes 442376 | tf_op jit(solution)/shard_map/ppermute | solution.py:57
  105.5 1.4 %collective-permute-start.22 = (bf16[64,1152]{1,0:T(8,128)(2,1)S(1)}, bf16[64,1152]{1,0:T(8,128)(2,1)S(1)}, u32[]{:S(2)}, u32[]{:S(2)}) collective-permute-start(bf16[64,1152]{1,0:T(8,128)(2,1)S(1)} %collective-permute-done.21.refs_2_), channel_id=1, source_target_pairs={{0,8},{8,0},{16,24},{24,16},{1,9},{9,1},{17,25},{25,17},{2,10},{10... | collective-permute-start | bytes 442376 | tf_op jit(solution)/shard_map/ppermute | solution.py:57
  121.1 3.2 %collective-permute-start.25 = (f32[32,128]{1,0:T(8,128)S(1)}, f32[32,128]{1,0:T(8,128)S(1)}, u32[]{:S(2)}, u32[]{:S(2)}) collective-permute-start(f32[32,128]{1,0:T(8,128)S(1)} %get-tuple-element.66.refs_0_), channel_id=1, source_target_pairs={{0,24},{8,16},{16,8},{24,0},{1,25},{9,17},{17,9},{25,1},{2,26},{10... | collective-permute-start | bytes 49160 | tf_op jit(solution)/shard_map/ppermute | solution.py:57
  121.1 3.8 %collective-permute-start.24 = (f32[32,128]{1,0:T(8,128)S(1)}, f32[32,128]{1,0:T(8,128)S(1)}, u32[]{:S(2)}, u32[]{:S(2)}) collective-permute-start(f32[32,128]{1,0:T(8,128)S(1)} %get-tuple-element.66.refs_0_), channel_id=1, source_target_pairs={{0,16},{8,24},{16,0},{24,8},{1,17},{9,25},{17,1},{25,9},{2,18},{10... | collective-permute-start | bytes 49160 | tf_op jit(solution)/shard_map/ppermute | solution.py:57
  121.5 3.3 %collective-permute-start.23 = (f32[32,128]{1,0:T(8,128)S(1)}, f32[32,128]{1,0:T(8,128)S(1)}, u32[]{:S(2)}, u32[]{:S(2)}) collective-permute-start(f32[32,128]{1,0:T(8,128)S(1)} %get-tuple-element.66.refs_0_), channel_id=1, source_target_pairs={{0,8},{8,0},{16,24},{24,16},{1,9},{9,1},{17,25},{25,17},{2,10},{10... | collective-permute-start | bytes 49160 | tf_op jit(solution)/shard_map/ppermute | solution.py:57
  (9 other events, 136.1 us)

commit v8 on v7

--- a/solution.py
+++ b/solution.py
@@ -239,13 +239,15 @@
     x_own, x_all = run(
         "spread", spread, [((rows, width), BF), ((ny, packed, 128), BF)], (inputs,), micros=12
     )
+    w_own = w_out.T
+    x_all, w_split = lax.optimization_barrier((x_all, w_own))
     x_all = exchange(x_all, "gy")
 
-    w_own = w_out.T
-    w_blocks = {0: w_own, 1: permute(w_own, "gy", 1), 4: permute(w_own, "gy", 4)}
-    w_late, _ = lax.optimization_barrier((w_blocks, x_all))
-    w_blocks[2] = permute(w_late[0], "gy", 2)
-    w_blocks[5] = permute(w_late[4], "gy", 1)
+    w_blocks = {0: w_own, 1: permute(w_own, "gy", 1), 2: permute(w_own, "gy", 2)}
+    w_first = permute(w_split[: width // 2], "gy", 4)
+    w_late, _ = lax.optimization_barrier(((w_blocks, w_split[width // 2 :]), x_all))
+    w_blocks[3] = permute(w_late[0][2], "gy", 1)
+    w_second = permute(w_late[1], "gy", 4)
 
     def project(x_ref, gain_ref, q_ref, k_ref, v_ref, z0_ref, z2_ref, z13_ref, held):
         gain = 1.0 + gain_ref[0:1]
@@ -289,7 +291,7 @@
     cos, sin = rope_tables(late[1], rows, steps)
     tables = make_tables(*late, cache_pool.shape[1], rows, steps)
     shares = exchange(shares, "gy")
-    beside = tables, cos, sin, w_blocks[2], w_blocks[5]
+    beside = tables, cos, sin, w_blocks[3], w_first, w_second
     shares, (tables, cos, sin, *_) = lax.optimization_barrier((shares, beside))
 
     def pack_shares(share_ref, x_ref, out_ref):
@@ -301,9 +303,10 @@
         "pack_shares", pack_shares, [((ny + 1, rows, HALF), BF)], (shares, x_own), micros=5
     )
     shares = gather_gx(shares)
-    w_late, _ = lax.optimization_barrier((w_blocks, shares[2]))
-    w_blocks[6] = permute(w_late[4], "gy", 2)
-    w_blocks[3] = permute(w_late[2], "gy", 1)
+    w_blocks[4] = jnp.concatenate([w_first, w_second], axis=0)
+    w_late, _ = lax.optimization_barrier((w_blocks[4], shares[2]))
+    w_blocks[6] = permute(w_late, "gy", 2)
+    w_blocks[5] = permute(w_late, "gy", 1)
 
     def attention(*refs):
         a_refs, tables, pool_ref, outs = refs[:nx], refs[nx : nx + 4], refs[nx + 4], refs[nx + 5 :]

time: 126 us -> 121 us (0.960)
  waiting for transfers between devices: 57.6 us -> 49.2 us
  starting transfers between devices: 29.1 us -> 31.9 us
    all_to_all x2, waiting for transfers between devices: 19 us -> 11.1 us  [exchange(): return lax.all_to_all(values, axes, split_axis=0, concat_axis=0, tiled=True)]
    ppermute x26 -> x27, starting transfers between devices: 18.4 us -> 20.9 us  [permute(): return lax.ppermute(values, axis, [(i, i ^ m) for i in range(count)])]
    ppermute x26 -> x27, waiting for transfers between devices: 38.7 us -> 38 us  [permute(): return lax.ppermute(values, axis, [(i, i ^ m) for i in range(count)])]
  transfers between devices with their start and end apart: 28 -> 29, of which waited for: 20 -> 21; matrix products, arithmetic and copies ran while one was open for 0% -> 0% of each run, Pallas kernels for 4% -> 5%
where the time goes in v8:
time: 121 us; the launch traced here: 120 us
  waiting for transfers between devices  49.2 us (41%)
  starting transfers between devices  31.9 us (26%)
  blocking collectives  26.6 us (22%)
  Pallas kernels  10.7 us (9%)
    ppermute x27, waiting for transfers between devices, permute(): return lax.ppermute(values, axis, [(i, i ^ m) for i in range(count)])  38 us
    all_to_all x2, blocking collectives, exchange(): return lax.all_to_all(values, axes, split_axis=0, concat_axis=0, tiled=True)  26.6 us
    ppermute x27, starting transfers between devices, permute(): return lax.ppermute(values, axis, [(i, i ^ m) for i in range(count)])  20.9 us
    all_to_all x2, waiting for transfers between devices, exchange(): return lax.all_to_all(values, axes, split_axis=0, concat_axis=0, tiled=True)  11.1 us
    all_to_all x2, starting transfers between devices, exchange(): return lax.all_to_all(values, axes, split_axis=0, concat_axis=0, tiled=True)  10.9 us
    pallas_call x17, Pallas kernels, run(): pl.pallas_call(kernel, out_shape=[jax.ShapeDtypeStruct(s, d) for s, d in...  10.7 us
  transfers between devices with their start and end apart: 29, of which 21 were waited for; matrix products, arithmetic and copies ran while one was open for 0% of the time, Pallas kernels for 5%

profile of v8, /device:TPU:0, one launch (start us, length us, event | category | flops | bytes accessed | tf_op | source)
XLA Modules:
  0.0 120.4 jit_solution(4236016913954278804)
XLA Ops:
  1.6 7.4 %all-to-all-start = ((bf16[8,144,128]{2,1,0:T(8,128)(2,1)}), bf16[8,144,128]{2,1,0:T(8,128)(2,1)S(1)}, u32[]{:S(2)}, u32[]{:S(2)}) async-start(bf16[8,144,128]{2,1,0:T(8,128)(2,1)} %get-tuple-element.39), calls=%async_computation | async-start | bytes 589824 | tf_op jit(solution)/shard_map/all_to_all | solution.py:46
  9.1 2.1 %collective-permute-start.3 = (bf16[576,256]{1,0:T(8,128)(2,1)S(1)}, bf16[576,256]{1,0:T(8,128)(2,1)S(1)}, u32[]{:S(2)}, u32[]{:S(2)}) collective-permute-start(bf16[576,256]{1,0:T(8,128)(2,1)S(1)} %bitcast.7), channel_id=1, source_target_pairs={{0,2},{1,3},{2,0},{3,1},{4,6},{5,7},{6,4},{7,5},{8,10},{9,11},{10,... | collective-permute-start | bytes 884744 | tf_op jit(solution)/shard_map/ppermute | solution.py:57
  11.1 1.5 %collective-permute-start.2 = (bf16[576,256]{1,0:T(8,128)(2,1)S(1)}, bf16[576,256]{1,0:T(8,128)(2,1)S(1)}, u32[]{:S(2)}, u32[]{:S(2)}) collective-permute-start(bf16[576,256]{1,0:T(8,128)(2,1)S(1)} %bitcast.8), channel_id=1, source_target_pairs={{0,1},{1,0},{2,3},{3,2},{4,5},{5,4},{6,7},{7,6},{8,9},{9,8},{10,11... | collective-permute-start | bytes 884744 | tf_op jit(solution)/shard_map/ppermute | solution.py:57
  12.6 2.4 %collective-permute-start.5 = (bf16[288,256]{1,0:T(8,128)(2,1)S(1)}, bf16[288,256]{1,0:T(8,128)(2,1)S(1)}, u32[]{:S(2)}, u32[]{:S(2)}) collective-permute-start(bf16[288,256]{1,0:T(8,128)(2,1)S(1)} %get-tuple-element.71), channel_id=1, source_target_pairs={{0,4},{1,5},{2,6},{3,7},{4,0},{5,1},{6,2},{7,3},{8,12},{9,13},{10,... | collective-permute-start | bytes 442376 | tf_op jit(solution)/shard_map/ppermute | solution.py:57
  15.0 5.0 %all-to-all-done.x_ref = bf16[8,144,128]{2,1,0:T(8,128)(2,1)S(1)} async-done(((bf16[8,144,128]{2,1,0:T(8,128)(2,1)}), bf16[8,144,128]{2,1,0:T(8,128)(2,1)S(1)}, u32[]{:S(2)}, u32[]{:S(2)}) %all-to-all-start) | async-done | bytes 294944 | tf_op jit(solution)/shard_map/all_to_all | solution.py:46
  21.3 4.3 %collective-permute-done.3.refs_2_ = bf16[576,256]{1,0:T(8,128)(2,1)S(1)} collective-permute-done((bf16[576,256]{1,0:T(8,128)(2,1)S(1)}, bf16[576,256]{1,0:T(8,128)(2,1)S(1)}, u32[]{:S(2)}, u32[]{:S(2)}) %collective-permute-start.3) | collective-permute-done | bytes 294944 | tf_op jit(solution)/shard_map/ppermute | solution.py:57
  26.3 1.5 %collective-permute-start.4 = (bf16[576,256]{1,0:T(8,128)(2,1)S(1)}, bf16[576,256]{1,0:T(8,128)(2,1)S(1)}, u32[]{:S(2)}, u32[]{:S(2)}) collective-permute-start(bf16[576,256]{1,0:T(8,128)(2,1)S(1)} %collective-permute-done.3.refs_2_), channel_id=1, source_target_pairs={{0,1},{1,0},{2,3},{3,2},{4,5},{5,4},{6,7},{7,6},{8,9},{9,8},{10,11... | collective-permute-start | bytes 884744 | tf_op jit(solution)/shard_map/ppermute | solution.py:57
  27.8 1.6 %collective-permute-start.1 = (bf16[256,128]{1,0:T(8,128)(2,1)S(1)}, bf16[256,128]{1,0:T(8,128)(2,1)S(1)}, u32[]{:S(2)}, u32[]{:S(2)}) collective-permute-start(bf16[256,128]{1,0:T(8,128)(2,1)S(1)} %pair_sum.1), channel_id=1, source_target_pairs={{0,16},{8,24},{16,0},{24,8},{1,17},{9,25},{17,1},{25,9},{2,18},{10... | collective-permute-start | bytes 196616 | tf_op jit(solution)/shard_map/ppermute | solution.py:57
  29.5 2.6 %collective-permute-done.1.z2_ref = bf16[256,128]{1,0:T(8,128)(2,1)S(1)} collective-permute-done((bf16[256,128]{1,0:T(8,128)(2,1)S(1)}, bf16[256,128]{1,0:T(8,128)(2,1)S(1)}, u32[]{:S(2)}, u32[]{:S(2)}) %collective-permute-start.1) | collective-permute-done | bytes 65568 | tf_op jit(solution)/shard_map/ppermute | solution.py:57
  32.7 3.5 %all-to-all-start.1 = ((bf16[8,32,128]{2,1,0:T(8,128)(2,1)}), bf16[8,32,128]{2,1,0:T(8,128)(2,1)S(1)}, u32[]{:S(2)}, u32[]{:S(2)}) async-start(bf16[8,32,128]{2,1,0:T(8,128)(2,1)} %share_sum.1), calls=%async_computation.1 | async-start | bytes 131072 | tf_op jit(solution)/shard_map/all_to_all | solution.py:46
  37.1 6.1 %all-to-all-done.1.share_ref = bf16[8,32,128]{2,1,0:T(8,128)(2,1)S(1)} async-done(((bf16[8,32,128]{2,1,0:T(8,128)(2,1)}), bf16[8,32,128]{2,1,0:T(8,128)(2,1)S(1)}, u32[]{:S(2)}, u32[]{:S(2)}) %all-to-all-start.1) | async-done | bytes 65568 | tf_op jit(solution)/shard_map/all_to_all | solution.py:46
  43.3 1.5 %collective-permute-start.8 = (bf16[9,32,128]{2,1,0:T(8,128)(2,1)S(1)}, bf16[9,32,128]{2,1,0:T(8,128)(2,1)S(1)}, u32[]{:S(2)}, u32[]{:S(2)}) collective-permute-start(bf16[9,32,128]{2,1,0:T(8,128)(2,1)S(1)} %pack_shares.1.refs_0_), channel_id=1, source_target_pairs={{0,16},{8,24},{16,0},{24,8},{1,17},{9,25},{17,1},{25,9},{2,18},{10... | collective-permute-start | bytes 221192 | tf_op jit(solution)/shard_map/ppermute | solution.py:57
  44.8 2.8 %collective-permute-done.8.refs_2_ = bf16[9,32,128]{2,1,0:T(8,128)(2,1)S(1)} collective-permute-done((bf16[9,32,128]{2,1,0:T(8,128)(2,1)S(1)}, bf16[9,32,128]{2,1,0:T(8,128)(2,1)S(1)}, u32[]{:S(2)}, u32[]{:S(2)}) %collective-permute-start.8) | collective-permute-done | bytes 73760 | tf_op jit(solution)/shard_map/ppermute | solution.py:57
  47.8 1.0 collective-permute-start.13
  50.3 3.5 %attention.1 = (bf16[17,16,128]{2,1,0:T(8,128)(2,1)S(1)}, bf16[17,16,128]{2,1,0:T(8,128)(2,1)S(1)}) custom-call(bf16[9,32,128]{2,1,0:T(8,128)(2,1)S(1)} %pack_shares.1.refs_0_, bf16[9,32,128]{2,1,0:T(8,128)(2,1)S(1)} %collective-permute-done.7.refs_1_, bf16[9,32,128]{2,1,0:T(8,128)(2,1)S(1)} %collective-permute-done.8.refs_2_, ...), custom_call_target="tpu_custom_call" | custom-call | tf_op jit(solution)/shard_map/attention/pallas_call | solution.py:34
  54.6 1.0 collective-permute-start.15
  55.6 1.3 %collective-permute-done.10.pair_ref = bf16[17,16,128]{2,1,0:T(8,128)(2,1)S(1)} collective-permute-done((bf16[17,16,128]{2,1,0:T(8,128)(2,1)S(1)}, bf16[17,16,128]{2,1,0:T(8,128)(2,1)S(1)}, u32[]{:S(2)}, u32[]{:S(2)}) %collective-permute-start.10) | collective-permute-done | bytes 69664 | tf_op jit(solution)/shard_map/ppermute | solution.py:57
  57.0 1.5 %collective-permute-start.11 = (bf16[17,16,128]{2,1,0:T(8,128)(2,1)S(1)}, bf16[17,16,128]{2,1,0:T(8,128)(2,1)S(1)}, u32[]{:S(2)}, u32[]{:S(2)}) collective-permute-start(bf16[17,16,128]{2,1,0:T(8,128)(2,1)S(1)} %pair_terms.1.own_ref), channel_id=1, source_target_pairs={{0,16},{8,24},{16,0},{24,8},{1,17},{9,25},{17,1},{25,9},{2,18},{10... | collective-permute-start | bytes 208904 | tf_op jit(solution)/shard_map/ppermute | solution.py:57
  58.5 2.8 %collective-permute-done.11.across_ref = bf16[17,16,128]{2,1,0:T(8,128)(2,1)S(1)} collective-permute-done((bf16[17,16,128]{2,1,0:T(8,128)(2,1)S(1)}, bf16[17,16,128]{2,1,0:T(8,128)(2,1)S(1)}, u32[]{:S(2)}, u32[]{:S(2)}) %collective-permute-start.11) | collective-permute-done | bytes 69664 | tf_op jit(solution)/shard_map/ppermute | solution.py:57
  61.6 1.2 %collective-permute-done.12.other_ref = bf16[16,16,128]{2,1,0:T(8,128)(2,1)S(1)} collective-permute-done((bf16[16,16,128]{2,1,0:T(8,128)(2,1)S(1)}, bf16[16,16,128]{2,1,0:T(8,128)(2,1)S(1)}, u32[]{:S(2)}, u32[]{:S(2)}) %collective-permute-start.12) | collective-permute-done | bytes 65568 | tf_op jit(solution)/shard_map/ppermute | solution.py:57
  63.9 1.1 collective-permute-start.18
  65.8 1.4 %collective-permute-done.18.refs_3_ = f32[32,128]{1,0:T(8,128)S(1)} collective-permute-done((f32[32,128]{1,0:T(8,128)S(1)}, f32[32,128]{1,0:T(8,128)S(1)}, u32[]{:S(2)}, u32[]{:S(2)}) %collective-permute-start.18) | collective-permute-done | bytes 16416 | tf_op jit(solution)/shard_map/ppermute | solution.py:57
  67.2 1.5 %collective-permute-done.17.refs_2_ = f32[32,128]{1,0:T(8,128)S(1)} collective-permute-done((f32[32,128]{1,0:T(8,128)S(1)}, f32[32,128]{1,0:T(8,128)S(1)}, u32[]{:S(2)}, u32[]{:S(2)}) %collective-permute-start.17) | collective-permute-done | bytes 16416 | tf_op jit(solution)/shard_map/ppermute | solution.py:57
  69.0 13.3 %all_to_all.20.ff_ref = bf16[8,144,128]{2,1,0:T(8,128)(2,1)S(1)} all-to-all(bf16[8,144,128]{2,1,0:T(8,128)(2,1)S(1)} %get-tuple-element.64), channel_id=1, replica_groups=mesh['gx'=4,'gy'=8] {'gy'}, dimensions={0} | all-to-all | bytes 589824 | tf_op jit(solution)/shard_map/all_to_all | solution.py:46
  82.4 1.2 gate_up.1
  83.6 2.0 %collective-permute-done.19.from_pair_ref.z13_ref = bf16[2,64,2304]{2,1,0:T(8,128)(2,1)S(1)} collective-permute-done((bf16[2,64,2304]{2,1,0:T(8,128)(2,1)S(1)}, bf16[2,64,2304]{2,1,0:T(8,128)(2,1)S(1)}, u32[]{:S(2)}, u32[]{:S(2)}) %collective-permute-start.19) | collective-permute-done | bytes 589856 | tf_op jit(solution)/shard_map/ppermute | solution.py:57
  86.4 8.4 %collective-permute-done.20.z2_ref = bf16[64,2304]{1,0:T(8,128)(2,1)S(1)} collective-permute-done((bf16[64,2304]{1,0:T(8,128)(2,1)S(1)}, bf16[64,2304]{1,0:T(8,128)(2,1)S(1)}, u32[]{:S(2)}, u32[]{:S(2)}) %collective-permute-start.20) | collective-permute-done | bytes 294944 | tf_op jit(solution)/shard_map/ppermute | solution.py:57
  95.8 4.5 %collective-permute-done.22.refs_2_ = bf16[64,1152]{1,0:T(8,128)(2,1)S(1)} collective-permute-done((bf16[64,1152]{1,0:T(8,128)(2,1)S(1)}, bf16[64,1152]{1,0:T(8,128)(2,1)S(1)}, u32[]{:S(2)}, u32[]{:S(2)}) %collective-permute-start.22) | collective-permute-done | bytes 147488 | tf_op jit(solution)/shard_map/ppermute | solution.py:57
  100.2 1.4 %collective-permute-done.23.refs_3_ = bf16[64,1152]{1,0:T(8,128)(2,1)S(1)} collective-permute-done((bf16[64,1152]{1,0:T(8,128)(2,1)S(1)}, bf16[64,1152]{1,0:T(8,128)(2,1)S(1)}, u32[]{:S(2)}, u32[]{:S(2)}) %collective-permute-start.23) | collective-permute-done | bytes 147488 | tf_op jit(solution)/shard_map/ppermute | solution.py:57
  102.4 13.3 %all_to_all.21.parts_ref = bf16[8,144,128]{2,1,0:T(8,128)(2,1)S(1)} all-to-all(bf16[8,144,128]{2,1,0:T(8,128)(2,1)S(1)} %project_down.1), channel_id=1, replica_groups=mesh['gx'=4,'gy'=8] {'gy'}, dimensions={0} | all-to-all | bytes 589824 | tf_op jit(solution)/shard_map/all_to_all | solution.py:46
  116.6 1.1 collective-permute-start.24
  117.7 1.3 %collective-permute-done.26.refs_3_ = f32[32,128]{1,0:T(8,128)S(1)} collective-permute-done((f32[32,128]{1,0:T(8,128)S(1)}, f32[32,128]{1,0:T(8,128)S(1)}, u32[]{:S(2)}, u32[]{:S(2)}) %collective-permute-start.26) | collective-permute-done | bytes 16416 | tf_op jit(solution)/shard_map/ppermute | solution.py:57
  (78 shorter events, 14.5 us)
Async XLA Ops:
  1.6 18.5 %all-to-all-start = ((bf16[8,144,128]{2,1,0:T(8,128)(2,1)}), bf16[8,144,128]{2,1,0:T(8,128)(2,1)S(1)}, u32[]{:S(2)}, u32[]{:S(2)}) async-start(bf16[8,144,128]{2,1,0:T(8,128)(2,1)} %get-tuple-element.39), calls=%async_computation | async-start | bytes 589824 | tf_op jit(solution)/shard_map/all_to_all | solution.py:46
  9.0 27.3 %copy-start.8 = (s32[3,8]{1,0:T(4,128)S(1)}, s32[3,8]{1,0:T(4,128)}, u32[]{:S(2)}) copy-start(s32[3,8]{1,0:T(4,128)} %parents_ref) | copy-start | bytes 292
  9.0 27.3 %copy-start.9 = (s32[1,33]{1,0:T(1,128)S(1)}, s32[1,33]{1,0:T(1,128)}, u32[]{:S(2)}) copy-start(s32[1,33]{1,0:T(1,128)} %table_ref) | copy-start | bytes 400
  9.1 16.5 %collective-permute-start.3 = (bf16[576,256]{1,0:T(8,128)(2,1)S(1)}, bf16[576,256]{1,0:T(8,128)(2,1)S(1)}, u32[]{:S(2)}, u32[]{:S(2)}) collective-permute-start(bf16[576,256]{1,0:T(8,128)(2,1)S(1)} %bitcast.7), channel_id=1, source_target_pairs={{0,2},{1,3},{2,0},{3,1},{4,6},{5,7},{6,4},{7,5},{8,10},{9,11},{10,... | collective-permute-start | bytes 884744 | tf_op jit(solution)/shard_map/ppermute | solution.py:57
  11.1 14.5 %collective-permute-start.2 = (bf16[576,256]{1,0:T(8,128)(2,1)S(1)}, bf16[576,256]{1,0:T(8,128)(2,1)S(1)}, u32[]{:S(2)}, u32[]{:S(2)}) collective-permute-start(bf16[576,256]{1,0:T(8,128)(2,1)S(1)} %bitcast.8), channel_id=1, source_target_pairs={{0,1},{1,0},{2,3},{3,2},{4,5},{5,4},{6,7},{7,6},{8,9},{9,8},{10,11... | collective-permute-start | bytes 884744 | tf_op jit(solution)/shard_map/ppermute | solution.py:57
  12.6 23.7 %collective-permute-start.5 = (bf16[288,256]{1,0:T(8,128)(2,1)S(1)}, bf16[288,256]{1,0:T(8,128)(2,1)S(1)}, u32[]{:S(2)}, u32[]{:S(2)}) collective-permute-start(bf16[288,256]{1,0:T(8,128)(2,1)S(1)} %get-tuple-element.71), channel_id=1, source_target_pairs={{0,4},{1,5},{2,6},{3,7},{4,0},{5,1},{6,2},{7,3},{8,12},{9,13},{10,... | collective-permute-start | bytes 442376 | tf_op jit(solution)/shard_map/ppermute | solution.py:57
  20.6 7.2 %collective-permute-start = (bf16[2,256,128]{2,1,0:T(8,128)(2,1)S(1)}, bf16[2,256,128]{2,1,0:T(8,128)(2,1)S(1)}, u32[]{:S(2)}, u32[]{:S(2)}) collective-permute-start(bf16[2,256,128]{2,1,0:T(8,128)(2,1)S(1)} %get-tuple-element.41), channel_id=1, source_target_pairs={{0,8},{8,0},{16,24},{24,16},{1,9},{9,1},{17,25},{25,17},{2,10},{10... | collective-permute-start | bytes 393224 | tf_op jit(solution)/shard_map/ppermute | solution.py:57
  25.6 11.5 %collective-permute-start.6 = (bf16[288,256]{1,0:T(8,128)(2,1)S(1)}, bf16[288,256]{1,0:T(8,128)(2,1)S(1)}, u32[]{:S(2)}, u32[]{:S(2)}) collective-permute-start(bf16[288,256]{1,0:T(8,128)(2,1)S(1)} %get-tuple-element.51), channel_id=1, source_target_pairs={{0,4},{1,5},{2,6},{3,7},{4,0},{5,1},{6,2},{7,3},{8,12},{9,13},{10,... | collective-permute-start | bytes 442376 | tf_op jit(solution)/shard_map/ppermute | solution.py:57
  26.3 10.8 %collective-permute-start.4 = (bf16[576,256]{1,0:T(8,128)(2,1)S(1)}, bf16[576,256]{1,0:T(8,128)(2,1)S(1)}, u32[]{:S(2)}, u32[]{:S(2)}) collective-permute-start(bf16[576,256]{1,0:T(8,128)(2,1)S(1)} %collective-permute-done.3.refs_2_), channel_id=1, source_target_pairs={{0,1},{1,0},{2,3},{3,2},{4,5},{5,4},{6,7},{7,6},{8,9},{9,8},{10,11... | collective-permute-start | bytes 884744 | tf_op jit(solution)/shard_map/ppermute | solution.py:57
  27.8 4.3 %collective-permute-start.1 = (bf16[256,128]{1,0:T(8,128)(2,1)S(1)}, bf16[256,128]{1,0:T(8,128)(2,1)S(1)}, u32[]{:S(2)}, u32[]{:S(2)}) collective-permute-start(bf16[256,128]{1,0:T(8,128)(2,1)S(1)} %pair_sum.1), channel_id=1, source_target_pairs={{0,16},{8,24},{16,0},{24,8},{1,17},{9,25},{17,1},{25,9},{2,18},{10... | collective-permute-start | bytes 196616 | tf_op jit(solution)/shard_map/ppermute | solution.py:57
  32.7 10.4 %all-to-all-start.1 = ((bf16[8,32,128]{2,1,0:T(8,128)(2,1)}), bf16[8,32,128]{2,1,0:T(8,128)(2,1)S(1)}, u32[]{:S(2)}, u32[]{:S(2)}) async-start(bf16[8,32,128]{2,1,0:T(8,128)(2,1)} %share_sum.1), calls=%async_computation.1 | async-start | bytes 131072 | tf_op jit(solution)/shard_map/all_to_all | solution.py:46
  43.3 4.4 %collective-permute-start.8 = (bf16[9,32,128]{2,1,0:T(8,128)(2,1)S(1)}, bf16[9,32,128]{2,1,0:T(8,128)(2,1)S(1)}, u32[]{:S(2)}, u32[]{:S(2)}) collective-permute-start(bf16[9,32,128]{2,1,0:T(8,128)(2,1)S(1)} %pack_shares.1.refs_0_), channel_id=1, source_target_pairs={{0,16},{8,24},{16,0},{24,8},{1,17},{9,25},{17,1},{25,9},{2,18},{10... | collective-permute-start | bytes 221192 | tf_op jit(solution)/shard_map/ppermute | solution.py:57
  47.6 6.7 %collective-permute-start.14 = (bf16[576,256]{1,0:T(8,128)(2,1)S(1)}, bf16[576,256]{1,0:T(8,128)(2,1)S(1)}, u32[]{:S(2)}, u32[]{:S(2)}) collective-permute-start(bf16[576,256]{1,0:T(8,128)(2,1)S(1)} %constant_dynamic-update-slice_fusion.refs_4_), channel_id=1, source_target_pairs={{0,2},{1,3},{2,0},{3,1},{4,6},{5,7},{6,4},{7,5},{8,10},{9,11},{10,... | collective-permute-start | bytes 884744 | tf_op jit(solution)/shard_map/ppermute | solution.py:57
  47.8 6.7 %collective-permute-start.13 = (bf16[576,256]{1,0:T(8,128)(2,1)S(1)}, bf16[576,256]{1,0:T(8,128)(2,1)S(1)}, u32[]{:S(2)}, u32[]{:S(2)}) collective-permute-start(bf16[576,256]{1,0:T(8,128)(2,1)S(1)} %constant_dynamic-update-slice_fusion.refs_4_), channel_id=1, source_target_pairs={{0,1},{1,0},{2,3},{3,2},{4,5},{5,4},{6,7},{7,6},{8,9},{9,8},{10,11... | collective-permute-start | bytes 884744 | tf_op jit(solution)/shard_map/ppermute | solution.py:57
  48.8 1.3 %collective-permute-start.7 = (bf16[9,32,128]{2,1,0:T(8,128)(2,1)S(1)}, bf16[9,32,128]{2,1,0:T(8,128)(2,1)S(1)}, u32[]{:S(2)}, u32[]{:S(2)}) collective-permute-start(bf16[9,32,128]{2,1,0:T(8,128)(2,1)S(1)} %pack_shares.1.refs_0_), channel_id=1, source_target_pairs={{0,8},{8,0},{16,24},{24,16},{1,9},{9,1},{17,25},{25,17},{2,10},{10... | collective-permute-start | bytes 221192 | tf_op jit(solution)/shard_map/ppermute | solution.py:57
  48.9 1.4 %collective-permute-start.9 = (bf16[9,32,128]{2,1,0:T(8,128)(2,1)S(1)}, bf16[9,32,128]{2,1,0:T(8,128)(2,1)S(1)}, u32[]{:S(2)}, u32[]{:S(2)}) collective-permute-start(bf16[9,32,128]{2,1,0:T(8,128)(2,1)S(1)} %collective-permute-done.8.refs_2_), channel_id=1, source_target_pairs={{0,8},{8,0},{16,24},{24,16},{1,9},{9,1},{17,25},{25,17},{2,10},{10... | collective-permute-start | bytes 221192 | tf_op jit(solution)/shard_map/ppermute | solution.py:57
  54.6 8.5 %collective-permute-start.15 = (bf16[576,256]{1,0:T(8,128)(2,1)S(1)}, bf16[576,256]{1,0:T(8,128)(2,1)S(1)}, u32[]{:S(2)}, u32[]{:S(2)}) collective-permute-start(bf16[576,256]{1,0:T(8,128)(2,1)S(1)} %collective-permute-done.14.refs_6_), channel_id=1, source_target_pairs={{0,1},{1,0},{2,3},{3,2},{4,5},{5,4},{6,7},{7,6},{8,9},{9,8},{10,11... | collective-permute-start | bytes 884744 | tf_op jit(solution)/shard_map/ppermute | solution.py:57
  55.6 1.3 %collective-permute-start.10 = (bf16[17,16,128]{2,1,0:T(8,128)(2,1)S(1)}, bf16[17,16,128]{2,1,0:T(8,128)(2,1)S(1)}, u32[]{:S(2)}, u32[]{:S(2)}) collective-permute-start(bf16[17,16,128]{2,1,0:T(8,128)(2,1)S(1)} %get-tuple-element.59), channel_id=1, source_target_pairs={{0,8},{8,0},{16,24},{24,16},{1,9},{9,1},{17,25},{25,17},{2,10},{10... | collective-permute-start | bytes 208904 | tf_op jit(solution)/shard_map/ppermute | solution.py:57
  57.0 4.3 %collective-permute-start.11 = (bf16[17,16,128]{2,1,0:T(8,128)(2,1)S(1)}, bf16[17,16,128]{2,1,0:T(8,128)(2,1)S(1)}, u32[]{:S(2)}, u32[]{:S(2)}) collective-permute-start(bf16[17,16,128]{2,1,0:T(8,128)(2,1)S(1)} %pair_terms.1.own_ref), channel_id=1, source_target_pairs={{0,16},{8,24},{16,0},{24,8},{1,17},{9,25},{17,1},{25,9},{2,18},{10... | collective-permute-start | bytes 208904 | tf_op jit(solution)/shard_map/ppermute | solution.py:57
  61.5 20.9 %copy-start.1 = (bf16[576,1152]{1,0:T(8,128)(2,1)S(1)}, bf16[576,1152]{1,0:T(8,128)(2,1)}, u32[]{:S(2)}) copy-start(bf16[576,1152]{1,0:T(8,128)(2,1)} %gate_ref.1) | copy-start | bytes 3981316
  61.5 1.3 %collective-permute-start.12 = (bf16[16,16,128]{2,1,0:T(8,128)(2,1)S(1)}, bf16[16,16,128]{2,1,0:T(8,128)(2,1)S(1)}, u32[]{:S(2)}, u32[]{:S(2)}) collective-permute-start(bf16[16,16,128]{2,1,0:T(8,128)(2,1)S(1)} %divide.1.own_ref), channel_id=1, source_target_pairs={{0,8},{8,0},{16,24},{24,16},{1,9},{9,1},{17,25},{25,17},{2,10},{10... | collective-permute-start | bytes 196616 | tf_op jit(solution)/shard_map/ppermute | solution.py:57
  63.9 3.3 %collective-permute-start.18 = (f32[32,128]{1,0:T(8,128)S(1)}, f32[32,128]{1,0:T(8,128)S(1)}, u32[]{:S(2)}, u32[]{:S(2)}) collective-permute-start(f32[32,128]{1,0:T(8,128)S(1)} %get-tuple-element.62.refs_0_), channel_id=1, source_target_pairs={{0,24},{8,16},{16,8},{24,0},{1,25},{9,17},{17,9},{25,1},{2,26},{10... | collective-permute-start | bytes 49160 | tf_op jit(solution)/shard_map/ppermute | solution.py:57
  65.0 3.7 %collective-permute-start.17 = (f32[32,128]{1,0:T(8,128)S(1)}, f32[32,128]{1,0:T(8,128)S(1)}, u32[]{:S(2)}, u32[]{:S(2)}) collective-permute-start(f32[32,128]{1,0:T(8,128)S(1)} %get-tuple-element.62.refs_0_), channel_id=1, source_target_pairs={{0,16},{8,24},{16,0},{24,8},{1,17},{9,25},{17,1},{25,9},{2,18},{10... | collective-permute-start | bytes 49160 | tf_op jit(solution)/shard_map/ppermute | solution.py:57
  65.6 3.2 %collective-permute-start.16 = (f32[32,128]{1,0:T(8,128)S(1)}, f32[32,128]{1,0:T(8,128)S(1)}, u32[]{:S(2)}, u32[]{:S(2)}) collective-permute-start(f32[32,128]{1,0:T(8,128)S(1)} %get-tuple-element.62.refs_0_), channel_id=1, source_target_pairs={{0,8},{8,0},{16,24},{24,16},{1,9},{9,1},{17,25},{25,17},{2,10},{10... | collective-permute-start | bytes 49160 | tf_op jit(solution)/shard_map/ppermute | solution.py:57
  83.6 2.1 %collective-permute-start.19 = (bf16[2,64,2304]{2,1,0:T(8,128)(2,1)S(1)}, bf16[2,64,2304]{2,1,0:T(8,128)(2,1)S(1)}, u32[]{:S(2)}, u32[]{:S(2)}) collective-permute-start(bf16[2,64,2304]{2,1,0:T(8,128)(2,1)S(1)} %get-tuple-element.66), channel_id=1, source_target_pairs={{0,8},{8,0},{16,24},{24,16},{1,9},{9,1},{17,25},{25,17},{2,10},{10... | collective-permute-start | bytes 1769480 | tf_op jit(solution)/shard_map/ppermute | solution.py:57
  85.7 9.1 %collective-permute-start.20 = (bf16[64,2304]{1,0:T(8,128)(2,1)S(1)}, bf16[64,2304]{1,0:T(8,128)(2,1)S(1)}, u32[]{:S(2)}, u32[]{:S(2)}) collective-permute-start(bf16[64,2304]{1,0:T(8,128)(2,1)S(1)} %pair_sum_ff.1), channel_id=1, source_target_pairs={{0,16},{8,24},{16,0},{24,8},{1,17},{9,25},{17,1},{25,9},{2,18},{10... | collective-permute-start | bytes 884744 | tf_op jit(solution)/shard_map/ppermute | solution.py:57
  95.0 5.2 %collective-permute-start.22 = (bf16[64,1152]{1,0:T(8,128)(2,1)S(1)}, bf16[64,1152]{1,0:T(8,128)(2,1)S(1)}, u32[]{:S(2)}, u32[]{:S(2)}) collective-permute-start(bf16[64,1152]{1,0:T(8,128)(2,1)S(1)} %activate.1.refs_0_), channel_id=1, source_target_pairs={{0,16},{8,24},{16,0},{24,8},{1,17},{9,25},{17,1},{25,9},{2,18},{10... | collective-permute-start | bytes 442376 | tf_op jit(solution)/shard_map/ppermute | solution.py:57
  95.8 4.5 %collective-permute-start.21 = (bf16[64,1152]{1,0:T(8,128)(2,1)S(1)}, bf16[64,1152]{1,0:T(8,128)(2,1)S(1)}, u32[]{:S(2)}, u32[]{:S(2)}) collective-permute-start(bf16[64,1152]{1,0:T(8,128)(2,1)S(1)} %activate.1.refs_0_), channel_id=1, source_target_pairs={{0,8},{8,0},{16,24},{24,16},{1,9},{9,1},{17,25},{25,17},{2,10},{10... | collective-permute-start | bytes 442376 | tf_op jit(solution)/shard_map/ppermute | solution.py:57
  100.2 1.4 %collective-permute-start.23 = (bf16[64,1152]{1,0:T(8,128)(2,1)S(1)}, bf16[64,1152]{1,0:T(8,128)(2,1)S(1)}, u32[]{:S(2)}, u32[]{:S(2)}) collective-permute-start(bf16[64,1152]{1,0:T(8,128)(2,1)S(1)} %collective-permute-done.22.refs_2_), channel_id=1, source_target_pairs={{0,8},{8,0},{16,24},{24,16},{1,9},{9,1},{17,25},{25,17},{2,10},{10... | collective-permute-start | bytes 442376 | tf_op jit(solution)/shard_map/ppermute | solution.py:57
  115.8 3.2 %collective-permute-start.26 = (f32[32,128]{1,0:T(8,128)S(1)}, f32[32,128]{1,0:T(8,128)S(1)}, u32[]{:S(2)}, u32[]{:S(2)}) collective-permute-start(f32[32,128]{1,0:T(8,128)S(1)} %get-tuple-element.68.refs_0_), channel_id=1, source_target_pairs={{0,24},{8,16},{16,8},{24,0},{1,25},{9,17},{17,9},{25,1},{2,26},{10... | collective-permute-start | bytes 49160 | tf_op jit(solution)/shard_map/ppermute | solution.py:57
  115.8 3.8 %collective-permute-start.25 = (f32[32,128]{1,0:T(8,128)S(1)}, f32[32,128]{1,0:T(8,128)S(1)}, u32[]{:S(2)}, u32[]{:S(2)}) collective-permute-start(f32[32,128]{1,0:T(8,128)S(1)} %get-tuple-element.68.refs_0_), channel_id=1, source_target_pairs={{0,16},{8,24},{16,0},{24,8},{1,17},{9,25},{17,1},{25,9},{2,18},{10... | collective-permute-start | bytes 49160 | tf_op jit(solution)/shard_map/ppermute | solution.py:57
  116.6 3.1 %collective-permute-start.24 = (f32[32,128]{1,0:T(8,128)S(1)}, f32[32,128]{1,0:T(8,128)S(1)}, u32[]{:S(2)}, u32[]{:S(2)}) collective-permute-start(f32[32,128]{1,0:T(8,128)S(1)} %get-tuple-element.68.refs_0_), channel_id=1, source_target_pairs={{0,8},{8,0},{16,24},{24,16},{1,9},{9,1},{17,25},{25,17},{2,10},{10... | collective-permute-start | bytes 49160 | tf_op jit(solution)/shard_map/ppermute | solution.py:57
  (10 other events, 141.8 us)

commit v9 on v8

--- a/solution.py
+++ b/solution.py
@@ -245,9 +245,6 @@
 
     w_blocks = {0: w_own, 1: permute(w_own, "gy", 1), 2: permute(w_own, "gy", 2)}
     w_first = permute(w_split[: width // 2], "gy", 4)
-    w_late, _ = lax.optimization_barrier(((w_blocks, w_split[width // 2 :]), x_all))
-    w_blocks[3] = permute(w_late[0][2], "gy", 1)
-    w_second = permute(w_late[1], "gy", 4)
 
     def project(x_ref, gain_ref, q_ref, k_ref, v_ref, z0_ref, z2_ref, z13_ref, held):
         gain = 1.0 + gain_ref[0:1]
@@ -280,7 +277,13 @@
         out_ref[...] = total.astype(BF)
 
     (z2,) = run("pair_sum", pair_sum, [(shape, BF)], (z2, z13))
+    late, _ = lax.optimization_barrier((lengths, z2))
+    cos, sin = rope_tables(late, rows, steps)
     z2 = permute(z2, "gx", 2)
+    early = w_split[width // 2 :], w_blocks[2], w_blocks[1], w_first
+    early, _ = lax.optimization_barrier((early, cos))
+    w_second = permute(early[0], "gy", 4)
+    w_blocks[3] = permute(early[1], "gy", 1)
 
     def share_sum(z0_ref, z13_ref, z2_ref, out_ref):
         total = z0_ref[...].astype(F32) + z13_ref[0].astype(F32) + z2_ref[...].astype(F32)
@@ -288,11 +291,10 @@
 
     (shares,) = run("share_sum", share_sum, [((ny, rows, HALF), BF)], (z0, z13, z2))
     shares, *late = lax.optimization_barrier((shares, block_table, lengths, parents))
-    cos, sin = rope_tables(late[1], rows, steps)
     tables = make_tables(*late, cache_pool.shape[1], rows, steps)
     shares = exchange(shares, "gy")
-    beside = tables, cos, sin, w_blocks[3], w_first, w_second
-    shares, (tables, cos, sin, *_) = lax.optimization_barrier((shares, beside))
+    beside = tables, w_first, w_second, w_blocks[3]
+    shares, (tables, *_) = lax.optimization_barrier((shares, beside))
 
     def pack_shares(share_ref, x_ref, out_ref):
         x = x_ref[...].astype(F32)
@@ -304,7 +306,7 @@
     )
     shares = gather_gx(shares)
     w_blocks[4] = jnp.concatenate([w_first, w_second], axis=0)
-    w_late, _ = lax.optimization_barrier((w_blocks[4], shares[2]))
+    w_late, _ = lax.optimization_barrier((w_blocks[4], shares[1]))
     w_blocks[6] = permute(w_late, "gy", 2)
     w_blocks[5] = permute(w_late, "gy", 1)
 
@@ -354,9 +356,8 @@
         ],
         limit=24,
         specs={nx + 4: IN_HBM},
-    )
-    w_late, _ = lax.optimization_barrier((w_blocks, own))
-    w_blocks[7] = permute(w_late[6], "gy", 1)
+        micros=8,
+    )
     pair = permute(pair, "gx", 1)
 
     def pair_terms(own_ref, pair_ref, out_ref):
@@ -369,6 +370,9 @@
 
     (own,) = run("pair_terms", pair_terms, [(shape, BF)], (own, pair))
     across = permute(own, "gx", 2)
+
+    w_late, _ = lax.optimization_barrier(((w_blocks[6], w_blocks[5]), own))
+    w_blocks[7] = permute(w_late[0], "gy", 1)
 
     def divide(own_ref, across_ref, out_ref):
         total = own_ref[...].astype(F32) + across_ref[...].astype(F32)
@@ -380,7 +384,9 @@
                 at = 2 * head + tile
                 out_ref[at] = (total[at] * scale).astype(BF)
 
-    (attended,) = run("divide", divide, [((2 * HEADS, half, PAGE), BF)], (own, across))
+    (attended,) = run(
+        "divide", divide, [((2 * HEADS, half, PAGE), BF)], (own, across), micros=4
+    )
     others = permute(attended, "gx", 1)
 
     def project_out(own_ref, other_ref, x_ref, gain_ref, *refs):
@@ -436,45 +442,56 @@
 
     groups = ny // nx
 
-    def gate_up(ff_ref, gate_ref, up_ref, z0_ref, z2_ref, z13_ref):
+    cut = (hidden // 128 + 1) // 2 * 128
+    column_parts = (0, cut), (cut, hidden)
+
+    def gate_up(start, end):
+        def kernel(ff_ref, gate_ref, up_ref, z0_ref, z2_ref, z13_ref):
+            me = my("gx")
+            flat = [
+                unpack_lanes(ff_ref[(me ^ n) * groups + group], rows)
+                for n in range(nx)
+                for group in range(groups)
+            ]
+            flat = jnp.concatenate(flat, axis=0)
+            for n, w_ref in enumerate((gate_ref, up_ref)):
+                sums = jnp.dot(flat, w_ref[:, start:end], preferred_element_type=F32).astype(BF)
+                here = pl.ds(n * (end - start), end - start)
+                for p, out in enumerate((z0_ref, z13_ref.at[0], z2_ref, z13_ref.at[1])):
+                    out[:, here] = sums[p * share_rows : (p + 1) * share_rows]
+
+        shape = (share_rows, 2 * (end - start))
+        return run(
+            "gate_up",
+            kernel,
+            [(shape, BF), (shape, BF), ((2,) + shape, BF)],
+            (ff_input, w_gate, w_up),
+            limit=24,
+        )
+
+    def activate(z0_ref, z13_ref, z2_ref, out_ref):
+        total = z0_ref[...].astype(F32) + z13_ref[0].astype(F32) + z2_ref[...].astype(F32)
+        count = total.shape[1] // 2
+        gate, up = total[:, :count], total[:, count:]
+        out_ref[...] = (jax.nn.gelu(gate, approximate=True) * up).astype(BF)
+
+    parts = [gate_up(*columns) for columns in column_parts]
+    blocks = []
+    for z0, z2, z13 in parts:
+        shape = z0.shape
+        z13 = permute(z13, "gx", 1)
+        (z2,) = run("pair_sum_ff", pair_sum, [(shape, BF)], (z2, z13))
+        z2 = permute(z2, "gx", 2)
+        shape = (share_rows, shape[1] // 2)
+        blocks += gather_gx(run("activate", activate, [(shape, BF)], (z0, z13, z2))[0])
+
+    def project_down(*refs):
+        w_ref, out_ref = refs[2 * nx :]
         me = my("gx")
         flat = [
-            unpack_lanes(ff_ref[(me ^ n) * groups + group], rows)
-            for n in range(nx)
-            for group in range(groups)
+            jnp.concatenate([refs[n][...], refs[nx + n][...]], axis=1) for n in range(nx)
         ]
         flat = jnp.concatenate(flat, axis=0)
-        w_refs = gate_ref, up_ref
-        for n, w_ref in enumerate(w_refs):
-            sums = jnp.dot(flat, w_ref[...], preferred_element_type=F32).astype(BF)
-            here = pl.ds(n * hidden, hidden)
-            for p, out in enumerate((z0_ref, z13_ref.at[0], z2_ref, z13_ref.at[1])):
-                out[:, here] = sums[p * share_rows : (p + 1) * share_rows]
-
-    shape = (share_rows, 2 * hidden)
-    z0, z2, z13 = run(
-        "gate_up",
-        gate_up,
-        [(shape, BF), (shape, BF), ((2,) + shape, BF)],
-        (ff_input, w_gate, w_up),
-        limit=24,
-    )
-    z13 = permute(z13, "gx", 1)
-    (z2,) = run("pair_sum_ff", pair_sum, [(shape, BF)], (z2, z13))
-    z2 = permute(z2, "gx", 2)
-
-    def activate(z0_ref, z13_ref, z2_ref, out_ref):
-        total = z0_ref[...].astype(F32) + z13_ref[0].astype(F32) + z2_ref[...].astype(F32)
-        gate, up = total[:, :hidden], total[:, hidden:]
-        out_ref[...] = (jax.nn.gelu(gate, approximate=True) * up).astype(BF)
-
-    (blocks,) = run("activate", activate, [((share_rows, hidden), BF)], (z0, z13, z2))
-    blocks = gather_gx(blocks)
-
-    def project_down(*refs):
-        w_ref, out_ref = refs[nx:]
-        me = my("gx")
-        flat = jnp.concatenate([r[...] for r in refs[:nx]], axis=0)
         sums = lax.dot_general(flat, w_ref[...], NT, preferred_element_type=F32)
         for n in range(nx):
             for group in range(groups):

time: 121 us -> 122 us (level)
  waiting for transfers between devices: 49.2 us -> 42.4 us
  starting transfers between devices: 31.9 us -> 36.8 us
  local copies, waits for them, and re-layouts: 0.94 us -> 3.41 us
    ppermute x27 -> x32, waiting for transfers between devices: 38 us -> 32.3 us  [permute(): return lax.ppermute(values, axis, [(i, i ^ m) for i in range(count)])]
    ppermute x27 -> x32, starting transfers between devices: 20.9 us -> 25.8 us  [permute(): return lax.ppermute(values, axis, [(i, i ^ m) for i in range(count)])]
    unnamed x27 -> x25, local copies, waits for them, and re-layouts: 0.9 us -> 3.38 us
    pallas_call x17 -> x20, Pallas kernels: 10.7 us -> 10.9 us  [run(): pl.pallas_call(kernel, out_shape=[jax.ShapeDtypeStruct(s, d) for s, d in...]
  transfers between devices with their start and end apart: 29 -> 34, of which waited for: 21 -> 21; matrix products, arithmetic and copies ran while one was open for 0% -> 0% of each run, Pallas kernels for 5% -> 5%
where the time goes in v9:
time: 122 us; the launch traced here: 121 us
  waiting for transfers between devices  42.4 us (35%)
  starting transfers between devices  36.8 us (30%)
  blocking collectives  26.6 us (22%)
  Pallas kernels  10.9 us (9%)
  local copies, waits for them, and re-layouts  3.41 us (3%)
    ppermute x32, waiting for transfers between devices, permute(): return lax.ppermute(values, axis, [(i, i ^ m) for i in range(count)])  32.3 us
    all_to_all x2, blocking collectives, exchange(): return lax.all_to_all(values, axes, split_axis=0, concat_axis=0, tiled=True)  26.6 us
    ppermute x32, starting transfers between devices, permute(): return lax.ppermute(values, axis, [(i, i ^ m) for i in range(count)])  25.8 us
    all_to_all x2, starting transfers between devices, exchange(): return lax.all_to_all(values, axes, split_axis=0, concat_axis=0, tiled=True)  11 us
    pallas_call x20, Pallas kernels, run(): pl.pallas_call(kernel, out_shape=[jax.ShapeDtypeStruct(s, d) for s, d in...  10.9 us
    all_to_all x2, waiting for transfers between devices, exchange(): return lax.all_to_all(values, axes, split_axis=0, concat_axis=0, tiled=True)  10.1 us
    unnamed x25, local copies, waits for them, and re-layouts  3.38 us
  transfers between devices with their start and end apart: 34, of which 21 were waited for; matrix products, arithmetic and copies ran while one was open for 0% of the time, Pallas kernels for 5%

profile of v9, /device:TPU:0, one launch (start us, length us, event | category | flops | bytes accessed | tf_op | source)
XLA Modules:
  0.0 121.2 jit_solution(4331348242160599945)
XLA Ops:
  1.7 7.4 %all-to-all-start = ((bf16[8,144,128]{2,1,0:T(8,128)(2,1)}), bf16[8,144,128]{2,1,0:T(8,128)(2,1)S(1)}, u32[]{:S(2)}, u32[]{:S(2)}) async-start(bf16[8,144,128]{2,1,0:T(8,128)(2,1)} %get-tuple-element.41), calls=%async_computation | async-start | bytes 589824 | tf_op jit(solution)/shard_map/all_to_all | solution.py:46
  9.1 2.0 %collective-permute-start.4 = (bf16[576,256]{1,0:T(8,128)(2,1)S(1)}, bf16[576,256]{1,0:T(8,128)(2,1)S(1)}, u32[]{:S(2)}, u32[]{:S(2)}) collective-permute-start(bf16[576,256]{1,0:T(8,128)(2,1)S(1)} %bitcast.5), channel_id=1, source_target_pairs={{0,1},{1,0},{2,3},{3,2},{4,5},{5,4},{6,7},{7,6},{8,9},{9,8},{10,11... | collective-permute-start | bytes 884744 | tf_op jit(solution)/shard_map/ppermute | solution.py:57
  11.1 1.5 %collective-permute-start.3 = (bf16[576,256]{1,0:T(8,128)(2,1)S(1)}, bf16[576,256]{1,0:T(8,128)(2,1)S(1)}, u32[]{:S(2)}, u32[]{:S(2)}) collective-permute-start(bf16[576,256]{1,0:T(8,128)(2,1)S(1)} %bitcast.6), channel_id=1, source_target_pairs={{0,2},{1,3},{2,0},{3,1},{4,6},{5,7},{6,4},{7,5},{8,10},{9,11},{10,... | collective-permute-start | bytes 884744 | tf_op jit(solution)/shard_map/ppermute | solution.py:57
  12.6 2.4 %collective-permute-start.2 = (bf16[288,256]{1,0:T(8,128)(2,1)S(1)}, bf16[288,256]{1,0:T(8,128)(2,1)S(1)}, u32[]{:S(2)}, u32[]{:S(2)}) collective-permute-start(bf16[288,256]{1,0:T(8,128)(2,1)S(1)} %get-tuple-element.76), channel_id=1, source_target_pairs={{0,4},{1,5},{2,6},{3,7},{4,0},{5,1},{6,2},{7,3},{8,12},{9,13},{10,... | collective-permute-start | bytes 442376 | tf_op jit(solution)/shard_map/ppermute | solution.py:57
  15.7 4.5 %all-to-all-done.x_ref = bf16[8,144,128]{2,1,0:T(8,128)(2,1)S(1)} async-done(((bf16[8,144,128]{2,1,0:T(8,128)(2,1)}), bf16[8,144,128]{2,1,0:T(8,128)(2,1)S(1)}, u32[]{:S(2)}, u32[]{:S(2)}) %all-to-all-start) | async-done | bytes 294944 | tf_op jit(solution)/shard_map/all_to_all | solution.py:46
  20.8 2.6 %collective-permute-done.2 = bf16[288,256]{1,0:T(8,128)(2,1)S(1)} collective-permute-done((bf16[288,256]{1,0:T(8,128)(2,1)S(1)}, bf16[288,256]{1,0:T(8,128)(2,1)S(1)}, u32[]{:S(2)}, u32[]{:S(2)}) %collective-permute-start.2) | collective-permute-done | bytes 147488 | tf_op jit(solution)/shard_map/ppermute | solution.py:57
  23.4 2.7 %collective-permute-done.3.refs_2_ = bf16[576,256]{1,0:T(8,128)(2,1)S(1)} collective-permute-done((bf16[576,256]{1,0:T(8,128)(2,1)S(1)}, bf16[576,256]{1,0:T(8,128)(2,1)S(1)}, u32[]{:S(2)}, u32[]{:S(2)}) %collective-permute-start.3) | collective-permute-done | bytes 294944 | tf_op jit(solution)/shard_map/ppermute | solution.py:57
  27.1 1.6 %collective-permute-start.1 = (bf16[256,128]{1,0:T(8,128)(2,1)S(1)}, bf16[256,128]{1,0:T(8,128)(2,1)S(1)}, u32[]{:S(2)}, u32[]{:S(2)}) collective-permute-start(bf16[256,128]{1,0:T(8,128)(2,1)S(1)} %pair_sum.1), channel_id=1, source_target_pairs={{0,16},{8,24},{16,0},{24,8},{1,17},{9,25},{17,1},{25,9},{2,18},{10... | collective-permute-start | bytes 196616 | tf_op jit(solution)/shard_map/ppermute | solution.py:57
  28.7 1.5 %collective-permute-start.5 = (bf16[288,256]{1,0:T(8,128)(2,1)S(1)}, bf16[288,256]{1,0:T(8,128)(2,1)S(1)}, u32[]{:S(2)}, u32[]{:S(2)}) collective-permute-start(bf16[288,256]{1,0:T(8,128)(2,1)S(1)} %get-tuple-element.53), channel_id=1, source_target_pairs={{0,4},{1,5},{2,6},{3,7},{4,0},{5,1},{6,2},{7,3},{8,12},{9,13},{10,... | collective-permute-start | bytes 442376 | tf_op jit(solution)/shard_map/ppermute | solution.py:57
  30.2 1.3 %collective-permute-done.1.z2_ref = bf16[256,128]{1,0:T(8,128)(2,1)S(1)} collective-permute-done((bf16[256,128]{1,0:T(8,128)(2,1)S(1)}, bf16[256,128]{1,0:T(8,128)(2,1)S(1)}, u32[]{:S(2)}, u32[]{:S(2)}) %collective-permute-start.1) | collective-permute-done | bytes 65568 | tf_op jit(solution)/shard_map/ppermute | solution.py:57
  32.1 3.6 %all-to-all-start.1 = ((bf16[8,32,128]{2,1,0:T(8,128)(2,1)}), bf16[8,32,128]{2,1,0:T(8,128)(2,1)S(1)}, u32[]{:S(2)}, u32[]{:S(2)}) async-start(bf16[8,32,128]{2,1,0:T(8,128)(2,1)} %share_sum.1), calls=%async_computation.1 | async-start | bytes 131072 | tf_op jit(solution)/shard_map/all_to_all | solution.py:46
  37.0 5.6 %all-to-all-done.1.share_ref = bf16[8,32,128]{2,1,0:T(8,128)(2,1)S(1)} async-done(((bf16[8,32,128]{2,1,0:T(8,128)(2,1)}), bf16[8,32,128]{2,1,0:T(8,128)(2,1)S(1)}, u32[]{:S(2)}, u32[]{:S(2)}) %all-to-all-start.1) | async-done | bytes 65568 | tf_op jit(solution)/shard_map/all_to_all | solution.py:46
  42.7 1.5 %collective-permute-start.8 = (bf16[9,32,128]{2,1,0:T(8,128)(2,1)S(1)}, bf16[9,32,128]{2,1,0:T(8,128)(2,1)S(1)}, u32[]{:S(2)}, u32[]{:S(2)}) collective-permute-start(bf16[9,32,128]{2,1,0:T(8,128)(2,1)S(1)} %pack_shares.1.refs_0_), channel_id=1, source_target_pairs={{0,16},{8,24},{16,0},{24,8},{1,17},{9,25},{17,1},{25,9},{2,18},{10... | collective-permute-start | bytes 221192 | tf_op jit(solution)/shard_map/ppermute | solution.py:57
  44.4 2.7 %collective-permute-done.8.refs_2_ = bf16[9,32,128]{2,1,0:T(8,128)(2,1)S(1)} collective-permute-done((bf16[9,32,128]{2,1,0:T(8,128)(2,1)S(1)}, bf16[9,32,128]{2,1,0:T(8,128)(2,1)S(1)}, u32[]{:S(2)}, u32[]{:S(2)}) %collective-permute-start.8) | collective-permute-done | bytes 73760 | tf_op jit(solution)/shard_map/ppermute | solution.py:57
  48.4 2.5 %copy-done.10 = bf16[2,10,128,1024]{3,2,1,0:T(8,128)(2,1)S(1)} copy-done((bf16[2,10,128,1024]{3,2,1,0:T(8,128)(2,1)S(1)}, bf16[2,10,128,1024]{3,2,1,0:T(8,128)(2,1)}, u32[]{:S(2)}) %copy-start.10) | copy-done | bytes 5242904
  50.9 3.4 %attention.1 = (bf16[17,16,128]{2,1,0:T(8,128)(2,1)S(1)}, bf16[17,16,128]{2,1,0:T(8,128)(2,1)S(1)}) custom-call(bf16[9,32,128]{2,1,0:T(8,128)(2,1)S(1)} %pack_shares.1.refs_0_, bf16[9,32,128]{2,1,0:T(8,128)(2,1)S(1)} %collective-permute-done.7.refs_1_, bf16[9,32,128]{2,1,0:T(8,128)(2,1)S(1)} %collective-permute-done.8.refs_2_, ...), custom_call_target="tpu_custom_call" | custom-call | flops 8000000000 | tf_op jit(solution)/shard_map/attention/pallas_call | solution.py:34
  55.8 1.5 %collective-permute-start.11 = (bf16[17,16,128]{2,1,0:T(8,128)(2,1)S(1)}, bf16[17,16,128]{2,1,0:T(8,128)(2,1)S(1)}, u32[]{:S(2)}, u32[]{:S(2)}) collective-permute-start(bf16[17,16,128]{2,1,0:T(8,128)(2,1)S(1)} %pair_terms.1.own_ref), channel_id=1, source_target_pairs={{0,16},{8,24},{16,0},{24,8},{1,17},{9,25},{17,1},{25,9},{2,18},{10... | collective-permute-start | bytes 208904 | tf_op jit(solution)/shard_map/ppermute | solution.py:57
  58.4 1.7 %collective-permute-done.11.across_ref = bf16[17,16,128]{2,1,0:T(8,128)(2,1)S(1)} collective-permute-done((bf16[17,16,128]{2,1,0:T(8,128)(2,1)S(1)}, bf16[17,16,128]{2,1,0:T(8,128)(2,1)S(1)}, u32[]{:S(2)}, u32[]{:S(2)}) %collective-permute-start.11) | collective-permute-done | bytes 69664 | tf_op jit(solution)/shard_map/ppermute | solution.py:57
  60.4 1.2 %collective-permute-done.12.other_ref = bf16[16,16,128]{2,1,0:T(8,128)(2,1)S(1)} collective-permute-done((bf16[16,16,128]{2,1,0:T(8,128)(2,1)S(1)}, bf16[16,16,128]{2,1,0:T(8,128)(2,1)S(1)}, u32[]{:S(2)}, u32[]{:S(2)}) %collective-permute-start.12) | collective-permute-done | bytes 65568 | tf_op jit(solution)/shard_map/ppermute | solution.py:57
  61.7 4.5 %collective-permute-done.15.refs_7_ = bf16[576,256]{1,0:T(8,128)(2,1)S(1)} collective-permute-done((bf16[576,256]{1,0:T(8,128)(2,1)S(1)}, bf16[576,256]{1,0:T(8,128)(2,1)S(1)}, u32[]{:S(2)}, u32[]{:S(2)}) %collective-permute-start.15) | collective-permute-done | bytes 294944 | tf_op jit(solution)/shard_map/ppermute | solution.py:57
  67.8 1.2 collective-permute-start.16
  68.9 1.3 %collective-permute-done.18.refs_3_ = f32[32,128]{1,0:T(8,128)S(1)} collective-permute-done((f32[32,128]{1,0:T(8,128)S(1)}, f32[32,128]{1,0:T(8,128)S(1)}, u32[]{:S(2)}, u32[]{:S(2)}) %collective-permute-start.18) | collective-permute-done | bytes 16416 | tf_op jit(solution)/shard_map/ppermute | solution.py:57
  71.2 13.3 %all_to_all.20.ff_ref = bf16[8,144,128]{2,1,0:T(8,128)(2,1)S(1)} all-to-all(bf16[8,144,128]{2,1,0:T(8,128)(2,1)S(1)} %get-tuple-element.65), channel_id=1, replica_groups=mesh['gx'=4,'gy'=8] {'gy'}, dimensions={0} | all-to-all | bytes 589824 | tf_op jit(solution)/shard_map/all_to_all | solution.py:46
  87.0 1.5 %collective-permute-start.20 = (bf16[64,1280]{1,0:T(8,128)(2,1)S(1)}, bf16[64,1280]{1,0:T(8,128)(2,1)S(1)}, u32[]{:S(2)}, u32[]{:S(2)}) collective-permute-start(bf16[64,1280]{1,0:T(8,128)(2,1)S(1)} %pair_sum_ff.2), channel_id=1, source_target_pairs={{0,16},{8,24},{16,0},{24,8},{1,17},{9,25},{17,1},{25,9},{2,18},{10... | collective-permute-start | bytes 491528 | tf_op jit(solution)/shard_map/ppermute | solution.py:57
  89.2 4.9 %collective-permute-done.20.z2_ref = bf16[64,1280]{1,0:T(8,128)(2,1)S(1)} collective-permute-done((bf16[64,1280]{1,0:T(8,128)(2,1)S(1)}, bf16[64,1280]{1,0:T(8,128)(2,1)S(1)}, u32[]{:S(2)}, u32[]{:S(2)}) %collective-permute-start.20) | collective-permute-done | bytes 163872 | tf_op jit(solution)/shard_map/ppermute | solution.py:57
  94.2 1.5 %collective-permute-start.22 = (bf16[64,640]{1,0:T(8,128)(2,1)S(1)}, bf16[64,640]{1,0:T(8,128)(2,1)S(1)}, u32[]{:S(2)}, u32[]{:S(2)}) collective-permute-start(bf16[64,640]{1,0:T(8,128)(2,1)S(1)} %activate.2.refs_0_), channel_id=1, source_target_pairs={{0,16},{8,24},{16,0},{24,8},{1,17},{9,25},{17,1},{25,9},{2,18},{10... | collective-permute-start | bytes 245768 | tf_op jit(solution)/shard_map/ppermute | solution.py:57
  96.9 1.5 %collective-permute-start.27 = (bf16[64,512]{1,0:T(8,128)(2,1)S(1)}, bf16[64,512]{1,0:T(8,128)(2,1)S(1)}, u32[]{:S(2)}, u32[]{:S(2)}) collective-permute-start(bf16[64,512]{1,0:T(8,128)(2,1)S(1)} %activate.3.refs_4_), channel_id=1, source_target_pairs={{0,16},{8,24},{16,0},{24,8},{1,17},{9,25},{17,1},{25,9},{2,18},{10... | collective-permute-start | bytes 196616 | tf_op jit(solution)/shard_map/ppermute | solution.py:57
  99.8 1.4 %collective-permute-done.27.refs_6_ = bf16[64,512]{1,0:T(8,128)(2,1)S(1)} collective-permute-done((bf16[64,512]{1,0:T(8,128)(2,1)S(1)}, bf16[64,512]{1,0:T(8,128)(2,1)S(1)}, u32[]{:S(2)}, u32[]{:S(2)}) %collective-permute-start.27) | collective-permute-done | bytes 65568 | tf_op jit(solution)/shard_map/ppermute | solution.py:57
  101.2 1.2 %collective-permute-done.28.refs_7_ = bf16[64,512]{1,0:T(8,128)(2,1)S(1)} collective-permute-done((bf16[64,512]{1,0:T(8,128)(2,1)S(1)}, bf16[64,512]{1,0:T(8,128)(2,1)S(1)}, u32[]{:S(2)}, u32[]{:S(2)}) %collective-permute-start.28) | collective-permute-done | bytes 65568 | tf_op jit(solution)/shard_map/ppermute | solution.py:57
  103.2 13.3 %all_to_all.21.parts_ref = bf16[8,144,128]{2,1,0:T(8,128)(2,1)S(1)} all-to-all(bf16[8,144,128]{2,1,0:T(8,128)(2,1)S(1)} %project_down.1), channel_id=1, replica_groups=mesh['gx'=4,'gy'=8] {'gy'}, dimensions={0} | all-to-all | bytes 589824 | tf_op jit(solution)/shard_map/all_to_all | solution.py:46
  116.7 1.5 %collective-permute-start.30 = (f32[32,128]{1,0:T(8,128)S(1)}, f32[32,128]{1,0:T(8,128)S(1)}, u32[]{:S(2)}, u32[]{:S(2)}) collective-permute-start(f32[32,128]{1,0:T(8,128)S(1)} %get-tuple-element.72.refs_0_), channel_id=1, source_target_pairs={{0,16},{8,24},{16,0},{24,8},{1,17},{9,25},{17,1},{25,9},{2,18},{10... | collective-permute-start | bytes 49160 | tf_op jit(solution)/shard_map/ppermute | solution.py:57
  118.6 1.5 %collective-permute-done.31.refs_3_ = f32[32,128]{1,0:T(8,128)S(1)} collective-permute-done((f32[32,128]{1,0:T(8,128)S(1)}, f32[32,128]{1,0:T(8,128)S(1)}, u32[]{:S(2)}, u32[]{:S(2)}) %collective-permute-start.31) | collective-permute-done | bytes 16416 | tf_op jit(solution)/shard_map/ppermute | solution.py:57
  (88 shorter events, 20.4 us)
Async XLA Ops:
  1.7 18.5 %all-to-all-start = ((bf16[8,144,128]{2,1,0:T(8,128)(2,1)}), bf16[8,144,128]{2,1,0:T(8,128)(2,1)S(1)}, u32[]{:S(2)}, u32[]{:S(2)}) async-start(bf16[8,144,128]{2,1,0:T(8,128)(2,1)} %get-tuple-element.41), calls=%async_computation | async-start | bytes 589824 | tf_op jit(solution)/shard_map/all_to_all | solution.py:46
  9.1 14.4 %collective-permute-start.4 = (bf16[576,256]{1,0:T(8,128)(2,1)S(1)}, bf16[576,256]{1,0:T(8,128)(2,1)S(1)}, u32[]{:S(2)}, u32[]{:S(2)}) collective-permute-start(bf16[576,256]{1,0:T(8,128)(2,1)S(1)} %bitcast.5), channel_id=1, source_target_pairs={{0,1},{1,0},{2,3},{3,2},{4,5},{5,4},{6,7},{7,6},{8,9},{9,8},{10,11... | collective-permute-start | bytes 884744 | tf_op jit(solution)/shard_map/ppermute | solution.py:57
  11.1 15.0 %collective-permute-start.3 = (bf16[576,256]{1,0:T(8,128)(2,1)S(1)}, bf16[576,256]{1,0:T(8,128)(2,1)S(1)}, u32[]{:S(2)}, u32[]{:S(2)}) collective-permute-start(bf16[576,256]{1,0:T(8,128)(2,1)S(1)} %bitcast.6), channel_id=1, source_target_pairs={{0,2},{1,3},{2,0},{3,1},{4,6},{5,7},{6,4},{7,5},{8,10},{9,11},{10,... | collective-permute-start | bytes 884744 | tf_op jit(solution)/shard_map/ppermute | solution.py:57
  12.6 10.9 %collective-permute-start.2 = (bf16[288,256]{1,0:T(8,128)(2,1)S(1)}, bf16[288,256]{1,0:T(8,128)(2,1)S(1)}, u32[]{:S(2)}, u32[]{:S(2)}) collective-permute-start(bf16[288,256]{1,0:T(8,128)(2,1)S(1)} %get-tuple-element.76), channel_id=1, source_target_pairs={{0,4},{1,5},{2,6},{3,7},{4,0},{5,1},{6,2},{7,3},{8,12},{9,13},{10,... | collective-permute-start | bytes 442376 | tf_op jit(solution)/shard_map/ppermute | solution.py:57
  20.6 6.5 %collective-permute-start = (bf16[2,256,128]{2,1,0:T(8,128)(2,1)S(1)}, bf16[2,256,128]{2,1,0:T(8,128)(2,1)S(1)}, u32[]{:S(2)}, u32[]{:S(2)}) collective-permute-start(bf16[2,256,128]{2,1,0:T(8,128)(2,1)S(1)} %get-tuple-element.43), channel_id=1, source_target_pairs={{0,8},{8,0},{16,24},{24,16},{1,9},{9,1},{17,25},{25,17},{2,10},{10... | collective-permute-start | bytes 393224 | tf_op jit(solution)/shard_map/ppermute | solution.py:57
  26.1 10.9 %collective-permute-start.6 = (bf16[576,256]{1,0:T(8,128)(2,1)S(1)}, bf16[576,256]{1,0:T(8,128)(2,1)S(1)}, u32[]{:S(2)}, u32[]{:S(2)}) collective-permute-start(bf16[576,256]{1,0:T(8,128)(2,1)S(1)} %collective-permute-done.3.refs_2_), channel_id=1, source_target_pairs={{0,1},{1,0},{2,3},{3,2},{4,5},{5,4},{6,7},{7,6},{8,9},{9,8},{10,11... | collective-permute-start | bytes 884744 | tf_op jit(solution)/shard_map/ppermute | solution.py:57
  27.1 4.3 %collective-permute-start.1 = (bf16[256,128]{1,0:T(8,128)(2,1)S(1)}, bf16[256,128]{1,0:T(8,128)(2,1)S(1)}, u32[]{:S(2)}, u32[]{:S(2)}) collective-permute-start(bf16[256,128]{1,0:T(8,128)(2,1)S(1)} %pair_sum.1), channel_id=1, source_target_pairs={{0,16},{8,24},{16,0},{24,8},{1,17},{9,25},{17,1},{25,9},{2,18},{10... | collective-permute-start | bytes 196616 | tf_op jit(solution)/shard_map/ppermute | solution.py:57
  28.7 8.3 %collective-permute-start.5 = (bf16[288,256]{1,0:T(8,128)(2,1)S(1)}, bf16[288,256]{1,0:T(8,128)(2,1)S(1)}, u32[]{:S(2)}, u32[]{:S(2)}) collective-permute-start(bf16[288,256]{1,0:T(8,128)(2,1)S(1)} %get-tuple-element.53), channel_id=1, source_target_pairs={{0,4},{1,5},{2,6},{3,7},{4,0},{5,1},{6,2},{7,3},{8,12},{9,13},{10,... | collective-permute-start | bytes 442376 | tf_op jit(solution)/shard_map/ppermute | solution.py:57
  32.1 10.6 %all-to-all-start.1 = ((bf16[8,32,128]{2,1,0:T(8,128)(2,1)}), bf16[8,32,128]{2,1,0:T(8,128)(2,1)S(1)}, u32[]{:S(2)}, u32[]{:S(2)}) async-start(bf16[8,32,128]{2,1,0:T(8,128)(2,1)} %share_sum.1), calls=%async_computation.1 | async-start | bytes 131072 | tf_op jit(solution)/shard_map/all_to_all | solution.py:46
  42.7 4.4 %collective-permute-start.8 = (bf16[9,32,128]{2,1,0:T(8,128)(2,1)S(1)}, bf16[9,32,128]{2,1,0:T(8,128)(2,1)S(1)}, u32[]{:S(2)}, u32[]{:S(2)}) collective-permute-start(bf16[9,32,128]{2,1,0:T(8,128)(2,1)S(1)} %pack_shares.1.refs_0_), channel_id=1, source_target_pairs={{0,16},{8,24},{16,0},{24,8},{1,17},{9,25},{17,1},{25,9},{2,18},{10... | collective-permute-start | bytes 221192 | tf_op jit(solution)/shard_map/ppermute | solution.py:57
  44.3 2.8 %collective-permute-start.7 = (bf16[9,32,128]{2,1,0:T(8,128)(2,1)S(1)}, bf16[9,32,128]{2,1,0:T(8,128)(2,1)S(1)}, u32[]{:S(2)}, u32[]{:S(2)}) collective-permute-start(bf16[9,32,128]{2,1,0:T(8,128)(2,1)S(1)} %pack_shares.1.refs_0_), channel_id=1, source_target_pairs={{0,8},{8,0},{16,24},{24,16},{1,9},{9,1},{17,25},{25,17},{2,10},{10... | collective-permute-start | bytes 221192 | tf_op jit(solution)/shard_map/ppermute | solution.py:57
  47.1 10.2 %collective-permute-start.14 = (bf16[576,256]{1,0:T(8,128)(2,1)S(1)}, bf16[576,256]{1,0:T(8,128)(2,1)S(1)}, u32[]{:S(2)}, u32[]{:S(2)}) collective-permute-start(bf16[576,256]{1,0:T(8,128)(2,1)S(1)} %constant_dynamic-update-slice_fusion.refs_4_), channel_id=1, source_target_pairs={{0,2},{1,3},{2,0},{3,1},{4,6},{5,7},{6,4},{7,5},{8,10},{9,11},{10,... | collective-permute-start | bytes 884744 | tf_op jit(solution)/shard_map/ppermute | solution.py:57
  47.4 10.0 %collective-permute-start.13 = (bf16[576,256]{1,0:T(8,128)(2,1)S(1)}, bf16[576,256]{1,0:T(8,128)(2,1)S(1)}, u32[]{:S(2)}, u32[]{:S(2)}) collective-permute-start(bf16[576,256]{1,0:T(8,128)(2,1)S(1)} %constant_dynamic-update-slice_fusion.refs_4_), channel_id=1, source_target_pairs={{0,1},{1,0},{2,3},{3,2},{4,5},{5,4},{6,7},{7,6},{8,9},{9,8},{10,11... | collective-permute-start | bytes 884744 | tf_op jit(solution)/shard_map/ppermute | solution.py:57
  54.4 1.3 %collective-permute-start.10 = (bf16[17,16,128]{2,1,0:T(8,128)(2,1)S(1)}, bf16[17,16,128]{2,1,0:T(8,128)(2,1)S(1)}, u32[]{:S(2)}, u32[]{:S(2)}) collective-permute-start(bf16[17,16,128]{2,1,0:T(8,128)(2,1)S(1)} %get-tuple-element.60), channel_id=1, source_target_pairs={{0,8},{8,0},{16,24},{24,16},{1,9},{9,1},{17,25},{25,17},{2,10},{10... | collective-permute-start | bytes 208904 | tf_op jit(solution)/shard_map/ppermute | solution.py:57
  55.8 4.3 %collective-permute-start.11 = (bf16[17,16,128]{2,1,0:T(8,128)(2,1)S(1)}, bf16[17,16,128]{2,1,0:T(8,128)(2,1)S(1)}, u32[]{:S(2)}, u32[]{:S(2)}) collective-permute-start(bf16[17,16,128]{2,1,0:T(8,128)(2,1)S(1)} %pair_terms.1.own_ref), channel_id=1, source_target_pairs={{0,16},{8,24},{16,0},{24,8},{1,17},{9,25},{17,1},{25,9},{2,18},{10... | collective-permute-start | bytes 208904 | tf_op jit(solution)/shard_map/ppermute | solution.py:57
  57.4 8.8 %collective-permute-start.15 = (bf16[576,256]{1,0:T(8,128)(2,1)S(1)}, bf16[576,256]{1,0:T(8,128)(2,1)S(1)}, u32[]{:S(2)}, u32[]{:S(2)}) collective-permute-start(bf16[576,256]{1,0:T(8,128)(2,1)S(1)} %collective-permute-done.14.refs_6_), channel_id=1, source_target_pairs={{0,1},{1,0},{2,3},{3,2},{4,5},{5,4},{6,7},{7,6},{8,9},{9,8},{10,11... | collective-permute-start | bytes 884744 | tf_op jit(solution)/shard_map/ppermute | solution.py:57
  60.3 1.3 %collective-permute-start.12 = (bf16[16,16,128]{2,1,0:T(8,128)(2,1)S(1)}, bf16[16,16,128]{2,1,0:T(8,128)(2,1)S(1)}, u32[]{:S(2)}, u32[]{:S(2)}) collective-permute-start(bf16[16,16,128]{2,1,0:T(8,128)(2,1)S(1)} %divide.1.own_ref), channel_id=1, source_target_pairs={{0,8},{8,0},{16,24},{24,16},{1,9},{9,1},{17,25},{25,17},{2,10},{10... | collective-permute-start | bytes 196616 | tf_op jit(solution)/shard_map/ppermute | solution.py:57
  67.0 3.2 %collective-permute-start.18 = (f32[32,128]{1,0:T(8,128)S(1)}, f32[32,128]{1,0:T(8,128)S(1)}, u32[]{:S(2)}, u32[]{:S(2)}) collective-permute-start(f32[32,128]{1,0:T(8,128)S(1)} %get-tuple-element.63.refs_0_), channel_id=1, source_target_pairs={{0,24},{8,16},{16,8},{24,0},{1,25},{9,17},{17,9},{25,1},{2,26},{10... | collective-permute-start | bytes 49160 | tf_op jit(solution)/shard_map/ppermute | solution.py:57
  67.1 3.8 %collective-permute-start.17 = (f32[32,128]{1,0:T(8,128)S(1)}, f32[32,128]{1,0:T(8,128)S(1)}, u32[]{:S(2)}, u32[]{:S(2)}) collective-permute-start(f32[32,128]{1,0:T(8,128)S(1)} %get-tuple-element.63.refs_0_), channel_id=1, source_target_pairs={{0,16},{8,24},{16,0},{24,8},{1,17},{9,25},{17,1},{25,9},{2,18},{10... | collective-permute-start | bytes 49160 | tf_op jit(solution)/shard_map/ppermute | solution.py:57
  67.8 3.1 %collective-permute-start.16 = (f32[32,128]{1,0:T(8,128)S(1)}, f32[32,128]{1,0:T(8,128)S(1)}, u32[]{:S(2)}, u32[]{:S(2)}) collective-permute-start(f32[32,128]{1,0:T(8,128)S(1)} %get-tuple-element.63.refs_0_), channel_id=1, source_target_pairs={{0,8},{8,0},{16,24},{24,16},{1,9},{9,1},{17,25},{25,17},{2,10},{10... | collective-permute-start | bytes 49160 | tf_op jit(solution)/shard_map/ppermute | solution.py:57
  85.3 1.7 %collective-permute-start.19 = (bf16[2,64,1280]{2,1,0:T(8,128)(2,1)S(1)}, bf16[2,64,1280]{2,1,0:T(8,128)(2,1)S(1)}, u32[]{:S(2)}, u32[]{:S(2)}) collective-permute-start(bf16[2,64,1280]{2,1,0:T(8,128)(2,1)S(1)} %get-tuple-element.67), channel_id=1, source_target_pairs={{0,8},{8,0},{16,24},{24,16},{1,9},{9,1},{17,25},{25,17},{2,10},{10... | collective-permute-start | bytes 983048 | tf_op jit(solution)/shard_map/ppermute | solution.py:57
  85.9 2.6 %collective-permute-start.24 = (bf16[2,64,1024]{2,1,0:T(8,128)(2,1)S(1)}, bf16[2,64,1024]{2,1,0:T(8,128)(2,1)S(1)}, u32[]{:S(2)}, u32[]{:S(2)}) collective-permute-start(bf16[2,64,1024]{2,1,0:T(8,128)(2,1)S(1)} %get-tuple-element.70), channel_id=1, source_target_pairs={{0,8},{8,0},{16,24},{24,16},{1,9},{9,1},{17,25},{25,17},{2,10},{10... | collective-permute-start | bytes 786440 | tf_op jit(solution)/shard_map/ppermute | solution.py:57
  87.0 7.1 %collective-permute-start.20 = (bf16[64,1280]{1,0:T(8,128)(2,1)S(1)}, bf16[64,1280]{1,0:T(8,128)(2,1)S(1)}, u32[]{:S(2)}, u32[]{:S(2)}) collective-permute-start(bf16[64,1280]{1,0:T(8,128)(2,1)S(1)} %pair_sum_ff.2), channel_id=1, source_target_pairs={{0,16},{8,24},{16,0},{24,8},{1,17},{9,25},{17,1},{25,9},{2,18},{10... | collective-permute-start | bytes 491528 | tf_op jit(solution)/shard_map/ppermute | solution.py:57
  88.5 8.2 %collective-permute-start.25 = (bf16[64,1024]{1,0:T(8,128)(2,1)S(1)}, bf16[64,1024]{1,0:T(8,128)(2,1)S(1)}, u32[]{:S(2)}, u32[]{:S(2)}) collective-permute-start(bf16[64,1024]{1,0:T(8,128)(2,1)S(1)} %pair_sum_ff.3), channel_id=1, source_target_pairs={{0,16},{8,24},{16,0},{24,8},{1,17},{9,25},{17,1},{25,9},{2,18},{10... | collective-permute-start | bytes 393224 | tf_op jit(solution)/shard_map/ppermute | solution.py:57
  94.2 5.1 %collective-permute-start.22 = (bf16[64,640]{1,0:T(8,128)(2,1)S(1)}, bf16[64,640]{1,0:T(8,128)(2,1)S(1)}, u32[]{:S(2)}, u32[]{:S(2)}) collective-permute-start(bf16[64,640]{1,0:T(8,128)(2,1)S(1)} %activate.2.refs_0_), channel_id=1, source_target_pairs={{0,16},{8,24},{16,0},{24,8},{1,17},{9,25},{17,1},{25,9},{2,18},{10... | collective-permute-start | bytes 245768 | tf_op jit(solution)/shard_map/ppermute | solution.py:57
  96.9 4.3 %collective-permute-start.27 = (bf16[64,512]{1,0:T(8,128)(2,1)S(1)}, bf16[64,512]{1,0:T(8,128)(2,1)S(1)}, u32[]{:S(2)}, u32[]{:S(2)}) collective-permute-start(bf16[64,512]{1,0:T(8,128)(2,1)S(1)} %activate.3.refs_4_), channel_id=1, source_target_pairs={{0,16},{8,24},{16,0},{24,8},{1,17},{9,25},{17,1},{25,9},{2,18},{10... | collective-permute-start | bytes 196616 | tf_op jit(solution)/shard_map/ppermute | solution.py:57
  98.4 4.1 %collective-permute-start.21 = (bf16[64,640]{1,0:T(8,128)(2,1)S(1)}, bf16[64,640]{1,0:T(8,128)(2,1)S(1)}, u32[]{:S(2)}, u32[]{:S(2)}) collective-permute-start(bf16[64,640]{1,0:T(8,128)(2,1)S(1)} %activate.2.refs_0_), channel_id=1, source_target_pairs={{0,8},{8,0},{16,24},{24,16},{1,9},{9,1},{17,25},{25,17},{2,10},{10... | collective-permute-start | bytes 245768 | tf_op jit(solution)/shard_map/ppermute | solution.py:57
  99.3 3.2 %collective-permute-start.23 = (bf16[64,640]{1,0:T(8,128)(2,1)S(1)}, bf16[64,640]{1,0:T(8,128)(2,1)S(1)}, u32[]{:S(2)}, u32[]{:S(2)}) collective-permute-start(bf16[64,640]{1,0:T(8,128)(2,1)S(1)} %collective-permute-done.22.refs_2_), channel_id=1, source_target_pairs={{0,8},{8,0},{16,24},{24,16},{1,9},{9,1},{17,25},{25,17},{2,10},{10... | collective-permute-start | bytes 245768 | tf_op jit(solution)/shard_map/ppermute | solution.py:57
  99.3 1.9 %collective-permute-start.26 = (bf16[64,512]{1,0:T(8,128)(2,1)S(1)}, bf16[64,512]{1,0:T(8,128)(2,1)S(1)}, u32[]{:S(2)}, u32[]{:S(2)}) collective-permute-start(bf16[64,512]{1,0:T(8,128)(2,1)S(1)} %activate.3.refs_4_), channel_id=1, source_target_pairs={{0,8},{8,0},{16,24},{24,16},{1,9},{9,1},{17,25},{25,17},{2,10},{10... | collective-permute-start | bytes 196616 | tf_op jit(solution)/shard_map/ppermute | solution.py:57
  116.7 3.3 %collective-permute-start.31 = (f32[32,128]{1,0:T(8,128)S(1)}, f32[32,128]{1,0:T(8,128)S(1)}, u32[]{:S(2)}, u32[]{:S(2)}) collective-permute-start(f32[32,128]{1,0:T(8,128)S(1)} %get-tuple-element.72.refs_0_), channel_id=1, source_target_pairs={{0,24},{8,16},{16,8},{24,0},{1,25},{9,17},{17,9},{25,1},{2,26},{10... | collective-permute-start | bytes 49160 | tf_op jit(solution)/shard_map/ppermute | solution.py:57
  116.7 3.8 %collective-permute-start.30 = (f32[32,128]{1,0:T(8,128)S(1)}, f32[32,128]{1,0:T(8,128)S(1)}, u32[]{:S(2)}, u32[]{:S(2)}) collective-permute-start(f32[32,128]{1,0:T(8,128)S(1)} %get-tuple-element.72.refs_0_), channel_id=1, source_target_pairs={{0,16},{8,24},{16,0},{24,8},{1,17},{9,25},{17,1},{25,9},{2,18},{10... | collective-permute-start | bytes 49160 | tf_op jit(solution)/shard_map/ppermute | solution.py:57
  118.2 2.3 %collective-permute-start.29 = (f32[32,128]{1,0:T(8,128)S(1)}, f32[32,128]{1,0:T(8,128)S(1)}, u32[]{:S(2)}, u32[]{:S(2)}) collective-permute-start(f32[32,128]{1,0:T(8,128)S(1)} %get-tuple-element.72.refs_0_), channel_id=1, source_target_pairs={{0,8},{8,0},{16,24},{24,16},{1,9},{9,1},{17,25},{25,17},{2,10},{10... | collective-permute-start | bytes 49160 | tf_op jit(solution)/shard_map/ppermute | solution.py:57
  (14 other events, 227.0 us)

commit v10 on v9

--- a/solution.py
+++ b/solution.py
@@ -245,6 +245,9 @@
 
     w_blocks = {0: w_own, 1: permute(w_own, "gy", 1), 2: permute(w_own, "gy", 2)}
     w_first = permute(w_split[: width // 2], "gy", 4)
+    w_late, _ = lax.optimization_barrier(((w_blocks[1], w_split[width // 2 :]), x_all))
+    w_blocks[3] = permute(w_late[0], "gy", 2)
+    w_second = permute(w_late[1], "gy", 4)
 
     def project(x_ref, gain_ref, q_ref, k_ref, v_ref, z0_ref, z2_ref, z13_ref, held):
         gain = 1.0 + gain_ref[0:1]
@@ -277,13 +280,7 @@
         out_ref[...] = total.astype(BF)
 
     (z2,) = run("pair_sum", pair_sum, [(shape, BF)], (z2, z13))
-    late, _ = lax.optimization_barrier((lengths, z2))
-    cos, sin = rope_tables(late, rows, steps)
     z2 = permute(z2, "gx", 2)
-    early = w_split[width // 2 :], w_blocks[2], w_blocks[1], w_first
-    early, _ = lax.optimization_barrier((early, cos))
-    w_second = permute(early[0], "gy", 4)
-    w_blocks[3] = permute(early[1], "gy", 1)
 
     def share_sum(z0_ref, z13_ref, z2_ref, out_ref):
         total = z0_ref[...].astype(F32) + z13_ref[0].astype(F32) + z2_ref[...].astype(F32)
@@ -291,10 +288,11 @@
 
     (shares,) = run("share_sum", share_sum, [((ny, rows, HALF), BF)], (z0, z13, z2))
     shares, *late = lax.optimization_barrier((shares, block_table, lengths, parents))
+    cos, sin = rope_tables(late[1], rows, steps)
     tables = make_tables(*late, cache_pool.shape[1], rows, steps)
     shares = exchange(shares, "gy")
-    beside = tables, w_first, w_second, w_blocks[3]
-    shares, (tables, *_) = lax.optimization_barrier((shares, beside))
+    beside = tables, cos, sin, w_blocks[2], w_blocks[3], w_first, w_second
+    shares, (tables, cos, sin, *_) = lax.optimization_barrier((shares, beside))
 
     def pack_shares(share_ref, x_ref, out_ref):
         x = x_ref[...].astype(F32)
@@ -306,7 +304,7 @@
     )
     shares = gather_gx(shares)
     w_blocks[4] = jnp.concatenate([w_first, w_second], axis=0)
-    w_late, _ = lax.optimization_barrier((w_blocks[4], shares[1]))
+    w_late, _ = lax.optimization_barrier((w_blocks[4], shares[2]))
     w_blocks[6] = permute(w_late, "gy", 2)
     w_blocks[5] = permute(w_late, "gy", 1)
 
@@ -356,8 +354,9 @@
         ],
         limit=24,
         specs={nx + 4: IN_HBM},
-        micros=8,
-    )
+    )
+    w_late, _ = lax.optimization_barrier((w_blocks, own))
+    w_blocks[7] = permute(w_late[6], "gy", 1)
     pair = permute(pair, "gx", 1)
 
     def pair_terms(own_ref, pair_ref, out_ref):
@@ -370,9 +369,6 @@
 
     (own,) = run("pair_terms", pair_terms, [(shape, BF)], (own, pair))
     across = permute(own, "gx", 2)
-
-    w_late, _ = lax.optimization_barrier(((w_blocks[6], w_blocks[5]), own))
-    w_blocks[7] = permute(w_late[0], "gy", 1)
 
     def divide(own_ref, across_ref, out_ref):
         total = own_ref[...].astype(F32) + across_ref[...].astype(F32)
@@ -384,9 +380,7 @@
                 at = 2 * head + tile
                 out_ref[at] = (total[at] * scale).astype(BF)
 
-    (attended,) = run(
-        "divide", divide, [((2 * HEADS, half, PAGE), BF)], (own, across), micros=4
-    )
+    (attended,) = run("divide", divide, [((2 * HEADS, half, PAGE), BF)], (own, across))
     others = permute(attended, "gx", 1)
 
     def project_out(own_ref, other_ref, x_ref, gain_ref, *refs):

time: 122 us -> 116 us (0.951)
  local copies, waits for them, and re-layouts: 3.41 us -> 0.94 us
  waiting for transfers between devices: 42.4 us -> 40.1 us
    unnamed x25 -> x27, local copies, waits for them, and re-layouts: 3.38 us -> 0.9 us
  transfers between devices with their start and end apart: 34 -> 34, of which waited for: 21 -> 23; matrix products, arithmetic and copies ran while one was open for 0% -> 0% of each run, Pallas kernels for 5% -> 6%
where the time goes in v10:
time: 116 us
  waiting for transfers between devices  40.1 us (35%)
  starting transfers between devices  36.1 us (31%)
  blocking collectives  26.7 us (23%)
  Pallas kernels  10.9 us (9%)
    ppermute x32, waiting for transfers between devices, permute(): return lax.ppermute(values, axis, [(i, i ^ m) for i in range(count)])  31.2 us
    all_to_all x2, blocking collectives, exchange(): return lax.all_to_all(values, axes, split_axis=0, concat_axis=0, tiled=True)  26.7 us
    ppermute x32, starting transfers between devices, permute(): return lax.ppermute(values, axis, [(i, i ^ m) for i in range(count)])  25.4 us
    pallas_call x20, Pallas kernels, run(): pl.pallas_call(kernel, out_shape=[jax.ShapeDtypeStruct(s, d) for s, d in...  10.9 us
    all_to_all x2, starting transfers between devices, exchange(): return lax.all_to_all(values, axes, split_axis=0, concat_axis=0, tiled=True)  10.7 us
    all_to_all x2, waiting for transfers between devices, exchange(): return lax.all_to_all(values, axes, split_axis=0, concat_axis=0, tiled=True)  8.95 us
  transfers between devices with their start and end apart: 34, of which 23 were waited for; matrix products, arithmetic and copies ran while one was open for 0% of the time, Pallas kernels for 6%

profile of v10, /device:TPU:0, one launch (start us, length us, event | category | flops | bytes accessed | tf_op | source)
XLA Modules:
  0.0 115.8 jit_solution(5557038194988674105)
XLA Ops:
  1.7 7.4 %all-to-all-start = ((bf16[8,144,128]{2,1,0:T(8,128)(2,1)}), bf16[8,144,128]{2,1,0:T(8,128)(2,1)S(1)}, u32[]{:S(2)}, u32[]{:S(2)}) async-start(bf16[8,144,128]{2,1,0:T(8,128)(2,1)} %get-tuple-element.42), calls=%async_computation | async-start | bytes 589824 | tf_op jit(solution)/shard_map/all_to_all | solution.py:46
  9.1 2.1 %collective-permute-start.3 = (bf16[576,256]{1,0:T(8,128)(2,1)S(1)}, bf16[576,256]{1,0:T(8,128)(2,1)S(1)}, u32[]{:S(2)}, u32[]{:S(2)}) collective-permute-start(bf16[576,256]{1,0:T(8,128)(2,1)S(1)} %bitcast.7), channel_id=1, source_target_pairs={{0,1},{1,0},{2,3},{3,2},{4,5},{5,4},{6,7},{7,6},{8,9},{9,8},{10,11... | collective-permute-start | bytes 884744 | tf_op jit(solution)/shard_map/ppermute | solution.py:57
  11.2 1.5 %collective-permute-start.2 = (bf16[576,256]{1,0:T(8,128)(2,1)S(1)}, bf16[576,256]{1,0:T(8,128)(2,1)S(1)}, u32[]{:S(2)}, u32[]{:S(2)}) collective-permute-start(bf16[576,256]{1,0:T(8,128)(2,1)S(1)} %bitcast.8), channel_id=1, source_target_pairs={{0,2},{1,3},{2,0},{3,1},{4,6},{5,7},{6,4},{7,5},{8,10},{9,11},{10,... | collective-permute-start | bytes 884744 | tf_op jit(solution)/shard_map/ppermute | solution.py:57
  12.6 2.4 %collective-permute-start.5 = (bf16[288,256]{1,0:T(8,128)(2,1)S(1)}, bf16[288,256]{1,0:T(8,128)(2,1)S(1)}, u32[]{:S(2)}, u32[]{:S(2)}) collective-permute-start(bf16[288,256]{1,0:T(8,128)(2,1)S(1)} %get-tuple-element.77), channel_id=1, source_target_pairs={{0,4},{1,5},{2,6},{3,7},{4,0},{5,1},{6,2},{7,3},{8,12},{9,13},{10,... | collective-permute-start | bytes 442376 | tf_op jit(solution)/shard_map/ppermute | solution.py:57
  15.1 5.0 %all-to-all-done.x_ref = bf16[8,144,128]{2,1,0:T(8,128)(2,1)S(1)} async-done(((bf16[8,144,128]{2,1,0:T(8,128)(2,1)}), bf16[8,144,128]{2,1,0:T(8,128)(2,1)S(1)}, u32[]{:S(2)}, u32[]{:S(2)}) %all-to-all-start) | async-done | bytes 294944 | tf_op jit(solution)/shard_map/all_to_all | solution.py:46
  21.4 1.9 %collective-permute-start.6 = (bf16[288,256]{1,0:T(8,128)(2,1)S(1)}, bf16[288,256]{1,0:T(8,128)(2,1)S(1)}, u32[]{:S(2)}, u32[]{:S(2)}) collective-permute-start(bf16[288,256]{1,0:T(8,128)(2,1)S(1)} %get-tuple-element.54), channel_id=1, source_target_pairs={{0,4},{1,5},{2,6},{3,7},{4,0},{5,1},{6,2},{7,3},{8,12},{9,13},{10,... | collective-permute-start | bytes 442376 | tf_op jit(solution)/shard_map/ppermute | solution.py:57
  23.2 1.5 %collective-permute-start.4 = (bf16[576,256]{1,0:T(8,128)(2,1)S(1)}, bf16[576,256]{1,0:T(8,128)(2,1)S(1)}, u32[]{:S(2)}, u32[]{:S(2)}) collective-permute-start(bf16[576,256]{1,0:T(8,128)(2,1)S(1)} %collective-permute-done.3.refs_1_), channel_id=1, source_target_pairs={{0,2},{1,3},{2,0},{3,1},{4,6},{5,7},{6,4},{7,5},{8,10},{9,11},{10,... | collective-permute-start | bytes 884744 | tf_op jit(solution)/shard_map/ppermute | solution.py:57
  24.7 1.6 %collective-permute-start.1 = (bf16[256,128]{1,0:T(8,128)(2,1)S(1)}, bf16[256,128]{1,0:T(8,128)(2,1)S(1)}, u32[]{:S(2)}, u32[]{:S(2)}) collective-permute-start(bf16[256,128]{1,0:T(8,128)(2,1)S(1)} %pair_sum.1), channel_id=1, source_target_pairs={{0,16},{8,24},{16,0},{24,8},{1,17},{9,25},{17,1},{25,9},{2,18},{10... | collective-permute-start | bytes 196616 | tf_op jit(solution)/shard_map/ppermute | solution.py:57
  26.5 2.6 %collective-permute-done.1.z2_ref = bf16[256,128]{1,0:T(8,128)(2,1)S(1)} collective-permute-done((bf16[256,128]{1,0:T(8,128)(2,1)S(1)}, bf16[256,128]{1,0:T(8,128)(2,1)S(1)}, u32[]{:S(2)}, u32[]{:S(2)}) %collective-permute-start.1) | collective-permute-done | bytes 65568 | tf_op jit(solution)/shard_map/ppermute | solution.py:57
  29.7 3.3 %all-to-all-start.1 = ((bf16[8,32,128]{2,1,0:T(8,128)(2,1)}), bf16[8,32,128]{2,1,0:T(8,128)(2,1)S(1)}, u32[]{:S(2)}, u32[]{:S(2)}) async-start(bf16[8,32,128]{2,1,0:T(8,128)(2,1)} %share_sum.1), calls=%async_computation.1 | async-start | bytes 131072 | tf_op jit(solution)/shard_map/all_to_all | solution.py:46
  33.9 2.1 %collective-permute-done.4.refs_3_ = bf16[576,256]{1,0:T(8,128)(2,1)S(1)} collective-permute-done((bf16[576,256]{1,0:T(8,128)(2,1)S(1)}, bf16[576,256]{1,0:T(8,128)(2,1)S(1)}, u32[]{:S(2)}, u32[]{:S(2)}) %collective-permute-start.4) | collective-permute-done | bytes 294944 | tf_op jit(solution)/shard_map/ppermute | solution.py:57
  36.0 3.9 %all-to-all-done.1.share_ref = bf16[8,32,128]{2,1,0:T(8,128)(2,1)S(1)} async-done(((bf16[8,32,128]{2,1,0:T(8,128)(2,1)}), bf16[8,32,128]{2,1,0:T(8,128)(2,1)S(1)}, u32[]{:S(2)}, u32[]{:S(2)}) %all-to-all-start.1) | async-done | bytes 65568 | tf_op jit(solution)/shard_map/all_to_all | solution.py:46
  40.0 1.5 %collective-permute-start.8 = (bf16[9,32,128]{2,1,0:T(8,128)(2,1)S(1)}, bf16[9,32,128]{2,1,0:T(8,128)(2,1)S(1)}, u32[]{:S(2)}, u32[]{:S(2)}) collective-permute-start(bf16[9,32,128]{2,1,0:T(8,128)(2,1)S(1)} %pack_shares.1.refs_0_), channel_id=1, source_target_pairs={{0,16},{8,24},{16,0},{24,8},{1,17},{9,25},{17,1},{25,9},{2,18},{10... | collective-permute-start | bytes 221192 | tf_op jit(solution)/shard_map/ppermute | solution.py:57
  41.5 2.8 %collective-permute-done.8.refs_2_ = bf16[9,32,128]{2,1,0:T(8,128)(2,1)S(1)} collective-permute-done((bf16[9,32,128]{2,1,0:T(8,128)(2,1)S(1)}, bf16[9,32,128]{2,1,0:T(8,128)(2,1)S(1)}, u32[]{:S(2)}, u32[]{:S(2)}) %collective-permute-start.8) | collective-permute-done | bytes 73760 | tf_op jit(solution)/shard_map/ppermute | solution.py:57
  47.0 3.4 %attention.1 = (bf16[17,16,128]{2,1,0:T(8,128)(2,1)S(1)}, bf16[17,16,128]{2,1,0:T(8,128)(2,1)S(1)}) custom-call(bf16[9,32,128]{2,1,0:T(8,128)(2,1)S(1)} %pack_shares.1.refs_0_, bf16[9,32,128]{2,1,0:T(8,128)(2,1)S(1)} %collective-permute-done.7.refs_1_, bf16[9,32,128]{2,1,0:T(8,128)(2,1)S(1)} %collective-permute-done.8.refs_2_, ...), custom_call_target="tpu_custom_call" | custom-call | tf_op jit(solution)/shard_map/attention/pallas_call | solution.py:34
  52.3 1.3 %collective-permute-done.10.pair_ref = bf16[17,16,128]{2,1,0:T(8,128)(2,1)S(1)} collective-permute-done((bf16[17,16,128]{2,1,0:T(8,128)(2,1)S(1)}, bf16[17,16,128]{2,1,0:T(8,128)(2,1)S(1)}, u32[]{:S(2)}, u32[]{:S(2)}) %collective-permute-start.10) | collective-permute-done | bytes 69664 | tf_op jit(solution)/shard_map/ppermute | solution.py:57
  53.7 1.5 %collective-permute-start.11 = (bf16[17,16,128]{2,1,0:T(8,128)(2,1)S(1)}, bf16[17,16,128]{2,1,0:T(8,128)(2,1)S(1)}, u32[]{:S(2)}, u32[]{:S(2)}) collective-permute-start(bf16[17,16,128]{2,1,0:T(8,128)(2,1)S(1)} %pair_terms.1.own_ref), channel_id=1, source_target_pairs={{0,16},{8,24},{16,0},{24,8},{1,17},{9,25},{17,1},{25,9},{2,18},{10... | collective-permute-start | bytes 208904 | tf_op jit(solution)/shard_map/ppermute | solution.py:57
  55.2 2.8 %collective-permute-done.11.across_ref = bf16[17,16,128]{2,1,0:T(8,128)(2,1)S(1)} collective-permute-done((bf16[17,16,128]{2,1,0:T(8,128)(2,1)S(1)}, bf16[17,16,128]{2,1,0:T(8,128)(2,1)S(1)}, u32[]{:S(2)}, u32[]{:S(2)}) %collective-permute-start.11) | collective-permute-done | bytes 69664 | tf_op jit(solution)/shard_map/ppermute | solution.py:57
  58.3 1.2 %collective-permute-done.12.other_ref = bf16[16,16,128]{2,1,0:T(8,128)(2,1)S(1)} collective-permute-done((bf16[16,16,128]{2,1,0:T(8,128)(2,1)S(1)}, bf16[16,16,128]{2,1,0:T(8,128)(2,1)S(1)}, u32[]{:S(2)}, u32[]{:S(2)}) %collective-permute-start.12) | collective-permute-done | bytes 65568 | tf_op jit(solution)/shard_map/ppermute | solution.py:57
  60.6 1.1 collective-permute-start.18
  62.6 1.4 %collective-permute-done.18.refs_3_ = f32[32,128]{1,0:T(8,128)S(1)} collective-permute-done((f32[32,128]{1,0:T(8,128)S(1)}, f32[32,128]{1,0:T(8,128)S(1)}, u32[]{:S(2)}, u32[]{:S(2)}) %collective-permute-start.18) | collective-permute-done | bytes 16416 | tf_op jit(solution)/shard_map/ppermute | solution.py:57
  64.0 1.5 %collective-permute-done.17.refs_2_ = f32[32,128]{1,0:T(8,128)S(1)} collective-permute-done((f32[32,128]{1,0:T(8,128)S(1)}, f32[32,128]{1,0:T(8,128)S(1)}, u32[]{:S(2)}, u32[]{:S(2)}) %collective-permute-start.17) | collective-permute-done | bytes 16416 | tf_op jit(solution)/shard_map/ppermute | solution.py:57
  65.8 13.3 %all_to_all.20.ff_ref = bf16[8,144,128]{2,1,0:T(8,128)(2,1)S(1)} all-to-all(bf16[8,144,128]{2,1,0:T(8,128)(2,1)S(1)} %get-tuple-element.67), channel_id=1, replica_groups=mesh['gx'=4,'gy'=8] {'gy'}, dimensions={0} | all-to-all | bytes 589824 | tf_op jit(solution)/shard_map/all_to_all | solution.py:46
  82.4 1.4 %collective-permute-start.25 = (bf16[64,1024]{1,0:T(8,128)(2,1)S(1)}, bf16[64,1024]{1,0:T(8,128)(2,1)S(1)}, u32[]{:S(2)}, u32[]{:S(2)}) collective-permute-start(bf16[64,1024]{1,0:T(8,128)(2,1)S(1)} %pair_sum_ff.3), channel_id=1, source_target_pairs={{0,16},{8,24},{16,0},{24,8},{1,17},{9,25},{17,1},{25,9},{2,18},{10... | collective-permute-start | bytes 393224 | tf_op jit(solution)/shard_map/ppermute | solution.py:57
  83.8 4.9 %collective-permute-done.20.z2_ref = bf16[64,1280]{1,0:T(8,128)(2,1)S(1)} collective-permute-done((bf16[64,1280]{1,0:T(8,128)(2,1)S(1)}, bf16[64,1280]{1,0:T(8,128)(2,1)S(1)}, u32[]{:S(2)}, u32[]{:S(2)}) %collective-permute-start.20) | collective-permute-done | bytes 163872 | tf_op jit(solution)/shard_map/ppermute | solution.py:57
  89.6 1.8 %collective-permute-done.25.z2_ref = bf16[64,1024]{1,0:T(8,128)(2,1)S(1)} collective-permute-done((bf16[64,1024]{1,0:T(8,128)(2,1)S(1)}, bf16[64,1024]{1,0:T(8,128)(2,1)S(1)}, u32[]{:S(2)}, u32[]{:S(2)}) %collective-permute-start.25) | collective-permute-done | bytes 131104 | tf_op jit(solution)/shard_map/ppermute | solution.py:57
  92.2 1.7 %collective-permute-done.22.refs_2_ = bf16[64,640]{1,0:T(8,128)(2,1)S(1)} collective-permute-done((bf16[64,640]{1,0:T(8,128)(2,1)S(1)}, bf16[64,640]{1,0:T(8,128)(2,1)S(1)}, u32[]{:S(2)}, u32[]{:S(2)}) %collective-permute-start.22) | collective-permute-done | bytes 81952 | tf_op jit(solution)/shard_map/ppermute | solution.py:57
  94.4 1.4 %collective-permute-done.27.refs_6_ = bf16[64,512]{1,0:T(8,128)(2,1)S(1)} collective-permute-done((bf16[64,512]{1,0:T(8,128)(2,1)S(1)}, bf16[64,512]{1,0:T(8,128)(2,1)S(1)}, u32[]{:S(2)}, u32[]{:S(2)}) %collective-permute-start.27) | collective-permute-done | bytes 65568 | tf_op jit(solution)/shard_map/ppermute | solution.py:57
  95.8 1.2 %collective-permute-done.28.refs_7_ = bf16[64,512]{1,0:T(8,128)(2,1)S(1)} collective-permute-done((bf16[64,512]{1,0:T(8,128)(2,1)S(1)}, bf16[64,512]{1,0:T(8,128)(2,1)S(1)}, u32[]{:S(2)}, u32[]{:S(2)}) %collective-permute-start.28) | collective-permute-done | bytes 65568 | tf_op jit(solution)/shard_map/ppermute | solution.py:57
  97.8 13.3 %all_to_all.21.parts_ref = bf16[8,144,128]{2,1,0:T(8,128)(2,1)S(1)} all-to-all(bf16[8,144,128]{2,1,0:T(8,128)(2,1)S(1)} %project_down.1), channel_id=1, replica_groups=mesh['gx'=4,'gy'=8] {'gy'}, dimensions={0} | all-to-all | bytes 589824 | tf_op jit(solution)/shard_map/all_to_all | solution.py:46
  112.1 1.1 collective-permute-start.29
  113.2 1.3 %collective-permute-done.31.refs_3_ = f32[32,128]{1,0:T(8,128)S(1)} collective-permute-done((f32[32,128]{1,0:T(8,128)S(1)}, f32[32,128]{1,0:T(8,128)S(1)}, u32[]{:S(2)}, u32[]{:S(2)}) %collective-permute-start.31) | collective-permute-done | bytes 16416 | tf_op jit(solution)/shard_map/ppermute | solution.py:57
  (91 shorter events, 19.5 us)
Async XLA Ops:
  1.7 18.5 %all-to-all-start = ((bf16[8,144,128]{2,1,0:T(8,128)(2,1)}), bf16[8,144,128]{2,1,0:T(8,128)(2,1)S(1)}, u32[]{:S(2)}, u32[]{:S(2)}) async-start(bf16[8,144,128]{2,1,0:T(8,128)(2,1)} %get-tuple-element.42), calls=%async_computation | async-start | bytes 589824 | tf_op jit(solution)/shard_map/all_to_all | solution.py:46
  9.1 12.3 %collective-permute-start.3 = (bf16[576,256]{1,0:T(8,128)(2,1)S(1)}, bf16[576,256]{1,0:T(8,128)(2,1)S(1)}, u32[]{:S(2)}, u32[]{:S(2)}) collective-permute-start(bf16[576,256]{1,0:T(8,128)(2,1)S(1)} %bitcast.7), channel_id=1, source_target_pairs={{0,1},{1,0},{2,3},{3,2},{4,5},{5,4},{6,7},{7,6},{8,9},{9,8},{10,11... | collective-permute-start | bytes 884744 | tf_op jit(solution)/shard_map/ppermute | solution.py:57
  11.2 22.7 %collective-permute-start.2 = (bf16[576,256]{1,0:T(8,128)(2,1)S(1)}, bf16[576,256]{1,0:T(8,128)(2,1)S(1)}, u32[]{:S(2)}, u32[]{:S(2)}) collective-permute-start(bf16[576,256]{1,0:T(8,128)(2,1)S(1)} %bitcast.8), channel_id=1, source_target_pairs={{0,2},{1,3},{2,0},{3,1},{4,6},{5,7},{6,4},{7,5},{8,10},{9,11},{10,... | collective-permute-start | bytes 884744 | tf_op jit(solution)/shard_map/ppermute | solution.py:57
  12.6 20.4 %collective-permute-start.5 = (bf16[288,256]{1,0:T(8,128)(2,1)S(1)}, bf16[288,256]{1,0:T(8,128)(2,1)S(1)}, u32[]{:S(2)}, u32[]{:S(2)}) collective-permute-start(bf16[288,256]{1,0:T(8,128)(2,1)S(1)} %get-tuple-element.77), channel_id=1, source_target_pairs={{0,4},{1,5},{2,6},{3,7},{4,0},{5,1},{6,2},{7,3},{8,12},{9,13},{10,... | collective-permute-start | bytes 442376 | tf_op jit(solution)/shard_map/ppermute | solution.py:57
  20.6 4.1 %collective-permute-start = (bf16[2,256,128]{2,1,0:T(8,128)(2,1)S(1)}, bf16[2,256,128]{2,1,0:T(8,128)(2,1)S(1)}, u32[]{:S(2)}, u32[]{:S(2)}) collective-permute-start(bf16[2,256,128]{2,1,0:T(8,128)(2,1)S(1)} %get-tuple-element.44), channel_id=1, source_target_pairs={{0,8},{8,0},{16,24},{24,16},{1,9},{9,1},{17,25},{25,17},{2,10},{10... | collective-permute-start | bytes 393224 | tf_op jit(solution)/shard_map/ppermute | solution.py:57
  21.4 12.5 %collective-permute-start.6 = (bf16[288,256]{1,0:T(8,128)(2,1)S(1)}, bf16[288,256]{1,0:T(8,128)(2,1)S(1)}, u32[]{:S(2)}, u32[]{:S(2)}) collective-permute-start(bf16[288,256]{1,0:T(8,128)(2,1)S(1)} %get-tuple-element.54), channel_id=1, source_target_pairs={{0,4},{1,5},{2,6},{3,7},{4,0},{5,1},{6,2},{7,3},{8,12},{9,13},{10,... | collective-permute-start | bytes 442376 | tf_op jit(solution)/shard_map/ppermute | solution.py:57
  23.2 12.8 %collective-permute-start.4 = (bf16[576,256]{1,0:T(8,128)(2,1)S(1)}, bf16[576,256]{1,0:T(8,128)(2,1)S(1)}, u32[]{:S(2)}, u32[]{:S(2)}) collective-permute-start(bf16[576,256]{1,0:T(8,128)(2,1)S(1)} %collective-permute-done.3.refs_1_), channel_id=1, source_target_pairs={{0,2},{1,3},{2,0},{3,1},{4,6},{5,7},{6,4},{7,5},{8,10},{9,11},{10,... | collective-permute-start | bytes 884744 | tf_op jit(solution)/shard_map/ppermute | solution.py:57
  24.7 4.3 %collective-permute-start.1 = (bf16[256,128]{1,0:T(8,128)(2,1)S(1)}, bf16[256,128]{1,0:T(8,128)(2,1)S(1)}, u32[]{:S(2)}, u32[]{:S(2)}) collective-permute-start(bf16[256,128]{1,0:T(8,128)(2,1)S(1)} %pair_sum.1), channel_id=1, source_target_pairs={{0,16},{8,24},{16,0},{24,8},{1,17},{9,25},{17,1},{25,9},{2,18},{10... | collective-permute-start | bytes 196616 | tf_op jit(solution)/shard_map/ppermute | solution.py:57
  29.7 10.2 %all-to-all-start.1 = ((bf16[8,32,128]{2,1,0:T(8,128)(2,1)}), bf16[8,32,128]{2,1,0:T(8,128)(2,1)S(1)}, u32[]{:S(2)}, u32[]{:S(2)}) async-start(bf16[8,32,128]{2,1,0:T(8,128)(2,1)} %share_sum.1), calls=%async_computation.1 | async-start | bytes 131072 | tf_op jit(solution)/shard_map/all_to_all | solution.py:46
  40.0 4.4 %collective-permute-start.8 = (bf16[9,32,128]{2,1,0:T(8,128)(2,1)S(1)}, bf16[9,32,128]{2,1,0:T(8,128)(2,1)S(1)}, u32[]{:S(2)}, u32[]{:S(2)}) collective-permute-start(bf16[9,32,128]{2,1,0:T(8,128)(2,1)S(1)} %pack_shares.1.refs_0_), channel_id=1, source_target_pairs={{0,16},{8,24},{16,0},{24,8},{1,17},{9,25},{17,1},{25,9},{2,18},{10... | collective-permute-start | bytes 221192 | tf_op jit(solution)/shard_map/ppermute | solution.py:57
  44.4 6.7 %collective-permute-start.14 = (bf16[576,256]{1,0:T(8,128)(2,1)S(1)}, bf16[576,256]{1,0:T(8,128)(2,1)S(1)}, u32[]{:S(2)}, u32[]{:S(2)}) collective-permute-start(bf16[576,256]{1,0:T(8,128)(2,1)S(1)} %constant_dynamic-update-slice_fusion.refs_4_), channel_id=1, source_target_pairs={{0,2},{1,3},{2,0},{3,1},{4,6},{5,7},{6,4},{7,5},{8,10},{9,11},{10,... | collective-permute-start | bytes 884744 | tf_op jit(solution)/shard_map/ppermute | solution.py:57
  44.6 6.7 %collective-permute-start.13 = (bf16[576,256]{1,0:T(8,128)(2,1)S(1)}, bf16[576,256]{1,0:T(8,128)(2,1)S(1)}, u32[]{:S(2)}, u32[]{:S(2)}) collective-permute-start(bf16[576,256]{1,0:T(8,128)(2,1)S(1)} %constant_dynamic-update-slice_fusion.refs_4_), channel_id=1, source_target_pairs={{0,1},{1,0},{2,3},{3,2},{4,5},{5,4},{6,7},{7,6},{8,9},{9,8},{10,11... | collective-permute-start | bytes 884744 | tf_op jit(solution)/shard_map/ppermute | solution.py:57
  45.6 1.3 %collective-permute-start.7 = (bf16[9,32,128]{2,1,0:T(8,128)(2,1)S(1)}, bf16[9,32,128]{2,1,0:T(8,128)(2,1)S(1)}, u32[]{:S(2)}, u32[]{:S(2)}) collective-permute-start(bf16[9,32,128]{2,1,0:T(8,128)(2,1)S(1)} %pack_shares.1.refs_0_), channel_id=1, source_target_pairs={{0,8},{8,0},{16,24},{24,16},{1,9},{9,1},{17,25},{25,17},{2,10},{10... | collective-permute-start | bytes 221192 | tf_op jit(solution)/shard_map/ppermute | solution.py:57
  45.6 1.4 %collective-permute-start.9 = (bf16[9,32,128]{2,1,0:T(8,128)(2,1)S(1)}, bf16[9,32,128]{2,1,0:T(8,128)(2,1)S(1)}, u32[]{:S(2)}, u32[]{:S(2)}) collective-permute-start(bf16[9,32,128]{2,1,0:T(8,128)(2,1)S(1)} %collective-permute-done.8.refs_2_), channel_id=1, source_target_pairs={{0,8},{8,0},{16,24},{24,16},{1,9},{9,1},{17,25},{25,17},{2,10},{10... | collective-permute-start | bytes 221192 | tf_op jit(solution)/shard_map/ppermute | solution.py:57
  51.3 8.5 %collective-permute-start.15 = (bf16[576,256]{1,0:T(8,128)(2,1)S(1)}, bf16[576,256]{1,0:T(8,128)(2,1)S(1)}, u32[]{:S(2)}, u32[]{:S(2)}) collective-permute-start(bf16[576,256]{1,0:T(8,128)(2,1)S(1)} %collective-permute-done.14.refs_6_), channel_id=1, source_target_pairs={{0,1},{1,0},{2,3},{3,2},{4,5},{5,4},{6,7},{7,6},{8,9},{9,8},{10,11... | collective-permute-start | bytes 884744 | tf_op jit(solution)/shard_map/ppermute | solution.py:57
  53.7 4.3 %collective-permute-start.11 = (bf16[17,16,128]{2,1,0:T(8,128)(2,1)S(1)}, bf16[17,16,128]{2,1,0:T(8,128)(2,1)S(1)}, u32[]{:S(2)}, u32[]{:S(2)}) collective-permute-start(bf16[17,16,128]{2,1,0:T(8,128)(2,1)S(1)} %pair_terms.1.own_ref), channel_id=1, source_target_pairs={{0,16},{8,24},{16,0},{24,8},{1,17},{9,25},{17,1},{25,9},{2,18},{10... | collective-permute-start | bytes 208904 | tf_op jit(solution)/shard_map/ppermute | solution.py:57
  58.2 1.3 %collective-permute-start.12 = (bf16[16,16,128]{2,1,0:T(8,128)(2,1)S(1)}, bf16[16,16,128]{2,1,0:T(8,128)(2,1)S(1)}, u32[]{:S(2)}, u32[]{:S(2)}) collective-permute-start(bf16[16,16,128]{2,1,0:T(8,128)(2,1)S(1)} %divide.1.own_ref), channel_id=1, source_target_pairs={{0,8},{8,0},{16,24},{24,16},{1,9},{9,1},{17,25},{25,17},{2,10},{10... | collective-permute-start | bytes 196616 | tf_op jit(solution)/shard_map/ppermute | solution.py:57
  60.6 3.3 %collective-permute-start.18 = (f32[32,128]{1,0:T(8,128)S(1)}, f32[32,128]{1,0:T(8,128)S(1)}, u32[]{:S(2)}, u32[]{:S(2)}) collective-permute-start(f32[32,128]{1,0:T(8,128)S(1)} %get-tuple-element.65.refs_0_), channel_id=1, source_target_pairs={{0,24},{8,16},{16,8},{24,0},{1,25},{9,17},{17,9},{25,1},{2,26},{10... | collective-permute-start | bytes 49160 | tf_op jit(solution)/shard_map/ppermute | solution.py:57
  61.7 3.7 %collective-permute-start.17 = (f32[32,128]{1,0:T(8,128)S(1)}, f32[32,128]{1,0:T(8,128)S(1)}, u32[]{:S(2)}, u32[]{:S(2)}) collective-permute-start(f32[32,128]{1,0:T(8,128)S(1)} %get-tuple-element.65.refs_0_), channel_id=1, source_target_pairs={{0,16},{8,24},{16,0},{24,8},{1,17},{9,25},{17,1},{25,9},{2,18},{10... | collective-permute-start | bytes 49160 | tf_op jit(solution)/shard_map/ppermute | solution.py:57
  62.3 3.2 %collective-permute-start.16 = (f32[32,128]{1,0:T(8,128)S(1)}, f32[32,128]{1,0:T(8,128)S(1)}, u32[]{:S(2)}, u32[]{:S(2)}) collective-permute-start(f32[32,128]{1,0:T(8,128)S(1)} %get-tuple-element.65.refs_0_), channel_id=1, source_target_pairs={{0,8},{8,0},{16,24},{24,16},{1,9},{9,1},{17,25},{25,17},{2,10},{10... | collective-permute-start | bytes 49160 | tf_op jit(solution)/shard_map/ppermute | solution.py:57
  79.9 1.7 %collective-permute-start.19 = (bf16[2,64,1280]{2,1,0:T(8,128)(2,1)S(1)}, bf16[2,64,1280]{2,1,0:T(8,128)(2,1)S(1)}, u32[]{:S(2)}, u32[]{:S(2)}) collective-permute-start(bf16[2,64,1280]{2,1,0:T(8,128)(2,1)S(1)} %get-tuple-element.69), channel_id=1, source_target_pairs={{0,8},{8,0},{16,24},{24,16},{1,9},{9,1},{17,25},{25,17},{2,10},{10... | collective-permute-start | bytes 983048 | tf_op jit(solution)/shard_map/ppermute | solution.py:57
  80.5 1.8 %collective-permute-start.24 = (bf16[2,64,1024]{2,1,0:T(8,128)(2,1)S(1)}, bf16[2,64,1024]{2,1,0:T(8,128)(2,1)S(1)}, u32[]{:S(2)}, u32[]{:S(2)}) collective-permute-start(bf16[2,64,1024]{2,1,0:T(8,128)(2,1)S(1)} %get-tuple-element.72), channel_id=1, source_target_pairs={{0,8},{8,0},{16,24},{24,16},{1,9},{9,1},{17,25},{25,17},{2,10},{10... | collective-permute-start | bytes 786440 | tf_op jit(solution)/shard_map/ppermute | solution.py:57
  81.6 7.1 %collective-permute-start.20 = (bf16[64,1280]{1,0:T(8,128)(2,1)S(1)}, bf16[64,1280]{1,0:T(8,128)(2,1)S(1)}, u32[]{:S(2)}, u32[]{:S(2)}) collective-permute-start(bf16[64,1280]{1,0:T(8,128)(2,1)S(1)} %pair_sum_ff.2), channel_id=1, source_target_pairs={{0,16},{8,24},{16,0},{24,8},{1,17},{9,25},{17,1},{25,9},{2,18},{10... | collective-permute-start | bytes 491528 | tf_op jit(solution)/shard_map/ppermute | solution.py:57
  82.4 9.0 %collective-permute-start.25 = (bf16[64,1024]{1,0:T(8,128)(2,1)S(1)}, bf16[64,1024]{1,0:T(8,128)(2,1)S(1)}, u32[]{:S(2)}, u32[]{:S(2)}) collective-permute-start(bf16[64,1024]{1,0:T(8,128)(2,1)S(1)} %pair_sum_ff.3), channel_id=1, source_target_pairs={{0,16},{8,24},{16,0},{24,8},{1,17},{9,25},{17,1},{25,9},{2,18},{10... | collective-permute-start | bytes 393224 | tf_op jit(solution)/shard_map/ppermute | solution.py:57
  88.8 5.1 %collective-permute-start.22 = (bf16[64,640]{1,0:T(8,128)(2,1)S(1)}, bf16[64,640]{1,0:T(8,128)(2,1)S(1)}, u32[]{:S(2)}, u32[]{:S(2)}) collective-permute-start(bf16[64,640]{1,0:T(8,128)(2,1)S(1)} %activate.2.refs_0_), channel_id=1, source_target_pairs={{0,16},{8,24},{16,0},{24,8},{1,17},{9,25},{17,1},{25,9},{2,18},{10... | collective-permute-start | bytes 245768 | tf_op jit(solution)/shard_map/ppermute | solution.py:57
  91.5 4.3 %collective-permute-start.27 = (bf16[64,512]{1,0:T(8,128)(2,1)S(1)}, bf16[64,512]{1,0:T(8,128)(2,1)S(1)}, u32[]{:S(2)}, u32[]{:S(2)}) collective-permute-start(bf16[64,512]{1,0:T(8,128)(2,1)S(1)} %activate.3.refs_4_), channel_id=1, source_target_pairs={{0,16},{8,24},{16,0},{24,8},{1,17},{9,25},{17,1},{25,9},{2,18},{10... | collective-permute-start | bytes 196616 | tf_op jit(solution)/shard_map/ppermute | solution.py:57
  92.2 4.8 %collective-permute-start.21 = (bf16[64,640]{1,0:T(8,128)(2,1)S(1)}, bf16[64,640]{1,0:T(8,128)(2,1)S(1)}, u32[]{:S(2)}, u32[]{:S(2)}) collective-permute-start(bf16[64,640]{1,0:T(8,128)(2,1)S(1)} %activate.2.refs_0_), channel_id=1, source_target_pairs={{0,8},{8,0},{16,24},{24,16},{1,9},{9,1},{17,25},{25,17},{2,10},{10... | collective-permute-start | bytes 245768 | tf_op jit(solution)/shard_map/ppermute | solution.py:57
  93.9 3.2 %collective-permute-start.23 = (bf16[64,640]{1,0:T(8,128)(2,1)S(1)}, bf16[64,640]{1,0:T(8,128)(2,1)S(1)}, u32[]{:S(2)}, u32[]{:S(2)}) collective-permute-start(bf16[64,640]{1,0:T(8,128)(2,1)S(1)} %collective-permute-done.22.refs_2_), channel_id=1, source_target_pairs={{0,8},{8,0},{16,24},{24,16},{1,9},{9,1},{17,25},{25,17},{2,10},{10... | collective-permute-start | bytes 245768 | tf_op jit(solution)/shard_map/ppermute | solution.py:57
  93.9 1.9 %collective-permute-start.26 = (bf16[64,512]{1,0:T(8,128)(2,1)S(1)}, bf16[64,512]{1,0:T(8,128)(2,1)S(1)}, u32[]{:S(2)}, u32[]{:S(2)}) collective-permute-start(bf16[64,512]{1,0:T(8,128)(2,1)S(1)} %activate.3.refs_4_), channel_id=1, source_target_pairs={{0,8},{8,0},{16,24},{24,16},{1,9},{9,1},{17,25},{25,17},{2,10},{10... | collective-permute-start | bytes 196616 | tf_op jit(solution)/shard_map/ppermute | solution.py:57
  111.3 3.2 %collective-permute-start.31 = (f32[32,128]{1,0:T(8,128)S(1)}, f32[32,128]{1,0:T(8,128)S(1)}, u32[]{:S(2)}, u32[]{:S(2)}) collective-permute-start(f32[32,128]{1,0:T(8,128)S(1)} %get-tuple-element.74.refs_0_), channel_id=1, source_target_pairs={{0,24},{8,16},{16,8},{24,0},{1,25},{9,17},{17,9},{25,1},{2,26},{10... | collective-permute-start | bytes 49160 | tf_op jit(solution)/shard_map/ppermute | solution.py:57
  111.3 3.8 %collective-permute-start.30 = (f32[32,128]{1,0:T(8,128)S(1)}, f32[32,128]{1,0:T(8,128)S(1)}, u32[]{:S(2)}, u32[]{:S(2)}) collective-permute-start(f32[32,128]{1,0:T(8,128)S(1)} %get-tuple-element.74.refs_0_), channel_id=1, source_target_pairs={{0,16},{8,24},{16,0},{24,8},{1,17},{9,25},{17,1},{25,9},{2,18},{10... | collective-permute-start | bytes 49160 | tf_op jit(solution)/shard_map/ppermute | solution.py:57
  112.1 3.1 %collective-permute-start.29 = (f32[32,128]{1,0:T(8,128)S(1)}, f32[32,128]{1,0:T(8,128)S(1)}, u32[]{:S(2)}, u32[]{:S(2)}) collective-permute-start(f32[32,128]{1,0:T(8,128)S(1)} %get-tuple-element.74.refs_0_), channel_id=1, source_target_pairs={{0,8},{8,0},{16,24},{24,16},{1,9},{9,1},{17,25},{25,17},{2,10},{10... | collective-permute-start | bytes 49160 | tf_op jit(solution)/shard_map/ppermute | solution.py:57
  (15 other events, 211.9 us)

commit v11 on v10

--- a/solution.py
+++ b/solution.py
@@ -137,6 +137,7 @@
         (table, lengths, parents),
         scratch=[pltpu.SMEM((slots + 1,), jnp.int32)],
         specs={0: IN_SMEM, 1: IN_SMEM, 2: IN_SMEM},
+        micros=5,
     )
 
 
@@ -287,26 +288,28 @@
         out_ref[...] = total.reshape(ny, rows, HALF).astype(BF)
 
     (shares,) = run("share_sum", share_sum, [((ny, rows, HALF), BF)], (z0, z13, z2))
-    shares, *late = lax.optimization_barrier((shares, block_table, lengths, parents))
+    late = block_table, lengths, parents
+    late, _ = lax.optimization_barrier((late, (shares, w_blocks[2], w_blocks[3])))
     cos, sin = rope_tables(late[1], rows, steps)
     tables = make_tables(*late, cache_pool.shape[1], rows, steps)
+    w_blocks[4] = jnp.concatenate([w_first, w_second], axis=0)
+    late, _ = lax.optimization_barrier((w_blocks[4], tables))
+    w_blocks[6] = permute(late, "gy", 2)
+    w_blocks[5] = permute(late, "gy", 1)
     shares = exchange(shares, "gy")
-    beside = tables, cos, sin, w_blocks[2], w_blocks[3], w_first, w_second
-    shares, (tables, cos, sin, *_) = lax.optimization_barrier((shares, beside))
+    shares, tables, cos, sin = lax.optimization_barrier((shares, tables, cos, sin))
 
     def pack_shares(share_ref, x_ref, out_ref):
         x = x_ref[...].astype(F32)
         out_ref[0:ny] = share_ref[...]
         out_ref[ny] = high_low(row_sum(x * x), HALF).astype(BF)
 
-    (shares,) = run(
-        "pack_shares", pack_shares, [((ny + 1, rows, HALF), BF)], (shares, x_own), micros=5
-    )
-    shares = gather_gx(shares)
-    w_blocks[4] = jnp.concatenate([w_first, w_second], axis=0)
-    w_late, _ = lax.optimization_barrier((w_blocks[4], shares[2]))
-    w_blocks[6] = permute(w_late, "gy", 2)
-    w_blocks[5] = permute(w_late, "gy", 1)
+    (shares,) = run("pack_shares", pack_shares, [((ny + 1, rows, HALF), BF)], (shares, x_own))
+    near, across = permute(shares, "gx", 1), permute(shares, "gx", 2)
+    across, _ = lax.optimization_barrier((across, (w_blocks[6], w_blocks[5])))
+    shares = [shares, near, across, permute(across, "gx", 1)]
+    late, _ = lax.optimization_barrier((w_blocks[6], near))
+    w_blocks[7] = permute(late, "gy", 1)
 
     def attention(*refs):
         a_refs, tables, pool_ref, outs = refs[:nx], refs[nx : nx + 4], refs[nx + 4], refs[nx + 5 :]
@@ -355,8 +358,6 @@
         limit=24,
         specs={nx + 4: IN_HBM},
     )
-    w_late, _ = lax.optimization_barrier((w_blocks, own))
-    w_blocks[7] = permute(w_late[6], "gy", 1)
     pair = permute(pair, "gx", 1)
 
     def pair_terms(own_ref, pair_ref, out_ref):
@@ -369,6 +370,7 @@
 
     (own,) = run("pair_terms", pair_terms, [(shape, BF)], (own, pair))
     across = permute(own, "gx", 2)
+    across, _ = lax.optimization_barrier((across, w_blocks[7]))
 
     def divide(own_ref, across_ref, out_ref):
         total = own_ref[...].astype(F32) + across_ref[...].astype(F32)

time: 116 us -> 126 us (1.086)
  waiting for transfers between devices: 40.1 us -> 44.1 us
  local copies, waits for them, and re-layouts: 0.94 us -> 3.41 us
  starting transfers between devices: 36.1 us -> 38.4 us
    ppermute x32, waiting for transfers between devices: 31.2 us -> 36.8 us  [permute(): return lax.ppermute(values, axis, [(i, i ^ m) for i in range(count)])]
    unnamed x27 -> x25, local copies, waits for them, and re-layouts: 0.9 us -> 3.38 us
    ppermute x32, starting transfers between devices: 25.4 us -> 27.6 us  [permute(): return lax.ppermute(values, axis, [(i, i ^ m) for i in range(count)])]
    all_to_all x2, waiting for transfers between devices: 8.95 us -> 7.28 us  [exchange(): return lax.all_to_all(values, axes, split_axis=0, concat_axis=0, tiled=True)]
  transfers between devices with their start and end apart: 34 -> 34, of which waited for: 23 -> 21; matrix products, arithmetic and copies ran while one was open for 0% -> 0% of each run, Pallas kernels for 6% -> 5%
where the time goes in v11:
time: 126 us
  waiting for transfers between devices  44.1 us (35%)
  starting transfers between devices  38.4 us (30%)
  blocking collectives  27.7 us (22%)
  Pallas kernels  10.9 us (9%)
  local copies, waits for them, and re-layouts  3.41 us (3%)
    ppermute x32, waiting for transfers between devices, permute(): return lax.ppermute(values, axis, [(i, i ^ m) for i in range(count)])  36.8 us
    all_to_all x2, blocking collectives, exchange(): return lax.all_to_all(values, axes, split_axis=0, concat_axis=0, tiled=True)  27.7 us
    ppermute x32, starting transfers between devices, permute(): return lax.ppermute(values, axis, [(i, i ^ m) for i in range(count)])  27.6 us
    pallas_call x20, Pallas kernels, run(): pl.pallas_call(kernel, out_shape=[jax.ShapeDtypeStruct(s, d) for s, d in...  10.9 us
    all_to_all x2, starting transfers between devices, exchange(): return lax.all_to_all(values, axes, split_axis=0, concat_axis=0, tiled=True)  10.7 us
    all_to_all x2, waiting for transfers between devices, exchange(): return lax.all_to_all(values, axes, split_axis=0, concat_axis=0, tiled=True)  7.28 us
    unnamed x25, local copies, waits for them, and re-layouts  3.38 us
  transfers between devices with their start and end apart: 34, of which 21 were waited for; matrix products, arithmetic and copies ran while one was open for 0% of the time, Pallas kernels for 5%

profile of v11, /device:TPU:0, one launch (start us, length us, event | category | flops | bytes accessed | tf_op | source)
XLA Modules:
  0.0 125.5 jit_solution(8648021863966030346)
XLA Ops:
  1.7 7.4 %all-to-all-start = ((bf16[8,144,128]{2,1,0:T(8,128)(2,1)}), bf16[8,144,128]{2,1,0:T(8,128)(2,1)S(1)}, u32[]{:S(2)}, u32[]{:S(2)}) async-start(bf16[8,144,128]{2,1,0:T(8,128)(2,1)} %get-tuple-element.43), calls=%async_computation | async-start | bytes 589824 | tf_op jit(solution)/shard_map/all_to_all | solution.py:46
  9.1 2.1 %collective-permute-start.3 = (bf16[576,256]{1,0:T(8,128)(2,1)S(1)}, bf16[576,256]{1,0:T(8,128)(2,1)S(1)}, u32[]{:S(2)}, u32[]{:S(2)}) collective-permute-start(bf16[576,256]{1,0:T(8,128)(2,1)S(1)} %bitcast.5), channel_id=1, source_target_pairs={{0,1},{1,0},{2,3},{3,2},{4,5},{5,4},{6,7},{7,6},{8,9},{9,8},{10,11... | collective-permute-start | bytes 884744 | tf_op jit(solution)/shard_map/ppermute | solution.py:57
  11.1 1.5 %collective-permute-start.2 = (bf16[576,256]{1,0:T(8,128)(2,1)S(1)}, bf16[576,256]{1,0:T(8,128)(2,1)S(1)}, u32[]{:S(2)}, u32[]{:S(2)}) collective-permute-start(bf16[576,256]{1,0:T(8,128)(2,1)S(1)} %bitcast.6), channel_id=1, source_target_pairs={{0,2},{1,3},{2,0},{3,1},{4,6},{5,7},{6,4},{7,5},{8,10},{9,11},{10,... | collective-permute-start | bytes 884744 | tf_op jit(solution)/shard_map/ppermute | solution.py:57
  12.6 2.4 %collective-permute-start.7 = (bf16[288,256]{1,0:T(8,128)(2,1)S(1)}, bf16[288,256]{1,0:T(8,128)(2,1)S(1)}, u32[]{:S(2)}, u32[]{:S(2)}) collective-permute-start(bf16[288,256]{1,0:T(8,128)(2,1)S(1)} %get-tuple-element.79), channel_id=1, source_target_pairs={{0,4},{1,5},{2,6},{3,7},{4,0},{5,1},{6,2},{7,3},{8,12},{9,13},{10,... | collective-permute-start | bytes 442376 | tf_op jit(solution)/shard_map/ppermute | solution.py:57
  15.7 4.4 %all-to-all-done.x_ref = bf16[8,144,128]{2,1,0:T(8,128)(2,1)S(1)} async-done(((bf16[8,144,128]{2,1,0:T(8,128)(2,1)}), bf16[8,144,128]{2,1,0:T(8,128)(2,1)S(1)}, u32[]{:S(2)}, u32[]{:S(2)}) %all-to-all-start) | async-done | bytes 294944 | tf_op jit(solution)/shard_map/all_to_all | solution.py:46
  20.9 2.4 %collective-permute-start.8 = (bf16[288,256]{1,0:T(8,128)(2,1)S(1)}, bf16[288,256]{1,0:T(8,128)(2,1)S(1)}, u32[]{:S(2)}, u32[]{:S(2)}) collective-permute-start(bf16[288,256]{1,0:T(8,128)(2,1)S(1)} %get-tuple-element.56), channel_id=1, source_target_pairs={{0,4},{1,5},{2,6},{3,7},{4,0},{5,1},{6,2},{7,3},{8,12},{9,13},{10,... | collective-permute-start | bytes 442376 | tf_op jit(solution)/shard_map/ppermute | solution.py:57
  23.2 1.5 %collective-permute-start.4 = (bf16[576,256]{1,0:T(8,128)(2,1)S(1)}, bf16[576,256]{1,0:T(8,128)(2,1)S(1)}, u32[]{:S(2)}, u32[]{:S(2)}) collective-permute-start(bf16[576,256]{1,0:T(8,128)(2,1)S(1)} %collective-permute-done.3.refs_1_), channel_id=1, source_target_pairs={{0,2},{1,3},{2,0},{3,1},{4,6},{5,7},{6,4},{7,5},{8,10},{9,11},{10,... | collective-permute-start | bytes 884744 | tf_op jit(solution)/shard_map/ppermute | solution.py:57
  24.8 1.6 %collective-permute-start.1 = (bf16[256,128]{1,0:T(8,128)(2,1)S(1)}, bf16[256,128]{1,0:T(8,128)(2,1)S(1)}, u32[]{:S(2)}, u32[]{:S(2)}) collective-permute-start(bf16[256,128]{1,0:T(8,128)(2,1)S(1)} %pair_sum.1), channel_id=1, source_target_pairs={{0,16},{8,24},{16,0},{24,8},{1,17},{9,25},{17,1},{25,9},{2,18},{10... | collective-permute-start | bytes 196616 | tf_op jit(solution)/shard_map/ppermute | solution.py:57
  26.4 7.0 %collective-permute-done.8 = bf16[288,256]{1,0:T(8,128)(2,1)S(1)} collective-permute-done((bf16[288,256]{1,0:T(8,128)(2,1)S(1)}, bf16[288,256]{1,0:T(8,128)(2,1)S(1)}, u32[]{:S(2)}, u32[]{:S(2)}) %collective-permute-start.8) | collective-permute-done | bytes 147488 | tf_op jit(solution)/shard_map/ppermute | solution.py:57
  34.0 3.3 %all-to-all-start.1 = ((bf16[8,32,128]{2,1,0:T(8,128)(2,1)}), bf16[8,32,128]{2,1,0:T(8,128)(2,1)S(1)}, u32[]{:S(2)}, u32[]{:S(2)}) async-start(bf16[8,32,128]{2,1,0:T(8,128)(2,1)} %share_sum.1), calls=%async_computation.1 | async-start | bytes 131072 | tf_op jit(solution)/shard_map/all_to_all | solution.py:46
  38.1 2.0 %collective-permute-start.10 = (bf16[576,256]{1,0:T(8,128)(2,1)S(1)}, bf16[576,256]{1,0:T(8,128)(2,1)S(1)}, u32[]{:S(2)}, u32[]{:S(2)}) collective-permute-start(bf16[576,256]{1,0:T(8,128)(2,1)S(1)} %constant_dynamic-update-slice_fusion.refs_4_), channel_id=1, source_target_pairs={{0,1},{1,0},{2,3},{3,2},{4,5},{5,4},{6,7},{7,6},{8,9},{9,8},{10,11... | collective-permute-start | bytes 884744 | tf_op jit(solution)/shard_map/ppermute | solution.py:57
  40.1 1.5 %collective-permute-start.9 = (bf16[576,256]{1,0:T(8,128)(2,1)S(1)}, bf16[576,256]{1,0:T(8,128)(2,1)S(1)}, u32[]{:S(2)}, u32[]{:S(2)}) collective-permute-start(bf16[576,256]{1,0:T(8,128)(2,1)S(1)} %constant_dynamic-update-slice_fusion.refs_4_), channel_id=1, source_target_pairs={{0,2},{1,3},{2,0},{3,1},{4,6},{5,7},{6,4},{7,5},{8,10},{9,11},{10,... | collective-permute-start | bytes 884744 | tf_op jit(solution)/shard_map/ppermute | solution.py:57
  41.7 2.9 %all-to-all-done.1.share_ref = bf16[8,32,128]{2,1,0:T(8,128)(2,1)S(1)} async-done(((bf16[8,32,128]{2,1,0:T(8,128)(2,1)}), bf16[8,32,128]{2,1,0:T(8,128)(2,1)S(1)}, u32[]{:S(2)}, u32[]{:S(2)}) %all-to-all-start.1) | async-done | bytes 65568 | tf_op jit(solution)/shard_map/all_to_all | solution.py:46
  46.0 2.6 %collective-permute-done.9.refs_6_ = bf16[576,256]{1,0:T(8,128)(2,1)S(1)} collective-permute-done((bf16[576,256]{1,0:T(8,128)(2,1)S(1)}, bf16[576,256]{1,0:T(8,128)(2,1)S(1)}, u32[]{:S(2)}, u32[]{:S(2)}) %collective-permute-start.9) | collective-permute-done | bytes 294944 | tf_op jit(solution)/shard_map/ppermute | solution.py:57
  49.3 1.5 %collective-permute-start.6 = (bf16[9,32,128]{2,1,0:T(8,128)(2,1)S(1)}, bf16[9,32,128]{2,1,0:T(8,128)(2,1)S(1)}, u32[]{:S(2)}, u32[]{:S(2)}) collective-permute-start(bf16[9,32,128]{2,1,0:T(8,128)(2,1)S(1)} %pack_shares.1.refs_0_), channel_id=1, source_target_pairs={{0,16},{8,24},{16,0},{24,8},{1,17},{9,25},{17,1},{25,9},{2,18},{10... | collective-permute-start | bytes 221192 | tf_op jit(solution)/shard_map/ppermute | solution.py:57
  50.8 2.8 %collective-permute-done.6.refs_2_ = bf16[9,32,128]{2,1,0:T(8,128)(2,1)S(1)} collective-permute-done((bf16[9,32,128]{2,1,0:T(8,128)(2,1)S(1)}, bf16[9,32,128]{2,1,0:T(8,128)(2,1)S(1)}, u32[]{:S(2)}, u32[]{:S(2)}) %collective-permute-start.6) | collective-permute-done | bytes 73760 | tf_op jit(solution)/shard_map/ppermute | solution.py:57
  53.7 1.3 %collective-permute-done.11.refs_3_ = bf16[9,32,128]{2,1,0:T(8,128)(2,1)S(1)} collective-permute-done((bf16[9,32,128]{2,1,0:T(8,128)(2,1)S(1)}, bf16[9,32,128]{2,1,0:T(8,128)(2,1)S(1)}, u32[]{:S(2)}, u32[]{:S(2)}) %collective-permute-start.11) | collective-permute-done | bytes 73760 | tf_op jit(solution)/shard_map/ppermute | solution.py:57
  54.9 2.5 %copy-done.2 = bf16[2,10,128,1024]{3,2,1,0:T(8,128)(2,1)S(1)} copy-done((bf16[2,10,128,1024]{3,2,1,0:T(8,128)(2,1)S(1)}, bf16[2,10,128,1024]{3,2,1,0:T(8,128)(2,1)}, u32[]{:S(2)}) %copy-start.2) | copy-done | bytes 5242904
  57.4 3.4 %attention.1 = (bf16[17,16,128]{2,1,0:T(8,128)(2,1)S(1)}, bf16[17,16,128]{2,1,0:T(8,128)(2,1)S(1)}) custom-call(bf16[9,32,128]{2,1,0:T(8,128)(2,1)S(1)} %pack_shares.1.refs_0_, bf16[9,32,128]{2,1,0:T(8,128)(2,1)S(1)} %collective-permute-done.5.refs_1_, bf16[9,32,128]{2,1,0:T(8,128)(2,1)S(1)} %collective-permute-done.6.refs_2_, ...), custom_call_target="tpu_custom_call" | custom-call | tf_op jit(solution)/shard_map/attention/pallas_call | solution.py:34
  62.4 1.5 %collective-permute-start.13 = (bf16[17,16,128]{2,1,0:T(8,128)(2,1)S(1)}, bf16[17,16,128]{2,1,0:T(8,128)(2,1)S(1)}, u32[]{:S(2)}, u32[]{:S(2)}) collective-permute-start(bf16[17,16,128]{2,1,0:T(8,128)(2,1)S(1)} %pair_terms.1.own_ref), channel_id=1, source_target_pairs={{0,16},{8,24},{16,0},{24,8},{1,17},{9,25},{17,1},{25,9},{2,18},{10... | collective-permute-start | bytes 208904 | tf_op jit(solution)/shard_map/ppermute | solution.py:57
  63.9 2.8 %collective-permute-done.13.across_ref = bf16[17,16,128]{2,1,0:T(8,128)(2,1)S(1)} collective-permute-done((bf16[17,16,128]{2,1,0:T(8,128)(2,1)S(1)}, bf16[17,16,128]{2,1,0:T(8,128)(2,1)S(1)}, u32[]{:S(2)}, u32[]{:S(2)}) %collective-permute-start.13) | collective-permute-done | bytes 69664 | tf_op jit(solution)/shard_map/ppermute | solution.py:57
  69.0 1.3 %collective-permute-start.18 = (f32[32,128]{1,0:T(8,128)S(1)}, f32[32,128]{1,0:T(8,128)S(1)}, u32[]{:S(2)}, u32[]{:S(2)}) collective-permute-start(f32[32,128]{1,0:T(8,128)S(1)} %get-tuple-element.67.refs_0_), channel_id=1, source_target_pairs={{0,24},{8,16},{16,8},{24,0},{1,25},{9,17},{17,9},{25,1},{2,26},{10... | collective-permute-start | bytes 49160 | tf_op jit(solution)/shard_map/ppermute | solution.py:57
  71.0 1.3 %collective-permute-done.18.refs_3_ = f32[32,128]{1,0:T(8,128)S(1)} collective-permute-done((f32[32,128]{1,0:T(8,128)S(1)}, f32[32,128]{1,0:T(8,128)S(1)}, u32[]{:S(2)}, u32[]{:S(2)}) %collective-permute-start.18) | collective-permute-done | bytes 16416 | tf_op jit(solution)/shard_map/ppermute | solution.py:57
  72.3 1.9 %collective-permute-done.17.refs_2_ = f32[32,128]{1,0:T(8,128)S(1)} collective-permute-done((f32[32,128]{1,0:T(8,128)S(1)}, f32[32,128]{1,0:T(8,128)S(1)}, u32[]{:S(2)}, u32[]{:S(2)}) %collective-permute-start.17) | collective-permute-done | bytes 16416 | tf_op jit(solution)/shard_map/ppermute | solution.py:57
  74.4 14.3 %all_to_all.20.ff_ref = bf16[8,144,128]{2,1,0:T(8,128)(2,1)S(1)} all-to-all(bf16[8,144,128]{2,1,0:T(8,128)(2,1)S(1)} %get-tuple-element.69), channel_id=1, replica_groups=mesh['gx'=4,'gy'=8] {'gy'}, dimensions={0} | all-to-all | bytes 589824 | tf_op jit(solution)/shard_map/all_to_all | solution.py:46
  92.1 1.4 %collective-permute-start.25 = (bf16[64,1024]{1,0:T(8,128)(2,1)S(1)}, bf16[64,1024]{1,0:T(8,128)(2,1)S(1)}, u32[]{:S(2)}, u32[]{:S(2)}) collective-permute-start(bf16[64,1024]{1,0:T(8,128)(2,1)S(1)} %pair_sum_ff.3), channel_id=1, source_target_pairs={{0,16},{8,24},{16,0},{24,8},{1,17},{9,25},{17,1},{25,9},{2,18},{10... | collective-permute-start | bytes 393224 | tf_op jit(solution)/shard_map/ppermute | solution.py:57
  93.5 4.9 %collective-permute-done.20.z2_ref = bf16[64,1280]{1,0:T(8,128)(2,1)S(1)} collective-permute-done((bf16[64,1280]{1,0:T(8,128)(2,1)S(1)}, bf16[64,1280]{1,0:T(8,128)(2,1)S(1)}, u32[]{:S(2)}, u32[]{:S(2)}) %collective-permute-start.20) | collective-permute-done | bytes 163872 | tf_op jit(solution)/shard_map/ppermute | solution.py:57
  99.3 1.8 %collective-permute-done.25.z2_ref = bf16[64,1024]{1,0:T(8,128)(2,1)S(1)} collective-permute-done((bf16[64,1024]{1,0:T(8,128)(2,1)S(1)}, bf16[64,1024]{1,0:T(8,128)(2,1)S(1)}, u32[]{:S(2)}, u32[]{:S(2)}) %collective-permute-start.25) | collective-permute-done | bytes 131104 | tf_op jit(solution)/shard_map/ppermute | solution.py:57
  101.9 1.6 %collective-permute-done.22.refs_2_ = bf16[64,640]{1,0:T(8,128)(2,1)S(1)} collective-permute-done((bf16[64,640]{1,0:T(8,128)(2,1)S(1)}, bf16[64,640]{1,0:T(8,128)(2,1)S(1)}, u32[]{:S(2)}, u32[]{:S(2)}) %collective-permute-start.22) | collective-permute-done | bytes 81952 | tf_op jit(solution)/shard_map/ppermute | solution.py:57
  104.1 1.4 %collective-permute-done.27.refs_6_ = bf16[64,512]{1,0:T(8,128)(2,1)S(1)} collective-permute-done((bf16[64,512]{1,0:T(8,128)(2,1)S(1)}, bf16[64,512]{1,0:T(8,128)(2,1)S(1)}, u32[]{:S(2)}, u32[]{:S(2)}) %collective-permute-start.27) | collective-permute-done | bytes 65568 | tf_op jit(solution)/shard_map/ppermute | solution.py:57
  107.5 13.3 %all_to_all.21.parts_ref = bf16[8,144,128]{2,1,0:T(8,128)(2,1)S(1)} all-to-all(bf16[8,144,128]{2,1,0:T(8,128)(2,1)S(1)} %project_down.1), channel_id=1, replica_groups=mesh['gx'=4,'gy'=8] {'gy'}, dimensions={0} | all-to-all | bytes 589824 | tf_op jit(solution)/shard_map/all_to_all | solution.py:46
  122.8 1.3 %collective-permute-done.31.refs_3_ = f32[32,128]{1,0:T(8,128)S(1)} collective-permute-done((f32[32,128]{1,0:T(8,128)S(1)}, f32[32,128]{1,0:T(8,128)S(1)}, u32[]{:S(2)}, u32[]{:S(2)}) %collective-permute-start.31) | collective-permute-done | bytes 16416 | tf_op jit(solution)/shard_map/ppermute | solution.py:57
  (88 shorter events, 21.8 us)
Async XLA Ops:
  1.7 18.5 %all-to-all-start = ((bf16[8,144,128]{2,1,0:T(8,128)(2,1)}), bf16[8,144,128]{2,1,0:T(8,128)(2,1)S(1)}, u32[]{:S(2)}, u32[]{:S(2)}) async-start(bf16[8,144,128]{2,1,0:T(8,128)(2,1)} %get-tuple-element.43), calls=%async_computation | async-start | bytes 589824 | tf_op jit(solution)/shard_map/all_to_all | solution.py:46
  9.1 11.8 %collective-permute-start.3 = (bf16[576,256]{1,0:T(8,128)(2,1)S(1)}, bf16[576,256]{1,0:T(8,128)(2,1)S(1)}, u32[]{:S(2)}, u32[]{:S(2)}) collective-permute-start(bf16[576,256]{1,0:T(8,128)(2,1)S(1)} %bitcast.5), channel_id=1, source_target_pairs={{0,1},{1,0},{2,3},{3,2},{4,5},{5,4},{6,7},{7,6},{8,9},{9,8},{10,11... | collective-permute-start | bytes 884744 | tf_op jit(solution)/shard_map/ppermute | solution.py:57
  11.1 26.2 %collective-permute-start.2 = (bf16[576,256]{1,0:T(8,128)(2,1)S(1)}, bf16[576,256]{1,0:T(8,128)(2,1)S(1)}, u32[]{:S(2)}, u32[]{:S(2)}) collective-permute-start(bf16[576,256]{1,0:T(8,128)(2,1)S(1)} %bitcast.6), channel_id=1, source_target_pairs={{0,2},{1,3},{2,0},{3,1},{4,6},{5,7},{6,4},{7,5},{8,10},{9,11},{10,... | collective-permute-start | bytes 884744 | tf_op jit(solution)/shard_map/ppermute | solution.py:57
  12.6 12.1 %collective-permute-start.7 = (bf16[288,256]{1,0:T(8,128)(2,1)S(1)}, bf16[288,256]{1,0:T(8,128)(2,1)S(1)}, u32[]{:S(2)}, u32[]{:S(2)}) collective-permute-start(bf16[288,256]{1,0:T(8,128)(2,1)S(1)} %get-tuple-element.79), channel_id=1, source_target_pairs={{0,4},{1,5},{2,6},{3,7},{4,0},{5,1},{6,2},{7,3},{8,12},{9,13},{10,... | collective-permute-start | bytes 442376 | tf_op jit(solution)/shard_map/ppermute | solution.py:57
  20.6 4.2 %collective-permute-start = (bf16[2,256,128]{2,1,0:T(8,128)(2,1)S(1)}, bf16[2,256,128]{2,1,0:T(8,128)(2,1)S(1)}, u32[]{:S(2)}, u32[]{:S(2)}) collective-permute-start(bf16[2,256,128]{2,1,0:T(8,128)(2,1)S(1)} %get-tuple-element.45), channel_id=1, source_target_pairs={{0,8},{8,0},{16,24},{24,16},{1,9},{9,1},{17,25},{25,17},{2,10},{10... | collective-permute-start | bytes 393224 | tf_op jit(solution)/shard_map/ppermute | solution.py:57
  20.9 12.4 %collective-permute-start.8 = (bf16[288,256]{1,0:T(8,128)(2,1)S(1)}, bf16[288,256]{1,0:T(8,128)(2,1)S(1)}, u32[]{:S(2)}, u32[]{:S(2)}) collective-permute-start(bf16[288,256]{1,0:T(8,128)(2,1)S(1)} %get-tuple-element.56), channel_id=1, source_target_pairs={{0,4},{1,5},{2,6},{3,7},{4,0},{5,1},{6,2},{7,3},{8,12},{9,13},{10,... | collective-permute-start | bytes 442376 | tf_op jit(solution)/shard_map/ppermute | solution.py:57
  23.2 14.1 %collective-permute-start.4 = (bf16[576,256]{1,0:T(8,128)(2,1)S(1)}, bf16[576,256]{1,0:T(8,128)(2,1)S(1)}, u32[]{:S(2)}, u32[]{:S(2)}) collective-permute-start(bf16[576,256]{1,0:T(8,128)(2,1)S(1)} %collective-permute-done.3.refs_1_), channel_id=1, source_target_pairs={{0,2},{1,3},{2,0},{3,1},{4,6},{5,7},{6,4},{7,5},{8,10},{9,11},{10,... | collective-permute-start | bytes 884744 | tf_op jit(solution)/shard_map/ppermute | solution.py:57
  24.8 8.6 %collective-permute-start.1 = (bf16[256,128]{1,0:T(8,128)(2,1)S(1)}, bf16[256,128]{1,0:T(8,128)(2,1)S(1)}, u32[]{:S(2)}, u32[]{:S(2)}) collective-permute-start(bf16[256,128]{1,0:T(8,128)(2,1)S(1)} %pair_sum.1), channel_id=1, source_target_pairs={{0,16},{8,24},{16,0},{24,8},{1,17},{9,25},{17,1},{25,9},{2,18},{10... | collective-permute-start | bytes 196616 | tf_op jit(solution)/shard_map/ppermute | solution.py:57
  34.0 10.6 %all-to-all-start.1 = ((bf16[8,32,128]{2,1,0:T(8,128)(2,1)}), bf16[8,32,128]{2,1,0:T(8,128)(2,1)S(1)}, u32[]{:S(2)}, u32[]{:S(2)}) async-start(bf16[8,32,128]{2,1,0:T(8,128)(2,1)} %share_sum.1), calls=%async_computation.1 | async-start | bytes 131072 | tf_op jit(solution)/shard_map/all_to_all | solution.py:46
  38.1 15.5 %collective-permute-start.10 = (bf16[576,256]{1,0:T(8,128)(2,1)S(1)}, bf16[576,256]{1,0:T(8,128)(2,1)S(1)}, u32[]{:S(2)}, u32[]{:S(2)}) collective-permute-start(bf16[576,256]{1,0:T(8,128)(2,1)S(1)} %constant_dynamic-update-slice_fusion.refs_4_), channel_id=1, source_target_pairs={{0,1},{1,0},{2,3},{3,2},{4,5},{5,4},{6,7},{7,6},{8,9},{9,8},{10,11... | collective-permute-start | bytes 884744 | tf_op jit(solution)/shard_map/ppermute | solution.py:57
  40.1 8.5 %collective-permute-start.9 = (bf16[576,256]{1,0:T(8,128)(2,1)S(1)}, bf16[576,256]{1,0:T(8,128)(2,1)S(1)}, u32[]{:S(2)}, u32[]{:S(2)}) collective-permute-start(bf16[576,256]{1,0:T(8,128)(2,1)S(1)} %constant_dynamic-update-slice_fusion.refs_4_), channel_id=1, source_target_pairs={{0,2},{1,3},{2,0},{3,1},{4,6},{5,7},{6,4},{7,5},{8,10},{9,11},{10,... | collective-permute-start | bytes 884744 | tf_op jit(solution)/shard_map/ppermute | solution.py:57
  44.7 1.3 %collective-permute-start.5 = (bf16[9,32,128]{2,1,0:T(8,128)(2,1)S(1)}, bf16[9,32,128]{2,1,0:T(8,128)(2,1)S(1)}, u32[]{:S(2)}, u32[]{:S(2)}) collective-permute-start(bf16[9,32,128]{2,1,0:T(8,128)(2,1)S(1)} %pack_shares.1.refs_0_), channel_id=1, source_target_pairs={{0,8},{8,0},{16,24},{24,16},{1,9},{9,1},{17,25},{25,17},{2,10},{10... | collective-permute-start | bytes 221192 | tf_op jit(solution)/shard_map/ppermute | solution.py:57
  48.6 18.1 %collective-permute-start.14 = (bf16[576,256]{1,0:T(8,128)(2,1)S(1)}, bf16[576,256]{1,0:T(8,128)(2,1)S(1)}, u32[]{:S(2)}, u32[]{:S(2)}) collective-permute-start(bf16[576,256]{1,0:T(8,128)(2,1)S(1)} %collective-permute-done.9.refs_6_), channel_id=1, source_target_pairs={{0,1},{1,0},{2,3},{3,2},{4,5},{5,4},{6,7},{7,6},{8,9},{9,8},{10,11... | collective-permute-start | bytes 884744 | tf_op jit(solution)/shard_map/ppermute | solution.py:57
  49.3 4.4 %collective-permute-start.6 = (bf16[9,32,128]{2,1,0:T(8,128)(2,1)S(1)}, bf16[9,32,128]{2,1,0:T(8,128)(2,1)S(1)}, u32[]{:S(2)}, u32[]{:S(2)}) collective-permute-start(bf16[9,32,128]{2,1,0:T(8,128)(2,1)S(1)} %pack_shares.1.refs_0_), channel_id=1, source_target_pairs={{0,16},{8,24},{16,0},{24,8},{1,17},{9,25},{17,1},{25,9},{2,18},{10... | collective-permute-start | bytes 221192 | tf_op jit(solution)/shard_map/ppermute | solution.py:57
  60.9 1.3 %collective-permute-start.12 = (bf16[17,16,128]{2,1,0:T(8,128)(2,1)S(1)}, bf16[17,16,128]{2,1,0:T(8,128)(2,1)S(1)}, u32[]{:S(2)}, u32[]{:S(2)}) collective-permute-start(bf16[17,16,128]{2,1,0:T(8,128)(2,1)S(1)} %get-tuple-element.64), channel_id=1, source_target_pairs={{0,8},{8,0},{16,24},{24,16},{1,9},{9,1},{17,25},{25,17},{2,10},{10... | collective-permute-start | bytes 208904 | tf_op jit(solution)/shard_map/ppermute | solution.py:57
  62.4 4.3 %collective-permute-start.13 = (bf16[17,16,128]{2,1,0:T(8,128)(2,1)S(1)}, bf16[17,16,128]{2,1,0:T(8,128)(2,1)S(1)}, u32[]{:S(2)}, u32[]{:S(2)}) collective-permute-start(bf16[17,16,128]{2,1,0:T(8,128)(2,1)S(1)} %pair_terms.1.own_ref), channel_id=1, source_target_pairs={{0,16},{8,24},{16,0},{24,8},{1,17},{9,25},{17,1},{25,9},{2,18},{10... | collective-permute-start | bytes 208904 | tf_op jit(solution)/shard_map/ppermute | solution.py:57
  66.9 1.3 %collective-permute-start.15 = (bf16[16,16,128]{2,1,0:T(8,128)(2,1)S(1)}, bf16[16,16,128]{2,1,0:T(8,128)(2,1)S(1)}, u32[]{:S(2)}, u32[]{:S(2)}) collective-permute-start(bf16[16,16,128]{2,1,0:T(8,128)(2,1)S(1)} %divide.1.own_ref), channel_id=1, source_target_pairs={{0,8},{8,0},{16,24},{24,16},{1,9},{9,1},{17,25},{25,17},{2,10},{10... | collective-permute-start | bytes 196616 | tf_op jit(solution)/shard_map/ppermute | solution.py:57
  69.0 3.2 %collective-permute-start.18 = (f32[32,128]{1,0:T(8,128)S(1)}, f32[32,128]{1,0:T(8,128)S(1)}, u32[]{:S(2)}, u32[]{:S(2)}) collective-permute-start(f32[32,128]{1,0:T(8,128)S(1)} %get-tuple-element.67.refs_0_), channel_id=1, source_target_pairs={{0,24},{8,16},{16,8},{24,0},{1,25},{9,17},{17,9},{25,1},{2,26},{10... | collective-permute-start | bytes 49160 | tf_op jit(solution)/shard_map/ppermute | solution.py:57
  70.4 3.7 %collective-permute-start.17 = (f32[32,128]{1,0:T(8,128)S(1)}, f32[32,128]{1,0:T(8,128)S(1)}, u32[]{:S(2)}, u32[]{:S(2)}) collective-permute-start(f32[32,128]{1,0:T(8,128)S(1)} %get-tuple-element.67.refs_0_), channel_id=1, source_target_pairs={{0,16},{8,24},{16,0},{24,8},{1,17},{9,25},{17,1},{25,9},{2,18},{10... | collective-permute-start | bytes 49160 | tf_op jit(solution)/shard_map/ppermute | solution.py:57
  70.9 3.2 %collective-permute-start.16 = (f32[32,128]{1,0:T(8,128)S(1)}, f32[32,128]{1,0:T(8,128)S(1)}, u32[]{:S(2)}, u32[]{:S(2)}) collective-permute-start(f32[32,128]{1,0:T(8,128)S(1)} %get-tuple-element.67.refs_0_), channel_id=1, source_target_pairs={{0,8},{8,0},{16,24},{24,16},{1,9},{9,1},{17,25},{25,17},{2,10},{10... | collective-permute-start | bytes 49160 | tf_op jit(solution)/shard_map/ppermute | solution.py:57
  89.5 1.7 %collective-permute-start.19 = (bf16[2,64,1280]{2,1,0:T(8,128)(2,1)S(1)}, bf16[2,64,1280]{2,1,0:T(8,128)(2,1)S(1)}, u32[]{:S(2)}, u32[]{:S(2)}) collective-permute-start(bf16[2,64,1280]{2,1,0:T(8,128)(2,1)S(1)} %get-tuple-element.71), channel_id=1, source_target_pairs={{0,8},{8,0},{16,24},{24,16},{1,9},{9,1},{17,25},{25,17},{2,10},{10... | collective-permute-start | bytes 983048 | tf_op jit(solution)/shard_map/ppermute | solution.py:57
  90.2 1.9 %collective-permute-start.24 = (bf16[2,64,1024]{2,1,0:T(8,128)(2,1)S(1)}, bf16[2,64,1024]{2,1,0:T(8,128)(2,1)S(1)}, u32[]{:S(2)}, u32[]{:S(2)}) collective-permute-start(bf16[2,64,1024]{2,1,0:T(8,128)(2,1)S(1)} %get-tuple-element.74), channel_id=1, source_target_pairs={{0,8},{8,0},{16,24},{24,16},{1,9},{9,1},{17,25},{25,17},{2,10},{10... | collective-permute-start | bytes 786440 | tf_op jit(solution)/shard_map/ppermute | solution.py:57
  91.3 7.1 %collective-permute-start.20 = (bf16[64,1280]{1,0:T(8,128)(2,1)S(1)}, bf16[64,1280]{1,0:T(8,128)(2,1)S(1)}, u32[]{:S(2)}, u32[]{:S(2)}) collective-permute-start(bf16[64,1280]{1,0:T(8,128)(2,1)S(1)} %pair_sum_ff.2), channel_id=1, source_target_pairs={{0,16},{8,24},{16,0},{24,8},{1,17},{9,25},{17,1},{25,9},{2,18},{10... | collective-permute-start | bytes 491528 | tf_op jit(solution)/shard_map/ppermute | solution.py:57
  92.1 8.9 %collective-permute-start.25 = (bf16[64,1024]{1,0:T(8,128)(2,1)S(1)}, bf16[64,1024]{1,0:T(8,128)(2,1)S(1)}, u32[]{:S(2)}, u32[]{:S(2)}) collective-permute-start(bf16[64,1024]{1,0:T(8,128)(2,1)S(1)} %pair_sum_ff.3), channel_id=1, source_target_pairs={{0,16},{8,24},{16,0},{24,8},{1,17},{9,25},{17,1},{25,9},{2,18},{10... | collective-permute-start | bytes 393224 | tf_op jit(solution)/shard_map/ppermute | solution.py:57
  98.5 5.1 %collective-permute-start.22 = (bf16[64,640]{1,0:T(8,128)(2,1)S(1)}, bf16[64,640]{1,0:T(8,128)(2,1)S(1)}, u32[]{:S(2)}, u32[]{:S(2)}) collective-permute-start(bf16[64,640]{1,0:T(8,128)(2,1)S(1)} %activate.2.refs_0_), channel_id=1, source_target_pairs={{0,16},{8,24},{16,0},{24,8},{1,17},{9,25},{17,1},{25,9},{2,18},{10... | collective-permute-start | bytes 245768 | tf_op jit(solution)/shard_map/ppermute | solution.py:57
  101.1 4.3 %collective-permute-start.27 = (bf16[64,512]{1,0:T(8,128)(2,1)S(1)}, bf16[64,512]{1,0:T(8,128)(2,1)S(1)}, u32[]{:S(2)}, u32[]{:S(2)}) collective-permute-start(bf16[64,512]{1,0:T(8,128)(2,1)S(1)} %activate.3.refs_4_), channel_id=1, source_target_pairs={{0,16},{8,24},{16,0},{24,8},{1,17},{9,25},{17,1},{25,9},{2,18},{10... | collective-permute-start | bytes 196616 | tf_op jit(solution)/shard_map/ppermute | solution.py:57
  101.9 4.8 %collective-permute-start.21 = (bf16[64,640]{1,0:T(8,128)(2,1)S(1)}, bf16[64,640]{1,0:T(8,128)(2,1)S(1)}, u32[]{:S(2)}, u32[]{:S(2)}) collective-permute-start(bf16[64,640]{1,0:T(8,128)(2,1)S(1)} %activate.2.refs_0_), channel_id=1, source_target_pairs={{0,8},{8,0},{16,24},{24,16},{1,9},{9,1},{17,25},{25,17},{2,10},{10... | collective-permute-start | bytes 245768 | tf_op jit(solution)/shard_map/ppermute | solution.py:57
  103.5 3.2 %collective-permute-start.23 = (bf16[64,640]{1,0:T(8,128)(2,1)S(1)}, bf16[64,640]{1,0:T(8,128)(2,1)S(1)}, u32[]{:S(2)}, u32[]{:S(2)}) collective-permute-start(bf16[64,640]{1,0:T(8,128)(2,1)S(1)} %collective-permute-done.22.refs_2_), channel_id=1, source_target_pairs={{0,8},{8,0},{16,24},{24,16},{1,9},{9,1},{17,25},{25,17},{2,10},{10... | collective-permute-start | bytes 245768 | tf_op jit(solution)/shard_map/ppermute | solution.py:57
  103.5 1.9 %collective-permute-start.26 = (bf16[64,512]{1,0:T(8,128)(2,1)S(1)}, bf16[64,512]{1,0:T(8,128)(2,1)S(1)}, u32[]{:S(2)}, u32[]{:S(2)}) collective-permute-start(bf16[64,512]{1,0:T(8,128)(2,1)S(1)} %activate.3.refs_4_), channel_id=1, source_target_pairs={{0,8},{8,0},{16,24},{24,16},{1,9},{9,1},{17,25},{25,17},{2,10},{10... | collective-permute-start | bytes 196616 | tf_op jit(solution)/shard_map/ppermute | solution.py:57
  121.0 3.2 %collective-permute-start.31 = (f32[32,128]{1,0:T(8,128)S(1)}, f32[32,128]{1,0:T(8,128)S(1)}, u32[]{:S(2)}, u32[]{:S(2)}) collective-permute-start(f32[32,128]{1,0:T(8,128)S(1)} %get-tuple-element.76.refs_0_), channel_id=1, source_target_pairs={{0,24},{8,16},{16,8},{24,0},{1,25},{9,17},{17,9},{25,1},{2,26},{10... | collective-permute-start | bytes 49160 | tf_op jit(solution)/shard_map/ppermute | solution.py:57
  121.0 3.8 %collective-permute-start.30 = (f32[32,128]{1,0:T(8,128)S(1)}, f32[32,128]{1,0:T(8,128)S(1)}, u32[]{:S(2)}, u32[]{:S(2)}) collective-permute-start(f32[32,128]{1,0:T(8,128)S(1)} %get-tuple-element.76.refs_0_), channel_id=1, source_target_pairs={{0,16},{8,24},{16,0},{24,8},{1,17},{9,25},{17,1},{25,9},{2,18},{10... | collective-permute-start | bytes 49160 | tf_op jit(solution)/shard_map/ppermute | solution.py:57
  121.7 3.0 %collective-permute-start.29 = (f32[32,128]{1,0:T(8,128)S(1)}, f32[32,128]{1,0:T(8,128)S(1)}, u32[]{:S(2)}, u32[]{:S(2)}) collective-permute-start(f32[32,128]{1,0:T(8,128)S(1)} %get-tuple-element.76.refs_0_), channel_id=1, source_target_pairs={{0,8},{8,0},{16,24},{24,16},{1,9},{9,1},{17,25},{25,17},{2,10},{10... | collective-permute-start | bytes 49160 | tf_op jit(solution)/shard_map/ppermute | solution.py:57
  (14 other events, 210.7 us)

commit v12 on v11

--- a/solution.py
+++ b/solution.py
@@ -137,20 +137,35 @@
         (table, lengths, parents),
         scratch=[pltpu.SMEM((slots + 1,), jnp.int32)],
         specs={0: IN_SMEM, 1: IN_SMEM, 2: IN_SMEM},
-        micros=5,
-    )
-
-
-def attend(shares, squares, tables, pool_ref, kept, store):
+    )
+
+
+def by_head(pool):
+    def kernel(pool_ref, out_ref, sems):
+        copies = []
+        for head in range(KV_HEADS):
+            here = pool_ref.at[:, :, :, head * HEAD_DIM : (head + 1) * HEAD_DIM]
+            copies.append(pltpu.make_async_copy(here, out_ref.at[head], sems.at[head]))
+            copies[-1].start()
+        for copy in copies:
+            copy.wait()
+
+    shape = (KV_HEADS,) + pool.shape[:3] + (HEAD_DIM,)
+    return run(
+        "by_head",
+        kernel,
+        [(shape, BF)],
+        (pool,),
+        scratch=[pltpu.SemaphoreType.DMA((KV_HEADS,))],
+        specs={0: IN_HBM},
+        micros=3,
+    )[0]
+
+
+def attend(shares, squares, tables, keys_ref, store):
     cos_ref, sin_ref, cached_ref, own_ref = tables
-    keys_ref, sems = kept
-    slots = pool_ref.shape[1]
+    slots = keys_ref.shape[2]
     rows = cos_ref.shape[0]
-    copies = []
-    for head in range(KV_HEADS):
-        here = pool_ref.at[:, :, :, head * HEAD_DIM : (head + 1) * HEAD_DIM]
-        copies.append(pltpu.make_async_copy(here, keys_ref.at[head], sems.at[head]))
-        copies[-1].start()
     square = jnp.sum(squares.astype(F32), axis=0)
     square = square[:, 0:1] + square[:, HALF // 2 : HALF // 2 + 1]
     scale = lax.rsqrt(square / D + EPSILON)
@@ -178,7 +193,6 @@
         den = row_sum(weights)
         num = jnp.dot(weights.astype(BF), value_step, preferred_element_type=F32)
 
-        copies[head].wait()
         keys = keys_ref[head, 0].reshape(slots * PAGE, HEAD_DIM)
         values = keys_ref[head, 1].reshape(slots * PAGE, HEAD_DIM)
         scores = lax.dot_general(query, keys, NT, preferred_element_type=F32)
@@ -187,13 +201,6 @@
         den = den + row_sum(weights)
         num = num + jnp.dot(weights.astype(BF), values, preferred_element_type=F32)
         store(head, num, den)
-
-
-def key_scratch(pool):
-    return [
-        pltpu.VMEM((KV_HEADS, 2) + pool.shape[1:3] + (HEAD_DIM,), BF),
-        pltpu.SemaphoreType.DMA((KV_HEADS,)),
-    ]
 
 
 def rope_tables(lengths, rows, steps):
@@ -243,6 +250,7 @@
     w_own = w_out.T
     x_all, w_split = lax.optimization_barrier((x_all, w_own))
     x_all = exchange(x_all, "gy")
+    x_all, keys = lax.optimization_barrier((x_all, by_head(cache_pool)))
 
     w_blocks = {0: w_own, 1: permute(w_own, "gy", 1), 2: permute(w_own, "gy", 2)}
     w_first = permute(w_split[: width // 2], "gy", 4)
@@ -292,8 +300,9 @@
     late, _ = lax.optimization_barrier((late, (shares, w_blocks[2], w_blocks[3])))
     cos, sin = rope_tables(late[1], rows, steps)
     tables = make_tables(*late, cache_pool.shape[1], rows, steps)
-    w_blocks[4] = jnp.concatenate([w_first, w_second], axis=0)
-    late, _ = lax.optimization_barrier((w_blocks[4], tables))
+    halves, _ = lax.optimization_barrier(((w_first, w_second), tables))
+    w_blocks[4] = jnp.concatenate(halves, axis=0)
+    late = w_blocks[4]
     w_blocks[6] = permute(late, "gy", 2)
     w_blocks[5] = permute(late, "gy", 1)
     shares = exchange(shares, "gy")
@@ -312,8 +321,8 @@
     w_blocks[7] = permute(late, "gy", 1)
 
     def attention(*refs):
-        a_refs, tables, pool_ref, outs = refs[:nx], refs[nx : nx + 4], refs[nx + 4], refs[nx + 5 :]
-        own_ref, pair_ref, keys_ref, sems, held, num_held, den_held = outs
+        a_refs, tables, keys_ref, outs = refs[:nx], refs[nx : nx + 4], refs[nx + 4], refs[nx + 5 :]
+        own_ref, pair_ref, held, num_held, den_held = outs
         me = my("gx")
         core = me & 1
         for n, ref in enumerate(a_refs):
@@ -336,8 +345,7 @@
             lambda share, which: held[share, which],
             held[:, ny],
             tables,
-            pool_ref,
-            (keys_ref, sems),
+            keys_ref,
             store,
         )
         for n, out in enumerate((own_ref, pair_ref)):
@@ -348,15 +356,14 @@
         "attention",
         attention,
         [(shape, BF), (shape, BF)],
-        (*shares, cos, sin, *tables, cache_pool),
-        scratch=key_scratch(cache_pool)
-        + [
+        (*shares, cos, sin, *tables, keys),
+        scratch=[
             pltpu.VMEM((nx,) + shares[0].shape, BF),
             pltpu.VMEM((KV_HEADS, REPS, 2, half, HEAD_DIM), F32),
             pltpu.VMEM((2, half, PAGE), F32),
         ],
         limit=24,
-        specs={nx + 4: IN_HBM},
+        micros=8,
     )
     pair = permute(pair, "gx", 1)
 
@@ -568,8 +575,7 @@
     cos, sin = rope_tables(lengths, rows, steps)
 
     def attention(*refs):
-        g_ref, square_ref, tables, pool_ref = refs[0], refs[1], refs[2:6], refs[6]
-        out_ref, keys_ref, sems = refs[7:]
+        g_ref, square_ref, tables, keys_ref, out_ref = refs[0], refs[1], refs[2:6], *refs[6:]
 
         def store(head, num, den):
             den = high_low(den, PAGE)
@@ -582,8 +588,7 @@
             lambda share, which: g_ref[share, which],
             square_ref[...],
             tables,
-            pool_ref,
-            (keys_ref, sems),
+            keys_ref,
             store,
         )
 
@@ -592,10 +597,8 @@
         "attention",
         attention,
         [((HEADS, rows, WIDE), BF)],
-        (shares, squares, cos, sin, *tables, cache_pool),
-        scratch=key_scratch(cache_pool),
+        (shares, squares, cos, sin, *tables, by_head(cache_pool)),
         limit=24,
-        specs={6: IN_HBM},
     )
     num = terms[..., :HEAD_DIM].transpose(1, 0, 2).reshape(nx, part, ny, head_part)
     den = terms[..., HEAD_DIM :: PAGE // 2].transpose(1, 0, 2)

time: 126 us -> 116 us (0.921)
  starting transfers between devices: 38.4 us -> 31.7 us
  waiting for transfers between devices: 44.1 us -> 38.4 us
  local copies, waits for them, and re-layouts: 3.41 us -> 8.17 us
    unnamed x25 -> x29, local copies, waits for them, and re-layouts: 3.38 us -> 8.14 us
    all_to_all x2, starting transfers between devices: 10.7 us -> 7.21 us  [exchange(): return lax.all_to_all(values, axes, split_axis=0, concat_axis=0, tiled=True)]
    ppermute x32, starting transfers between devices: 27.6 us -> 24.5 us  [permute(): return lax.ppermute(values, axis, [(i, i ^ m) for i in range(count)])]
    all_to_all x2, waiting for transfers between devices: 7.28 us -> 4.21 us  [exchange(): return lax.all_to_all(values, axes, split_axis=0, concat_axis=0, tiled=True)]
    ppermute x32, waiting for transfers between devices: 36.8 us -> 34.2 us  [permute(): return lax.ppermute(values, axis, [(i, i ^ m) for i in range(count)])]
    pallas_call x20 -> x21, Pallas kernels: 10.9 us -> 9.93 us  [run(): pl.pallas_call(kernel, out_shape=[jax.ShapeDtypeStruct(s, d) for s, d in...]
where the time goes in v12:
time: 116 us
  waiting for transfers between devices  38.4 us (33%)
  starting transfers between devices  31.7 us (27%)
  blocking collectives  26.5 us (23%)
  Pallas kernels  9.93 us (9%)
  local copies, waits for them, and re-layouts  8.17 us (7%)
    ppermute x32, waiting for transfers between devices, permute(): return lax.ppermute(values, axis, [(i, i ^ m) for i in range(count)])  34.2 us
    all_to_all x2, blocking collectives, exchange(): return lax.all_to_all(values, axes, split_axis=0, concat_axis=0, tiled=True)  26.5 us
    ppermute x32, starting transfers between devices, permute(): return lax.ppermute(values, axis, [(i, i ^ m) for i in range(count)])  24.5 us
    pallas_call x21, Pallas kernels, run(): pl.pallas_call(kernel, out_shape=[jax.ShapeDtypeStruct(s, d) for s, d in...  9.93 us
    unnamed x29, local copies, waits for them, and re-layouts  8.14 us
    all_to_all x2, starting transfers between devices, exchange(): return lax.all_to_all(values, axes, split_axis=0, concat_axis=0, tiled=True)  7.21 us
    all_to_all x2, waiting for transfers between devices, exchange(): return lax.all_to_all(values, axes, split_axis=0, concat_axis=0, tiled=True)  4.21 us
  transfers between devices with their start and end apart: 34, of which 21 were waited for; matrix products, arithmetic and copies ran while one was open for 0% of the time, Pallas kernels for 5%

profile of v12, /device:TPU:0, one launch (start us, length us, event | category | flops | bytes accessed | tf_op | source)
XLA Modules:
  0.0 115.9 jit_solution(4868985754179867480)
XLA Ops:
  0.0 2.9 %collective-permute-start.3 = (bf16[576,256]{1,0:T(8,128)(2,1)}, bf16[576,256]{1,0:T(8,128)(2,1)S(1)}, u32[]{:S(2)}, u32[]{:S(2)}) collective-permute-start(bf16[576,256]{1,0:T(8,128)(2,1)} %bitcast.5), channel_id=1, source_target_pairs={{0,1},{1,0},{2,3},{3,2},{4,5},{5,4},{6,7},{7,6},{8,9},{9,8},{10,11... | collective-permute-start | bytes 884744 | tf_op jit(solution)/shard_map/ppermute | solution.py:57
  2.9 1.6 %collective-permute-start.2 = (bf16[576,256]{1,0:T(8,128)(2,1)}, bf16[576,256]{1,0:T(8,128)(2,1)S(1)}, u32[]{:S(2)}, u32[]{:S(2)}) collective-permute-start(bf16[576,256]{1,0:T(8,128)(2,1)} %bitcast.6), channel_id=1, source_target_pairs={{0,2},{1,3},{2,0},{3,1},{4,6},{5,7},{6,4},{7,5},{8,10},{9,11},{10,... | collective-permute-start | bytes 884744 | tf_op jit(solution)/shard_map/ppermute | solution.py:57
  6.1 3.9 %all-to-all-start = ((bf16[8,144,128]{2,1,0:T(8,128)(2,1)}), bf16[8,144,128]{2,1,0:T(8,128)(2,1)S(1)}, u32[]{:S(2)}, u32[]{:S(2)}) async-start(bf16[8,144,128]{2,1,0:T(8,128)(2,1)} %get-tuple-element.46), calls=%async_computation | async-start | bytes 589824 | tf_op jit(solution)/shard_map/all_to_all | solution.py:46
  10.0 2.5 %copy-done.10 = bf16[2,10,128,1024]{3,2,1,0:T(8,128)(2,1)S(1)} copy-done((bf16[2,10,128,1024]{3,2,1,0:T(8,128)(2,1)S(1)}, bf16[2,10,128,1024]{3,2,1,0:T(8,128)(2,1)}, u32[]{:S(2)}) %copy-start.10) | copy-done | bytes 5242904
  13.3 2.3 %copy-done.12 = bf16[4,2,10,128,256]{4,3,2,1,0:T(8,128)(2,1)} copy-done((bf16[4,2,10,128,256]{4,3,2,1,0:T(8,128)(2,1)}, bf16[4,2,10,128,256]{4,3,2,1,0:T(8,128)(2,1)S(1)}, u32[]{:S(2)}) %copy-start.12) | copy-done | bytes 5242904
  15.6 3.4 %all-to-all-done.x_ref = bf16[8,144,128]{2,1,0:T(8,128)(2,1)S(1)} async-done(((bf16[8,144,128]{2,1,0:T(8,128)(2,1)}), bf16[8,144,128]{2,1,0:T(8,128)(2,1)S(1)}, u32[]{:S(2)}, u32[]{:S(2)}) %all-to-all-start) | async-done | bytes 294944 | tf_op jit(solution)/shard_map/all_to_all | solution.py:46
  21.6 2.1 %collective-permute-start.8 = (bf16[288,256]{1,0:T(8,128)(2,1)S(1)}, bf16[288,256]{1,0:T(8,128)(2,1)S(1)}, u32[]{:S(2)}, u32[]{:S(2)}) collective-permute-start(bf16[288,256]{1,0:T(8,128)(2,1)S(1)} %get-tuple-element.60), channel_id=1, source_target_pairs={{0,4},{1,5},{2,6},{3,7},{4,0},{5,1},{6,2},{7,3},{8,12},{9,13},{10,... | collective-permute-start | bytes 442376 | tf_op jit(solution)/shard_map/ppermute | solution.py:57
  24.3 1.6 %collective-permute-start.1 = (bf16[256,128]{1,0:T(8,128)(2,1)S(1)}, bf16[256,128]{1,0:T(8,128)(2,1)S(1)}, u32[]{:S(2)}, u32[]{:S(2)}) collective-permute-start(bf16[256,128]{1,0:T(8,128)(2,1)S(1)} %pair_sum.1), channel_id=1, source_target_pairs={{0,16},{8,24},{16,0},{24,8},{1,17},{9,25},{17,1},{25,9},{2,18},{10... | collective-permute-start | bytes 196616 | tf_op jit(solution)/shard_map/ppermute | solution.py:57
  25.9 2.7 %collective-permute-done.1.z2_ref = bf16[256,128]{1,0:T(8,128)(2,1)S(1)} collective-permute-done((bf16[256,128]{1,0:T(8,128)(2,1)S(1)}, bf16[256,128]{1,0:T(8,128)(2,1)S(1)}, u32[]{:S(2)}, u32[]{:S(2)}) %collective-permute-start.1) | collective-permute-done | bytes 65568 | tf_op jit(solution)/shard_map/ppermute | solution.py:57
  29.3 3.3 %all-to-all-start.1 = ((bf16[8,32,128]{2,1,0:T(8,128)(2,1)}), bf16[8,32,128]{2,1,0:T(8,128)(2,1)S(1)}, u32[]{:S(2)}, u32[]{:S(2)}) async-start(bf16[8,32,128]{2,1,0:T(8,128)(2,1)} %share_sum.1), calls=%async_computation.1 | async-start | bytes 131072 | tf_op jit(solution)/shard_map/all_to_all | solution.py:46
  34.5 3.5 %collective-permute-done.8 = bf16[288,256]{1,0:T(8,128)(2,1)S(1)} collective-permute-done((bf16[288,256]{1,0:T(8,128)(2,1)S(1)}, bf16[288,256]{1,0:T(8,128)(2,1)S(1)}, u32[]{:S(2)}, u32[]{:S(2)}) %collective-permute-start.8) | collective-permute-done | bytes 147488 | tf_op jit(solution)/shard_map/ppermute | solution.py:57
  39.6 1.5 %collective-permute-start.6 = (bf16[9,32,128]{2,1,0:T(8,128)(2,1)S(1)}, bf16[9,32,128]{2,1,0:T(8,128)(2,1)S(1)}, u32[]{:S(2)}, u32[]{:S(2)}) collective-permute-start(bf16[9,32,128]{2,1,0:T(8,128)(2,1)S(1)} %pack_shares.1.refs_0_), channel_id=1, source_target_pairs={{0,16},{8,24},{16,0},{24,8},{1,17},{9,25},{17,1},{25,9},{2,18},{10... | collective-permute-start | bytes 221192 | tf_op jit(solution)/shard_map/ppermute | solution.py:57
  41.1 2.8 %collective-permute-done.6.refs_2_ = bf16[9,32,128]{2,1,0:T(8,128)(2,1)S(1)} collective-permute-done((bf16[9,32,128]{2,1,0:T(8,128)(2,1)S(1)}, bf16[9,32,128]{2,1,0:T(8,128)(2,1)S(1)}, u32[]{:S(2)}, u32[]{:S(2)}) %collective-permute-start.6) | collective-permute-done | bytes 73760 | tf_op jit(solution)/shard_map/ppermute | solution.py:57
  44.0 2.4 %collective-permute-done.10.refs_5_ = bf16[576,256]{1,0:T(8,128)(2,1)S(1)} collective-permute-done((bf16[576,256]{1,0:T(8,128)(2,1)S(1)}, bf16[576,256]{1,0:T(8,128)(2,1)S(1)}, u32[]{:S(2)}, u32[]{:S(2)}) %collective-permute-start.10) | collective-permute-done | bytes 294944 | tf_op jit(solution)/shard_map/ppermute | solution.py:57
  46.5 1.7 %collective-permute-start.14 = (bf16[576,256]{1,0:T(8,128)(2,1)S(1)}, bf16[576,256]{1,0:T(8,128)(2,1)S(1)}, u32[]{:S(2)}, u32[]{:S(2)}) collective-permute-start(bf16[576,256]{1,0:T(8,128)(2,1)S(1)} %collective-permute-done.9.refs_6_), channel_id=1, source_target_pairs={{0,1},{1,0},{2,3},{3,2},{4,5},{5,4},{6,7},{7,6},{8,9},{9,8},{10,11... | collective-permute-start | bytes 884744 | tf_op jit(solution)/shard_map/ppermute | solution.py:57
  48.2 2.5 %copy-done.13 = bf16[4,2,10,128,256]{4,3,2,1,0:T(8,128)(2,1)S(1)} copy-done((bf16[4,2,10,128,256]{4,3,2,1,0:T(8,128)(2,1)S(1)}, bf16[4,2,10,128,256]{4,3,2,1,0:T(8,128)(2,1)}, u32[]{:S(2)}) %copy-start.13) | copy-done | bytes 5242904
  50.6 1.7 %attention.1 = (bf16[17,16,128]{2,1,0:T(8,128)(2,1)S(1)}, bf16[17,16,128]{2,1,0:T(8,128)(2,1)S(1)}) custom-call(bf16[9,32,128]{2,1,0:T(8,128)(2,1)S(1)} %pack_shares.1.refs_0_, bf16[9,32,128]{2,1,0:T(8,128)(2,1)S(1)} %collective-permute-done.5.refs_1_, bf16[9,32,128]{2,1,0:T(8,128)(2,1)S(1)} %collective-permute-done.6.refs_2_, ...), custom_call_target="tpu_custom_call" | custom-call | flops 8000000000 | tf_op jit(solution)/shard_map/attention/pallas_call | solution.py:34
  53.9 1.5 %collective-permute-start.13 = (bf16[17,16,128]{2,1,0:T(8,128)(2,1)S(1)}, bf16[17,16,128]{2,1,0:T(8,128)(2,1)S(1)}, u32[]{:S(2)}, u32[]{:S(2)}) collective-permute-start(bf16[17,16,128]{2,1,0:T(8,128)(2,1)S(1)} %pair_terms.1.own_ref), channel_id=1, source_target_pairs={{0,16},{8,24},{16,0},{24,8},{1,17},{9,25},{17,1},{25,9},{2,18},{10... | collective-permute-start | bytes 208904 | tf_op jit(solution)/shard_map/ppermute | solution.py:57
  55.4 2.8 %collective-permute-done.13.across_ref = bf16[17,16,128]{2,1,0:T(8,128)(2,1)S(1)} collective-permute-done((bf16[17,16,128]{2,1,0:T(8,128)(2,1)S(1)}, bf16[17,16,128]{2,1,0:T(8,128)(2,1)S(1)}, u32[]{:S(2)}, u32[]{:S(2)}) %collective-permute-start.13) | collective-permute-done | bytes 69664 | tf_op jit(solution)/shard_map/ppermute | solution.py:57
  58.5 1.2 %collective-permute-done.15.other_ref = bf16[16,16,128]{2,1,0:T(8,128)(2,1)S(1)} collective-permute-done((bf16[16,16,128]{2,1,0:T(8,128)(2,1)S(1)}, bf16[16,16,128]{2,1,0:T(8,128)(2,1)S(1)}, u32[]{:S(2)}, u32[]{:S(2)}) %collective-permute-start.15) | collective-permute-done | bytes 65568 | tf_op jit(solution)/shard_map/ppermute | solution.py:57
  60.5 1.3 %collective-permute-start.18 = (f32[32,128]{1,0:T(8,128)S(1)}, f32[32,128]{1,0:T(8,128)S(1)}, u32[]{:S(2)}, u32[]{:S(2)}) collective-permute-start(f32[32,128]{1,0:T(8,128)S(1)} %get-tuple-element.73.refs_0_), channel_id=1, source_target_pairs={{0,24},{8,16},{16,8},{24,0},{1,25},{9,17},{17,9},{25,1},{2,26},{10... | collective-permute-start | bytes 49160 | tf_op jit(solution)/shard_map/ppermute | solution.py:57
  62.5 1.3 %collective-permute-done.18.refs_3_ = f32[32,128]{1,0:T(8,128)S(1)} collective-permute-done((f32[32,128]{1,0:T(8,128)S(1)}, f32[32,128]{1,0:T(8,128)S(1)}, u32[]{:S(2)}, u32[]{:S(2)}) %collective-permute-start.18) | collective-permute-done | bytes 16416 | tf_op jit(solution)/shard_map/ppermute | solution.py:57
  63.8 1.9 %collective-permute-done.17.refs_2_ = f32[32,128]{1,0:T(8,128)S(1)} collective-permute-done((f32[32,128]{1,0:T(8,128)S(1)}, f32[32,128]{1,0:T(8,128)S(1)}, u32[]{:S(2)}, u32[]{:S(2)}) %collective-permute-start.17) | collective-permute-done | bytes 16416 | tf_op jit(solution)/shard_map/ppermute | solution.py:57
  65.9 13.2 %all_to_all.20.ff_ref = bf16[8,144,128]{2,1,0:T(8,128)(2,1)S(1)} all-to-all(bf16[8,144,128]{2,1,0:T(8,128)(2,1)S(1)} %get-tuple-element.75), channel_id=1, replica_groups=mesh['gx'=4,'gy'=8] {'gy'}, dimensions={0} | all-to-all | bytes 589824 | tf_op jit(solution)/shard_map/all_to_all | solution.py:46
  82.5 1.4 %collective-permute-start.25 = (bf16[64,1024]{1,0:T(8,128)(2,1)S(1)}, bf16[64,1024]{1,0:T(8,128)(2,1)S(1)}, u32[]{:S(2)}, u32[]{:S(2)}) collective-permute-start(bf16[64,1024]{1,0:T(8,128)(2,1)S(1)} %pair_sum_ff.3), channel_id=1, source_target_pairs={{0,16},{8,24},{16,0},{24,8},{1,17},{9,25},{17,1},{25,9},{2,18},{10... | collective-permute-start | bytes 393224 | tf_op jit(solution)/shard_map/ppermute | solution.py:57
  83.8 4.9 %collective-permute-done.20.z2_ref = bf16[64,1280]{1,0:T(8,128)(2,1)S(1)} collective-permute-done((bf16[64,1280]{1,0:T(8,128)(2,1)S(1)}, bf16[64,1280]{1,0:T(8,128)(2,1)S(1)}, u32[]{:S(2)}, u32[]{:S(2)}) %collective-permute-start.20) | collective-permute-done | bytes 163872 | tf_op jit(solution)/shard_map/ppermute | solution.py:57
  89.6 1.8 %collective-permute-done.25.z2_ref = bf16[64,1024]{1,0:T(8,128)(2,1)S(1)} collective-permute-done((bf16[64,1024]{1,0:T(8,128)(2,1)S(1)}, bf16[64,1024]{1,0:T(8,128)(2,1)S(1)}, u32[]{:S(2)}, u32[]{:S(2)}) %collective-permute-start.25) | collective-permute-done | bytes 131104 | tf_op jit(solution)/shard_map/ppermute | solution.py:57
  92.3 1.6 %collective-permute-done.22.refs_2_ = bf16[64,640]{1,0:T(8,128)(2,1)S(1)} collective-permute-done((bf16[64,640]{1,0:T(8,128)(2,1)S(1)}, bf16[64,640]{1,0:T(8,128)(2,1)S(1)}, u32[]{:S(2)}, u32[]{:S(2)}) %collective-permute-start.22) | collective-permute-done | bytes 81952 | tf_op jit(solution)/shard_map/ppermute | solution.py:57
  94.4 1.4 %collective-permute-done.27.refs_6_ = bf16[64,512]{1,0:T(8,128)(2,1)S(1)} collective-permute-done((bf16[64,512]{1,0:T(8,128)(2,1)S(1)}, bf16[64,512]{1,0:T(8,128)(2,1)S(1)}, u32[]{:S(2)}, u32[]{:S(2)}) %collective-permute-start.27) | collective-permute-done | bytes 65568 | tf_op jit(solution)/shard_map/ppermute | solution.py:57
  95.8 1.2 %collective-permute-done.28.refs_7_ = bf16[64,512]{1,0:T(8,128)(2,1)S(1)} collective-permute-done((bf16[64,512]{1,0:T(8,128)(2,1)S(1)}, bf16[64,512]{1,0:T(8,128)(2,1)S(1)}, u32[]{:S(2)}, u32[]{:S(2)}) %collective-permute-start.28) | collective-permute-done | bytes 65568 | tf_op jit(solution)/shard_map/ppermute | solution.py:57
  97.9 13.3 %all_to_all.21.parts_ref = bf16[8,144,128]{2,1,0:T(8,128)(2,1)S(1)} all-to-all(bf16[8,144,128]{2,1,0:T(8,128)(2,1)S(1)} %project_down.1), channel_id=1, replica_groups=mesh['gx'=4,'gy'=8] {'gy'}, dimensions={0} | all-to-all | bytes 589824 | tf_op jit(solution)/shard_map/all_to_all | solution.py:46
  113.2 1.3 %collective-permute-done.31.refs_3_ = f32[32,128]{1,0:T(8,128)S(1)} collective-permute-done((f32[32,128]{1,0:T(8,128)S(1)}, f32[32,128]{1,0:T(8,128)S(1)}, u32[]{:S(2)}, u32[]{:S(2)}) %collective-permute-start.31) | collective-permute-done | bytes 16416 | tf_op jit(solution)/shard_map/ppermute | solution.py:57
  (93 shorter events, 22.2 us)
Async XLA Ops:
  0.0 19.0 %collective-permute-start.3 = (bf16[576,256]{1,0:T(8,128)(2,1)}, bf16[576,256]{1,0:T(8,128)(2,1)S(1)}, u32[]{:S(2)}, u32[]{:S(2)}) collective-permute-start(bf16[576,256]{1,0:T(8,128)(2,1)} %bitcast.5), channel_id=1, source_target_pairs={{0,1},{1,0},{2,3},{3,2},{4,5},{5,4},{6,7},{7,6},{8,9},{9,8},{10,11... | collective-permute-start | bytes 884744 | tf_op jit(solution)/shard_map/ppermute | solution.py:57
  2.9 29.8 %collective-permute-start.2 = (bf16[576,256]{1,0:T(8,128)(2,1)}, bf16[576,256]{1,0:T(8,128)(2,1)S(1)}, u32[]{:S(2)}, u32[]{:S(2)}) collective-permute-start(bf16[576,256]{1,0:T(8,128)(2,1)} %bitcast.6), channel_id=1, source_target_pairs={{0,2},{1,3},{2,0},{3,1},{4,6},{5,7},{6,4},{7,5},{8,10},{9,11},{10,... | collective-permute-start | bytes 884744 | tf_op jit(solution)/shard_map/ppermute | solution.py:57
  6.1 12.9 %all-to-all-start = ((bf16[8,144,128]{2,1,0:T(8,128)(2,1)}), bf16[8,144,128]{2,1,0:T(8,128)(2,1)S(1)}, u32[]{:S(2)}, u32[]{:S(2)}) async-start(bf16[8,144,128]{2,1,0:T(8,128)(2,1)} %get-tuple-element.46), calls=%async_computation | async-start | bytes 589824 | tf_op jit(solution)/shard_map/all_to_all | solution.py:46
  19.0 13.7 %collective-permute-start.4 = (bf16[576,256]{1,0:T(8,128)(2,1)S(1)}, bf16[576,256]{1,0:T(8,128)(2,1)S(1)}, u32[]{:S(2)}, u32[]{:S(2)}) collective-permute-start(bf16[576,256]{1,0:T(8,128)(2,1)S(1)} %collective-permute-done.3.refs_1_), channel_id=1, source_target_pairs={{0,2},{1,3},{2,0},{3,1},{4,6},{5,7},{6,4},{7,5},{8,10},{9,11},{10,... | collective-permute-start | bytes 884744 | tf_op jit(solution)/shard_map/ppermute | solution.py:57
  20.6 3.7 %collective-permute-start = (bf16[2,256,128]{2,1,0:T(8,128)(2,1)S(1)}, bf16[2,256,128]{2,1,0:T(8,128)(2,1)S(1)}, u32[]{:S(2)}, u32[]{:S(2)}) collective-permute-start(bf16[2,256,128]{2,1,0:T(8,128)(2,1)S(1)} %get-tuple-element.49), channel_id=1, source_target_pairs={{0,8},{8,0},{16,24},{24,16},{1,9},{9,1},{17,25},{25,17},{2,10},{10... | collective-permute-start | bytes 393224 | tf_op jit(solution)/shard_map/ppermute | solution.py:57
  20.6 13.9 %collective-permute-start.7 = (bf16[288,256]{1,0:T(8,128)(2,1)S(1)}, bf16[288,256]{1,0:T(8,128)(2,1)S(1)}, u32[]{:S(2)}, u32[]{:S(2)}) collective-permute-start(bf16[288,256]{1,0:T(8,128)(2,1)S(1)} %get-tuple-element.85), channel_id=1, source_target_pairs={{0,4},{1,5},{2,6},{3,7},{4,0},{5,1},{6,2},{7,3},{8,12},{9,13},{10,... | collective-permute-start | bytes 442376 | tf_op jit(solution)/shard_map/ppermute | solution.py:57
  21.6 16.5 %collective-permute-start.8 = (bf16[288,256]{1,0:T(8,128)(2,1)S(1)}, bf16[288,256]{1,0:T(8,128)(2,1)S(1)}, u32[]{:S(2)}, u32[]{:S(2)}) collective-permute-start(bf16[288,256]{1,0:T(8,128)(2,1)S(1)} %get-tuple-element.60), channel_id=1, source_target_pairs={{0,4},{1,5},{2,6},{3,7},{4,0},{5,1},{6,2},{7,3},{8,12},{9,13},{10,... | collective-permute-start | bytes 442376 | tf_op jit(solution)/shard_map/ppermute | solution.py:57
  24.3 4.3 %collective-permute-start.1 = (bf16[256,128]{1,0:T(8,128)(2,1)S(1)}, bf16[256,128]{1,0:T(8,128)(2,1)S(1)}, u32[]{:S(2)}, u32[]{:S(2)}) collective-permute-start(bf16[256,128]{1,0:T(8,128)(2,1)S(1)} %pair_sum.1), channel_id=1, source_target_pairs={{0,16},{8,24},{16,0},{24,8},{1,17},{9,25},{17,1},{25,9},{2,18},{10... | collective-permute-start | bytes 196616 | tf_op jit(solution)/shard_map/ppermute | solution.py:57
  29.3 10.2 %all-to-all-start.1 = ((bf16[8,32,128]{2,1,0:T(8,128)(2,1)}), bf16[8,32,128]{2,1,0:T(8,128)(2,1)S(1)}, u32[]{:S(2)}, u32[]{:S(2)}) async-start(bf16[8,32,128]{2,1,0:T(8,128)(2,1)} %share_sum.1), calls=%async_computation.1 | async-start | bytes 131072 | tf_op jit(solution)/shard_map/all_to_all | solution.py:46
  38.1 8.3 %collective-permute-start.10 = (bf16[576,256]{1,0:T(8,128)(2,1)S(1)}, bf16[576,256]{1,0:T(8,128)(2,1)S(1)}, u32[]{:S(2)}, u32[]{:S(2)}) collective-permute-start(bf16[576,256]{1,0:T(8,128)(2,1)S(1)} %constant_dynamic-update-slice_fusion.refs_4_), channel_id=1, source_target_pairs={{0,1},{1,0},{2,3},{3,2},{4,5},{5,4},{6,7},{7,6},{8,9},{9,8},{10,11... | collective-permute-start | bytes 884744 | tf_op jit(solution)/shard_map/ppermute | solution.py:57
  38.6 7.9 %collective-permute-start.9 = (bf16[576,256]{1,0:T(8,128)(2,1)S(1)}, bf16[576,256]{1,0:T(8,128)(2,1)S(1)}, u32[]{:S(2)}, u32[]{:S(2)}) collective-permute-start(bf16[576,256]{1,0:T(8,128)(2,1)S(1)} %constant_dynamic-update-slice_fusion.refs_4_), channel_id=1, source_target_pairs={{0,2},{1,3},{2,0},{3,1},{4,6},{5,7},{6,4},{7,5},{8,10},{9,11},{10,... | collective-permute-start | bytes 884744 | tf_op jit(solution)/shard_map/ppermute | solution.py:57
  39.6 4.4 %collective-permute-start.6 = (bf16[9,32,128]{2,1,0:T(8,128)(2,1)S(1)}, bf16[9,32,128]{2,1,0:T(8,128)(2,1)S(1)}, u32[]{:S(2)}, u32[]{:S(2)}) collective-permute-start(bf16[9,32,128]{2,1,0:T(8,128)(2,1)S(1)} %pack_shares.1.refs_0_), channel_id=1, source_target_pairs={{0,16},{8,24},{16,0},{24,8},{1,17},{9,25},{17,1},{25,9},{2,18},{10... | collective-permute-start | bytes 221192 | tf_op jit(solution)/shard_map/ppermute | solution.py:57
  41.1 5.3 %collective-permute-start.5 = (bf16[9,32,128]{2,1,0:T(8,128)(2,1)S(1)}, bf16[9,32,128]{2,1,0:T(8,128)(2,1)S(1)}, u32[]{:S(2)}, u32[]{:S(2)}) collective-permute-start(bf16[9,32,128]{2,1,0:T(8,128)(2,1)S(1)} %pack_shares.1.refs_0_), channel_id=1, source_target_pairs={{0,8},{8,0},{16,24},{24,16},{1,9},{9,1},{17,25},{25,17},{2,10},{10... | collective-permute-start | bytes 221192 | tf_op jit(solution)/shard_map/ppermute | solution.py:57
  46.5 1.7 %collective-permute-start.11 = (bf16[9,32,128]{2,1,0:T(8,128)(2,1)S(1)}, bf16[9,32,128]{2,1,0:T(8,128)(2,1)S(1)}, u32[]{:S(2)}, u32[]{:S(2)}) collective-permute-start(bf16[9,32,128]{2,1,0:T(8,128)(2,1)S(1)} %collective-permute-done.6.refs_2_), channel_id=1, source_target_pairs={{0,8},{8,0},{16,24},{24,16},{1,9},{9,1},{17,25},{25,17},{2,10},{10... | collective-permute-start | bytes 221192 | tf_op jit(solution)/shard_map/ppermute | solution.py:57
  46.5 11.7 %collective-permute-start.14 = (bf16[576,256]{1,0:T(8,128)(2,1)S(1)}, bf16[576,256]{1,0:T(8,128)(2,1)S(1)}, u32[]{:S(2)}, u32[]{:S(2)}) collective-permute-start(bf16[576,256]{1,0:T(8,128)(2,1)S(1)} %collective-permute-done.9.refs_6_), channel_id=1, source_target_pairs={{0,1},{1,0},{2,3},{3,2},{4,5},{5,4},{6,7},{7,6},{8,9},{9,8},{10,11... | collective-permute-start | bytes 884744 | tf_op jit(solution)/shard_map/ppermute | solution.py:57
  52.4 1.3 %collective-permute-start.12 = (bf16[17,16,128]{2,1,0:T(8,128)(2,1)S(1)}, bf16[17,16,128]{2,1,0:T(8,128)(2,1)S(1)}, u32[]{:S(2)}, u32[]{:S(2)}) collective-permute-start(bf16[17,16,128]{2,1,0:T(8,128)(2,1)S(1)} %get-tuple-element.70), channel_id=1, source_target_pairs={{0,8},{8,0},{16,24},{24,16},{1,9},{9,1},{17,25},{25,17},{2,10},{10... | collective-permute-start | bytes 208904 | tf_op jit(solution)/shard_map/ppermute | solution.py:57
  53.9 4.3 %collective-permute-start.13 = (bf16[17,16,128]{2,1,0:T(8,128)(2,1)S(1)}, bf16[17,16,128]{2,1,0:T(8,128)(2,1)S(1)}, u32[]{:S(2)}, u32[]{:S(2)}) collective-permute-start(bf16[17,16,128]{2,1,0:T(8,128)(2,1)S(1)} %pair_terms.1.own_ref), channel_id=1, source_target_pairs={{0,16},{8,24},{16,0},{24,8},{1,17},{9,25},{17,1},{25,9},{2,18},{10... | collective-permute-start | bytes 208904 | tf_op jit(solution)/shard_map/ppermute | solution.py:57
  60.5 3.2 %collective-permute-start.18 = (f32[32,128]{1,0:T(8,128)S(1)}, f32[32,128]{1,0:T(8,128)S(1)}, u32[]{:S(2)}, u32[]{:S(2)}) collective-permute-start(f32[32,128]{1,0:T(8,128)S(1)} %get-tuple-element.73.refs_0_), channel_id=1, source_target_pairs={{0,24},{8,16},{16,8},{24,0},{1,25},{9,17},{17,9},{25,1},{2,26},{10... | collective-permute-start | bytes 49160 | tf_op jit(solution)/shard_map/ppermute | solution.py:57
  61.9 3.7 %collective-permute-start.17 = (f32[32,128]{1,0:T(8,128)S(1)}, f32[32,128]{1,0:T(8,128)S(1)}, u32[]{:S(2)}, u32[]{:S(2)}) collective-permute-start(f32[32,128]{1,0:T(8,128)S(1)} %get-tuple-element.73.refs_0_), channel_id=1, source_target_pairs={{0,16},{8,24},{16,0},{24,8},{1,17},{9,25},{17,1},{25,9},{2,18},{10... | collective-permute-start | bytes 49160 | tf_op jit(solution)/shard_map/ppermute | solution.py:57
  62.4 3.2 %collective-permute-start.16 = (f32[32,128]{1,0:T(8,128)S(1)}, f32[32,128]{1,0:T(8,128)S(1)}, u32[]{:S(2)}, u32[]{:S(2)}) collective-permute-start(f32[32,128]{1,0:T(8,128)S(1)} %get-tuple-element.73.refs_0_), channel_id=1, source_target_pairs={{0,8},{8,0},{16,24},{24,16},{1,9},{9,1},{17,25},{25,17},{2,10},{10... | collective-permute-start | bytes 49160 | tf_op jit(solution)/shard_map/ppermute | solution.py:57
  79.9 1.7 %collective-permute-start.19 = (bf16[2,64,1280]{2,1,0:T(8,128)(2,1)S(1)}, bf16[2,64,1280]{2,1,0:T(8,128)(2,1)S(1)}, u32[]{:S(2)}, u32[]{:S(2)}) collective-permute-start(bf16[2,64,1280]{2,1,0:T(8,128)(2,1)S(1)} %get-tuple-element.77), channel_id=1, source_target_pairs={{0,8},{8,0},{16,24},{24,16},{1,9},{9,1},{17,25},{25,17},{2,10},{10... | collective-permute-start | bytes 983048 | tf_op jit(solution)/shard_map/ppermute | solution.py:57
  80.6 1.8 %collective-permute-start.24 = (bf16[2,64,1024]{2,1,0:T(8,128)(2,1)S(1)}, bf16[2,64,1024]{2,1,0:T(8,128)(2,1)S(1)}, u32[]{:S(2)}, u32[]{:S(2)}) collective-permute-start(bf16[2,64,1024]{2,1,0:T(8,128)(2,1)S(1)} %get-tuple-element.80), channel_id=1, source_target_pairs={{0,8},{8,0},{16,24},{24,16},{1,9},{9,1},{17,25},{25,17},{2,10},{10... | collective-permute-start | bytes 786440 | tf_op jit(solution)/shard_map/ppermute | solution.py:57
  81.6 7.1 %collective-permute-start.20 = (bf16[64,1280]{1,0:T(8,128)(2,1)S(1)}, bf16[64,1280]{1,0:T(8,128)(2,1)S(1)}, u32[]{:S(2)}, u32[]{:S(2)}) collective-permute-start(bf16[64,1280]{1,0:T(8,128)(2,1)S(1)} %pair_sum_ff.2), channel_id=1, source_target_pairs={{0,16},{8,24},{16,0},{24,8},{1,17},{9,25},{17,1},{25,9},{2,18},{10... | collective-permute-start | bytes 491528 | tf_op jit(solution)/shard_map/ppermute | solution.py:57
  82.5 9.0 %collective-permute-start.25 = (bf16[64,1024]{1,0:T(8,128)(2,1)S(1)}, bf16[64,1024]{1,0:T(8,128)(2,1)S(1)}, u32[]{:S(2)}, u32[]{:S(2)}) collective-permute-start(bf16[64,1024]{1,0:T(8,128)(2,1)S(1)} %pair_sum_ff.3), channel_id=1, source_target_pairs={{0,16},{8,24},{16,0},{24,8},{1,17},{9,25},{17,1},{25,9},{2,18},{10... | collective-permute-start | bytes 393224 | tf_op jit(solution)/shard_map/ppermute | solution.py:57
  88.9 5.1 %collective-permute-start.22 = (bf16[64,640]{1,0:T(8,128)(2,1)S(1)}, bf16[64,640]{1,0:T(8,128)(2,1)S(1)}, u32[]{:S(2)}, u32[]{:S(2)}) collective-permute-start(bf16[64,640]{1,0:T(8,128)(2,1)S(1)} %activate.2.refs_0_), channel_id=1, source_target_pairs={{0,16},{8,24},{16,0},{24,8},{1,17},{9,25},{17,1},{25,9},{2,18},{10... | collective-permute-start | bytes 245768 | tf_op jit(solution)/shard_map/ppermute | solution.py:57
  91.5 4.3 %collective-permute-start.27 = (bf16[64,512]{1,0:T(8,128)(2,1)S(1)}, bf16[64,512]{1,0:T(8,128)(2,1)S(1)}, u32[]{:S(2)}, u32[]{:S(2)}) collective-permute-start(bf16[64,512]{1,0:T(8,128)(2,1)S(1)} %activate.3.refs_4_), channel_id=1, source_target_pairs={{0,16},{8,24},{16,0},{24,8},{1,17},{9,25},{17,1},{25,9},{2,18},{10... | collective-permute-start | bytes 196616 | tf_op jit(solution)/shard_map/ppermute | solution.py:57
  92.3 4.8 %collective-permute-start.21 = (bf16[64,640]{1,0:T(8,128)(2,1)S(1)}, bf16[64,640]{1,0:T(8,128)(2,1)S(1)}, u32[]{:S(2)}, u32[]{:S(2)}) collective-permute-start(bf16[64,640]{1,0:T(8,128)(2,1)S(1)} %activate.2.refs_0_), channel_id=1, source_target_pairs={{0,8},{8,0},{16,24},{24,16},{1,9},{9,1},{17,25},{25,17},{2,10},{10... | collective-permute-start | bytes 245768 | tf_op jit(solution)/shard_map/ppermute | solution.py:57
  93.9 3.2 %collective-permute-start.23 = (bf16[64,640]{1,0:T(8,128)(2,1)S(1)}, bf16[64,640]{1,0:T(8,128)(2,1)S(1)}, u32[]{:S(2)}, u32[]{:S(2)}) collective-permute-start(bf16[64,640]{1,0:T(8,128)(2,1)S(1)} %collective-permute-done.22.refs_2_), channel_id=1, source_target_pairs={{0,8},{8,0},{16,24},{24,16},{1,9},{9,1},{17,25},{25,17},{2,10},{10... | collective-permute-start | bytes 245768 | tf_op jit(solution)/shard_map/ppermute | solution.py:57
  93.9 1.9 %collective-permute-start.26 = (bf16[64,512]{1,0:T(8,128)(2,1)S(1)}, bf16[64,512]{1,0:T(8,128)(2,1)S(1)}, u32[]{:S(2)}, u32[]{:S(2)}) collective-permute-start(bf16[64,512]{1,0:T(8,128)(2,1)S(1)} %activate.3.refs_4_), channel_id=1, source_target_pairs={{0,8},{8,0},{16,24},{24,16},{1,9},{9,1},{17,25},{25,17},{2,10},{10... | collective-permute-start | bytes 196616 | tf_op jit(solution)/shard_map/ppermute | solution.py:57
  111.4 3.2 %collective-permute-start.31 = (f32[32,128]{1,0:T(8,128)S(1)}, f32[32,128]{1,0:T(8,128)S(1)}, u32[]{:S(2)}, u32[]{:S(2)}) collective-permute-start(f32[32,128]{1,0:T(8,128)S(1)} %get-tuple-element.82.refs_0_), channel_id=1, source_target_pairs={{0,24},{8,16},{16,8},{24,0},{1,25},{9,17},{17,9},{25,1},{2,26},{10... | collective-permute-start | bytes 49160 | tf_op jit(solution)/shard_map/ppermute | solution.py:57
  111.4 3.8 %collective-permute-start.30 = (f32[32,128]{1,0:T(8,128)S(1)}, f32[32,128]{1,0:T(8,128)S(1)}, u32[]{:S(2)}, u32[]{:S(2)}) collective-permute-start(f32[32,128]{1,0:T(8,128)S(1)} %get-tuple-element.82.refs_0_), channel_id=1, source_target_pairs={{0,16},{8,24},{16,0},{24,8},{1,17},{9,25},{17,1},{25,9},{2,18},{10... | collective-permute-start | bytes 49160 | tf_op jit(solution)/shard_map/ppermute | solution.py:57
  112.1 3.0 %collective-permute-start.29 = (f32[32,128]{1,0:T(8,128)S(1)}, f32[32,128]{1,0:T(8,128)S(1)}, u32[]{:S(2)}, u32[]{:S(2)}) collective-permute-start(f32[32,128]{1,0:T(8,128)S(1)} %get-tuple-element.82.refs_0_), channel_id=1, source_target_pairs={{0,8},{8,0},{16,24},{24,16},{1,9},{9,1},{17,25},{25,17},{2,10},{10... | collective-permute-start | bytes 49160 | tf_op jit(solution)/shard_map/ppermute | solution.py:57
  (16 other events, 143.4 us)

commit v13 on v10

--- a/solution.py
+++ b/solution.py
@@ -23,7 +23,6 @@
 F32 = jnp.float32
 MIB = 1024 * 1024
 NT = (((1,), (1,)), ((), ()))
-IN_HBM = pl.BlockSpec(memory_space=pltpu.HBM)
 IN_SMEM = pl.BlockSpec(memory_space=pltpu.SMEM)
 
 
@@ -140,16 +139,10 @@
     )
 
 
-def attend(shares, squares, tables, pool_ref, kept, store):
+def attend(shares, squares, tables, pool_ref, store):
     cos_ref, sin_ref, cached_ref, own_ref = tables
-    keys_ref, sems = kept
     slots = pool_ref.shape[1]
     rows = cos_ref.shape[0]
-    copies = []
-    for head in range(KV_HEADS):
-        here = pool_ref.at[:, :, :, head * HEAD_DIM : (head + 1) * HEAD_DIM]
-        copies.append(pltpu.make_async_copy(here, keys_ref.at[head], sems.at[head]))
-        copies[-1].start()
     square = jnp.sum(squares.astype(F32), axis=0)
     square = square[:, 0:1] + square[:, HALF // 2 : HALF // 2 + 1]
     scale = lax.rsqrt(square / D + EPSILON)
@@ -177,22 +170,15 @@
         den = row_sum(weights)
         num = jnp.dot(weights.astype(BF), value_step, preferred_element_type=F32)
 
-        copies[head].wait()
-        keys = keys_ref[head, 0].reshape(slots * PAGE, HEAD_DIM)
-        values = keys_ref[head, 1].reshape(slots * PAGE, HEAD_DIM)
+        here = slice(head * HEAD_DIM, (head + 1) * HEAD_DIM)
+        keys = pool_ref[0, :, :, here].reshape(slots * PAGE, HEAD_DIM)
+        values = pool_ref[1, :, :, here].reshape(slots * PAGE, HEAD_DIM)
         scores = lax.dot_general(query, keys, NT, preferred_element_type=F32)
         weights = weight_of(scores).reshape(REPS * rows // 8, 8, slots * PAGE) * cached[None]
         weights = weights.reshape(REPS * rows, slots * PAGE)
         den = den + row_sum(weights)
         num = num + jnp.dot(weights.astype(BF), values, preferred_element_type=F32)
         store(head, num, den)
-
-
-def key_scratch(pool):
-    return [
-        pltpu.VMEM((KV_HEADS, 2) + pool.shape[1:3] + (HEAD_DIM,), BF),
-        pltpu.SemaphoreType.DMA((KV_HEADS,)),
-    ]
 
 
 def rope_tables(lengths, rows, steps):
@@ -290,8 +276,12 @@
     shares, *late = lax.optimization_barrier((shares, block_table, lengths, parents))
     cos, sin = rope_tables(late[1], rows, steps)
     tables = make_tables(*late, cache_pool.shape[1], rows, steps)
+    halves, _ = lax.optimization_barrier(((w_first, w_second), tables))
+    w_blocks[4] = jnp.concatenate(halves, axis=0)
+    w_blocks[6] = permute(w_blocks[4], "gy", 2)
+    w_blocks[5] = permute(w_blocks[4], "gy", 1)
     shares = exchange(shares, "gy")
-    beside = tables, cos, sin, w_blocks[2], w_blocks[3], w_first, w_second
+    beside = tables, cos, sin, w_blocks[2], w_blocks[3], w_blocks[4]
     shares, (tables, cos, sin, *_) = lax.optimization_barrier((shares, beside))
 
     def pack_shares(share_ref, x_ref, out_ref):
@@ -303,14 +293,10 @@
         "pack_shares", pack_shares, [((ny + 1, rows, HALF), BF)], (shares, x_own), micros=5
     )
     shares = gather_gx(shares)
-    w_blocks[4] = jnp.concatenate([w_first, w_second], axis=0)
-    w_late, _ = lax.optimization_barrier((w_blocks[4], shares[2]))
-    w_blocks[6] = permute(w_late, "gy", 2)
-    w_blocks[5] = permute(w_late, "gy", 1)
 
     def attention(*refs):
         a_refs, tables, pool_ref, outs = refs[:nx], refs[nx : nx + 4], refs[nx + 4], refs[nx + 5 :]
-        own_ref, pair_ref, keys_ref, sems, held, num_held, den_held = outs
+        own_ref, pair_ref, held, num_held, den_held = outs
         me = my("gx")
         core = me & 1
         for n, ref in enumerate(a_refs):
@@ -334,7 +320,6 @@
             held[:, ny],
             tables,
             pool_ref,
-            (keys_ref, sems),
             store,
         )
         for n, out in enumerate((own_ref, pair_ref)):
@@ -346,14 +331,12 @@
         attention,
         [(shape, BF), (shape, BF)],
         (*shares, cos, sin, *tables, cache_pool),
-        scratch=key_scratch(cache_pool)
-        + [
+        scratch=[
             pltpu.VMEM((nx,) + shares[0].shape, BF),
             pltpu.VMEM((KV_HEADS, REPS, 2, half, HEAD_DIM), F32),
             pltpu.VMEM((2, half, PAGE), F32),
         ],
         limit=24,
-        specs={nx + 4: IN_HBM},
     )
     w_late, _ = lax.optimization_barrier((w_blocks, own))
     w_blocks[7] = permute(w_late[6], "gy", 1)
@@ -566,8 +549,7 @@
     cos, sin = rope_tables(lengths, rows, steps)
 
     def attention(*refs):
-        g_ref, square_ref, tables, pool_ref = refs[0], refs[1], refs[2:6], refs[6]
-        out_ref, keys_ref, sems = refs[7:]
+        g_ref, square_ref, tables, pool_ref, out_ref = refs[0], refs[1], refs[2:6], *refs[6:]
 
         def store(head, num, den):
             den = high_low(den, PAGE)
@@ -581,7 +563,6 @@
             square_ref[...],
             tables,
             pool_ref,
-            (keys_ref, sems),
             store,
         )
 
@@ -591,9 +572,7 @@
         attention,
         [((HEADS, rows, WIDE), BF)],
         (shares, squares, cos, sin, *tables, cache_pool),
-        scratch=key_scratch(cache_pool),
         limit=24,
-        specs={6: IN_HBM},
     )
     num = terms[..., :HEAD_DIM].transpose(1, 0, 2).reshape(nx, part, ny, head_part)
     den = terms[..., HEAD_DIM :: PAGE // 2].transpose(1, 0, 2)

time: 116 us -> 118 us (1.017)
  waiting for transfers between devices: 40.1 us -> 42.4 us
  Pallas kernels: 10.9 us -> 9.16 us
    ppermute x32, waiting for transfers between devices: 31.2 us -> 33.4 us  [permute(): return lax.ppermute(values, axis, [(i, i ^ m) for i in range(count)])]
    pallas_call x20, Pallas kernels: 10.9 us -> 9.16 us  [run(): pl.pallas_call(kernel, out_shape=[jax.ShapeDtypeStruct(s, d) for s, d in...]
  transfers between devices with their start and end apart: 34 -> 34, of which waited for: 23 -> 20; matrix products, arithmetic and copies ran while one was open for 0% -> 0% of each run, Pallas kernels for 6% -> 4%
where the time goes in v13:
time: 118 us; the launch traced here: 117 us
  waiting for transfers between devices  42.4 us (36%)
  starting transfers between devices  37 us (31%)
  blocking collectives  26.6 us (23%)
  Pallas kernels  9.16 us (8%)
    ppermute x32, waiting for transfers between devices, permute(): return lax.ppermute(values, axis, [(i, i ^ m) for i in range(count)])  33.4 us
    all_to_all x2, blocking collectives, exchange(): return lax.all_to_all(values, axes, split_axis=0, concat_axis=0, tiled=True)  26.6 us
    ppermute x32, starting transfers between devices, permute(): return lax.ppermute(values, axis, [(i, i ^ m) for i in range(count)])  26.3 us
    all_to_all x2, starting transfers between devices, exchange(): return lax.all_to_all(values, axes, split_axis=0, concat_axis=0, tiled=True)  10.7 us
    pallas_call x20, Pallas kernels, run(): pl.pallas_call(kernel, out_shape=[jax.ShapeDtypeStruct(s, d) for s, d in...  9.16 us
    all_to_all x2, waiting for transfers between devices, exchange(): return lax.all_to_all(values, axes, split_axis=0, concat_axis=0, tiled=True)  8.96 us
  transfers between devices with their start and end apart: 34, of which 20 were waited for; matrix products, arithmetic and copies ran while one was open for 0% of the time, Pallas kernels for 4%

profile of v13, /device:TPU:0, one launch (start us, length us, event | category | flops | bytes accessed | tf_op | source)
XLA Modules:
  0.0 117.2 jit_solution(17415404313687935369)
XLA Ops:
  1.7 7.4 %all-to-all-start = ((bf16[8,144,128]{2,1,0:T(8,128)(2,1)}), bf16[8,144,128]{2,1,0:T(8,128)(2,1)S(1)}, u32[]{:S(2)}, u32[]{:S(2)}) async-start(bf16[8,144,128]{2,1,0:T(8,128)(2,1)} %get-tuple-element.43), calls=%async_computation | async-start | bytes 589824 | tf_op jit(solution)/shard_map/all_to_all | solution.py:45
  9.1 2.0 %collective-permute-start.3 = (bf16[576,256]{1,0:T(8,128)(2,1)S(1)}, bf16[576,256]{1,0:T(8,128)(2,1)S(1)}, u32[]{:S(2)}, u32[]{:S(2)}) collective-permute-start(bf16[576,256]{1,0:T(8,128)(2,1)S(1)} %bitcast.7), channel_id=1, source_target_pairs={{0,1},{1,0},{2,3},{3,2},{4,5},{5,4},{6,7},{7,6},{8,9},{9,8},{10,11... | collective-permute-start | bytes 884744 | tf_op jit(solution)/shard_map/ppermute | solution.py:56
  11.1 1.5 %collective-permute-start.2 = (bf16[576,256]{1,0:T(8,128)(2,1)S(1)}, bf16[576,256]{1,0:T(8,128)(2,1)S(1)}, u32[]{:S(2)}, u32[]{:S(2)}) collective-permute-start(bf16[576,256]{1,0:T(8,128)(2,1)S(1)} %bitcast.8), channel_id=1, source_target_pairs={{0,2},{1,3},{2,0},{3,1},{4,6},{5,7},{6,4},{7,5},{8,10},{9,11},{10,... | collective-permute-start | bytes 884744 | tf_op jit(solution)/shard_map/ppermute | solution.py:56
  12.6 2.4 %collective-permute-start.5 = (bf16[288,256]{1,0:T(8,128)(2,1)S(1)}, bf16[288,256]{1,0:T(8,128)(2,1)S(1)}, u32[]{:S(2)}, u32[]{:S(2)}) collective-permute-start(bf16[288,256]{1,0:T(8,128)(2,1)S(1)} %get-tuple-element.79), channel_id=1, source_target_pairs={{0,4},{1,5},{2,6},{3,7},{4,0},{5,1},{6,2},{7,3},{8,12},{9,13},{10,... | collective-permute-start | bytes 442376 | tf_op jit(solution)/shard_map/ppermute | solution.py:56
  15.0 5.2 %all-to-all-done.x_ref = bf16[8,144,128]{2,1,0:T(8,128)(2,1)S(1)} async-done(((bf16[8,144,128]{2,1,0:T(8,128)(2,1)}), bf16[8,144,128]{2,1,0:T(8,128)(2,1)S(1)}, u32[]{:S(2)}, u32[]{:S(2)}) %all-to-all-start) | async-done | bytes 294944 | tf_op jit(solution)/shard_map/all_to_all | solution.py:45
  21.4 1.9 %collective-permute-start.6 = (bf16[288,256]{1,0:T(8,128)(2,1)S(1)}, bf16[288,256]{1,0:T(8,128)(2,1)S(1)}, u32[]{:S(2)}, u32[]{:S(2)}) collective-permute-start(bf16[288,256]{1,0:T(8,128)(2,1)S(1)} %get-tuple-element.55), channel_id=1, source_target_pairs={{0,4},{1,5},{2,6},{3,7},{4,0},{5,1},{6,2},{7,3},{8,12},{9,13},{10,... | collective-permute-start | bytes 442376 | tf_op jit(solution)/shard_map/ppermute | solution.py:56
  23.2 1.5 %collective-permute-start.4 = (bf16[576,256]{1,0:T(8,128)(2,1)S(1)}, bf16[576,256]{1,0:T(8,128)(2,1)S(1)}, u32[]{:S(2)}, u32[]{:S(2)}) collective-permute-start(bf16[576,256]{1,0:T(8,128)(2,1)S(1)} %collective-permute-done.3.refs_1_), channel_id=1, source_target_pairs={{0,2},{1,3},{2,0},{3,1},{4,6},{5,7},{6,4},{7,5},{8,10},{9,11},{10,... | collective-permute-start | bytes 884744 | tf_op jit(solution)/shard_map/ppermute | solution.py:56
  24.7 1.6 %collective-permute-start.1 = (bf16[256,128]{1,0:T(8,128)(2,1)S(1)}, bf16[256,128]{1,0:T(8,128)(2,1)S(1)}, u32[]{:S(2)}, u32[]{:S(2)}) collective-permute-start(bf16[256,128]{1,0:T(8,128)(2,1)S(1)} %pair_sum.1), channel_id=1, source_target_pairs={{0,16},{8,24},{16,0},{24,8},{1,17},{9,25},{17,1},{25,9},{2,18},{10... | collective-permute-start | bytes 196616 | tf_op jit(solution)/shard_map/ppermute | solution.py:56
  26.5 2.6 %collective-permute-done.1.z2_ref = bf16[256,128]{1,0:T(8,128)(2,1)S(1)} collective-permute-done((bf16[256,128]{1,0:T(8,128)(2,1)S(1)}, bf16[256,128]{1,0:T(8,128)(2,1)S(1)}, u32[]{:S(2)}, u32[]{:S(2)}) %collective-permute-start.1) | collective-permute-done | bytes 65568 | tf_op jit(solution)/shard_map/ppermute | solution.py:56
  30.5 3.2 %collective-permute-done.6 = bf16[288,256]{1,0:T(8,128)(2,1)S(1)} collective-permute-done((bf16[288,256]{1,0:T(8,128)(2,1)S(1)}, bf16[288,256]{1,0:T(8,128)(2,1)S(1)}, u32[]{:S(2)}, u32[]{:S(2)}) %collective-permute-start.6) | collective-permute-done | bytes 147488 | tf_op jit(solution)/shard_map/ppermute | solution.py:56
  33.7 3.3 %all-to-all-start.1 = ((bf16[8,32,128]{2,1,0:T(8,128)(2,1)}), bf16[8,32,128]{2,1,0:T(8,128)(2,1)S(1)}, u32[]{:S(2)}, u32[]{:S(2)}) async-start(bf16[8,32,128]{2,1,0:T(8,128)(2,1)} %share_sum.1), calls=%async_computation.1 | async-start | bytes 131072 | tf_op jit(solution)/shard_map/all_to_all | solution.py:45
  37.1 2.0 %collective-permute-start.13 = (bf16[576,256]{1,0:T(8,128)(2,1)S(1)}, bf16[576,256]{1,0:T(8,128)(2,1)S(1)}, u32[]{:S(2)}, u32[]{:S(2)}) collective-permute-start(bf16[576,256]{1,0:T(8,128)(2,1)S(1)} %constant_dynamic-update-slice_fusion.refs_4_), channel_id=1, source_target_pairs={{0,1},{1,0},{2,3},{3,2},{4,5},{5,4},{6,7},{7,6},{8,9},{9,8},{10,11... | collective-permute-start | bytes 884744 | tf_op jit(solution)/shard_map/ppermute | solution.py:56
  39.1 1.5 %collective-permute-start.14 = (bf16[576,256]{1,0:T(8,128)(2,1)S(1)}, bf16[576,256]{1,0:T(8,128)(2,1)S(1)}, u32[]{:S(2)}, u32[]{:S(2)}) collective-permute-start(bf16[576,256]{1,0:T(8,128)(2,1)S(1)} %constant_dynamic-update-slice_fusion.refs_4_), channel_id=1, source_target_pairs={{0,2},{1,3},{2,0},{3,1},{4,6},{5,7},{6,4},{7,5},{8,10},{9,11},{10,... | collective-permute-start | bytes 884744 | tf_op jit(solution)/shard_map/ppermute | solution.py:56
  40.6 3.8 %all-to-all-done.1.share_ref = bf16[8,32,128]{2,1,0:T(8,128)(2,1)S(1)} async-done(((bf16[8,32,128]{2,1,0:T(8,128)(2,1)}), bf16[8,32,128]{2,1,0:T(8,128)(2,1)S(1)}, u32[]{:S(2)}, u32[]{:S(2)}) %all-to-all-start.1) | async-done | bytes 65568 | tf_op jit(solution)/shard_map/all_to_all | solution.py:45
  44.5 1.5 %collective-permute-start.8 = (bf16[9,32,128]{2,1,0:T(8,128)(2,1)S(1)}, bf16[9,32,128]{2,1,0:T(8,128)(2,1)S(1)}, u32[]{:S(2)}, u32[]{:S(2)}) collective-permute-start(bf16[9,32,128]{2,1,0:T(8,128)(2,1)S(1)} %pack_shares.1.refs_0_), channel_id=1, source_target_pairs={{0,16},{8,24},{16,0},{24,8},{1,17},{9,25},{17,1},{25,9},{2,18},{10... | collective-permute-start | bytes 221192 | tf_op jit(solution)/shard_map/ppermute | solution.py:56
  46.0 2.8 %collective-permute-done.8.refs_2_ = bf16[9,32,128]{2,1,0:T(8,128)(2,1)S(1)} collective-permute-done((bf16[9,32,128]{2,1,0:T(8,128)(2,1)S(1)}, bf16[9,32,128]{2,1,0:T(8,128)(2,1)S(1)}, u32[]{:S(2)}, u32[]{:S(2)}) %collective-permute-start.8) | collective-permute-done | bytes 73760 | tf_op jit(solution)/shard_map/ppermute | solution.py:56
  48.8 1.3 %collective-permute-done.9.refs_3_ = bf16[9,32,128]{2,1,0:T(8,128)(2,1)S(1)} collective-permute-done((bf16[9,32,128]{2,1,0:T(8,128)(2,1)S(1)}, bf16[9,32,128]{2,1,0:T(8,128)(2,1)S(1)}, u32[]{:S(2)}, u32[]{:S(2)}) %collective-permute-start.9) | collective-permute-done | bytes 73760 | tf_op jit(solution)/shard_map/ppermute | solution.py:56
  50.1 1.7 %attention.1 = (bf16[17,16,128]{2,1,0:T(8,128)(2,1)S(1)}, bf16[17,16,128]{2,1,0:T(8,128)(2,1)S(1)}) custom-call(bf16[9,32,128]{2,1,0:T(8,128)(2,1)S(1)} %pack_shares.1.refs_0_, bf16[9,32,128]{2,1,0:T(8,128)(2,1)S(1)} %collective-permute-done.7.refs_1_, bf16[9,32,128]{2,1,0:T(8,128)(2,1)S(1)} %collective-permute-done.8.refs_2_, ...), custom_call_target="tpu_custom_call" | custom-call | tf_op jit(solution)/shard_map/attention/pallas_call | solution.py:33
  53.6 1.5 %collective-permute-start.11 = (bf16[17,16,128]{2,1,0:T(8,128)(2,1)S(1)}, bf16[17,16,128]{2,1,0:T(8,128)(2,1)S(1)}, u32[]{:S(2)}, u32[]{:S(2)}) collective-permute-start(bf16[17,16,128]{2,1,0:T(8,128)(2,1)S(1)} %pair_terms.1.own_ref), channel_id=1, source_target_pairs={{0,16},{8,24},{16,0},{24,8},{1,17},{9,25},{17,1},{25,9},{2,18},{10... | collective-permute-start | bytes 208904 | tf_op jit(solution)/shard_map/ppermute | solution.py:56
  55.1 2.8 %collective-permute-done.11.across_ref = bf16[17,16,128]{2,1,0:T(8,128)(2,1)S(1)} collective-permute-done((bf16[17,16,128]{2,1,0:T(8,128)(2,1)S(1)}, bf16[17,16,128]{2,1,0:T(8,128)(2,1)S(1)}, u32[]{:S(2)}, u32[]{:S(2)}) %collective-permute-start.11) | collective-permute-done | bytes 69664 | tf_op jit(solution)/shard_map/ppermute | solution.py:56
  59.4 1.6 %collective-permute-done.15.refs_7_ = bf16[576,256]{1,0:T(8,128)(2,1)S(1)} collective-permute-done((bf16[576,256]{1,0:T(8,128)(2,1)S(1)}, bf16[576,256]{1,0:T(8,128)(2,1)S(1)}, u32[]{:S(2)}, u32[]{:S(2)}) %collective-permute-start.15) | collective-permute-done | bytes 294944 | tf_op jit(solution)/shard_map/ppermute | solution.py:56
  61.9 1.6 %collective-permute-start.17 = (f32[32,128]{1,0:T(8,128)S(1)}, f32[32,128]{1,0:T(8,128)S(1)}, u32[]{:S(2)}, u32[]{:S(2)}) collective-permute-start(f32[32,128]{1,0:T(8,128)S(1)} %get-tuple-element.67.refs_0_), channel_id=1, source_target_pairs={{0,16},{8,24},{16,0},{24,8},{1,17},{9,25},{17,1},{25,9},{2,18},{10... | collective-permute-start | bytes 49160 | tf_op jit(solution)/shard_map/ppermute | solution.py:56
  63.8 1.9 %collective-permute-done.17.refs_2_ = f32[32,128]{1,0:T(8,128)S(1)} collective-permute-done((f32[32,128]{1,0:T(8,128)S(1)}, f32[32,128]{1,0:T(8,128)S(1)}, u32[]{:S(2)}, u32[]{:S(2)}) %collective-permute-start.17) | collective-permute-done | bytes 16416 | tf_op jit(solution)/shard_map/ppermute | solution.py:56
  67.0 13.3 %all_to_all.20.ff_ref = bf16[8,144,128]{2,1,0:T(8,128)(2,1)S(1)} all-to-all(bf16[8,144,128]{2,1,0:T(8,128)(2,1)S(1)} %get-tuple-element.69), channel_id=1, replica_groups=mesh['gx'=4,'gy'=8] {'gy'}, dimensions={0} | all-to-all | bytes 589824 | tf_op jit(solution)/shard_map/all_to_all | solution.py:45
  83.5 1.5 %collective-permute-start.25 = (bf16[64,1024]{1,0:T(8,128)(2,1)S(1)}, bf16[64,1024]{1,0:T(8,128)(2,1)S(1)}, u32[]{:S(2)}, u32[]{:S(2)}) collective-permute-start(bf16[64,1024]{1,0:T(8,128)(2,1)S(1)} %pair_sum_ff.3), channel_id=1, source_target_pairs={{0,16},{8,24},{16,0},{24,8},{1,17},{9,25},{17,1},{25,9},{2,18},{10... | collective-permute-start | bytes 393224 | tf_op jit(solution)/shard_map/ppermute | solution.py:56
  85.0 4.9 %collective-permute-done.20.z2_ref = bf16[64,1280]{1,0:T(8,128)(2,1)S(1)} collective-permute-done((bf16[64,1280]{1,0:T(8,128)(2,1)S(1)}, bf16[64,1280]{1,0:T(8,128)(2,1)S(1)}, u32[]{:S(2)}, u32[]{:S(2)}) %collective-permute-start.20) | collective-permute-done | bytes 163872 | tf_op jit(solution)/shard_map/ppermute | solution.py:56
  90.7 1.8 %collective-permute-done.25.z2_ref = bf16[64,1024]{1,0:T(8,128)(2,1)S(1)} collective-permute-done((bf16[64,1024]{1,0:T(8,128)(2,1)S(1)}, bf16[64,1024]{1,0:T(8,128)(2,1)S(1)}, u32[]{:S(2)}, u32[]{:S(2)}) %collective-permute-start.25) | collective-permute-done | bytes 131104 | tf_op jit(solution)/shard_map/ppermute | solution.py:56
  93.3 1.7 %collective-permute-done.22.refs_2_ = bf16[64,640]{1,0:T(8,128)(2,1)S(1)} collective-permute-done((bf16[64,640]{1,0:T(8,128)(2,1)S(1)}, bf16[64,640]{1,0:T(8,128)(2,1)S(1)}, u32[]{:S(2)}, u32[]{:S(2)}) %collective-permute-start.22) | collective-permute-done | bytes 81952 | tf_op jit(solution)/shard_map/ppermute | solution.py:56
  95.6 1.4 %collective-permute-done.27.refs_6_ = bf16[64,512]{1,0:T(8,128)(2,1)S(1)} collective-permute-done((bf16[64,512]{1,0:T(8,128)(2,1)S(1)}, bf16[64,512]{1,0:T(8,128)(2,1)S(1)}, u32[]{:S(2)}, u32[]{:S(2)}) %collective-permute-start.27) | collective-permute-done | bytes 65568 | tf_op jit(solution)/shard_map/ppermute | solution.py:56
  97.0 1.2 %collective-permute-done.28.refs_7_ = bf16[64,512]{1,0:T(8,128)(2,1)S(1)} collective-permute-done((bf16[64,512]{1,0:T(8,128)(2,1)S(1)}, bf16[64,512]{1,0:T(8,128)(2,1)S(1)}, u32[]{:S(2)}, u32[]{:S(2)}) %collective-permute-start.28) | collective-permute-done | bytes 65568 | tf_op jit(solution)/shard_map/ppermute | solution.py:56
  99.0 13.3 %all_to_all.21.parts_ref = bf16[8,144,128]{2,1,0:T(8,128)(2,1)S(1)} all-to-all(bf16[8,144,128]{2,1,0:T(8,128)(2,1)S(1)} %project_down.1), channel_id=1, replica_groups=mesh['gx'=4,'gy'=8] {'gy'}, dimensions={0} | all-to-all | bytes 589824 | tf_op jit(solution)/shard_map/all_to_all | solution.py:45
  114.3 2.0 %collective-permute-done.30.refs_2_ = f32[32,128]{1,0:T(8,128)S(1)} collective-permute-done((f32[32,128]{1,0:T(8,128)S(1)}, f32[32,128]{1,0:T(8,128)S(1)}, u32[]{:S(2)}, u32[]{:S(2)}) %collective-permute-start.30) | collective-permute-done | bytes 16416 | tf_op jit(solution)/shard_map/ppermute | solution.py:56
  (91 shorter events, 18.4 us)
Async XLA Ops:
  1.7 18.5 %all-to-all-start = ((bf16[8,144,128]{2,1,0:T(8,128)(2,1)}), bf16[8,144,128]{2,1,0:T(8,128)(2,1)S(1)}, u32[]{:S(2)}, u32[]{:S(2)}) async-start(bf16[8,144,128]{2,1,0:T(8,128)(2,1)} %get-tuple-element.43), calls=%async_computation | async-start | bytes 589824 | tf_op jit(solution)/shard_map/all_to_all | solution.py:45
  9.1 12.3 %collective-permute-start.3 = (bf16[576,256]{1,0:T(8,128)(2,1)S(1)}, bf16[576,256]{1,0:T(8,128)(2,1)S(1)}, u32[]{:S(2)}, u32[]{:S(2)}) collective-permute-start(bf16[576,256]{1,0:T(8,128)(2,1)S(1)} %bitcast.7), channel_id=1, source_target_pairs={{0,1},{1,0},{2,3},{3,2},{4,5},{5,4},{6,7},{7,6},{8,9},{9,8},{10,11... | collective-permute-start | bytes 884744 | tf_op jit(solution)/shard_map/ppermute | solution.py:56
  11.1 29.5 %collective-permute-start.2 = (bf16[576,256]{1,0:T(8,128)(2,1)S(1)}, bf16[576,256]{1,0:T(8,128)(2,1)S(1)}, u32[]{:S(2)}, u32[]{:S(2)}) collective-permute-start(bf16[576,256]{1,0:T(8,128)(2,1)S(1)} %bitcast.8), channel_id=1, source_target_pairs={{0,2},{1,3},{2,0},{3,1},{4,6},{5,7},{6,4},{7,5},{8,10},{9,11},{10,... | collective-permute-start | bytes 884744 | tf_op jit(solution)/shard_map/ppermute | solution.py:56
  12.6 17.9 %collective-permute-start.5 = (bf16[288,256]{1,0:T(8,128)(2,1)S(1)}, bf16[288,256]{1,0:T(8,128)(2,1)S(1)}, u32[]{:S(2)}, u32[]{:S(2)}) collective-permute-start(bf16[288,256]{1,0:T(8,128)(2,1)S(1)} %get-tuple-element.79), channel_id=1, source_target_pairs={{0,4},{1,5},{2,6},{3,7},{4,0},{5,1},{6,2},{7,3},{8,12},{9,13},{10,... | collective-permute-start | bytes 442376 | tf_op jit(solution)/shard_map/ppermute | solution.py:56
  20.6 4.1 %collective-permute-start = (bf16[2,256,128]{2,1,0:T(8,128)(2,1)S(1)}, bf16[2,256,128]{2,1,0:T(8,128)(2,1)S(1)}, u32[]{:S(2)}, u32[]{:S(2)}) collective-permute-start(bf16[2,256,128]{2,1,0:T(8,128)(2,1)S(1)} %get-tuple-element.45), channel_id=1, source_target_pairs={{0,8},{8,0},{16,24},{24,16},{1,9},{9,1},{17,25},{25,17},{2,10},{10... | collective-permute-start | bytes 393224 | tf_op jit(solution)/shard_map/ppermute | solution.py:56
  21.4 12.3 %collective-permute-start.6 = (bf16[288,256]{1,0:T(8,128)(2,1)S(1)}, bf16[288,256]{1,0:T(8,128)(2,1)S(1)}, u32[]{:S(2)}, u32[]{:S(2)}) collective-permute-start(bf16[288,256]{1,0:T(8,128)(2,1)S(1)} %get-tuple-element.55), channel_id=1, source_target_pairs={{0,4},{1,5},{2,6},{3,7},{4,0},{5,1},{6,2},{7,3},{8,12},{9,13},{10,... | collective-permute-start | bytes 442376 | tf_op jit(solution)/shard_map/ppermute | solution.py:56
  23.2 17.3 %collective-permute-start.4 = (bf16[576,256]{1,0:T(8,128)(2,1)S(1)}, bf16[576,256]{1,0:T(8,128)(2,1)S(1)}, u32[]{:S(2)}, u32[]{:S(2)}) collective-permute-start(bf16[576,256]{1,0:T(8,128)(2,1)S(1)} %collective-permute-done.3.refs_1_), channel_id=1, source_target_pairs={{0,2},{1,3},{2,0},{3,1},{4,6},{5,7},{6,4},{7,5},{8,10},{9,11},{10,... | collective-permute-start | bytes 884744 | tf_op jit(solution)/shard_map/ppermute | solution.py:56
  24.7 4.3 %collective-permute-start.1 = (bf16[256,128]{1,0:T(8,128)(2,1)S(1)}, bf16[256,128]{1,0:T(8,128)(2,1)S(1)}, u32[]{:S(2)}, u32[]{:S(2)}) collective-permute-start(bf16[256,128]{1,0:T(8,128)(2,1)S(1)} %pair_sum.1), channel_id=1, source_target_pairs={{0,16},{8,24},{16,0},{24,8},{1,17},{9,25},{17,1},{25,9},{2,18},{10... | collective-permute-start | bytes 196616 | tf_op jit(solution)/shard_map/ppermute | solution.py:56
  33.7 10.7 %all-to-all-start.1 = ((bf16[8,32,128]{2,1,0:T(8,128)(2,1)}), bf16[8,32,128]{2,1,0:T(8,128)(2,1)S(1)}, u32[]{:S(2)}, u32[]{:S(2)}) async-start(bf16[8,32,128]{2,1,0:T(8,128)(2,1)} %share_sum.1), calls=%async_computation.1 | async-start | bytes 131072 | tf_op jit(solution)/shard_map/all_to_all | solution.py:45
  37.1 14.7 %collective-permute-start.13 = (bf16[576,256]{1,0:T(8,128)(2,1)S(1)}, bf16[576,256]{1,0:T(8,128)(2,1)S(1)}, u32[]{:S(2)}, u32[]{:S(2)}) collective-permute-start(bf16[576,256]{1,0:T(8,128)(2,1)S(1)} %constant_dynamic-update-slice_fusion.refs_4_), channel_id=1, source_target_pairs={{0,1},{1,0},{2,3},{3,2},{4,5},{5,4},{6,7},{7,6},{8,9},{9,8},{10,11... | collective-permute-start | bytes 884744 | tf_op jit(solution)/shard_map/ppermute | solution.py:56
  39.1 12.8 %collective-permute-start.14 = (bf16[576,256]{1,0:T(8,128)(2,1)S(1)}, bf16[576,256]{1,0:T(8,128)(2,1)S(1)}, u32[]{:S(2)}, u32[]{:S(2)}) collective-permute-start(bf16[576,256]{1,0:T(8,128)(2,1)S(1)} %constant_dynamic-update-slice_fusion.refs_4_), channel_id=1, source_target_pairs={{0,2},{1,3},{2,0},{3,1},{4,6},{5,7},{6,4},{7,5},{8,10},{9,11},{10,... | collective-permute-start | bytes 884744 | tf_op jit(solution)/shard_map/ppermute | solution.py:56
  44.5 4.4 %collective-permute-start.8 = (bf16[9,32,128]{2,1,0:T(8,128)(2,1)S(1)}, bf16[9,32,128]{2,1,0:T(8,128)(2,1)S(1)}, u32[]{:S(2)}, u32[]{:S(2)}) collective-permute-start(bf16[9,32,128]{2,1,0:T(8,128)(2,1)S(1)} %pack_shares.1.refs_0_), channel_id=1, source_target_pairs={{0,16},{8,24},{16,0},{24,8},{1,17},{9,25},{17,1},{25,9},{2,18},{10... | collective-permute-start | bytes 221192 | tf_op jit(solution)/shard_map/ppermute | solution.py:56
  46.0 2.8 %collective-permute-start.7 = (bf16[9,32,128]{2,1,0:T(8,128)(2,1)S(1)}, bf16[9,32,128]{2,1,0:T(8,128)(2,1)S(1)}, u32[]{:S(2)}, u32[]{:S(2)}) collective-permute-start(bf16[9,32,128]{2,1,0:T(8,128)(2,1)S(1)} %pack_shares.1.refs_0_), channel_id=1, source_target_pairs={{0,8},{8,0},{16,24},{24,16},{1,9},{9,1},{17,25},{25,17},{2,10},{10... | collective-permute-start | bytes 221192 | tf_op jit(solution)/shard_map/ppermute | solution.py:56
  48.8 1.3 %collective-permute-start.9 = (bf16[9,32,128]{2,1,0:T(8,128)(2,1)S(1)}, bf16[9,32,128]{2,1,0:T(8,128)(2,1)S(1)}, u32[]{:S(2)}, u32[]{:S(2)}) collective-permute-start(bf16[9,32,128]{2,1,0:T(8,128)(2,1)S(1)} %collective-permute-done.8.refs_2_), channel_id=1, source_target_pairs={{0,8},{8,0},{16,24},{24,16},{1,9},{9,1},{17,25},{25,17},{2,10},{10... | collective-permute-start | bytes 221192 | tf_op jit(solution)/shard_map/ppermute | solution.py:56
  51.9 9.1 %collective-permute-start.15 = (bf16[576,256]{1,0:T(8,128)(2,1)S(1)}, bf16[576,256]{1,0:T(8,128)(2,1)S(1)}, u32[]{:S(2)}, u32[]{:S(2)}) collective-permute-start(bf16[576,256]{1,0:T(8,128)(2,1)S(1)} %collective-permute-done.14.refs_6_), channel_id=1, source_target_pairs={{0,1},{1,0},{2,3},{3,2},{4,5},{5,4},{6,7},{7,6},{8,9},{9,8},{10,11... | collective-permute-start | bytes 884744 | tf_op jit(solution)/shard_map/ppermute | solution.py:56
  53.6 4.3 %collective-permute-start.11 = (bf16[17,16,128]{2,1,0:T(8,128)(2,1)S(1)}, bf16[17,16,128]{2,1,0:T(8,128)(2,1)S(1)}, u32[]{:S(2)}, u32[]{:S(2)}) collective-permute-start(bf16[17,16,128]{2,1,0:T(8,128)(2,1)S(1)} %pair_terms.1.own_ref), channel_id=1, source_target_pairs={{0,16},{8,24},{16,0},{24,8},{1,17},{9,25},{17,1},{25,9},{2,18},{10... | collective-permute-start | bytes 208904 | tf_op jit(solution)/shard_map/ppermute | solution.py:56
  58.1 1.3 %collective-permute-start.12 = (bf16[16,16,128]{2,1,0:T(8,128)(2,1)S(1)}, bf16[16,16,128]{2,1,0:T(8,128)(2,1)S(1)}, u32[]{:S(2)}, u32[]{:S(2)}) collective-permute-start(bf16[16,16,128]{2,1,0:T(8,128)(2,1)S(1)} %divide.1.own_ref), channel_id=1, source_target_pairs={{0,8},{8,0},{16,24},{24,16},{1,9},{9,1},{17,25},{25,17},{2,10},{10... | collective-permute-start | bytes 196616 | tf_op jit(solution)/shard_map/ppermute | solution.py:56
  61.8 1.9 %collective-permute-start.16 = (f32[32,128]{1,0:T(8,128)S(1)}, f32[32,128]{1,0:T(8,128)S(1)}, u32[]{:S(2)}, u32[]{:S(2)}) collective-permute-start(f32[32,128]{1,0:T(8,128)S(1)} %get-tuple-element.67.refs_0_), channel_id=1, source_target_pairs={{0,8},{8,0},{16,24},{24,16},{1,9},{9,1},{17,25},{25,17},{2,10},{10... | collective-permute-start | bytes 49160 | tf_op jit(solution)/shard_map/ppermute | solution.py:56
  61.9 3.8 %collective-permute-start.17 = (f32[32,128]{1,0:T(8,128)S(1)}, f32[32,128]{1,0:T(8,128)S(1)}, u32[]{:S(2)}, u32[]{:S(2)}) collective-permute-start(f32[32,128]{1,0:T(8,128)S(1)} %get-tuple-element.67.refs_0_), channel_id=1, source_target_pairs={{0,16},{8,24},{16,0},{24,8},{1,17},{9,25},{17,1},{25,9},{2,18},{10... | collective-permute-start | bytes 49160 | tf_op jit(solution)/shard_map/ppermute | solution.py:56
  63.5 3.2 %collective-permute-start.18 = (f32[32,128]{1,0:T(8,128)S(1)}, f32[32,128]{1,0:T(8,128)S(1)}, u32[]{:S(2)}, u32[]{:S(2)}) collective-permute-start(f32[32,128]{1,0:T(8,128)S(1)} %get-tuple-element.67.refs_0_), channel_id=1, source_target_pairs={{0,24},{8,16},{16,8},{24,0},{1,25},{9,17},{17,9},{25,1},{2,26},{10... | collective-permute-start | bytes 49160 | tf_op jit(solution)/shard_map/ppermute | solution.py:56
  81.0 1.7 %collective-permute-start.19 = (bf16[2,64,1280]{2,1,0:T(8,128)(2,1)S(1)}, bf16[2,64,1280]{2,1,0:T(8,128)(2,1)S(1)}, u32[]{:S(2)}, u32[]{:S(2)}) collective-permute-start(bf16[2,64,1280]{2,1,0:T(8,128)(2,1)S(1)} %get-tuple-element.71), channel_id=1, source_target_pairs={{0,8},{8,0},{16,24},{24,16},{1,9},{9,1},{17,25},{25,17},{2,10},{10... | collective-permute-start | bytes 983048 | tf_op jit(solution)/shard_map/ppermute | solution.py:56
  81.7 1.8 %collective-permute-start.24 = (bf16[2,64,1024]{2,1,0:T(8,128)(2,1)S(1)}, bf16[2,64,1024]{2,1,0:T(8,128)(2,1)S(1)}, u32[]{:S(2)}, u32[]{:S(2)}) collective-permute-start(bf16[2,64,1024]{2,1,0:T(8,128)(2,1)S(1)} %get-tuple-element.74), channel_id=1, source_target_pairs={{0,8},{8,0},{16,24},{24,16},{1,9},{9,1},{17,25},{25,17},{2,10},{10... | collective-permute-start | bytes 786440 | tf_op jit(solution)/shard_map/ppermute | solution.py:56
  82.8 7.1 %collective-permute-start.20 = (bf16[64,1280]{1,0:T(8,128)(2,1)S(1)}, bf16[64,1280]{1,0:T(8,128)(2,1)S(1)}, u32[]{:S(2)}, u32[]{:S(2)}) collective-permute-start(bf16[64,1280]{1,0:T(8,128)(2,1)S(1)} %pair_sum_ff.2), channel_id=1, source_target_pairs={{0,16},{8,24},{16,0},{24,8},{1,17},{9,25},{17,1},{25,9},{2,18},{10... | collective-permute-start | bytes 491528 | tf_op jit(solution)/shard_map/ppermute | solution.py:56
  83.5 9.0 %collective-permute-start.25 = (bf16[64,1024]{1,0:T(8,128)(2,1)S(1)}, bf16[64,1024]{1,0:T(8,128)(2,1)S(1)}, u32[]{:S(2)}, u32[]{:S(2)}) collective-permute-start(bf16[64,1024]{1,0:T(8,128)(2,1)S(1)} %pair_sum_ff.3), channel_id=1, source_target_pairs={{0,16},{8,24},{16,0},{24,8},{1,17},{9,25},{17,1},{25,9},{2,18},{10... | collective-permute-start | bytes 393224 | tf_op jit(solution)/shard_map/ppermute | solution.py:56
  90.0 5.1 %collective-permute-start.22 = (bf16[64,640]{1,0:T(8,128)(2,1)S(1)}, bf16[64,640]{1,0:T(8,128)(2,1)S(1)}, u32[]{:S(2)}, u32[]{:S(2)}) collective-permute-start(bf16[64,640]{1,0:T(8,128)(2,1)S(1)} %activate.2.refs_0_), channel_id=1, source_target_pairs={{0,16},{8,24},{16,0},{24,8},{1,17},{9,25},{17,1},{25,9},{2,18},{10... | collective-permute-start | bytes 245768 | tf_op jit(solution)/shard_map/ppermute | solution.py:56
  92.6 4.3 %collective-permute-start.27 = (bf16[64,512]{1,0:T(8,128)(2,1)S(1)}, bf16[64,512]{1,0:T(8,128)(2,1)S(1)}, u32[]{:S(2)}, u32[]{:S(2)}) collective-permute-start(bf16[64,512]{1,0:T(8,128)(2,1)S(1)} %activate.3.refs_4_), channel_id=1, source_target_pairs={{0,16},{8,24},{16,0},{24,8},{1,17},{9,25},{17,1},{25,9},{2,18},{10... | collective-permute-start | bytes 196616 | tf_op jit(solution)/shard_map/ppermute | solution.py:56
  93.3 4.9 %collective-permute-start.21 = (bf16[64,640]{1,0:T(8,128)(2,1)S(1)}, bf16[64,640]{1,0:T(8,128)(2,1)S(1)}, u32[]{:S(2)}, u32[]{:S(2)}) collective-permute-start(bf16[64,640]{1,0:T(8,128)(2,1)S(1)} %activate.2.refs_0_), channel_id=1, source_target_pairs={{0,8},{8,0},{16,24},{24,16},{1,9},{9,1},{17,25},{25,17},{2,10},{10... | collective-permute-start | bytes 245768 | tf_op jit(solution)/shard_map/ppermute | solution.py:56
  95.1 3.2 %collective-permute-start.23 = (bf16[64,640]{1,0:T(8,128)(2,1)S(1)}, bf16[64,640]{1,0:T(8,128)(2,1)S(1)}, u32[]{:S(2)}, u32[]{:S(2)}) collective-permute-start(bf16[64,640]{1,0:T(8,128)(2,1)S(1)} %collective-permute-done.22.refs_2_), channel_id=1, source_target_pairs={{0,8},{8,0},{16,24},{24,16},{1,9},{9,1},{17,25},{25,17},{2,10},{10... | collective-permute-start | bytes 245768 | tf_op jit(solution)/shard_map/ppermute | solution.py:56
  95.1 1.9 %collective-permute-start.26 = (bf16[64,512]{1,0:T(8,128)(2,1)S(1)}, bf16[64,512]{1,0:T(8,128)(2,1)S(1)}, u32[]{:S(2)}, u32[]{:S(2)}) collective-permute-start(bf16[64,512]{1,0:T(8,128)(2,1)S(1)} %activate.3.refs_4_), channel_id=1, source_target_pairs={{0,8},{8,0},{16,24},{24,16},{1,9},{9,1},{17,25},{25,17},{2,10},{10... | collective-permute-start | bytes 196616 | tf_op jit(solution)/shard_map/ppermute | solution.py:56
  112.5 1.9 %collective-permute-start.29 = (f32[32,128]{1,0:T(8,128)S(1)}, f32[32,128]{1,0:T(8,128)S(1)}, u32[]{:S(2)}, u32[]{:S(2)}) collective-permute-start(f32[32,128]{1,0:T(8,128)S(1)} %get-tuple-element.76.refs_0_), channel_id=1, source_target_pairs={{0,8},{8,0},{16,24},{24,16},{1,9},{9,1},{17,25},{25,17},{2,10},{10... | collective-permute-start | bytes 49160 | tf_op jit(solution)/shard_map/ppermute | solution.py:56
  112.5 3.9 %collective-permute-start.30 = (f32[32,128]{1,0:T(8,128)S(1)}, f32[32,128]{1,0:T(8,128)S(1)}, u32[]{:S(2)}, u32[]{:S(2)}) collective-permute-start(f32[32,128]{1,0:T(8,128)S(1)} %get-tuple-element.76.refs_0_), channel_id=1, source_target_pairs={{0,16},{8,24},{16,0},{24,8},{1,17},{9,25},{17,1},{25,9},{2,18},{10... | collective-permute-start | bytes 49160 | tf_op jit(solution)/shard_map/ppermute | solution.py:56
  113.2 3.3 %collective-permute-start.31 = (f32[32,128]{1,0:T(8,128)S(1)}, f32[32,128]{1,0:T(8,128)S(1)}, u32[]{:S(2)}, u32[]{:S(2)}) collective-permute-start(f32[32,128]{1,0:T(8,128)S(1)} %get-tuple-element.76.refs_0_), channel_id=1, source_target_pairs={{0,24},{8,16},{16,8},{24,0},{1,25},{9,17},{17,9},{25,1},{2,26},{10... | collective-permute-start | bytes 49160 | tf_op jit(solution)/shard_map/ppermute | solution.py:56
  (15 other events, 220.0 us)

commit v14 on v13

--- a/solution.py
+++ b/solution.py
@@ -276,12 +276,8 @@
     shares, *late = lax.optimization_barrier((shares, block_table, lengths, parents))
     cos, sin = rope_tables(late[1], rows, steps)
     tables = make_tables(*late, cache_pool.shape[1], rows, steps)
-    halves, _ = lax.optimization_barrier(((w_first, w_second), tables))
-    w_blocks[4] = jnp.concatenate(halves, axis=0)
-    w_blocks[6] = permute(w_blocks[4], "gy", 2)
-    w_blocks[5] = permute(w_blocks[4], "gy", 1)
     shares = exchange(shares, "gy")
-    beside = tables, cos, sin, w_blocks[2], w_blocks[3], w_blocks[4]
+    beside = tables, cos, sin, w_blocks[2], w_blocks[3], w_first, w_second
     shares, (tables, cos, sin, *_) = lax.optimization_barrier((shares, beside))
 
     def pack_shares(share_ref, x_ref, out_ref):
@@ -293,6 +289,10 @@
         "pack_shares", pack_shares, [((ny + 1, rows, HALF), BF)], (shares, x_own), micros=5
     )
     shares = gather_gx(shares)
+    w_blocks[4] = jnp.concatenate([w_first, w_second], axis=0)
+    w_late, _ = lax.optimization_barrier((w_blocks[4], shares[2]))
+    w_blocks[6] = permute(w_late, "gy", 2)
+    w_blocks[5] = permute(w_late, "gy", 1)
 
     def attention(*refs):
         a_refs, tables, pool_ref, outs = refs[:nx], refs[nx : nx + 4], refs[nx + 4], refs[nx + 5 :]
@@ -419,7 +419,7 @@
 
     groups = ny // nx
 
-    cut = (hidden // 128 + 1) // 2 * 128
+    cut = hidden // 384 * 256
     column_parts = (0, cut), (cut, hidden)
 
     def gate_up(start, end):

time: 118 us -> 115 us (0.975)
  waiting for transfers between devices: 42.4 us -> 41 us
    ppermute x32, waiting for transfers between devices: 33.4 us -> 32 us  [permute(): return lax.ppermute(values, axis, [(i, i ^ m) for i in range(count)])]
  transfers between devices with their start and end apart: 34 -> 34, of which waited for: 20 -> 23; matrix products, arithmetic and copies ran while one was open for 0% -> 0% of each run, Pallas kernels for 4% -> 4%
where the time goes in v14:
time: 115 us
  waiting for transfers between devices  41 us (36%)
  starting transfers between devices  36.4 us (32%)
  blocking collectives  26.4 us (23%)
  Pallas kernels  9.18 us (8%)
    ppermute x32, waiting for transfers between devices, permute(): return lax.ppermute(values, axis, [(i, i ^ m) for i in range(count)])  32 us
    all_to_all x2, blocking collectives, exchange(): return lax.all_to_all(values, axes, split_axis=0, concat_axis=0, tiled=True)  26.4 us
    ppermute x32, starting transfers between devices, permute(): return lax.ppermute(values, axis, [(i, i ^ m) for i in range(count)])  25.7 us
    all_to_all x2, starting transfers between devices, exchange(): return lax.all_to_all(values, axes, split_axis=0, concat_axis=0, tiled=True)  10.7 us
    pallas_call x20, Pallas kernels, run(): pl.pallas_call(kernel, out_shape=[jax.ShapeDtypeStruct(s, d) for s, d in...  9.18 us
    all_to_all x2, waiting for transfers between devices, exchange(): return lax.all_to_all(values, axes, split_axis=0, concat_axis=0, tiled=True)  8.95 us
  transfers between devices with their start and end apart: 34, of which 23 were waited for; matrix products, arithmetic and copies ran while one was open for 0% of the time, Pallas kernels for 4%

profile of v14, /device:TPU:0, one launch (start us, length us, event | category | flops | bytes accessed | tf_op | source)
XLA Modules:
  0.0 115.0 jit_solution(8759637127033420581)
XLA Ops:
  1.7 7.4 %all-to-all-start = ((bf16[8,144,128]{2,1,0:T(8,128)(2,1)}), bf16[8,144,128]{2,1,0:T(8,128)(2,1)S(1)}, u32[]{:S(2)}, u32[]{:S(2)}) async-start(bf16[8,144,128]{2,1,0:T(8,128)(2,1)} %get-tuple-element.42), calls=%async_computation | async-start | bytes 589824 | tf_op jit(solution)/shard_map/all_to_all | solution.py:45
  9.1 2.1 %collective-permute-start.3 = (bf16[576,256]{1,0:T(8,128)(2,1)S(1)}, bf16[576,256]{1,0:T(8,128)(2,1)S(1)}, u32[]{:S(2)}, u32[]{:S(2)}) collective-permute-start(bf16[576,256]{1,0:T(8,128)(2,1)S(1)} %bitcast.7), channel_id=1, source_target_pairs={{0,1},{1,0},{2,3},{3,2},{4,5},{5,4},{6,7},{7,6},{8,9},{9,8},{10,11... | collective-permute-start | bytes 884744 | tf_op jit(solution)/shard_map/ppermute | solution.py:56
  11.2 1.5 %collective-permute-start.2 = (bf16[576,256]{1,0:T(8,128)(2,1)S(1)}, bf16[576,256]{1,0:T(8,128)(2,1)S(1)}, u32[]{:S(2)}, u32[]{:S(2)}) collective-permute-start(bf16[576,256]{1,0:T(8,128)(2,1)S(1)} %bitcast.8), channel_id=1, source_target_pairs={{0,2},{1,3},{2,0},{3,1},{4,6},{5,7},{6,4},{7,5},{8,10},{9,11},{10,... | collective-permute-start | bytes 884744 | tf_op jit(solution)/shard_map/ppermute | solution.py:56
  12.6 2.4 %collective-permute-start.5 = (bf16[288,256]{1,0:T(8,128)(2,1)S(1)}, bf16[288,256]{1,0:T(8,128)(2,1)S(1)}, u32[]{:S(2)}, u32[]{:S(2)}) collective-permute-start(bf16[288,256]{1,0:T(8,128)(2,1)S(1)} %get-tuple-element.77), channel_id=1, source_target_pairs={{0,4},{1,5},{2,6},{3,7},{4,0},{5,1},{6,2},{7,3},{8,12},{9,13},{10,... | collective-permute-start | bytes 442376 | tf_op jit(solution)/shard_map/ppermute | solution.py:56
  15.1 5.0 %all-to-all-done.x_ref = bf16[8,144,128]{2,1,0:T(8,128)(2,1)S(1)} async-done(((bf16[8,144,128]{2,1,0:T(8,128)(2,1)}), bf16[8,144,128]{2,1,0:T(8,128)(2,1)S(1)}, u32[]{:S(2)}, u32[]{:S(2)}) %all-to-all-start) | async-done | bytes 294944 | tf_op jit(solution)/shard_map/all_to_all | solution.py:45
  21.4 1.9 %collective-permute-start.6 = (bf16[288,256]{1,0:T(8,128)(2,1)S(1)}, bf16[288,256]{1,0:T(8,128)(2,1)S(1)}, u32[]{:S(2)}, u32[]{:S(2)}) collective-permute-start(bf16[288,256]{1,0:T(8,128)(2,1)S(1)} %get-tuple-element.54), channel_id=1, source_target_pairs={{0,4},{1,5},{2,6},{3,7},{4,0},{5,1},{6,2},{7,3},{8,12},{9,13},{10,... | collective-permute-start | bytes 442376 | tf_op jit(solution)/shard_map/ppermute | solution.py:56
  23.2 1.5 %collective-permute-start.4 = (bf16[576,256]{1,0:T(8,128)(2,1)S(1)}, bf16[576,256]{1,0:T(8,128)(2,1)S(1)}, u32[]{:S(2)}, u32[]{:S(2)}) collective-permute-start(bf16[576,256]{1,0:T(8,128)(2,1)S(1)} %collective-permute-done.3.refs_1_), channel_id=1, source_target_pairs={{0,2},{1,3},{2,0},{3,1},{4,6},{5,7},{6,4},{7,5},{8,10},{9,11},{10,... | collective-permute-start | bytes 884744 | tf_op jit(solution)/shard_map/ppermute | solution.py:56
  24.7 1.6 %collective-permute-start.1 = (bf16[256,128]{1,0:T(8,128)(2,1)S(1)}, bf16[256,128]{1,0:T(8,128)(2,1)S(1)}, u32[]{:S(2)}, u32[]{:S(2)}) collective-permute-start(bf16[256,128]{1,0:T(8,128)(2,1)S(1)} %pair_sum.1), channel_id=1, source_target_pairs={{0,16},{8,24},{16,0},{24,8},{1,17},{9,25},{17,1},{25,9},{2,18},{10... | collective-permute-start | bytes 196616 | tf_op jit(solution)/shard_map/ppermute | solution.py:56
  26.5 2.6 %collective-permute-done.1.z2_ref = bf16[256,128]{1,0:T(8,128)(2,1)S(1)} collective-permute-done((bf16[256,128]{1,0:T(8,128)(2,1)S(1)}, bf16[256,128]{1,0:T(8,128)(2,1)S(1)}, u32[]{:S(2)}, u32[]{:S(2)}) %collective-permute-start.1) | collective-permute-done | bytes 65568 | tf_op jit(solution)/shard_map/ppermute | solution.py:56
  29.7 3.3 %all-to-all-start.1 = ((bf16[8,32,128]{2,1,0:T(8,128)(2,1)}), bf16[8,32,128]{2,1,0:T(8,128)(2,1)S(1)}, u32[]{:S(2)}, u32[]{:S(2)}) async-start(bf16[8,32,128]{2,1,0:T(8,128)(2,1)} %share_sum.1), calls=%async_computation.1 | async-start | bytes 131072 | tf_op jit(solution)/shard_map/all_to_all | solution.py:45
  33.9 2.1 %collective-permute-done.4.refs_3_ = bf16[576,256]{1,0:T(8,128)(2,1)S(1)} collective-permute-done((bf16[576,256]{1,0:T(8,128)(2,1)S(1)}, bf16[576,256]{1,0:T(8,128)(2,1)S(1)}, u32[]{:S(2)}, u32[]{:S(2)}) %collective-permute-start.4) | collective-permute-done | bytes 294944 | tf_op jit(solution)/shard_map/ppermute | solution.py:56
  36.0 3.9 %all-to-all-done.1.share_ref = bf16[8,32,128]{2,1,0:T(8,128)(2,1)S(1)} async-done(((bf16[8,32,128]{2,1,0:T(8,128)(2,1)}), bf16[8,32,128]{2,1,0:T(8,128)(2,1)S(1)}, u32[]{:S(2)}, u32[]{:S(2)}) %all-to-all-start.1) | async-done | bytes 65568 | tf_op jit(solution)/shard_map/all_to_all | solution.py:45
  40.0 1.5 %collective-permute-start.8 = (bf16[9,32,128]{2,1,0:T(8,128)(2,1)S(1)}, bf16[9,32,128]{2,1,0:T(8,128)(2,1)S(1)}, u32[]{:S(2)}, u32[]{:S(2)}) collective-permute-start(bf16[9,32,128]{2,1,0:T(8,128)(2,1)S(1)} %pack_shares.1.refs_0_), channel_id=1, source_target_pairs={{0,16},{8,24},{16,0},{24,8},{1,17},{9,25},{17,1},{25,9},{2,18},{10... | collective-permute-start | bytes 221192 | tf_op jit(solution)/shard_map/ppermute | solution.py:56
  41.5 2.8 %collective-permute-done.8.refs_2_ = bf16[9,32,128]{2,1,0:T(8,128)(2,1)S(1)} collective-permute-done((bf16[9,32,128]{2,1,0:T(8,128)(2,1)S(1)}, bf16[9,32,128]{2,1,0:T(8,128)(2,1)S(1)}, u32[]{:S(2)}, u32[]{:S(2)}) %collective-permute-start.8) | collective-permute-done | bytes 73760 | tf_op jit(solution)/shard_map/ppermute | solution.py:56
  44.6 1.0 collective-permute-start.13
  47.0 1.7 %attention.1 = (bf16[17,16,128]{2,1,0:T(8,128)(2,1)S(1)}, bf16[17,16,128]{2,1,0:T(8,128)(2,1)S(1)}) custom-call(bf16[9,32,128]{2,1,0:T(8,128)(2,1)S(1)} %pack_shares.1.refs_0_, bf16[9,32,128]{2,1,0:T(8,128)(2,1)S(1)} %collective-permute-done.7.refs_1_, bf16[9,32,128]{2,1,0:T(8,128)(2,1)S(1)} %collective-permute-done.8.refs_2_, ...), custom_call_target="tpu_custom_call" | custom-call | tf_op jit(solution)/shard_map/attention/pallas_call | solution.py:33
  48.8 2.3 %collective-permute-done.14.refs_6_ = bf16[576,256]{1,0:T(8,128)(2,1)S(1)} collective-permute-done((bf16[576,256]{1,0:T(8,128)(2,1)S(1)}, bf16[576,256]{1,0:T(8,128)(2,1)S(1)}, u32[]{:S(2)}, u32[]{:S(2)}) %collective-permute-start.14) | collective-permute-done | bytes 294944 | tf_op jit(solution)/shard_map/ppermute | solution.py:56
  51.3 1.0 collective-permute-start.15
  52.3 1.3 %collective-permute-done.10.pair_ref = bf16[17,16,128]{2,1,0:T(8,128)(2,1)S(1)} collective-permute-done((bf16[17,16,128]{2,1,0:T(8,128)(2,1)S(1)}, bf16[17,16,128]{2,1,0:T(8,128)(2,1)S(1)}, u32[]{:S(2)}, u32[]{:S(2)}) %collective-permute-start.10) | collective-permute-done | bytes 69664 | tf_op jit(solution)/shard_map/ppermute | solution.py:56
  53.7 1.5 %collective-permute-start.11 = (bf16[17,16,128]{2,1,0:T(8,128)(2,1)S(1)}, bf16[17,16,128]{2,1,0:T(8,128)(2,1)S(1)}, u32[]{:S(2)}, u32[]{:S(2)}) collective-permute-start(bf16[17,16,128]{2,1,0:T(8,128)(2,1)S(1)} %pair_terms.1.own_ref), channel_id=1, source_target_pairs={{0,16},{8,24},{16,0},{24,8},{1,17},{9,25},{17,1},{25,9},{2,18},{10... | collective-permute-start | bytes 208904 | tf_op jit(solution)/shard_map/ppermute | solution.py:56
  55.2 2.8 %collective-permute-done.11.across_ref = bf16[17,16,128]{2,1,0:T(8,128)(2,1)S(1)} collective-permute-done((bf16[17,16,128]{2,1,0:T(8,128)(2,1)S(1)}, bf16[17,16,128]{2,1,0:T(8,128)(2,1)S(1)}, u32[]{:S(2)}, u32[]{:S(2)}) %collective-permute-start.11) | collective-permute-done | bytes 69664 | tf_op jit(solution)/shard_map/ppermute | solution.py:56
  58.3 1.2 %collective-permute-done.12.other_ref = bf16[16,16,128]{2,1,0:T(8,128)(2,1)S(1)} collective-permute-done((bf16[16,16,128]{2,1,0:T(8,128)(2,1)S(1)}, bf16[16,16,128]{2,1,0:T(8,128)(2,1)S(1)}, u32[]{:S(2)}, u32[]{:S(2)}) %collective-permute-start.12) | collective-permute-done | bytes 65568 | tf_op jit(solution)/shard_map/ppermute | solution.py:56
  60.4 1.3 %collective-permute-start.18 = (f32[32,128]{1,0:T(8,128)S(1)}, f32[32,128]{1,0:T(8,128)S(1)}, u32[]{:S(2)}, u32[]{:S(2)}) collective-permute-start(f32[32,128]{1,0:T(8,128)S(1)} %get-tuple-element.65.refs_0_), channel_id=1, source_target_pairs={{0,24},{8,16},{16,8},{24,0},{1,25},{9,17},{17,9},{25,1},{2,26},{10... | collective-permute-start | bytes 49160 | tf_op jit(solution)/shard_map/ppermute | solution.py:56
  62.3 1.3 %collective-permute-done.18.refs_3_ = f32[32,128]{1,0:T(8,128)S(1)} collective-permute-done((f32[32,128]{1,0:T(8,128)S(1)}, f32[32,128]{1,0:T(8,128)S(1)}, u32[]{:S(2)}, u32[]{:S(2)}) %collective-permute-start.18) | collective-permute-done | bytes 16416 | tf_op jit(solution)/shard_map/ppermute | solution.py:56
  63.6 1.9 %collective-permute-done.17.refs_2_ = f32[32,128]{1,0:T(8,128)S(1)} collective-permute-done((f32[32,128]{1,0:T(8,128)S(1)}, f32[32,128]{1,0:T(8,128)S(1)}, u32[]{:S(2)}, u32[]{:S(2)}) %collective-permute-start.17) | collective-permute-done | bytes 16416 | tf_op jit(solution)/shard_map/ppermute | solution.py:56
  65.8 13.1 %all_to_all.20.ff_ref = bf16[8,144,128]{2,1,0:T(8,128)(2,1)S(1)} all-to-all(bf16[8,144,128]{2,1,0:T(8,128)(2,1)S(1)} %get-tuple-element.67), channel_id=1, replica_groups=mesh['gx'=4,'gy'=8] {'gy'}, dimensions={0} | all-to-all | bytes 589824 | tf_op jit(solution)/shard_map/all_to_all | solution.py:45
  82.3 1.4 %collective-permute-start.25 = (bf16[64,768]{1,0:T(8,128)(2,1)S(1)}, bf16[64,768]{1,0:T(8,128)(2,1)S(1)}, u32[]{:S(2)}, u32[]{:S(2)}) collective-permute-start(bf16[64,768]{1,0:T(8,128)(2,1)S(1)} %pair_sum_ff.3), channel_id=1, source_target_pairs={{0,16},{8,24},{16,0},{24,8},{1,17},{9,25},{17,1},{25,9},{2,18},{10... | collective-permute-start | bytes 294920 | tf_op jit(solution)/shard_map/ppermute | solution.py:56
  83.7 5.6 %collective-permute-done.20.z2_ref = bf16[64,1536]{1,0:T(8,128)(2,1)S(1)} collective-permute-done((bf16[64,1536]{1,0:T(8,128)(2,1)S(1)}, bf16[64,1536]{1,0:T(8,128)(2,1)S(1)}, u32[]{:S(2)}, u32[]{:S(2)}) %collective-permute-start.20) | collective-permute-done | bytes 196640 | tf_op jit(solution)/shard_map/ppermute | solution.py:56
  90.7 1.0 collective-permute-start.27
  91.7 2.5 %collective-permute-done.22.refs_2_ = bf16[64,768]{1,0:T(8,128)(2,1)S(1)} collective-permute-done((bf16[64,768]{1,0:T(8,128)(2,1)S(1)}, bf16[64,768]{1,0:T(8,128)(2,1)S(1)}, u32[]{:S(2)}, u32[]{:S(2)}) %collective-permute-start.22) | collective-permute-done | bytes 98336 | tf_op jit(solution)/shard_map/ppermute | solution.py:56
  96.9 13.3 %all_to_all.21.parts_ref = bf16[8,144,128]{2,1,0:T(8,128)(2,1)S(1)} all-to-all(bf16[8,144,128]{2,1,0:T(8,128)(2,1)S(1)} %project_down.1), channel_id=1, replica_groups=mesh['gx'=4,'gy'=8] {'gy'}, dimensions={0} | all-to-all | bytes 589824 | tf_op jit(solution)/shard_map/all_to_all | solution.py:45
  112.2 1.3 %collective-permute-done.31.refs_3_ = f32[32,128]{1,0:T(8,128)S(1)} collective-permute-done((f32[32,128]{1,0:T(8,128)S(1)}, f32[32,128]{1,0:T(8,128)S(1)}, u32[]{:S(2)}, u32[]{:S(2)}) %collective-permute-start.31) | collective-permute-done | bytes 16416 | tf_op jit(solution)/shard_map/ppermute | solution.py:56
  (91 shorter events, 18.8 us)
Async XLA Ops:
  1.7 18.5 %all-to-all-start = ((bf16[8,144,128]{2,1,0:T(8,128)(2,1)}), bf16[8,144,128]{2,1,0:T(8,128)(2,1)S(1)}, u32[]{:S(2)}, u32[]{:S(2)}) async-start(bf16[8,144,128]{2,1,0:T(8,128)(2,1)} %get-tuple-element.42), calls=%async_computation | async-start | bytes 589824 | tf_op jit(solution)/shard_map/all_to_all | solution.py:45
  9.1 12.3 %collective-permute-start.3 = (bf16[576,256]{1,0:T(8,128)(2,1)S(1)}, bf16[576,256]{1,0:T(8,128)(2,1)S(1)}, u32[]{:S(2)}, u32[]{:S(2)}) collective-permute-start(bf16[576,256]{1,0:T(8,128)(2,1)S(1)} %bitcast.7), channel_id=1, source_target_pairs={{0,1},{1,0},{2,3},{3,2},{4,5},{5,4},{6,7},{7,6},{8,9},{9,8},{10,11... | collective-permute-start | bytes 884744 | tf_op jit(solution)/shard_map/ppermute | solution.py:56
  11.2 22.7 %collective-permute-start.2 = (bf16[576,256]{1,0:T(8,128)(2,1)S(1)}, bf16[576,256]{1,0:T(8,128)(2,1)S(1)}, u32[]{:S(2)}, u32[]{:S(2)}) collective-permute-start(bf16[576,256]{1,0:T(8,128)(2,1)S(1)} %bitcast.8), channel_id=1, source_target_pairs={{0,2},{1,3},{2,0},{3,1},{4,6},{5,7},{6,4},{7,5},{8,10},{9,11},{10,... | collective-permute-start | bytes 884744 | tf_op jit(solution)/shard_map/ppermute | solution.py:56
  12.6 20.4 %collective-permute-start.5 = (bf16[288,256]{1,0:T(8,128)(2,1)S(1)}, bf16[288,256]{1,0:T(8,128)(2,1)S(1)}, u32[]{:S(2)}, u32[]{:S(2)}) collective-permute-start(bf16[288,256]{1,0:T(8,128)(2,1)S(1)} %get-tuple-element.77), channel_id=1, source_target_pairs={{0,4},{1,5},{2,6},{3,7},{4,0},{5,1},{6,2},{7,3},{8,12},{9,13},{10,... | collective-permute-start | bytes 442376 | tf_op jit(solution)/shard_map/ppermute | solution.py:56
  20.6 4.1 %collective-permute-start = (bf16[2,256,128]{2,1,0:T(8,128)(2,1)S(1)}, bf16[2,256,128]{2,1,0:T(8,128)(2,1)S(1)}, u32[]{:S(2)}, u32[]{:S(2)}) collective-permute-start(bf16[2,256,128]{2,1,0:T(8,128)(2,1)S(1)} %get-tuple-element.44), channel_id=1, source_target_pairs={{0,8},{8,0},{16,24},{24,16},{1,9},{9,1},{17,25},{25,17},{2,10},{10... | collective-permute-start | bytes 393224 | tf_op jit(solution)/shard_map/ppermute | solution.py:56
  21.4 12.5 %collective-permute-start.6 = (bf16[288,256]{1,0:T(8,128)(2,1)S(1)}, bf16[288,256]{1,0:T(8,128)(2,1)S(1)}, u32[]{:S(2)}, u32[]{:S(2)}) collective-permute-start(bf16[288,256]{1,0:T(8,128)(2,1)S(1)} %get-tuple-element.54), channel_id=1, source_target_pairs={{0,4},{1,5},{2,6},{3,7},{4,0},{5,1},{6,2},{7,3},{8,12},{9,13},{10,... | collective-permute-start | bytes 442376 | tf_op jit(solution)/shard_map/ppermute | solution.py:56
  23.2 12.8 %collective-permute-start.4 = (bf16[576,256]{1,0:T(8,128)(2,1)S(1)}, bf16[576,256]{1,0:T(8,128)(2,1)S(1)}, u32[]{:S(2)}, u32[]{:S(2)}) collective-permute-start(bf16[576,256]{1,0:T(8,128)(2,1)S(1)} %collective-permute-done.3.refs_1_), channel_id=1, source_target_pairs={{0,2},{1,3},{2,0},{3,1},{4,6},{5,7},{6,4},{7,5},{8,10},{9,11},{10,... | collective-permute-start | bytes 884744 | tf_op jit(solution)/shard_map/ppermute | solution.py:56
  24.7 4.3 %collective-permute-start.1 = (bf16[256,128]{1,0:T(8,128)(2,1)S(1)}, bf16[256,128]{1,0:T(8,128)(2,1)S(1)}, u32[]{:S(2)}, u32[]{:S(2)}) collective-permute-start(bf16[256,128]{1,0:T(8,128)(2,1)S(1)} %pair_sum.1), channel_id=1, source_target_pairs={{0,16},{8,24},{16,0},{24,8},{1,17},{9,25},{17,1},{25,9},{2,18},{10... | collective-permute-start | bytes 196616 | tf_op jit(solution)/shard_map/ppermute | solution.py:56
  29.7 10.2 %all-to-all-start.1 = ((bf16[8,32,128]{2,1,0:T(8,128)(2,1)}), bf16[8,32,128]{2,1,0:T(8,128)(2,1)S(1)}, u32[]{:S(2)}, u32[]{:S(2)}) async-start(bf16[8,32,128]{2,1,0:T(8,128)(2,1)} %share_sum.1), calls=%async_computation.1 | async-start | bytes 131072 | tf_op jit(solution)/shard_map/all_to_all | solution.py:45
  40.0 4.4 %collective-permute-start.8 = (bf16[9,32,128]{2,1,0:T(8,128)(2,1)S(1)}, bf16[9,32,128]{2,1,0:T(8,128)(2,1)S(1)}, u32[]{:S(2)}, u32[]{:S(2)}) collective-permute-start(bf16[9,32,128]{2,1,0:T(8,128)(2,1)S(1)} %pack_shares.1.refs_0_), channel_id=1, source_target_pairs={{0,16},{8,24},{16,0},{24,8},{1,17},{9,25},{17,1},{25,9},{2,18},{10... | collective-permute-start | bytes 221192 | tf_op jit(solution)/shard_map/ppermute | solution.py:56
  44.4 6.7 %collective-permute-start.14 = (bf16[576,256]{1,0:T(8,128)(2,1)S(1)}, bf16[576,256]{1,0:T(8,128)(2,1)S(1)}, u32[]{:S(2)}, u32[]{:S(2)}) collective-permute-start(bf16[576,256]{1,0:T(8,128)(2,1)S(1)} %constant_dynamic-update-slice_fusion.refs_4_), channel_id=1, source_target_pairs={{0,2},{1,3},{2,0},{3,1},{4,6},{5,7},{6,4},{7,5},{8,10},{9,11},{10,... | collective-permute-start | bytes 884744 | tf_op jit(solution)/shard_map/ppermute | solution.py:56
  44.6 6.7 %collective-permute-start.13 = (bf16[576,256]{1,0:T(8,128)(2,1)S(1)}, bf16[576,256]{1,0:T(8,128)(2,1)S(1)}, u32[]{:S(2)}, u32[]{:S(2)}) collective-permute-start(bf16[576,256]{1,0:T(8,128)(2,1)S(1)} %constant_dynamic-update-slice_fusion.refs_4_), channel_id=1, source_target_pairs={{0,1},{1,0},{2,3},{3,2},{4,5},{5,4},{6,7},{7,6},{8,9},{9,8},{10,11... | collective-permute-start | bytes 884744 | tf_op jit(solution)/shard_map/ppermute | solution.py:56
  45.6 1.3 %collective-permute-start.7 = (bf16[9,32,128]{2,1,0:T(8,128)(2,1)S(1)}, bf16[9,32,128]{2,1,0:T(8,128)(2,1)S(1)}, u32[]{:S(2)}, u32[]{:S(2)}) collective-permute-start(bf16[9,32,128]{2,1,0:T(8,128)(2,1)S(1)} %pack_shares.1.refs_0_), channel_id=1, source_target_pairs={{0,8},{8,0},{16,24},{24,16},{1,9},{9,1},{17,25},{25,17},{2,10},{10... | collective-permute-start | bytes 221192 | tf_op jit(solution)/shard_map/ppermute | solution.py:56
  45.6 1.4 %collective-permute-start.9 = (bf16[9,32,128]{2,1,0:T(8,128)(2,1)S(1)}, bf16[9,32,128]{2,1,0:T(8,128)(2,1)S(1)}, u32[]{:S(2)}, u32[]{:S(2)}) collective-permute-start(bf16[9,32,128]{2,1,0:T(8,128)(2,1)S(1)} %collective-permute-done.8.refs_2_), channel_id=1, source_target_pairs={{0,8},{8,0},{16,24},{24,16},{1,9},{9,1},{17,25},{25,17},{2,10},{10... | collective-permute-start | bytes 221192 | tf_op jit(solution)/shard_map/ppermute | solution.py:56
  51.3 8.2 %collective-permute-start.15 = (bf16[576,256]{1,0:T(8,128)(2,1)S(1)}, bf16[576,256]{1,0:T(8,128)(2,1)S(1)}, u32[]{:S(2)}, u32[]{:S(2)}) collective-permute-start(bf16[576,256]{1,0:T(8,128)(2,1)S(1)} %collective-permute-done.14.refs_6_), channel_id=1, source_target_pairs={{0,1},{1,0},{2,3},{3,2},{4,5},{5,4},{6,7},{7,6},{8,9},{9,8},{10,11... | collective-permute-start | bytes 884744 | tf_op jit(solution)/shard_map/ppermute | solution.py:56
  53.7 4.3 %collective-permute-start.11 = (bf16[17,16,128]{2,1,0:T(8,128)(2,1)S(1)}, bf16[17,16,128]{2,1,0:T(8,128)(2,1)S(1)}, u32[]{:S(2)}, u32[]{:S(2)}) collective-permute-start(bf16[17,16,128]{2,1,0:T(8,128)(2,1)S(1)} %pair_terms.1.own_ref), channel_id=1, source_target_pairs={{0,16},{8,24},{16,0},{24,8},{1,17},{9,25},{17,1},{25,9},{2,18},{10... | collective-permute-start | bytes 208904 | tf_op jit(solution)/shard_map/ppermute | solution.py:56
  58.2 1.3 %collective-permute-start.12 = (bf16[16,16,128]{2,1,0:T(8,128)(2,1)S(1)}, bf16[16,16,128]{2,1,0:T(8,128)(2,1)S(1)}, u32[]{:S(2)}, u32[]{:S(2)}) collective-permute-start(bf16[16,16,128]{2,1,0:T(8,128)(2,1)S(1)} %divide.1.own_ref), channel_id=1, source_target_pairs={{0,8},{8,0},{16,24},{24,16},{1,9},{9,1},{17,25},{25,17},{2,10},{10... | collective-permute-start | bytes 196616 | tf_op jit(solution)/shard_map/ppermute | solution.py:56
  60.4 3.2 %collective-permute-start.18 = (f32[32,128]{1,0:T(8,128)S(1)}, f32[32,128]{1,0:T(8,128)S(1)}, u32[]{:S(2)}, u32[]{:S(2)}) collective-permute-start(f32[32,128]{1,0:T(8,128)S(1)} %get-tuple-element.65.refs_0_), channel_id=1, source_target_pairs={{0,24},{8,16},{16,8},{24,0},{1,25},{9,17},{17,9},{25,1},{2,26},{10... | collective-permute-start | bytes 49160 | tf_op jit(solution)/shard_map/ppermute | solution.py:56
  61.7 3.7 %collective-permute-start.17 = (f32[32,128]{1,0:T(8,128)S(1)}, f32[32,128]{1,0:T(8,128)S(1)}, u32[]{:S(2)}, u32[]{:S(2)}) collective-permute-start(f32[32,128]{1,0:T(8,128)S(1)} %get-tuple-element.65.refs_0_), channel_id=1, source_target_pairs={{0,16},{8,24},{16,0},{24,8},{1,17},{9,25},{17,1},{25,9},{2,18},{10... | collective-permute-start | bytes 49160 | tf_op jit(solution)/shard_map/ppermute | solution.py:56
  62.2 3.2 %collective-permute-start.16 = (f32[32,128]{1,0:T(8,128)S(1)}, f32[32,128]{1,0:T(8,128)S(1)}, u32[]{:S(2)}, u32[]{:S(2)}) collective-permute-start(f32[32,128]{1,0:T(8,128)S(1)} %get-tuple-element.65.refs_0_), channel_id=1, source_target_pairs={{0,8},{8,0},{16,24},{24,16},{1,9},{9,1},{17,25},{25,17},{2,10},{10... | collective-permute-start | bytes 49160 | tf_op jit(solution)/shard_map/ppermute | solution.py:56
  79.7 1.8 %collective-permute-start.19 = (bf16[2,64,1536]{2,1,0:T(8,128)(2,1)S(1)}, bf16[2,64,1536]{2,1,0:T(8,128)(2,1)S(1)}, u32[]{:S(2)}, u32[]{:S(2)}) collective-permute-start(bf16[2,64,1536]{2,1,0:T(8,128)(2,1)S(1)} %get-tuple-element.69), channel_id=1, source_target_pairs={{0,8},{8,0},{16,24},{24,16},{1,9},{9,1},{17,25},{25,17},{2,10},{10... | collective-permute-start | bytes 1179656 | tf_op jit(solution)/shard_map/ppermute | solution.py:56
  80.3 2.0 %collective-permute-start.24 = (bf16[2,64,768]{2,1,0:T(8,128)(2,1)S(1)}, bf16[2,64,768]{2,1,0:T(8,128)(2,1)S(1)}, u32[]{:S(2)}, u32[]{:S(2)}) collective-permute-start(bf16[2,64,768]{2,1,0:T(8,128)(2,1)S(1)} %get-tuple-element.72), channel_id=1, source_target_pairs={{0,8},{8,0},{16,24},{24,16},{1,9},{9,1},{17,25},{25,17},{2,10},{10... | collective-permute-start | bytes 589832 | tf_op jit(solution)/shard_map/ppermute | solution.py:56
  81.5 7.8 %collective-permute-start.20 = (bf16[64,1536]{1,0:T(8,128)(2,1)S(1)}, bf16[64,1536]{1,0:T(8,128)(2,1)S(1)}, u32[]{:S(2)}, u32[]{:S(2)}) collective-permute-start(bf16[64,1536]{1,0:T(8,128)(2,1)S(1)} %pair_sum_ff.2), channel_id=1, source_target_pairs={{0,16},{8,24},{16,0},{24,8},{1,17},{9,25},{17,1},{25,9},{2,18},{10... | collective-permute-start | bytes 589832 | tf_op jit(solution)/shard_map/ppermute | solution.py:56
  82.3 8.3 %collective-permute-start.25 = (bf16[64,768]{1,0:T(8,128)(2,1)S(1)}, bf16[64,768]{1,0:T(8,128)(2,1)S(1)}, u32[]{:S(2)}, u32[]{:S(2)}) collective-permute-start(bf16[64,768]{1,0:T(8,128)(2,1)S(1)} %pair_sum_ff.3), channel_id=1, source_target_pairs={{0,16},{8,24},{16,0},{24,8},{1,17},{9,25},{17,1},{25,9},{2,18},{10... | collective-permute-start | bytes 294920 | tf_op jit(solution)/shard_map/ppermute | solution.py:56
  89.4 4.8 %collective-permute-start.22 = (bf16[64,768]{1,0:T(8,128)(2,1)S(1)}, bf16[64,768]{1,0:T(8,128)(2,1)S(1)}, u32[]{:S(2)}, u32[]{:S(2)}) collective-permute-start(bf16[64,768]{1,0:T(8,128)(2,1)S(1)} %activate.2.refs_0_), channel_id=1, source_target_pairs={{0,16},{8,24},{16,0},{24,8},{1,17},{9,25},{17,1},{25,9},{2,18},{10... | collective-permute-start | bytes 294920 | tf_op jit(solution)/shard_map/ppermute | solution.py:56
  90.7 4.2 %collective-permute-start.27 = (bf16[64,384]{1,0:T(8,128)(2,1)S(1)}, bf16[64,384]{1,0:T(8,128)(2,1)S(1)}, u32[]{:S(2)}, u32[]{:S(2)}) collective-permute-start(bf16[64,384]{1,0:T(8,128)(2,1)S(1)} %activate.3.refs_4_), channel_id=1, source_target_pairs={{0,16},{8,24},{16,0},{24,8},{1,17},{9,25},{17,1},{25,9},{2,18},{10... | collective-permute-start | bytes 147464 | tf_op jit(solution)/shard_map/ppermute | solution.py:56
  91.7 4.4 %collective-permute-start.21 = (bf16[64,768]{1,0:T(8,128)(2,1)S(1)}, bf16[64,768]{1,0:T(8,128)(2,1)S(1)}, u32[]{:S(2)}, u32[]{:S(2)}) collective-permute-start(bf16[64,768]{1,0:T(8,128)(2,1)S(1)} %activate.2.refs_0_), channel_id=1, source_target_pairs={{0,8},{8,0},{16,24},{24,16},{1,9},{9,1},{17,25},{25,17},{2,10},{10... | collective-permute-start | bytes 294920 | tf_op jit(solution)/shard_map/ppermute | solution.py:56
  94.2 1.8 %collective-permute-start.23 = (bf16[64,768]{1,0:T(8,128)(2,1)S(1)}, bf16[64,768]{1,0:T(8,128)(2,1)S(1)}, u32[]{:S(2)}, u32[]{:S(2)}) collective-permute-start(bf16[64,768]{1,0:T(8,128)(2,1)S(1)} %collective-permute-done.22.refs_2_), channel_id=1, source_target_pairs={{0,8},{8,0},{16,24},{24,16},{1,9},{9,1},{17,25},{25,17},{2,10},{10... | collective-permute-start | bytes 294920 | tf_op jit(solution)/shard_map/ppermute | solution.py:56
  94.2 1.4 %collective-permute-start.26 = (bf16[64,384]{1,0:T(8,128)(2,1)S(1)}, bf16[64,384]{1,0:T(8,128)(2,1)S(1)}, u32[]{:S(2)}, u32[]{:S(2)}) collective-permute-start(bf16[64,384]{1,0:T(8,128)(2,1)S(1)} %activate.3.refs_4_), channel_id=1, source_target_pairs={{0,8},{8,0},{16,24},{24,16},{1,9},{9,1},{17,25},{25,17},{2,10},{10... | collective-permute-start | bytes 147464 | tf_op jit(solution)/shard_map/ppermute | solution.py:56
  110.3 3.2 %collective-permute-start.31 = (f32[32,128]{1,0:T(8,128)S(1)}, f32[32,128]{1,0:T(8,128)S(1)}, u32[]{:S(2)}, u32[]{:S(2)}) collective-permute-start(f32[32,128]{1,0:T(8,128)S(1)} %get-tuple-element.74.refs_0_), channel_id=1, source_target_pairs={{0,24},{8,16},{16,8},{24,0},{1,25},{9,17},{17,9},{25,1},{2,26},{10... | collective-permute-start | bytes 49160 | tf_op jit(solution)/shard_map/ppermute | solution.py:56
  110.3 4.0 %collective-permute-start.30 = (f32[32,128]{1,0:T(8,128)S(1)}, f32[32,128]{1,0:T(8,128)S(1)}, u32[]{:S(2)}, u32[]{:S(2)}) collective-permute-start(f32[32,128]{1,0:T(8,128)S(1)} %get-tuple-element.74.refs_0_), channel_id=1, source_target_pairs={{0,16},{8,24},{16,0},{24,8},{1,17},{9,25},{17,1},{25,9},{2,18},{10... | collective-permute-start | bytes 49160 | tf_op jit(solution)/shard_map/ppermute | solution.py:56
  111.3 3.0 %collective-permute-start.29 = (f32[32,128]{1,0:T(8,128)S(1)}, f32[32,128]{1,0:T(8,128)S(1)}, u32[]{:S(2)}, u32[]{:S(2)}) collective-permute-start(f32[32,128]{1,0:T(8,128)S(1)} %get-tuple-element.74.refs_0_), channel_id=1, source_target_pairs={{0,8},{8,0},{16,24},{24,16},{1,9},{9,1},{17,25},{25,17},{2,10},{10... | collective-permute-start | bytes 49160 | tf_op jit(solution)/shard_map/ppermute | solution.py:56
  (15 other events, 210.6 us)

commit v15 on v13

--- a/solution.py
+++ b/solution.py
@@ -136,6 +136,7 @@
         (table, lengths, parents),
         scratch=[pltpu.SMEM((slots + 1,), jnp.int32)],
         specs={0: IN_SMEM, 1: IN_SMEM, 2: IN_SMEM},
+        micros=3,
     )
 
 
@@ -226,12 +227,14 @@
         "spread", spread, [((rows, width), BF), ((ny, packed, 128), BF)], (inputs,), micros=12
     )
     w_own = w_out.T
-    x_all, w_split = lax.optimization_barrier((x_all, w_own))
+    x_all, *late = lax.optimization_barrier((x_all, block_table, lengths, parents))
+    tables = make_tables(*late, cache_pool.shape[1], rows, steps)
     x_all = exchange(x_all, "gy")
+    x_all, tables = lax.optimization_barrier((x_all, tables))
 
     w_blocks = {0: w_own, 1: permute(w_own, "gy", 1), 2: permute(w_own, "gy", 2)}
-    w_first = permute(w_split[: width // 2], "gy", 4)
-    w_late, _ = lax.optimization_barrier(((w_blocks[1], w_split[width // 2 :]), x_all))
+    w_first = permute(w_own[: width // 2], "gy", 4)
+    w_late, _ = lax.optimization_barrier(((w_blocks[1], w_own[width // 2 :]), x_all))
     w_blocks[3] = permute(w_late[0], "gy", 2)
     w_second = permute(w_late[1], "gy", 4)
 
@@ -273,16 +276,15 @@
         out_ref[...] = total.reshape(ny, rows, HALF).astype(BF)
 
     (shares,) = run("share_sum", share_sum, [((ny, rows, HALF), BF)], (z0, z13, z2))
-    shares, *late = lax.optimization_barrier((shares, block_table, lengths, parents))
-    cos, sin = rope_tables(late[1], rows, steps)
-    tables = make_tables(*late, cache_pool.shape[1], rows, steps)
-    halves, _ = lax.optimization_barrier(((w_first, w_second), tables))
+    shares, late = lax.optimization_barrier((shares, lengths))
+    cos, sin = rope_tables(late, rows, steps)
+    halves, _ = lax.optimization_barrier(((w_first, w_second), shares))
     w_blocks[4] = jnp.concatenate(halves, axis=0)
     w_blocks[6] = permute(w_blocks[4], "gy", 2)
     w_blocks[5] = permute(w_blocks[4], "gy", 1)
     shares = exchange(shares, "gy")
-    beside = tables, cos, sin, w_blocks[2], w_blocks[3], w_blocks[4]
-    shares, (tables, cos, sin, *_) = lax.optimization_barrier((shares, beside))
+    beside = cos, sin, w_blocks[2], w_blocks[3], w_blocks[4]
+    shares, (cos, sin, *_) = lax.optimization_barrier((shares, beside))
 
     def pack_shares(share_ref, x_ref, out_ref):
         x = x_ref[...].astype(F32)
@@ -419,7 +421,7 @@
 
     groups = ny // nx
 
-    cut = (hidden // 128 + 1) // 2 * 128
+    cut = hidden // 384 * 256
     column_parts = (0, cut), (cut, hidden)
 
     def gate_up(start, end):

time: 118 us -> 116 us (0.983)
  starting transfers between devices: 37 us -> 35.2 us
    all_to_all x2, waiting for transfers between devices: 8.96 us -> 13.1 us  [exchange(): return lax.all_to_all(values, axes, split_axis=0, concat_axis=0, tiled=True)]
    ppermute x32, waiting for transfers between devices: 33.4 us -> 29.3 us  [permute(): return lax.ppermute(values, axis, [(i, i ^ m) for i in range(count)])]
    all_to_all x2, starting transfers between devices: 10.7 us -> 8.42 us  [exchange(): return lax.all_to_all(values, axes, split_axis=0, concat_axis=0, tiled=True)]
  transfers between devices with their start and end apart: 34 -> 34, of which waited for: 20 -> 20; matrix products, arithmetic and copies ran while one was open for 0% -> 0% of each run, Pallas kernels for 4% -> 5%
where the time goes in v15:
time: 116 us; the launch traced here: 115 us
  waiting for transfers between devices  42.4 us (37%)
  starting transfers between devices  35.2 us (30%)
  blocking collectives  26.6 us (23%)
  Pallas kernels  9.16 us (8%)
    ppermute x32, waiting for transfers between devices, permute(): return lax.ppermute(values, axis, [(i, i ^ m) for i in range(count)])  29.3 us
    ppermute x32, starting transfers between devices, permute(): return lax.ppermute(values, axis, [(i, i ^ m) for i in range(count)])  26.8 us
    all_to_all x2, blocking collectives, exchange(): return lax.all_to_all(values, axes, split_axis=0, concat_axis=0, tiled=True)  26.6 us
    all_to_all x2, waiting for transfers between devices, exchange(): return lax.all_to_all(values, axes, split_axis=0, concat_axis=0, tiled=True)  13.1 us
    pallas_call x20, Pallas kernels, run(): pl.pallas_call(kernel, out_shape=[jax.ShapeDtypeStruct(s, d) for s, d in...  9.16 us
    all_to_all x2, starting transfers between devices, exchange(): return lax.all_to_all(values, axes, split_axis=0, concat_axis=0, tiled=True)  8.42 us
  transfers between devices with their start and end apart: 34, of which 20 were waited for; matrix products, arithmetic and copies ran while one was open for 0% of the time, Pallas kernels for 5%

profile of v15, /device:TPU:0, one launch (start us, length us, event | category | flops | bytes accessed | tf_op | source)
XLA Modules:
  0.0 115.4 jit_solution(10295530993488685037)
XLA Ops:
  0.0 2.9 %collective-permute-start.3 = (bf16[576,256]{1,0:T(8,128)(2,1)}, bf16[576,256]{1,0:T(8,128)(2,1)S(1)}, u32[]{:S(2)}, u32[]{:S(2)}) collective-permute-start(bf16[576,256]{1,0:T(8,128)(2,1)} %bitcast.7), channel_id=1, source_target_pairs={{0,1},{1,0},{2,3},{3,2},{4,5},{5,4},{6,7},{7,6},{8,9},{9,8},{10,11... | collective-permute-start | bytes 884744 | tf_op jit(solution)/shard_map/ppermute | solution.py:56
  2.9 1.6 %collective-permute-start.2 = (bf16[576,256]{1,0:T(8,128)(2,1)}, bf16[576,256]{1,0:T(8,128)(2,1)S(1)}, u32[]{:S(2)}, u32[]{:S(2)}) collective-permute-start(bf16[576,256]{1,0:T(8,128)(2,1)} %bitcast.8), channel_id=1, source_target_pairs={{0,2},{1,3},{2,0},{3,1},{4,6},{5,7},{6,4},{7,5},{8,10},{9,11},{10,... | collective-permute-start | bytes 884744 | tf_op jit(solution)/shard_map/ppermute | solution.py:56
  6.1 3.9 %all-to-all-start = ((bf16[8,144,128]{2,1,0:T(8,128)(2,1)}), bf16[8,144,128]{2,1,0:T(8,128)(2,1)S(1)}, u32[]{:S(2)}, u32[]{:S(2)}) async-start(bf16[8,144,128]{2,1,0:T(8,128)(2,1)} %get-tuple-element.44), calls=%async_computation | async-start | bytes 589824 | tf_op jit(solution)/shard_map/all_to_all | solution.py:45
  10.0 3.0 %collective-permute-start.5 = (bf16[288,256]{1,0:T(8,128)(2,1)S(1)}, bf16[288,256]{1,0:T(8,128)(2,1)S(1)}, u32[]{:S(2)}, u32[]{:S(2)}) collective-permute-start(bf16[288,256]{1,0:T(8,128)(2,1)S(1)} %get-tuple-element.81), channel_id=1, source_target_pairs={{0,4},{1,5},{2,6},{3,7},{4,0},{5,1},{6,2},{7,3},{8,12},{9,13},{10,... | collective-permute-start | bytes 442376 | tf_op jit(solution)/shard_map/ppermute | solution.py:56
  14.5 9.3 %all-to-all-done.x_ref = bf16[8,144,128]{2,1,0:T(8,128)(2,1)S(1)} async-done(((bf16[8,144,128]{2,1,0:T(8,128)(2,1)}), bf16[8,144,128]{2,1,0:T(8,128)(2,1)S(1)}, u32[]{:S(2)}, u32[]{:S(2)}) %all-to-all-start) | async-done | bytes 294944 | tf_op jit(solution)/shard_map/all_to_all | solution.py:45
  24.4 1.8 %collective-permute-start.4 = (bf16[576,256]{1,0:T(8,128)(2,1)S(1)}, bf16[576,256]{1,0:T(8,128)(2,1)S(1)}, u32[]{:S(2)}, u32[]{:S(2)}) collective-permute-start(bf16[576,256]{1,0:T(8,128)(2,1)S(1)} %collective-permute-done.3.refs_1_), channel_id=1, source_target_pairs={{0,2},{1,3},{2,0},{3,1},{4,6},{5,7},{6,4},{7,5},{8,10},{9,11},{10,... | collective-permute-start | bytes 884744 | tf_op jit(solution)/shard_map/ppermute | solution.py:56
  26.2 1.6 %collective-permute-start.1 = (bf16[256,128]{1,0:T(8,128)(2,1)S(1)}, bf16[256,128]{1,0:T(8,128)(2,1)S(1)}, u32[]{:S(2)}, u32[]{:S(2)}) collective-permute-start(bf16[256,128]{1,0:T(8,128)(2,1)S(1)} %pair_sum.1), channel_id=1, source_target_pairs={{0,16},{8,24},{16,0},{24,8},{1,17},{9,25},{17,1},{25,9},{2,18},{10... | collective-permute-start | bytes 196616 | tf_op jit(solution)/shard_map/ppermute | solution.py:56
  28.0 2.6 %collective-permute-done.1.z2_ref = bf16[256,128]{1,0:T(8,128)(2,1)S(1)} collective-permute-done((bf16[256,128]{1,0:T(8,128)(2,1)S(1)}, bf16[256,128]{1,0:T(8,128)(2,1)S(1)}, u32[]{:S(2)}, u32[]{:S(2)}) %collective-permute-start.1) | collective-permute-done | bytes 65568 | tf_op jit(solution)/shard_map/ppermute | solution.py:56
  31.2 4.6 %all-to-all-start.1 = ((bf16[8,32,128]{2,1,0:T(8,128)(2,1)}), bf16[8,32,128]{2,1,0:T(8,128)(2,1)S(1)}, u32[]{:S(2)}, u32[]{:S(2)}) async-start(bf16[8,32,128]{2,1,0:T(8,128)(2,1)} %share_sum.1), calls=%async_computation.1 | async-start | bytes 131072 | tf_op jit(solution)/shard_map/all_to_all | solution.py:45
  35.8 2.1 %collective-permute-start.13 = (bf16[576,256]{1,0:T(8,128)(2,1)S(1)}, bf16[576,256]{1,0:T(8,128)(2,1)S(1)}, u32[]{:S(2)}, u32[]{:S(2)}) collective-permute-start(bf16[576,256]{1,0:T(8,128)(2,1)S(1)} %constant_dynamic-update-slice_fusion.refs_4_), channel_id=1, source_target_pairs={{0,1},{1,0},{2,3},{3,2},{4,5},{5,4},{6,7},{7,6},{8,9},{9,8},{10,11... | collective-permute-start | bytes 884744 | tf_op jit(solution)/shard_map/ppermute | solution.py:56
  37.9 1.5 %collective-permute-start.14 = (bf16[576,256]{1,0:T(8,128)(2,1)S(1)}, bf16[576,256]{1,0:T(8,128)(2,1)S(1)}, u32[]{:S(2)}, u32[]{:S(2)}) collective-permute-start(bf16[576,256]{1,0:T(8,128)(2,1)S(1)} %constant_dynamic-update-slice_fusion.refs_4_), channel_id=1, source_target_pairs={{0,2},{1,3},{2,0},{3,1},{4,6},{5,7},{6,4},{7,5},{8,10},{9,11},{10,... | collective-permute-start | bytes 884744 | tf_op jit(solution)/shard_map/ppermute | solution.py:56
  39.4 3.8 %all-to-all-done.1.share_ref = bf16[8,32,128]{2,1,0:T(8,128)(2,1)S(1)} async-done(((bf16[8,32,128]{2,1,0:T(8,128)(2,1)}), bf16[8,32,128]{2,1,0:T(8,128)(2,1)S(1)}, u32[]{:S(2)}, u32[]{:S(2)}) %all-to-all-start.1) | async-done | bytes 65568 | tf_op jit(solution)/shard_map/all_to_all | solution.py:45
  43.3 1.5 %collective-permute-start.8 = (bf16[9,32,128]{2,1,0:T(8,128)(2,1)S(1)}, bf16[9,32,128]{2,1,0:T(8,128)(2,1)S(1)}, u32[]{:S(2)}, u32[]{:S(2)}) collective-permute-start(bf16[9,32,128]{2,1,0:T(8,128)(2,1)S(1)} %pack_shares.1.refs_0_), channel_id=1, source_target_pairs={{0,16},{8,24},{16,0},{24,8},{1,17},{9,25},{17,1},{25,9},{2,18},{10... | collective-permute-start | bytes 221192 | tf_op jit(solution)/shard_map/ppermute | solution.py:56
  44.8 2.8 %collective-permute-done.8.refs_2_ = bf16[9,32,128]{2,1,0:T(8,128)(2,1)S(1)} collective-permute-done((bf16[9,32,128]{2,1,0:T(8,128)(2,1)S(1)}, bf16[9,32,128]{2,1,0:T(8,128)(2,1)S(1)}, u32[]{:S(2)}, u32[]{:S(2)}) %collective-permute-start.8) | collective-permute-done | bytes 73760 | tf_op jit(solution)/shard_map/ppermute | solution.py:56
  47.6 1.3 %collective-permute-done.9.refs_3_ = bf16[9,32,128]{2,1,0:T(8,128)(2,1)S(1)} collective-permute-done((bf16[9,32,128]{2,1,0:T(8,128)(2,1)S(1)}, bf16[9,32,128]{2,1,0:T(8,128)(2,1)S(1)}, u32[]{:S(2)}, u32[]{:S(2)}) %collective-permute-start.9) | collective-permute-done | bytes 73760 | tf_op jit(solution)/shard_map/ppermute | solution.py:56
  48.9 1.7 %attention.1 = (bf16[17,16,128]{2,1,0:T(8,128)(2,1)S(1)}, bf16[17,16,128]{2,1,0:T(8,128)(2,1)S(1)}) custom-call(bf16[9,32,128]{2,1,0:T(8,128)(2,1)S(1)} %pack_shares.1.refs_0_, bf16[9,32,128]{2,1,0:T(8,128)(2,1)S(1)} %collective-permute-done.7.refs_1_, bf16[9,32,128]{2,1,0:T(8,128)(2,1)S(1)} %collective-permute-done.8.refs_2_, ...), custom_call_target="tpu_custom_call" | custom-call | tf_op jit(solution)/shard_map/attention/pallas_call | solution.py:33
  51.0 1.2 %collective-permute-done.10.pair_ref = bf16[17,16,128]{2,1,0:T(8,128)(2,1)S(1)} collective-permute-done((bf16[17,16,128]{2,1,0:T(8,128)(2,1)S(1)}, bf16[17,16,128]{2,1,0:T(8,128)(2,1)S(1)}, u32[]{:S(2)}, u32[]{:S(2)}) %collective-permute-start.10) | collective-permute-done | bytes 69664 | tf_op jit(solution)/shard_map/ppermute | solution.py:56
  52.4 1.5 %collective-permute-start.11 = (bf16[17,16,128]{2,1,0:T(8,128)(2,1)S(1)}, bf16[17,16,128]{2,1,0:T(8,128)(2,1)S(1)}, u32[]{:S(2)}, u32[]{:S(2)}) collective-permute-start(bf16[17,16,128]{2,1,0:T(8,128)(2,1)S(1)} %pair_terms.1.own_ref), channel_id=1, source_target_pairs={{0,16},{8,24},{16,0},{24,8},{1,17},{9,25},{17,1},{25,9},{2,18},{10... | collective-permute-start | bytes 208904 | tf_op jit(solution)/shard_map/ppermute | solution.py:56
  53.9 2.8 %collective-permute-done.11.across_ref = bf16[17,16,128]{2,1,0:T(8,128)(2,1)S(1)} collective-permute-done((bf16[17,16,128]{2,1,0:T(8,128)(2,1)S(1)}, bf16[17,16,128]{2,1,0:T(8,128)(2,1)S(1)}, u32[]{:S(2)}, u32[]{:S(2)}) %collective-permute-start.11) | collective-permute-done | bytes 69664 | tf_op jit(solution)/shard_map/ppermute | solution.py:56
  56.9 1.2 %collective-permute-done.12.other_ref = bf16[16,16,128]{2,1,0:T(8,128)(2,1)S(1)} collective-permute-done((bf16[16,16,128]{2,1,0:T(8,128)(2,1)S(1)}, bf16[16,16,128]{2,1,0:T(8,128)(2,1)S(1)}, u32[]{:S(2)}, u32[]{:S(2)}) %collective-permute-start.12) | collective-permute-done | bytes 65568 | tf_op jit(solution)/shard_map/ppermute | solution.py:56
  58.2 1.6 %collective-permute-done.15.refs_7_ = bf16[576,256]{1,0:T(8,128)(2,1)S(1)} collective-permute-done((bf16[576,256]{1,0:T(8,128)(2,1)S(1)}, bf16[576,256]{1,0:T(8,128)(2,1)S(1)}, u32[]{:S(2)}, u32[]{:S(2)}) %collective-permute-start.15) | collective-permute-done | bytes 294944 | tf_op jit(solution)/shard_map/ppermute | solution.py:56
  60.7 1.6 %collective-permute-start.17 = (f32[32,128]{1,0:T(8,128)S(1)}, f32[32,128]{1,0:T(8,128)S(1)}, u32[]{:S(2)}, u32[]{:S(2)}) collective-permute-start(f32[32,128]{1,0:T(8,128)S(1)} %get-tuple-element.69.refs_0_), channel_id=1, source_target_pairs={{0,16},{8,24},{16,0},{24,8},{1,17},{9,25},{17,1},{25,9},{2,18},{10... | collective-permute-start | bytes 49160 | tf_op jit(solution)/shard_map/ppermute | solution.py:56
  62.6 1.9 %collective-permute-done.17.refs_2_ = f32[32,128]{1,0:T(8,128)S(1)} collective-permute-done((f32[32,128]{1,0:T(8,128)S(1)}, f32[32,128]{1,0:T(8,128)S(1)}, u32[]{:S(2)}, u32[]{:S(2)}) %collective-permute-start.17) | collective-permute-done | bytes 16416 | tf_op jit(solution)/shard_map/ppermute | solution.py:56
  64.5 0.9 collective-permute-done.18.refs_3_
  65.8 13.3 %all_to_all.20.ff_ref = bf16[8,144,128]{2,1,0:T(8,128)(2,1)S(1)} all-to-all(bf16[8,144,128]{2,1,0:T(8,128)(2,1)S(1)} %get-tuple-element.71), channel_id=1, replica_groups=mesh['gx'=4,'gy'=8] {'gy'}, dimensions={0} | all-to-all | bytes 589824 | tf_op jit(solution)/shard_map/all_to_all | solution.py:45
  82.4 1.5 %collective-permute-start.25 = (bf16[64,768]{1,0:T(8,128)(2,1)S(1)}, bf16[64,768]{1,0:T(8,128)(2,1)S(1)}, u32[]{:S(2)}, u32[]{:S(2)}) collective-permute-start(bf16[64,768]{1,0:T(8,128)(2,1)S(1)} %pair_sum_ff.3), channel_id=1, source_target_pairs={{0,16},{8,24},{16,0},{24,8},{1,17},{9,25},{17,1},{25,9},{2,18},{10... | collective-permute-start | bytes 294920 | tf_op jit(solution)/shard_map/ppermute | solution.py:56
  83.9 5.6 %collective-permute-done.20.z2_ref = bf16[64,1536]{1,0:T(8,128)(2,1)S(1)} collective-permute-done((bf16[64,1536]{1,0:T(8,128)(2,1)S(1)}, bf16[64,1536]{1,0:T(8,128)(2,1)S(1)}, u32[]{:S(2)}, u32[]{:S(2)}) %collective-permute-start.20) | collective-permute-done | bytes 196640 | tf_op jit(solution)/shard_map/ppermute | solution.py:56
  90.9 1.0 collective-permute-start.27
  91.9 2.5 %collective-permute-done.22.refs_2_ = bf16[64,768]{1,0:T(8,128)(2,1)S(1)} collective-permute-done((bf16[64,768]{1,0:T(8,128)(2,1)S(1)}, bf16[64,768]{1,0:T(8,128)(2,1)S(1)}, u32[]{:S(2)}, u32[]{:S(2)}) %collective-permute-start.22) | collective-permute-done | bytes 98336 | tf_op jit(solution)/shard_map/ppermute | solution.py:56
  97.1 13.3 %all_to_all.21.parts_ref = bf16[8,144,128]{2,1,0:T(8,128)(2,1)S(1)} all-to-all(bf16[8,144,128]{2,1,0:T(8,128)(2,1)S(1)} %project_down.1), channel_id=1, replica_groups=mesh['gx'=4,'gy'=8] {'gy'}, dimensions={0} | all-to-all | bytes 589824 | tf_op jit(solution)/shard_map/all_to_all | solution.py:45
  110.5 1.0 collective-permute-start.30
  112.4 1.9 %collective-permute-done.30.refs_2_ = f32[32,128]{1,0:T(8,128)S(1)} collective-permute-done((f32[32,128]{1,0:T(8,128)S(1)}, f32[32,128]{1,0:T(8,128)S(1)}, u32[]{:S(2)}, u32[]{:S(2)}) %collective-permute-start.30) | collective-permute-done | bytes 16416 | tf_op jit(solution)/shard_map/ppermute | solution.py:56
  (91 shorter events, 15.5 us)
Async XLA Ops:
  0.0 24.3 %collective-permute-start.3 = (bf16[576,256]{1,0:T(8,128)(2,1)}, bf16[576,256]{1,0:T(8,128)(2,1)S(1)}, u32[]{:S(2)}, u32[]{:S(2)}) collective-permute-start(bf16[576,256]{1,0:T(8,128)(2,1)} %bitcast.7), channel_id=1, source_target_pairs={{0,1},{1,0},{2,3},{3,2},{4,5},{5,4},{6,7},{7,6},{8,9},{9,8},{10,11... | collective-permute-start | bytes 884744 | tf_op jit(solution)/shard_map/ppermute | solution.py:56
  2.9 36.4 %collective-permute-start.2 = (bf16[576,256]{1,0:T(8,128)(2,1)}, bf16[576,256]{1,0:T(8,128)(2,1)S(1)}, u32[]{:S(2)}, u32[]{:S(2)}) collective-permute-start(bf16[576,256]{1,0:T(8,128)(2,1)} %bitcast.8), channel_id=1, source_target_pairs={{0,2},{1,3},{2,0},{3,1},{4,6},{5,7},{6,4},{7,5},{8,10},{9,11},{10,... | collective-permute-start | bytes 884744 | tf_op jit(solution)/shard_map/ppermute | solution.py:56
  6.1 17.6 %all-to-all-start = ((bf16[8,144,128]{2,1,0:T(8,128)(2,1)}), bf16[8,144,128]{2,1,0:T(8,128)(2,1)S(1)}, u32[]{:S(2)}, u32[]{:S(2)}) async-start(bf16[8,144,128]{2,1,0:T(8,128)(2,1)} %get-tuple-element.44), calls=%async_computation | async-start | bytes 589824 | tf_op jit(solution)/shard_map/all_to_all | solution.py:45
  10.0 25.8 %collective-permute-start.5 = (bf16[288,256]{1,0:T(8,128)(2,1)S(1)}, bf16[288,256]{1,0:T(8,128)(2,1)S(1)}, u32[]{:S(2)}, u32[]{:S(2)}) collective-permute-start(bf16[288,256]{1,0:T(8,128)(2,1)S(1)} %get-tuple-element.81), channel_id=1, source_target_pairs={{0,4},{1,5},{2,6},{3,7},{4,0},{5,1},{6,2},{7,3},{8,12},{9,13},{10,... | collective-permute-start | bytes 442376 | tf_op jit(solution)/shard_map/ppermute | solution.py:56
  24.2 2.0 %collective-permute-start = (bf16[2,256,128]{2,1,0:T(8,128)(2,1)S(1)}, bf16[2,256,128]{2,1,0:T(8,128)(2,1)S(1)}, u32[]{:S(2)}, u32[]{:S(2)}) collective-permute-start(bf16[2,256,128]{2,1,0:T(8,128)(2,1)S(1)} %get-tuple-element.52), channel_id=1, source_target_pairs={{0,8},{8,0},{16,24},{24,16},{1,9},{9,1},{17,25},{25,17},{2,10},{10... | collective-permute-start | bytes 393224 | tf_op jit(solution)/shard_map/ppermute | solution.py:56
  24.3 11.5 %collective-permute-start.6 = (bf16[288,256]{1,0:T(8,128)(2,1)S(1)}, bf16[288,256]{1,0:T(8,128)(2,1)S(1)}, u32[]{:S(2)}, u32[]{:S(2)}) collective-permute-start(bf16[288,256]{1,0:T(8,128)(2,1)S(1)} %get-tuple-element.57), channel_id=1, source_target_pairs={{0,4},{1,5},{2,6},{3,7},{4,0},{5,1},{6,2},{7,3},{8,12},{9,13},{10,... | collective-permute-start | bytes 442376 | tf_op jit(solution)/shard_map/ppermute | solution.py:56
  24.4 15.0 %collective-permute-start.4 = (bf16[576,256]{1,0:T(8,128)(2,1)S(1)}, bf16[576,256]{1,0:T(8,128)(2,1)S(1)}, u32[]{:S(2)}, u32[]{:S(2)}) collective-permute-start(bf16[576,256]{1,0:T(8,128)(2,1)S(1)} %collective-permute-done.3.refs_1_), channel_id=1, source_target_pairs={{0,2},{1,3},{2,0},{3,1},{4,6},{5,7},{6,4},{7,5},{8,10},{9,11},{10,... | collective-permute-start | bytes 884744 | tf_op jit(solution)/shard_map/ppermute | solution.py:56
  26.2 4.3 %collective-permute-start.1 = (bf16[256,128]{1,0:T(8,128)(2,1)S(1)}, bf16[256,128]{1,0:T(8,128)(2,1)S(1)}, u32[]{:S(2)}, u32[]{:S(2)}) collective-permute-start(bf16[256,128]{1,0:T(8,128)(2,1)S(1)} %pair_sum.1), channel_id=1, source_target_pairs={{0,16},{8,24},{16,0},{24,8},{1,17},{9,25},{17,1},{25,9},{2,18},{10... | collective-permute-start | bytes 196616 | tf_op jit(solution)/shard_map/ppermute | solution.py:56
  31.2 12.0 %all-to-all-start.1 = ((bf16[8,32,128]{2,1,0:T(8,128)(2,1)}), bf16[8,32,128]{2,1,0:T(8,128)(2,1)S(1)}, u32[]{:S(2)}, u32[]{:S(2)}) async-start(bf16[8,32,128]{2,1,0:T(8,128)(2,1)} %share_sum.1), calls=%async_computation.1 | async-start | bytes 131072 | tf_op jit(solution)/shard_map/all_to_all | solution.py:45
  35.8 14.8 %collective-permute-start.13 = (bf16[576,256]{1,0:T(8,128)(2,1)S(1)}, bf16[576,256]{1,0:T(8,128)(2,1)S(1)}, u32[]{:S(2)}, u32[]{:S(2)}) collective-permute-start(bf16[576,256]{1,0:T(8,128)(2,1)S(1)} %constant_dynamic-update-slice_fusion.refs_4_), channel_id=1, source_target_pairs={{0,1},{1,0},{2,3},{3,2},{4,5},{5,4},{6,7},{7,6},{8,9},{9,8},{10,11... | collective-permute-start | bytes 884744 | tf_op jit(solution)/shard_map/ppermute | solution.py:56
  37.9 12.8 %collective-permute-start.14 = (bf16[576,256]{1,0:T(8,128)(2,1)S(1)}, bf16[576,256]{1,0:T(8,128)(2,1)S(1)}, u32[]{:S(2)}, u32[]{:S(2)}) collective-permute-start(bf16[576,256]{1,0:T(8,128)(2,1)S(1)} %constant_dynamic-update-slice_fusion.refs_4_), channel_id=1, source_target_pairs={{0,2},{1,3},{2,0},{3,1},{4,6},{5,7},{6,4},{7,5},{8,10},{9,11},{10,... | collective-permute-start | bytes 884744 | tf_op jit(solution)/shard_map/ppermute | solution.py:56
  43.3 4.4 %collective-permute-start.8 = (bf16[9,32,128]{2,1,0:T(8,128)(2,1)S(1)}, bf16[9,32,128]{2,1,0:T(8,128)(2,1)S(1)}, u32[]{:S(2)}, u32[]{:S(2)}) collective-permute-start(bf16[9,32,128]{2,1,0:T(8,128)(2,1)S(1)} %pack_shares.1.refs_0_), channel_id=1, source_target_pairs={{0,16},{8,24},{16,0},{24,8},{1,17},{9,25},{17,1},{25,9},{2,18},{10... | collective-permute-start | bytes 221192 | tf_op jit(solution)/shard_map/ppermute | solution.py:56
  44.8 2.8 %collective-permute-start.7 = (bf16[9,32,128]{2,1,0:T(8,128)(2,1)S(1)}, bf16[9,32,128]{2,1,0:T(8,128)(2,1)S(1)}, u32[]{:S(2)}, u32[]{:S(2)}) collective-permute-start(bf16[9,32,128]{2,1,0:T(8,128)(2,1)S(1)} %pack_shares.1.refs_0_), channel_id=1, source_target_pairs={{0,8},{8,0},{16,24},{24,16},{1,9},{9,1},{17,25},{25,17},{2,10},{10... | collective-permute-start | bytes 221192 | tf_op jit(solution)/shard_map/ppermute | solution.py:56
  47.6 1.3 %collective-permute-start.9 = (bf16[9,32,128]{2,1,0:T(8,128)(2,1)S(1)}, bf16[9,32,128]{2,1,0:T(8,128)(2,1)S(1)}, u32[]{:S(2)}, u32[]{:S(2)}) collective-permute-start(bf16[9,32,128]{2,1,0:T(8,128)(2,1)S(1)} %collective-permute-done.8.refs_2_), channel_id=1, source_target_pairs={{0,8},{8,0},{16,24},{24,16},{1,9},{9,1},{17,25},{25,17},{2,10},{10... | collective-permute-start | bytes 221192 | tf_op jit(solution)/shard_map/ppermute | solution.py:56
  50.7 9.1 %collective-permute-start.15 = (bf16[576,256]{1,0:T(8,128)(2,1)S(1)}, bf16[576,256]{1,0:T(8,128)(2,1)S(1)}, u32[]{:S(2)}, u32[]{:S(2)}) collective-permute-start(bf16[576,256]{1,0:T(8,128)(2,1)S(1)} %collective-permute-done.14.refs_6_), channel_id=1, source_target_pairs={{0,1},{1,0},{2,3},{3,2},{4,5},{5,4},{6,7},{7,6},{8,9},{9,8},{10,11... | collective-permute-start | bytes 884744 | tf_op jit(solution)/shard_map/ppermute | solution.py:56
  52.4 4.3 %collective-permute-start.11 = (bf16[17,16,128]{2,1,0:T(8,128)(2,1)S(1)}, bf16[17,16,128]{2,1,0:T(8,128)(2,1)S(1)}, u32[]{:S(2)}, u32[]{:S(2)}) collective-permute-start(bf16[17,16,128]{2,1,0:T(8,128)(2,1)S(1)} %pair_terms.1.own_ref), channel_id=1, source_target_pairs={{0,16},{8,24},{16,0},{24,8},{1,17},{9,25},{17,1},{25,9},{2,18},{10... | collective-permute-start | bytes 208904 | tf_op jit(solution)/shard_map/ppermute | solution.py:56
  56.9 1.3 %collective-permute-start.12 = (bf16[16,16,128]{2,1,0:T(8,128)(2,1)S(1)}, bf16[16,16,128]{2,1,0:T(8,128)(2,1)S(1)}, u32[]{:S(2)}, u32[]{:S(2)}) collective-permute-start(bf16[16,16,128]{2,1,0:T(8,128)(2,1)S(1)} %divide.1.own_ref), channel_id=1, source_target_pairs={{0,8},{8,0},{16,24},{24,16},{1,9},{9,1},{17,25},{25,17},{2,10},{10... | collective-permute-start | bytes 196616 | tf_op jit(solution)/shard_map/ppermute | solution.py:56
  60.6 1.9 %collective-permute-start.16 = (f32[32,128]{1,0:T(8,128)S(1)}, f32[32,128]{1,0:T(8,128)S(1)}, u32[]{:S(2)}, u32[]{:S(2)}) collective-permute-start(f32[32,128]{1,0:T(8,128)S(1)} %get-tuple-element.69.refs_0_), channel_id=1, source_target_pairs={{0,8},{8,0},{16,24},{24,16},{1,9},{9,1},{17,25},{25,17},{2,10},{10... | collective-permute-start | bytes 49160 | tf_op jit(solution)/shard_map/ppermute | solution.py:56
  60.7 3.8 %collective-permute-start.17 = (f32[32,128]{1,0:T(8,128)S(1)}, f32[32,128]{1,0:T(8,128)S(1)}, u32[]{:S(2)}, u32[]{:S(2)}) collective-permute-start(f32[32,128]{1,0:T(8,128)S(1)} %get-tuple-element.69.refs_0_), channel_id=1, source_target_pairs={{0,16},{8,24},{16,0},{24,8},{1,17},{9,25},{17,1},{25,9},{2,18},{10... | collective-permute-start | bytes 49160 | tf_op jit(solution)/shard_map/ppermute | solution.py:56
  62.3 3.2 %collective-permute-start.18 = (f32[32,128]{1,0:T(8,128)S(1)}, f32[32,128]{1,0:T(8,128)S(1)}, u32[]{:S(2)}, u32[]{:S(2)}) collective-permute-start(f32[32,128]{1,0:T(8,128)S(1)} %get-tuple-element.69.refs_0_), channel_id=1, source_target_pairs={{0,24},{8,16},{16,8},{24,0},{1,25},{9,17},{17,9},{25,1},{2,26},{10... | collective-permute-start | bytes 49160 | tf_op jit(solution)/shard_map/ppermute | solution.py:56
  79.9 1.8 %collective-permute-start.19 = (bf16[2,64,1536]{2,1,0:T(8,128)(2,1)S(1)}, bf16[2,64,1536]{2,1,0:T(8,128)(2,1)S(1)}, u32[]{:S(2)}, u32[]{:S(2)}) collective-permute-start(bf16[2,64,1536]{2,1,0:T(8,128)(2,1)S(1)} %get-tuple-element.73), channel_id=1, source_target_pairs={{0,8},{8,0},{16,24},{24,16},{1,9},{9,1},{17,25},{25,17},{2,10},{10... | collective-permute-start | bytes 1179656 | tf_op jit(solution)/shard_map/ppermute | solution.py:56
  80.5 1.9 %collective-permute-start.24 = (bf16[2,64,768]{2,1,0:T(8,128)(2,1)S(1)}, bf16[2,64,768]{2,1,0:T(8,128)(2,1)S(1)}, u32[]{:S(2)}, u32[]{:S(2)}) collective-permute-start(bf16[2,64,768]{2,1,0:T(8,128)(2,1)S(1)} %get-tuple-element.76), channel_id=1, source_target_pairs={{0,8},{8,0},{16,24},{24,16},{1,9},{9,1},{17,25},{25,17},{2,10},{10... | collective-permute-start | bytes 589832 | tf_op jit(solution)/shard_map/ppermute | solution.py:56
  81.7 7.8 %collective-permute-start.20 = (bf16[64,1536]{1,0:T(8,128)(2,1)S(1)}, bf16[64,1536]{1,0:T(8,128)(2,1)S(1)}, u32[]{:S(2)}, u32[]{:S(2)}) collective-permute-start(bf16[64,1536]{1,0:T(8,128)(2,1)S(1)} %pair_sum_ff.2), channel_id=1, source_target_pairs={{0,16},{8,24},{16,0},{24,8},{1,17},{9,25},{17,1},{25,9},{2,18},{10... | collective-permute-start | bytes 589832 | tf_op jit(solution)/shard_map/ppermute | solution.py:56
  82.4 8.4 %collective-permute-start.25 = (bf16[64,768]{1,0:T(8,128)(2,1)S(1)}, bf16[64,768]{1,0:T(8,128)(2,1)S(1)}, u32[]{:S(2)}, u32[]{:S(2)}) collective-permute-start(bf16[64,768]{1,0:T(8,128)(2,1)S(1)} %pair_sum_ff.3), channel_id=1, source_target_pairs={{0,16},{8,24},{16,0},{24,8},{1,17},{9,25},{17,1},{25,9},{2,18},{10... | collective-permute-start | bytes 294920 | tf_op jit(solution)/shard_map/ppermute | solution.py:56
  89.7 4.8 %collective-permute-start.22 = (bf16[64,768]{1,0:T(8,128)(2,1)S(1)}, bf16[64,768]{1,0:T(8,128)(2,1)S(1)}, u32[]{:S(2)}, u32[]{:S(2)}) collective-permute-start(bf16[64,768]{1,0:T(8,128)(2,1)S(1)} %activate.2.refs_0_), channel_id=1, source_target_pairs={{0,16},{8,24},{16,0},{24,8},{1,17},{9,25},{17,1},{25,9},{2,18},{10... | collective-permute-start | bytes 294920 | tf_op jit(solution)/shard_map/ppermute | solution.py:56
  90.9 4.2 %collective-permute-start.27 = (bf16[64,384]{1,0:T(8,128)(2,1)S(1)}, bf16[64,384]{1,0:T(8,128)(2,1)S(1)}, u32[]{:S(2)}, u32[]{:S(2)}) collective-permute-start(bf16[64,384]{1,0:T(8,128)(2,1)S(1)} %activate.3.refs_4_), channel_id=1, source_target_pairs={{0,16},{8,24},{16,0},{24,8},{1,17},{9,25},{17,1},{25,9},{2,18},{10... | collective-permute-start | bytes 147464 | tf_op jit(solution)/shard_map/ppermute | solution.py:56
  91.9 4.4 %collective-permute-start.21 = (bf16[64,768]{1,0:T(8,128)(2,1)S(1)}, bf16[64,768]{1,0:T(8,128)(2,1)S(1)}, u32[]{:S(2)}, u32[]{:S(2)}) collective-permute-start(bf16[64,768]{1,0:T(8,128)(2,1)S(1)} %activate.2.refs_0_), channel_id=1, source_target_pairs={{0,8},{8,0},{16,24},{24,16},{1,9},{9,1},{17,25},{25,17},{2,10},{10... | collective-permute-start | bytes 294920 | tf_op jit(solution)/shard_map/ppermute | solution.py:56
  94.4 1.8 %collective-permute-start.23 = (bf16[64,768]{1,0:T(8,128)(2,1)S(1)}, bf16[64,768]{1,0:T(8,128)(2,1)S(1)}, u32[]{:S(2)}, u32[]{:S(2)}) collective-permute-start(bf16[64,768]{1,0:T(8,128)(2,1)S(1)} %collective-permute-done.22.refs_2_), channel_id=1, source_target_pairs={{0,8},{8,0},{16,24},{24,16},{1,9},{9,1},{17,25},{25,17},{2,10},{10... | collective-permute-start | bytes 294920 | tf_op jit(solution)/shard_map/ppermute | solution.py:56
  94.4 1.4 %collective-permute-start.26 = (bf16[64,384]{1,0:T(8,128)(2,1)S(1)}, bf16[64,384]{1,0:T(8,128)(2,1)S(1)}, u32[]{:S(2)}, u32[]{:S(2)}) collective-permute-start(bf16[64,384]{1,0:T(8,128)(2,1)S(1)} %activate.3.refs_4_), channel_id=1, source_target_pairs={{0,8},{8,0},{16,24},{24,16},{1,9},{9,1},{17,25},{25,17},{2,10},{10... | collective-permute-start | bytes 147464 | tf_op jit(solution)/shard_map/ppermute | solution.py:56
  110.5 1.9 %collective-permute-start.29 = (f32[32,128]{1,0:T(8,128)S(1)}, f32[32,128]{1,0:T(8,128)S(1)}, u32[]{:S(2)}, u32[]{:S(2)}) collective-permute-start(f32[32,128]{1,0:T(8,128)S(1)} %get-tuple-element.78.refs_0_), channel_id=1, source_target_pairs={{0,8},{8,0},{16,24},{24,16},{1,9},{9,1},{17,25},{25,17},{2,10},{10... | collective-permute-start | bytes 49160 | tf_op jit(solution)/shard_map/ppermute | solution.py:56
  110.5 3.8 %collective-permute-start.30 = (f32[32,128]{1,0:T(8,128)S(1)}, f32[32,128]{1,0:T(8,128)S(1)}, u32[]{:S(2)}, u32[]{:S(2)}) collective-permute-start(f32[32,128]{1,0:T(8,128)S(1)} %get-tuple-element.78.refs_0_), channel_id=1, source_target_pairs={{0,16},{8,24},{16,0},{24,8},{1,17},{9,25},{17,1},{25,9},{2,18},{10... | collective-permute-start | bytes 49160 | tf_op jit(solution)/shard_map/ppermute | solution.py:56
  111.5 3.2 %collective-permute-start.31 = (f32[32,128]{1,0:T(8,128)S(1)}, f32[32,128]{1,0:T(8,128)S(1)}, u32[]{:S(2)}, u32[]{:S(2)}) collective-permute-start(f32[32,128]{1,0:T(8,128)S(1)} %get-tuple-element.78.refs_0_), channel_id=1, source_target_pairs={{0,24},{8,16},{16,8},{24,0},{1,25},{9,17},{17,9},{25,1},{2,26},{10... | collective-permute-start | bytes 49160 | tf_op jit(solution)/shard_map/ppermute | solution.py:56
  (15 other events, 147.2 us)

commit v16 on v13

--- a/solution.py
+++ b/solution.py
@@ -276,7 +276,7 @@
     shares, *late = lax.optimization_barrier((shares, block_table, lengths, parents))
     cos, sin = rope_tables(late[1], rows, steps)
     tables = make_tables(*late, cache_pool.shape[1], rows, steps)
-    halves, _ = lax.optimization_barrier(((w_first, w_second), tables))
+    halves, _ = lax.optimization_barrier(((w_first, w_second), shares))
     w_blocks[4] = jnp.concatenate(halves, axis=0)
     w_blocks[6] = permute(w_blocks[4], "gy", 2)
     w_blocks[5] = permute(w_blocks[4], "gy", 1)
@@ -419,7 +419,7 @@
 
     groups = ny // nx
 
-    cut = (hidden // 128 + 1) // 2 * 128
+    cut = hidden // 384 * 256
     column_parts = (0, cut), (cut, hidden)
 
     def gate_up(start, end):

time: 118 us -> 113 us (0.958)
  waiting for transfers between devices: 42.4 us -> 38.1 us
    ppermute x32, waiting for transfers between devices: 33.4 us -> 30 us  [permute(): return lax.ppermute(values, axis, [(i, i ^ m) for i in range(count)])]
  transfers between devices with their start and end apart: 34 -> 34, of which waited for: 20 -> 21; matrix products, arithmetic and copies ran while one was open for 0% -> 0% of each run, Pallas kernels for 4% -> 4%
where the time goes in v16:
time: 113 us
  waiting for transfers between devices  38.1 us (34%)
  starting transfers between devices  36.8 us (33%)
  blocking collectives  26.6 us (24%)
  Pallas kernels  9.16 us (8%)
    ppermute x32, waiting for transfers between devices, permute(): return lax.ppermute(values, axis, [(i, i ^ m) for i in range(count)])  30 us
    all_to_all x2, blocking collectives, exchange(): return lax.all_to_all(values, axes, split_axis=0, concat_axis=0, tiled=True)  26.6 us
    ppermute x32, starting transfers between devices, permute(): return lax.ppermute(values, axis, [(i, i ^ m) for i in range(count)])  26 us
    all_to_all x2, starting transfers between devices, exchange(): return lax.all_to_all(values, axes, split_axis=0, concat_axis=0, tiled=True)  10.7 us
    pallas_call x20, Pallas kernels, run(): pl.pallas_call(kernel, out_shape=[jax.ShapeDtypeStruct(s, d) for s, d in...  9.16 us
    all_to_all x2, waiting for transfers between devices, exchange(): return lax.all_to_all(values, axes, split_axis=0, concat_axis=0, tiled=True)  8.11 us
  transfers between devices with their start and end apart: 34, of which 21 were waited for; matrix products, arithmetic and copies ran while one was open for 0% of the time, Pallas kernels for 4%

profile of v16, /device:TPU:0, one launch (start us, length us, event | category | flops | bytes accessed | tf_op | source)
XLA Modules:
  0.0 112.7 jit_solution(16066117028978444374)
XLA Ops:
  1.7 7.4 %all-to-all-start = ((bf16[8,144,128]{2,1,0:T(8,128)(2,1)}), bf16[8,144,128]{2,1,0:T(8,128)(2,1)S(1)}, u32[]{:S(2)}, u32[]{:S(2)}) async-start(bf16[8,144,128]{2,1,0:T(8,128)(2,1)} %get-tuple-element.43), calls=%async_computation | async-start | bytes 589824 | tf_op jit(solution)/shard_map/all_to_all | solution.py:45
  9.1 2.1 %collective-permute-start.3 = (bf16[576,256]{1,0:T(8,128)(2,1)S(1)}, bf16[576,256]{1,0:T(8,128)(2,1)S(1)}, u32[]{:S(2)}, u32[]{:S(2)}) collective-permute-start(bf16[576,256]{1,0:T(8,128)(2,1)S(1)} %bitcast.7), channel_id=1, source_target_pairs={{0,1},{1,0},{2,3},{3,2},{4,5},{5,4},{6,7},{7,6},{8,9},{9,8},{10,11... | collective-permute-start | bytes 884744 | tf_op jit(solution)/shard_map/ppermute | solution.py:56
  11.2 1.5 %collective-permute-start.2 = (bf16[576,256]{1,0:T(8,128)(2,1)S(1)}, bf16[576,256]{1,0:T(8,128)(2,1)S(1)}, u32[]{:S(2)}, u32[]{:S(2)}) collective-permute-start(bf16[576,256]{1,0:T(8,128)(2,1)S(1)} %bitcast.8), channel_id=1, source_target_pairs={{0,2},{1,3},{2,0},{3,1},{4,6},{5,7},{6,4},{7,5},{8,10},{9,11},{10,... | collective-permute-start | bytes 884744 | tf_op jit(solution)/shard_map/ppermute | solution.py:56
  12.6 2.4 %collective-permute-start.5 = (bf16[288,256]{1,0:T(8,128)(2,1)S(1)}, bf16[288,256]{1,0:T(8,128)(2,1)S(1)}, u32[]{:S(2)}, u32[]{:S(2)}) collective-permute-start(bf16[288,256]{1,0:T(8,128)(2,1)S(1)} %get-tuple-element.79), channel_id=1, source_target_pairs={{0,4},{1,5},{2,6},{3,7},{4,0},{5,1},{6,2},{7,3},{8,12},{9,13},{10,... | collective-permute-start | bytes 442376 | tf_op jit(solution)/shard_map/ppermute | solution.py:56
  15.1 5.0 %all-to-all-done.x_ref = bf16[8,144,128]{2,1,0:T(8,128)(2,1)S(1)} async-done(((bf16[8,144,128]{2,1,0:T(8,128)(2,1)}), bf16[8,144,128]{2,1,0:T(8,128)(2,1)S(1)}, u32[]{:S(2)}, u32[]{:S(2)}) %all-to-all-start) | async-done | bytes 294944 | tf_op jit(solution)/shard_map/all_to_all | solution.py:45
  21.4 1.9 %collective-permute-start.6 = (bf16[288,256]{1,0:T(8,128)(2,1)S(1)}, bf16[288,256]{1,0:T(8,128)(2,1)S(1)}, u32[]{:S(2)}, u32[]{:S(2)}) collective-permute-start(bf16[288,256]{1,0:T(8,128)(2,1)S(1)} %get-tuple-element.55), channel_id=1, source_target_pairs={{0,4},{1,5},{2,6},{3,7},{4,0},{5,1},{6,2},{7,3},{8,12},{9,13},{10,... | collective-permute-start | bytes 442376 | tf_op jit(solution)/shard_map/ppermute | solution.py:56
  23.2 1.5 %collective-permute-start.4 = (bf16[576,256]{1,0:T(8,128)(2,1)S(1)}, bf16[576,256]{1,0:T(8,128)(2,1)S(1)}, u32[]{:S(2)}, u32[]{:S(2)}) collective-permute-start(bf16[576,256]{1,0:T(8,128)(2,1)S(1)} %collective-permute-done.3.refs_1_), channel_id=1, source_target_pairs={{0,2},{1,3},{2,0},{3,1},{4,6},{5,7},{6,4},{7,5},{8,10},{9,11},{10,... | collective-permute-start | bytes 884744 | tf_op jit(solution)/shard_map/ppermute | solution.py:56
  24.7 1.6 %collective-permute-start.1 = (bf16[256,128]{1,0:T(8,128)(2,1)S(1)}, bf16[256,128]{1,0:T(8,128)(2,1)S(1)}, u32[]{:S(2)}, u32[]{:S(2)}) collective-permute-start(bf16[256,128]{1,0:T(8,128)(2,1)S(1)} %pair_sum.1), channel_id=1, source_target_pairs={{0,16},{8,24},{16,0},{24,8},{1,17},{9,25},{17,1},{25,9},{2,18},{10... | collective-permute-start | bytes 196616 | tf_op jit(solution)/shard_map/ppermute | solution.py:56
  26.5 2.6 %collective-permute-done.1.z2_ref = bf16[256,128]{1,0:T(8,128)(2,1)S(1)} collective-permute-done((bf16[256,128]{1,0:T(8,128)(2,1)S(1)}, bf16[256,128]{1,0:T(8,128)(2,1)S(1)}, u32[]{:S(2)}, u32[]{:S(2)}) %collective-permute-start.1) | collective-permute-done | bytes 65568 | tf_op jit(solution)/shard_map/ppermute | solution.py:56
  29.7 3.3 %all-to-all-start.1 = ((bf16[8,32,128]{2,1,0:T(8,128)(2,1)}), bf16[8,32,128]{2,1,0:T(8,128)(2,1)S(1)}, u32[]{:S(2)}, u32[]{:S(2)}) async-start(bf16[8,32,128]{2,1,0:T(8,128)(2,1)} %share_sum.1), calls=%async_computation.1 | async-start | bytes 131072 | tf_op jit(solution)/shard_map/all_to_all | solution.py:45
  33.7 1.4 %collective-permute-start.13 = (bf16[576,256]{1,0:T(8,128)(2,1)S(1)}, bf16[576,256]{1,0:T(8,128)(2,1)S(1)}, u32[]{:S(2)}, u32[]{:S(2)}) collective-permute-start(bf16[576,256]{1,0:T(8,128)(2,1)S(1)} %constant_dynamic-update-slice_fusion.refs_4_), channel_id=1, source_target_pairs={{0,1},{1,0},{2,3},{3,2},{4,5},{5,4},{6,7},{7,6},{8,9},{9,8},{10,11... | collective-permute-start | bytes 884744 | tf_op jit(solution)/shard_map/ppermute | solution.py:56
  35.1 1.5 %collective-permute-start.14 = (bf16[576,256]{1,0:T(8,128)(2,1)S(1)}, bf16[576,256]{1,0:T(8,128)(2,1)S(1)}, u32[]{:S(2)}, u32[]{:S(2)}) collective-permute-start(bf16[576,256]{1,0:T(8,128)(2,1)S(1)} %constant_dynamic-update-slice_fusion.refs_4_), channel_id=1, source_target_pairs={{0,2},{1,3},{2,0},{3,1},{4,6},{5,7},{6,4},{7,5},{8,10},{9,11},{10,... | collective-permute-start | bytes 884744 | tf_op jit(solution)/shard_map/ppermute | solution.py:56
  37.3 3.1 %all-to-all-done.1.share_ref = bf16[8,32,128]{2,1,0:T(8,128)(2,1)S(1)} async-done(((bf16[8,32,128]{2,1,0:T(8,128)(2,1)}), bf16[8,32,128]{2,1,0:T(8,128)(2,1)S(1)}, u32[]{:S(2)}, u32[]{:S(2)}) %all-to-all-start.1) | async-done | bytes 65568 | tf_op jit(solution)/shard_map/all_to_all | solution.py:45
  40.5 1.5 %collective-permute-start.8 = (bf16[9,32,128]{2,1,0:T(8,128)(2,1)S(1)}, bf16[9,32,128]{2,1,0:T(8,128)(2,1)S(1)}, u32[]{:S(2)}, u32[]{:S(2)}) collective-permute-start(bf16[9,32,128]{2,1,0:T(8,128)(2,1)S(1)} %pack_shares.1.refs_0_), channel_id=1, source_target_pairs={{0,16},{8,24},{16,0},{24,8},{1,17},{9,25},{17,1},{25,9},{2,18},{10... | collective-permute-start | bytes 221192 | tf_op jit(solution)/shard_map/ppermute | solution.py:56
  42.0 2.8 %collective-permute-done.8.refs_2_ = bf16[9,32,128]{2,1,0:T(8,128)(2,1)S(1)} collective-permute-done((bf16[9,32,128]{2,1,0:T(8,128)(2,1)S(1)}, bf16[9,32,128]{2,1,0:T(8,128)(2,1)S(1)}, u32[]{:S(2)}, u32[]{:S(2)}) %collective-permute-start.8) | collective-permute-done | bytes 73760 | tf_op jit(solution)/shard_map/ppermute | solution.py:56
  44.9 1.3 %collective-permute-done.9.refs_3_ = bf16[9,32,128]{2,1,0:T(8,128)(2,1)S(1)} collective-permute-done((bf16[9,32,128]{2,1,0:T(8,128)(2,1)S(1)}, bf16[9,32,128]{2,1,0:T(8,128)(2,1)S(1)}, u32[]{:S(2)}, u32[]{:S(2)}) %collective-permute-start.9) | collective-permute-done | bytes 73760 | tf_op jit(solution)/shard_map/ppermute | solution.py:56
  46.1 1.7 %attention.1 = (bf16[17,16,128]{2,1,0:T(8,128)(2,1)S(1)}, bf16[17,16,128]{2,1,0:T(8,128)(2,1)S(1)}) custom-call(bf16[9,32,128]{2,1,0:T(8,128)(2,1)S(1)} %pack_shares.1.refs_0_, bf16[9,32,128]{2,1,0:T(8,128)(2,1)S(1)} %collective-permute-done.7.refs_1_, bf16[9,32,128]{2,1,0:T(8,128)(2,1)S(1)} %collective-permute-done.8.refs_2_, ...), custom_call_target="tpu_custom_call" | custom-call | tf_op jit(solution)/shard_map/attention/pallas_call | solution.py:33
  48.2 1.2 %collective-permute-done.10.pair_ref = bf16[17,16,128]{2,1,0:T(8,128)(2,1)S(1)} collective-permute-done((bf16[17,16,128]{2,1,0:T(8,128)(2,1)S(1)}, bf16[17,16,128]{2,1,0:T(8,128)(2,1)S(1)}, u32[]{:S(2)}, u32[]{:S(2)}) %collective-permute-start.10) | collective-permute-done | bytes 69664 | tf_op jit(solution)/shard_map/ppermute | solution.py:56
  49.6 1.5 %collective-permute-start.11 = (bf16[17,16,128]{2,1,0:T(8,128)(2,1)S(1)}, bf16[17,16,128]{2,1,0:T(8,128)(2,1)S(1)}, u32[]{:S(2)}, u32[]{:S(2)}) collective-permute-start(bf16[17,16,128]{2,1,0:T(8,128)(2,1)S(1)} %pair_terms.1.own_ref), channel_id=1, source_target_pairs={{0,16},{8,24},{16,0},{24,8},{1,17},{9,25},{17,1},{25,9},{2,18},{10... | collective-permute-start | bytes 208904 | tf_op jit(solution)/shard_map/ppermute | solution.py:56
  51.1 2.8 %collective-permute-done.11.across_ref = bf16[17,16,128]{2,1,0:T(8,128)(2,1)S(1)} collective-permute-done((bf16[17,16,128]{2,1,0:T(8,128)(2,1)S(1)}, bf16[17,16,128]{2,1,0:T(8,128)(2,1)S(1)}, u32[]{:S(2)}, u32[]{:S(2)}) %collective-permute-start.11) | collective-permute-done | bytes 69664 | tf_op jit(solution)/shard_map/ppermute | solution.py:56
  54.2 1.2 %collective-permute-done.12.other_ref = bf16[16,16,128]{2,1,0:T(8,128)(2,1)S(1)} collective-permute-done((bf16[16,16,128]{2,1,0:T(8,128)(2,1)S(1)}, bf16[16,16,128]{2,1,0:T(8,128)(2,1)S(1)}, u32[]{:S(2)}, u32[]{:S(2)}) %collective-permute-start.12) | collective-permute-done | bytes 65568 | tf_op jit(solution)/shard_map/ppermute | solution.py:56
  55.4 1.6 %collective-permute-done.15.refs_7_ = bf16[576,256]{1,0:T(8,128)(2,1)S(1)} collective-permute-done((bf16[576,256]{1,0:T(8,128)(2,1)S(1)}, bf16[576,256]{1,0:T(8,128)(2,1)S(1)}, u32[]{:S(2)}, u32[]{:S(2)}) %collective-permute-start.15) | collective-permute-done | bytes 294944 | tf_op jit(solution)/shard_map/ppermute | solution.py:56
  58.0 1.6 %collective-permute-start.17 = (f32[32,128]{1,0:T(8,128)S(1)}, f32[32,128]{1,0:T(8,128)S(1)}, u32[]{:S(2)}, u32[]{:S(2)}) collective-permute-start(f32[32,128]{1,0:T(8,128)S(1)} %get-tuple-element.67.refs_0_), channel_id=1, source_target_pairs={{0,16},{8,24},{16,0},{24,8},{1,17},{9,25},{17,1},{25,9},{2,18},{10... | collective-permute-start | bytes 49160 | tf_op jit(solution)/shard_map/ppermute | solution.py:56
  59.8 1.9 %collective-permute-done.17.refs_2_ = f32[32,128]{1,0:T(8,128)S(1)} collective-permute-done((f32[32,128]{1,0:T(8,128)S(1)}, f32[32,128]{1,0:T(8,128)S(1)}, u32[]{:S(2)}, u32[]{:S(2)}) %collective-permute-start.17) | collective-permute-done | bytes 16416 | tf_op jit(solution)/shard_map/ppermute | solution.py:56
  63.0 13.3 %all_to_all.20.ff_ref = bf16[8,144,128]{2,1,0:T(8,128)(2,1)S(1)} all-to-all(bf16[8,144,128]{2,1,0:T(8,128)(2,1)S(1)} %get-tuple-element.69), channel_id=1, replica_groups=mesh['gx'=4,'gy'=8] {'gy'}, dimensions={0} | all-to-all | bytes 589824 | tf_op jit(solution)/shard_map/all_to_all | solution.py:45
  79.7 1.5 %collective-permute-start.25 = (bf16[64,768]{1,0:T(8,128)(2,1)S(1)}, bf16[64,768]{1,0:T(8,128)(2,1)S(1)}, u32[]{:S(2)}, u32[]{:S(2)}) collective-permute-start(bf16[64,768]{1,0:T(8,128)(2,1)S(1)} %pair_sum_ff.3), channel_id=1, source_target_pairs={{0,16},{8,24},{16,0},{24,8},{1,17},{9,25},{17,1},{25,9},{2,18},{10... | collective-permute-start | bytes 294920 | tf_op jit(solution)/shard_map/ppermute | solution.py:56
  81.1 5.6 %collective-permute-done.20.z2_ref = bf16[64,1536]{1,0:T(8,128)(2,1)S(1)} collective-permute-done((bf16[64,1536]{1,0:T(8,128)(2,1)S(1)}, bf16[64,1536]{1,0:T(8,128)(2,1)S(1)}, u32[]{:S(2)}, u32[]{:S(2)}) %collective-permute-start.20) | collective-permute-done | bytes 196640 | tf_op jit(solution)/shard_map/ppermute | solution.py:56
  88.1 1.0 collective-permute-start.27
  89.1 2.5 %collective-permute-done.22.refs_2_ = bf16[64,768]{1,0:T(8,128)(2,1)S(1)} collective-permute-done((bf16[64,768]{1,0:T(8,128)(2,1)S(1)}, bf16[64,768]{1,0:T(8,128)(2,1)S(1)}, u32[]{:S(2)}, u32[]{:S(2)}) %collective-permute-start.22) | collective-permute-done | bytes 98336 | tf_op jit(solution)/shard_map/ppermute | solution.py:56
  94.3 13.3 %all_to_all.21.parts_ref = bf16[8,144,128]{2,1,0:T(8,128)(2,1)S(1)} all-to-all(bf16[8,144,128]{2,1,0:T(8,128)(2,1)S(1)} %project_down.1), channel_id=1, replica_groups=mesh['gx'=4,'gy'=8] {'gy'}, dimensions={0} | all-to-all | bytes 589824 | tf_op jit(solution)/shard_map/all_to_all | solution.py:45
  107.8 1.0 collective-permute-start.30
  109.7 1.9 %collective-permute-done.30.refs_2_ = f32[32,128]{1,0:T(8,128)S(1)} collective-permute-done((f32[32,128]{1,0:T(8,128)S(1)}, f32[32,128]{1,0:T(8,128)S(1)}, u32[]{:S(2)}, u32[]{:S(2)}) %collective-permute-start.30) | collective-permute-done | bytes 16416 | tf_op jit(solution)/shard_map/ppermute | solution.py:56
  (91 shorter events, 17.1 us)
Async XLA Ops:
  1.7 18.5 %all-to-all-start = ((bf16[8,144,128]{2,1,0:T(8,128)(2,1)}), bf16[8,144,128]{2,1,0:T(8,128)(2,1)S(1)}, u32[]{:S(2)}, u32[]{:S(2)}) async-start(bf16[8,144,128]{2,1,0:T(8,128)(2,1)} %get-tuple-element.43), calls=%async_computation | async-start | bytes 589824 | tf_op jit(solution)/shard_map/all_to_all | solution.py:45
  9.1 12.3 %collective-permute-start.3 = (bf16[576,256]{1,0:T(8,128)(2,1)S(1)}, bf16[576,256]{1,0:T(8,128)(2,1)S(1)}, u32[]{:S(2)}, u32[]{:S(2)}) collective-permute-start(bf16[576,256]{1,0:T(8,128)(2,1)S(1)} %bitcast.7), channel_id=1, source_target_pairs={{0,1},{1,0},{2,3},{3,2},{4,5},{5,4},{6,7},{7,6},{8,9},{9,8},{10,11... | collective-permute-start | bytes 884744 | tf_op jit(solution)/shard_map/ppermute | solution.py:56
  11.2 26.2 %collective-permute-start.2 = (bf16[576,256]{1,0:T(8,128)(2,1)S(1)}, bf16[576,256]{1,0:T(8,128)(2,1)S(1)}, u32[]{:S(2)}, u32[]{:S(2)}) collective-permute-start(bf16[576,256]{1,0:T(8,128)(2,1)S(1)} %bitcast.8), channel_id=1, source_target_pairs={{0,2},{1,3},{2,0},{3,1},{4,6},{5,7},{6,4},{7,5},{8,10},{9,11},{10,... | collective-permute-start | bytes 884744 | tf_op jit(solution)/shard_map/ppermute | solution.py:56
  12.6 20.4 %collective-permute-start.5 = (bf16[288,256]{1,0:T(8,128)(2,1)S(1)}, bf16[288,256]{1,0:T(8,128)(2,1)S(1)}, u32[]{:S(2)}, u32[]{:S(2)}) collective-permute-start(bf16[288,256]{1,0:T(8,128)(2,1)S(1)} %get-tuple-element.79), channel_id=1, source_target_pairs={{0,4},{1,5},{2,6},{3,7},{4,0},{5,1},{6,2},{7,3},{8,12},{9,13},{10,... | collective-permute-start | bytes 442376 | tf_op jit(solution)/shard_map/ppermute | solution.py:56
  20.6 4.1 %collective-permute-start = (bf16[2,256,128]{2,1,0:T(8,128)(2,1)S(1)}, bf16[2,256,128]{2,1,0:T(8,128)(2,1)S(1)}, u32[]{:S(2)}, u32[]{:S(2)}) collective-permute-start(bf16[2,256,128]{2,1,0:T(8,128)(2,1)S(1)} %get-tuple-element.45), channel_id=1, source_target_pairs={{0,8},{8,0},{16,24},{24,16},{1,9},{9,1},{17,25},{25,17},{2,10},{10... | collective-permute-start | bytes 393224 | tf_op jit(solution)/shard_map/ppermute | solution.py:56
  21.4 12.3 %collective-permute-start.6 = (bf16[288,256]{1,0:T(8,128)(2,1)S(1)}, bf16[288,256]{1,0:T(8,128)(2,1)S(1)}, u32[]{:S(2)}, u32[]{:S(2)}) collective-permute-start(bf16[288,256]{1,0:T(8,128)(2,1)S(1)} %get-tuple-element.55), channel_id=1, source_target_pairs={{0,4},{1,5},{2,6},{3,7},{4,0},{5,1},{6,2},{7,3},{8,12},{9,13},{10,... | collective-permute-start | bytes 442376 | tf_op jit(solution)/shard_map/ppermute | solution.py:56
  23.2 14.1 %collective-permute-start.4 = (bf16[576,256]{1,0:T(8,128)(2,1)S(1)}, bf16[576,256]{1,0:T(8,128)(2,1)S(1)}, u32[]{:S(2)}, u32[]{:S(2)}) collective-permute-start(bf16[576,256]{1,0:T(8,128)(2,1)S(1)} %collective-permute-done.3.refs_1_), channel_id=1, source_target_pairs={{0,2},{1,3},{2,0},{3,1},{4,6},{5,7},{6,4},{7,5},{8,10},{9,11},{10,... | collective-permute-start | bytes 884744 | tf_op jit(solution)/shard_map/ppermute | solution.py:56
  24.7 4.3 %collective-permute-start.1 = (bf16[256,128]{1,0:T(8,128)(2,1)S(1)}, bf16[256,128]{1,0:T(8,128)(2,1)S(1)}, u32[]{:S(2)}, u32[]{:S(2)}) collective-permute-start(bf16[256,128]{1,0:T(8,128)(2,1)S(1)} %pair_sum.1), channel_id=1, source_target_pairs={{0,16},{8,24},{16,0},{24,8},{1,17},{9,25},{17,1},{25,9},{2,18},{10... | collective-permute-start | bytes 196616 | tf_op jit(solution)/shard_map/ppermute | solution.py:56
  29.7 10.7 %all-to-all-start.1 = ((bf16[8,32,128]{2,1,0:T(8,128)(2,1)}), bf16[8,32,128]{2,1,0:T(8,128)(2,1)S(1)}, u32[]{:S(2)}, u32[]{:S(2)}) async-start(bf16[8,32,128]{2,1,0:T(8,128)(2,1)} %share_sum.1), calls=%async_computation.1 | async-start | bytes 131072 | tf_op jit(solution)/shard_map/all_to_all | solution.py:45
  33.7 14.2 %collective-permute-start.13 = (bf16[576,256]{1,0:T(8,128)(2,1)S(1)}, bf16[576,256]{1,0:T(8,128)(2,1)S(1)}, u32[]{:S(2)}, u32[]{:S(2)}) collective-permute-start(bf16[576,256]{1,0:T(8,128)(2,1)S(1)} %constant_dynamic-update-slice_fusion.refs_4_), channel_id=1, source_target_pairs={{0,1},{1,0},{2,3},{3,2},{4,5},{5,4},{6,7},{7,6},{8,9},{9,8},{10,11... | collective-permute-start | bytes 884744 | tf_op jit(solution)/shard_map/ppermute | solution.py:56
  35.1 12.8 %collective-permute-start.14 = (bf16[576,256]{1,0:T(8,128)(2,1)S(1)}, bf16[576,256]{1,0:T(8,128)(2,1)S(1)}, u32[]{:S(2)}, u32[]{:S(2)}) collective-permute-start(bf16[576,256]{1,0:T(8,128)(2,1)S(1)} %constant_dynamic-update-slice_fusion.refs_4_), channel_id=1, source_target_pairs={{0,2},{1,3},{2,0},{3,1},{4,6},{5,7},{6,4},{7,5},{8,10},{9,11},{10,... | collective-permute-start | bytes 884744 | tf_op jit(solution)/shard_map/ppermute | solution.py:56
  40.5 4.4 %collective-permute-start.8 = (bf16[9,32,128]{2,1,0:T(8,128)(2,1)S(1)}, bf16[9,32,128]{2,1,0:T(8,128)(2,1)S(1)}, u32[]{:S(2)}, u32[]{:S(2)}) collective-permute-start(bf16[9,32,128]{2,1,0:T(8,128)(2,1)S(1)} %pack_shares.1.refs_0_), channel_id=1, source_target_pairs={{0,16},{8,24},{16,0},{24,8},{1,17},{9,25},{17,1},{25,9},{2,18},{10... | collective-permute-start | bytes 221192 | tf_op jit(solution)/shard_map/ppermute | solution.py:56
  42.0 2.8 %collective-permute-start.7 = (bf16[9,32,128]{2,1,0:T(8,128)(2,1)S(1)}, bf16[9,32,128]{2,1,0:T(8,128)(2,1)S(1)}, u32[]{:S(2)}, u32[]{:S(2)}) collective-permute-start(bf16[9,32,128]{2,1,0:T(8,128)(2,1)S(1)} %pack_shares.1.refs_0_), channel_id=1, source_target_pairs={{0,8},{8,0},{16,24},{24,16},{1,9},{9,1},{17,25},{25,17},{2,10},{10... | collective-permute-start | bytes 221192 | tf_op jit(solution)/shard_map/ppermute | solution.py:56
  44.9 1.3 %collective-permute-start.9 = (bf16[9,32,128]{2,1,0:T(8,128)(2,1)S(1)}, bf16[9,32,128]{2,1,0:T(8,128)(2,1)S(1)}, u32[]{:S(2)}, u32[]{:S(2)}) collective-permute-start(bf16[9,32,128]{2,1,0:T(8,128)(2,1)S(1)} %collective-permute-done.8.refs_2_), channel_id=1, source_target_pairs={{0,8},{8,0},{16,24},{24,16},{1,9},{9,1},{17,25},{25,17},{2,10},{10... | collective-permute-start | bytes 221192 | tf_op jit(solution)/shard_map/ppermute | solution.py:56
  47.9 9.1 %collective-permute-start.15 = (bf16[576,256]{1,0:T(8,128)(2,1)S(1)}, bf16[576,256]{1,0:T(8,128)(2,1)S(1)}, u32[]{:S(2)}, u32[]{:S(2)}) collective-permute-start(bf16[576,256]{1,0:T(8,128)(2,1)S(1)} %collective-permute-done.14.refs_6_), channel_id=1, source_target_pairs={{0,1},{1,0},{2,3},{3,2},{4,5},{5,4},{6,7},{7,6},{8,9},{9,8},{10,11... | collective-permute-start | bytes 884744 | tf_op jit(solution)/shard_map/ppermute | solution.py:56
  49.6 4.3 %collective-permute-start.11 = (bf16[17,16,128]{2,1,0:T(8,128)(2,1)S(1)}, bf16[17,16,128]{2,1,0:T(8,128)(2,1)S(1)}, u32[]{:S(2)}, u32[]{:S(2)}) collective-permute-start(bf16[17,16,128]{2,1,0:T(8,128)(2,1)S(1)} %pair_terms.1.own_ref), channel_id=1, source_target_pairs={{0,16},{8,24},{16,0},{24,8},{1,17},{9,25},{17,1},{25,9},{2,18},{10... | collective-permute-start | bytes 208904 | tf_op jit(solution)/shard_map/ppermute | solution.py:56
  54.1 1.3 %collective-permute-start.12 = (bf16[16,16,128]{2,1,0:T(8,128)(2,1)S(1)}, bf16[16,16,128]{2,1,0:T(8,128)(2,1)S(1)}, u32[]{:S(2)}, u32[]{:S(2)}) collective-permute-start(bf16[16,16,128]{2,1,0:T(8,128)(2,1)S(1)} %divide.1.own_ref), channel_id=1, source_target_pairs={{0,8},{8,0},{16,24},{24,16},{1,9},{9,1},{17,25},{25,17},{2,10},{10... | collective-permute-start | bytes 196616 | tf_op jit(solution)/shard_map/ppermute | solution.py:56
  57.9 1.9 %collective-permute-start.16 = (f32[32,128]{1,0:T(8,128)S(1)}, f32[32,128]{1,0:T(8,128)S(1)}, u32[]{:S(2)}, u32[]{:S(2)}) collective-permute-start(f32[32,128]{1,0:T(8,128)S(1)} %get-tuple-element.67.refs_0_), channel_id=1, source_target_pairs={{0,8},{8,0},{16,24},{24,16},{1,9},{9,1},{17,25},{25,17},{2,10},{10... | collective-permute-start | bytes 49160 | tf_op jit(solution)/shard_map/ppermute | solution.py:56
  58.0 3.8 %collective-permute-start.17 = (f32[32,128]{1,0:T(8,128)S(1)}, f32[32,128]{1,0:T(8,128)S(1)}, u32[]{:S(2)}, u32[]{:S(2)}) collective-permute-start(f32[32,128]{1,0:T(8,128)S(1)} %get-tuple-element.67.refs_0_), channel_id=1, source_target_pairs={{0,16},{8,24},{16,0},{24,8},{1,17},{9,25},{17,1},{25,9},{2,18},{10... | collective-permute-start | bytes 49160 | tf_op jit(solution)/shard_map/ppermute | solution.py:56
  59.5 3.2 %collective-permute-start.18 = (f32[32,128]{1,0:T(8,128)S(1)}, f32[32,128]{1,0:T(8,128)S(1)}, u32[]{:S(2)}, u32[]{:S(2)}) collective-permute-start(f32[32,128]{1,0:T(8,128)S(1)} %get-tuple-element.67.refs_0_), channel_id=1, source_target_pairs={{0,24},{8,16},{16,8},{24,0},{1,25},{9,17},{17,9},{25,1},{2,26},{10... | collective-permute-start | bytes 49160 | tf_op jit(solution)/shard_map/ppermute | solution.py:56
  77.1 1.8 %collective-permute-start.19 = (bf16[2,64,1536]{2,1,0:T(8,128)(2,1)S(1)}, bf16[2,64,1536]{2,1,0:T(8,128)(2,1)S(1)}, u32[]{:S(2)}, u32[]{:S(2)}) collective-permute-start(bf16[2,64,1536]{2,1,0:T(8,128)(2,1)S(1)} %get-tuple-element.71), channel_id=1, source_target_pairs={{0,8},{8,0},{16,24},{24,16},{1,9},{9,1},{17,25},{25,17},{2,10},{10... | collective-permute-start | bytes 1179656 | tf_op jit(solution)/shard_map/ppermute | solution.py:56
  77.7 1.9 %collective-permute-start.24 = (bf16[2,64,768]{2,1,0:T(8,128)(2,1)S(1)}, bf16[2,64,768]{2,1,0:T(8,128)(2,1)S(1)}, u32[]{:S(2)}, u32[]{:S(2)}) collective-permute-start(bf16[2,64,768]{2,1,0:T(8,128)(2,1)S(1)} %get-tuple-element.74), channel_id=1, source_target_pairs={{0,8},{8,0},{16,24},{24,16},{1,9},{9,1},{17,25},{25,17},{2,10},{10... | collective-permute-start | bytes 589832 | tf_op jit(solution)/shard_map/ppermute | solution.py:56
  78.9 7.8 %collective-permute-start.20 = (bf16[64,1536]{1,0:T(8,128)(2,1)S(1)}, bf16[64,1536]{1,0:T(8,128)(2,1)S(1)}, u32[]{:S(2)}, u32[]{:S(2)}) collective-permute-start(bf16[64,1536]{1,0:T(8,128)(2,1)S(1)} %pair_sum_ff.2), channel_id=1, source_target_pairs={{0,16},{8,24},{16,0},{24,8},{1,17},{9,25},{17,1},{25,9},{2,18},{10... | collective-permute-start | bytes 589832 | tf_op jit(solution)/shard_map/ppermute | solution.py:56
  79.7 8.4 %collective-permute-start.25 = (bf16[64,768]{1,0:T(8,128)(2,1)S(1)}, bf16[64,768]{1,0:T(8,128)(2,1)S(1)}, u32[]{:S(2)}, u32[]{:S(2)}) collective-permute-start(bf16[64,768]{1,0:T(8,128)(2,1)S(1)} %pair_sum_ff.3), channel_id=1, source_target_pairs={{0,16},{8,24},{16,0},{24,8},{1,17},{9,25},{17,1},{25,9},{2,18},{10... | collective-permute-start | bytes 294920 | tf_op jit(solution)/shard_map/ppermute | solution.py:56
  86.9 4.8 %collective-permute-start.22 = (bf16[64,768]{1,0:T(8,128)(2,1)S(1)}, bf16[64,768]{1,0:T(8,128)(2,1)S(1)}, u32[]{:S(2)}, u32[]{:S(2)}) collective-permute-start(bf16[64,768]{1,0:T(8,128)(2,1)S(1)} %activate.2.refs_0_), channel_id=1, source_target_pairs={{0,16},{8,24},{16,0},{24,8},{1,17},{9,25},{17,1},{25,9},{2,18},{10... | collective-permute-start | bytes 294920 | tf_op jit(solution)/shard_map/ppermute | solution.py:56
  88.1 4.2 %collective-permute-start.27 = (bf16[64,384]{1,0:T(8,128)(2,1)S(1)}, bf16[64,384]{1,0:T(8,128)(2,1)S(1)}, u32[]{:S(2)}, u32[]{:S(2)}) collective-permute-start(bf16[64,384]{1,0:T(8,128)(2,1)S(1)} %activate.3.refs_4_), channel_id=1, source_target_pairs={{0,16},{8,24},{16,0},{24,8},{1,17},{9,25},{17,1},{25,9},{2,18},{10... | collective-permute-start | bytes 147464 | tf_op jit(solution)/shard_map/ppermute | solution.py:56
  89.1 4.4 %collective-permute-start.21 = (bf16[64,768]{1,0:T(8,128)(2,1)S(1)}, bf16[64,768]{1,0:T(8,128)(2,1)S(1)}, u32[]{:S(2)}, u32[]{:S(2)}) collective-permute-start(bf16[64,768]{1,0:T(8,128)(2,1)S(1)} %activate.2.refs_0_), channel_id=1, source_target_pairs={{0,8},{8,0},{16,24},{24,16},{1,9},{9,1},{17,25},{25,17},{2,10},{10... | collective-permute-start | bytes 294920 | tf_op jit(solution)/shard_map/ppermute | solution.py:56
  91.7 1.8 %collective-permute-start.23 = (bf16[64,768]{1,0:T(8,128)(2,1)S(1)}, bf16[64,768]{1,0:T(8,128)(2,1)S(1)}, u32[]{:S(2)}, u32[]{:S(2)}) collective-permute-start(bf16[64,768]{1,0:T(8,128)(2,1)S(1)} %collective-permute-done.22.refs_2_), channel_id=1, source_target_pairs={{0,8},{8,0},{16,24},{24,16},{1,9},{9,1},{17,25},{25,17},{2,10},{10... | collective-permute-start | bytes 294920 | tf_op jit(solution)/shard_map/ppermute | solution.py:56
  91.7 1.4 %collective-permute-start.26 = (bf16[64,384]{1,0:T(8,128)(2,1)S(1)}, bf16[64,384]{1,0:T(8,128)(2,1)S(1)}, u32[]{:S(2)}, u32[]{:S(2)}) collective-permute-start(bf16[64,384]{1,0:T(8,128)(2,1)S(1)} %activate.3.refs_4_), channel_id=1, source_target_pairs={{0,8},{8,0},{16,24},{24,16},{1,9},{9,1},{17,25},{25,17},{2,10},{10... | collective-permute-start | bytes 147464 | tf_op jit(solution)/shard_map/ppermute | solution.py:56
  107.8 1.9 %collective-permute-start.29 = (f32[32,128]{1,0:T(8,128)S(1)}, f32[32,128]{1,0:T(8,128)S(1)}, u32[]{:S(2)}, u32[]{:S(2)}) collective-permute-start(f32[32,128]{1,0:T(8,128)S(1)} %get-tuple-element.76.refs_0_), channel_id=1, source_target_pairs={{0,8},{8,0},{16,24},{24,16},{1,9},{9,1},{17,25},{25,17},{2,10},{10... | collective-permute-start | bytes 49160 | tf_op jit(solution)/shard_map/ppermute | solution.py:56
  107.8 3.8 %collective-permute-start.30 = (f32[32,128]{1,0:T(8,128)S(1)}, f32[32,128]{1,0:T(8,128)S(1)}, u32[]{:S(2)}, u32[]{:S(2)}) collective-permute-start(f32[32,128]{1,0:T(8,128)S(1)} %get-tuple-element.76.refs_0_), channel_id=1, source_target_pairs={{0,16},{8,24},{16,0},{24,8},{1,17},{9,25},{17,1},{25,9},{2,18},{10... | collective-permute-start | bytes 49160 | tf_op jit(solution)/shard_map/ppermute | solution.py:56
  108.8 3.2 %collective-permute-start.31 = (f32[32,128]{1,0:T(8,128)S(1)}, f32[32,128]{1,0:T(8,128)S(1)}, u32[]{:S(2)}, u32[]{:S(2)}) collective-permute-start(f32[32,128]{1,0:T(8,128)S(1)} %get-tuple-element.76.refs_0_), channel_id=1, source_target_pairs={{0,24},{8,16},{16,8},{24,0},{1,25},{9,17},{17,9},{25,1},{2,26},{10... | collective-permute-start | bytes 49160 | tf_op jit(solution)/shard_map/ppermute | solution.py:56
  (15 other events, 217.9 us)

commit v17 on v16

--- a/solution.py
+++ b/solution.py
@@ -56,13 +56,19 @@
     return lax.ppermute(values, axis, [(i, i ^ m) for i in range(count)])
 
 
-def trade(blocks, axis):
-    return [blocks[0]] + [permute(blocks[m], axis, m) for m in range(1, len(blocks))]
-
-
 def gather_gx(values):
     across = permute(values, "gx", 2)
     return [values, permute(values, "gx", 1), across, permute(across, "gx", 1)]
+
+
+def gx_terms(values):
+    def add(a_ref, b_ref, out_ref):
+        out_ref[...] = a_ref[...] + b_ref[...]
+
+    (pair,) = run(
+        "pair_add", add, [(values.shape, values.dtype)], (values, permute(values, "gx", 1))
+    )
+    return pair, permute(pair, "gx", 2)
 
 
 def weight_of(scores):
@@ -393,11 +399,11 @@
         (attended, others, x_own, norm_gains, *[w_blocks[m] for m in range(ny)]),
         scratch=[pltpu.VMEM((2, 2 * HEADS, half, PAGE), BF)],
     )
-    sums = trade([sums] * nx, "gx")
+    sums = gx_terms(sums)
 
     def mix(*refs):
-        attn_ref, x_ref, gain_ref, mixed_ref, ff_ref = refs[nx:]
-        total = sum(r[...] for r in refs[:nx])
+        attn_ref, x_ref, gain_ref, mixed_ref, ff_ref = refs[2:]
+        total = refs[0][...] + refs[1][...]
         plain, scaled, cross, square = (total[:, n : n + 1] for n in range(4))
         scale = lax.rsqrt(plain / D + EPSILON)
         mixed = x_ref[...].astype(F32) + attn_ref[...] * scale * (1.0 + gain_ref[1:2])
@@ -489,11 +495,11 @@
     down, sums = run(
         "down_sum", down_sum, [((rows, width), F32), ((rows, PAGE), F32)], (down,)
     )
-    sums = trade([sums] * nx, "gx")
+    sums = gx_terms(sums)
 
     def finish(*refs):
-        down_ref, mixed_ref, gain_ref, out_ref = refs[nx:]
-        square = sum(r[...] for r in refs[:nx])[:, 0:1]
+        down_ref, mixed_ref, gain_ref, out_ref = refs[2:]
+        square = (refs[0][...] + refs[1][...])[:, 0:1]
         scale = lax.rsqrt(square / D + EPSILON)
         out = mixed_ref[...] + down_ref[...] * scale * (1.0 + gain_ref[3:4])
         out_ref[...] = out.reshape(beams, steps, width).astype(BF)

time: 113 us -> 113 us (level)
  waiting for transfers between devices: 38.1 us -> 39.4 us
    ppermute x32 -> x30, waiting for transfers between devices: 30 us -> 31.3 us  [permute(): return lax.ppermute(values, axis, [(i, i ^ m) for i in range(count)])]
    all_to_all x2, blocking collectives: 26.6 us -> 25.5 us  [exchange(): return lax.all_to_all(values, axes, split_axis=0, concat_axis=0, tiled=True)]
    pallas_call x20 -> x22, Pallas kernels: 9.16 us -> 9.17 us  [run(): pl.pallas_call(kernel, out_shape=[jax.ShapeDtypeStruct(s, d) for s, d in...]
    ppermute x32 -> x30, starting transfers between devices: 26 us -> 26 us  [permute(): return lax.ppermute(values, axis, [(i, i ^ m) for i in range(count)])]
  transfers between devices with their start and end apart: 34 -> 32, of which waited for: 21 -> 20; matrix products, arithmetic and copies ran while one was open for 0% -> 0% of each run, Pallas kernels for 4% -> 4%
where the time goes in v17:
time: 113 us
  waiting for transfers between devices  39.4 us (35%)
  starting transfers between devices  36.8 us (33%)
  blocking collectives  25.5 us (23%)
  Pallas kernels  9.17 us (8%)
    ppermute x30, waiting for transfers between devices, permute(): return lax.ppermute(values, axis, [(i, i ^ m) for i in range(count)])  31.3 us
    ppermute x30, starting transfers between devices, permute(): return lax.ppermute(values, axis, [(i, i ^ m) for i in range(count)])  26 us
    all_to_all x2, blocking collectives, exchange(): return lax.all_to_all(values, axes, split_axis=0, concat_axis=0, tiled=True)  25.5 us
    all_to_all x2, starting transfers between devices, exchange(): return lax.all_to_all(values, axes, split_axis=0, concat_axis=0, tiled=True)  10.7 us
    pallas_call x22, Pallas kernels, run(): pl.pallas_call(kernel, out_shape=[jax.ShapeDtypeStruct(s, d) for s, d in...  9.17 us
    all_to_all x2, waiting for transfers between devices, exchange(): return lax.all_to_all(values, axes, split_axis=0, concat_axis=0, tiled=True)  8.11 us
  transfers between devices with their start and end apart: 32, of which 20 were waited for; matrix products, arithmetic and copies ran while one was open for 0% of the time, Pallas kernels for 4%

profile of v17, /device:TPU:0, one launch (start us, length us, event | category | flops | bytes accessed | tf_op | source)
XLA Modules:
  0.0 112.9 jit_solution(1114256104184617986)
XLA Ops:
  1.6 7.4 %all-to-all-start = ((bf16[8,144,128]{2,1,0:T(8,128)(2,1)}), bf16[8,144,128]{2,1,0:T(8,128)(2,1)S(1)}, u32[]{:S(2)}, u32[]{:S(2)}) async-start(bf16[8,144,128]{2,1,0:T(8,128)(2,1)} %get-tuple-element.43), calls=%async_computation | async-start | bytes 589824 | tf_op jit(solution)/shard_map/all_to_all | solution.py:45
  9.1 2.1 %collective-permute-start.3 = (bf16[576,256]{1,0:T(8,128)(2,1)S(1)}, bf16[576,256]{1,0:T(8,128)(2,1)S(1)}, u32[]{:S(2)}, u32[]{:S(2)}) collective-permute-start(bf16[576,256]{1,0:T(8,128)(2,1)S(1)} %bitcast.7), channel_id=1, source_target_pairs={{0,1},{1,0},{2,3},{3,2},{4,5},{5,4},{6,7},{7,6},{8,9},{9,8},{10,11... | collective-permute-start | bytes 884744 | tf_op jit(solution)/shard_map/ppermute | solution.py:56
  11.1 1.5 %collective-permute-start.2 = (bf16[576,256]{1,0:T(8,128)(2,1)S(1)}, bf16[576,256]{1,0:T(8,128)(2,1)S(1)}, u32[]{:S(2)}, u32[]{:S(2)}) collective-permute-start(bf16[576,256]{1,0:T(8,128)(2,1)S(1)} %bitcast.8), channel_id=1, source_target_pairs={{0,2},{1,3},{2,0},{3,1},{4,6},{5,7},{6,4},{7,5},{8,10},{9,11},{10,... | collective-permute-start | bytes 884744 | tf_op jit(solution)/shard_map/ppermute | solution.py:56
  12.6 2.4 %collective-permute-start.5 = (bf16[288,256]{1,0:T(8,128)(2,1)S(1)}, bf16[288,256]{1,0:T(8,128)(2,1)S(1)}, u32[]{:S(2)}, u32[]{:S(2)}) collective-permute-start(bf16[288,256]{1,0:T(8,128)(2,1)S(1)} %get-tuple-element.79), channel_id=1, source_target_pairs={{0,4},{1,5},{2,6},{3,7},{4,0},{5,1},{6,2},{7,3},{8,12},{9,13},{10,... | collective-permute-start | bytes 442376 | tf_op jit(solution)/shard_map/ppermute | solution.py:56
  15.1 5.0 %all-to-all-done.x_ref = bf16[8,144,128]{2,1,0:T(8,128)(2,1)S(1)} async-done(((bf16[8,144,128]{2,1,0:T(8,128)(2,1)}), bf16[8,144,128]{2,1,0:T(8,128)(2,1)S(1)}, u32[]{:S(2)}, u32[]{:S(2)}) %all-to-all-start) | async-done | bytes 294944 | tf_op jit(solution)/shard_map/all_to_all | solution.py:45
  21.3 1.9 %collective-permute-start.6 = (bf16[288,256]{1,0:T(8,128)(2,1)S(1)}, bf16[288,256]{1,0:T(8,128)(2,1)S(1)}, u32[]{:S(2)}, u32[]{:S(2)}) collective-permute-start(bf16[288,256]{1,0:T(8,128)(2,1)S(1)} %get-tuple-element.55), channel_id=1, source_target_pairs={{0,4},{1,5},{2,6},{3,7},{4,0},{5,1},{6,2},{7,3},{8,12},{9,13},{10,... | collective-permute-start | bytes 442376 | tf_op jit(solution)/shard_map/ppermute | solution.py:56
  23.2 1.5 %collective-permute-start.4 = (bf16[576,256]{1,0:T(8,128)(2,1)S(1)}, bf16[576,256]{1,0:T(8,128)(2,1)S(1)}, u32[]{:S(2)}, u32[]{:S(2)}) collective-permute-start(bf16[576,256]{1,0:T(8,128)(2,1)S(1)} %collective-permute-done.3.refs_1_), channel_id=1, source_target_pairs={{0,2},{1,3},{2,0},{3,1},{4,6},{5,7},{6,4},{7,5},{8,10},{9,11},{10,... | collective-permute-start | bytes 884744 | tf_op jit(solution)/shard_map/ppermute | solution.py:56
  24.7 1.6 %collective-permute-start.1 = (bf16[256,128]{1,0:T(8,128)(2,1)S(1)}, bf16[256,128]{1,0:T(8,128)(2,1)S(1)}, u32[]{:S(2)}, u32[]{:S(2)}) collective-permute-start(bf16[256,128]{1,0:T(8,128)(2,1)S(1)} %pair_sum.1), channel_id=1, source_target_pairs={{0,16},{8,24},{16,0},{24,8},{1,17},{9,25},{17,1},{25,9},{2,18},{10... | collective-permute-start | bytes 196616 | tf_op jit(solution)/shard_map/ppermute | solution.py:56
  26.5 2.6 %collective-permute-done.1.z2_ref = bf16[256,128]{1,0:T(8,128)(2,1)S(1)} collective-permute-done((bf16[256,128]{1,0:T(8,128)(2,1)S(1)}, bf16[256,128]{1,0:T(8,128)(2,1)S(1)}, u32[]{:S(2)}, u32[]{:S(2)}) %collective-permute-start.1) | collective-permute-done | bytes 65568 | tf_op jit(solution)/shard_map/ppermute | solution.py:56
  29.7 3.3 %all-to-all-start.1 = ((bf16[8,32,128]{2,1,0:T(8,128)(2,1)}), bf16[8,32,128]{2,1,0:T(8,128)(2,1)S(1)}, u32[]{:S(2)}, u32[]{:S(2)}) async-start(bf16[8,32,128]{2,1,0:T(8,128)(2,1)} %share_sum.1), calls=%async_computation.1 | async-start | bytes 131072 | tf_op jit(solution)/shard_map/all_to_all | solution.py:45
  33.7 1.4 %collective-permute-start.13 = (bf16[576,256]{1,0:T(8,128)(2,1)S(1)}, bf16[576,256]{1,0:T(8,128)(2,1)S(1)}, u32[]{:S(2)}, u32[]{:S(2)}) collective-permute-start(bf16[576,256]{1,0:T(8,128)(2,1)S(1)} %constant_dynamic-update-slice_fusion.refs_4_), channel_id=1, source_target_pairs={{0,1},{1,0},{2,3},{3,2},{4,5},{5,4},{6,7},{7,6},{8,9},{9,8},{10,11... | collective-permute-start | bytes 884744 | tf_op jit(solution)/shard_map/ppermute | solution.py:56
  35.1 1.5 %collective-permute-start.14 = (bf16[576,256]{1,0:T(8,128)(2,1)S(1)}, bf16[576,256]{1,0:T(8,128)(2,1)S(1)}, u32[]{:S(2)}, u32[]{:S(2)}) collective-permute-start(bf16[576,256]{1,0:T(8,128)(2,1)S(1)} %constant_dynamic-update-slice_fusion.refs_4_), channel_id=1, source_target_pairs={{0,2},{1,3},{2,0},{3,1},{4,6},{5,7},{6,4},{7,5},{8,10},{9,11},{10,... | collective-permute-start | bytes 884744 | tf_op jit(solution)/shard_map/ppermute | solution.py:56
  37.4 3.1 %all-to-all-done.1.share_ref = bf16[8,32,128]{2,1,0:T(8,128)(2,1)S(1)} async-done(((bf16[8,32,128]{2,1,0:T(8,128)(2,1)}), bf16[8,32,128]{2,1,0:T(8,128)(2,1)S(1)}, u32[]{:S(2)}, u32[]{:S(2)}) %all-to-all-start.1) | async-done | bytes 65568 | tf_op jit(solution)/shard_map/all_to_all | solution.py:45
  40.5 1.5 %collective-permute-start.8 = (bf16[9,32,128]{2,1,0:T(8,128)(2,1)S(1)}, bf16[9,32,128]{2,1,0:T(8,128)(2,1)S(1)}, u32[]{:S(2)}, u32[]{:S(2)}) collective-permute-start(bf16[9,32,128]{2,1,0:T(8,128)(2,1)S(1)} %pack_shares.1.refs_0_), channel_id=1, source_target_pairs={{0,16},{8,24},{16,0},{24,8},{1,17},{9,25},{17,1},{25,9},{2,18},{10... | collective-permute-start | bytes 221192 | tf_op jit(solution)/shard_map/ppermute | solution.py:56
  42.0 2.8 %collective-permute-done.8.refs_2_ = bf16[9,32,128]{2,1,0:T(8,128)(2,1)S(1)} collective-permute-done((bf16[9,32,128]{2,1,0:T(8,128)(2,1)S(1)}, bf16[9,32,128]{2,1,0:T(8,128)(2,1)S(1)}, u32[]{:S(2)}, u32[]{:S(2)}) %collective-permute-start.8) | collective-permute-done | bytes 73760 | tf_op jit(solution)/shard_map/ppermute | solution.py:56
  44.9 1.3 %collective-permute-done.9.refs_3_ = bf16[9,32,128]{2,1,0:T(8,128)(2,1)S(1)} collective-permute-done((bf16[9,32,128]{2,1,0:T(8,128)(2,1)S(1)}, bf16[9,32,128]{2,1,0:T(8,128)(2,1)S(1)}, u32[]{:S(2)}, u32[]{:S(2)}) %collective-permute-start.9) | collective-permute-done | bytes 73760 | tf_op jit(solution)/shard_map/ppermute | solution.py:56
  46.1 1.7 %attention.1 = (bf16[17,16,128]{2,1,0:T(8,128)(2,1)S(1)}, bf16[17,16,128]{2,1,0:T(8,128)(2,1)S(1)}) custom-call(bf16[9,32,128]{2,1,0:T(8,128)(2,1)S(1)} %pack_shares.1.refs_0_, bf16[9,32,128]{2,1,0:T(8,128)(2,1)S(1)} %collective-permute-done.7.refs_1_, bf16[9,32,128]{2,1,0:T(8,128)(2,1)S(1)} %collective-permute-done.8.refs_2_, ...), custom_call_target="tpu_custom_call" | custom-call | tf_op jit(solution)/shard_map/attention/pallas_call | solution.py:33
  48.2 1.2 %collective-permute-done.10.pair_ref = bf16[17,16,128]{2,1,0:T(8,128)(2,1)S(1)} collective-permute-done((bf16[17,16,128]{2,1,0:T(8,128)(2,1)S(1)}, bf16[17,16,128]{2,1,0:T(8,128)(2,1)S(1)}, u32[]{:S(2)}, u32[]{:S(2)}) %collective-permute-start.10) | collective-permute-done | bytes 69664 | tf_op jit(solution)/shard_map/ppermute | solution.py:56
  49.6 1.5 %collective-permute-start.11 = (bf16[17,16,128]{2,1,0:T(8,128)(2,1)S(1)}, bf16[17,16,128]{2,1,0:T(8,128)(2,1)S(1)}, u32[]{:S(2)}, u32[]{:S(2)}) collective-permute-start(bf16[17,16,128]{2,1,0:T(8,128)(2,1)S(1)} %pair_terms.1.own_ref), channel_id=1, source_target_pairs={{0,16},{8,24},{16,0},{24,8},{1,17},{9,25},{17,1},{25,9},{2,18},{10... | collective-permute-start | bytes 208904 | tf_op jit(solution)/shard_map/ppermute | solution.py:56
  51.1 2.8 %collective-permute-done.11.across_ref = bf16[17,16,128]{2,1,0:T(8,128)(2,1)S(1)} collective-permute-done((bf16[17,16,128]{2,1,0:T(8,128)(2,1)S(1)}, bf16[17,16,128]{2,1,0:T(8,128)(2,1)S(1)}, u32[]{:S(2)}, u32[]{:S(2)}) %collective-permute-start.11) | collective-permute-done | bytes 69664 | tf_op jit(solution)/shard_map/ppermute | solution.py:56
  54.2 1.2 %collective-permute-done.12.other_ref = bf16[16,16,128]{2,1,0:T(8,128)(2,1)S(1)} collective-permute-done((bf16[16,16,128]{2,1,0:T(8,128)(2,1)S(1)}, bf16[16,16,128]{2,1,0:T(8,128)(2,1)S(1)}, u32[]{:S(2)}, u32[]{:S(2)}) %collective-permute-start.12) | collective-permute-done | bytes 65568 | tf_op jit(solution)/shard_map/ppermute | solution.py:56
  55.4 1.6 %collective-permute-done.15.refs_7_ = bf16[576,256]{1,0:T(8,128)(2,1)S(1)} collective-permute-done((bf16[576,256]{1,0:T(8,128)(2,1)S(1)}, bf16[576,256]{1,0:T(8,128)(2,1)S(1)}, u32[]{:S(2)}, u32[]{:S(2)}) %collective-permute-start.15) | collective-permute-done | bytes 294944 | tf_op jit(solution)/shard_map/ppermute | solution.py:56
  59.1 1.5 %collective-permute-start.17 = (f32[32,128]{1,0:T(8,128)S(1)}, f32[32,128]{1,0:T(8,128)S(1)}, u32[]{:S(2)}, u32[]{:S(2)}) collective-permute-start(f32[32,128]{1,0:T(8,128)S(1)} %pair_add.2.refs_0_), channel_id=1, source_target_pairs={{0,16},{8,24},{16,0},{24,8},{1,17},{9,25},{17,1},{25,9},{2,18},{10... | collective-permute-start | bytes 49160 | tf_op jit(solution)/shard_map/ppermute | solution.py:56
  60.7 2.2 %collective-permute-done.17.refs_1_ = f32[32,128]{1,0:T(8,128)S(1)} collective-permute-done((f32[32,128]{1,0:T(8,128)S(1)}, f32[32,128]{1,0:T(8,128)S(1)}, u32[]{:S(2)}, u32[]{:S(2)}) %collective-permute-start.17) | collective-permute-done | bytes 16416 | tf_op jit(solution)/shard_map/ppermute | solution.py:56
  63.2 12.2 %all_to_all.20.ff_ref = bf16[8,144,128]{2,1,0:T(8,128)(2,1)S(1)} all-to-all(bf16[8,144,128]{2,1,0:T(8,128)(2,1)S(1)} %get-tuple-element.69), channel_id=1, replica_groups=mesh['gx'=4,'gy'=8] {'gy'}, dimensions={0} | all-to-all | bytes 589824 | tf_op jit(solution)/shard_map/all_to_all | solution.py:45
  78.0 1.6 %collective-permute-start.19 = (bf16[64,1536]{1,0:T(8,128)(2,1)S(1)}, bf16[64,1536]{1,0:T(8,128)(2,1)S(1)}, u32[]{:S(2)}, u32[]{:S(2)}) collective-permute-start(bf16[64,1536]{1,0:T(8,128)(2,1)S(1)} %pair_sum_ff.2), channel_id=1, source_target_pairs={{0,16},{8,24},{16,0},{24,8},{1,17},{9,25},{17,1},{25,9},{2,18},{10... | collective-permute-start | bytes 589832 | tf_op jit(solution)/shard_map/ppermute | solution.py:56
  80.2 5.6 %collective-permute-done.19.z2_ref = bf16[64,1536]{1,0:T(8,128)(2,1)S(1)} collective-permute-done((bf16[64,1536]{1,0:T(8,128)(2,1)S(1)}, bf16[64,1536]{1,0:T(8,128)(2,1)S(1)}, u32[]{:S(2)}, u32[]{:S(2)}) %collective-permute-start.19) | collective-permute-done | bytes 196640 | tf_op jit(solution)/shard_map/ppermute | solution.py:56
  85.9 1.6 %collective-permute-start.21 = (bf16[64,768]{1,0:T(8,128)(2,1)S(1)}, bf16[64,768]{1,0:T(8,128)(2,1)S(1)}, u32[]{:S(2)}, u32[]{:S(2)}) collective-permute-start(bf16[64,768]{1,0:T(8,128)(2,1)S(1)} %activate.2.refs_0_), channel_id=1, source_target_pairs={{0,16},{8,24},{16,0},{24,8},{1,17},{9,25},{17,1},{25,9},{2,18},{10... | collective-permute-start | bytes 294920 | tf_op jit(solution)/shard_map/ppermute | solution.py:56
  88.8 2.0 %collective-permute-done.21.refs_2_ = bf16[64,768]{1,0:T(8,128)(2,1)S(1)} collective-permute-done((bf16[64,768]{1,0:T(8,128)(2,1)S(1)}, bf16[64,768]{1,0:T(8,128)(2,1)S(1)}, u32[]{:S(2)}, u32[]{:S(2)}) %collective-permute-start.21) | collective-permute-done | bytes 98336 | tf_op jit(solution)/shard_map/ppermute | solution.py:56
  93.8 13.3 %all_to_all.21.parts_ref = bf16[8,144,128]{2,1,0:T(8,128)(2,1)S(1)} all-to-all(bf16[8,144,128]{2,1,0:T(8,128)(2,1)S(1)} %project_down.1), channel_id=1, replica_groups=mesh['gx'=4,'gy'=8] {'gy'}, dimensions={0} | all-to-all | bytes 589824 | tf_op jit(solution)/shard_map/all_to_all | solution.py:45
  107.3 1.2 %collective-permute-done.28.b_ref = f32[32,128]{1,0:T(8,128)S(1)} collective-permute-done((f32[32,128]{1,0:T(8,128)S(1)}, f32[32,128]{1,0:T(8,128)S(1)}, u32[]{:S(2)}, u32[]{:S(2)}) %collective-permute-start.28) | collective-permute-done | bytes 16416 | tf_op jit(solution)/shard_map/ppermute | solution.py:56
  109.5 2.6 %collective-permute-done.29.refs_1_ = f32[32,128]{1,0:T(8,128)S(1)} collective-permute-done((f32[32,128]{1,0:T(8,128)S(1)}, f32[32,128]{1,0:T(8,128)S(1)}, u32[]{:S(2)}, u32[]{:S(2)}) %collective-permute-start.29) | collective-permute-done | bytes 16416 | tf_op jit(solution)/shard_map/ppermute | solution.py:56
  (89 shorter events, 17.2 us)
Async XLA Ops:
  1.6 18.5 %all-to-all-start = ((bf16[8,144,128]{2,1,0:T(8,128)(2,1)}), bf16[8,144,128]{2,1,0:T(8,128)(2,1)S(1)}, u32[]{:S(2)}, u32[]{:S(2)}) async-start(bf16[8,144,128]{2,1,0:T(8,128)(2,1)} %get-tuple-element.43), calls=%async_computation | async-start | bytes 589824 | tf_op jit(solution)/shard_map/all_to_all | solution.py:45
  9.1 12.3 %collective-permute-start.3 = (bf16[576,256]{1,0:T(8,128)(2,1)S(1)}, bf16[576,256]{1,0:T(8,128)(2,1)S(1)}, u32[]{:S(2)}, u32[]{:S(2)}) collective-permute-start(bf16[576,256]{1,0:T(8,128)(2,1)S(1)} %bitcast.7), channel_id=1, source_target_pairs={{0,1},{1,0},{2,3},{3,2},{4,5},{5,4},{6,7},{7,6},{8,9},{9,8},{10,11... | collective-permute-start | bytes 884744 | tf_op jit(solution)/shard_map/ppermute | solution.py:56
  11.1 26.2 %collective-permute-start.2 = (bf16[576,256]{1,0:T(8,128)(2,1)S(1)}, bf16[576,256]{1,0:T(8,128)(2,1)S(1)}, u32[]{:S(2)}, u32[]{:S(2)}) collective-permute-start(bf16[576,256]{1,0:T(8,128)(2,1)S(1)} %bitcast.8), channel_id=1, source_target_pairs={{0,2},{1,3},{2,0},{3,1},{4,6},{5,7},{6,4},{7,5},{8,10},{9,11},{10,... | collective-permute-start | bytes 884744 | tf_op jit(solution)/shard_map/ppermute | solution.py:56
  12.6 20.4 %collective-permute-start.5 = (bf16[288,256]{1,0:T(8,128)(2,1)S(1)}, bf16[288,256]{1,0:T(8,128)(2,1)S(1)}, u32[]{:S(2)}, u32[]{:S(2)}) collective-permute-start(bf16[288,256]{1,0:T(8,128)(2,1)S(1)} %get-tuple-element.79), channel_id=1, source_target_pairs={{0,4},{1,5},{2,6},{3,7},{4,0},{5,1},{6,2},{7,3},{8,12},{9,13},{10,... | collective-permute-start | bytes 442376 | tf_op jit(solution)/shard_map/ppermute | solution.py:56
  20.6 4.1 %collective-permute-start = (bf16[2,256,128]{2,1,0:T(8,128)(2,1)S(1)}, bf16[2,256,128]{2,1,0:T(8,128)(2,1)S(1)}, u32[]{:S(2)}, u32[]{:S(2)}) collective-permute-start(bf16[2,256,128]{2,1,0:T(8,128)(2,1)S(1)} %get-tuple-element.45), channel_id=1, source_target_pairs={{0,8},{8,0},{16,24},{24,16},{1,9},{9,1},{17,25},{25,17},{2,10},{10... | collective-permute-start | bytes 393224 | tf_op jit(solution)/shard_map/ppermute | solution.py:56
  21.3 12.3 %collective-permute-start.6 = (bf16[288,256]{1,0:T(8,128)(2,1)S(1)}, bf16[288,256]{1,0:T(8,128)(2,1)S(1)}, u32[]{:S(2)}, u32[]{:S(2)}) collective-permute-start(bf16[288,256]{1,0:T(8,128)(2,1)S(1)} %get-tuple-element.55), channel_id=1, source_target_pairs={{0,4},{1,5},{2,6},{3,7},{4,0},{5,1},{6,2},{7,3},{8,12},{9,13},{10,... | collective-permute-start | bytes 442376 | tf_op jit(solution)/shard_map/ppermute | solution.py:56
  23.2 14.1 %collective-permute-start.4 = (bf16[576,256]{1,0:T(8,128)(2,1)S(1)}, bf16[576,256]{1,0:T(8,128)(2,1)S(1)}, u32[]{:S(2)}, u32[]{:S(2)}) collective-permute-start(bf16[576,256]{1,0:T(8,128)(2,1)S(1)} %collective-permute-done.3.refs_1_), channel_id=1, source_target_pairs={{0,2},{1,3},{2,0},{3,1},{4,6},{5,7},{6,4},{7,5},{8,10},{9,11},{10,... | collective-permute-start | bytes 884744 | tf_op jit(solution)/shard_map/ppermute | solution.py:56
  24.7 4.3 %collective-permute-start.1 = (bf16[256,128]{1,0:T(8,128)(2,1)S(1)}, bf16[256,128]{1,0:T(8,128)(2,1)S(1)}, u32[]{:S(2)}, u32[]{:S(2)}) collective-permute-start(bf16[256,128]{1,0:T(8,128)(2,1)S(1)} %pair_sum.1), channel_id=1, source_target_pairs={{0,16},{8,24},{16,0},{24,8},{1,17},{9,25},{17,1},{25,9},{2,18},{10... | collective-permute-start | bytes 196616 | tf_op jit(solution)/shard_map/ppermute | solution.py:56
  29.7 10.7 %all-to-all-start.1 = ((bf16[8,32,128]{2,1,0:T(8,128)(2,1)}), bf16[8,32,128]{2,1,0:T(8,128)(2,1)S(1)}, u32[]{:S(2)}, u32[]{:S(2)}) async-start(bf16[8,32,128]{2,1,0:T(8,128)(2,1)} %share_sum.1), calls=%async_computation.1 | async-start | bytes 131072 | tf_op jit(solution)/shard_map/all_to_all | solution.py:45
  33.7 14.2 %collective-permute-start.13 = (bf16[576,256]{1,0:T(8,128)(2,1)S(1)}, bf16[576,256]{1,0:T(8,128)(2,1)S(1)}, u32[]{:S(2)}, u32[]{:S(2)}) collective-permute-start(bf16[576,256]{1,0:T(8,128)(2,1)S(1)} %constant_dynamic-update-slice_fusion.refs_4_), channel_id=1, source_target_pairs={{0,1},{1,0},{2,3},{3,2},{4,5},{5,4},{6,7},{7,6},{8,9},{9,8},{10,11... | collective-permute-start | bytes 884744 | tf_op jit(solution)/shard_map/ppermute | solution.py:56
  35.1 12.8 %collective-permute-start.14 = (bf16[576,256]{1,0:T(8,128)(2,1)S(1)}, bf16[576,256]{1,0:T(8,128)(2,1)S(1)}, u32[]{:S(2)}, u32[]{:S(2)}) collective-permute-start(bf16[576,256]{1,0:T(8,128)(2,1)S(1)} %constant_dynamic-update-slice_fusion.refs_4_), channel_id=1, source_target_pairs={{0,2},{1,3},{2,0},{3,1},{4,6},{5,7},{6,4},{7,5},{8,10},{9,11},{10,... | collective-permute-start | bytes 884744 | tf_op jit(solution)/shard_map/ppermute | solution.py:56
  40.5 4.4 %collective-permute-start.8 = (bf16[9,32,128]{2,1,0:T(8,128)(2,1)S(1)}, bf16[9,32,128]{2,1,0:T(8,128)(2,1)S(1)}, u32[]{:S(2)}, u32[]{:S(2)}) collective-permute-start(bf16[9,32,128]{2,1,0:T(8,128)(2,1)S(1)} %pack_shares.1.refs_0_), channel_id=1, source_target_pairs={{0,16},{8,24},{16,0},{24,8},{1,17},{9,25},{17,1},{25,9},{2,18},{10... | collective-permute-start | bytes 221192 | tf_op jit(solution)/shard_map/ppermute | solution.py:56
  42.0 2.8 %collective-permute-start.7 = (bf16[9,32,128]{2,1,0:T(8,128)(2,1)S(1)}, bf16[9,32,128]{2,1,0:T(8,128)(2,1)S(1)}, u32[]{:S(2)}, u32[]{:S(2)}) collective-permute-start(bf16[9,32,128]{2,1,0:T(8,128)(2,1)S(1)} %pack_shares.1.refs_0_), channel_id=1, source_target_pairs={{0,8},{8,0},{16,24},{24,16},{1,9},{9,1},{17,25},{25,17},{2,10},{10... | collective-permute-start | bytes 221192 | tf_op jit(solution)/shard_map/ppermute | solution.py:56
  44.9 1.3 %collective-permute-start.9 = (bf16[9,32,128]{2,1,0:T(8,128)(2,1)S(1)}, bf16[9,32,128]{2,1,0:T(8,128)(2,1)S(1)}, u32[]{:S(2)}, u32[]{:S(2)}) collective-permute-start(bf16[9,32,128]{2,1,0:T(8,128)(2,1)S(1)} %collective-permute-done.8.refs_2_), channel_id=1, source_target_pairs={{0,8},{8,0},{16,24},{24,16},{1,9},{9,1},{17,25},{25,17},{2,10},{10... | collective-permute-start | bytes 221192 | tf_op jit(solution)/shard_map/ppermute | solution.py:56
  47.9 9.1 %collective-permute-start.15 = (bf16[576,256]{1,0:T(8,128)(2,1)S(1)}, bf16[576,256]{1,0:T(8,128)(2,1)S(1)}, u32[]{:S(2)}, u32[]{:S(2)}) collective-permute-start(bf16[576,256]{1,0:T(8,128)(2,1)S(1)} %collective-permute-done.14.refs_6_), channel_id=1, source_target_pairs={{0,1},{1,0},{2,3},{3,2},{4,5},{5,4},{6,7},{7,6},{8,9},{9,8},{10,11... | collective-permute-start | bytes 884744 | tf_op jit(solution)/shard_map/ppermute | solution.py:56
  48.2 1.3 %collective-permute-start.10 = (bf16[17,16,128]{2,1,0:T(8,128)(2,1)S(1)}, bf16[17,16,128]{2,1,0:T(8,128)(2,1)S(1)}, u32[]{:S(2)}, u32[]{:S(2)}) collective-permute-start(bf16[17,16,128]{2,1,0:T(8,128)(2,1)S(1)} %get-tuple-element.65), channel_id=1, source_target_pairs={{0,8},{8,0},{16,24},{24,16},{1,9},{9,1},{17,25},{25,17},{2,10},{10... | collective-permute-start | bytes 208904 | tf_op jit(solution)/shard_map/ppermute | solution.py:56
  49.6 4.3 %collective-permute-start.11 = (bf16[17,16,128]{2,1,0:T(8,128)(2,1)S(1)}, bf16[17,16,128]{2,1,0:T(8,128)(2,1)S(1)}, u32[]{:S(2)}, u32[]{:S(2)}) collective-permute-start(bf16[17,16,128]{2,1,0:T(8,128)(2,1)S(1)} %pair_terms.1.own_ref), channel_id=1, source_target_pairs={{0,16},{8,24},{16,0},{24,8},{1,17},{9,25},{17,1},{25,9},{2,18},{10... | collective-permute-start | bytes 208904 | tf_op jit(solution)/shard_map/ppermute | solution.py:56
  54.1 1.3 %collective-permute-start.12 = (bf16[16,16,128]{2,1,0:T(8,128)(2,1)S(1)}, bf16[16,16,128]{2,1,0:T(8,128)(2,1)S(1)}, u32[]{:S(2)}, u32[]{:S(2)}) collective-permute-start(bf16[16,16,128]{2,1,0:T(8,128)(2,1)S(1)} %divide.1.own_ref), channel_id=1, source_target_pairs={{0,8},{8,0},{16,24},{24,16},{1,9},{9,1},{17,25},{25,17},{2,10},{10... | collective-permute-start | bytes 196616 | tf_op jit(solution)/shard_map/ppermute | solution.py:56
  57.9 1.2 %collective-permute-start.16 = (f32[32,128]{1,0:T(8,128)S(1)}, f32[32,128]{1,0:T(8,128)S(1)}, u32[]{:S(2)}, u32[]{:S(2)}) collective-permute-start(f32[32,128]{1,0:T(8,128)S(1)} %get-tuple-element.67.a_ref), channel_id=1, source_target_pairs={{0,8},{8,0},{16,24},{24,16},{1,9},{9,1},{17,25},{25,17},{2,10},{10... | collective-permute-start | bytes 49160 | tf_op jit(solution)/shard_map/ppermute | solution.py:56
  59.1 3.7 %collective-permute-start.17 = (f32[32,128]{1,0:T(8,128)S(1)}, f32[32,128]{1,0:T(8,128)S(1)}, u32[]{:S(2)}, u32[]{:S(2)}) collective-permute-start(f32[32,128]{1,0:T(8,128)S(1)} %pair_add.2.refs_0_), channel_id=1, source_target_pairs={{0,16},{8,24},{16,0},{24,8},{1,17},{9,25},{17,1},{25,9},{2,18},{10... | collective-permute-start | bytes 49160 | tf_op jit(solution)/shard_map/ppermute | solution.py:56
  76.1 1.8 %collective-permute-start.18 = (bf16[2,64,1536]{2,1,0:T(8,128)(2,1)S(1)}, bf16[2,64,1536]{2,1,0:T(8,128)(2,1)S(1)}, u32[]{:S(2)}, u32[]{:S(2)}) collective-permute-start(bf16[2,64,1536]{2,1,0:T(8,128)(2,1)S(1)} %get-tuple-element.71), channel_id=1, source_target_pairs={{0,8},{8,0},{16,24},{24,16},{1,9},{9,1},{17,25},{25,17},{2,10},{10... | collective-permute-start | bytes 1179656 | tf_op jit(solution)/shard_map/ppermute | solution.py:56
  76.8 2.8 %collective-permute-start.23 = (bf16[2,64,768]{2,1,0:T(8,128)(2,1)S(1)}, bf16[2,64,768]{2,1,0:T(8,128)(2,1)S(1)}, u32[]{:S(2)}, u32[]{:S(2)}) collective-permute-start(bf16[2,64,768]{2,1,0:T(8,128)(2,1)S(1)} %get-tuple-element.74), channel_id=1, source_target_pairs={{0,8},{8,0},{16,24},{24,16},{1,9},{9,1},{17,25},{25,17},{2,10},{10... | collective-permute-start | bytes 589832 | tf_op jit(solution)/shard_map/ppermute | solution.py:56
  78.0 7.8 %collective-permute-start.19 = (bf16[64,1536]{1,0:T(8,128)(2,1)S(1)}, bf16[64,1536]{1,0:T(8,128)(2,1)S(1)}, u32[]{:S(2)}, u32[]{:S(2)}) collective-permute-start(bf16[64,1536]{1,0:T(8,128)(2,1)S(1)} %pair_sum_ff.2), channel_id=1, source_target_pairs={{0,16},{8,24},{16,0},{24,8},{1,17},{9,25},{17,1},{25,9},{2,18},{10... | collective-permute-start | bytes 589832 | tf_op jit(solution)/shard_map/ppermute | solution.py:56
  79.6 7.9 %collective-permute-start.24 = (bf16[64,768]{1,0:T(8,128)(2,1)S(1)}, bf16[64,768]{1,0:T(8,128)(2,1)S(1)}, u32[]{:S(2)}, u32[]{:S(2)}) collective-permute-start(bf16[64,768]{1,0:T(8,128)(2,1)S(1)} %pair_sum_ff.3), channel_id=1, source_target_pairs={{0,16},{8,24},{16,0},{24,8},{1,17},{9,25},{17,1},{25,9},{2,18},{10... | collective-permute-start | bytes 294920 | tf_op jit(solution)/shard_map/ppermute | solution.py:56
  85.9 4.8 %collective-permute-start.21 = (bf16[64,768]{1,0:T(8,128)(2,1)S(1)}, bf16[64,768]{1,0:T(8,128)(2,1)S(1)}, u32[]{:S(2)}, u32[]{:S(2)}) collective-permute-start(bf16[64,768]{1,0:T(8,128)(2,1)S(1)} %activate.2.refs_0_), channel_id=1, source_target_pairs={{0,16},{8,24},{16,0},{24,8},{1,17},{9,25},{17,1},{25,9},{2,18},{10... | collective-permute-start | bytes 294920 | tf_op jit(solution)/shard_map/ppermute | solution.py:56
  87.6 4.2 %collective-permute-start.26 = (bf16[64,384]{1,0:T(8,128)(2,1)S(1)}, bf16[64,384]{1,0:T(8,128)(2,1)S(1)}, u32[]{:S(2)}, u32[]{:S(2)}) collective-permute-start(bf16[64,384]{1,0:T(8,128)(2,1)S(1)} %activate.3.refs_4_), channel_id=1, source_target_pairs={{0,16},{8,24},{16,0},{24,8},{1,17},{9,25},{17,1},{25,9},{2,18},{10... | collective-permute-start | bytes 147464 | tf_op jit(solution)/shard_map/ppermute | solution.py:56
  88.8 4.2 %collective-permute-start.20 = (bf16[64,768]{1,0:T(8,128)(2,1)S(1)}, bf16[64,768]{1,0:T(8,128)(2,1)S(1)}, u32[]{:S(2)}, u32[]{:S(2)}) collective-permute-start(bf16[64,768]{1,0:T(8,128)(2,1)S(1)} %activate.2.refs_0_), channel_id=1, source_target_pairs={{0,8},{8,0},{16,24},{24,16},{1,9},{9,1},{17,25},{25,17},{2,10},{10... | collective-permute-start | bytes 294920 | tf_op jit(solution)/shard_map/ppermute | solution.py:56
  90.7 2.3 %collective-permute-start.22 = (bf16[64,768]{1,0:T(8,128)(2,1)S(1)}, bf16[64,768]{1,0:T(8,128)(2,1)S(1)}, u32[]{:S(2)}, u32[]{:S(2)}) collective-permute-start(bf16[64,768]{1,0:T(8,128)(2,1)S(1)} %collective-permute-done.21.refs_2_), channel_id=1, source_target_pairs={{0,8},{8,0},{16,24},{24,16},{1,9},{9,1},{17,25},{25,17},{2,10},{10... | collective-permute-start | bytes 294920 | tf_op jit(solution)/shard_map/ppermute | solution.py:56
  90.7 1.4 %collective-permute-start.25 = (bf16[64,384]{1,0:T(8,128)(2,1)S(1)}, bf16[64,384]{1,0:T(8,128)(2,1)S(1)}, u32[]{:S(2)}, u32[]{:S(2)}) collective-permute-start(bf16[64,384]{1,0:T(8,128)(2,1)S(1)} %activate.3.refs_4_), channel_id=1, source_target_pairs={{0,8},{8,0},{16,24},{24,16},{1,9},{9,1},{17,25},{25,17},{2,10},{10... | collective-permute-start | bytes 147464 | tf_op jit(solution)/shard_map/ppermute | solution.py:56
  91.8 1.2 %collective-permute-start.27 = (bf16[64,384]{1,0:T(8,128)(2,1)S(1)}, bf16[64,384]{1,0:T(8,128)(2,1)S(1)}, u32[]{:S(2)}, u32[]{:S(2)}) collective-permute-start(bf16[64,384]{1,0:T(8,128)(2,1)S(1)} %collective-permute-done.26.refs_6_), channel_id=1, source_target_pairs={{0,8},{8,0},{16,24},{24,16},{1,9},{9,1},{17,25},{25,17},{2,10},{10... | collective-permute-start | bytes 147464 | tf_op jit(solution)/shard_map/ppermute | solution.py:56
  107.2 1.2 %collective-permute-start.28 = (f32[32,128]{1,0:T(8,128)S(1)}, f32[32,128]{1,0:T(8,128)S(1)}, u32[]{:S(2)}, u32[]{:S(2)}) collective-permute-start(f32[32,128]{1,0:T(8,128)S(1)} %get-tuple-element.76.a_ref), channel_id=1, source_target_pairs={{0,8},{8,0},{16,24},{24,16},{1,9},{9,1},{17,25},{25,17},{2,10},{10... | collective-permute-start | bytes 49160 | tf_op jit(solution)/shard_map/ppermute | solution.py:56
  108.4 3.7 %collective-permute-start.29 = (f32[32,128]{1,0:T(8,128)S(1)}, f32[32,128]{1,0:T(8,128)S(1)}, u32[]{:S(2)}, u32[]{:S(2)}) collective-permute-start(f32[32,128]{1,0:T(8,128)S(1)} %pair_add.3.refs_0_), channel_id=1, source_target_pairs={{0,16},{8,24},{16,0},{24,8},{1,17},{9,25},{17,1},{25,9},{2,18},{10... | collective-permute-start | bytes 49160 | tf_op jit(solution)/shard_map/ppermute | solution.py:56
  (13 other events, 213.9 us)

commit v18 on v17

--- a/solution.py
+++ b/solution.py
@@ -54,6 +54,10 @@
 def permute(values, axis, m):
     count = lax.axis_size(axis)
     return lax.ppermute(values, axis, [(i, i ^ m) for i in range(count)])
+
+
+def trade(blocks, axis):
+    return [blocks[0]] + [permute(blocks[m], axis, m) for m in range(1, len(blocks))]
 
 
 def gather_gx(values):
@@ -237,9 +241,9 @@
 
     w_blocks = {0: w_own, 1: permute(w_own, "gy", 1), 2: permute(w_own, "gy", 2)}
     w_first = permute(w_split[: width // 2], "gy", 4)
-    w_late, _ = lax.optimization_barrier(((w_blocks[1], w_split[width // 2 :]), x_all))
-    w_blocks[3] = permute(w_late[0], "gy", 2)
-    w_second = permute(w_late[1], "gy", 4)
+    w_blocks[3] = permute(w_own, "gy", 3)
+    w_late, _ = lax.optimization_barrier((w_split[width // 2 :], x_all))
+    w_second = permute(w_late, "gy", 4)
 
     def project(x_ref, gain_ref, q_ref, k_ref, v_ref, z0_ref, z2_ref, z13_ref, held):
         gain = 1.0 + gain_ref[0:1]
@@ -287,7 +291,7 @@
     w_blocks[6] = permute(w_blocks[4], "gy", 2)
     w_blocks[5] = permute(w_blocks[4], "gy", 1)
     shares = exchange(shares, "gy")
-    beside = tables, cos, sin, w_blocks[2], w_blocks[3], w_blocks[4]
+    beside = tables, cos, sin, w_blocks[1], w_blocks[2], w_blocks[3], w_blocks[4]
     shares, (tables, cos, sin, *_) = lax.optimization_barrier((shares, beside))
 
     def pack_shares(share_ref, x_ref, out_ref):
@@ -495,11 +499,11 @@
     down, sums = run(
         "down_sum", down_sum, [((rows, width), F32), ((rows, PAGE), F32)], (down,)
     )
-    sums = gx_terms(sums)
+    sums = trade([sums] * nx, "gx")
 
     def finish(*refs):
-        down_ref, mixed_ref, gain_ref, out_ref = refs[2:]
-        square = (refs[0][...] + refs[1][...])[:, 0:1]
+        down_ref, mixed_ref, gain_ref, out_ref = refs[nx:]
+        square = sum(r[...] for r in refs[:nx])[:, 0:1]
         scale = lax.rsqrt(square / D + EPSILON)
         out = mixed_ref[...] + down_ref[...] * scale * (1.0 + gain_ref[3:4])
         out_ref[...] = out.reshape(beams, steps, width).astype(BF)

time: 113 us -> 114 us (level)
  starting transfers between devices: 36.8 us -> 33.4 us
  waiting for transfers between devices: 39.4 us -> 41.5 us
  blocking collectives: 25.5 us -> 27.4 us
    ppermute x30 -> x31, waiting for transfers between devices: 31.3 us -> 34.7 us  [permute(): return lax.ppermute(values, axis, [(i, i ^ m) for i in range(count)])]
    ppermute x30 -> x31, starting transfers between devices: 26 us -> 22.8 us  [permute(): return lax.ppermute(values, axis, [(i, i ^ m) for i in range(count)])]
    all_to_all x2, blocking collectives: 25.5 us -> 27.4 us  [exchange(): return lax.all_to_all(values, axes, split_axis=0, concat_axis=0, tiled=True)]
    all_to_all x2, waiting for transfers between devices: 8.11 us -> 6.89 us  [exchange(): return lax.all_to_all(values, axes, split_axis=0, concat_axis=0, tiled=True)]
    pallas_call x22 -> x21, Pallas kernels: 9.17 us -> 9.18 us  [run(): pl.pallas_call(kernel, out_shape=[jax.ShapeDtypeStruct(s, d) for s, d in...]
  transfers between devices with their start and end apart: 32 -> 33, of which waited for: 20 -> 20; matrix products, arithmetic and copies ran while one was open for 0% -> 0% of each run, Pallas kernels for 4% -> 4%
where the time goes in v18:
time: 114 us
  waiting for transfers between devices  41.5 us (36%)
  starting transfers between devices  33.4 us (29%)
  blocking collectives  27.4 us (24%)
  Pallas kernels  9.18 us (8%)
    ppermute x31, waiting for transfers between devices, permute(): return lax.ppermute(values, axis, [(i, i ^ m) for i in range(count)])  34.7 us
    all_to_all x2, blocking collectives, exchange(): return lax.all_to_all(values, axes, split_axis=0, concat_axis=0, tiled=True)  27.4 us
    ppermute x31, starting transfers between devices, permute(): return lax.ppermute(values, axis, [(i, i ^ m) for i in range(count)])  22.8 us
    all_to_all x2, starting transfers between devices, exchange(): return lax.all_to_all(values, axes, split_axis=0, concat_axis=0, tiled=True)  10.6 us
    pallas_call x21, Pallas kernels, run(): pl.pallas_call(kernel, out_shape=[jax.ShapeDtypeStruct(s, d) for s, d in...  9.18 us
    all_to_all x2, waiting for transfers between devices, exchange(): return lax.all_to_all(values, axes, split_axis=0, concat_axis=0, tiled=True)  6.89 us
  transfers between devices with their start and end apart: 33, of which 20 were waited for; matrix products, arithmetic and copies ran while one was open for 0% of the time, Pallas kernels for 4%

profile of v18, /device:TPU:0, one launch (start us, length us, event | category | flops | bytes accessed | tf_op | source)
XLA Modules:
  0.0 113.6 jit_solution(3933852089070220402)
XLA Ops:
  0.0 0.8 copy-done.10
  1.7 7.3 %all-to-all-start = ((bf16[8,144,128]{2,1,0:T(8,128)(2,1)}), bf16[8,144,128]{2,1,0:T(8,128)(2,1)S(1)}, u32[]{:S(2)}, u32[]{:S(2)}) async-start(bf16[8,144,128]{2,1,0:T(8,128)(2,1)} %get-tuple-element.42), calls=%async_computation | async-start | bytes 589824 | tf_op jit(solution)/shard_map/all_to_all | solution.py:45
  9.0 3.0 %collective-permute-start.4 = (bf16[576,256]{1,0:T(8,128)(2,1)S(1)}, bf16[576,256]{1,0:T(8,128)(2,1)S(1)}, u32[]{:S(2)}, u32[]{:S(2)}) collective-permute-start(bf16[576,256]{1,0:T(8,128)(2,1)S(1)} %bitcast.7), channel_id=1, source_target_pairs={{0,3},{1,2},{2,1},{3,0},{4,7},{5,6},{6,5},{7,4},{8,11},{9,10},{10,... | collective-permute-start | bytes 884744 | tf_op jit(solution)/shard_map/ppermute | solution.py:56
  12.6 6.9 %all-to-all-done.x_ref = bf16[8,144,128]{2,1,0:T(8,128)(2,1)S(1)} async-done(((bf16[8,144,128]{2,1,0:T(8,128)(2,1)}), bf16[8,144,128]{2,1,0:T(8,128)(2,1)S(1)}, u32[]{:S(2)}, u32[]{:S(2)}) %all-to-all-start) | async-done | bytes 294944 | tf_op jit(solution)/shard_map/all_to_all | solution.py:45
  21.4 1.6 %collective-permute-start.1 = (bf16[256,128]{1,0:T(8,128)(2,1)S(1)}, bf16[256,128]{1,0:T(8,128)(2,1)S(1)}, u32[]{:S(2)}, u32[]{:S(2)}) collective-permute-start(bf16[256,128]{1,0:T(8,128)(2,1)S(1)} %pair_sum.1), channel_id=1, source_target_pairs={{0,16},{8,24},{16,0},{24,8},{1,17},{9,25},{17,1},{25,9},{2,18},{10... | collective-permute-start | bytes 196616 | tf_op jit(solution)/shard_map/ppermute | solution.py:56
  23.0 2.7 %collective-permute-done.1.z2_ref = bf16[256,128]{1,0:T(8,128)(2,1)S(1)} collective-permute-done((bf16[256,128]{1,0:T(8,128)(2,1)S(1)}, bf16[256,128]{1,0:T(8,128)(2,1)S(1)}, u32[]{:S(2)}, u32[]{:S(2)}) %collective-permute-start.1) | collective-permute-done | bytes 65568 | tf_op jit(solution)/shard_map/ppermute | solution.py:56
  25.7 2.4 %collective-permute-start.6 = (bf16[288,256]{1,0:T(8,128)(2,1)S(1)}, bf16[288,256]{1,0:T(8,128)(2,1)S(1)}, u32[]{:S(2)}, u32[]{:S(2)}) collective-permute-start(bf16[288,256]{1,0:T(8,128)(2,1)S(1)} %get-tuple-element.53), channel_id=1, source_target_pairs={{0,4},{1,5},{2,6},{3,7},{4,0},{5,1},{6,2},{7,3},{8,12},{9,13},{10,... | collective-permute-start | bytes 442376 | tf_op jit(solution)/shard_map/ppermute | solution.py:56
  28.9 3.3 %all-to-all-start.1 = ((bf16[8,32,128]{2,1,0:T(8,128)(2,1)}), bf16[8,32,128]{2,1,0:T(8,128)(2,1)S(1)}, u32[]{:S(2)}, u32[]{:S(2)}) async-start(bf16[8,32,128]{2,1,0:T(8,128)(2,1)} %share_sum.1), calls=%async_computation.1 | async-start | bytes 131072 | tf_op jit(solution)/shard_map/all_to_all | solution.py:45
  32.2 6.8 %collective-permute-done.6 = bf16[288,256]{1,0:T(8,128)(2,1)S(1)} collective-permute-done((bf16[288,256]{1,0:T(8,128)(2,1)S(1)}, bf16[288,256]{1,0:T(8,128)(2,1)S(1)}, u32[]{:S(2)}, u32[]{:S(2)}) %collective-permute-start.6) | collective-permute-done | bytes 147488 | tf_op jit(solution)/shard_map/ppermute | solution.py:56
  40.4 1.5 %collective-permute-start.8 = (bf16[9,32,128]{2,1,0:T(8,128)(2,1)S(1)}, bf16[9,32,128]{2,1,0:T(8,128)(2,1)S(1)}, u32[]{:S(2)}, u32[]{:S(2)}) collective-permute-start(bf16[9,32,128]{2,1,0:T(8,128)(2,1)S(1)} %pack_shares.1.refs_0_), channel_id=1, source_target_pairs={{0,16},{8,24},{16,0},{24,8},{1,17},{9,25},{17,1},{25,9},{2,18},{10... | collective-permute-start | bytes 221192 | tf_op jit(solution)/shard_map/ppermute | solution.py:56
  41.9 2.8 %collective-permute-done.8.refs_2_ = bf16[9,32,128]{2,1,0:T(8,128)(2,1)S(1)} collective-permute-done((bf16[9,32,128]{2,1,0:T(8,128)(2,1)S(1)}, bf16[9,32,128]{2,1,0:T(8,128)(2,1)S(1)}, u32[]{:S(2)}, u32[]{:S(2)}) %collective-permute-start.8) | collective-permute-done | bytes 73760 | tf_op jit(solution)/shard_map/ppermute | solution.py:56
  44.8 1.3 %collective-permute-done.9.refs_3_ = bf16[9,32,128]{2,1,0:T(8,128)(2,1)S(1)} collective-permute-done((bf16[9,32,128]{2,1,0:T(8,128)(2,1)S(1)}, bf16[9,32,128]{2,1,0:T(8,128)(2,1)S(1)}, u32[]{:S(2)}, u32[]{:S(2)}) %collective-permute-start.9) | collective-permute-done | bytes 73760 | tf_op jit(solution)/shard_map/ppermute | solution.py:56
  46.0 1.7 %attention.1 = (bf16[17,16,128]{2,1,0:T(8,128)(2,1)S(1)}, bf16[17,16,128]{2,1,0:T(8,128)(2,1)S(1)}) custom-call(bf16[9,32,128]{2,1,0:T(8,128)(2,1)S(1)} %pack_shares.1.refs_0_, bf16[9,32,128]{2,1,0:T(8,128)(2,1)S(1)} %collective-permute-done.7.refs_1_, bf16[9,32,128]{2,1,0:T(8,128)(2,1)S(1)} %collective-permute-done.8.refs_2_, ...), custom_call_target="tpu_custom_call" | custom-call | tf_op jit(solution)/shard_map/attention/pallas_call | solution.py:33
  47.8 1.9 %collective-permute-start.15 = (bf16[576,256]{1,0:T(8,128)(2,1)S(1)}, bf16[576,256]{1,0:T(8,128)(2,1)S(1)}, u32[]{:S(2)}, u32[]{:S(2)}) collective-permute-start(bf16[576,256]{1,0:T(8,128)(2,1)S(1)} %collective-permute-done.14.refs_6_), channel_id=1, source_target_pairs={{0,1},{1,0},{2,3},{3,2},{4,5},{5,4},{6,7},{7,6},{8,9},{9,8},{10,11... | collective-permute-start | bytes 884744 | tf_op jit(solution)/shard_map/ppermute | solution.py:56
  49.7 1.3 %collective-permute-done.10.pair_ref = bf16[17,16,128]{2,1,0:T(8,128)(2,1)S(1)} collective-permute-done((bf16[17,16,128]{2,1,0:T(8,128)(2,1)S(1)}, bf16[17,16,128]{2,1,0:T(8,128)(2,1)S(1)}, u32[]{:S(2)}, u32[]{:S(2)}) %collective-permute-start.10) | collective-permute-done | bytes 69664 | tf_op jit(solution)/shard_map/ppermute | solution.py:56
  51.1 1.5 %collective-permute-start.11 = (bf16[17,16,128]{2,1,0:T(8,128)(2,1)S(1)}, bf16[17,16,128]{2,1,0:T(8,128)(2,1)S(1)}, u32[]{:S(2)}, u32[]{:S(2)}) collective-permute-start(bf16[17,16,128]{2,1,0:T(8,128)(2,1)S(1)} %pair_terms.1.own_ref), channel_id=1, source_target_pairs={{0,16},{8,24},{16,0},{24,8},{1,17},{9,25},{17,1},{25,9},{2,18},{10... | collective-permute-start | bytes 208904 | tf_op jit(solution)/shard_map/ppermute | solution.py:56
  52.6 2.8 %collective-permute-done.11.across_ref = bf16[17,16,128]{2,1,0:T(8,128)(2,1)S(1)} collective-permute-done((bf16[17,16,128]{2,1,0:T(8,128)(2,1)S(1)}, bf16[17,16,128]{2,1,0:T(8,128)(2,1)S(1)}, u32[]{:S(2)}, u32[]{:S(2)}) %collective-permute-start.11) | collective-permute-done | bytes 69664 | tf_op jit(solution)/shard_map/ppermute | solution.py:56
  55.7 1.2 %collective-permute-done.12.other_ref = bf16[16,16,128]{2,1,0:T(8,128)(2,1)S(1)} collective-permute-done((bf16[16,16,128]{2,1,0:T(8,128)(2,1)S(1)}, bf16[16,16,128]{2,1,0:T(8,128)(2,1)S(1)}, u32[]{:S(2)}, u32[]{:S(2)}) %collective-permute-start.12) | collective-permute-done | bytes 65568 | tf_op jit(solution)/shard_map/ppermute | solution.py:56
  57.0 0.8 project_out.1
  58.0 1.1 collective-permute-done.16.b_ref
  59.1 1.5 %collective-permute-start.17 = (f32[32,128]{1,0:T(8,128)S(1)}, f32[32,128]{1,0:T(8,128)S(1)}, u32[]{:S(2)}, u32[]{:S(2)}) collective-permute-start(f32[32,128]{1,0:T(8,128)S(1)} %pair_add.1.refs_0_), channel_id=1, source_target_pairs={{0,16},{8,24},{16,0},{24,8},{1,17},{9,25},{17,1},{25,9},{2,18},{10... | collective-permute-start | bytes 49160 | tf_op jit(solution)/shard_map/ppermute | solution.py:56
  60.6 2.2 %collective-permute-done.17.refs_1_ = f32[32,128]{1,0:T(8,128)S(1)} collective-permute-done((f32[32,128]{1,0:T(8,128)S(1)}, f32[32,128]{1,0:T(8,128)S(1)}, u32[]{:S(2)}, u32[]{:S(2)}) %collective-permute-start.17) | collective-permute-done | bytes 16416 | tf_op jit(solution)/shard_map/ppermute | solution.py:56
  63.1 14.1 %all_to_all.20.ff_ref = bf16[8,144,128]{2,1,0:T(8,128)(2,1)S(1)} all-to-all(bf16[8,144,128]{2,1,0:T(8,128)(2,1)S(1)} %get-tuple-element.67), channel_id=1, replica_groups=mesh['gx'=4,'gy'=8] {'gy'}, dimensions={0} | all-to-all | bytes 589824 | tf_op jit(solution)/shard_map/all_to_all | solution.py:45
  79.8 1.6 %collective-permute-start.19 = (bf16[64,1536]{1,0:T(8,128)(2,1)S(1)}, bf16[64,1536]{1,0:T(8,128)(2,1)S(1)}, u32[]{:S(2)}, u32[]{:S(2)}) collective-permute-start(bf16[64,1536]{1,0:T(8,128)(2,1)S(1)} %pair_sum_ff.2), channel_id=1, source_target_pairs={{0,16},{8,24},{16,0},{24,8},{1,17},{9,25},{17,1},{25,9},{2,18},{10... | collective-permute-start | bytes 589832 | tf_op jit(solution)/shard_map/ppermute | solution.py:56
  82.0 5.6 %collective-permute-done.19.z2_ref = bf16[64,1536]{1,0:T(8,128)(2,1)S(1)} collective-permute-done((bf16[64,1536]{1,0:T(8,128)(2,1)S(1)}, bf16[64,1536]{1,0:T(8,128)(2,1)S(1)}, u32[]{:S(2)}, u32[]{:S(2)}) %collective-permute-start.19) | collective-permute-done | bytes 196640 | tf_op jit(solution)/shard_map/ppermute | solution.py:56
  87.8 1.6 %collective-permute-start.21 = (bf16[64,768]{1,0:T(8,128)(2,1)S(1)}, bf16[64,768]{1,0:T(8,128)(2,1)S(1)}, u32[]{:S(2)}, u32[]{:S(2)}) collective-permute-start(bf16[64,768]{1,0:T(8,128)(2,1)S(1)} %activate.2.refs_0_), channel_id=1, source_target_pairs={{0,16},{8,24},{16,0},{24,8},{1,17},{9,25},{17,1},{25,9},{2,18},{10... | collective-permute-start | bytes 294920 | tf_op jit(solution)/shard_map/ppermute | solution.py:56
  89.4 1.2 %collective-permute-start.26 = (bf16[64,384]{1,0:T(8,128)(2,1)S(1)}, bf16[64,384]{1,0:T(8,128)(2,1)S(1)}, u32[]{:S(2)}, u32[]{:S(2)}) collective-permute-start(bf16[64,384]{1,0:T(8,128)(2,1)S(1)} %activate.3.refs_4_), channel_id=1, source_target_pairs={{0,16},{8,24},{16,0},{24,8},{1,17},{9,25},{17,1},{25,9},{2,18},{10... | collective-permute-start | bytes 147464 | tf_op jit(solution)/shard_map/ppermute | solution.py:56
  90.6 2.0 %collective-permute-done.21.refs_2_ = bf16[64,768]{1,0:T(8,128)(2,1)S(1)} collective-permute-done((bf16[64,768]{1,0:T(8,128)(2,1)S(1)}, bf16[64,768]{1,0:T(8,128)(2,1)S(1)}, u32[]{:S(2)}, u32[]{:S(2)}) %collective-permute-start.21) | collective-permute-done | bytes 98336 | tf_op jit(solution)/shard_map/ppermute | solution.py:56
  93.9 0.9 collective-permute-done.27.refs_7_
  95.6 13.3 %all_to_all.21.parts_ref = bf16[8,144,128]{2,1,0:T(8,128)(2,1)S(1)} all-to-all(bf16[8,144,128]{2,1,0:T(8,128)(2,1)S(1)} %project_down.1), channel_id=1, replica_groups=mesh['gx'=4,'gy'=8] {'gy'}, dimensions={0} | all-to-all | bytes 589824 | tf_op jit(solution)/shard_map/all_to_all | solution.py:45
  109.1 1.1 %collective-permute-start.29 = (f32[32,128]{1,0:T(8,128)S(1)}, f32[32,128]{1,0:T(8,128)S(1)}, u32[]{:S(2)}, u32[]{:S(2)}) collective-permute-start(f32[32,128]{1,0:T(8,128)S(1)} %get-tuple-element.74.refs_0_), channel_id=1, source_target_pairs={{0,16},{8,24},{16,0},{24,8},{1,17},{9,25},{17,1},{25,9},{2,18},{10... | collective-permute-start | bytes 49160 | tf_op jit(solution)/shard_map/ppermute | solution.py:56
  111.0 1.3 %collective-permute-done.30.refs_3_ = f32[32,128]{1,0:T(8,128)S(1)} collective-permute-done((f32[32,128]{1,0:T(8,128)S(1)}, f32[32,128]{1,0:T(8,128)S(1)}, u32[]{:S(2)}, u32[]{:S(2)}) %collective-permute-start.30) | collective-permute-done | bytes 16416 | tf_op jit(solution)/shard_map/ppermute | solution.py:56
  (90 shorter events, 13.5 us)
Async XLA Ops:
  1.7 17.8 %all-to-all-start = ((bf16[8,144,128]{2,1,0:T(8,128)(2,1)}), bf16[8,144,128]{2,1,0:T(8,128)(2,1)S(1)}, u32[]{:S(2)}, u32[]{:S(2)}) async-start(bf16[8,144,128]{2,1,0:T(8,128)(2,1)} %get-tuple-element.42), calls=%async_computation | async-start | bytes 589824 | tf_op jit(solution)/shard_map/all_to_all | solution.py:45
  9.0 31.3 %collective-permute-start.4 = (bf16[576,256]{1,0:T(8,128)(2,1)S(1)}, bf16[576,256]{1,0:T(8,128)(2,1)S(1)}, u32[]{:S(2)}, u32[]{:S(2)}) collective-permute-start(bf16[576,256]{1,0:T(8,128)(2,1)S(1)} %bitcast.7), channel_id=1, source_target_pairs={{0,3},{1,2},{2,1},{3,0},{4,7},{5,6},{6,5},{7,4},{8,11},{9,10},{10,... | collective-permute-start | bytes 884744 | tf_op jit(solution)/shard_map/ppermute | solution.py:56
  11.9 28.3 %collective-permute-start.3 = (bf16[576,256]{1,0:T(8,128)(2,1)S(1)}, bf16[576,256]{1,0:T(8,128)(2,1)S(1)}, u32[]{:S(2)}, u32[]{:S(2)}) collective-permute-start(bf16[576,256]{1,0:T(8,128)(2,1)S(1)} %bitcast.8), channel_id=1, source_target_pairs={{0,2},{1,3},{2,0},{3,1},{4,6},{5,7},{6,4},{7,5},{8,10},{9,11},{10,... | collective-permute-start | bytes 884744 | tf_op jit(solution)/shard_map/ppermute | solution.py:56
  12.5 27.8 %collective-permute-start.2 = (bf16[576,256]{1,0:T(8,128)(2,1)S(1)}, bf16[576,256]{1,0:T(8,128)(2,1)S(1)}, u32[]{:S(2)}, u32[]{:S(2)}) collective-permute-start(bf16[576,256]{1,0:T(8,128)(2,1)S(1)} %bitcast.9), channel_id=1, source_target_pairs={{0,1},{1,0},{2,3},{3,2},{4,5},{5,4},{6,7},{7,6},{8,9},{9,8},{10,11... | collective-permute-start | bytes 884744 | tf_op jit(solution)/shard_map/ppermute | solution.py:56
  19.9 1.4 %collective-permute-start = (bf16[2,256,128]{2,1,0:T(8,128)(2,1)S(1)}, bf16[2,256,128]{2,1,0:T(8,128)(2,1)S(1)}, u32[]{:S(2)}, u32[]{:S(2)}) collective-permute-start(bf16[2,256,128]{2,1,0:T(8,128)(2,1)S(1)} %get-tuple-element.44), channel_id=1, source_target_pairs={{0,8},{8,0},{16,24},{24,16},{1,9},{9,1},{17,25},{25,17},{2,10},{10... | collective-permute-start | bytes 393224 | tf_op jit(solution)/shard_map/ppermute | solution.py:56
  20.0 12.2 %collective-permute-start.5 = (bf16[288,256]{1,0:T(8,128)(2,1)S(1)}, bf16[288,256]{1,0:T(8,128)(2,1)S(1)}, u32[]{:S(2)}, u32[]{:S(2)}) collective-permute-start(bf16[288,256]{1,0:T(8,128)(2,1)S(1)} %get-tuple-element.78), channel_id=1, source_target_pairs={{0,4},{1,5},{2,6},{3,7},{4,0},{5,1},{6,2},{7,3},{8,12},{9,13},{10,... | collective-permute-start | bytes 442376 | tf_op jit(solution)/shard_map/ppermute | solution.py:56
  21.4 4.3 %collective-permute-start.1 = (bf16[256,128]{1,0:T(8,128)(2,1)S(1)}, bf16[256,128]{1,0:T(8,128)(2,1)S(1)}, u32[]{:S(2)}, u32[]{:S(2)}) collective-permute-start(bf16[256,128]{1,0:T(8,128)(2,1)S(1)} %pair_sum.1), channel_id=1, source_target_pairs={{0,16},{8,24},{16,0},{24,8},{1,17},{9,25},{17,1},{25,9},{2,18},{10... | collective-permute-start | bytes 196616 | tf_op jit(solution)/shard_map/ppermute | solution.py:56
  25.7 13.4 %collective-permute-start.6 = (bf16[288,256]{1,0:T(8,128)(2,1)S(1)}, bf16[288,256]{1,0:T(8,128)(2,1)S(1)}, u32[]{:S(2)}, u32[]{:S(2)}) collective-permute-start(bf16[288,256]{1,0:T(8,128)(2,1)S(1)} %get-tuple-element.53), channel_id=1, source_target_pairs={{0,4},{1,5},{2,6},{3,7},{4,0},{5,1},{6,2},{7,3},{8,12},{9,13},{10,... | collective-permute-start | bytes 442376 | tf_op jit(solution)/shard_map/ppermute | solution.py:56
  28.9 11.4 %all-to-all-start.1 = ((bf16[8,32,128]{2,1,0:T(8,128)(2,1)}), bf16[8,32,128]{2,1,0:T(8,128)(2,1)S(1)}, u32[]{:S(2)}, u32[]{:S(2)}) async-start(bf16[8,32,128]{2,1,0:T(8,128)(2,1)} %share_sum.1), calls=%async_computation.1 | async-start | bytes 131072 | tf_op jit(solution)/shard_map/all_to_all | solution.py:45
  39.1 8.7 %collective-permute-start.14 = (bf16[576,256]{1,0:T(8,128)(2,1)S(1)}, bf16[576,256]{1,0:T(8,128)(2,1)S(1)}, u32[]{:S(2)}, u32[]{:S(2)}) collective-permute-start(bf16[576,256]{1,0:T(8,128)(2,1)S(1)} %constant_dynamic-update-slice_fusion.refs_4_), channel_id=1, source_target_pairs={{0,2},{1,3},{2,0},{3,1},{4,6},{5,7},{6,4},{7,5},{8,10},{9,11},{10,... | collective-permute-start | bytes 884744 | tf_op jit(solution)/shard_map/ppermute | solution.py:56
  39.2 8.6 %collective-permute-start.13 = (bf16[576,256]{1,0:T(8,128)(2,1)S(1)}, bf16[576,256]{1,0:T(8,128)(2,1)S(1)}, u32[]{:S(2)}, u32[]{:S(2)}) collective-permute-start(bf16[576,256]{1,0:T(8,128)(2,1)S(1)} %constant_dynamic-update-slice_fusion.refs_4_), channel_id=1, source_target_pairs={{0,1},{1,0},{2,3},{3,2},{4,5},{5,4},{6,7},{7,6},{8,9},{9,8},{10,11... | collective-permute-start | bytes 884744 | tf_op jit(solution)/shard_map/ppermute | solution.py:56
  40.4 4.4 %collective-permute-start.8 = (bf16[9,32,128]{2,1,0:T(8,128)(2,1)S(1)}, bf16[9,32,128]{2,1,0:T(8,128)(2,1)S(1)}, u32[]{:S(2)}, u32[]{:S(2)}) collective-permute-start(bf16[9,32,128]{2,1,0:T(8,128)(2,1)S(1)} %pack_shares.1.refs_0_), channel_id=1, source_target_pairs={{0,16},{8,24},{16,0},{24,8},{1,17},{9,25},{17,1},{25,9},{2,18},{10... | collective-permute-start | bytes 221192 | tf_op jit(solution)/shard_map/ppermute | solution.py:56
  41.9 2.8 %collective-permute-start.7 = (bf16[9,32,128]{2,1,0:T(8,128)(2,1)S(1)}, bf16[9,32,128]{2,1,0:T(8,128)(2,1)S(1)}, u32[]{:S(2)}, u32[]{:S(2)}) collective-permute-start(bf16[9,32,128]{2,1,0:T(8,128)(2,1)S(1)} %pack_shares.1.refs_0_), channel_id=1, source_target_pairs={{0,8},{8,0},{16,24},{24,16},{1,9},{9,1},{17,25},{25,17},{2,10},{10... | collective-permute-start | bytes 221192 | tf_op jit(solution)/shard_map/ppermute | solution.py:56
  44.8 1.3 %collective-permute-start.9 = (bf16[9,32,128]{2,1,0:T(8,128)(2,1)S(1)}, bf16[9,32,128]{2,1,0:T(8,128)(2,1)S(1)}, u32[]{:S(2)}, u32[]{:S(2)}) collective-permute-start(bf16[9,32,128]{2,1,0:T(8,128)(2,1)S(1)} %collective-permute-done.8.refs_2_), channel_id=1, source_target_pairs={{0,8},{8,0},{16,24},{24,16},{1,9},{9,1},{17,25},{25,17},{2,10},{10... | collective-permute-start | bytes 221192 | tf_op jit(solution)/shard_map/ppermute | solution.py:56
  47.8 9.2 %collective-permute-start.15 = (bf16[576,256]{1,0:T(8,128)(2,1)S(1)}, bf16[576,256]{1,0:T(8,128)(2,1)S(1)}, u32[]{:S(2)}, u32[]{:S(2)}) collective-permute-start(bf16[576,256]{1,0:T(8,128)(2,1)S(1)} %collective-permute-done.14.refs_6_), channel_id=1, source_target_pairs={{0,1},{1,0},{2,3},{3,2},{4,5},{5,4},{6,7},{7,6},{8,9},{9,8},{10,11... | collective-permute-start | bytes 884744 | tf_op jit(solution)/shard_map/ppermute | solution.py:56
  49.7 1.3 %collective-permute-start.10 = (bf16[17,16,128]{2,1,0:T(8,128)(2,1)S(1)}, bf16[17,16,128]{2,1,0:T(8,128)(2,1)S(1)}, u32[]{:S(2)}, u32[]{:S(2)}) collective-permute-start(bf16[17,16,128]{2,1,0:T(8,128)(2,1)S(1)} %get-tuple-element.63), channel_id=1, source_target_pairs={{0,8},{8,0},{16,24},{24,16},{1,9},{9,1},{17,25},{25,17},{2,10},{10... | collective-permute-start | bytes 208904 | tf_op jit(solution)/shard_map/ppermute | solution.py:56
  51.1 4.3 %collective-permute-start.11 = (bf16[17,16,128]{2,1,0:T(8,128)(2,1)S(1)}, bf16[17,16,128]{2,1,0:T(8,128)(2,1)S(1)}, u32[]{:S(2)}, u32[]{:S(2)}) collective-permute-start(bf16[17,16,128]{2,1,0:T(8,128)(2,1)S(1)} %pair_terms.1.own_ref), channel_id=1, source_target_pairs={{0,16},{8,24},{16,0},{24,8},{1,17},{9,25},{17,1},{25,9},{2,18},{10... | collective-permute-start | bytes 208904 | tf_op jit(solution)/shard_map/ppermute | solution.py:56
  55.6 1.3 %collective-permute-start.12 = (bf16[16,16,128]{2,1,0:T(8,128)(2,1)S(1)}, bf16[16,16,128]{2,1,0:T(8,128)(2,1)S(1)}, u32[]{:S(2)}, u32[]{:S(2)}) collective-permute-start(bf16[16,16,128]{2,1,0:T(8,128)(2,1)S(1)} %divide.1.own_ref), channel_id=1, source_target_pairs={{0,8},{8,0},{16,24},{24,16},{1,9},{9,1},{17,25},{25,17},{2,10},{10... | collective-permute-start | bytes 196616 | tf_op jit(solution)/shard_map/ppermute | solution.py:56
  57.8 1.2 %collective-permute-start.16 = (f32[32,128]{1,0:T(8,128)S(1)}, f32[32,128]{1,0:T(8,128)S(1)}, u32[]{:S(2)}, u32[]{:S(2)}) collective-permute-start(f32[32,128]{1,0:T(8,128)S(1)} %get-tuple-element.65.a_ref), channel_id=1, source_target_pairs={{0,8},{8,0},{16,24},{24,16},{1,9},{9,1},{17,25},{25,17},{2,10},{10... | collective-permute-start | bytes 49160 | tf_op jit(solution)/shard_map/ppermute | solution.py:56
  59.1 3.7 %collective-permute-start.17 = (f32[32,128]{1,0:T(8,128)S(1)}, f32[32,128]{1,0:T(8,128)S(1)}, u32[]{:S(2)}, u32[]{:S(2)}) collective-permute-start(f32[32,128]{1,0:T(8,128)S(1)} %pair_add.1.refs_0_), channel_id=1, source_target_pairs={{0,16},{8,24},{16,0},{24,8},{1,17},{9,25},{17,1},{25,9},{2,18},{10... | collective-permute-start | bytes 49160 | tf_op jit(solution)/shard_map/ppermute | solution.py:56
  78.0 1.8 %collective-permute-start.18 = (bf16[2,64,1536]{2,1,0:T(8,128)(2,1)S(1)}, bf16[2,64,1536]{2,1,0:T(8,128)(2,1)S(1)}, u32[]{:S(2)}, u32[]{:S(2)}) collective-permute-start(bf16[2,64,1536]{2,1,0:T(8,128)(2,1)S(1)} %get-tuple-element.69), channel_id=1, source_target_pairs={{0,8},{8,0},{16,24},{24,16},{1,9},{9,1},{17,25},{25,17},{2,10},{10... | collective-permute-start | bytes 1179656 | tf_op jit(solution)/shard_map/ppermute | solution.py:56
  78.6 2.8 %collective-permute-start.23 = (bf16[2,64,768]{2,1,0:T(8,128)(2,1)S(1)}, bf16[2,64,768]{2,1,0:T(8,128)(2,1)S(1)}, u32[]{:S(2)}, u32[]{:S(2)}) collective-permute-start(bf16[2,64,768]{2,1,0:T(8,128)(2,1)S(1)} %get-tuple-element.72), channel_id=1, source_target_pairs={{0,8},{8,0},{16,24},{24,16},{1,9},{9,1},{17,25},{25,17},{2,10},{10... | collective-permute-start | bytes 589832 | tf_op jit(solution)/shard_map/ppermute | solution.py:56
  79.8 7.8 %collective-permute-start.19 = (bf16[64,1536]{1,0:T(8,128)(2,1)S(1)}, bf16[64,1536]{1,0:T(8,128)(2,1)S(1)}, u32[]{:S(2)}, u32[]{:S(2)}) collective-permute-start(bf16[64,1536]{1,0:T(8,128)(2,1)S(1)} %pair_sum_ff.2), channel_id=1, source_target_pairs={{0,16},{8,24},{16,0},{24,8},{1,17},{9,25},{17,1},{25,9},{2,18},{10... | collective-permute-start | bytes 589832 | tf_op jit(solution)/shard_map/ppermute | solution.py:56
  81.4 7.9 %collective-permute-start.24 = (bf16[64,768]{1,0:T(8,128)(2,1)S(1)}, bf16[64,768]{1,0:T(8,128)(2,1)S(1)}, u32[]{:S(2)}, u32[]{:S(2)}) collective-permute-start(bf16[64,768]{1,0:T(8,128)(2,1)S(1)} %pair_sum_ff.3), channel_id=1, source_target_pairs={{0,16},{8,24},{16,0},{24,8},{1,17},{9,25},{17,1},{25,9},{2,18},{10... | collective-permute-start | bytes 294920 | tf_op jit(solution)/shard_map/ppermute | solution.py:56
  87.8 4.8 %collective-permute-start.21 = (bf16[64,768]{1,0:T(8,128)(2,1)S(1)}, bf16[64,768]{1,0:T(8,128)(2,1)S(1)}, u32[]{:S(2)}, u32[]{:S(2)}) collective-permute-start(bf16[64,768]{1,0:T(8,128)(2,1)S(1)} %activate.2.refs_0_), channel_id=1, source_target_pairs={{0,16},{8,24},{16,0},{24,8},{1,17},{9,25},{17,1},{25,9},{2,18},{10... | collective-permute-start | bytes 294920 | tf_op jit(solution)/shard_map/ppermute | solution.py:56
  89.4 4.2 %collective-permute-start.26 = (bf16[64,384]{1,0:T(8,128)(2,1)S(1)}, bf16[64,384]{1,0:T(8,128)(2,1)S(1)}, u32[]{:S(2)}, u32[]{:S(2)}) collective-permute-start(bf16[64,384]{1,0:T(8,128)(2,1)S(1)} %activate.3.refs_4_), channel_id=1, source_target_pairs={{0,16},{8,24},{16,0},{24,8},{1,17},{9,25},{17,1},{25,9},{2,18},{10... | collective-permute-start | bytes 147464 | tf_op jit(solution)/shard_map/ppermute | solution.py:56
  90.6 4.2 %collective-permute-start.20 = (bf16[64,768]{1,0:T(8,128)(2,1)S(1)}, bf16[64,768]{1,0:T(8,128)(2,1)S(1)}, u32[]{:S(2)}, u32[]{:S(2)}) collective-permute-start(bf16[64,768]{1,0:T(8,128)(2,1)S(1)} %activate.2.refs_0_), channel_id=1, source_target_pairs={{0,8},{8,0},{16,24},{24,16},{1,9},{9,1},{17,25},{25,17},{2,10},{10... | collective-permute-start | bytes 294920 | tf_op jit(solution)/shard_map/ppermute | solution.py:56
  92.6 2.3 %collective-permute-start.22 = (bf16[64,768]{1,0:T(8,128)(2,1)S(1)}, bf16[64,768]{1,0:T(8,128)(2,1)S(1)}, u32[]{:S(2)}, u32[]{:S(2)}) collective-permute-start(bf16[64,768]{1,0:T(8,128)(2,1)S(1)} %collective-permute-done.21.refs_2_), channel_id=1, source_target_pairs={{0,8},{8,0},{16,24},{24,16},{1,9},{9,1},{17,25},{25,17},{2,10},{10... | collective-permute-start | bytes 294920 | tf_op jit(solution)/shard_map/ppermute | solution.py:56
  92.6 1.4 %collective-permute-start.25 = (bf16[64,384]{1,0:T(8,128)(2,1)S(1)}, bf16[64,384]{1,0:T(8,128)(2,1)S(1)}, u32[]{:S(2)}, u32[]{:S(2)}) collective-permute-start(bf16[64,384]{1,0:T(8,128)(2,1)S(1)} %activate.3.refs_4_), channel_id=1, source_target_pairs={{0,8},{8,0},{16,24},{24,16},{1,9},{9,1},{17,25},{25,17},{2,10},{10... | collective-permute-start | bytes 147464 | tf_op jit(solution)/shard_map/ppermute | solution.py:56
  109.1 3.2 %collective-permute-start.30 = (f32[32,128]{1,0:T(8,128)S(1)}, f32[32,128]{1,0:T(8,128)S(1)}, u32[]{:S(2)}, u32[]{:S(2)}) collective-permute-start(f32[32,128]{1,0:T(8,128)S(1)} %get-tuple-element.74.refs_0_), channel_id=1, source_target_pairs={{0,24},{8,16},{16,8},{24,0},{1,25},{9,17},{17,9},{25,1},{2,26},{10... | collective-permute-start | bytes 49160 | tf_op jit(solution)/shard_map/ppermute | solution.py:56
  109.1 3.8 %collective-permute-start.29 = (f32[32,128]{1,0:T(8,128)S(1)}, f32[32,128]{1,0:T(8,128)S(1)}, u32[]{:S(2)}, u32[]{:S(2)}) collective-permute-start(f32[32,128]{1,0:T(8,128)S(1)} %get-tuple-element.74.refs_0_), channel_id=1, source_target_pairs={{0,16},{8,24},{16,0},{24,8},{1,17},{9,25},{17,1},{25,9},{2,18},{10... | collective-permute-start | bytes 49160 | tf_op jit(solution)/shard_map/ppermute | solution.py:56
  110.2 2.7 %collective-permute-start.28 = (f32[32,128]{1,0:T(8,128)S(1)}, f32[32,128]{1,0:T(8,128)S(1)}, u32[]{:S(2)}, u32[]{:S(2)}) collective-permute-start(f32[32,128]{1,0:T(8,128)S(1)} %get-tuple-element.74.refs_0_), channel_id=1, source_target_pairs={{0,8},{8,0},{16,24},{24,16},{1,9},{9,1},{17,25},{25,17},{2,10},{10... | collective-permute-start | bytes 49160 | tf_op jit(solution)/shard_map/ppermute | solution.py:56
  (14 other events, 221.0 us)

commit v19 on v18

--- a/solution.py
+++ b/solution.py
@@ -241,9 +241,9 @@
 
     w_blocks = {0: w_own, 1: permute(w_own, "gy", 1), 2: permute(w_own, "gy", 2)}
     w_first = permute(w_split[: width // 2], "gy", 4)
-    w_blocks[3] = permute(w_own, "gy", 3)
-    w_late, _ = lax.optimization_barrier((w_split[width // 2 :], x_all))
-    w_second = permute(w_late, "gy", 4)
+    w_late, _ = lax.optimization_barrier(((w_blocks[1], w_split[width // 2 :]), x_all))
+    w_blocks[3] = permute(w_late[0], "gy", 2)
+    w_second = permute(w_late[1], "gy", 4)
 
     def project(x_ref, gain_ref, q_ref, k_ref, v_ref, z0_ref, z2_ref, z13_ref, held):
         gain = 1.0 + gain_ref[0:1]
@@ -291,7 +291,7 @@
     w_blocks[6] = permute(w_blocks[4], "gy", 2)
     w_blocks[5] = permute(w_blocks[4], "gy", 1)
     shares = exchange(shares, "gy")
-    beside = tables, cos, sin, w_blocks[1], w_blocks[2], w_blocks[3], w_blocks[4]
+    beside = tables, cos, sin, w_blocks[2], w_blocks[3], w_blocks[4]
     shares, (tables, cos, sin, *_) = lax.optimization_barrier((shares, beside))
 
     def pack_shares(share_ref, x_ref, out_ref):

time: 114 us -> 113 us (level)
  starting transfers between devices: 33.4 us -> 37.5 us
  waiting for transfers between devices: 41.5 us -> 38.1 us
  blocking collectives: 27.4 us -> 25.5 us
    ppermute x31, waiting for transfers between devices: 34.7 us -> 30 us  [permute(): return lax.ppermute(values, axis, [(i, i ^ m) for i in range(count)])]
    ppermute x31, starting transfers between devices: 22.8 us -> 26.8 us  [permute(): return lax.ppermute(values, axis, [(i, i ^ m) for i in range(count)])]
    all_to_all x2, blocking collectives: 27.4 us -> 25.5 us  [exchange(): return lax.all_to_all(values, axes, split_axis=0, concat_axis=0, tiled=True)]
    all_to_all x2, waiting for transfers between devices: 6.89 us -> 8.11 us  [exchange(): return lax.all_to_all(values, axes, split_axis=0, concat_axis=0, tiled=True)]
where the time goes in v19:
time: 113 us; the launch traced here: 112 us
  waiting for transfers between devices  38.1 us (34%)
  starting transfers between devices  37.5 us (33%)
  blocking collectives  25.5 us (23%)
  Pallas kernels  9.18 us (8%)
    ppermute x31, waiting for transfers between devices, permute(): return lax.ppermute(values, axis, [(i, i ^ m) for i in range(count)])  30 us
    ppermute x31, starting transfers between devices, permute(): return lax.ppermute(values, axis, [(i, i ^ m) for i in range(count)])  26.8 us
    all_to_all x2, blocking collectives, exchange(): return lax.all_to_all(values, axes, split_axis=0, concat_axis=0, tiled=True)  25.5 us
    all_to_all x2, starting transfers between devices, exchange(): return lax.all_to_all(values, axes, split_axis=0, concat_axis=0, tiled=True)  10.7 us
    pallas_call x21, Pallas kernels, run(): pl.pallas_call(kernel, out_shape=[jax.ShapeDtypeStruct(s, d) for s, d in...  9.18 us
    all_to_all x2, waiting for transfers between devices, exchange(): return lax.all_to_all(values, axes, split_axis=0, concat_axis=0, tiled=True)  8.11 us
  transfers between devices with their start and end apart: 33, of which 20 were waited for; matrix products, arithmetic and copies ran while one was open for 0% of the time, Pallas kernels for 4%

profile of v19, /device:TPU:0, one launch (start us, length us, event | category | flops | bytes accessed | tf_op | source)
XLA Modules:
  0.0 112.3 jit_solution(3462653663781392805)
XLA Ops:
  1.7 7.4 %all-to-all-start = ((bf16[8,144,128]{2,1,0:T(8,128)(2,1)}), bf16[8,144,128]{2,1,0:T(8,128)(2,1)S(1)}, u32[]{:S(2)}, u32[]{:S(2)}) async-start(bf16[8,144,128]{2,1,0:T(8,128)(2,1)} %get-tuple-element.43), calls=%async_computation | async-start | bytes 589824 | tf_op jit(solution)/shard_map/all_to_all | solution.py:45
  9.1 2.1 %collective-permute-start.3 = (bf16[576,256]{1,0:T(8,128)(2,1)S(1)}, bf16[576,256]{1,0:T(8,128)(2,1)S(1)}, u32[]{:S(2)}, u32[]{:S(2)}) collective-permute-start(bf16[576,256]{1,0:T(8,128)(2,1)S(1)} %bitcast.7), channel_id=1, source_target_pairs={{0,1},{1,0},{2,3},{3,2},{4,5},{5,4},{6,7},{7,6},{8,9},{9,8},{10,11... | collective-permute-start | bytes 884744 | tf_op jit(solution)/shard_map/ppermute | solution.py:56
  11.2 1.5 %collective-permute-start.2 = (bf16[576,256]{1,0:T(8,128)(2,1)S(1)}, bf16[576,256]{1,0:T(8,128)(2,1)S(1)}, u32[]{:S(2)}, u32[]{:S(2)}) collective-permute-start(bf16[576,256]{1,0:T(8,128)(2,1)S(1)} %bitcast.8), channel_id=1, source_target_pairs={{0,2},{1,3},{2,0},{3,1},{4,6},{5,7},{6,4},{7,5},{8,10},{9,11},{10,... | collective-permute-start | bytes 884744 | tf_op jit(solution)/shard_map/ppermute | solution.py:56
  12.6 2.4 %collective-permute-start.5 = (bf16[288,256]{1,0:T(8,128)(2,1)S(1)}, bf16[288,256]{1,0:T(8,128)(2,1)S(1)}, u32[]{:S(2)}, u32[]{:S(2)}) collective-permute-start(bf16[288,256]{1,0:T(8,128)(2,1)S(1)} %get-tuple-element.79), channel_id=1, source_target_pairs={{0,4},{1,5},{2,6},{3,7},{4,0},{5,1},{6,2},{7,3},{8,12},{9,13},{10,... | collective-permute-start | bytes 442376 | tf_op jit(solution)/shard_map/ppermute | solution.py:56
  15.1 5.0 %all-to-all-done.x_ref = bf16[8,144,128]{2,1,0:T(8,128)(2,1)S(1)} async-done(((bf16[8,144,128]{2,1,0:T(8,128)(2,1)}), bf16[8,144,128]{2,1,0:T(8,128)(2,1)S(1)}, u32[]{:S(2)}, u32[]{:S(2)}) %all-to-all-start) | async-done | bytes 294944 | tf_op jit(solution)/shard_map/all_to_all | solution.py:45
  21.4 1.9 %collective-permute-start.6 = (bf16[288,256]{1,0:T(8,128)(2,1)S(1)}, bf16[288,256]{1,0:T(8,128)(2,1)S(1)}, u32[]{:S(2)}, u32[]{:S(2)}) collective-permute-start(bf16[288,256]{1,0:T(8,128)(2,1)S(1)} %get-tuple-element.55), channel_id=1, source_target_pairs={{0,4},{1,5},{2,6},{3,7},{4,0},{5,1},{6,2},{7,3},{8,12},{9,13},{10,... | collective-permute-start | bytes 442376 | tf_op jit(solution)/shard_map/ppermute | solution.py:56
  23.2 1.5 %collective-permute-start.4 = (bf16[576,256]{1,0:T(8,128)(2,1)S(1)}, bf16[576,256]{1,0:T(8,128)(2,1)S(1)}, u32[]{:S(2)}, u32[]{:S(2)}) collective-permute-start(bf16[576,256]{1,0:T(8,128)(2,1)S(1)} %collective-permute-done.3.refs_1_), channel_id=1, source_target_pairs={{0,2},{1,3},{2,0},{3,1},{4,6},{5,7},{6,4},{7,5},{8,10},{9,11},{10,... | collective-permute-start | bytes 884744 | tf_op jit(solution)/shard_map/ppermute | solution.py:56
  24.7 1.6 %collective-permute-start.1 = (bf16[256,128]{1,0:T(8,128)(2,1)S(1)}, bf16[256,128]{1,0:T(8,128)(2,1)S(1)}, u32[]{:S(2)}, u32[]{:S(2)}) collective-permute-start(bf16[256,128]{1,0:T(8,128)(2,1)S(1)} %pair_sum.1), channel_id=1, source_target_pairs={{0,16},{8,24},{16,0},{24,8},{1,17},{9,25},{17,1},{25,9},{2,18},{10... | collective-permute-start | bytes 196616 | tf_op jit(solution)/shard_map/ppermute | solution.py:56
  26.5 2.6 %collective-permute-done.1.z2_ref = bf16[256,128]{1,0:T(8,128)(2,1)S(1)} collective-permute-done((bf16[256,128]{1,0:T(8,128)(2,1)S(1)}, bf16[256,128]{1,0:T(8,128)(2,1)S(1)}, u32[]{:S(2)}, u32[]{:S(2)}) %collective-permute-start.1) | collective-permute-done | bytes 65568 | tf_op jit(solution)/shard_map/ppermute | solution.py:56
  29.7 3.3 %all-to-all-start.1 = ((bf16[8,32,128]{2,1,0:T(8,128)(2,1)}), bf16[8,32,128]{2,1,0:T(8,128)(2,1)S(1)}, u32[]{:S(2)}, u32[]{:S(2)}) async-start(bf16[8,32,128]{2,1,0:T(8,128)(2,1)} %share_sum.1), calls=%async_computation.1 | async-start | bytes 131072 | tf_op jit(solution)/shard_map/all_to_all | solution.py:45
  33.7 1.4 %collective-permute-start.13 = (bf16[576,256]{1,0:T(8,128)(2,1)S(1)}, bf16[576,256]{1,0:T(8,128)(2,1)S(1)}, u32[]{:S(2)}, u32[]{:S(2)}) collective-permute-start(bf16[576,256]{1,0:T(8,128)(2,1)S(1)} %constant_dynamic-update-slice_fusion.refs_4_), channel_id=1, source_target_pairs={{0,1},{1,0},{2,3},{3,2},{4,5},{5,4},{6,7},{7,6},{8,9},{9,8},{10,11... | collective-permute-start | bytes 884744 | tf_op jit(solution)/shard_map/ppermute | solution.py:56
  35.1 1.5 %collective-permute-start.14 = (bf16[576,256]{1,0:T(8,128)(2,1)S(1)}, bf16[576,256]{1,0:T(8,128)(2,1)S(1)}, u32[]{:S(2)}, u32[]{:S(2)}) collective-permute-start(bf16[576,256]{1,0:T(8,128)(2,1)S(1)} %constant_dynamic-update-slice_fusion.refs_4_), channel_id=1, source_target_pairs={{0,2},{1,3},{2,0},{3,1},{4,6},{5,7},{6,4},{7,5},{8,10},{9,11},{10,... | collective-permute-start | bytes 884744 | tf_op jit(solution)/shard_map/ppermute | solution.py:56
  37.4 3.1 %all-to-all-done.1.share_ref = bf16[8,32,128]{2,1,0:T(8,128)(2,1)S(1)} async-done(((bf16[8,32,128]{2,1,0:T(8,128)(2,1)}), bf16[8,32,128]{2,1,0:T(8,128)(2,1)S(1)}, u32[]{:S(2)}, u32[]{:S(2)}) %all-to-all-start.1) | async-done | bytes 65568 | tf_op jit(solution)/shard_map/all_to_all | solution.py:45
  40.5 1.5 %collective-permute-start.8 = (bf16[9,32,128]{2,1,0:T(8,128)(2,1)S(1)}, bf16[9,32,128]{2,1,0:T(8,128)(2,1)S(1)}, u32[]{:S(2)}, u32[]{:S(2)}) collective-permute-start(bf16[9,32,128]{2,1,0:T(8,128)(2,1)S(1)} %pack_shares.1.refs_0_), channel_id=1, source_target_pairs={{0,16},{8,24},{16,0},{24,8},{1,17},{9,25},{17,1},{25,9},{2,18},{10... | collective-permute-start | bytes 221192 | tf_op jit(solution)/shard_map/ppermute | solution.py:56
  42.1 2.8 %collective-permute-done.8.refs_2_ = bf16[9,32,128]{2,1,0:T(8,128)(2,1)S(1)} collective-permute-done((bf16[9,32,128]{2,1,0:T(8,128)(2,1)S(1)}, bf16[9,32,128]{2,1,0:T(8,128)(2,1)S(1)}, u32[]{:S(2)}, u32[]{:S(2)}) %collective-permute-start.8) | collective-permute-done | bytes 73760 | tf_op jit(solution)/shard_map/ppermute | solution.py:56
  44.9 1.3 %collective-permute-done.9.refs_3_ = bf16[9,32,128]{2,1,0:T(8,128)(2,1)S(1)} collective-permute-done((bf16[9,32,128]{2,1,0:T(8,128)(2,1)S(1)}, bf16[9,32,128]{2,1,0:T(8,128)(2,1)S(1)}, u32[]{:S(2)}, u32[]{:S(2)}) %collective-permute-start.9) | collective-permute-done | bytes 73760 | tf_op jit(solution)/shard_map/ppermute | solution.py:56
  46.2 1.7 %attention.1 = (bf16[17,16,128]{2,1,0:T(8,128)(2,1)S(1)}, bf16[17,16,128]{2,1,0:T(8,128)(2,1)S(1)}) custom-call(bf16[9,32,128]{2,1,0:T(8,128)(2,1)S(1)} %pack_shares.1.refs_0_, bf16[9,32,128]{2,1,0:T(8,128)(2,1)S(1)} %collective-permute-done.7.refs_1_, bf16[9,32,128]{2,1,0:T(8,128)(2,1)S(1)} %collective-permute-done.8.refs_2_, ...), custom_call_target="tpu_custom_call" | custom-call | tf_op jit(solution)/shard_map/attention/pallas_call | solution.py:33
  48.2 1.2 %collective-permute-done.10.pair_ref = bf16[17,16,128]{2,1,0:T(8,128)(2,1)S(1)} collective-permute-done((bf16[17,16,128]{2,1,0:T(8,128)(2,1)S(1)}, bf16[17,16,128]{2,1,0:T(8,128)(2,1)S(1)}, u32[]{:S(2)}, u32[]{:S(2)}) %collective-permute-start.10) | collective-permute-done | bytes 69664 | tf_op jit(solution)/shard_map/ppermute | solution.py:56
  49.6 1.5 %collective-permute-start.11 = (bf16[17,16,128]{2,1,0:T(8,128)(2,1)S(1)}, bf16[17,16,128]{2,1,0:T(8,128)(2,1)S(1)}, u32[]{:S(2)}, u32[]{:S(2)}) collective-permute-start(bf16[17,16,128]{2,1,0:T(8,128)(2,1)S(1)} %pair_terms.1.own_ref), channel_id=1, source_target_pairs={{0,16},{8,24},{16,0},{24,8},{1,17},{9,25},{17,1},{25,9},{2,18},{10... | collective-permute-start | bytes 208904 | tf_op jit(solution)/shard_map/ppermute | solution.py:56
  51.1 2.8 %collective-permute-done.11.across_ref = bf16[17,16,128]{2,1,0:T(8,128)(2,1)S(1)} collective-permute-done((bf16[17,16,128]{2,1,0:T(8,128)(2,1)S(1)}, bf16[17,16,128]{2,1,0:T(8,128)(2,1)S(1)}, u32[]{:S(2)}, u32[]{:S(2)}) %collective-permute-start.11) | collective-permute-done | bytes 69664 | tf_op jit(solution)/shard_map/ppermute | solution.py:56
  54.2 1.2 %collective-permute-done.12.other_ref = bf16[16,16,128]{2,1,0:T(8,128)(2,1)S(1)} collective-permute-done((bf16[16,16,128]{2,1,0:T(8,128)(2,1)S(1)}, bf16[16,16,128]{2,1,0:T(8,128)(2,1)S(1)}, u32[]{:S(2)}, u32[]{:S(2)}) %collective-permute-start.12) | collective-permute-done | bytes 65568 | tf_op jit(solution)/shard_map/ppermute | solution.py:56
  55.4 1.6 %collective-permute-done.15.refs_7_ = bf16[576,256]{1,0:T(8,128)(2,1)S(1)} collective-permute-done((bf16[576,256]{1,0:T(8,128)(2,1)S(1)}, bf16[576,256]{1,0:T(8,128)(2,1)S(1)}, u32[]{:S(2)}, u32[]{:S(2)}) %collective-permute-start.15) | collective-permute-done | bytes 294944 | tf_op jit(solution)/shard_map/ppermute | solution.py:56
  58.0 1.2 %collective-permute-done.16.b_ref = f32[32,128]{1,0:T(8,128)S(1)} collective-permute-done((f32[32,128]{1,0:T(8,128)S(1)}, f32[32,128]{1,0:T(8,128)S(1)}, u32[]{:S(2)}, u32[]{:S(2)}) %collective-permute-start.16) | collective-permute-done | bytes 16416 | tf_op jit(solution)/shard_map/ppermute | solution.py:56
  59.1 1.5 %collective-permute-start.17 = (f32[32,128]{1,0:T(8,128)S(1)}, f32[32,128]{1,0:T(8,128)S(1)}, u32[]{:S(2)}, u32[]{:S(2)}) collective-permute-start(f32[32,128]{1,0:T(8,128)S(1)} %pair_add.1.refs_0_), channel_id=1, source_target_pairs={{0,16},{8,24},{16,0},{24,8},{1,17},{9,25},{17,1},{25,9},{2,18},{10... | collective-permute-start | bytes 49160 | tf_op jit(solution)/shard_map/ppermute | solution.py:56
  60.7 2.2 %collective-permute-done.17.refs_1_ = f32[32,128]{1,0:T(8,128)S(1)} collective-permute-done((f32[32,128]{1,0:T(8,128)S(1)}, f32[32,128]{1,0:T(8,128)S(1)}, u32[]{:S(2)}, u32[]{:S(2)}) %collective-permute-start.17) | collective-permute-done | bytes 16416 | tf_op jit(solution)/shard_map/ppermute | solution.py:56
  63.2 12.2 %all_to_all.20.ff_ref = bf16[8,144,128]{2,1,0:T(8,128)(2,1)S(1)} all-to-all(bf16[8,144,128]{2,1,0:T(8,128)(2,1)S(1)} %get-tuple-element.69), channel_id=1, replica_groups=mesh['gx'=4,'gy'=8] {'gy'}, dimensions={0} | all-to-all | bytes 589824 | tf_op jit(solution)/shard_map/all_to_all | solution.py:45
  78.0 1.6 %collective-permute-start.19 = (bf16[64,1536]{1,0:T(8,128)(2,1)S(1)}, bf16[64,1536]{1,0:T(8,128)(2,1)S(1)}, u32[]{:S(2)}, u32[]{:S(2)}) collective-permute-start(bf16[64,1536]{1,0:T(8,128)(2,1)S(1)} %pair_sum_ff.2), channel_id=1, source_target_pairs={{0,16},{8,24},{16,0},{24,8},{1,17},{9,25},{17,1},{25,9},{2,18},{10... | collective-permute-start | bytes 589832 | tf_op jit(solution)/shard_map/ppermute | solution.py:56
  80.2 5.6 %collective-permute-done.19.z2_ref = bf16[64,1536]{1,0:T(8,128)(2,1)S(1)} collective-permute-done((bf16[64,1536]{1,0:T(8,128)(2,1)S(1)}, bf16[64,1536]{1,0:T(8,128)(2,1)S(1)}, u32[]{:S(2)}, u32[]{:S(2)}) %collective-permute-start.19) | collective-permute-done | bytes 196640 | tf_op jit(solution)/shard_map/ppermute | solution.py:56
  86.0 1.6 %collective-permute-start.21 = (bf16[64,768]{1,0:T(8,128)(2,1)S(1)}, bf16[64,768]{1,0:T(8,128)(2,1)S(1)}, u32[]{:S(2)}, u32[]{:S(2)}) collective-permute-start(bf16[64,768]{1,0:T(8,128)(2,1)S(1)} %activate.2.refs_0_), channel_id=1, source_target_pairs={{0,16},{8,24},{16,0},{24,8},{1,17},{9,25},{17,1},{25,9},{2,18},{10... | collective-permute-start | bytes 294920 | tf_op jit(solution)/shard_map/ppermute | solution.py:56
  88.8 2.0 %collective-permute-done.21.refs_2_ = bf16[64,768]{1,0:T(8,128)(2,1)S(1)} collective-permute-done((bf16[64,768]{1,0:T(8,128)(2,1)S(1)}, bf16[64,768]{1,0:T(8,128)(2,1)S(1)}, u32[]{:S(2)}, u32[]{:S(2)}) %collective-permute-start.21) | collective-permute-done | bytes 98336 | tf_op jit(solution)/shard_map/ppermute | solution.py:56
  93.8 13.3 %all_to_all.21.parts_ref = bf16[8,144,128]{2,1,0:T(8,128)(2,1)S(1)} all-to-all(bf16[8,144,128]{2,1,0:T(8,128)(2,1)S(1)} %project_down.1), channel_id=1, replica_groups=mesh['gx'=4,'gy'=8] {'gy'}, dimensions={0} | all-to-all | bytes 589824 | tf_op jit(solution)/shard_map/all_to_all | solution.py:45
  109.1 1.9 %collective-permute-done.29.refs_2_ = f32[32,128]{1,0:T(8,128)S(1)} collective-permute-done((f32[32,128]{1,0:T(8,128)S(1)}, f32[32,128]{1,0:T(8,128)S(1)}, u32[]{:S(2)}, u32[]{:S(2)}) %collective-permute-start.29) | collective-permute-done | bytes 16416 | tf_op jit(solution)/shard_map/ppermute | solution.py:56
  (90 shorter events, 17.3 us)
Async XLA Ops:
  1.7 18.5 %all-to-all-start = ((bf16[8,144,128]{2,1,0:T(8,128)(2,1)}), bf16[8,144,128]{2,1,0:T(8,128)(2,1)S(1)}, u32[]{:S(2)}, u32[]{:S(2)}) async-start(bf16[8,144,128]{2,1,0:T(8,128)(2,1)} %get-tuple-element.43), calls=%async_computation | async-start | bytes 589824 | tf_op jit(solution)/shard_map/all_to_all | solution.py:45
  9.1 12.3 %collective-permute-start.3 = (bf16[576,256]{1,0:T(8,128)(2,1)S(1)}, bf16[576,256]{1,0:T(8,128)(2,1)S(1)}, u32[]{:S(2)}, u32[]{:S(2)}) collective-permute-start(bf16[576,256]{1,0:T(8,128)(2,1)S(1)} %bitcast.7), channel_id=1, source_target_pairs={{0,1},{1,0},{2,3},{3,2},{4,5},{5,4},{6,7},{7,6},{8,9},{9,8},{10,11... | collective-permute-start | bytes 884744 | tf_op jit(solution)/shard_map/ppermute | solution.py:56
  11.2 26.2 %collective-permute-start.2 = (bf16[576,256]{1,0:T(8,128)(2,1)S(1)}, bf16[576,256]{1,0:T(8,128)(2,1)S(1)}, u32[]{:S(2)}, u32[]{:S(2)}) collective-permute-start(bf16[576,256]{1,0:T(8,128)(2,1)S(1)} %bitcast.8), channel_id=1, source_target_pairs={{0,2},{1,3},{2,0},{3,1},{4,6},{5,7},{6,4},{7,5},{8,10},{9,11},{10,... | collective-permute-start | bytes 884744 | tf_op jit(solution)/shard_map/ppermute | solution.py:56
  12.6 20.4 %collective-permute-start.5 = (bf16[288,256]{1,0:T(8,128)(2,1)S(1)}, bf16[288,256]{1,0:T(8,128)(2,1)S(1)}, u32[]{:S(2)}, u32[]{:S(2)}) collective-permute-start(bf16[288,256]{1,0:T(8,128)(2,1)S(1)} %get-tuple-element.79), channel_id=1, source_target_pairs={{0,4},{1,5},{2,6},{3,7},{4,0},{5,1},{6,2},{7,3},{8,12},{9,13},{10,... | collective-permute-start | bytes 442376 | tf_op jit(solution)/shard_map/ppermute | solution.py:56
  20.6 4.1 %collective-permute-start = (bf16[2,256,128]{2,1,0:T(8,128)(2,1)S(1)}, bf16[2,256,128]{2,1,0:T(8,128)(2,1)S(1)}, u32[]{:S(2)}, u32[]{:S(2)}) collective-permute-start(bf16[2,256,128]{2,1,0:T(8,128)(2,1)S(1)} %get-tuple-element.45), channel_id=1, source_target_pairs={{0,8},{8,0},{16,24},{24,16},{1,9},{9,1},{17,25},{25,17},{2,10},{10... | collective-permute-start | bytes 393224 | tf_op jit(solution)/shard_map/ppermute | solution.py:56
  21.4 12.3 %collective-permute-start.6 = (bf16[288,256]{1,0:T(8,128)(2,1)S(1)}, bf16[288,256]{1,0:T(8,128)(2,1)S(1)}, u32[]{:S(2)}, u32[]{:S(2)}) collective-permute-start(bf16[288,256]{1,0:T(8,128)(2,1)S(1)} %get-tuple-element.55), channel_id=1, source_target_pairs={{0,4},{1,5},{2,6},{3,7},{4,0},{5,1},{6,2},{7,3},{8,12},{9,13},{10,... | collective-permute-start | bytes 442376 | tf_op jit(solution)/shard_map/ppermute | solution.py:56
  23.2 14.1 %collective-permute-start.4 = (bf16[576,256]{1,0:T(8,128)(2,1)S(1)}, bf16[576,256]{1,0:T(8,128)(2,1)S(1)}, u32[]{:S(2)}, u32[]{:S(2)}) collective-permute-start(bf16[576,256]{1,0:T(8,128)(2,1)S(1)} %collective-permute-done.3.refs_1_), channel_id=1, source_target_pairs={{0,2},{1,3},{2,0},{3,1},{4,6},{5,7},{6,4},{7,5},{8,10},{9,11},{10,... | collective-permute-start | bytes 884744 | tf_op jit(solution)/shard_map/ppermute | solution.py:56
  24.7 4.3 %collective-permute-start.1 = (bf16[256,128]{1,0:T(8,128)(2,1)S(1)}, bf16[256,128]{1,0:T(8,128)(2,1)S(1)}, u32[]{:S(2)}, u32[]{:S(2)}) collective-permute-start(bf16[256,128]{1,0:T(8,128)(2,1)S(1)} %pair_sum.1), channel_id=1, source_target_pairs={{0,16},{8,24},{16,0},{24,8},{1,17},{9,25},{17,1},{25,9},{2,18},{10... | collective-permute-start | bytes 196616 | tf_op jit(solution)/shard_map/ppermute | solution.py:56
  29.7 10.7 %all-to-all-start.1 = ((bf16[8,32,128]{2,1,0:T(8,128)(2,1)}), bf16[8,32,128]{2,1,0:T(8,128)(2,1)S(1)}, u32[]{:S(2)}, u32[]{:S(2)}) async-start(bf16[8,32,128]{2,1,0:T(8,128)(2,1)} %share_sum.1), calls=%async_computation.1 | async-start | bytes 131072 | tf_op jit(solution)/shard_map/all_to_all | solution.py:45
  33.7 14.2 %collective-permute-start.13 = (bf16[576,256]{1,0:T(8,128)(2,1)S(1)}, bf16[576,256]{1,0:T(8,128)(2,1)S(1)}, u32[]{:S(2)}, u32[]{:S(2)}) collective-permute-start(bf16[576,256]{1,0:T(8,128)(2,1)S(1)} %constant_dynamic-update-slice_fusion.refs_4_), channel_id=1, source_target_pairs={{0,1},{1,0},{2,3},{3,2},{4,5},{5,4},{6,7},{7,6},{8,9},{9,8},{10,11... | collective-permute-start | bytes 884744 | tf_op jit(solution)/shard_map/ppermute | solution.py:56
  35.1 12.8 %collective-permute-start.14 = (bf16[576,256]{1,0:T(8,128)(2,1)S(1)}, bf16[576,256]{1,0:T(8,128)(2,1)S(1)}, u32[]{:S(2)}, u32[]{:S(2)}) collective-permute-start(bf16[576,256]{1,0:T(8,128)(2,1)S(1)} %constant_dynamic-update-slice_fusion.refs_4_), channel_id=1, source_target_pairs={{0,2},{1,3},{2,0},{3,1},{4,6},{5,7},{6,4},{7,5},{8,10},{9,11},{10,... | collective-permute-start | bytes 884744 | tf_op jit(solution)/shard_map/ppermute | solution.py:56
  40.5 4.4 %collective-permute-start.8 = (bf16[9,32,128]{2,1,0:T(8,128)(2,1)S(1)}, bf16[9,32,128]{2,1,0:T(8,128)(2,1)S(1)}, u32[]{:S(2)}, u32[]{:S(2)}) collective-permute-start(bf16[9,32,128]{2,1,0:T(8,128)(2,1)S(1)} %pack_shares.1.refs_0_), channel_id=1, source_target_pairs={{0,16},{8,24},{16,0},{24,8},{1,17},{9,25},{17,1},{25,9},{2,18},{10... | collective-permute-start | bytes 221192 | tf_op jit(solution)/shard_map/ppermute | solution.py:56
  42.1 2.8 %collective-permute-start.7 = (bf16[9,32,128]{2,1,0:T(8,128)(2,1)S(1)}, bf16[9,32,128]{2,1,0:T(8,128)(2,1)S(1)}, u32[]{:S(2)}, u32[]{:S(2)}) collective-permute-start(bf16[9,32,128]{2,1,0:T(8,128)(2,1)S(1)} %pack_shares.1.refs_0_), channel_id=1, source_target_pairs={{0,8},{8,0},{16,24},{24,16},{1,9},{9,1},{17,25},{25,17},{2,10},{10... | collective-permute-start | bytes 221192 | tf_op jit(solution)/shard_map/ppermute | solution.py:56
  44.9 1.3 %collective-permute-start.9 = (bf16[9,32,128]{2,1,0:T(8,128)(2,1)S(1)}, bf16[9,32,128]{2,1,0:T(8,128)(2,1)S(1)}, u32[]{:S(2)}, u32[]{:S(2)}) collective-permute-start(bf16[9,32,128]{2,1,0:T(8,128)(2,1)S(1)} %collective-permute-done.8.refs_2_), channel_id=1, source_target_pairs={{0,8},{8,0},{16,24},{24,16},{1,9},{9,1},{17,25},{25,17},{2,10},{10... | collective-permute-start | bytes 221192 | tf_op jit(solution)/shard_map/ppermute | solution.py:56
  47.9 9.1 %collective-permute-start.15 = (bf16[576,256]{1,0:T(8,128)(2,1)S(1)}, bf16[576,256]{1,0:T(8,128)(2,1)S(1)}, u32[]{:S(2)}, u32[]{:S(2)}) collective-permute-start(bf16[576,256]{1,0:T(8,128)(2,1)S(1)} %collective-permute-done.14.refs_6_), channel_id=1, source_target_pairs={{0,1},{1,0},{2,3},{3,2},{4,5},{5,4},{6,7},{7,6},{8,9},{9,8},{10,11... | collective-permute-start | bytes 884744 | tf_op jit(solution)/shard_map/ppermute | solution.py:56
  48.2 1.3 %collective-permute-start.10 = (bf16[17,16,128]{2,1,0:T(8,128)(2,1)S(1)}, bf16[17,16,128]{2,1,0:T(8,128)(2,1)S(1)}, u32[]{:S(2)}, u32[]{:S(2)}) collective-permute-start(bf16[17,16,128]{2,1,0:T(8,128)(2,1)S(1)} %get-tuple-element.65), channel_id=1, source_target_pairs={{0,8},{8,0},{16,24},{24,16},{1,9},{9,1},{17,25},{25,17},{2,10},{10... | collective-permute-start | bytes 208904 | tf_op jit(solution)/shard_map/ppermute | solution.py:56
  49.6 4.3 %collective-permute-start.11 = (bf16[17,16,128]{2,1,0:T(8,128)(2,1)S(1)}, bf16[17,16,128]{2,1,0:T(8,128)(2,1)S(1)}, u32[]{:S(2)}, u32[]{:S(2)}) collective-permute-start(bf16[17,16,128]{2,1,0:T(8,128)(2,1)S(1)} %pair_terms.1.own_ref), channel_id=1, source_target_pairs={{0,16},{8,24},{16,0},{24,8},{1,17},{9,25},{17,1},{25,9},{2,18},{10... | collective-permute-start | bytes 208904 | tf_op jit(solution)/shard_map/ppermute | solution.py:56
  54.1 1.3 %collective-permute-start.12 = (bf16[16,16,128]{2,1,0:T(8,128)(2,1)S(1)}, bf16[16,16,128]{2,1,0:T(8,128)(2,1)S(1)}, u32[]{:S(2)}, u32[]{:S(2)}) collective-permute-start(bf16[16,16,128]{2,1,0:T(8,128)(2,1)S(1)} %divide.1.own_ref), channel_id=1, source_target_pairs={{0,8},{8,0},{16,24},{24,16},{1,9},{9,1},{17,25},{25,17},{2,10},{10... | collective-permute-start | bytes 196616 | tf_op jit(solution)/shard_map/ppermute | solution.py:56
  57.9 1.2 %collective-permute-start.16 = (f32[32,128]{1,0:T(8,128)S(1)}, f32[32,128]{1,0:T(8,128)S(1)}, u32[]{:S(2)}, u32[]{:S(2)}) collective-permute-start(f32[32,128]{1,0:T(8,128)S(1)} %get-tuple-element.67.a_ref), channel_id=1, source_target_pairs={{0,8},{8,0},{16,24},{24,16},{1,9},{9,1},{17,25},{25,17},{2,10},{10... | collective-permute-start | bytes 49160 | tf_op jit(solution)/shard_map/ppermute | solution.py:56
  59.1 3.7 %collective-permute-start.17 = (f32[32,128]{1,0:T(8,128)S(1)}, f32[32,128]{1,0:T(8,128)S(1)}, u32[]{:S(2)}, u32[]{:S(2)}) collective-permute-start(f32[32,128]{1,0:T(8,128)S(1)} %pair_add.1.refs_0_), channel_id=1, source_target_pairs={{0,16},{8,24},{16,0},{24,8},{1,17},{9,25},{17,1},{25,9},{2,18},{10... | collective-permute-start | bytes 49160 | tf_op jit(solution)/shard_map/ppermute | solution.py:56
  76.2 1.8 %collective-permute-start.18 = (bf16[2,64,1536]{2,1,0:T(8,128)(2,1)S(1)}, bf16[2,64,1536]{2,1,0:T(8,128)(2,1)S(1)}, u32[]{:S(2)}, u32[]{:S(2)}) collective-permute-start(bf16[2,64,1536]{2,1,0:T(8,128)(2,1)S(1)} %get-tuple-element.71), channel_id=1, source_target_pairs={{0,8},{8,0},{16,24},{24,16},{1,9},{9,1},{17,25},{25,17},{2,10},{10... | collective-permute-start | bytes 1179656 | tf_op jit(solution)/shard_map/ppermute | solution.py:56
  76.8 2.8 %collective-permute-start.23 = (bf16[2,64,768]{2,1,0:T(8,128)(2,1)S(1)}, bf16[2,64,768]{2,1,0:T(8,128)(2,1)S(1)}, u32[]{:S(2)}, u32[]{:S(2)}) collective-permute-start(bf16[2,64,768]{2,1,0:T(8,128)(2,1)S(1)} %get-tuple-element.74), channel_id=1, source_target_pairs={{0,8},{8,0},{16,24},{24,16},{1,9},{9,1},{17,25},{25,17},{2,10},{10... | collective-permute-start | bytes 589832 | tf_op jit(solution)/shard_map/ppermute | solution.py:56
  78.0 7.8 %collective-permute-start.19 = (bf16[64,1536]{1,0:T(8,128)(2,1)S(1)}, bf16[64,1536]{1,0:T(8,128)(2,1)S(1)}, u32[]{:S(2)}, u32[]{:S(2)}) collective-permute-start(bf16[64,1536]{1,0:T(8,128)(2,1)S(1)} %pair_sum_ff.2), channel_id=1, source_target_pairs={{0,16},{8,24},{16,0},{24,8},{1,17},{9,25},{17,1},{25,9},{2,18},{10... | collective-permute-start | bytes 589832 | tf_op jit(solution)/shard_map/ppermute | solution.py:56
  79.6 7.9 %collective-permute-start.24 = (bf16[64,768]{1,0:T(8,128)(2,1)S(1)}, bf16[64,768]{1,0:T(8,128)(2,1)S(1)}, u32[]{:S(2)}, u32[]{:S(2)}) collective-permute-start(bf16[64,768]{1,0:T(8,128)(2,1)S(1)} %pair_sum_ff.3), channel_id=1, source_target_pairs={{0,16},{8,24},{16,0},{24,8},{1,17},{9,25},{17,1},{25,9},{2,18},{10... | collective-permute-start | bytes 294920 | tf_op jit(solution)/shard_map/ppermute | solution.py:56
  86.0 4.8 %collective-permute-start.21 = (bf16[64,768]{1,0:T(8,128)(2,1)S(1)}, bf16[64,768]{1,0:T(8,128)(2,1)S(1)}, u32[]{:S(2)}, u32[]{:S(2)}) collective-permute-start(bf16[64,768]{1,0:T(8,128)(2,1)S(1)} %activate.2.refs_0_), channel_id=1, source_target_pairs={{0,16},{8,24},{16,0},{24,8},{1,17},{9,25},{17,1},{25,9},{2,18},{10... | collective-permute-start | bytes 294920 | tf_op jit(solution)/shard_map/ppermute | solution.py:56
  87.6 4.2 %collective-permute-start.26 = (bf16[64,384]{1,0:T(8,128)(2,1)S(1)}, bf16[64,384]{1,0:T(8,128)(2,1)S(1)}, u32[]{:S(2)}, u32[]{:S(2)}) collective-permute-start(bf16[64,384]{1,0:T(8,128)(2,1)S(1)} %activate.3.refs_4_), channel_id=1, source_target_pairs={{0,16},{8,24},{16,0},{24,8},{1,17},{9,25},{17,1},{25,9},{2,18},{10... | collective-permute-start | bytes 147464 | tf_op jit(solution)/shard_map/ppermute | solution.py:56
  88.8 4.2 %collective-permute-start.20 = (bf16[64,768]{1,0:T(8,128)(2,1)S(1)}, bf16[64,768]{1,0:T(8,128)(2,1)S(1)}, u32[]{:S(2)}, u32[]{:S(2)}) collective-permute-start(bf16[64,768]{1,0:T(8,128)(2,1)S(1)} %activate.2.refs_0_), channel_id=1, source_target_pairs={{0,8},{8,0},{16,24},{24,16},{1,9},{9,1},{17,25},{25,17},{2,10},{10... | collective-permute-start | bytes 294920 | tf_op jit(solution)/shard_map/ppermute | solution.py:56
  90.7 2.3 %collective-permute-start.22 = (bf16[64,768]{1,0:T(8,128)(2,1)S(1)}, bf16[64,768]{1,0:T(8,128)(2,1)S(1)}, u32[]{:S(2)}, u32[]{:S(2)}) collective-permute-start(bf16[64,768]{1,0:T(8,128)(2,1)S(1)} %collective-permute-done.21.refs_2_), channel_id=1, source_target_pairs={{0,8},{8,0},{16,24},{24,16},{1,9},{9,1},{17,25},{25,17},{2,10},{10... | collective-permute-start | bytes 294920 | tf_op jit(solution)/shard_map/ppermute | solution.py:56
  90.7 1.4 %collective-permute-start.25 = (bf16[64,384]{1,0:T(8,128)(2,1)S(1)}, bf16[64,384]{1,0:T(8,128)(2,1)S(1)}, u32[]{:S(2)}, u32[]{:S(2)}) collective-permute-start(bf16[64,384]{1,0:T(8,128)(2,1)S(1)} %activate.3.refs_4_), channel_id=1, source_target_pairs={{0,8},{8,0},{16,24},{24,16},{1,9},{9,1},{17,25},{25,17},{2,10},{10... | collective-permute-start | bytes 147464 | tf_op jit(solution)/shard_map/ppermute | solution.py:56
  107.3 1.9 %collective-permute-start.28 = (f32[32,128]{1,0:T(8,128)S(1)}, f32[32,128]{1,0:T(8,128)S(1)}, u32[]{:S(2)}, u32[]{:S(2)}) collective-permute-start(f32[32,128]{1,0:T(8,128)S(1)} %get-tuple-element.76.refs_0_), channel_id=1, source_target_pairs={{0,8},{8,0},{16,24},{24,16},{1,9},{9,1},{17,25},{25,17},{2,10},{10... | collective-permute-start | bytes 49160 | tf_op jit(solution)/shard_map/ppermute | solution.py:56
  107.3 3.8 %collective-permute-start.29 = (f32[32,128]{1,0:T(8,128)S(1)}, f32[32,128]{1,0:T(8,128)S(1)}, u32[]{:S(2)}, u32[]{:S(2)}) collective-permute-start(f32[32,128]{1,0:T(8,128)S(1)} %get-tuple-element.76.refs_0_), channel_id=1, source_target_pairs={{0,16},{8,24},{16,0},{24,8},{1,17},{9,25},{17,1},{25,9},{2,18},{10... | collective-permute-start | bytes 49160 | tf_op jit(solution)/shard_map/ppermute | solution.py:56
  108.4 3.2 %collective-permute-start.30 = (f32[32,128]{1,0:T(8,128)S(1)}, f32[32,128]{1,0:T(8,128)S(1)}, u32[]{:S(2)}, u32[]{:S(2)}) collective-permute-start(f32[32,128]{1,0:T(8,128)S(1)} %get-tuple-element.76.refs_0_), channel_id=1, source_target_pairs={{0,24},{8,16},{16,8},{24,0},{1,25},{9,17},{17,9},{25,1},{2,26},{10... | collective-permute-start | bytes 49160 | tf_op jit(solution)/shard_map/ppermute | solution.py:56
  (14 other events, 215.2 us)
